TPU v7x, 32 devices: a whole 2x2x4 slice. The times are simulated.
32 devices in a mesh: grp: 2 (over y), ops: 4 (over z), sec: 2 (over x), rep: 2 (over core).
Axes of the slice: x: 2, y: 2, z: 4, core: 2. Of those that a mesh axis runs over, the one named last changes fastest.
Arguments:
- wavefunction: bfloat16 [4, 512, 512], P(('grp', 'sec'), 'rep'), parts along dimension 0, may hold values from -135 to 135
- sector_sizes: int32 [4, 2], P('grp'), parts along dimension 0, may hold values from 256 to 512, as said below
- left_blocks: bfloat16 [32, 512, 512], P(('grp', 'ops')), parts along dimension 0, may hold values from -0.25 to 0.25
- right_blocks: bfloat16 [32, 512, 512], P(('grp', 'ops')), parts along dimension 0, may hold values from -0.25 to 0.25
- sector_pairs: int32 [32, 8, 2], P(('grp', 'ops')), parts along dimension 0, may hold values from 0 to 1, as said below
- pair_weights: float32 [32, 8], P(('grp', 'ops')), parts along dimension 0, may hold values from -0.6 to 0.6
Outputs:
- second_wave: bfloat16 [4, 512, 512], P(('grp', 'sec'), 'rep'), parts along dimension 0
- second_sigma: float32 [4, 512, 512], P(('grp', 'sec'), 'rep'), parts along dimension 0
There are 2 independent parts, one for each index of `grp`. A program takes and returns all parts, laid end to end along the dimension named above; each array names one. Nothing has to cross between parts.
Inputs may be any that keep to these rules, and one draw needn't show every extreme that they name: `sector_sizes`: each row holds the live left and right dimension of a sector; some sector has both equal to 512. `sector_pairs`: each row names the input sector and the output sector that the term maps it to.
All inputs are finite; a program needn't handle non-finite values.
Results may differ from a plain program's by a relative error of at most 0.0058.
Values may be sent and summed in bfloat16 or wider, within the bound.
No kernel may reach another device: no remote copies, remote signals or barrier semaphores. Data moves between devices by JAX's collectives and lax.ppermute only.
A program may use at most 64 MiB of HBM per device.

v0:
```python
import jax
import jax.numpy as jnp
from jax import lax
from jax.sharding import PartitionSpec as P

epsilon = 1e-06


def local_mask(sector_sizes, first_sector, per_group, row_start, row_count, columns):
    bounds = lax.dynamic_slice_in_dim(sector_sizes, first_sector, per_group, 0)
    rows = row_start + lax.broadcasted_iota(jnp.int32, (per_group, row_count, columns), 1)
    cols_index = lax.broadcasted_iota(jnp.int32, (per_group, row_count, columns), 2)
    return (rows < bounds[:, 0][:, None, None]) & (cols_index < bounds[:, 1][:, None, None])


def spread_tiles(wave_part):
    return lax.all_gather(wave_part, ("sec", "rep"), axis=1, tiled=True)


def mixing_matrix(term_pairs, term_weights, sector_total):
    sectors = jnp.arange(sector_total, dtype=jnp.int32)
    source_hot = (term_pairs[:, 0][:, None] == sectors[None, :]).astype(jnp.float32)
    target_hot = (term_pairs[:, 1][:, None] == sectors[None, :]).astype(jnp.float32) * term_weights[
        :, None
    ]
    return jnp.dot(
        target_hot.T,
        source_hot,
        precision=lax.Precision.HIGHEST,
        preferred_element_type=jnp.float32,
    )


def term_update(left_part, right_full, mixing_rows, tiles, sector_total):
    left_product = jnp.einsum("ik,wgkj->gwij", left_part, tiles, preferred_element_type=jnp.float32)
    left_product = left_product.reshape(sector_total, left_part.shape[0], tiles.shape[3])
    combined = jnp.einsum(
        "ba,aij->bij",
        mixing_rows,
        left_product,
        precision=lax.Precision.HIGHEST,
        preferred_element_type=jnp.float32,
    ).astype(jnp.bfloat16)
    return jnp.einsum("bij,kj->bik", combined, right_full, preferred_element_type=jnp.float32)


def sigma_terms(
    gathered,
    left_rows,
    right_blocks,
    sector_pairs,
    pair_weights,
    sec_index,
    sec_count,
    per_group,
    columns,
):
    term_count = pair_weights.shape[0]
    row_count = left_rows.shape[1]
    sector_total = per_group * sec_count
    tiles = gathered.reshape(per_group, sec_count, columns, columns)

    def visit(term_index, running):
        mixing = mixing_matrix(sector_pairs[term_index], pair_weights[term_index], sector_total)
        mixing_rows = lax.dynamic_slice_in_dim(mixing, sec_index * per_group, per_group, 0)
        return running + term_update(
            left_rows[term_index], right_blocks[term_index], mixing_rows, tiles, sector_total
        )

    start = jnp.zeros((per_group, row_count, columns), jnp.float32)
    return lax.fori_loop(0, term_count, visit, start)


def davidson_stats(wave_share, sigma_share):
    correlation, norm_square, sigma_square = lax.psum(
        (
            jnp.sum(wave_share * sigma_share),
            jnp.sum(wave_share * wave_share),
            jnp.sum(sigma_share * sigma_share),
        ),
        ("ops", "sec", "rep"),
    )
    rayleigh = correlation / norm_square
    residual_square = (
        sigma_square - 2.0 * rayleigh * correlation + rayleigh * rayleigh * norm_square
    )
    return (rayleigh, residual_square)


def local(wavefunction, sector_sizes, left_blocks, right_blocks, sector_pairs, pair_weights):
    sec_count = lax.axis_size("sec")
    sec_index = lax.axis_index("sec")
    rep_index = lax.axis_index("rep")
    ops_count = lax.axis_size("ops")
    ops_index = lax.axis_index("ops")
    per_group, row_count, columns = wavefunction.shape
    row_start = rep_index * row_count
    first_sector = sec_index * per_group
    flat_rows = per_group * row_count
    share_rows = flat_rows // ops_count
    share_start = ops_index * share_rows
    live_mask = local_mask(sector_sizes, first_sector, per_group, row_start, row_count, columns)
    left_rows = lax.dynamic_slice_in_dim(left_blocks, row_start, row_count, 1)
    live_count = jnp.sum(
        sector_sizes[:, 0].astype(jnp.float32) * sector_sizes[:, 1].astype(jnp.float32)
    )
    first_wave = jnp.where(live_mask, wavefunction, jnp.zeros_like(wavefunction))
    partial_first = sigma_terms(
        spread_tiles(first_wave),
        left_rows,
        right_blocks,
        sector_pairs,
        pair_weights,
        sec_index,
        sec_count,
        per_group,
        columns,
    )
    wave_share = lax.dynamic_slice_in_dim(
        first_wave.reshape(flat_rows, columns), share_start, share_rows, 0
    ).astype(jnp.float32)
    first_sigma = lax.psum(partial_first, "ops")
    first_sigma = jnp.where(live_mask, first_sigma, jnp.zeros((), jnp.float32))
    wave_float = first_wave.astype(jnp.float32)
    sigma_share = lax.dynamic_slice_in_dim(
        first_sigma.reshape(flat_rows, columns), share_start, share_rows, 0
    )
    rayleigh, residual_square = davidson_stats(wave_share, sigma_share)
    residual = first_sigma - rayleigh * wave_float
    second_wave = (residual / jnp.sqrt(residual_square / live_count + epsilon)).astype(jnp.bfloat16)
    partial_second = sigma_terms(
        spread_tiles(second_wave),
        left_rows,
        right_blocks,
        sector_pairs,
        pair_weights,
        sec_index,
        sec_count,
        per_group,
        columns,
    )
    second_sigma = lax.psum(partial_second, "ops")
    second_sigma = jnp.where(live_mask, second_sigma, jnp.zeros((), jnp.float32))
    return (second_wave, second_sigma)


def solution(mesh):
    return jax.shard_map(
        local,
        mesh=mesh,
        in_specs=(
            P(("grp", "sec"), "rep", None),
            P("grp", None),
            P(("grp", "ops"), None, None),
            P(("grp", "ops"), None, None),
            P(("grp", "ops"), None, None),
            P(("grp", "ops"), None),
        ),
        out_specs=(P(("grp", "sec"), "rep", None), P(("grp", "sec"), "rep", None)),
        check_vma=False,
    )
```

profile of v0, /device:TPU:0, one launch (start us, length us, event | category | flops | bytes accessed | tf_op | source)
XLA Modules:
  0.0 233.2 jit_solution(579438192440524203)
XLA Ops:
  7.2 0.0 copy-start
  7.2 0.0 copy-start.4
  7.2 0.0 copy-start.6
  7.2 0.0 all-gather.3.cloned.1.call-start
  7.3 0.8 constant_dynamic-slice_fusion.7
  8.1 0.6 fusion.48
  8.7 0.7 add_compare_fusion
  9.3 2.4 %fusion.45 = bf16[1,256,512]{2,1,0:T(8,128)(2,1)} fusion(bf16[1,256,512]{2,1,0:T(8,128)(2,1)} %param.10, s32[]{:T(128)} %bitcast.1, pred[256]{0:T(512)(128)(4,1)S(1)} %add_compare_fusion), kind=kLoop, calls=%fused_computation.65 | loop fusion | flops 393216 | bytes 524548 | tf_op jit(solution)/shard_map/jit(_where)/select_n | solution.py:107
  11.7 0.0 all-gather.3.cloned.1.call-update
  11.7 0.0 all-reduce.4.cloned.1.call-start
  11.8 1.1 constant_dynamic-slice_fusion.6
  12.8 18.5 %all-gather.3.cloned.1.call-done = bf16[1,1024,512]{2,1,0:T(8,128)(2,1)} async-done(((bf16[1,256,512]{2,1,0:T(8,128)(2,1)}), bf16[1,1024,512]{2,1,0:T(8,128)(2,1)}) %all-gather.3.cloned.1.call-update) | async-done | bytes 1048592 | tf_op jit(solution)/shard_map/all_gather | solution.py:17
  31.3 29.4 %while.32 = (s32[]{:T(128)}, f32[1,256,512]{2,1,0:T(8,128)S(1)}, s32[4,8,2]{1,2,0:T(2,128)S(1)}, f32[4,8]{1,0:T(4,128)S(1)}, s32[]{:T(128)}, /*index=5*/bf16[4,2...) while((s32[]{:T(128)}, f32[1,256,512]{2,1,0:T(8,128)S(1)}, ...), condition=%wide.region_1.2_spmd.clone, body=%wide.region_0.0_spmd.clone.sunk | while | flops 406061504 | bytes 5507115 | solution.py:71
  31.3 0.3 fusion.79
  31.6 1.8 convolution_bitcast_fusion.6
  33.4 3.8 %fusion.80 = bf16[1,256,512]{2,0,1:T(2,128)(2,1)S(1)} fusion(f32[2,256,512]{2,1,0:T(8,128)S(1)} %convolution_bitcast_fusion.6, f32[2,2]{1,0:T(2,128)S(1)} %fusion.79, s32[]{:T(128)} %get-tuple-element.618), kind=kOutput, calls=%fused_computation.4.clone.1 | convolution fusion | flops 3145728 | bytes 1311236 | tf_op jit(solution)/shard_map/while/body/eval_jaxpr/ba,aij->bij/dot_general | solution.py:37
  37.2 1.4 fusion.81
  38.7 0.3 fusion.79
  38.9 1.8 convolution_bitcast_fusion.6
  40.7 3.8 %fusion.80 = bf16[1,256,512]{2,0,1:T(2,128)(2,1)S(1)} fusion(f32[2,256,512]{2,1,0:T(8,128)S(1)} %convolution_bitcast_fusion.6, f32[2,2]{1,0:T(2,128)S(1)} %fusion.79, s32[]{:T(128)} %get-tuple-element.618), kind=kOutput, calls=%fused_computation.4.clone.1 | convolution fusion | flops 3145728 | bytes 1311236 | tf_op jit(solution)/shard_map/while/body/eval_jaxpr/ba,aij->bij/dot_general | solution.py:37
  44.5 1.4 fusion.81
  46.0 0.3 fusion.79
  46.3 1.8 convolution_bitcast_fusion.6
  48.1 3.8 %fusion.80 = bf16[1,256,512]{2,0,1:T(2,128)(2,1)S(1)} fusion(f32[2,256,512]{2,1,0:T(8,128)S(1)} %convolution_bitcast_fusion.6, f32[2,2]{1,0:T(2,128)S(1)} %fusion.79, s32[]{:T(128)} %get-tuple-element.618), kind=kOutput, calls=%fused_computation.4.clone.1 | convolution fusion | flops 3145728 | bytes 1311236 | tf_op jit(solution)/shard_map/while/body/eval_jaxpr/ba,aij->bij/dot_general | solution.py:37
  51.9 1.4 fusion.81
  53.4 0.3 fusion.79
  53.6 1.8 convolution_bitcast_fusion.6
  55.4 3.8 %fusion.80 = bf16[1,256,512]{2,0,1:T(2,128)(2,1)S(1)} fusion(f32[2,256,512]{2,1,0:T(8,128)S(1)} %convolution_bitcast_fusion.6, f32[2,2]{1,0:T(2,128)S(1)} %fusion.79, s32[]{:T(128)} %get-tuple-element.618), kind=kOutput, calls=%fused_computation.4.clone.1 | convolution fusion | flops 3145728 | bytes 1311236 | tf_op jit(solution)/shard_map/while/body/eval_jaxpr/ba,aij->bij/dot_general | solution.py:37
  59.2 1.4 fusion.81
  60.7 0.0 copy-start.1
  60.7 0.8 copy-done.1
  61.5 0.0 all-reduce.4.cloned.1.call-update
  61.5 0.0 all-gather.5.cloned.1.call-start
  61.6 0.7 multiply_reduce_fusion.1
  62.3 37.7 %all-reduce.4.cloned.1.call-done = f32[1,256,512]{2,1,0:T(8,128)} async-done(((f32[1,256,512]{2,1,0:T(8,128)}), f32[1,256,512]{2,1,0:T(8,128)}) %all-reduce.4.cloned.1.call-update) | async-done | bytes 524304 | tf_op jit(solution)/shard_map/psum | solution.py:122
  99.9 1.7 fusion.44
  101.7 1.6 fusion.46
  103.2 31.6 %all-reduce = (f32[]{:T(128)}, f32[]{:T(128)}, f32[]{:T(128)}) all-reduce(f32[]{:T(128)} %get-tuple-element.445, f32[]{:T(128)} %get-tuple-element.444, f32[]{:T(128)} %get-tuple-element.446), channel_id=1, replica_groups=mesh['grp'=2,'ops'=4,'sec'=2,'rep'=2] {'ops','sec','rep'}, use_global_device_ids=true, to_apply=%region_8.9 | all-reduce | flops 3 | bytes 24 | tf_op jit(solution)/shard_map/psum | solution.py:75
  138.9 2.5 %divide_convert_fusion = bf16[1,256,512]{2,1,0:T(8,128)(2,1)} fusion(f32[]{:T(128)S(6)} %sqrt.3, f32[]{:T(128)S(6)} %div.12, f32[1,256,512]{2,1,0:T(8,128)} %all-reduce.4.cloned.1.call-done, s32[]{:T(128)} %bitcast.1, pred[256]{0:T(512)(128)(4,1)S(1)} %add_compare_fusion, bf16[1,256,512]{2,1,0:T(8,128)(2,1)S(1)} %copy-done.3), kind=kLoop, calls=%fused_computation.60 | loop fusion | flops 1179648 | bytes 1048844 | tf_op jit(solution)/shard_map/convert_element_type | solution.py:130
  141.4 0.0 all-gather.5.cloned.1.call-update
  141.4 0.0 all-reduce.6.cloned.1.call-start
  141.5 14.1 %all-gather.5.cloned.1.call-done = bf16[1,1024,512]{2,1,0:T(8,128)(2,1)} async-done(((bf16[1,256,512]{2,1,0:T(8,128)(2,1)}), bf16[1,1024,512]{2,1,0:T(8,128)(2,1)}) %all-gather.5.cloned.1.call-update) | async-done | bytes 1048592 | tf_op jit(solution)/shard_map/all_gather | solution.py:17
  155.5 29.4 %while.33 = (s32[]{:T(128)}, f32[1,256,512]{2,1,0:T(8,128)S(1)}, s32[4,8,2]{1,2,0:T(2,128)S(1)}, f32[4,8]{1,0:T(4,128)S(1)}, s32[]{:T(128)}, /*index=5*/bf16[4,2...) while((s32[]{:T(128)}, f32[1,256,512]{2,1,0:T(8,128)S(1)}, ...), condition=%wide.region_11.12_spmd.clone, body=%wide.region_10.11_spmd.clone.sunk | while | flops 406061504 | bytes 5507115 | solution.py:71
  155.5 0.3 fusion.90
  155.8 1.8 convolution_bitcast_fusion.7
  157.6 3.8 %fusion.91 = bf16[1,256,512]{2,0,1:T(2,128)(2,1)S(1)} fusion(f32[2,256,512]{2,1,0:T(8,128)S(1)} %convolution_bitcast_fusion.7, f32[2,2]{1,0:T(2,128)S(1)} %fusion.90, s32[]{:T(128)} %get-tuple-element.648), kind=kOutput, calls=%fused_computation.34.clone.1 | convolution fusion | flops 3145728 | bytes 1311236 | tf_op jit(solution)/shard_map/while/body/eval_jaxpr/ba,aij->bij/dot_general | solution.py:37
  161.4 1.4 fusion.92
  162.9 0.3 fusion.90
  163.1 1.8 convolution_bitcast_fusion.7
  164.9 3.8 %fusion.91 = bf16[1,256,512]{2,0,1:T(2,128)(2,1)S(1)} fusion(f32[2,256,512]{2,1,0:T(8,128)S(1)} %convolution_bitcast_fusion.7, f32[2,2]{1,0:T(2,128)S(1)} %fusion.90, s32[]{:T(128)} %get-tuple-element.648), kind=kOutput, calls=%fused_computation.34.clone.1 | convolution fusion | flops 3145728 | bytes 1311236 | tf_op jit(solution)/shard_map/while/body/eval_jaxpr/ba,aij->bij/dot_general | solution.py:37
  168.7 1.4 fusion.92
  170.2 0.3 fusion.90
  170.5 1.8 convolution_bitcast_fusion.7
  172.3 3.8 %fusion.91 = bf16[1,256,512]{2,0,1:T(2,128)(2,1)S(1)} fusion(f32[2,256,512]{2,1,0:T(8,128)S(1)} %convolution_bitcast_fusion.7, f32[2,2]{1,0:T(2,128)S(1)} %fusion.90, s32[]{:T(128)} %get-tuple-element.648), kind=kOutput, calls=%fused_computation.34.clone.1 | convolution fusion | flops 3145728 | bytes 1311236 | tf_op jit(solution)/shard_map/while/body/eval_jaxpr/ba,aij->bij/dot_general | solution.py:37
  176.1 1.4 fusion.92
  177.6 0.3 fusion.90
  177.8 1.8 convolution_bitcast_fusion.7
  179.6 3.8 %fusion.91 = bf16[1,256,512]{2,0,1:T(2,128)(2,1)S(1)} fusion(f32[2,256,512]{2,1,0:T(8,128)S(1)} %convolution_bitcast_fusion.7, f32[2,2]{1,0:T(2,128)S(1)} %fusion.90, s32[]{:T(128)} %get-tuple-element.648), kind=kOutput, calls=%fused_computation.34.clone.1 | convolution fusion | flops 3145728 | bytes 1311236 | tf_op jit(solution)/shard_map/while/body/eval_jaxpr/ba,aij->bij/dot_general | solution.py:37
  183.4 1.4 fusion.92
  184.9 0.0 copy-start.2
  184.9 0.8 copy-done.2
  185.7 0.0 all-reduce.6.cloned.1.call-update
  185.7 38.5 %all-reduce.6.cloned.1.call-done = f32[1,256,512]{2,1,0:T(8,128)} async-done(((f32[1,256,512]{2,1,0:T(8,128)}), f32[1,256,512]{2,1,0:T(8,128)}) %all-reduce.6.cloned.1.call-update) | async-done | bytes 524304 | tf_op jit(solution)/shard_map/psum | solution.py:142
  224.2 2.5 %fusion.43 = f32[1,256,512]{2,1,0:T(8,128)} fusion(f32[1,256,512]{2,1,0:T(8,128)} %all-reduce.6.cloned.1.call-done, s32[]{:T(128)} %bitcast.1, pred[256]{0:T(512)(128)(4,1)S(1)} %add_compare_fusion), kind=kLoop, calls=%fused_computation.63 | loop fusion | flops 393216 | bytes 1048836 | tf_op jit(solution)/shard_map/jit(_where)/select_n | solution.py:143
  (33 shorter events, 0.2 us)
Async XLA Ops:
  7.2 4.6 %copy-start = (bf16[4,512,512]{2,1,0:T(8,128)(2,1)S(1)}, bf16[4,512,512]{2,1,0:T(8,128)(2,1)}, u32[]{:S(2)}) copy-start(bf16[4,512,512]{2,1,0:T(8,128)(2,1)} %param.12) | copy-start | bytes 6291460
  7.2 24.1 %copy-start.4 = (s32[4,8,2]{1,2,0:T(2,128)S(1)}, s32[4,8,2]{1,2,0:T(2,128)}, u32[]{:S(2)}) copy-start(s32[4,8,2]{1,2,0:T(2,128)} %param.14) | copy-start | bytes 772
  7.2 24.1 %copy-start.6 = (f32[4,8]{1,0:T(4,128)S(1)}, f32[4,8]{1,0:T(4,128)}, u32[]{:S(2)}) copy-start(f32[4,8]{1,0:T(4,128)} %param.15) | copy-start | bytes 388
  7.2 24.1 %all-gather.3.cloned.1.call-start = ((), (), s32[]{:S(2)}) async-start(), calls=%async_computation | async-start | bytes 1310720 | tf_op jit(solution)/shard_map/all_gather | solution.py:17
  11.7 88.2 %all-reduce.4.cloned.1.call-start = ((), (), s32[]{:S(2)}) async-start(), calls=%async_computation.1 | async-start | bytes 1048576 | tf_op jit(solution)/shard_map/psum | solution.py:122
  31.3 30.3 %copy-start.5 = (s32[2,2]{1,0:T(2,128)S(1)}, s32[2,2]{1,0:T(2,128)}, u32[]{:S(2)}) copy-start(s32[2,2]{1,0:T(2,128)} %param.11) | copy-start | bytes 52
  31.3 107.6 %copy-start.3 = (bf16[1,256,512]{2,1,0:T(8,128)(2,1)S(1)}, bf16[1,256,512]{2,1,0:T(8,128)(2,1)}, u32[]{:S(2)}) copy-start(bf16[1,256,512]{2,1,0:T(8,128)(2,1)} %param.10) | copy-start | bytes 786436
  60.7 0.8 copy-start.1
  61.5 94.0 %all-gather.5.cloned.1.call-start = ((), (), s32[]{:S(2)}) async-start(), calls=%async_computation.2 | async-start | bytes 1310720 | tf_op jit(solution)/shard_map/all_gather | solution.py:17
  141.4 82.8 %all-reduce.6.cloned.1.call-start = ((), (), s32[]{:S(2)}) async-start(), calls=%async_computation.3 | async-start | bytes 1048576 | tf_op jit(solution)/shard_map/psum | solution.py:142
  184.9 0.8 copy-start.2
Sparse Core Ops, SparseCore 0:
  11.8 19.4 all-gather.2
  61.6 38.2 all-reduce.3
  141.5 13.9 all-gather.4
  185.8 38.2 all-reduce.5
where the time goes:
time: 234 us; the launch traced here: 233 us
  waiting for transfers between devices  109 us (47%)
  matrix products  58.1 us (25%)
  blocking collectives  31.6 us (14%)
  between operations  17.9 us (8%)
  other arithmetic  12 us (5%)
  local copies, waits for them, and re-layouts  4.22 us (2%)
    psum x1, waiting for transfers between devices, local(): second_sigma = lax.psum(partial_second, 'ops')  38.5 us
    psum x1, waiting for transfers between devices, local(): first_sigma = lax.psum(partial_first, 'ops')  37.7 us
    all_gather x2, waiting for transfers between devices, spread_tiles(): return lax.all_gather(wave_part, ('sec', 'rep'), axis=1, tiled=True)  32.5 us
    psum x1, blocking collectives, davidson_stats(): lax.psum((jnp.sum(wave_share * sigma_share), jnp.sum(wave_share * wave_sh...  31.6 us
    dot_general x8, matrix products, term_update(): jnp.einsum('ba,aij->bij', mixing_rows, left_product, precision=lax.Precis...  30.3 us
    dot_general x8, matrix products, term_update(): jnp.einsum('ik,wgkj->gwij', left_part, tiles, preferred_element_type=jnp....  14.3 us
    dot_general x8, matrix products, term_update(): jnp.einsum('bij,kj->bik', combined, right_full, preferred_element_type=jn...  11.5 us
  transfers between devices with their start and end apart: 4, of which 4 were waited for; matrix products, arithmetic and copies ran while one was open for 1% of the time, Pallas kernels for 0%

commit v1 on v0

v1 whole, which is shorter than its diff:
```python
import jax
import jax.numpy as jnp
from jax import lax
from jax.experimental import pallas as pl
from jax.experimental.pallas import tpu as pltpu
from jax.sharding import PartitionSpec as P

epsilon = 1e-06
vmem_bytes = 40 * 1024 * 1024


def mixing_scalars(pairs_ref, weights_ref, target, terms, sectors):
    table = []
    for term in range(terms):
        row = [jnp.float32(0.0)] * sectors
        for pair in range(weights_ref.shape[1]):
            source = pairs_ref[term, pair, 0]
            hit = pairs_ref[term, pair, 1] == target
            weight = weights_ref[term, pair]
            for sector in range(sectors):
                row[sector] = row[sector] + jnp.where(
                    hit & (source == sector), weight, jnp.float32(0.0)
                )
        table.append(row)
    return table


def apply_operators(mixing, vector, left, right, arrived):
    total = None
    for term in range(left.shape[0]):
        arrived(term)
        combined = None
        for sector, weight in enumerate(mixing[term]):
            product = weight * jnp.dot(
                left[term], vector[sector], preferred_element_type=jnp.float32
            )
            combined = product if combined is None else combined + product
        part = lax.dot_general(
            combined.astype(jnp.bfloat16),
            right[term],
            (((1,), (1,)), ((), ())),
            preferred_element_type=jnp.float32,
        )
        total = part if total is None else total + part
    return total


def live_cells(sizes_ref, sector, row_start, rows, columns):
    row = row_start + lax.broadcasted_iota(jnp.int32, (rows, columns), 0)
    column = lax.broadcasted_iota(jnp.int32, (rows, columns), 1)
    return (row < sizes_ref[sector, 0]) & (column < sizes_ref[sector, 1])


def operator_copies(left_ref, right_ref, left, right, sems, row_start):
    rows = left.shape[1]
    copies = []
    for term in range(left.shape[0]):
        copies.append(
            (
                pltpu.make_async_copy(
                    left_ref.at[term, pl.ds(row_start, rows)], left.at[term], sems.at[0, term]
                ),
                pltpu.make_async_copy(right_ref.at[term], right.at[term], sems.at[1, term]),
            )
        )
    return copies


def first_kernel(
    sizes_ref, pairs_ref, weights_ref, left_ref, right_ref, wave_ref,
    masked_ref, partial_ref,
    left, right, vector, operator_sems, wave_sem, masked_sem,
):
    sectors, columns = vector.shape[0], vector.shape[2]
    rows = partial_ref.shape[0]
    target = lax.axis_index("sec")
    row_start = pl.multiple_of(lax.axis_index("rep") * rows, rows)
    wave_copy = pltpu.make_async_copy(wave_ref, vector, wave_sem)
    wave_copy.start()
    copies = operator_copies(left_ref, right_ref, left, right, operator_sems, row_start)
    for pair in copies:
        for copy in pair:
            copy.start()
    mixing = mixing_scalars(pairs_ref, weights_ref, target, left.shape[0], sectors)
    wave_copy.wait()
    step = 32

    for sector in range(sectors):

        def mask_rows(block, carry):
            start = pl.multiple_of(block * step, step)
            live = live_cells(sizes_ref, sector, start, step, columns)
            values = vector[sector, pl.ds(start, step), :].astype(jnp.float32)
            vector[sector, pl.ds(start, step), :] = jnp.where(live, values, 0.0).astype(
                jnp.bfloat16
            )
            return carry

        lax.fori_loop(0, vector.shape[1] // step, mask_rows, 0)
    masked_copy = pltpu.make_async_copy(vector, masked_ref, masked_sem)
    masked_copy.start()

    def arrived(term):
        for copy in copies[term]:
            copy.wait()

    total = apply_operators(mixing, vector, left, right, arrived)
    live = live_cells(sizes_ref, target, row_start, rows, columns)
    partial_ref[...] = jnp.where(live, total, 0.0).astype(partial_ref.dtype)
    masked_copy.wait()


def second_kernel(
    sizes_ref, pairs_ref, weights_ref, left_ref, right_ref, wave_ref, sigma_ref,
    second_ref, partial_ref,
    left, right, wave, sigma, operator_sems, wave_sem, sigma_sem, second_sem,
):
    sectors, columns = wave.shape[0], wave.shape[2]
    rows = partial_ref.shape[0]
    target = lax.axis_index("sec")
    row_start = pl.multiple_of(lax.axis_index("rep") * rows, rows)
    wave_copy = pltpu.make_async_copy(wave_ref, wave, wave_sem)
    sigma_copy = pltpu.make_async_copy(sigma_ref, sigma, sigma_sem)
    wave_copy.start()
    sigma_copy.start()
    copies = operator_copies(left_ref, right_ref, left, right, operator_sems, row_start)
    for pair in copies:
        for copy in pair:
            copy.start()
    mixing = mixing_scalars(pairs_ref, weights_ref, target, left.shape[0], sectors)
    live_count = jnp.float32(0.0)
    for sector in range(sectors):
        live_count = live_count + sizes_ref[sector, 0].astype(jnp.float32) * sizes_ref[
            sector, 1
        ].astype(jnp.float32)
    wave_copy.wait()
    sigma_copy.wait()
    step = 16
    blocks = wave.shape[1] // step
    sums = (jnp.zeros((step, columns), jnp.float32),) * 3

    for sector in range(sectors):

        def add_rows(block, carry):
            start = pl.multiple_of(block * step, step)
            w = wave[sector, pl.ds(start, step), :].astype(jnp.float32)
            s = sigma[sector, pl.ds(start, step), :].astype(jnp.float32)
            return (carry[0] + w * s, carry[1] + w * w, carry[2] + s * s)

        sums = lax.fori_loop(0, blocks, add_rows, sums)
    correlation, norm_square, sigma_square = (jnp.sum(x, keepdims=True) for x in sums)
    rayleigh = correlation / norm_square
    residual_square = (
        sigma_square - 2.0 * rayleigh * correlation + rayleigh * rayleigh * norm_square
    )
    residual_square = jnp.maximum(residual_square, 0.0)
    scale = 1.0 / jnp.sqrt(residual_square / jnp.full((1, 1), live_count) + epsilon)
    wave_scale = jnp.broadcast_to(rayleigh * scale, (step, columns))
    sigma_scale = jnp.broadcast_to(scale, (step, columns))

    for sector in range(sectors):

        def make_rows(block, carry):
            start = pl.multiple_of(block * step, step)
            w = wave[sector, pl.ds(start, step), :].astype(jnp.float32)
            s = sigma[sector, pl.ds(start, step), :].astype(jnp.float32)
            sigma[sector, pl.ds(start, step), :] = (sigma_scale * s - wave_scale * w).astype(
                jnp.bfloat16
            )
            return carry

        lax.fori_loop(0, blocks, make_rows, 0)
    second_copy = pltpu.make_async_copy(
        sigma.at[target, pl.ds(row_start, rows)], second_ref.at[0], second_sem
    )
    second_copy.start()

    def arrived(term):
        for copy in copies[term]:
            copy.wait()

    total = apply_operators(mixing, sigma, left, right, arrived)
    live = live_cells(sizes_ref, target, row_start, rows, columns)
    partial_ref[...] = jnp.where(live, total, 0.0).astype(partial_ref.dtype)
    second_copy.wait()


def kernel_specs(count):
    smem = pl.BlockSpec(memory_space=pltpu.SMEM)
    anywhere = pl.BlockSpec(memory_space=pl.ANY)
    return [smem] * 3 + [anywhere] * count


def local(wavefunction, sector_sizes, left_blocks, right_blocks, sector_pairs, pair_weights):
    sectors = sector_sizes.shape[0]
    ops_count = lax.axis_size("ops")
    _, rows, columns = wavefunction.shape
    terms, side = left_blocks.shape[0], left_blocks.shape[1]
    share = rows // ops_count
    operators = (sector_sizes, sector_pairs, pair_weights, left_blocks, right_blocks)
    bf16, f32 = jnp.bfloat16, jnp.float32
    operator_scratch = [
        pltpu.VMEM((terms, rows, side), bf16),
        pltpu.VMEM((terms, columns, columns), bf16),
    ]
    anywhere = pl.BlockSpec(memory_space=pl.ANY)
    inside = pl.BlockSpec(memory_space=pltpu.VMEM)
    full = jax.ShapeDtypeStruct((sectors, side, columns), bf16)
    partial = jax.ShapeDtypeStruct((rows, columns), bf16)
    params = pltpu.CompilerParams(vmem_limit_bytes=vmem_bytes)

    def summed(piece):
        pieces = lax.all_to_all(
            piece.reshape(ops_count, share, columns), "ops", 0, 0, tiled=True
        )
        return jnp.sum(pieces.astype(f32), axis=0).astype(bf16)

    gathered = lax.all_gather(wavefunction, ("sec", "rep"), axis=1, tiled=True)
    masked, first_part = pl.pallas_call(
        first_kernel,
        out_shape=(full, partial),
        in_specs=kernel_specs(3),
        out_specs=(anywhere, inside),
        scratch_shapes=operator_scratch
        + [
            pltpu.VMEM((sectors, side, columns), bf16),
            pltpu.SemaphoreType.DMA((2, terms)),
            pltpu.SemaphoreType.DMA,
            pltpu.SemaphoreType.DMA,
        ],
        compiler_params=params,
        name="first_sigma_terms",
    )(*operators, gathered.reshape(sectors, side, columns))
    first_sigma = lax.all_gather(summed(first_part), ("sec", "rep", "ops"), axis=0, tiled=True)
    second_wave, second_part = pl.pallas_call(
        second_kernel,
        out_shape=(jax.ShapeDtypeStruct((1, rows, columns), bf16), partial),
        in_specs=kernel_specs(4),
        out_specs=(anywhere, inside),
        scratch_shapes=operator_scratch
        + [
            pltpu.VMEM((sectors, side, columns), bf16),
            pltpu.VMEM((sectors, side, columns), bf16),
            pltpu.SemaphoreType.DMA((2, terms)),
            pltpu.SemaphoreType.DMA,
            pltpu.SemaphoreType.DMA,
            pltpu.SemaphoreType.DMA,
        ],
        compiler_params=params,
        name="second_sigma_terms",
    )(*operators, masked, first_sigma.reshape(sectors, side, columns))
    second_sigma = lax.all_gather(summed(second_part), "ops", axis=0, tiled=True)
    return (second_wave, second_sigma.astype(f32)[None])


def solution(mesh):
    return jax.shard_map(
        local,
        mesh=mesh,
        in_specs=(
            P(("grp", "sec"), "rep", None),
            P("grp", None),
            P(("grp", "ops"), None, None),
            P(("grp", "ops"), None, None),
            P(("grp", "ops"), None, None),
            P(("grp", "ops"), None),
        ),
        out_specs=(P(("grp", "sec"), "rep", None), P(("grp", "sec"), "rep", None)),
        check_vma=False,
    )
```

time: 234 us -> 133 us (0.57)
  matrix products: 58.1 us -> 0 us
  waiting for transfers between devices: 109 us -> 57.2 us
  other arithmetic: 12 us -> 1.56 us
  Pallas kernels: 0 us -> 9.97 us
  blocking collectives: 31.6 us -> 40.7 us
  local copies, waits for them, and re-layouts: 4.22 us -> 9.37 us
  between operations: 17.9 us -> 14.1 us
    psum x2 -> x0, waiting for transfers between devices: 76.1 us -> none  [the longest x1 38.5 us: local(): second_sigma = lax.psum(partial_second, 'ops')]
    dot_general x32 -> x0, matrix products: 58.1 us -> none  [the longest x8 30.3 us: term_update(): jnp.einsum('ba,aij->bij', mixing_rows, left_product, precision=lax.Precis...]
    psum x1 -> x0, blocking collectives: 31.6 us -> none  [davidson_stats(): lax.psum((jnp.sum(wave_share * sigma_share), jnp.sum(wave_share * wave_sh...]
    all_to_all x0 -> x2, blocking collectives: none -> 26.3 us  [summed(): lax.all_to_all(piece.reshape(ops_count, share, columns), 'ops', 0, 0, til...]
    all_gather x2, waiting for transfers between devices: 32.5 us -> 56.5 us  [the longest x1 36.3 us: local(): lax.all_gather(summed(first_part), ('sec', 'rep', 'ops'), axis=0, tiled=T...]
    all_gather x0 -> x1, blocking collectives: none -> 14.5 us  [local(): lax.all_gather(summed(second_part), 'ops', axis=0, tiled=True)]
    pallas_call x0 -> x2, Pallas kernels: none -> 9.97 us  [the longest x1 5.72 us: local(): pl.pallas_call(second_kernel, out_shape=(jax.ShapeDtypeStruct((1, rows, c...]
    unnamed x14 -> x21, local copies, waits for them, and re-layouts: 1.6 us -> 9.37 us
  transfers between devices with their start and end apart: 4 -> 2, of which waited for: 4 -> 2; matrix products, arithmetic and copies ran while one was open for 1% -> 1% of each run, Pallas kernels for 0% -> 0%
where the time goes in v1:
time: 133 us
  waiting for transfers between devices  57.2 us (43%)
  blocking collectives  40.7 us (31%)
  between operations  14.1 us (11%)
  Pallas kernels  9.97 us (7%)
  local copies, waits for them, and re-layouts  9.37 us (7%)
  other arithmetic  1.56 us (1%)
    all_gather x1, waiting for transfers between devices, local(): lax.all_gather(summed(first_part), ('sec', 'rep', 'ops'), axis=0, tiled=T...  36.3 us
    all_to_all x2, blocking collectives, summed(): lax.all_to_all(piece.reshape(ops_count, share, columns), 'ops', 0, 0, til...  26.3 us
    all_gather x1, waiting for transfers between devices, local(): gathered = lax.all_gather(wavefunction, ('sec', 'rep'), axis=1, tiled=True)  20.3 us
    all_gather x1, blocking collectives, local(): lax.all_gather(summed(second_part), 'ops', axis=0, tiled=True)  14.5 us
    unnamed x21, local copies, waits for them, and re-layouts  9.37 us
    pallas_call x1, Pallas kernels, local(): pl.pallas_call(second_kernel, out_shape=(jax.ShapeDtypeStruct((1, rows, c...  5.72 us
    pallas_call x1, Pallas kernels, local(): pl.pallas_call(first_kernel, out_shape=(full, partial), in_specs=kernel_s...  4.25 us
  transfers between devices with their start and end apart: 2, of which 2 were waited for; matrix products, arithmetic and copies ran while one was open for 1% of the time, Pallas kernels for 0%

profile of v1, /device:TPU:0, one launch (start us, length us, event | category | flops | bytes accessed | tf_op | source)
XLA Modules:
  0.0 133.0 jit_solution(1859047392960281014)
XLA Ops:
  7.2 0.0 all-gather.3.cloned.1.call-start
  7.2 0.7 all-gather.3.cloned.1.call-update
  7.9 0.0 all-gather.5.cloned.1.call-start
  7.9 0.8 copy.9.pairs_ref
  8.7 20.3 %all-gather.3.cloned.1.call-done = bf16[1,1024,512]{2,1,0:T(8,128)(2,1)} async-done(((bf16[1,256,512]{2,1,0:T(8,128)(2,1)}), bf16[1,1024,512]{2,1,0:T(8,128)(2,1)}) %all-gather.3.cloned.1.call-update) | async-done | bytes 1048592 | tf_op jit(solution)/shard_map/all_gather | solution.py:218
  29.0 0.0 copy-start
  29.0 1.6 %copy-done = bf16[4,512,512]{2,1,0:T(8,128)(2,1)S(1)} copy-done((bf16[4,512,512]{2,1,0:T(8,128)(2,1)S(1)}, bf16[4,512,512]{2,1,0:T(8,128)(2,1)}, u32[]{:S(2)}) %copy-start) | copy-done | bytes 2097176
  30.6 0.0 copy-start.2
  30.6 1.6 %copy-done.2 = bf16[4,512,512]{2,1,0:T(8,128)(2,1)S(1)} copy-done((bf16[4,512,512]{2,1,0:T(8,128)(2,1)S(1)}, bf16[4,512,512]{2,1,0:T(8,128)(2,1)}, u32[]{:S(2)}) %copy-start.2) | copy-done | bytes 2097176
  32.2 0.0 copy-start.5
  32.2 1.2 copy-done.5
  33.4 0.0 copy-start.6
  33.4 0.7 copy-done.6
  34.1 0.0 copy-start.8
  34.1 0.7 copy-done.8
  34.8 0.0 copy-start.1
  34.8 0.0 copy-start.7
  34.8 0.0 copy-start.9
  34.8 4.2 %first_sigma_terms.1 = (bf16[2,512,512]{2,1,0:T(8,128)(2,1)S(1)}, bf16[256,512]{1,0:T(8,128)(2,1)S(1)}) custom-call(s32[2,2]{1,0:T(2,128)S(1)} %copy-done.8, s32[4,8,2]{2,1,0:T(8,128)S(1)} %copy.9.pairs_ref, f32[4,8]{1,0:T(4,128)S(1)} %copy-done.6, bf16[4,512,512]{2,1,0:T(8,128)(2,1)S(1)} %copy-done, bf16[4,512,512]{2,1,0:T(8,128)(2,1)S(1)} %copy-done.2, ...), custom_call_target="tpu_custom_call" | custom-call | tf_op jit(solution)/shard_map/first_sigma_terms/pallas_call | solution.py:219
  39.0 13.7 %all_to_all.10 = bf16[4,64,512]{2,1,0:T(8,128)(2,1)S(1)} all-to-all(bf16[4,64,512]{2,1,0:T(8,128)(2,1)S(1)} %bitcast.10), channel_id=1, replica_groups=mesh['grp'=2,'ops'=4,'sec'=2,'rep'=2] {'ops'}, dimensions={0} | all-to-all | bytes 524288 | tf_op jit(solution)/shard_map/all_to_all | solution.py:213
  52.7 0.7 reduce_sum.24
  53.4 0.0 all-gather.5.cloned.1.call-update
  53.4 36.3 %all-gather.5.cloned.1.call-done = bf16[1024,512]{1,0:T(8,128)(2,1)} async-done(((bf16[64,512]{1,0:T(8,128)(2,1)}), bf16[1024,512]{1,0:T(8,128)(2,1)}) %all-gather.5.cloned.1.call-update) | async-done | bytes 1048592 | tf_op jit(solution)/shard_map/all_gather | solution.py:234
  89.7 0.0 copy-done.1
  89.7 0.0 copy-done.7
  89.7 0.0 copy-done.9
  89.7 0.0 copy-start.3
  89.7 1.6 %copy-done.3 = bf16[4,512,512]{2,1,0:T(8,128)(2,1)S(1)} copy-done((bf16[4,512,512]{2,1,0:T(8,128)(2,1)S(1)}, bf16[4,512,512]{2,1,0:T(8,128)(2,1)}, u32[]{:S(2)}) %copy-start.3) | copy-done | bytes 2097176
  91.3 0.0 copy-start.4
  91.3 1.2 copy-done.4
  92.5 5.7 %second_sigma_terms.1 = (bf16[1,256,512]{2,1,0:T(8,128)(2,1)}, bf16[256,512]{1,0:T(8,128)(2,1)S(1)}) custom-call(s32[2,2]{1,0:T(2,128)S(1)} %copy-done.9, s32[4,8,2]{2,1,0:T(8,128)S(1)} %copy.9.pairs_ref, f32[4,8]{1,0:T(4,128)S(1)} %copy-done.7, bf16[4,512,512]{2,1,0:T(8,128)(2,1)S(1)} %copy-done.1, bf16[4,512,512]{2,1,0:T(8,128)(2,1)S(1)} %copy-done.3, ...), custom_call_target="tpu_custom_call" | custom-call | tf_op jit(solution)/shard_map/second_sigma_terms/pallas_call | solution.py:235
  98.2 12.6 %all_to_all.11 = bf16[4,64,512]{2,1,0:T(8,128)(2,1)S(1)} all-to-all(bf16[4,64,512]{2,1,0:T(8,128)(2,1)S(1)} %bitcast.9), channel_id=1, replica_groups=mesh['grp'=2,'ops'=4,'sec'=2,'rep'=2] {'ops'}, dimensions={0} | all-to-all | bytes 524288 | tf_op jit(solution)/shard_map/all_to_all | solution.py:213
  110.9 14.5 %all_gather.11 = bf16[256,512]{1,0:T(8,128)(2,1)S(1)} all-gather(bf16[64,512]{1,0:T(8,128)(2,1)S(1)} %reduce_sum.25), channel_id=1, replica_groups=mesh['grp'=2,'ops'=4,'sec'=2,'rep'=2] {'ops'}, dimensions={0}, use_global_device_ids=true | all-gather | bytes 327680 | tf_op jit(solution)/shard_map/all_gather | solution.py:252
  125.3 0.9 bitcast_convert_fusion
  (1 shorter events, 0.0 us)
Async XLA Ops:
  7.2 21.8 %all-gather.3.cloned.1.call-start = ((), (), s32[]{:S(2)}) async-start(), calls=%async_computation.2 | async-start | bytes 1310720 | tf_op jit(solution)/shard_map/all_gather | solution.py:218
  7.9 81.8 %all-gather.5.cloned.1.call-start = ((), (), s32[]{:S(2)}) async-start(), calls=%async_computation.3 | async-start | bytes 1114112 | tf_op jit(solution)/shard_map/all_gather | solution.py:234
  29.0 1.6 %copy-start = (bf16[4,512,512]{2,1,0:T(8,128)(2,1)S(1)}, bf16[4,512,512]{2,1,0:T(8,128)(2,1)}, u32[]{:S(2)}) copy-start(bf16[4,512,512]{2,1,0:T(8,128)(2,1)} %left_ref.3) | copy-start | bytes 6291460
  30.6 1.6 %copy-start.2 = (bf16[4,512,512]{2,1,0:T(8,128)(2,1)S(1)}, bf16[4,512,512]{2,1,0:T(8,128)(2,1)}, u32[]{:S(2)}) copy-start(bf16[4,512,512]{2,1,0:T(8,128)(2,1)} %right_ref.3) | copy-start | bytes 6291460
  32.2 1.2 copy-start.5
  33.4 0.7 copy-start.6
  34.1 0.7 copy-start.8
  34.8 54.9 %copy-start.1 = (bf16[4,512,512]{2,1,0:T(8,128)(2,1)S(1)}, bf16[4,512,512]{2,1,0:T(8,128)(2,1)}, u32[]{:S(2)}) copy-start(bf16[4,512,512]{2,1,0:T(8,128)(2,1)} %left_ref.3) | copy-start | bytes 6291460
  34.8 54.9 %copy-start.7 = (f32[4,8]{1,0:T(4,128)S(1)}, f32[4,8]{1,0:T(4,128)}, u32[]{:S(2)}) copy-start(f32[4,8]{1,0:T(4,128)} %weights_ref.3) | copy-start | bytes 388
  34.8 54.9 %copy-start.9 = (s32[2,2]{1,0:T(2,128)S(1)}, s32[2,2]{1,0:T(2,128)}, u32[]{:S(2)}) copy-start(s32[2,2]{1,0:T(2,128)} %sizes_ref.3) | copy-start | bytes 52
  89.7 1.6 %copy-start.3 = (bf16[4,512,512]{2,1,0:T(8,128)(2,1)S(1)}, bf16[4,512,512]{2,1,0:T(8,128)(2,1)}, u32[]{:S(2)}) copy-start(bf16[4,512,512]{2,1,0:T(8,128)(2,1)} %right_ref.3) | copy-start | bytes 6291460
  91.3 1.2 copy-start.4
Sparse Core Ops, SparseCore 0:
  9.6 19.4 all-gather.2
  53.5 36.0 all-gather.4

commit v2 on v1

v2 whole, which is shorter than its diff:
```python
import jax
import jax.numpy as jnp
from jax import lax
from jax.experimental import pallas as pl
from jax.experimental.pallas import tpu as pltpu
from jax.sharding import PartitionSpec as P

epsilon = 1e-06
vmem_bytes = 24 * 1024 * 1024


def mixing_scalars(pairs_ref, weights_ref, target, terms, sectors):
    table = []
    for term in range(terms):
        row = [jnp.float32(0.0)] * sectors
        for pair in range(weights_ref.shape[1]):
            source = pairs_ref[term, pair, 0]
            hit = pairs_ref[term, pair, 1] == target
            weight = weights_ref[term, pair]
            for sector in range(sectors):
                row[sector] = row[sector] + jnp.where(
                    hit & (source == sector), weight, jnp.float32(0.0)
                )
        table.append(row)
    return table


def apply_operators(mixing, vector, left, right):
    total = None
    for term in range(left.shape[0]):
        combined = None
        for sector, weight in enumerate(mixing[term]):
            product = weight * jnp.dot(
                left[term], vector[sector], preferred_element_type=jnp.float32
            )
            combined = product if combined is None else combined + product
        part = lax.dot_general(
            combined.astype(jnp.bfloat16),
            right[term],
            (((1,), (1,)), ((), ())),
            preferred_element_type=jnp.float32,
        )
        total = part if total is None else total + part
    return total


def live_cells(sizes_ref, sector, row_start, rows, columns):
    row = row_start + lax.broadcasted_iota(jnp.int32, (rows, columns), 0)
    column = lax.broadcasted_iota(jnp.int32, (rows, columns), 1)
    return (row < sizes_ref[sector, 0]) & (column < sizes_ref[sector, 1])


def load_kernel(left_ref, right_ref, left, right, sems):
    rows = left.shape[1]
    row_start = pl.multiple_of(lax.axis_index("rep") * rows, rows)
    copies = [
        pltpu.make_async_copy(left_ref.at[:, pl.ds(row_start, rows)], left, sems.at[0]),
        pltpu.make_async_copy(right_ref, right, sems.at[1]),
    ]
    for copy in copies:
        copy.start()
    for copy in copies:
        copy.wait()


def place_pieces(pieces, spots, vector, sems):
    copies = []
    for index, (piece, (sector, row)) in enumerate(zip(pieces, spots)):
        rows = piece.shape[0]
        start = pl.multiple_of(row, rows)
        copies.append(
            pltpu.make_async_copy(piece, vector.at[sector, pl.ds(start, rows)], sems.at[index])
        )
    for copy in copies:
        copy.start()
    return copies


def give_shares(total, live, held, own_ref, send_refs):
    held[...] = jnp.where(live, total, 0.0)
    share = own_ref.shape[0]
    place = lax.axis_index("ops")
    own_ref[...] = held[pl.ds(pl.multiple_of(place * share, share), share), :]
    for step, send_ref in enumerate(send_refs, 1):
        start = pl.multiple_of((place ^ step) * share, share)
        send_ref[...] = held[pl.ds(start, share), :].astype(send_ref.dtype)


def first_kernel(counts, *refs):
    pieces_count, sends = counts
    sizes_ref, pairs_ref, weights_ref, left, right = refs[:5]
    pieces = refs[5 : 5 + pieces_count]
    masked, own_ref = refs[5 + pieces_count : 7 + pieces_count]
    send_refs = refs[7 + pieces_count : 7 + pieces_count + sends]
    held, sems = refs[7 + pieces_count + sends :]
    sectors, columns = masked.shape[0], masked.shape[2]
    rows = held.shape[0]
    target = lax.axis_index("sec")
    core = lax.axis_index("rep")
    spots = [
        (target ^ (index // 2), (core ^ (index % 2)) * rows) for index in range(pieces_count)
    ]
    copies = place_pieces([piece.at[0] for piece in pieces], spots, masked, sems)
    mixing = mixing_scalars(pairs_ref, weights_ref, target, left.shape[0], sectors)
    for copy in copies:
        copy.wait()
    step = 32

    for sector in range(sectors):

        def mask_rows(block, carry):
            start = pl.multiple_of(block * step, step)
            live = live_cells(sizes_ref, sector, start, step, columns)
            values = masked[sector, pl.ds(start, step), :].astype(jnp.float32)
            masked[sector, pl.ds(start, step), :] = jnp.where(live, values, 0.0).astype(
                jnp.bfloat16
            )
            return carry

        lax.fori_loop(0, masked.shape[1] // step, mask_rows, 0)
    total = apply_operators(mixing, masked, left, right)
    live = live_cells(sizes_ref, target, core * rows, rows, columns)
    give_shares(total, live, held, own_ref, send_refs)


def second_kernel(counts, *refs):
    pieces_count, sends = counts
    sizes_ref, pairs_ref, weights_ref, left, right, wave = refs[:6]
    pieces = refs[6 : 6 + pieces_count]
    second_ref, own_ref = refs[6 + pieces_count : 8 + pieces_count]
    send_refs = refs[8 + pieces_count : 8 + pieces_count + sends]
    sigma, held, sems, second_sem = refs[8 + pieces_count + sends :]
    sectors, columns = wave.shape[0], wave.shape[2]
    rows, share = held.shape[0], own_ref.shape[0]
    target = lax.axis_index("sec")
    core = lax.axis_index("rep")
    place = lax.axis_index("ops")
    spots = [
        (
            target ^ ((index // 2) % sectors),
            (core ^ (index % 2)) * rows + (place ^ (index // (2 * sectors))) * share,
        )
        for index in range(pieces_count)
    ]
    copies = place_pieces(pieces, spots, sigma, sems)
    mixing = mixing_scalars(pairs_ref, weights_ref, target, left.shape[0], sectors)
    live_count = jnp.float32(0.0)
    for sector in range(sectors):
        live_count = live_count + sizes_ref[sector, 0].astype(jnp.float32) * sizes_ref[
            sector, 1
        ].astype(jnp.float32)
    for copy in copies:
        copy.wait()
    step = 16
    blocks = wave.shape[1] // step
    sums = (jnp.zeros((step, columns), jnp.float32),) * 3

    for sector in range(sectors):

        def add_rows(block, carry):
            start = pl.multiple_of(block * step, step)
            w = wave[sector, pl.ds(start, step), :].astype(jnp.float32)
            s = sigma[sector, pl.ds(start, step), :].astype(jnp.float32)
            return (carry[0] + w * s, carry[1] + w * w, carry[2] + s * s)

        sums = lax.fori_loop(0, blocks, add_rows, sums)
    correlation, norm_square, sigma_square = (jnp.sum(x, keepdims=True) for x in sums)
    rayleigh = correlation / norm_square
    residual_square = (
        sigma_square - 2.0 * rayleigh * correlation + rayleigh * rayleigh * norm_square
    )
    residual_square = jnp.maximum(residual_square, 0.0)
    scale = 1.0 / jnp.sqrt(residual_square / jnp.full((1, 1), live_count) + epsilon)
    wave_scale = jnp.broadcast_to(rayleigh * scale, (step, columns))
    sigma_scale = jnp.broadcast_to(scale, (step, columns))

    for sector in range(sectors):

        def make_rows(block, carry):
            start = pl.multiple_of(block * step, step)
            w = wave[sector, pl.ds(start, step), :].astype(jnp.float32)
            s = sigma[sector, pl.ds(start, step), :].astype(jnp.float32)
            sigma[sector, pl.ds(start, step), :] = (sigma_scale * s - wave_scale * w).astype(
                jnp.bfloat16
            )
            return carry

        lax.fori_loop(0, blocks, make_rows, 0)
    second_copy = pltpu.make_async_copy(
        sigma.at[target, pl.ds(pl.multiple_of(core * rows, rows), rows)], second_ref.at[0], second_sem
    )
    second_copy.start()

    total = apply_operators(mixing, sigma, left, right)
    live = live_cells(sizes_ref, target, core * rows, rows, columns)
    give_shares(total, live, held, own_ref, send_refs)
    second_copy.wait()


def sum_kernel(own_ref, *refs):
    total = own_ref[...]
    for piece in refs[:-1]:
        total = total + piece[...].astype(jnp.float32)
    refs[-1][...] = total.astype(refs[-1].dtype)


def join_kernel(*refs):
    out_ref = refs[-1]
    share = refs[0].shape[0]
    place = lax.axis_index("ops")
    for step, piece in enumerate(refs[:-1]):
        start = pl.multiple_of((place ^ step) * share, share)
        out_ref[0, pl.ds(start, share), :] = piece[...].astype(out_ref.dtype)


def partner(value, axis, step):
    if step == 0:
        return value
    count = lax.axis_size(axis)
    return lax.ppermute(value, axis, [(i, i ^ step) for i in range(count)])


def local(wavefunction, sector_sizes, left_blocks, right_blocks, sector_pairs, pair_weights):
    sectors = sector_sizes.shape[0]
    ops_count, cores = lax.axis_size("ops"), lax.axis_size("rep")
    _, rows, columns = wavefunction.shape
    terms, side = left_blocks.shape[0], left_blocks.shape[1]
    share = rows // ops_count
    bf16, f32 = jnp.bfloat16, jnp.float32
    smem = pl.BlockSpec(memory_space=pltpu.SMEM)
    anywhere = pl.BlockSpec(memory_space=pl.ANY)
    inside = pl.BlockSpec(memory_space=pltpu.VMEM)
    full = jax.ShapeDtypeStruct((sectors, side, columns), bf16)
    shares = [jax.ShapeDtypeStruct((share, columns), f32)] + [
        jax.ShapeDtypeStruct((share, columns), bf16)
    ] * (ops_count - 1)
    params = pltpu.CompilerParams(vmem_limit_bytes=vmem_bytes)

    left_rows, right = pl.pallas_call(
        load_kernel,
        out_shape=(
            jax.ShapeDtypeStruct((terms, rows, side), bf16),
            jax.ShapeDtypeStruct(right_blocks.shape, bf16),
        ),
        in_specs=[anywhere] * 2,
        out_specs=(inside, inside),
        scratch_shapes=[pltpu.SemaphoreType.DMA((2,))],
        compiler_params=params,
        name="load_operators",
    )(left_blocks, right_blocks)
    operators = (sector_sizes, sector_pairs, pair_weights, left_rows, right)
    operator_specs = [smem] * 3 + [inside] * 2

    def summed(own, *sends):
        received = [partner(send, "ops", step) for step, send in enumerate(sends, 1)]
        return pl.pallas_call(
            sum_kernel,
            out_shape=jax.ShapeDtypeStruct((share, columns), bf16),
            in_specs=[inside] * ops_count,
            out_specs=inside,
            compiler_params=params,
            name="sum_over_terms",
        )(own, *received)

    pieces = []
    for sector in range(sectors):
        piece = partner(wavefunction, "sec", sector)
        pieces += [partner(piece, "rep", core) for core in range(cores)]
    masked, *first_shares = pl.pallas_call(
        lambda *refs: first_kernel((len(pieces), ops_count - 1), *refs),
        out_shape=[full] + shares,
        in_specs=operator_specs + [anywhere] * len(pieces),
        out_specs=[inside] * (1 + ops_count),
        scratch_shapes=[
            pltpu.VMEM((rows, columns), f32),
            pltpu.SemaphoreType.DMA((len(pieces),)),
        ],
        compiler_params=params,
        name="first_sigma_terms",
    )(*operators, *pieces)
    first_sum = summed(*first_shares)
    pieces = []
    for step in range(ops_count):
        along_ops = partner(first_sum, "ops", step)
        for sector in range(sectors):
            piece = partner(along_ops, "sec", sector)
            pieces += [partner(piece, "rep", core) for core in range(cores)]
    second_wave, *second_shares = pl.pallas_call(
        lambda *refs: second_kernel((len(pieces), ops_count - 1), *refs),
        out_shape=[jax.ShapeDtypeStruct((1, rows, columns), bf16)] + shares,
        in_specs=operator_specs + [inside] + [anywhere] * len(pieces),
        out_specs=[anywhere] + [inside] * ops_count,
        scratch_shapes=[
            pltpu.VMEM((sectors, side, columns), bf16),
            pltpu.VMEM((rows, columns), f32),
            pltpu.SemaphoreType.DMA((len(pieces),)),
            pltpu.SemaphoreType.DMA,
        ],
        compiler_params=params,
        name="second_sigma_terms",
    )(*operators, masked, *pieces)
    second_sum = summed(*second_shares)
    second_sigma = pl.pallas_call(
        join_kernel,
        out_shape=jax.ShapeDtypeStruct((1, rows, columns), f32),
        in_specs=[inside] * ops_count,
        out_specs=inside,
        compiler_params=params,
        name="join_second_sigma",
    )(*[partner(second_sum, "ops", step) for step in range(ops_count)])
    return (second_wave, second_sigma)


def solution(mesh):
    return jax.shard_map(
        local,
        mesh=mesh,
        in_specs=(
            P(("grp", "sec"), "rep", None),
            P("grp", None),
            P(("grp", "ops"), None, None),
            P(("grp", "ops"), None, None),
            P(("grp", "ops"), None, None),
            P(("grp", "ops"), None),
        ),
        out_specs=(P(("grp", "sec"), "rep", None), P(("grp", "sec"), "rep", None)),
        check_vma=False,
    )
```

time: 133 us -> 71.1 us (0.53)
  blocking collectives: 40.7 us -> 0 us
  waiting for transfers between devices: 57.2 us -> 26.4 us
  starting transfers between devices: 0.08 us -> 27.1 us
  between operations: 14.1 us -> 0.73 us
  local copies, waits for them, and re-layouts: 9.37 us -> 4.65 us
  Pallas kernels: 9.97 us -> 12 us
  other arithmetic: 1.56 us -> 0 us
    all_gather x2 -> x0, waiting for transfers between devices: 56.5 us -> none  [the longest x1 36.3 us: local(): lax.all_gather(summed(first_part), ('sec', 'rep', 'ops'), axis=0, tiled=T...]
    ppermute x0 -> x27, starting transfers between devices: none -> 27.1 us  [partner(): return lax.ppermute(value, axis, [(i, i ^ step) for i in range(count)])]
    ppermute x0 -> x27, waiting for transfers between devices: none -> 26.4 us  [partner(): return lax.ppermute(value, axis, [(i, i ^ step) for i in range(count)])]
    all_to_all x2 -> x0, blocking collectives: 26.3 us -> none  [summed(): lax.all_to_all(piece.reshape(ops_count, share, columns), 'ops', 0, 0, til...]
    all_gather x1 -> x0, blocking collectives: 14.5 us -> none  [local(): lax.all_gather(summed(second_part), 'ops', axis=0, tiled=True)]
    unnamed x21 -> x11, local copies, waits for them, and re-layouts: 9.37 us -> 4.65 us
    pallas_call x2 -> x6, Pallas kernels: 9.97 us -> 12 us  [the longest x1 7.23 us: local(): pl.pallas_call(lambda *refs: second_kernel((len(pieces), ops_count - 1),...]
  transfers between devices with their start and end apart: 2 -> 27, of which waited for: 2 -> 12; matrix products, arithmetic and copies ran while one was open for 1% -> 1% of each run, Pallas kernels for 0% -> 0%
where the time goes in v2:
time: 71.1 us; the launch traced here: 70.9 us
  starting transfers between devices  27.1 us (38%)
  waiting for transfers between devices  26.4 us (37%)
  Pallas kernels  12 us (17%)
  local copies, waits for them, and re-layouts  4.65 us (7%)
  between operations  0.73 us (1%)
    ppermute x27, starting transfers between devices, partner(): return lax.ppermute(value, axis, [(i, i ^ step) for i in range(count)])  27.1 us
    ppermute x27, waiting for transfers between devices, partner(): return lax.ppermute(value, axis, [(i, i ^ step) for i in range(count)])  26.4 us
    pallas_call x1, Pallas kernels, local(): pl.pallas_call(lambda *refs: second_kernel((len(pieces), ops_count - 1),...  7.23 us
    unnamed x11, local copies, waits for them, and re-layouts  4.65 us
    pallas_call x1, Pallas kernels, local(): pl.pallas_call(lambda *refs: first_kernel((len(pieces), ops_count - 1), *...  3.63 us
  transfers between devices with their start and end apart: 27, of which 12 were waited for; matrix products, arithmetic and copies ran while one was open for 1% of the time, Pallas kernels for 0%

profile of v2, /device:TPU:0, one launch (start us, length us, event | category | flops | bytes accessed | tf_op | source)
XLA Modules:
  0.0 70.9 jit_solution(7476617256396201001)
XLA Ops:
  0.6 3.0 %collective-permute-start.1 = (bf16[1,256,512]{2,1,0:T(8,128)(2,1)}, bf16[1,256,512]{2,1,0:T(8,128)(2,1)S(1)}, u32[]{:S(2)}, u32[]{:S(2)}) collective-permute-start(bf16[1,256,512]{2,1,0:T(8,128)(2,1)} %refs_5_.1), channel_id=1, source_target_pairs={{0,2},{2,0},{1,3},{3,1},{4,6},{6,4},{5,7},{7,5},{8,10},{10,8},{9,1... | collective-permute-start | bytes 786440 | tf_op jit(solution)/shard_map/ppermute | solution.py:220
  3.6 0.0 collective-permute-start
  3.6 6.5 %collective-permute-done.1.refs_7_ = bf16[1,256,512]{2,1,0:T(8,128)(2,1)S(1)} collective-permute-done((bf16[1,256,512]{2,1,0:T(8,128)(2,1)}, bf16[1,256,512]{2,1,0:T(8,128)(2,1)S(1)}, u32[]{:S(2)}, u32[]{:S(2)}) %collective-permute-start.1) | collective-permute-done | bytes 262176 | tf_op jit(solution)/shard_map/ppermute | solution.py:220
  10.2 0.0 collective-permute-start.2
  10.2 0.8 %copy.9.refs_1_ = s32[4,8,2]{2,1,0:T(8,128)S(1)} copy(s32[4,8,2]{1,2,0:T(2,128)} %param.10) | data formatting | bytes 512 | tf_op args[4]
  10.9 1.6 %copy-done = bf16[4,512,512]{2,1,0:T(8,128)(2,1)S(1)} copy-done((bf16[4,512,512]{2,1,0:T(8,128)(2,1)S(1)}, bf16[4,512,512]{2,1,0:T(8,128)(2,1)}, u32[]{:S(2)}) %copy-start) | copy-done | bytes 2097176
  12.5 1.6 %copy-done.1 = bf16[4,512,512]{2,1,0:T(8,128)(2,1)S(1)} copy-done((bf16[4,512,512]{2,1,0:T(8,128)(2,1)S(1)}, bf16[4,512,512]{2,1,0:T(8,128)(2,1)}, u32[]{:S(2)}) %copy-start.1) | copy-done | bytes 2097176
  14.1 0.2 load_operators.1
  14.4 0.0 collective-permute-done.refs_6_
  14.4 0.0 collective-permute-done.2.refs_8_
  14.4 0.7 copy-done.2
  15.1 0.0 copy-done.3
  15.1 0.0 copy-done.4
  15.1 3.6 %first_sigma_terms.1 = (bf16[2,512,512]{2,1,0:T(8,128)(2,1)S(1)}, f32[64,512]{1,0:T(8,128)S(1)}, bf16[64,512]{1,0:T(8,128)(2,1)S(1)}, bf16[64,512]{1,0:T(8,128)(2,1)S(1)}, bf16[64,512]{1,0:T(8,128)(2,1)S(1)}) custom-call(s32[2,2]{1,0:T(2,128)S(1)} %copy-done.4, s32[4,8,2]{2,1,0:T(8,128)S(1)} %copy.9.refs_1_, f32[4,8]{1,0:T(4,128)S(1)} %copy-done.3, ...), custom_call_target="tpu_custom_call" | custom-call | tf_op jit(solution)/shard_map/first_sigma_terms/pallas_call | solution.py:269
  18.7 1.9 %collective-permute-start.3 = (bf16[64,512]{1,0:T(8,128)(2,1)S(1)}, bf16[64,512]{1,0:T(8,128)(2,1)S(1)}, u32[]{:S(2)}, u32[]{:S(2)}) collective-permute-start(bf16[64,512]{1,0:T(8,128)(2,1)S(1)} %get-tuple-element.18), channel_id=1, source_target_pairs={{0,4},{4,0},{8,12},{12,8},{1,5},{5,1},{9,13},{13,9},{2,6},{6,2},{1... | collective-permute-start | bytes 196616 | tf_op jit(solution)/shard_map/ppermute | solution.py:220
  20.6 2.6 %collective-permute-start.4 = (bf16[64,512]{1,0:T(8,128)(2,1)S(1)}, bf16[64,512]{1,0:T(8,128)(2,1)S(1)}, u32[]{:S(2)}, u32[]{:S(2)}) collective-permute-start(bf16[64,512]{1,0:T(8,128)(2,1)S(1)} %get-tuple-element.19), channel_id=1, source_target_pairs={{0,8},{4,12},{8,0},{12,4},{1,9},{5,13},{9,1},{13,5},{2,10},{6,14},... | collective-permute-start | bytes 196616 | tf_op jit(solution)/shard_map/ppermute | solution.py:220
  23.2 0.0 collective-permute-start.5
  23.2 0.2 collective-permute-done.3.refs_0_
  23.4 4.2 %collective-permute-done.4.refs_1_ = bf16[64,512]{1,0:T(8,128)(2,1)S(1)} collective-permute-done((bf16[64,512]{1,0:T(8,128)(2,1)S(1)}, bf16[64,512]{1,0:T(8,128)(2,1)S(1)}, u32[]{:S(2)}, u32[]{:S(2)}) %collective-permute-start.4) | collective-permute-done | bytes 65568 | tf_op jit(solution)/shard_map/ppermute | solution.py:220
  27.5 1.8 %collective-permute-done.5.refs_2_ = bf16[64,512]{1,0:T(8,128)(2,1)S(1)} collective-permute-done((bf16[64,512]{1,0:T(8,128)(2,1)S(1)}, bf16[64,512]{1,0:T(8,128)(2,1)S(1)}, u32[]{:S(2)}, u32[]{:S(2)}) %collective-permute-start.5) | collective-permute-done | bytes 65568 | tf_op jit(solution)/shard_map/ppermute | solution.py:220
  29.4 2.5 %collective-permute-start.17 = (bf16[64,512]{1,0:T(8,128)(2,1)S(1)}, bf16[64,512]{1,0:T(8,128)(2,1)S(1)}, u32[]{:S(2)}, u32[]{:S(2)}) collective-permute-start(bf16[64,512]{1,0:T(8,128)(2,1)S(1)} %sum_over_terms.2.refs_6_), channel_id=1, source_target_pairs={{0,12},{4,8},{8,4},{12,0},{1,13},{5,9},{9,5},{13,1},{2,14},{6,10},... | collective-permute-start | bytes 196616 | tf_op jit(solution)/shard_map/ppermute | solution.py:220
  31.8 0.3 collective-permute-start.13
  32.1 1.7 %collective-permute-start.9 = (bf16[64,512]{1,0:T(8,128)(2,1)S(1)}, bf16[64,512]{1,0:T(8,128)(2,1)S(1)}, u32[]{:S(2)}, u32[]{:S(2)}) collective-permute-start(bf16[64,512]{1,0:T(8,128)(2,1)S(1)} %sum_over_terms.2.refs_6_), channel_id=1, source_target_pairs={{0,4},{4,0},{8,12},{12,8},{1,5},{5,1},{9,13},{13,9},{2,6},{6,2},{1... | collective-permute-start | bytes 196616 | tf_op jit(solution)/shard_map/ppermute | solution.py:220
  33.8 1.5 %collective-permute-start.7 = (bf16[64,512]{1,0:T(8,128)(2,1)S(1)}, bf16[64,512]{1,0:T(8,128)(2,1)S(1)}, u32[]{:S(2)}, u32[]{:S(2)}) collective-permute-start(bf16[64,512]{1,0:T(8,128)(2,1)S(1)} %sum_over_terms.2.refs_6_), channel_id=1, source_target_pairs={{0,2},{2,0},{1,3},{3,1},{4,6},{6,4},{5,7},{7,5},{8,10},{10,8},{9,1... | collective-permute-start | bytes 196616 | tf_op jit(solution)/shard_map/ppermute | solution.py:220
  35.3 0.0 collective-permute-start.6
  35.3 0.8 %collective-permute-done.17.refs_18_ = bf16[64,512]{1,0:T(8,128)(2,1)S(1)} collective-permute-done((bf16[64,512]{1,0:T(8,128)(2,1)S(1)}, bf16[64,512]{1,0:T(8,128)(2,1)S(1)}, u32[]{:S(2)}, u32[]{:S(2)}) %collective-permute-start.17) | collective-permute-done | bytes 65568 | tf_op jit(solution)/shard_map/ppermute | solution.py:220
  36.1 1.5 %collective-permute-start.19 = (bf16[64,512]{1,0:T(8,128)(2,1)S(1)}, bf16[64,512]{1,0:T(8,128)(2,1)S(1)}, u32[]{:S(2)}, u32[]{:S(2)}) collective-permute-start(bf16[64,512]{1,0:T(8,128)(2,1)S(1)} %collective-permute-done.17.refs_18_), channel_id=1, source_target_pairs={{0,2},{2,0},{1,3},{3,1},{4,6},{6,4},{5,7},{7,5},{8,10},{10,8},{9,1... | collective-permute-start | bytes 196616 | tf_op jit(solution)/shard_map/ppermute | solution.py:220
  37.6 0.4 collective-permute-done.13.refs_14_
  38.0 0.0 collective-permute-start.18
  38.0 0.0 collective-permute-done.9.refs_10_
  38.0 1.5 %collective-permute-start.15 = (bf16[64,512]{1,0:T(8,128)(2,1)S(1)}, bf16[64,512]{1,0:T(8,128)(2,1)S(1)}, u32[]{:S(2)}, u32[]{:S(2)}) collective-permute-start(bf16[64,512]{1,0:T(8,128)(2,1)S(1)} %collective-permute-done.13.refs_14_), channel_id=1, source_target_pairs={{0,2},{2,0},{1,3},{3,1},{4,6},{6,4},{5,7},{7,5},{8,10},{10,8},{9,1... | collective-permute-start | bytes 196616 | tf_op jit(solution)/shard_map/ppermute | solution.py:220
  39.5 0.0 collective-permute-done.7.refs_8_
  39.5 0.2 collective-permute-start.14
  39.8 0.0 collective-permute-done.6.refs_7_
  39.8 0.5 collective-permute-start.11
  40.3 0.0 collective-permute-done.19.refs_20_
  40.3 0.1 collective-permute-start.10
  40.5 0.0 collective-permute-done.18.refs_19_
  40.5 0.4 collective-permute-start.8
  40.8 1.7 %collective-permute-done.15.refs_16_ = bf16[64,512]{1,0:T(8,128)(2,1)S(1)} collective-permute-done((bf16[64,512]{1,0:T(8,128)(2,1)S(1)}, bf16[64,512]{1,0:T(8,128)(2,1)S(1)}, u32[]{:S(2)}, u32[]{:S(2)}) %collective-permute-start.15) | collective-permute-done | bytes 65568 | tf_op jit(solution)/shard_map/ppermute | solution.py:220
  42.5 0.0 collective-permute-start.20
  42.6 0.0 collective-permute-done.14.refs_15_
  42.6 0.5 collective-permute-start.16
  43.1 1.0 %collective-permute-done.11.refs_12_ = bf16[64,512]{1,0:T(8,128)(2,1)S(1)} collective-permute-done((bf16[64,512]{1,0:T(8,128)(2,1)S(1)}, bf16[64,512]{1,0:T(8,128)(2,1)S(1)}, u32[]{:S(2)}, u32[]{:S(2)}) %collective-permute-start.11) | collective-permute-done | bytes 65568 | tf_op jit(solution)/shard_map/ppermute | solution.py:220
  44.0 0.0 collective-permute-start.12
  44.0 0.0 collective-permute-done.10.refs_11_
  44.0 0.0 collective-permute-done.8.refs_9_
  44.1 0.0 collective-permute-done.20.refs_21_
  44.1 0.0 collective-permute-done.16.refs_17_
  44.1 1.2 %collective-permute-done.12.refs_13_ = bf16[64,512]{1,0:T(8,128)(2,1)S(1)} collective-permute-done((bf16[64,512]{1,0:T(8,128)(2,1)S(1)}, bf16[64,512]{1,0:T(8,128)(2,1)S(1)}, u32[]{:S(2)}, u32[]{:S(2)}) %collective-permute-start.12) | collective-permute-done | bytes 65568 | tf_op jit(solution)/shard_map/ppermute | solution.py:220
  45.3 7.2 %second_sigma_terms.1 = (bf16[1,256,512]{2,1,0:T(8,128)(2,1)}, f32[64,512]{1,0:T(8,128)S(1)}, bf16[64,512]{1,0:T(8,128)(2,1)S(1)}, bf16[64,512]{1,0:T(8,128)(2,1)S(1)}, bf16[64,512]{1,0:T(8,128)(2,1)S(1)}) custom-call(s32[2,2]{1,0:T(2,128)S(1)} %copy-done.4, s32[4,8,2]{2,1,0:T(8,128)S(1)} %copy.9.refs_1_, f32[4,8]{1,0:T(4,128)S(1)} %copy-done.3, ...), custom_call_target="tpu_custom_call" | custom-call | tf_op jit(solution)/shard_map/second_sigma_terms/pallas_call | solution.py:288
  52.5 1.2 %collective-permute-start.21 = (bf16[64,512]{1,0:T(8,128)(2,1)S(1)}, bf16[64,512]{1,0:T(8,128)(2,1)S(1)}, u32[]{:S(2)}, u32[]{:S(2)}) collective-permute-start(bf16[64,512]{1,0:T(8,128)(2,1)S(1)} %get-tuple-element.23), channel_id=1, source_target_pairs={{0,4},{4,0},{8,12},{12,8},{1,5},{5,1},{9,13},{13,9},{2,6},{6,2},{1... | collective-permute-start | bytes 196616 | tf_op jit(solution)/shard_map/ppermute | solution.py:220
  53.7 1.2 %collective-permute-start.22 = (bf16[64,512]{1,0:T(8,128)(2,1)S(1)}, bf16[64,512]{1,0:T(8,128)(2,1)S(1)}, u32[]{:S(2)}, u32[]{:S(2)}) collective-permute-start(bf16[64,512]{1,0:T(8,128)(2,1)S(1)} %get-tuple-element.24), channel_id=1, source_target_pairs={{0,8},{4,12},{8,0},{12,4},{1,9},{5,13},{9,1},{13,5},{2,10},{6,14},... | collective-permute-start | bytes 196616 | tf_op jit(solution)/shard_map/ppermute | solution.py:220
  55.0 2.0 %collective-permute-start.23 = (bf16[64,512]{1,0:T(8,128)(2,1)S(1)}, bf16[64,512]{1,0:T(8,128)(2,1)S(1)}, u32[]{:S(2)}, u32[]{:S(2)}) collective-permute-start(bf16[64,512]{1,0:T(8,128)(2,1)S(1)} %get-tuple-element.25), channel_id=1, source_target_pairs={{0,12},{4,8},{8,4},{12,0},{1,13},{5,9},{9,5},{13,1},{2,14},{6,10},... | collective-permute-start | bytes 196616 | tf_op jit(solution)/shard_map/ppermute | solution.py:220
  57.0 0.0 collective-permute-done.21.refs_0_
  57.0 5.0 %collective-permute-done.22.refs_1_ = bf16[64,512]{1,0:T(8,128)(2,1)S(1)} collective-permute-done((bf16[64,512]{1,0:T(8,128)(2,1)S(1)}, bf16[64,512]{1,0:T(8,128)(2,1)S(1)}, u32[]{:S(2)}, u32[]{:S(2)}) %collective-permute-start.22) | collective-permute-done | bytes 65568 | tf_op jit(solution)/shard_map/ppermute | solution.py:220
  62.0 0.0 collective-permute-done.23.refs_2_
  62.0 2.0 %collective-permute-start.26 = (bf16[64,512]{1,0:T(8,128)(2,1)S(1)}, bf16[64,512]{1,0:T(8,128)(2,1)S(1)}, u32[]{:S(2)}, u32[]{:S(2)}) collective-permute-start(bf16[64,512]{1,0:T(8,128)(2,1)S(1)} %sum_over_terms.3.refs_0_), channel_id=1, source_target_pairs={{0,12},{4,8},{8,4},{12,0},{1,13},{5,9},{9,5},{13,1},{2,14},{6,10},... | collective-permute-start | bytes 196616 | tf_op jit(solution)/shard_map/ppermute | solution.py:220
  64.0 0.8 %collective-permute-start.25 = (bf16[64,512]{1,0:T(8,128)(2,1)S(1)}, bf16[64,512]{1,0:T(8,128)(2,1)S(1)}, u32[]{:S(2)}, u32[]{:S(2)}) collective-permute-start(bf16[64,512]{1,0:T(8,128)(2,1)S(1)} %sum_over_terms.3.refs_0_), channel_id=1, source_target_pairs={{0,8},{4,12},{8,0},{12,4},{1,9},{5,13},{9,1},{13,5},{2,10},{6,14},... | collective-permute-start | bytes 196616 | tf_op jit(solution)/shard_map/ppermute | solution.py:220
  64.8 1.7 %collective-permute-start.24 = (bf16[64,512]{1,0:T(8,128)(2,1)S(1)}, bf16[64,512]{1,0:T(8,128)(2,1)S(1)}, u32[]{:S(2)}, u32[]{:S(2)}) collective-permute-start(bf16[64,512]{1,0:T(8,128)(2,1)S(1)} %sum_over_terms.3.refs_0_), channel_id=1, source_target_pairs={{0,4},{4,0},{8,12},{12,8},{1,5},{5,1},{9,13},{13,9},{2,6},{6,2},{1... | collective-permute-start | bytes 196616 | tf_op jit(solution)/shard_map/ppermute | solution.py:220
  66.5 2.2 %collective-permute-done.26.refs_3_ = bf16[64,512]{1,0:T(8,128)(2,1)S(1)} collective-permute-done((bf16[64,512]{1,0:T(8,128)(2,1)S(1)}, bf16[64,512]{1,0:T(8,128)(2,1)S(1)}, u32[]{:S(2)}, u32[]{:S(2)}) %collective-permute-start.26) | collective-permute-done | bytes 65568 | tf_op jit(solution)/shard_map/ppermute | solution.py:220
  68.7 1.4 %collective-permute-done.25.refs_2_ = bf16[64,512]{1,0:T(8,128)(2,1)S(1)} collective-permute-done((bf16[64,512]{1,0:T(8,128)(2,1)S(1)}, bf16[64,512]{1,0:T(8,128)(2,1)S(1)}, u32[]{:S(2)}, u32[]{:S(2)}) %collective-permute-start.25) | collective-permute-done | bytes 65568 | tf_op jit(solution)/shard_map/ppermute | solution.py:220
  70.0 0.0 collective-permute-done.24.refs_1_
  70.0 0.8 %join_second_sigma.1 = f32[1,256,512]{2,1,0:T(8,128)} custom-call(bf16[64,512]{1,0:T(8,128)(2,1)S(1)} %sum_over_terms.3.refs_0_, bf16[64,512]{1,0:T(8,128)(2,1)S(1)} %collective-permute-done.24.refs_1_, bf16[64,512]{1,0:T(8,128)(2,1)S(1)} %collective-permute-done.25.refs_2_, bf16[64,512]{1,0:T(8,128)(2,1)S(1)} %collective-permute-done.26.refs_3_), custom_call_target="tpu_custom_call" | custom-call | tf_op jit(solution)/shard_map/join_second_sigma/pallas_call | solution.py:303
  (7 shorter events, 0.1 us)
Async XLA Ops:
  0.6 9.5 %collective-permute-start.1 = (bf16[1,256,512]{2,1,0:T(8,128)(2,1)}, bf16[1,256,512]{2,1,0:T(8,128)(2,1)S(1)}, u32[]{:S(2)}, u32[]{:S(2)}) collective-permute-start(bf16[1,256,512]{2,1,0:T(8,128)(2,1)} %refs_5_.1), channel_id=1, source_target_pairs={{0,2},{2,0},{1,3},{3,1},{4,6},{6,4},{5,7},{7,5},{8,10},{10,8},{9,1... | collective-permute-start | bytes 786440 | tf_op jit(solution)/shard_map/ppermute | solution.py:220
  3.6 10.7 %collective-permute-start = (bf16[1,256,512]{2,1,0:T(8,128)(2,1)}, bf16[1,256,512]{2,1,0:T(8,128)(2,1)S(1)}, u32[]{:S(2)}, u32[]{:S(2)}) collective-permute-start(bf16[1,256,512]{2,1,0:T(8,128)(2,1)} %refs_5_.1), channel_id=1, source_target_pairs={{0,1},{1,0},{2,3},{3,2},{4,5},{5,4},{6,7},{7,6},{8,9},{9,8},{10,11... | collective-permute-start | bytes 786440 | tf_op jit(solution)/shard_map/ppermute | solution.py:220
  10.2 4.2 %collective-permute-start.2 = (bf16[1,256,512]{2,1,0:T(8,128)(2,1)S(1)}, bf16[1,256,512]{2,1,0:T(8,128)(2,1)S(1)}, u32[]{:S(2)}, u32[]{:S(2)}) collective-permute-start(bf16[1,256,512]{2,1,0:T(8,128)(2,1)S(1)} %collective-permute-done.1.refs_7_), channel_id=1, source_target_pairs={{0,1},{1,0},{2,3},{3,2},{4,5},{5,4},{6,7},{7,6},{8,9},{9,8},{10,11... | collective-permute-start | bytes 786440 | tf_op jit(solution)/shard_map/ppermute | solution.py:220
  10.9 1.6 %copy-start = (bf16[4,512,512]{2,1,0:T(8,128)(2,1)S(1)}, bf16[4,512,512]{2,1,0:T(8,128)(2,1)}, u32[]{:S(2)}) copy-start(bf16[4,512,512]{2,1,0:T(8,128)(2,1)} %left_ref.1) | copy-start | bytes 6291460
  12.5 1.6 %copy-start.1 = (bf16[4,512,512]{2,1,0:T(8,128)(2,1)S(1)}, bf16[4,512,512]{2,1,0:T(8,128)(2,1)}, u32[]{:S(2)}) copy-start(bf16[4,512,512]{2,1,0:T(8,128)(2,1)} %right_ref.1) | copy-start | bytes 6291460
  14.1 0.9 %copy-start.2 = (bf16[1,256,512]{2,1,0:T(8,128)(2,1)S(1)}, bf16[1,256,512]{2,1,0:T(8,128)(2,1)}, u32[]{:S(2)}) copy-start(bf16[1,256,512]{2,1,0:T(8,128)(2,1)} %refs_5_.1) | copy-start | bytes 786436
  14.1 1.0 %copy-start.3 = (f32[4,8]{1,0:T(4,128)S(1)}, f32[4,8]{1,0:T(4,128)}, u32[]{:S(2)}) copy-start(f32[4,8]{1,0:T(4,128)} %refs_2_.3) | copy-start | bytes 388
  14.1 1.0 %copy-start.4 = (s32[2,2]{1,0:T(2,128)S(1)}, s32[2,2]{1,0:T(2,128)}, u32[]{:S(2)}) copy-start(s32[2,2]{1,0:T(2,128)} %refs_0_.3) | copy-start | bytes 52
  18.7 4.7 %collective-permute-start.3 = (bf16[64,512]{1,0:T(8,128)(2,1)S(1)}, bf16[64,512]{1,0:T(8,128)(2,1)S(1)}, u32[]{:S(2)}, u32[]{:S(2)}) collective-permute-start(bf16[64,512]{1,0:T(8,128)(2,1)S(1)} %get-tuple-element.18), channel_id=1, source_target_pairs={{0,4},{4,0},{8,12},{12,8},{1,5},{5,1},{9,13},{13,9},{2,6},{6,2},{1... | collective-permute-start | bytes 196616 | tf_op jit(solution)/shard_map/ppermute | solution.py:220
  20.6 6.9 %collective-permute-start.4 = (bf16[64,512]{1,0:T(8,128)(2,1)S(1)}, bf16[64,512]{1,0:T(8,128)(2,1)S(1)}, u32[]{:S(2)}, u32[]{:S(2)}) collective-permute-start(bf16[64,512]{1,0:T(8,128)(2,1)S(1)} %get-tuple-element.19), channel_id=1, source_target_pairs={{0,8},{4,12},{8,0},{12,4},{1,9},{5,13},{9,1},{13,5},{2,10},{6,14},... | collective-permute-start | bytes 196616 | tf_op jit(solution)/shard_map/ppermute | solution.py:220
  23.2 6.1 %collective-permute-start.5 = (bf16[64,512]{1,0:T(8,128)(2,1)S(1)}, bf16[64,512]{1,0:T(8,128)(2,1)S(1)}, u32[]{:S(2)}, u32[]{:S(2)}) collective-permute-start(bf16[64,512]{1,0:T(8,128)(2,1)S(1)} %get-tuple-element.20), channel_id=1, source_target_pairs={{0,12},{4,8},{8,4},{12,0},{1,13},{5,9},{9,5},{13,1},{2,14},{6,10},... | collective-permute-start | bytes 196616 | tf_op jit(solution)/shard_map/ppermute | solution.py:220
  29.4 6.7 %collective-permute-start.17 = (bf16[64,512]{1,0:T(8,128)(2,1)S(1)}, bf16[64,512]{1,0:T(8,128)(2,1)S(1)}, u32[]{:S(2)}, u32[]{:S(2)}) collective-permute-start(bf16[64,512]{1,0:T(8,128)(2,1)S(1)} %sum_over_terms.2.refs_6_), channel_id=1, source_target_pairs={{0,12},{4,8},{8,4},{12,0},{1,13},{5,9},{9,5},{13,1},{2,14},{6,10},... | collective-permute-start | bytes 196616 | tf_op jit(solution)/shard_map/ppermute | solution.py:220
  31.8 6.2 %collective-permute-start.13 = (bf16[64,512]{1,0:T(8,128)(2,1)S(1)}, bf16[64,512]{1,0:T(8,128)(2,1)S(1)}, u32[]{:S(2)}, u32[]{:S(2)}) collective-permute-start(bf16[64,512]{1,0:T(8,128)(2,1)S(1)} %sum_over_terms.2.refs_6_), channel_id=1, source_target_pairs={{0,8},{4,12},{8,0},{12,4},{1,9},{5,13},{9,1},{13,5},{2,10},{6,14},... | collective-permute-start | bytes 196616 | tf_op jit(solution)/shard_map/ppermute | solution.py:220
  32.1 5.9 %collective-permute-start.9 = (bf16[64,512]{1,0:T(8,128)(2,1)S(1)}, bf16[64,512]{1,0:T(8,128)(2,1)S(1)}, u32[]{:S(2)}, u32[]{:S(2)}) collective-permute-start(bf16[64,512]{1,0:T(8,128)(2,1)S(1)} %sum_over_terms.2.refs_6_), channel_id=1, source_target_pairs={{0,4},{4,0},{8,12},{12,8},{1,5},{5,1},{9,13},{13,9},{2,6},{6,2},{1... | collective-permute-start | bytes 196616 | tf_op jit(solution)/shard_map/ppermute | solution.py:220
  33.8 5.7 %collective-permute-start.7 = (bf16[64,512]{1,0:T(8,128)(2,1)S(1)}, bf16[64,512]{1,0:T(8,128)(2,1)S(1)}, u32[]{:S(2)}, u32[]{:S(2)}) collective-permute-start(bf16[64,512]{1,0:T(8,128)(2,1)S(1)} %sum_over_terms.2.refs_6_), channel_id=1, source_target_pairs={{0,2},{2,0},{1,3},{3,1},{4,6},{6,4},{5,7},{7,5},{8,10},{10,8},{9,1... | collective-permute-start | bytes 196616 | tf_op jit(solution)/shard_map/ppermute | solution.py:220
  35.3 4.5 %collective-permute-start.6 = (bf16[64,512]{1,0:T(8,128)(2,1)S(1)}, bf16[64,512]{1,0:T(8,128)(2,1)S(1)}, u32[]{:S(2)}, u32[]{:S(2)}) collective-permute-start(bf16[64,512]{1,0:T(8,128)(2,1)S(1)} %sum_over_terms.2.refs_6_), channel_id=1, source_target_pairs={{0,1},{1,0},{2,3},{3,2},{4,5},{5,4},{6,7},{7,6},{8,9},{9,8},{10,11... | collective-permute-start | bytes 196616 | tf_op jit(solution)/shard_map/ppermute | solution.py:220
  36.1 4.3 %collective-permute-start.19 = (bf16[64,512]{1,0:T(8,128)(2,1)S(1)}, bf16[64,512]{1,0:T(8,128)(2,1)S(1)}, u32[]{:S(2)}, u32[]{:S(2)}) collective-permute-start(bf16[64,512]{1,0:T(8,128)(2,1)S(1)} %collective-permute-done.17.refs_18_), channel_id=1, source_target_pairs={{0,2},{2,0},{1,3},{3,1},{4,6},{6,4},{5,7},{7,5},{8,10},{10,8},{9,1... | collective-permute-start | bytes 196616 | tf_op jit(solution)/shard_map/ppermute | solution.py:220
  38.0 2.4 %collective-permute-start.18 = (bf16[64,512]{1,0:T(8,128)(2,1)S(1)}, bf16[64,512]{1,0:T(8,128)(2,1)S(1)}, u32[]{:S(2)}, u32[]{:S(2)}) collective-permute-start(bf16[64,512]{1,0:T(8,128)(2,1)S(1)} %collective-permute-done.17.refs_18_), channel_id=1, source_target_pairs={{0,1},{1,0},{2,3},{3,2},{4,5},{5,4},{6,7},{7,6},{8,9},{9,8},{10,11... | collective-permute-start | bytes 196616 | tf_op jit(solution)/shard_map/ppermute | solution.py:220
  38.0 4.5 %collective-permute-start.15 = (bf16[64,512]{1,0:T(8,128)(2,1)S(1)}, bf16[64,512]{1,0:T(8,128)(2,1)S(1)}, u32[]{:S(2)}, u32[]{:S(2)}) collective-permute-start(bf16[64,512]{1,0:T(8,128)(2,1)S(1)} %collective-permute-done.13.refs_14_), channel_id=1, source_target_pairs={{0,2},{2,0},{1,3},{3,1},{4,6},{6,4},{5,7},{7,5},{8,10},{10,8},{9,1... | collective-permute-start | bytes 196616 | tf_op jit(solution)/shard_map/ppermute | solution.py:220
  39.5 3.0 %collective-permute-start.14 = (bf16[64,512]{1,0:T(8,128)(2,1)S(1)}, bf16[64,512]{1,0:T(8,128)(2,1)S(1)}, u32[]{:S(2)}, u32[]{:S(2)}) collective-permute-start(bf16[64,512]{1,0:T(8,128)(2,1)S(1)} %collective-permute-done.13.refs_14_), channel_id=1, source_target_pairs={{0,1},{1,0},{2,3},{3,2},{4,5},{5,4},{6,7},{7,6},{8,9},{9,8},{10,11... | collective-permute-start | bytes 196616 | tf_op jit(solution)/shard_map/ppermute | solution.py:220
  39.8 4.3 %collective-permute-start.11 = (bf16[64,512]{1,0:T(8,128)(2,1)S(1)}, bf16[64,512]{1,0:T(8,128)(2,1)S(1)}, u32[]{:S(2)}, u32[]{:S(2)}) collective-permute-start(bf16[64,512]{1,0:T(8,128)(2,1)S(1)} %collective-permute-done.9.refs_10_), channel_id=1, source_target_pairs={{0,2},{2,0},{1,3},{3,1},{4,6},{6,4},{5,7},{7,5},{8,10},{10,8},{9,1... | collective-permute-start | bytes 196616 | tf_op jit(solution)/shard_map/ppermute | solution.py:220
  40.3 3.7 %collective-permute-start.10 = (bf16[64,512]{1,0:T(8,128)(2,1)S(1)}, bf16[64,512]{1,0:T(8,128)(2,1)S(1)}, u32[]{:S(2)}, u32[]{:S(2)}) collective-permute-start(bf16[64,512]{1,0:T(8,128)(2,1)S(1)} %collective-permute-done.9.refs_10_), channel_id=1, source_target_pairs={{0,1},{1,0},{2,3},{3,2},{4,5},{5,4},{6,7},{7,6},{8,9},{9,8},{10,11... | collective-permute-start | bytes 196616 | tf_op jit(solution)/shard_map/ppermute | solution.py:220
  40.5 3.6 %collective-permute-start.8 = (bf16[64,512]{1,0:T(8,128)(2,1)S(1)}, bf16[64,512]{1,0:T(8,128)(2,1)S(1)}, u32[]{:S(2)}, u32[]{:S(2)}) collective-permute-start(bf16[64,512]{1,0:T(8,128)(2,1)S(1)} %collective-permute-done.7.refs_8_), channel_id=1, source_target_pairs={{0,1},{1,0},{2,3},{3,2},{4,5},{5,4},{6,7},{7,6},{8,9},{9,8},{10,11... | collective-permute-start | bytes 196616 | tf_op jit(solution)/shard_map/ppermute | solution.py:220
  42.5 1.5 %collective-permute-start.20 = (bf16[64,512]{1,0:T(8,128)(2,1)S(1)}, bf16[64,512]{1,0:T(8,128)(2,1)S(1)}, u32[]{:S(2)}, u32[]{:S(2)}) collective-permute-start(bf16[64,512]{1,0:T(8,128)(2,1)S(1)} %collective-permute-done.19.refs_20_), channel_id=1, source_target_pairs={{0,1},{1,0},{2,3},{3,2},{4,5},{5,4},{6,7},{7,6},{8,9},{9,8},{10,11... | collective-permute-start | bytes 196616 | tf_op jit(solution)/shard_map/ppermute | solution.py:220
  42.6 1.5 %collective-permute-start.16 = (bf16[64,512]{1,0:T(8,128)(2,1)S(1)}, bf16[64,512]{1,0:T(8,128)(2,1)S(1)}, u32[]{:S(2)}, u32[]{:S(2)}) collective-permute-start(bf16[64,512]{1,0:T(8,128)(2,1)S(1)} %collective-permute-done.15.refs_16_), channel_id=1, source_target_pairs={{0,1},{1,0},{2,3},{3,2},{4,5},{5,4},{6,7},{7,6},{8,9},{9,8},{10,11... | collective-permute-start | bytes 196616 | tf_op jit(solution)/shard_map/ppermute | solution.py:220
  44.0 1.3 %collective-permute-start.12 = (bf16[64,512]{1,0:T(8,128)(2,1)S(1)}, bf16[64,512]{1,0:T(8,128)(2,1)S(1)}, u32[]{:S(2)}, u32[]{:S(2)}) collective-permute-start(bf16[64,512]{1,0:T(8,128)(2,1)S(1)} %collective-permute-done.11.refs_12_), channel_id=1, source_target_pairs={{0,1},{1,0},{2,3},{3,2},{4,5},{5,4},{6,7},{7,6},{8,9},{9,8},{10,11... | collective-permute-start | bytes 196616 | tf_op jit(solution)/shard_map/ppermute | solution.py:220
  52.5 4.5 %collective-permute-start.21 = (bf16[64,512]{1,0:T(8,128)(2,1)S(1)}, bf16[64,512]{1,0:T(8,128)(2,1)S(1)}, u32[]{:S(2)}, u32[]{:S(2)}) collective-permute-start(bf16[64,512]{1,0:T(8,128)(2,1)S(1)} %get-tuple-element.23), channel_id=1, source_target_pairs={{0,4},{4,0},{8,12},{12,8},{1,5},{5,1},{9,13},{13,9},{2,6},{6,2},{1... | collective-permute-start | bytes 196616 | tf_op jit(solution)/shard_map/ppermute | solution.py:220
  53.7 8.3 %collective-permute-start.22 = (bf16[64,512]{1,0:T(8,128)(2,1)S(1)}, bf16[64,512]{1,0:T(8,128)(2,1)S(1)}, u32[]{:S(2)}, u32[]{:S(2)}) collective-permute-start(bf16[64,512]{1,0:T(8,128)(2,1)S(1)} %get-tuple-element.24), channel_id=1, source_target_pairs={{0,8},{4,12},{8,0},{12,4},{1,9},{5,13},{9,1},{13,5},{2,10},{6,14},... | collective-permute-start | bytes 196616 | tf_op jit(solution)/shard_map/ppermute | solution.py:220
  55.0 7.0 %collective-permute-start.23 = (bf16[64,512]{1,0:T(8,128)(2,1)S(1)}, bf16[64,512]{1,0:T(8,128)(2,1)S(1)}, u32[]{:S(2)}, u32[]{:S(2)}) collective-permute-start(bf16[64,512]{1,0:T(8,128)(2,1)S(1)} %get-tuple-element.25), channel_id=1, source_target_pairs={{0,12},{4,8},{8,4},{12,0},{1,13},{5,9},{9,5},{13,1},{2,14},{6,10},... | collective-permute-start | bytes 196616 | tf_op jit(solution)/shard_map/ppermute | solution.py:220
  62.0 6.6 %collective-permute-start.26 = (bf16[64,512]{1,0:T(8,128)(2,1)S(1)}, bf16[64,512]{1,0:T(8,128)(2,1)S(1)}, u32[]{:S(2)}, u32[]{:S(2)}) collective-permute-start(bf16[64,512]{1,0:T(8,128)(2,1)S(1)} %sum_over_terms.3.refs_0_), channel_id=1, source_target_pairs={{0,12},{4,8},{8,4},{12,0},{1,13},{5,9},{9,5},{13,1},{2,14},{6,10},... | collective-permute-start | bytes 196616 | tf_op jit(solution)/shard_map/ppermute | solution.py:220
  64.0 6.0 %collective-permute-start.25 = (bf16[64,512]{1,0:T(8,128)(2,1)S(1)}, bf16[64,512]{1,0:T(8,128)(2,1)S(1)}, u32[]{:S(2)}, u32[]{:S(2)}) collective-permute-start(bf16[64,512]{1,0:T(8,128)(2,1)S(1)} %sum_over_terms.3.refs_0_), channel_id=1, source_target_pairs={{0,8},{4,12},{8,0},{12,4},{1,9},{5,13},{9,1},{13,5},{2,10},{6,14},... | collective-permute-start | bytes 196616 | tf_op jit(solution)/shard_map/ppermute | solution.py:220
  64.8 5.2 %collective-permute-start.24 = (bf16[64,512]{1,0:T(8,128)(2,1)S(1)}, bf16[64,512]{1,0:T(8,128)(2,1)S(1)}, u32[]{:S(2)}, u32[]{:S(2)}) collective-permute-start(bf16[64,512]{1,0:T(8,128)(2,1)S(1)} %sum_over_terms.3.refs_0_), channel_id=1, source_target_pairs={{0,4},{4,0},{8,12},{12,8},{1,5},{5,1},{9,13},{13,9},{2,6},{6,2},{1... | collective-permute-start | bytes 196616 | tf_op jit(solution)/shard_map/ppermute | solution.py:220

commit v3 on v0

v3 whole, which is shorter than its diff:
```python
import jax
import jax.numpy as jnp
from jax import lax
from jax.experimental import pallas as pl
from jax.experimental.pallas import tpu as pltpu
from jax.sharding import PartitionSpec as P

epsilon = 1e-06
vmem_bytes = 24 * 1024 * 1024


def mixing_scalar(pairs_ref, weights_ref, term, target, source):
    value = jnp.float32(0.0)
    for pair in range(weights_ref.shape[1]):
        hit = (pairs_ref[term, pair, 1] == target) & (pairs_ref[term, pair, 0] == source)
        value = value + jnp.where(hit, weights_ref[term, pair], jnp.float32(0.0))
    return value


def live_cells(sizes_ref, sector, row_start, rows, columns):
    row = row_start + lax.broadcasted_iota(jnp.int32, (rows, columns), 0)
    column = lax.broadcasted_iota(jnp.int32, (rows, columns), 1)
    return (row < sizes_ref[sector, 0]) & (column < sizes_ref[sector, 1])


def masked(values, live):
    return jnp.where(live, values.astype(jnp.float32), 0.0).astype(values.dtype)


def left_times(left_own, left_other, term, own, other):
    return jnp.dot(left_own[term], own, preferred_element_type=jnp.float32) + jnp.dot(
        left_other[term], other, preferred_element_type=jnp.float32
    )


def times_right(values, right, term):
    return lax.dot_general(
        values.astype(jnp.bfloat16),
        right[term],
        (((1,), (1,)), ((), ())),
        preferred_element_type=jnp.float32,
    )


def load_kernel(
    sizes_ref, left_ref, right_ref, wave_ref,
    left_own, left_other, right, wave_own,
    sems,
):
    rows, columns = wave_own.shape
    core = lax.axis_index("rep")
    own = pl.multiple_of(core * rows, rows)
    other = pl.multiple_of((core ^ 1) * rows, rows)
    copies = [
        pltpu.make_async_copy(wave_ref.at[0], wave_own, sems.at[0]),
        pltpu.make_async_copy(
            left_ref.at[:, pl.ds(own, rows), pl.ds(own, rows)], left_own, sems.at[1]
        ),
        pltpu.make_async_copy(
            left_ref.at[:, pl.ds(own, rows), pl.ds(other, rows)], left_other, sems.at[2]
        ),
        pltpu.make_async_copy(right_ref, right, sems.at[3]),
    ]
    for copy in copies:
        copy.start()
    copies[0].wait()
    live = live_cells(sizes_ref, lax.axis_index("sec"), own, rows, columns)
    wave_own[...] = masked(wave_own[...], live)
    for copy in copies[1:]:
        copy.wait()


def first_kernel(sectors, *refs):
    sizes_ref, pairs_ref, weights_ref, left_own, left_other, right, own, arrived = refs[:8]
    other, *shares = refs[8:-1]
    held = refs[-1]
    rows, columns = own.shape
    share = shares[0].shape[0]
    sector = lax.axis_index("sec")
    core = lax.axis_index("rep")
    place = lax.axis_index("ops")
    live = live_cells(sizes_ref, sector, (core ^ 1) * rows, rows, columns)
    other[...] = masked(arrived[0], live)
    totals = [None] * sectors
    for term in range(right.shape[0]):
        product = left_times(left_own, left_other, term, own[...], other[...])
        product = times_right(product, right, term)
        for step in range(sectors):
            weight = mixing_scalar(pairs_ref, weights_ref, term, sector ^ step, sector)
            part = weight * product
            totals[step] = part if totals[step] is None else totals[step] + part
    for step in range(sectors):
        live = live_cells(sizes_ref, sector ^ step, core * rows, rows, columns)
        held[step] = jnp.where(live, totals[step], 0.0)
    for index, out in enumerate(shares):
        along, across = index // sectors, index % sectors
        start = pl.multiple_of((place ^ along) * share, share)
        out[...] = held[across, pl.ds(start, share), :].astype(out.dtype)


def sum_kernel(own_ref, *refs):
    total = own_ref[...]
    for piece in refs[:-1]:
        total = total + piece[...].astype(jnp.float32)
    refs[-1][...] = total.astype(refs[-1].dtype)


def join_halves_kernel(*refs):
    pieces, half = refs[:-1], refs[-1]
    sectors = half.shape[0]
    share = pieces[0].shape[0]
    sector = lax.axis_index("sec")
    place = lax.axis_index("ops")
    for index, piece in enumerate(pieces):
        along, across = index // sectors, index % sectors
        start = pl.multiple_of((place ^ along) * share, share)
        half[sector ^ across, pl.ds(start, share), :] = piece[...]


def second_kernel(
    sizes_ref, pairs_ref, weights_ref, left_own, left_other, right, own, other, *refs
):
    shares, held = refs[:-1], refs[-1]
    sectors, rows, columns = own.shape
    share = shares[0].shape[0]
    target = lax.axis_index("sec")
    core = lax.axis_index("rep")
    place = lax.axis_index("ops")
    total = None
    for term in range(right.shape[0]):
        combined = None
        for source in range(sectors):
            weight = mixing_scalar(pairs_ref, weights_ref, term, target, source)
            part = weight * left_times(left_own, left_other, term, own[source], other[source])
            combined = part if combined is None else combined + part
        part = times_right(combined, right, term)
        total = part if total is None else total + part
    live = live_cells(sizes_ref, target, core * rows, rows, columns)
    held[...] = jnp.where(live, total, 0.0)
    for step, out in enumerate(shares):
        start = pl.multiple_of((place ^ step) * share, share)
        out[...] = held[pl.ds(start, share), :].astype(out.dtype)


def sums_kernel(wave_own, wave_other, sigma_own, sigma_other, out):
    sector = lax.axis_index("sec")
    step, columns = 16, wave_own.shape[1]
    sums = (jnp.zeros((step, columns), jnp.float32),) * 3
    for wave, sigma in ((wave_own, sigma_own), (wave_other, sigma_other)):

        def add_rows(block, carry):
            start = pl.multiple_of(block * step, step)
            w = wave[pl.ds(start, step), :].astype(jnp.float32)
            s = sigma[sector, pl.ds(start, step), :].astype(jnp.float32)
            return (carry[0] + w * s, carry[1] + w * w, carry[2] + s * s)

        sums = lax.fori_loop(0, wave.shape[0] // step, add_rows, sums, unroll=2)
    for index, value in enumerate(sums):
        out[index] = jnp.broadcast_to(jnp.sum(value, keepdims=True), out.shape[1:])


def wave_kernel(sizes_ref, wave_own, sigma_own, *refs):
    sums, (second, factors) = refs[:-2], refs[-2:]
    rows, columns = wave_own.shape
    live_count = jnp.float32(0.0)
    for sector in range(sizes_ref.shape[0]):
        live_count = live_count + sizes_ref[sector, 0].astype(jnp.float32) * sizes_ref[
            sector, 1
        ].astype(jnp.float32)
    total = sums[0][...]
    for other in sums[1:]:
        total = total + other[...]
    correlation, norm_square, sigma_square = total[0], total[1], total[2]
    rayleigh = correlation / norm_square
    residual_square = (
        sigma_square - 2.0 * rayleigh * correlation + rayleigh * rayleigh * norm_square
    )
    residual_square = jnp.maximum(residual_square, 0.0)
    scale = 1.0 / jnp.sqrt(residual_square / live_count + epsilon)
    factors[0] = scale
    factors[1] = rayleigh * scale
    sigma_factor = jnp.broadcast_to(scale[:1, :1], (rows, columns))
    wave_factor = jnp.broadcast_to((rayleigh * scale)[:1, :1], (rows, columns))
    sigma = sigma_own[lax.axis_index("sec")].astype(jnp.float32)
    wave = wave_own[...].astype(jnp.float32)
    second[0] = (sigma_factor * sigma - wave_factor * wave).astype(second.dtype)


def join_kernel(factors, sigma_own, *refs):
    pieces, out = refs[:-1], refs[-1]
    share, columns = pieces[0].shape
    sector = lax.axis_index("sec")
    place = lax.axis_index("ops")
    scale = jnp.broadcast_to(factors[0][:1, :1], (share, columns))
    shift = jnp.broadcast_to(factors[1][:1, :1], (share, columns))
    for step, piece in enumerate(pieces):
        start = pl.multiple_of((place ^ step) * share, share)
        sigma = sigma_own[sector, pl.ds(start, share), :].astype(jnp.float32)
        out[0, pl.ds(start, share), :] = scale * piece[...].astype(jnp.float32) - shift * sigma


def partner(value, steps):
    steps = {axis: step for axis, step in steps.items() if step}
    if not steps:
        return value
    axes = tuple(steps)
    places = [()]
    for axis in axes:
        places = [place + (i,) for place in places for i in range(lax.axis_size(axis))]
    index = {place: i for i, place in enumerate(places)}
    pairs = [
        (index[tuple(i ^ steps[axis] for i, axis in zip(place, axes))], index[place])
        for place in places
    ]
    return lax.ppermute(value, axes, pairs)


def local(wavefunction, sector_sizes, left_blocks, right_blocks, sector_pairs, pair_weights):
    sectors = sector_sizes.shape[0]
    ops_count = lax.axis_size("ops")
    _, rows, columns = wavefunction.shape
    terms, side = left_blocks.shape[0], left_blocks.shape[1]
    share = rows // ops_count
    bf16, f32 = jnp.bfloat16, jnp.float32
    smem = pl.BlockSpec(memory_space=pltpu.SMEM)
    outside = pl.BlockSpec(memory_space=pltpu.HBM)
    inside = pl.BlockSpec(memory_space=pltpu.VMEM)

    def shape(*dims, dtype=bf16):
        return jax.ShapeDtypeStruct(dims, dtype)

    def call(kernel, name, out_shape, in_specs, *operands, scratch=()):
        return pl.pallas_call(
            kernel,
            out_shape=out_shape,
            in_specs=list(in_specs) + [inside] * (len(operands) - len(in_specs)),
            out_specs=jax.tree.map(lambda _: inside, out_shape),
            scratch_shapes=list(scratch),
            compiler_params=pltpu.CompilerParams(vmem_limit_bytes=vmem_bytes),
            name=name,
        )(*operands)

    def share_shapes(count):
        return [shape(share, columns, dtype=f32)] + [shape(share, columns)] * (count - 1)

    arrived = partner(wavefunction, {"rep": 1})
    left_own, left_other, right, wave_own = call(
        load_kernel,
        "load_operators",
        [
            shape(terms, rows, rows),
            shape(terms, rows, side - rows),
            shape(*right_blocks.shape),
            shape(rows, columns),
        ],
        [smem] + [outside] * 3,
        sector_sizes,
        left_blocks,
        right_blocks,
        wavefunction,
        scratch=[pltpu.SemaphoreType.DMA((4,))],
    )
    operators = (sector_sizes, sector_pairs, pair_weights, left_own, left_other, right)

    wave_other, *shares = call(
        lambda *refs: first_kernel(sectors, *refs),
        "first_sigma_terms",
        [shape(rows, columns)] + share_shapes(ops_count * sectors),
        [smem] * 3,
        *operators,
        wave_own,
        arrived,
        scratch=[pltpu.VMEM((sectors, rows, columns), f32)],
    )
    received = [
        partner(shares[index], {"ops": index // sectors, "sec": index % sectors})
        for index in reversed(range(1, ops_count * sectors))
    ]
    first_share = call(
        sum_kernel, "sum_first_sigma", shape(share, columns), [], shares[0], *received
    )
    along = [None] * ops_count
    for step in reversed(range(ops_count)):
        along[step] = partner(first_share, {"ops": step})
    pieces = [
        partner(along[step], {"sec": across})
        for step in range(ops_count)
        for across in range(sectors)
    ]
    sigma_own = call(
        join_halves_kernel, "join_first_sigma", shape(sectors, rows, columns), [], *pieces
    )
    sigma_other = partner(sigma_own, {"rep": 1})

    shares = call(
        second_kernel,
        "second_sigma_terms",
        share_shapes(ops_count),
        [smem] * 3,
        *operators,
        sigma_own,
        sigma_other,
        scratch=[pltpu.VMEM((rows, columns), f32)],
    )
    received = [partner(shares[step], {"ops": step}) for step in reversed(range(1, ops_count))]
    sums = call(
        sums_kernel,
        "sums_for_rayleigh",
        shape(3, 8, 128, dtype=f32),
        [],
        wave_own,
        wave_other,
        sigma_own,
        sigma_other,
    )
    second_wave, factors = call(
        wave_kernel,
        "second_wave",
        [shape(1, rows, columns), shape(2, 8, 128, dtype=f32)],
        [smem],
        sector_sizes,
        wave_own,
        sigma_own,
        *[partner(sums, {"sec": step}) for step in range(sectors)],
    )
    second_share = call(
        sum_kernel, "sum_second_sigma", shape(share, columns), [], shares[0], *received
    )
    pieces = [None] * ops_count
    for step in reversed(range(ops_count)):
        pieces[step] = partner(second_share, {"ops": step})
    second_sigma = call(
        join_kernel,
        "join_second_sigma",
        shape(1, rows, columns, dtype=f32),
        [],
        factors,
        sigma_own,
        *pieces,
    )
    return (second_wave, second_sigma)


def solution(mesh):
    return jax.shard_map(
        local,
        mesh=mesh,
        in_specs=(
            P(("grp", "sec"), "rep", None),
            P("grp", None),
            P(("grp", "ops"), None, None),
            P(("grp", "ops"), None, None),
            P(("grp", "ops"), None, None),
            P(("grp", "ops"), None),
        ),
        out_specs=(P(("grp", "sec"), "rep", None), P(("grp", "sec"), "rep", None)),
        check_vma=False,
    )
```

time: 234 us -> 67.6 us (0.29)
  waiting for transfers between devices: 109 us -> 21.4 us
  matrix products: 58.1 us -> 0 us
  blocking collectives: 31.6 us -> 0 us
  starting transfers between devices: 0.16 us -> 30 us
  between operations: 17.9 us -> 0.74 us
  other arithmetic: 12 us -> 0 us
  Pallas kernels: 0 us -> 9.6 us
    psum x2 -> x0, waiting for transfers between devices: 76.1 us -> none  [the longest x1 38.5 us: local(): second_sigma = lax.psum(partial_second, 'ops')]
    dot_general x32 -> x0, matrix products: 58.1 us -> none  [the longest x8 30.3 us: term_update(): jnp.einsum('ba,aij->bij', mixing_rows, left_product, precision=lax.Precis...]
    all_gather x2 -> x0, waiting for transfers between devices: 32.5 us -> none  [spread_tiles(): return lax.all_gather(wave_part, ('sec', 'rep'), axis=1, tiled=True)]
    psum x1 -> x0, blocking collectives: 31.6 us -> none  [davidson_stats(): lax.psum((jnp.sum(wave_share * sigma_share), jnp.sum(wave_share * wave_sh...]
    ppermute x0 -> x23, starting transfers between devices: none -> 30 us  [partner(): return lax.ppermute(value, axes, pairs)]
    ppermute x0 -> x23, waiting for transfers between devices: none -> 21.4 us  [partner(): return lax.ppermute(value, axes, pairs)]
    pallas_call x0 -> x9, Pallas kernels: none -> 9.6 us  [call(): pl.pallas_call(kernel, out_shape=out_shape, in_specs=list(in_specs) + [in...]
    select_n x3 -> x0, other arithmetic: 6.6 us -> none  [the longest x1 2.52 us: local(): jnp.where(live_mask, second_sigma, jnp.zeros((), jnp.float32))]
  transfers between devices with their start and end apart: 4 -> 23, of which waited for: 4 -> 12; matrix products, arithmetic and copies ran while one was open for 1% -> 1% of each run, Pallas kernels for 0% -> 4%
where the time goes in v3:
time: 67.6 us; the launch traced here: 67.3 us
  starting transfers between devices  30 us (44%)
  waiting for transfers between devices  21.4 us (32%)
  Pallas kernels  9.6 us (14%)
  local copies, waits for them, and re-layouts  5.6 us (8%)
  between operations  0.74 us (1%)
    ppermute x23, starting transfers between devices, partner(): return lax.ppermute(value, axes, pairs)  30 us
    ppermute x23, waiting for transfers between devices, partner(): return lax.ppermute(value, axes, pairs)  21.4 us
    pallas_call x9, Pallas kernels, call(): pl.pallas_call(kernel, out_shape=out_shape, in_specs=list(in_specs) + [in...  9.6 us
    unnamed x13, local copies, waits for them, and re-layouts  5.6 us
  transfers between devices with their start and end apart: 23, of which 12 were waited for; matrix products, arithmetic and copies ran while one was open for 1% of the time, Pallas kernels for 4%

profile of v3, /device:TPU:0, one launch (start us, length us, event | category | flops | bytes accessed | tf_op | source)
XLA Modules:
  0.0 67.3 jit_solution(341271115169333390)
XLA Ops:
  0.6 0.5 collective-permute-start
  1.1 0.8 %copy.8.refs_1_.pairs_ref = s32[4,8,2]{2,1,0:T(8,128)S(1)} copy(s32[4,8,2]{1,2,0:T(2,128)} %param.10) | data formatting | bytes 512 | tf_op args[4]
  1.9 0.0 copy-start
  1.9 1.6 %copy-done = bf16[4,512,512]{2,1,0:T(8,128)(2,1)S(1)} copy-done((bf16[4,512,512]{2,1,0:T(8,128)(2,1)S(1)}, bf16[4,512,512]{2,1,0:T(8,128)(2,1)}, u32[]{:S(2)}) %copy-start) | copy-done | bytes 2097176
  3.5 0.0 copy-start.1
  3.5 1.6 %copy-done.1 = bf16[4,512,512]{2,1,0:T(8,128)(2,1)S(1)} copy-done((bf16[4,512,512]{2,1,0:T(8,128)(2,1)S(1)}, bf16[4,512,512]{2,1,0:T(8,128)(2,1)}, u32[]{:S(2)}) %copy-start.1) | copy-done | bytes 2097176
  5.1 0.0 copy-start.2
  5.1 0.9 %copy-done.2 = bf16[1,256,512]{2,1,0:T(8,128)(2,1)S(1)} copy-done((bf16[1,256,512]{2,1,0:T(8,128)(2,1)S(1)}, bf16[1,256,512]{2,1,0:T(8,128)(2,1)}, u32[]{:S(2)}) %copy-start.2) | copy-done | bytes 262168
  6.1 0.7 %copy-done.3 = s32[2,2]{1,0:T(2,128)S(1)} copy-done((s32[2,2]{1,0:T(2,128)S(1)}, s32[2,2]{1,0:T(2,128)}, u32[]{:S(2)}) %copy-start.3) | copy-done | bytes 40
  6.7 0.9 %load_operators.1 = (bf16[4,256,256]{2,1,0:T(8,128)(2,1)S(1)}, bf16[4,256,256]{2,1,0:T(8,128)(2,1)S(1)}, bf16[4,512,512]{2,1,0:T(8,128)(2,1)S(1)}, bf16[256,512]{1,0:T(8,128)(2,1)S(1)}) custom-call(s32[2,2]{1,0:T(2,128)S(1)} %copy-done.3, bf16[4,512,512]{2,1,0:T(8,128)(2,1)S(1)} %copy-done, bf16[4,512,512]{2,1,0:T(8,128)(2,1)S(1)} %copy-done.1, ...), custom_call_target="tpu_custom_call" | custom-call | tf_op jit(solution)/shard_map/load_operators/pallas_call | solution.py:233
  7.7 0.0 collective-permute-done.refs_7_
  7.7 0.0 copy-done.5
  7.7 0.0 copy-start.4
  7.7 2.8 %first_sigma_terms.1 = (bf16[256,512]{1,0:T(8,128)(2,1)S(1)}, f32[64,512]{1,0:T(8,128)S(1)}, bf16[64,512]{1,0:T(8,128)(2,1)S(1)}, bf16[64,512]{1,0:T(8,128)(2,1)...) custom-call(s32[2,2]{1,0:T(2,128)S(1)} %copy-done.3, ...), custom_call_target="tpu_custom_call" | custom-call | tf_op jit(solution)/shard_map/first_sigma_terms/pallas_call | solution.py:233
  10.4 5.6 %collective-permute-start.1 = (bf16[64,512]{1,0:T(8,128)(2,1)S(1)}, bf16[64,512]{1,0:T(8,128)(2,1)S(1)}, u32[]{:S(2)}, u32[]{:S(2)}) collective-permute-start(bf16[64,512]{1,0:T(8,128)(2,1)S(1)} %get-tuple-element.26), channel_id=1, source_target_pairs={{14,0},{12,2},{10,4},{8,6},{6,8},{4,10},{2,12},{0,14},{15,1},{13,3... | collective-permute-start | bytes 196616 | tf_op jit(solution)/shard_map/ppermute | solution.py:215
  16.1 0.2 collective-permute-start.2
  16.3 0.7 %collective-permute-start.3 = (bf16[64,512]{1,0:T(8,128)(2,1)S(1)}, bf16[64,512]{1,0:T(8,128)(2,1)S(1)}, u32[]{:S(2)}, u32[]{:S(2)}) collective-permute-start(bf16[64,512]{1,0:T(8,128)(2,1)S(1)} %get-tuple-element.28), channel_id=1, source_target_pairs={{10,0},{8,2},{14,4},{12,6},{2,8},{0,10},{6,12},{4,14},{11,1},{9,3}... | collective-permute-start | bytes 196616 | tf_op jit(solution)/shard_map/ppermute | solution.py:215
  17.0 2.0 %collective-permute-start.4 = (bf16[64,512]{1,0:T(8,128)(2,1)S(1)}, bf16[64,512]{1,0:T(8,128)(2,1)S(1)}, u32[]{:S(2)}, u32[]{:S(2)}) collective-permute-start(bf16[64,512]{1,0:T(8,128)(2,1)S(1)} %get-tuple-element.29), channel_id=1, source_target_pairs={{8,0},{12,4},{0,8},{4,12},{9,1},{13,5},{1,9},{5,13},{10,2},{14,6},... | collective-permute-start | bytes 196616 | tf_op jit(solution)/shard_map/ppermute | solution.py:215
  19.1 2.3 %collective-permute-start.5 = (bf16[64,512]{1,0:T(8,128)(2,1)S(1)}, bf16[64,512]{1,0:T(8,128)(2,1)S(1)}, u32[]{:S(2)}, u32[]{:S(2)}) collective-permute-start(bf16[64,512]{1,0:T(8,128)(2,1)S(1)} %get-tuple-element.30), channel_id=1, source_target_pairs={{6,0},{4,2},{2,4},{0,6},{14,8},{12,10},{10,12},{8,14},{7,1},{5,3},... | collective-permute-start | bytes 196616 | tf_op jit(solution)/shard_map/ppermute | solution.py:215
  21.4 0.0 collective-permute-done.1.refs_0_
  21.4 0.8 %collective-permute-start.6 = (bf16[64,512]{1,0:T(8,128)(2,1)S(1)}, bf16[64,512]{1,0:T(8,128)(2,1)S(1)}, u32[]{:S(2)}, u32[]{:S(2)}) collective-permute-start(bf16[64,512]{1,0:T(8,128)(2,1)S(1)} %get-tuple-element.31), channel_id=1, source_target_pairs={{4,0},{0,4},{12,8},{8,12},{5,1},{1,5},{13,9},{9,13},{6,2},{2,6},{1... | collective-permute-start | bytes 196616 | tf_op jit(solution)/shard_map/ppermute | solution.py:215
  22.1 0.8 %collective-permute-done.2.refs_1_ = bf16[64,512]{1,0:T(8,128)(2,1)S(1)} collective-permute-done((bf16[64,512]{1,0:T(8,128)(2,1)S(1)}, bf16[64,512]{1,0:T(8,128)(2,1)S(1)}, u32[]{:S(2)}, u32[]{:S(2)}) %collective-permute-start.2) | collective-permute-done | bytes 65568 | tf_op jit(solution)/shard_map/ppermute | solution.py:215
  23.0 0.5 collective-permute-start.7
  23.5 2.5 %collective-permute-done.3.refs_2_ = bf16[64,512]{1,0:T(8,128)(2,1)S(1)} collective-permute-done((bf16[64,512]{1,0:T(8,128)(2,1)S(1)}, bf16[64,512]{1,0:T(8,128)(2,1)S(1)}, u32[]{:S(2)}, u32[]{:S(2)}) %collective-permute-start.3) | collective-permute-done | bytes 65568 | tf_op jit(solution)/shard_map/ppermute | solution.py:215
  26.0 1.9 %collective-permute-done.4.refs_3_ = bf16[64,512]{1,0:T(8,128)(2,1)S(1)} collective-permute-done((bf16[64,512]{1,0:T(8,128)(2,1)S(1)}, bf16[64,512]{1,0:T(8,128)(2,1)S(1)}, u32[]{:S(2)}, u32[]{:S(2)}) %collective-permute-start.4) | collective-permute-done | bytes 65568 | tf_op jit(solution)/shard_map/ppermute | solution.py:215
  27.9 0.0 collective-permute-done.5.refs_4_
  27.9 0.1 collective-permute-done.6.refs_5_
  28.1 0.0 collective-permute-done.7.refs_6_
  28.1 0.1 sum_first_sigma.1.refs_0_
  28.1 1.8 %collective-permute-start.9 = (bf16[64,512]{1,0:T(8,128)(2,1)S(1)}, bf16[64,512]{1,0:T(8,128)(2,1)S(1)}, u32[]{:S(2)}, u32[]{:S(2)}) collective-permute-start(bf16[64,512]{1,0:T(8,128)(2,1)S(1)} %sum_first_sigma.1.refs_0_), channel_id=1, source_target_pairs={{4,0},{0,4},{12,8},{8,12},{5,1},{1,5},{13,9},{9,13},{6,2},{2,6},{1... | collective-permute-start | bytes 196616 | tf_op jit(solution)/shard_map/ppermute | solution.py:215
  29.9 2.1 %collective-permute-start.11 = (bf16[64,512]{1,0:T(8,128)(2,1)S(1)}, bf16[64,512]{1,0:T(8,128)(2,1)S(1)}, u32[]{:S(2)}, u32[]{:S(2)}) collective-permute-start(bf16[64,512]{1,0:T(8,128)(2,1)S(1)} %sum_first_sigma.1.refs_0_), channel_id=1, source_target_pairs={{8,0},{12,4},{0,8},{4,12},{9,1},{13,5},{1,9},{5,13},{10,2},{14,6},... | collective-permute-start | bytes 196616 | tf_op jit(solution)/shard_map/ppermute | solution.py:215
  32.1 0.7 %collective-permute-start.13 = (bf16[64,512]{1,0:T(8,128)(2,1)S(1)}, bf16[64,512]{1,0:T(8,128)(2,1)S(1)}, u32[]{:S(2)}, u32[]{:S(2)}) collective-permute-start(bf16[64,512]{1,0:T(8,128)(2,1)S(1)} %sum_first_sigma.1.refs_0_), channel_id=1, source_target_pairs={{12,0},{8,4},{4,8},{0,12},{13,1},{9,5},{5,9},{1,13},{14,2},{10,6},... | collective-permute-start | bytes 196616 | tf_op jit(solution)/shard_map/ppermute | solution.py:215
  32.8 0.5 collective-permute-start.8
  33.3 0.0 collective-permute-done.9.refs_2_
  33.3 1.5 %collective-permute-start.10 = (bf16[64,512]{1,0:T(8,128)(2,1)S(1)}, bf16[64,512]{1,0:T(8,128)(2,1)S(1)}, u32[]{:S(2)}, u32[]{:S(2)}) collective-permute-start(bf16[64,512]{1,0:T(8,128)(2,1)S(1)} %collective-permute-done.9.refs_2_), channel_id=1, source_target_pairs={{2,0},{0,2},{3,1},{1,3},{6,4},{4,6},{7,5},{5,7},{10,8},{8,10},{11,... | collective-permute-start | bytes 196616 | tf_op jit(solution)/shard_map/ppermute | solution.py:215
  34.8 0.7 %collective-permute-done.11.refs_4_ = bf16[64,512]{1,0:T(8,128)(2,1)S(1)} collective-permute-done((bf16[64,512]{1,0:T(8,128)(2,1)S(1)}, bf16[64,512]{1,0:T(8,128)(2,1)S(1)}, u32[]{:S(2)}, u32[]{:S(2)}) %collective-permute-start.11) | collective-permute-done | bytes 65568 | tf_op jit(solution)/shard_map/ppermute | solution.py:215
  35.6 0.0 collective-permute-start.12
  35.6 2.5 %collective-permute-done.13.refs_6_ = bf16[64,512]{1,0:T(8,128)(2,1)S(1)} collective-permute-done((bf16[64,512]{1,0:T(8,128)(2,1)S(1)}, bf16[64,512]{1,0:T(8,128)(2,1)S(1)}, u32[]{:S(2)}, u32[]{:S(2)}) %collective-permute-start.13) | collective-permute-done | bytes 65568 | tf_op jit(solution)/shard_map/ppermute | solution.py:215
  38.1 0.8 %collective-permute-start.14 = (bf16[64,512]{1,0:T(8,128)(2,1)S(1)}, bf16[64,512]{1,0:T(8,128)(2,1)S(1)}, u32[]{:S(2)}, u32[]{:S(2)}) collective-permute-start(bf16[64,512]{1,0:T(8,128)(2,1)S(1)} %collective-permute-done.13.refs_6_), channel_id=1, source_target_pairs={{2,0},{0,2},{3,1},{1,3},{6,4},{4,6},{7,5},{5,7},{10,8},{8,10},{11,... | collective-permute-start | bytes 196616 | tf_op jit(solution)/shard_map/ppermute | solution.py:215
  38.9 0.0 collective-permute-done.8.refs_1_
  38.9 0.0 collective-permute-done.10.refs_3_
  38.9 0.9 %collective-permute-done.12.refs_5_ = bf16[64,512]{1,0:T(8,128)(2,1)S(1)} collective-permute-done((bf16[64,512]{1,0:T(8,128)(2,1)S(1)}, bf16[64,512]{1,0:T(8,128)(2,1)S(1)}, u32[]{:S(2)}, u32[]{:S(2)}) %collective-permute-start.12) | collective-permute-done | bytes 65568 | tf_op jit(solution)/shard_map/ppermute | solution.py:215
  39.9 2.5 %collective-permute-done.14.refs_7_ = bf16[64,512]{1,0:T(8,128)(2,1)S(1)} collective-permute-done((bf16[64,512]{1,0:T(8,128)(2,1)S(1)}, bf16[64,512]{1,0:T(8,128)(2,1)S(1)}, u32[]{:S(2)}, u32[]{:S(2)}) %collective-permute-start.14) | collective-permute-done | bytes 65568 | tf_op jit(solution)/shard_map/ppermute | solution.py:215
  42.5 0.1 collective-permute-start.15
  42.5 1.9 %collective-permute-done.15.sigma_other.other = bf16[2,256,512]{2,1,0:T(8,128)(2,1)S(1)} collective-permute-done((bf16[2,256,512]{2,1,0:T(8,128)(2,1)S(1)}, bf16[2,256,512]{2,1,0:T(8,128)(2,1)S(1)}, u32[]{:S(2)}, u32[]{:S(2)}) %collective-permute-start.15) | collective-permute-done | bytes 524320 | tf_op jit(solution)/shard_map/ppermute | solution.py:215
  44.4 0.0 copy-done.4
  44.4 2.9 %second_sigma_terms.1 = (f32[64,512]{1,0:T(8,128)S(1)}, bf16[64,512]{1,0:T(8,128)(2,1)S(1)}, bf16[64,512]{1,0:T(8,128)(2,1)S(1)}, bf16[64,512]{1,0:T(8,128)(2,1)S(1)}) custom-call(s32[2,2]{1,0:T(2,128)S(1)} %copy-done.4, s32[4,8,2]{2,1,0:T(8,128)S(1)} %copy.8.refs_1_.pairs_ref, f32[4,8]{1,0:T(4,128)S(1)} %copy-done.5, ...), custom_call_target="tpu_custom_call" | custom-call | tf_op jit(solution)/shard_map/second_sigma_terms/pallas_call | solution.py:233
  47.4 2.0 %collective-permute-start.17 = (bf16[64,512]{1,0:T(8,128)(2,1)S(1)}, bf16[64,512]{1,0:T(8,128)(2,1)S(1)}, u32[]{:S(2)}, u32[]{:S(2)}) collective-permute-start(bf16[64,512]{1,0:T(8,128)(2,1)S(1)} %get-tuple-element.37), channel_id=1, source_target_pairs={{12,0},{8,4},{4,8},{0,12},{13,1},{9,5},{5,9},{1,13},{14,2},{10,6},... | collective-permute-start | bytes 196616 | tf_op jit(solution)/shard_map/ppermute | solution.py:215
  49.4 0.0 collective-permute-start.18
  49.4 2.4 %collective-permute-start.19 = (bf16[64,512]{1,0:T(8,128)(2,1)S(1)}, bf16[64,512]{1,0:T(8,128)(2,1)S(1)}, u32[]{:S(2)}, u32[]{:S(2)}) collective-permute-start(bf16[64,512]{1,0:T(8,128)(2,1)S(1)} %get-tuple-element.39), channel_id=1, source_target_pairs={{4,0},{0,4},{12,8},{8,12},{5,1},{1,5},{13,9},{9,13},{6,2},{2,6},{1... | collective-permute-start | bytes 196616 | tf_op jit(solution)/shard_map/ppermute | solution.py:215
  51.8 2.4 %collective-permute-done.17.refs_0_ = bf16[64,512]{1,0:T(8,128)(2,1)S(1)} collective-permute-done((bf16[64,512]{1,0:T(8,128)(2,1)S(1)}, bf16[64,512]{1,0:T(8,128)(2,1)S(1)}, u32[]{:S(2)}, u32[]{:S(2)}) %collective-permute-start.17) | collective-permute-done | bytes 65568 | tf_op jit(solution)/shard_map/ppermute | solution.py:215
  54.2 2.0 %collective-permute-done.18.refs_1_ = bf16[64,512]{1,0:T(8,128)(2,1)S(1)} collective-permute-done((bf16[64,512]{1,0:T(8,128)(2,1)S(1)}, bf16[64,512]{1,0:T(8,128)(2,1)S(1)}, u32[]{:S(2)}, u32[]{:S(2)}) %collective-permute-start.18) | collective-permute-done | bytes 65568 | tf_op jit(solution)/shard_map/ppermute | solution.py:215
  56.2 0.0 collective-permute-done.19.refs_2_
  56.2 0.2 collective-permute-start.20
  56.4 2.4 %collective-permute-start.21 = (bf16[64,512]{1,0:T(8,128)(2,1)S(1)}, bf16[64,512]{1,0:T(8,128)(2,1)S(1)}, u32[]{:S(2)}, u32[]{:S(2)}) collective-permute-start(bf16[64,512]{1,0:T(8,128)(2,1)S(1)} %sum_second_sigma.1.refs_0_), channel_id=1, source_target_pairs={{8,0},{12,4},{0,8},{4,12},{9,1},{13,5},{1,9},{5,13},{10,2},{14,6},... | collective-permute-start | bytes 196616 | tf_op jit(solution)/shard_map/ppermute | solution.py:215
  58.8 1.9 %collective-permute-start.22 = (bf16[64,512]{1,0:T(8,128)(2,1)S(1)}, bf16[64,512]{1,0:T(8,128)(2,1)S(1)}, u32[]{:S(2)}, u32[]{:S(2)}) collective-permute-start(bf16[64,512]{1,0:T(8,128)(2,1)S(1)} %sum_second_sigma.1.refs_0_), channel_id=1, source_target_pairs={{12,0},{8,4},{4,8},{0,12},{13,1},{9,5},{5,9},{1,13},{14,2},{10,6},... | collective-permute-start | bytes 196616 | tf_op jit(solution)/shard_map/ppermute | solution.py:215
  60.7 0.5 sums_for_rayleigh.1.refs_0_
  61.2 0.8 %collective-permute-start.16 = (f32[3,8,128]{2,1,0:T(8,128)S(1)}, f32[3,8,128]{2,1,0:T(8,128)S(1)}, u32[]{:S(2)}, u32[]{:S(2)}) collective-permute-start(f32[3,8,128]{2,1,0:T(8,128)S(1)} %sums_for_rayleigh.1.refs_0_), channel_id=1, source_target_pairs={{2,0},{0,2},{3,1},{1,3},{6,4},{4,6},{7,5},{5,7},{10,8},{8,10},{11,... | collective-permute-start | bytes 36872 | tf_op jit(solution)/shard_map/ppermute | solution.py:215
  62.0 2.9 %collective-permute-done.16.refs_1_ = f32[3,8,128]{2,1,0:T(8,128)S(1)} collective-permute-done((f32[3,8,128]{2,1,0:T(8,128)S(1)}, f32[3,8,128]{2,1,0:T(8,128)S(1)}, u32[]{:S(2)}, u32[]{:S(2)}) %collective-permute-start.16) | collective-permute-done | bytes 12320 | tf_op jit(solution)/shard_map/ppermute | solution.py:215
  64.9 1.4 %second_wave.1 = (bf16[1,256,512]{2,1,0:T(8,128)(2,1)}, f32[2,8,128]{2,1,0:T(8,128)S(1)}) custom-call(s32[2,2]{1,0:T(2,128)S(1)} %copy-done.4, bf16[256,512]{1,0:T(8,128)(2,1)S(1)} %get-tuple-element.21.refs_6_.wave_own, bf16[2,256,512]{2,1,0:T(8,128)(2,1)S(1)} %join_first_sigma.1.sigma_own.own, f32[3,8,128]{2,1,0:T(8,128)S(1)} %sums_for_rayleigh.1.refs_0_, ...), custom_call_target="tpu_custom_call" | custom-call | tf_op jit(solution)/shard_map/second_wave/pallas_call | solution.py:233
  66.4 0.0 collective-permute-done.20.refs_1_
  66.4 0.0 collective-permute-done.21.refs_2_
  66.4 0.0 collective-permute-done.22.refs_3_
  66.4 0.9 %join_second_sigma.1 = f32[1,256,512]{2,1,0:T(8,128)} custom-call(f32[2,8,128]{2,1,0:T(8,128)S(1)} %get-tuple-element.35.factors, bf16[2,256,512]{2,1,0:T(8,128)(2,1)S(1)} %join_first_sigma.1.sigma_own.own, bf16[64,512]{1,0:T(8,128)(2,1)S(1)} %sum_second_sigma.1.refs_0_, bf16[64,512]{1,0:T(8,128)(2,1)S(1)} %collective-permute-done.20.refs_1_, ...), custom_call_target="tpu_custom_call" | custom-call | tf_op jit(solution)/shard_map/join_second_sigma/pallas_call | solution.py:233
  (4 shorter events, 0.1 us)
Async XLA Ops:
  0.6 7.0 %collective-permute-start = (bf16[1,256,512]{2,1,0:T(8,128)(2,1)}, bf16[1,256,512]{2,1,0:T(8,128)(2,1)S(1)}, u32[]{:S(2)}, u32[]{:S(2)}) collective-permute-start(bf16[1,256,512]{2,1,0:T(8,128)(2,1)} %wave_ref.1), channel_id=1, source_target_pairs={{1,0},{0,1},{3,2},{2,3},{5,4},{4,5},{7,6},{6,7},{9,8},{8,9},{11,10... | collective-permute-start | bytes 786440 | tf_op jit(solution)/shard_map/ppermute | solution.py:215
  1.9 1.6 %copy-start = (bf16[4,512,512]{2,1,0:T(8,128)(2,1)S(1)}, bf16[4,512,512]{2,1,0:T(8,128)(2,1)}, u32[]{:S(2)}) copy-start(bf16[4,512,512]{2,1,0:T(8,128)(2,1)} %left_ref.1) | copy-start | bytes 6291460
  3.5 1.6 %copy-start.1 = (bf16[4,512,512]{2,1,0:T(8,128)(2,1)S(1)}, bf16[4,512,512]{2,1,0:T(8,128)(2,1)}, u32[]{:S(2)}) copy-start(bf16[4,512,512]{2,1,0:T(8,128)(2,1)} %right_ref.1) | copy-start | bytes 6291460
  5.1 0.9 %copy-start.2 = (bf16[1,256,512]{2,1,0:T(8,128)(2,1)S(1)}, bf16[1,256,512]{2,1,0:T(8,128)(2,1)}, u32[]{:S(2)}) copy-start(bf16[1,256,512]{2,1,0:T(8,128)(2,1)} %wave_ref.1) | copy-start | bytes 786436
  6.1 0.7 %copy-start.3 = (s32[2,2]{1,0:T(2,128)S(1)}, s32[2,2]{1,0:T(2,128)}, u32[]{:S(2)}) copy-start(s32[2,2]{1,0:T(2,128)} %sizes_ref.5) | copy-start | bytes 52
  6.7 0.9 %copy-start.5 = (f32[4,8]{1,0:T(4,128)S(1)}, f32[4,8]{1,0:T(4,128)}, u32[]{:S(2)}) copy-start(f32[4,8]{1,0:T(4,128)} %weights_ref.1) | copy-start | bytes 388
  7.7 36.8 %copy-start.4 = (s32[2,2]{1,0:T(2,128)S(1)}, s32[2,2]{1,0:T(2,128)}, u32[]{:S(2)}) copy-start(s32[2,2]{1,0:T(2,128)} %sizes_ref.5) | copy-start | bytes 52
  10.4 10.9 %collective-permute-start.1 = (bf16[64,512]{1,0:T(8,128)(2,1)S(1)}, bf16[64,512]{1,0:T(8,128)(2,1)S(1)}, u32[]{:S(2)}, u32[]{:S(2)}) collective-permute-start(bf16[64,512]{1,0:T(8,128)(2,1)S(1)} %get-tuple-element.26), channel_id=1, source_target_pairs={{14,0},{12,2},{10,4},{8,6},{6,8},{4,10},{2,12},{0,14},{15,1},{13,3... | collective-permute-start | bytes 196616 | tf_op jit(solution)/shard_map/ppermute | solution.py:215
  16.1 6.9 %collective-permute-start.2 = (bf16[64,512]{1,0:T(8,128)(2,1)S(1)}, bf16[64,512]{1,0:T(8,128)(2,1)S(1)}, u32[]{:S(2)}, u32[]{:S(2)}) collective-permute-start(bf16[64,512]{1,0:T(8,128)(2,1)S(1)} %get-tuple-element.27), channel_id=1, source_target_pairs={{12,0},{8,4},{4,8},{0,12},{13,1},{9,5},{5,9},{1,13},{14,2},{10,6},... | collective-permute-start | bytes 196616 | tf_op jit(solution)/shard_map/ppermute | solution.py:215
  16.3 9.8 %collective-permute-start.3 = (bf16[64,512]{1,0:T(8,128)(2,1)S(1)}, bf16[64,512]{1,0:T(8,128)(2,1)S(1)}, u32[]{:S(2)}, u32[]{:S(2)}) collective-permute-start(bf16[64,512]{1,0:T(8,128)(2,1)S(1)} %get-tuple-element.28), channel_id=1, source_target_pairs={{10,0},{8,2},{14,4},{12,6},{2,8},{0,10},{6,12},{4,14},{11,1},{9,3}... | collective-permute-start | bytes 196616 | tf_op jit(solution)/shard_map/ppermute | solution.py:215
  17.0 10.9 %collective-permute-start.4 = (bf16[64,512]{1,0:T(8,128)(2,1)S(1)}, bf16[64,512]{1,0:T(8,128)(2,1)S(1)}, u32[]{:S(2)}, u32[]{:S(2)}) collective-permute-start(bf16[64,512]{1,0:T(8,128)(2,1)S(1)} %get-tuple-element.29), channel_id=1, source_target_pairs={{8,0},{12,4},{0,8},{4,12},{9,1},{13,5},{1,9},{5,13},{10,2},{14,6},... | collective-permute-start | bytes 196616 | tf_op jit(solution)/shard_map/ppermute | solution.py:215
  19.1 8.8 %collective-permute-start.5 = (bf16[64,512]{1,0:T(8,128)(2,1)S(1)}, bf16[64,512]{1,0:T(8,128)(2,1)S(1)}, u32[]{:S(2)}, u32[]{:S(2)}) collective-permute-start(bf16[64,512]{1,0:T(8,128)(2,1)S(1)} %get-tuple-element.30), channel_id=1, source_target_pairs={{6,0},{4,2},{2,4},{0,6},{14,8},{12,10},{10,12},{8,14},{7,1},{5,3},... | collective-permute-start | bytes 196616 | tf_op jit(solution)/shard_map/ppermute | solution.py:215
  21.4 6.7 %collective-permute-start.6 = (bf16[64,512]{1,0:T(8,128)(2,1)S(1)}, bf16[64,512]{1,0:T(8,128)(2,1)S(1)}, u32[]{:S(2)}, u32[]{:S(2)}) collective-permute-start(bf16[64,512]{1,0:T(8,128)(2,1)S(1)} %get-tuple-element.31), channel_id=1, source_target_pairs={{4,0},{0,4},{12,8},{8,12},{5,1},{1,5},{13,9},{9,13},{6,2},{2,6},{1... | collective-permute-start | bytes 196616 | tf_op jit(solution)/shard_map/ppermute | solution.py:215
  23.0 5.1 %collective-permute-start.7 = (bf16[64,512]{1,0:T(8,128)(2,1)S(1)}, bf16[64,512]{1,0:T(8,128)(2,1)S(1)}, u32[]{:S(2)}, u32[]{:S(2)}) collective-permute-start(bf16[64,512]{1,0:T(8,128)(2,1)S(1)} %get-tuple-element.32), channel_id=1, source_target_pairs={{2,0},{0,2},{3,1},{1,3},{6,4},{4,6},{7,5},{5,7},{10,8},{8,10},{11,... | collective-permute-start | bytes 196616 | tf_op jit(solution)/shard_map/ppermute | solution.py:215
  28.1 5.2 %collective-permute-start.9 = (bf16[64,512]{1,0:T(8,128)(2,1)S(1)}, bf16[64,512]{1,0:T(8,128)(2,1)S(1)}, u32[]{:S(2)}, u32[]{:S(2)}) collective-permute-start(bf16[64,512]{1,0:T(8,128)(2,1)S(1)} %sum_first_sigma.1.refs_0_), channel_id=1, source_target_pairs={{4,0},{0,4},{12,8},{8,12},{5,1},{1,5},{13,9},{9,13},{6,2},{2,6},{1... | collective-permute-start | bytes 196616 | tf_op jit(solution)/shard_map/ppermute | solution.py:215
  29.9 5.7 %collective-permute-start.11 = (bf16[64,512]{1,0:T(8,128)(2,1)S(1)}, bf16[64,512]{1,0:T(8,128)(2,1)S(1)}, u32[]{:S(2)}, u32[]{:S(2)}) collective-permute-start(bf16[64,512]{1,0:T(8,128)(2,1)S(1)} %sum_first_sigma.1.refs_0_), channel_id=1, source_target_pairs={{8,0},{12,4},{0,8},{4,12},{9,1},{13,5},{1,9},{5,13},{10,2},{14,6},... | collective-permute-start | bytes 196616 | tf_op jit(solution)/shard_map/ppermute | solution.py:215
  32.1 6.1 %collective-permute-start.13 = (bf16[64,512]{1,0:T(8,128)(2,1)S(1)}, bf16[64,512]{1,0:T(8,128)(2,1)S(1)}, u32[]{:S(2)}, u32[]{:S(2)}) collective-permute-start(bf16[64,512]{1,0:T(8,128)(2,1)S(1)} %sum_first_sigma.1.refs_0_), channel_id=1, source_target_pairs={{12,0},{8,4},{4,8},{0,12},{13,1},{9,5},{5,9},{1,13},{14,2},{10,6},... | collective-permute-start | bytes 196616 | tf_op jit(solution)/shard_map/ppermute | solution.py:215
  32.8 6.1 %collective-permute-start.8 = (bf16[64,512]{1,0:T(8,128)(2,1)S(1)}, bf16[64,512]{1,0:T(8,128)(2,1)S(1)}, u32[]{:S(2)}, u32[]{:S(2)}) collective-permute-start(bf16[64,512]{1,0:T(8,128)(2,1)S(1)} %sum_first_sigma.1.refs_0_), channel_id=1, source_target_pairs={{2,0},{0,2},{3,1},{1,3},{6,4},{4,6},{7,5},{5,7},{10,8},{8,10},{11,... | collective-permute-start | bytes 196616 | tf_op jit(solution)/shard_map/ppermute | solution.py:215
  33.3 5.6 %collective-permute-start.10 = (bf16[64,512]{1,0:T(8,128)(2,1)S(1)}, bf16[64,512]{1,0:T(8,128)(2,1)S(1)}, u32[]{:S(2)}, u32[]{:S(2)}) collective-permute-start(bf16[64,512]{1,0:T(8,128)(2,1)S(1)} %collective-permute-done.9.refs_2_), channel_id=1, source_target_pairs={{2,0},{0,2},{3,1},{1,3},{6,4},{4,6},{7,5},{5,7},{10,8},{8,10},{11,... | collective-permute-start | bytes 196616 | tf_op jit(solution)/shard_map/ppermute | solution.py:215
  35.6 4.3 %collective-permute-start.12 = (bf16[64,512]{1,0:T(8,128)(2,1)S(1)}, bf16[64,512]{1,0:T(8,128)(2,1)S(1)}, u32[]{:S(2)}, u32[]{:S(2)}) collective-permute-start(bf16[64,512]{1,0:T(8,128)(2,1)S(1)} %collective-permute-done.11.refs_4_), channel_id=1, source_target_pairs={{2,0},{0,2},{3,1},{1,3},{6,4},{4,6},{7,5},{5,7},{10,8},{8,10},{11,... | collective-permute-start | bytes 196616 | tf_op jit(solution)/shard_map/ppermute | solution.py:215
  38.1 4.3 %collective-permute-start.14 = (bf16[64,512]{1,0:T(8,128)(2,1)S(1)}, bf16[64,512]{1,0:T(8,128)(2,1)S(1)}, u32[]{:S(2)}, u32[]{:S(2)}) collective-permute-start(bf16[64,512]{1,0:T(8,128)(2,1)S(1)} %collective-permute-done.13.refs_6_), channel_id=1, source_target_pairs={{2,0},{0,2},{3,1},{1,3},{6,4},{4,6},{7,5},{5,7},{10,8},{8,10},{11,... | collective-permute-start | bytes 196616 | tf_op jit(solution)/shard_map/ppermute | solution.py:215
  42.5 2.0 %collective-permute-start.15 = (bf16[2,256,512]{2,1,0:T(8,128)(2,1)S(1)}, bf16[2,256,512]{2,1,0:T(8,128)(2,1)S(1)}, u32[]{:S(2)}, u32[]{:S(2)}) collective-permute-start(bf16[2,256,512]{2,1,0:T(8,128)(2,1)S(1)} %join_first_sigma.1.sigma_own.own), channel_id=1, source_target_pairs={{1,0},{0,1},{3,2},{2,3},{5,4},{4,5},{7,6},{6,7},{9,8},{8,9},{11,10... | collective-permute-start | bytes 1572872 | tf_op jit(solution)/shard_map/ppermute | solution.py:215
  47.4 6.8 %collective-permute-start.17 = (bf16[64,512]{1,0:T(8,128)(2,1)S(1)}, bf16[64,512]{1,0:T(8,128)(2,1)S(1)}, u32[]{:S(2)}, u32[]{:S(2)}) collective-permute-start(bf16[64,512]{1,0:T(8,128)(2,1)S(1)} %get-tuple-element.37), channel_id=1, source_target_pairs={{12,0},{8,4},{4,8},{0,12},{13,1},{9,5},{5,9},{1,13},{14,2},{10,6},... | collective-permute-start | bytes 196616 | tf_op jit(solution)/shard_map/ppermute | solution.py:215
  49.4 6.8 %collective-permute-start.18 = (bf16[64,512]{1,0:T(8,128)(2,1)S(1)}, bf16[64,512]{1,0:T(8,128)(2,1)S(1)}, u32[]{:S(2)}, u32[]{:S(2)}) collective-permute-start(bf16[64,512]{1,0:T(8,128)(2,1)S(1)} %get-tuple-element.38), channel_id=1, source_target_pairs={{8,0},{12,4},{0,8},{4,12},{9,1},{13,5},{1,9},{5,13},{10,2},{14,6},... | collective-permute-start | bytes 196616 | tf_op jit(solution)/shard_map/ppermute | solution.py:215
  49.4 6.8 %collective-permute-start.19 = (bf16[64,512]{1,0:T(8,128)(2,1)S(1)}, bf16[64,512]{1,0:T(8,128)(2,1)S(1)}, u32[]{:S(2)}, u32[]{:S(2)}) collective-permute-start(bf16[64,512]{1,0:T(8,128)(2,1)S(1)} %get-tuple-element.39), channel_id=1, source_target_pairs={{4,0},{0,4},{12,8},{8,12},{5,1},{1,5},{13,9},{9,13},{6,2},{2,6},{1... | collective-permute-start | bytes 196616 | tf_op jit(solution)/shard_map/ppermute | solution.py:215
  56.2 10.2 %collective-permute-start.20 = (bf16[64,512]{1,0:T(8,128)(2,1)S(1)}, bf16[64,512]{1,0:T(8,128)(2,1)S(1)}, u32[]{:S(2)}, u32[]{:S(2)}) collective-permute-start(bf16[64,512]{1,0:T(8,128)(2,1)S(1)} %sum_second_sigma.1.refs_0_), channel_id=1, source_target_pairs={{4,0},{0,4},{12,8},{8,12},{5,1},{1,5},{13,9},{9,13},{6,2},{2,6},{1... | collective-permute-start | bytes 196616 | tf_op jit(solution)/shard_map/ppermute | solution.py:215
  56.4 10.0 %collective-permute-start.21 = (bf16[64,512]{1,0:T(8,128)(2,1)S(1)}, bf16[64,512]{1,0:T(8,128)(2,1)S(1)}, u32[]{:S(2)}, u32[]{:S(2)}) collective-permute-start(bf16[64,512]{1,0:T(8,128)(2,1)S(1)} %sum_second_sigma.1.refs_0_), channel_id=1, source_target_pairs={{8,0},{12,4},{0,8},{4,12},{9,1},{13,5},{1,9},{5,13},{10,2},{14,6},... | collective-permute-start | bytes 196616 | tf_op jit(solution)/shard_map/ppermute | solution.py:215
  58.8 7.6 %collective-permute-start.22 = (bf16[64,512]{1,0:T(8,128)(2,1)S(1)}, bf16[64,512]{1,0:T(8,128)(2,1)S(1)}, u32[]{:S(2)}, u32[]{:S(2)}) collective-permute-start(bf16[64,512]{1,0:T(8,128)(2,1)S(1)} %sum_second_sigma.1.refs_0_), channel_id=1, source_target_pairs={{12,0},{8,4},{4,8},{0,12},{13,1},{9,5},{5,9},{1,13},{14,2},{10,6},... | collective-permute-start | bytes 196616 | tf_op jit(solution)/shard_map/ppermute | solution.py:215
  61.2 3.8 %collective-permute-start.16 = (f32[3,8,128]{2,1,0:T(8,128)S(1)}, f32[3,8,128]{2,1,0:T(8,128)S(1)}, u32[]{:S(2)}, u32[]{:S(2)}) collective-permute-start(f32[3,8,128]{2,1,0:T(8,128)S(1)} %sums_for_rayleigh.1.refs_0_), channel_id=1, source_target_pairs={{2,0},{0,2},{3,1},{1,3},{6,4},{4,6},{7,5},{5,7},{10,8},{8,10},{11,... | collective-permute-start | bytes 36872 | tf_op jit(solution)/shard_map/ppermute | solution.py:215

commit v4 on v3

v4 whole, which is shorter than its diff:
```python
import jax
import jax.numpy as jnp
from jax import lax
from jax.experimental import pallas as pl
from jax.experimental.pallas import tpu as pltpu
from jax.sharding import PartitionSpec as P

epsilon = 1e-06
mebibyte = 1024 * 1024


def mixing_scalar(pairs_ref, weights_ref, term, target, source):
    value = jnp.float32(0.0)
    for pair in range(weights_ref.shape[1]):
        hit = (pairs_ref[term, 1, pair] == target) & (pairs_ref[term, 0, pair] == source)
        value = value + jnp.where(hit, weights_ref[term, pair], jnp.float32(0.0))
    return value


def live_cells(sizes_ref, sector, row_start, rows, columns):
    row = row_start + lax.broadcasted_iota(jnp.int32, (rows, columns), 0)
    column = lax.broadcasted_iota(jnp.int32, (rows, columns), 1)
    return (row < sizes_ref[sector, 0]) & (column < sizes_ref[sector, 1])


def masked(values, live):
    return jnp.where(live, values.astype(jnp.float32), 0.0).astype(values.dtype)


def times_right(values, right):
    return lax.dot_general(
        values.astype(jnp.bfloat16),
        right,
        (((1,), (1,)), ((), ())),
        preferred_element_type=jnp.float32,
    )


def start_operators(left_ref, right_ref, left, right, sems):
    rows = left.shape[1]
    start = pl.multiple_of(lax.axis_index("rep") * rows, rows)
    copies = []
    for term in range(left.shape[0]):
        pair = (
            pltpu.make_async_copy(
                left_ref.at[term, pl.ds(start, rows)], left.at[term], sems.at[0, term]
            ),
            pltpu.make_async_copy(right_ref.at[term], right.at[term], sems.at[1, term]),
        )
        for copy in pair:
            copy.start()
        copies.append(pair)
    return copies


def halves(rows):
    half = rows // 2
    kept = pl.multiple_of((lax.axis_index("ops") & 1) * half, half)
    given = pl.multiple_of(((lax.axis_index("ops") & 1) ^ 1) * half, half)
    return kept, given


def first_kernel(sectors, *refs):
    sizes_ref, pairs_ref, weights_ref, left_ref, right_ref, own_ref, arrived = refs[:7]
    wave, *parts = refs[7 : 8 + 2 * sectors]
    left, right, held, sems, own, own_sem = refs[8 + 2 * sectors :]
    rows, columns = own.shape[1:]
    half = rows // 2
    own_copy = pltpu.make_async_copy(own_ref, own, own_sem)
    own_copy.start()
    copies = start_operators(left_ref, right_ref, left, right, sems)
    sector = lax.axis_index("sec")
    core = lax.axis_index("rep")
    for piece, place in ((arrived, core ^ 1), (own, core)):
        if piece is own:
            own_copy.wait()
        start = pl.multiple_of(place * rows, rows)
        live = live_cells(sizes_ref, sector, start, rows, columns)
        wave[pl.ds(start, rows), :] = masked(piece[0], live)
    totals = [None] * sectors
    for term in range(right.shape[0]):
        copies[term][0].wait()
        product = jnp.dot(left[term], wave[...], preferred_element_type=jnp.float32)
        copies[term][1].wait()
        product = times_right(product, right[term])
        for step in range(sectors):
            weight = mixing_scalar(pairs_ref, weights_ref, term, sector ^ step, sector)
            part = weight * product
            totals[step] = part if totals[step] is None else totals[step] + part
    for step in range(sectors):
        live = live_cells(sizes_ref, sector ^ step, core * rows, rows, columns)
        held[step] = jnp.where(live, totals[step], 0.0)
    for index, out in enumerate(parts):
        start = halves(rows)[index // sectors]
        out[...] = held[index % sectors, pl.ds(start, half), :].astype(out.dtype)


def sum_kernel(count, *refs):
    total = refs[0][...].astype(jnp.float32)
    for piece in refs[1:count]:
        total = total + piece[...].astype(jnp.float32)
    refs[-1][...] = total.astype(refs[-1].dtype)


def join_halves_kernel(*refs):
    pieces, joined = refs[:-1], refs[-1]
    sectors, rows, _ = joined.shape
    sector = lax.axis_index("sec")
    starts = halves(rows)
    for index, piece in enumerate(pieces):
        along, across = index // sectors, index % sectors
        joined[sector ^ across, pl.ds(starts[along], rows // 2), :] = piece[...]


def second_kernel(
    sizes_ref, pairs_ref, weights_ref, left_ref, right_ref, own, arrived,
    sigma, kept, given,
    left, right, held, sems,
):
    sectors, rows, columns = own.shape
    copies = start_operators(left_ref, right_ref, left, right, sems)
    target = lax.axis_index("sec")
    core = lax.axis_index("rep")
    for piece, place in ((own, core), (arrived, core ^ 1)):
        sigma[:, pl.ds(pl.multiple_of(place * rows, rows), rows), :] = piece[...]
    total = None
    for term in range(right.shape[0]):
        combined = None
        copies[term][0].wait()
        for source in range(sectors):
            weight = mixing_scalar(pairs_ref, weights_ref, term, target, source)
            part = weight * jnp.dot(
                left[term], sigma[source], preferred_element_type=jnp.float32
            )
            combined = part if combined is None else combined + part
        copies[term][1].wait()
        part = times_right(combined, right[term])
        total = part if total is None else total + part
    live = live_cells(sizes_ref, target, core * rows, rows, columns)
    held[...] = jnp.where(live, total, 0.0)
    for out, start in zip((kept, given), halves(rows)):
        out[...] = held[pl.ds(start, rows // 2), :].astype(out.dtype)


def sums_kernel(wave, sigma, out):
    sector = lax.axis_index("sec")
    step, columns = 16, wave.shape[1]

    def add_rows(block, carry):
        start = pl.multiple_of(block * step, step)
        w = wave[pl.ds(start, step), :].astype(jnp.float32)
        s = sigma[sector, pl.ds(start, step), :].astype(jnp.float32)
        return (carry[0] + w * s, carry[1] + w * w, carry[2] + s * s)

    sums = (jnp.zeros((step, columns), jnp.float32),) * 3
    sums = lax.fori_loop(0, wave.shape[0] // step, add_rows, sums, unroll=2)
    for index, value in enumerate(sums):
        out[index] = jnp.broadcast_to(jnp.sum(value, keepdims=True), out.shape[1:])


def wave_kernel(sizes_ref, wave, sigma, *refs):
    sums, (second, factors) = refs[:-2], refs[-2:]
    rows, columns = second.shape[1:]
    live_count = jnp.float32(0.0)
    for sector in range(sizes_ref.shape[0]):
        live_count = live_count + sizes_ref[sector, 0].astype(jnp.float32) * sizes_ref[
            sector, 1
        ].astype(jnp.float32)
    total = sums[0][...]
    for other in sums[1:]:
        total = total + other[...]
    correlation, norm_square, sigma_square = total[0], total[1], total[2]
    rayleigh = correlation / norm_square
    residual_square = (
        sigma_square - 2.0 * rayleigh * correlation + rayleigh * rayleigh * norm_square
    )
    residual_square = jnp.maximum(residual_square, 0.0)
    scale = 1.0 / jnp.sqrt(residual_square / live_count + epsilon)
    factors[0] = scale
    factors[1] = rayleigh * scale
    sigma_factor = jnp.broadcast_to(scale[:1, :1], (rows, columns))
    wave_factor = jnp.broadcast_to((rayleigh * scale)[:1, :1], (rows, columns))
    mine = pl.ds(pl.multiple_of(lax.axis_index("rep") * rows, rows), rows)
    values = sigma_factor * sigma[lax.axis_index("sec"), mine, :].astype(jnp.float32)
    values = values - wave_factor * wave[mine, :].astype(jnp.float32)
    second[0] = values.astype(second.dtype)


def join_kernel(factors, sigma, *refs):
    pieces, out = refs[:-1], refs[-1]
    rows, columns = out.shape[1:]
    half = rows // 2
    sector = lax.axis_index("sec")
    first = lax.axis_index("rep") * rows
    scale = jnp.broadcast_to(factors[0][:1, :1], (half, columns))
    shift = jnp.broadcast_to(factors[1][:1, :1], (half, columns))
    for start, piece in zip(halves(rows), pieces):
        mine = pl.ds(pl.multiple_of(first + start, half), half)
        moved = shift * sigma[sector, mine, :].astype(jnp.float32)
        out[0, pl.ds(start, half), :] = scale * piece[...].astype(jnp.float32) - moved


def partner(value, steps):
    steps = {axis: step for axis, step in steps.items() if step}
    if not steps:
        return value
    axes = tuple(steps)
    places = [()]
    for axis in axes:
        places = [place + (i,) for place in places for i in range(lax.axis_size(axis))]
    index = {place: i for i, place in enumerate(places)}
    pairs = [
        (index[tuple(i ^ steps[axis] for i, axis in zip(place, axes))], index[place])
        for place in places
    ]
    return lax.ppermute(value, axes, pairs)


def local(wavefunction, sector_sizes, left_blocks, right_blocks, sector_pairs, pair_weights):
    sectors = sector_sizes.shape[0]
    ops_count = lax.axis_size("ops")
    _, rows, columns = wavefunction.shape
    terms, side = left_blocks.shape[0], left_blocks.shape[1]
    half = rows // 2
    bf16, f32 = jnp.bfloat16, jnp.float32
    smem = pl.BlockSpec(memory_space=pltpu.SMEM)
    outside = pl.BlockSpec(memory_space=pltpu.HBM)
    inside = pl.BlockSpec(memory_space=pltpu.VMEM)

    def shape(*dims, dtype=bf16):
        return jax.ShapeDtypeStruct(dims, dtype)

    def call(kernel, name, out_shape, in_specs, *operands, scratch=(), vmem=4):
        return pl.pallas_call(
            kernel,
            out_shape=out_shape,
            in_specs=list(in_specs) + [inside] * (len(operands) - len(in_specs)),
            out_specs=jax.tree.map(lambda _: inside, out_shape),
            scratch_shapes=list(scratch),
            compiler_params=pltpu.CompilerParams(vmem_limit_bytes=vmem * mebibyte),
            name=name,
        )(*operands)

    def summed(name, *pieces, after=()):
        count = len(pieces)
        return call(
            lambda *refs: sum_kernel(count, *refs), name, shape(half, columns), [], *pieces, *after
        )

    def doubled(name, value, after=()):
        step = 2
        while step < ops_count:
            value = summed(name, value, partner(value, {"ops": step}), after=after)
            step *= 2
        return value

    pairs = jnp.swapaxes(sector_pairs, 1, 2)
    operators = (sector_sizes, pairs, pair_weights, left_blocks, right_blocks)
    operator_specs = [smem] * 3 + [outside] * 2
    operator_scratch = [pltpu.VMEM((terms, rows, side), bf16), pltpu.VMEM(right_blocks.shape, bf16)]
    copy_sems = pltpu.SemaphoreType.DMA((2, terms))
    exact, sent = shape(half, columns, dtype=f32), shape(half, columns)

    wave, kept, *rest = call(
        lambda *refs: first_kernel(sectors, *refs),
        "first_sigma_terms",
        [shape(side, columns)] + ([exact] + [sent] * (sectors - 1)) * 2,
        operator_specs + [outside],
        *operators,
        wavefunction,
        partner(wavefunction, {"rep": 1}),
        scratch=operator_scratch + [
            pltpu.VMEM((sectors, rows, columns), f32),
            copy_sems,
            pltpu.VMEM((1, rows, columns), bf16),
            pltpu.SemaphoreType.DMA,
        ],
        vmem=51,
    )
    kept_parts, given, given_parts = rest[: sectors - 1], rest[sectors - 1], rest[sectors:]
    given_parts = [partner(part, {"sec": i}) for i, part in enumerate(given_parts, 1)]
    kept_parts = [partner(part, {"sec": i}) for i, part in enumerate(kept_parts, 1)]
    given = summed("sum_sectors", given, *given_parts)
    total = summed("sum_neighbours", kept, *kept_parts, partner(given, {"ops": 1}))
    total = doubled("sum_first_sigma", total)
    pieces = [
        partner(total, {"ops": along, "sec": across})
        for along in range(2)
        for across in range(sectors)
    ]
    joined = call(
        join_halves_kernel, "join_first_sigma", shape(sectors, rows, columns), [], *pieces
    )

    sigma, kept, given = call(
        second_kernel,
        "second_sigma_terms",
        [shape(sectors, side, columns), exact, sent],
        operator_specs,
        *operators,
        joined,
        partner(joined, {"rep": 1}),
        scratch=operator_scratch + [pltpu.VMEM((rows, columns), f32), copy_sems],
        vmem=51,
    )
    sums = call(sums_kernel, "sums_for_rayleigh", shape(3, 8, 128, dtype=f32), [], wave, sigma)
    second_wave, factors = call(
        wave_kernel,
        "second_wave",
        [shape(1, rows, columns), shape(2, 8, 128, dtype=f32)],
        [smem],
        sector_sizes,
        wave,
        sigma,
        *[partner(sums, {"sec": step}) for step in range(sectors)],
    )
    total = summed("sum_neighbours", kept, partner(given, {"ops": 1}), after=(sums,))
    total = doubled("sum_second_sigma", total, after=(factors,))
    second_sigma = call(
        join_kernel,
        "join_second_sigma",
        shape(1, rows, columns, dtype=f32),
        [],
        factors,
        sigma,
        total,
        partner(total, {"ops": 1}),
    )
    return (second_wave, second_sigma)


def solution(mesh):
    return jax.shard_map(
        local,
        mesh=mesh,
        in_specs=(
            P(("grp", "sec"), "rep", None),
            P("grp", None),
            P(("grp", "ops"), None, None),
            P(("grp", "ops"), None, None),
            P(("grp", "ops"), None, None),
            P(("grp", "ops"), None),
        ),
        out_specs=(P(("grp", "sec"), "rep", None), P(("grp", "sec"), "rep", None)),
        check_vma=False,
    )
```

time: 67.6 us -> 65.3 us (0.966)
  starting transfers between devices: 30 us -> 18.6 us
  waiting for transfers between devices: 21.4 us -> 30.7 us
  local copies, waits for them, and re-layouts: 5.6 us -> 3 us
  Pallas kernels: 9.6 us -> 12.1 us
    ppermute x23 -> x13, starting transfers between devices: 30 us -> 18.6 us  [partner(): return lax.ppermute(value, axes, pairs)]
    ppermute x23 -> x13, waiting for transfers between devices: 21.4 us -> 30.7 us  [partner(): return lax.ppermute(value, axes, pairs)]
    unnamed x13 -> x8, local copies, waits for them, and re-layouts: 5.6 us -> 3 us
    pallas_call x9 -> x11, Pallas kernels: 9.6 us -> 12.1 us  [call(): pl.pallas_call(kernel, out_shape=out_shape, in_specs=list(in_specs) + [in...]
  transfers between devices with their start and end apart: 23 -> 13, of which waited for: 12 -> 13; matrix products, arithmetic and copies ran while one was open for 1% -> 0% of each run, Pallas kernels for 4% -> 3%
where the time goes in v4:
time: 65.3 us; the launch traced here: 65.1 us
  waiting for transfers between devices  30.7 us (47%)
  starting transfers between devices  18.6 us (28%)
  Pallas kernels  12.1 us (19%)
  local copies, waits for them, and re-layouts  3 us (5%)
  between operations  0.7 us (1%)
    ppermute x13, waiting for transfers between devices, partner(): return lax.ppermute(value, axes, pairs)  30.7 us
    ppermute x13, starting transfers between devices, partner(): return lax.ppermute(value, axes, pairs)  18.6 us
    pallas_call x11, Pallas kernels, call(): pl.pallas_call(kernel, out_shape=out_shape, in_specs=list(in_specs) + [in...  12.1 us
    unnamed x8, local copies, waits for them, and re-layouts  3 us
  transfers between devices with their start and end apart: 13, of which 13 were waited for; matrix products, arithmetic and copies ran while one was open for 0% of the time, Pallas kernels for 3%

profile of v4, /device:TPU:0, one launch (start us, length us, event | category | flops | bytes accessed | tf_op | source)
XLA Modules:
  0.0 65.1 jit_solution(16935571258533370488)
XLA Ops:
  0.6 0.5 collective-permute-start
  1.1 1.4 %collective-permute-done.refs_6_ = bf16[1,256,512]{2,1,0:T(8,128)(2,1)S(1)} collective-permute-done((bf16[1,256,512]{2,1,0:T(8,128)(2,1)}, bf16[1,256,512]{2,1,0:T(8,128)(2,1)S(1)}, u32[]{:S(2)}, u32[]{:S(2)}) %collective-permute-start) | collective-permute-done | bytes 262176 | tf_op jit(solution)/shard_map/ppermute | solution.py:216
  2.5 0.0 copy-start
  2.5 0.9 %copy-done = bf16[1,256,512]{2,1,0:T(8,128)(2,1)S(1)} copy-done((bf16[1,256,512]{2,1,0:T(8,128)(2,1)S(1)}, bf16[1,256,512]{2,1,0:T(8,128)(2,1)}, u32[]{:S(2)}) %copy-start) | copy-done | bytes 262168
  3.5 0.0 copy-start.1
  3.5 0.7 %copy-done.1 = s32[4,8,2]{1,2,0:T(2,128)S(1)} copy-done((s32[4,8,2]{1,2,0:T(2,128)S(1)}, s32[4,8,2]{1,2,0:T(2,128)}, u32[]{:S(2)}) %copy-start.1) | copy-done | bytes 280
  4.2 0.0 copy-start.2
  4.2 0.7 %copy-done.2 = s32[2,2]{1,0:T(2,128)S(1)} copy-done((s32[2,2]{1,0:T(2,128)S(1)}, s32[2,2]{1,0:T(2,128)}, u32[]{:S(2)}) %copy-start.2) | copy-done | bytes 40
  4.8 0.0 copy-start.3
  4.8 0.7 %copy-done.3 = f32[4,8]{1,0:T(4,128)S(1)} copy-done((f32[4,8]{1,0:T(4,128)S(1)}, f32[4,8]{1,0:T(4,128)}, u32[]{:S(2)}) %copy-start.3) | copy-done | bytes 152
  5.5 4.5 %first_sigma_terms.1 = (bf16[512,512]{1,0:T(8,128)(2,1)S(1)}, f32[128,512]{1,0:T(8,128)S(1)}, bf16[128,512]{1,0:T(8,128)(2,1)S(1)}, f32[128,512]{1,0:T(8,128)S(1)}, bf16[128,512]{1,0:T(8,128)(2,1)S(1)}) custom-call(s32[2,2]{1,0:T(2,128)S(1)} %copy-done.2, s32[4,2,8]{2,1,0:T(2,128)S(1)} %bitcast.1, f32[4,8]{1,0:T(4,128)S(1)} %copy-done.3, ...), custom_call_target="tpu_custom_call" | custom-call | tf_op jit(solution)/shard_map/first_sigma_terms/pallas_call | solution.py:234
  10.0 2.9 %collective-permute-start.2 = (bf16[128,512]{1,0:T(8,128)(2,1)S(1)}, bf16[128,512]{1,0:T(8,128)(2,1)S(1)}, u32[]{:S(2)}, u32[]{:S(2)}) collective-permute-start(bf16[128,512]{1,0:T(8,128)(2,1)S(1)} %get-tuple-element.16), channel_id=1, source_target_pairs={{2,0},{0,2},{3,1},{1,3},{6,4},{4,6},{7,5},{5,7},{10,8},{8,10},{11,... | collective-permute-start | bytes 393224 | tf_op jit(solution)/shard_map/ppermute | solution.py:216
  12.9 0.1 collective-permute-start.1
  13.0 4.2 %collective-permute-done.2.refs_1_ = bf16[128,512]{1,0:T(8,128)(2,1)S(1)} collective-permute-done((bf16[128,512]{1,0:T(8,128)(2,1)S(1)}, bf16[128,512]{1,0:T(8,128)(2,1)S(1)}, u32[]{:S(2)}, u32[]{:S(2)}) %collective-permute-start.2) | collective-permute-done | bytes 131104 | tf_op jit(solution)/shard_map/ppermute | solution.py:216
  17.3 2.2 %collective-permute-start.3 = (bf16[128,512]{1,0:T(8,128)(2,1)S(1)}, bf16[128,512]{1,0:T(8,128)(2,1)S(1)}, u32[]{:S(2)}, u32[]{:S(2)}) collective-permute-start(bf16[128,512]{1,0:T(8,128)(2,1)S(1)} %sum_sectors.1), channel_id=1, source_target_pairs={{4,0},{0,4},{12,8},{8,12},{5,1},{1,5},{13,9},{9,13},{6,2},{2,6},{1... | collective-permute-start | bytes 393224 | tf_op jit(solution)/shard_map/ppermute | solution.py:216
  19.5 0.1 collective-permute-done.1.refs_1_
  19.6 2.9 %collective-permute-done.3.refs_2_ = bf16[128,512]{1,0:T(8,128)(2,1)S(1)} collective-permute-done((bf16[128,512]{1,0:T(8,128)(2,1)S(1)}, bf16[128,512]{1,0:T(8,128)(2,1)S(1)}, u32[]{:S(2)}, u32[]{:S(2)}) %collective-permute-start.3) | collective-permute-done | bytes 131104 | tf_op jit(solution)/shard_map/ppermute | solution.py:216
  22.5 3.1 %collective-permute-start.4 = (bf16[128,512]{1,0:T(8,128)(2,1)S(1)}, bf16[128,512]{1,0:T(8,128)(2,1)S(1)}, u32[]{:S(2)}, u32[]{:S(2)}) collective-permute-start(bf16[128,512]{1,0:T(8,128)(2,1)S(1)} %sum_neighbours.2.refs_0_), channel_id=1, source_target_pairs={{8,0},{12,4},{0,8},{4,12},{9,1},{13,5},{1,9},{5,13},{10,2},{14,6},... | collective-permute-start | bytes 393224 | tf_op jit(solution)/shard_map/ppermute | solution.py:216
  25.6 3.0 %collective-permute-done.4.refs_1_ = bf16[128,512]{1,0:T(8,128)(2,1)S(1)} collective-permute-done((bf16[128,512]{1,0:T(8,128)(2,1)S(1)}, bf16[128,512]{1,0:T(8,128)(2,1)S(1)}, u32[]{:S(2)}, u32[]{:S(2)}) %collective-permute-start.4) | collective-permute-done | bytes 131104 | tf_op jit(solution)/shard_map/ppermute | solution.py:216
  28.6 3.5 %collective-permute-start.7 = (bf16[128,512]{1,0:T(8,128)(2,1)S(1)}, bf16[128,512]{1,0:T(8,128)(2,1)S(1)}, u32[]{:S(2)}, u32[]{:S(2)}) collective-permute-start(bf16[128,512]{1,0:T(8,128)(2,1)S(1)} %sum_first_sigma.1.refs_0_), channel_id=1, source_target_pairs={{6,0},{4,2},{2,4},{0,6},{14,8},{12,10},{10,12},{8,14},{7,1},{5,3},... | collective-permute-start | bytes 393224 | tf_op jit(solution)/shard_map/ppermute | solution.py:216
  32.0 1.4 %collective-permute-start.6 = (bf16[128,512]{1,0:T(8,128)(2,1)S(1)}, bf16[128,512]{1,0:T(8,128)(2,1)S(1)}, u32[]{:S(2)}, u32[]{:S(2)}) collective-permute-start(bf16[128,512]{1,0:T(8,128)(2,1)S(1)} %sum_first_sigma.1.refs_0_), channel_id=1, source_target_pairs={{4,0},{0,4},{12,8},{8,12},{5,1},{1,5},{13,9},{9,13},{6,2},{2,6},{1... | collective-permute-start | bytes 393224 | tf_op jit(solution)/shard_map/ppermute | solution.py:216
  33.4 0.0 collective-permute-start.5
  33.4 1.6 %collective-permute-done.7.refs_3_ = bf16[128,512]{1,0:T(8,128)(2,1)S(1)} collective-permute-done((bf16[128,512]{1,0:T(8,128)(2,1)S(1)}, bf16[128,512]{1,0:T(8,128)(2,1)S(1)}, u32[]{:S(2)}, u32[]{:S(2)}) %collective-permute-start.7) | collective-permute-done | bytes 131104 | tf_op jit(solution)/shard_map/ppermute | solution.py:216
  35.0 2.8 %collective-permute-done.6.refs_2_ = bf16[128,512]{1,0:T(8,128)(2,1)S(1)} collective-permute-done((bf16[128,512]{1,0:T(8,128)(2,1)S(1)}, bf16[128,512]{1,0:T(8,128)(2,1)S(1)}, u32[]{:S(2)}, u32[]{:S(2)}) %collective-permute-start.6) | collective-permute-done | bytes 131104 | tf_op jit(solution)/shard_map/ppermute | solution.py:216
  37.8 0.6 collective-permute-done.5.refs_1_
  38.4 0.1 join_first_sigma.1.own
  38.4 0.1 collective-permute-start.8
  38.5 1.9 %collective-permute-done.8.arrived = bf16[2,256,512]{2,1,0:T(8,128)(2,1)S(1)} collective-permute-done((bf16[2,256,512]{2,1,0:T(8,128)(2,1)S(1)}, bf16[2,256,512]{2,1,0:T(8,128)(2,1)S(1)}, u32[]{:S(2)}, u32[]{:S(2)}) %collective-permute-start.8) | collective-permute-done | bytes 524320 | tf_op jit(solution)/shard_map/ppermute | solution.py:216
  40.4 4.5 %second_sigma_terms.1 = (bf16[2,512,512]{2,1,0:T(8,128)(2,1)S(1)}, f32[128,512]{1,0:T(8,128)S(1)}, bf16[128,512]{1,0:T(8,128)(2,1)S(1)}) custom-call(s32[2,2]{1,0:T(2,128)S(1)} %copy-done.2, s32[4,2,8]{2,1,0:T(2,128)S(1)} %bitcast.2, f32[4,8]{1,0:T(4,128)S(1)} %copy-done.3, bf16[4,512,512]{2,1,0:T(8,128)(2,1)} %left_ref.1, bf16[4,512,512]{2,1,0:T(8,128)(2,1)} %right_ref.1, ...), custom_call_target="tpu_custom_call" | custom-call | tf_op jit(solution)/shard_map/second_sigma_terms/pallas_call | solution.py:234
  44.9 0.7 %collective-permute-start.10 = (bf16[128,512]{1,0:T(8,128)(2,1)S(1)}, bf16[128,512]{1,0:T(8,128)(2,1)S(1)}, u32[]{:S(2)}, u32[]{:S(2)}) collective-permute-start(bf16[128,512]{1,0:T(8,128)(2,1)S(1)} %get-tuple-element.21), channel_id=1, source_target_pairs={{4,0},{0,4},{12,8},{8,12},{5,1},{1,5},{13,9},{9,13},{6,2},{2,6},{1... | collective-permute-start | bytes 393224 | tf_op jit(solution)/shard_map/ppermute | solution.py:216
  45.6 0.5 sums_for_rayleigh.1.refs_0_.refs_2_
  46.1 4.4 %collective-permute-done.10.refs_1_ = bf16[128,512]{1,0:T(8,128)(2,1)S(1)} collective-permute-done((bf16[128,512]{1,0:T(8,128)(2,1)S(1)}, bf16[128,512]{1,0:T(8,128)(2,1)S(1)}, u32[]{:S(2)}, u32[]{:S(2)}) %collective-permute-start.10) | collective-permute-done | bytes 131104 | tf_op jit(solution)/shard_map/ppermute | solution.py:216
  50.5 2.5 %collective-permute-start.11 = (bf16[128,512]{1,0:T(8,128)(2,1)S(1)}, bf16[128,512]{1,0:T(8,128)(2,1)S(1)}, u32[]{:S(2)}, u32[]{:S(2)}) collective-permute-start(bf16[128,512]{1,0:T(8,128)(2,1)S(1)} %sum_neighbours.3.refs_0_), channel_id=1, source_target_pairs={{8,0},{12,4},{0,8},{4,12},{9,1},{13,5},{1,9},{5,13},{10,2},{14,6},... | collective-permute-start | bytes 393224 | tf_op jit(solution)/shard_map/ppermute | solution.py:216
  53.0 0.8 %collective-permute-start.9 = (f32[3,8,128]{2,1,0:T(8,128)S(1)}, f32[3,8,128]{2,1,0:T(8,128)S(1)}, u32[]{:S(2)}, u32[]{:S(2)}) collective-permute-start(f32[3,8,128]{2,1,0:T(8,128)S(1)} %sums_for_rayleigh.1.refs_0_.refs_2_), channel_id=1, source_target_pairs={{2,0},{0,2},{3,1},{1,3},{6,4},{4,6},{7,5},{5,7},{10,8},{8,10},{11,... | collective-permute-start | bytes 36872 | tf_op jit(solution)/shard_map/ppermute | solution.py:216
  53.8 2.9 %collective-permute-done.9.refs_1_ = f32[3,8,128]{2,1,0:T(8,128)S(1)} collective-permute-done((f32[3,8,128]{2,1,0:T(8,128)S(1)}, f32[3,8,128]{2,1,0:T(8,128)S(1)}, u32[]{:S(2)}, u32[]{:S(2)}) %collective-permute-start.9) | collective-permute-done | bytes 12320 | tf_op jit(solution)/shard_map/ppermute | solution.py:216
  56.7 1.4 %second_wave.1 = (bf16[1,256,512]{2,1,0:T(8,128)(2,1)}, f32[2,8,128]{2,1,0:T(8,128)S(1)}) custom-call(s32[2,2]{1,0:T(2,128)S(1)} %copy-done.2, bf16[512,512]{1,0:T(8,128)(2,1)S(1)} %get-tuple-element.12.wave, bf16[2,512,512]{2,1,0:T(8,128)(2,1)S(1)} %get-tuple-element.17.sigma, f32[3,8,128]{2,1,0:T(8,128)S(1)} %sums_for_rayleigh.1.refs_0_.refs_2_, ...), custom_call_target="tpu_custom_call" | custom-call | tf_op jit(solution)/shard_map/second_wave/pallas_call | solution.py:234
  58.1 1.0 %collective-permute-done.11.refs_1_ = bf16[128,512]{1,0:T(8,128)(2,1)S(1)} collective-permute-done((bf16[128,512]{1,0:T(8,128)(2,1)S(1)}, bf16[128,512]{1,0:T(8,128)(2,1)S(1)}, u32[]{:S(2)}, u32[]{:S(2)}) %collective-permute-start.11) | collective-permute-done | bytes 131104 | tf_op jit(solution)/shard_map/ppermute | solution.py:216
  59.1 0.9 %collective-permute-start.12 = (bf16[128,512]{1,0:T(8,128)(2,1)S(1)}, bf16[128,512]{1,0:T(8,128)(2,1)S(1)}, u32[]{:S(2)}, u32[]{:S(2)}) collective-permute-start(bf16[128,512]{1,0:T(8,128)(2,1)S(1)} %sum_second_sigma.1.refs_0_), channel_id=1, source_target_pairs={{4,0},{0,4},{12,8},{8,12},{5,1},{1,5},{13,9},{9,13},{6,2},{2,6},{1... | collective-permute-start | bytes 393224 | tf_op jit(solution)/shard_map/ppermute | solution.py:216
  60.0 4.2 %collective-permute-done.12.refs_1_ = bf16[128,512]{1,0:T(8,128)(2,1)S(1)} collective-permute-done((bf16[128,512]{1,0:T(8,128)(2,1)S(1)}, bf16[128,512]{1,0:T(8,128)(2,1)S(1)}, u32[]{:S(2)}, u32[]{:S(2)}) %collective-permute-start.12) | collective-permute-done | bytes 131104 | tf_op jit(solution)/shard_map/ppermute | solution.py:216
  64.1 0.9 %join_second_sigma.1 = f32[1,256,512]{2,1,0:T(8,128)} custom-call(f32[2,8,128]{2,1,0:T(8,128)S(1)} %get-tuple-element.19.refs_2_.factors, bf16[2,512,512]{2,1,0:T(8,128)(2,1)S(1)} %get-tuple-element.17.sigma, bf16[128,512]{1,0:T(8,128)(2,1)S(1)} %sum_second_sigma.1.refs_0_, bf16[128,512]{1,0:T(8,128)(2,1)S(1)} %collective-permute-done.12.refs_1_), custom_call_target="tpu_custom_call" | custom-call | tf_op jit(solution)/shard_map/join_second_sigma/pallas_call | solution.py:234
  (5 shorter events, 0.2 us)
Async XLA Ops:
  0.6 1.9 %collective-permute-start = (bf16[1,256,512]{2,1,0:T(8,128)(2,1)}, bf16[1,256,512]{2,1,0:T(8,128)(2,1)S(1)}, u32[]{:S(2)}, u32[]{:S(2)}) collective-permute-start(bf16[1,256,512]{2,1,0:T(8,128)(2,1)} %refs_5_.1), channel_id=1, source_target_pairs={{1,0},{0,1},{3,2},{2,3},{5,4},{4,5},{7,6},{6,7},{9,8},{8,9},{11,10... | collective-permute-start | bytes 786440 | tf_op jit(solution)/shard_map/ppermute | solution.py:216
  2.5 0.9 %copy-start = (bf16[1,256,512]{2,1,0:T(8,128)(2,1)S(1)}, bf16[1,256,512]{2,1,0:T(8,128)(2,1)}, u32[]{:S(2)}) copy-start(bf16[1,256,512]{2,1,0:T(8,128)(2,1)} %refs_5_.1) | copy-start | bytes 786436
  3.5 0.7 %copy-start.1 = (s32[4,8,2]{1,2,0:T(2,128)S(1)}, s32[4,8,2]{1,2,0:T(2,128)}, u32[]{:S(2)}) copy-start(s32[4,8,2]{1,2,0:T(2,128)} %param.10) | copy-start | bytes 772
  4.2 0.7 %copy-start.2 = (s32[2,2]{1,0:T(2,128)S(1)}, s32[2,2]{1,0:T(2,128)}, u32[]{:S(2)}) copy-start(s32[2,2]{1,0:T(2,128)} %sizes_ref.3) | copy-start | bytes 52
  4.8 0.7 %copy-start.3 = (f32[4,8]{1,0:T(4,128)S(1)}, f32[4,8]{1,0:T(4,128)}, u32[]{:S(2)}) copy-start(f32[4,8]{1,0:T(4,128)} %weights_ref.1) | copy-start | bytes 388
  10.0 7.2 %collective-permute-start.2 = (bf16[128,512]{1,0:T(8,128)(2,1)S(1)}, bf16[128,512]{1,0:T(8,128)(2,1)S(1)}, u32[]{:S(2)}, u32[]{:S(2)}) collective-permute-start(bf16[128,512]{1,0:T(8,128)(2,1)S(1)} %get-tuple-element.16), channel_id=1, source_target_pairs={{2,0},{0,2},{3,1},{1,3},{6,4},{4,6},{7,5},{5,7},{10,8},{8,10},{11,... | collective-permute-start | bytes 393224 | tf_op jit(solution)/shard_map/ppermute | solution.py:216
  12.9 6.6 %collective-permute-start.1 = (bf16[128,512]{1,0:T(8,128)(2,1)S(1)}, bf16[128,512]{1,0:T(8,128)(2,1)S(1)}, u32[]{:S(2)}, u32[]{:S(2)}) collective-permute-start(bf16[128,512]{1,0:T(8,128)(2,1)S(1)} %get-tuple-element.14), channel_id=1, source_target_pairs={{2,0},{0,2},{3,1},{1,3},{6,4},{4,6},{7,5},{5,7},{10,8},{8,10},{11,... | collective-permute-start | bytes 393224 | tf_op jit(solution)/shard_map/ppermute | solution.py:216
  17.3 5.2 %collective-permute-start.3 = (bf16[128,512]{1,0:T(8,128)(2,1)S(1)}, bf16[128,512]{1,0:T(8,128)(2,1)S(1)}, u32[]{:S(2)}, u32[]{:S(2)}) collective-permute-start(bf16[128,512]{1,0:T(8,128)(2,1)S(1)} %sum_sectors.1), channel_id=1, source_target_pairs={{4,0},{0,4},{12,8},{8,12},{5,1},{1,5},{13,9},{9,13},{6,2},{2,6},{1... | collective-permute-start | bytes 393224 | tf_op jit(solution)/shard_map/ppermute | solution.py:216
  22.5 6.0 %collective-permute-start.4 = (bf16[128,512]{1,0:T(8,128)(2,1)S(1)}, bf16[128,512]{1,0:T(8,128)(2,1)S(1)}, u32[]{:S(2)}, u32[]{:S(2)}) collective-permute-start(bf16[128,512]{1,0:T(8,128)(2,1)S(1)} %sum_neighbours.2.refs_0_), channel_id=1, source_target_pairs={{8,0},{12,4},{0,8},{4,12},{9,1},{13,5},{1,9},{5,13},{10,2},{14,6},... | collective-permute-start | bytes 393224 | tf_op jit(solution)/shard_map/ppermute | solution.py:216
  28.6 6.4 %collective-permute-start.7 = (bf16[128,512]{1,0:T(8,128)(2,1)S(1)}, bf16[128,512]{1,0:T(8,128)(2,1)S(1)}, u32[]{:S(2)}, u32[]{:S(2)}) collective-permute-start(bf16[128,512]{1,0:T(8,128)(2,1)S(1)} %sum_first_sigma.1.refs_0_), channel_id=1, source_target_pairs={{6,0},{4,2},{2,4},{0,6},{14,8},{12,10},{10,12},{8,14},{7,1},{5,3},... | collective-permute-start | bytes 393224 | tf_op jit(solution)/shard_map/ppermute | solution.py:216
  32.0 5.7 %collective-permute-start.6 = (bf16[128,512]{1,0:T(8,128)(2,1)S(1)}, bf16[128,512]{1,0:T(8,128)(2,1)S(1)}, u32[]{:S(2)}, u32[]{:S(2)}) collective-permute-start(bf16[128,512]{1,0:T(8,128)(2,1)S(1)} %sum_first_sigma.1.refs_0_), channel_id=1, source_target_pairs={{4,0},{0,4},{12,8},{8,12},{5,1},{1,5},{13,9},{9,13},{6,2},{2,6},{1... | collective-permute-start | bytes 393224 | tf_op jit(solution)/shard_map/ppermute | solution.py:216
  33.4 5.0 %collective-permute-start.5 = (bf16[128,512]{1,0:T(8,128)(2,1)S(1)}, bf16[128,512]{1,0:T(8,128)(2,1)S(1)}, u32[]{:S(2)}, u32[]{:S(2)}) collective-permute-start(bf16[128,512]{1,0:T(8,128)(2,1)S(1)} %sum_first_sigma.1.refs_0_), channel_id=1, source_target_pairs={{2,0},{0,2},{3,1},{1,3},{6,4},{4,6},{7,5},{5,7},{10,8},{8,10},{11,... | collective-permute-start | bytes 393224 | tf_op jit(solution)/shard_map/ppermute | solution.py:216
  38.4 2.0 %collective-permute-start.8 = (bf16[2,256,512]{2,1,0:T(8,128)(2,1)S(1)}, bf16[2,256,512]{2,1,0:T(8,128)(2,1)S(1)}, u32[]{:S(2)}, u32[]{:S(2)}) collective-permute-start(bf16[2,256,512]{2,1,0:T(8,128)(2,1)S(1)} %join_first_sigma.1.own), channel_id=1, source_target_pairs={{1,0},{0,1},{3,2},{2,3},{5,4},{4,5},{7,6},{6,7},{9,8},{8,9},{11,10... | collective-permute-start | bytes 1572872 | tf_op jit(solution)/shard_map/ppermute | solution.py:216
  44.9 5.6 %collective-permute-start.10 = (bf16[128,512]{1,0:T(8,128)(2,1)S(1)}, bf16[128,512]{1,0:T(8,128)(2,1)S(1)}, u32[]{:S(2)}, u32[]{:S(2)}) collective-permute-start(bf16[128,512]{1,0:T(8,128)(2,1)S(1)} %get-tuple-element.21), channel_id=1, source_target_pairs={{4,0},{0,4},{12,8},{8,12},{5,1},{1,5},{13,9},{9,13},{6,2},{2,6},{1... | collective-permute-start | bytes 393224 | tf_op jit(solution)/shard_map/ppermute | solution.py:216
  50.5 8.6 %collective-permute-start.11 = (bf16[128,512]{1,0:T(8,128)(2,1)S(1)}, bf16[128,512]{1,0:T(8,128)(2,1)S(1)}, u32[]{:S(2)}, u32[]{:S(2)}) collective-permute-start(bf16[128,512]{1,0:T(8,128)(2,1)S(1)} %sum_neighbours.3.refs_0_), channel_id=1, source_target_pairs={{8,0},{12,4},{0,8},{4,12},{9,1},{13,5},{1,9},{5,13},{10,2},{14,6},... | collective-permute-start | bytes 393224 | tf_op jit(solution)/shard_map/ppermute | solution.py:216
  53.0 3.7 %collective-permute-start.9 = (f32[3,8,128]{2,1,0:T(8,128)S(1)}, f32[3,8,128]{2,1,0:T(8,128)S(1)}, u32[]{:S(2)}, u32[]{:S(2)}) collective-permute-start(f32[3,8,128]{2,1,0:T(8,128)S(1)} %sums_for_rayleigh.1.refs_0_.refs_2_), channel_id=1, source_target_pairs={{2,0},{0,2},{3,1},{1,3},{6,4},{4,6},{7,5},{5,7},{10,8},{8,10},{11,... | collective-permute-start | bytes 36872 | tf_op jit(solution)/shard_map/ppermute | solution.py:216
  59.1 5.0 %collective-permute-start.12 = (bf16[128,512]{1,0:T(8,128)(2,1)S(1)}, bf16[128,512]{1,0:T(8,128)(2,1)S(1)}, u32[]{:S(2)}, u32[]{:S(2)}) collective-permute-start(bf16[128,512]{1,0:T(8,128)(2,1)S(1)} %sum_second_sigma.1.refs_0_), channel_id=1, source_target_pairs={{4,0},{0,4},{12,8},{8,12},{5,1},{1,5},{13,9},{9,13},{6,2},{2,6},{1... | collective-permute-start | bytes 393224 | tf_op jit(solution)/shard_map/ppermute | solution.py:216

commit v5 on v3

--- a/solution.py
+++ b/solution.py
@@ -6,13 +6,13 @@
 from jax.sharding import PartitionSpec as P
 
 epsilon = 1e-06
-vmem_bytes = 24 * 1024 * 1024
+mebibyte = 1024 * 1024
 
 
 def mixing_scalar(pairs_ref, weights_ref, term, target, source):
     value = jnp.float32(0.0)
     for pair in range(weights_ref.shape[1]):
-        hit = (pairs_ref[term, pair, 1] == target) & (pairs_ref[term, pair, 0] == source)
+        hit = (pairs_ref[term, 1, pair] == target) & (pairs_ref[term, 0, pair] == source)
         value = value + jnp.where(hit, weights_ref[term, pair], jnp.float32(0.0))
     return value
 
@@ -42,43 +42,34 @@
     )
 
 
-def load_kernel(
-    sizes_ref, left_ref, right_ref, wave_ref,
-    left_own, left_other, right, wave_own,
-    sems,
-):
-    rows, columns = wave_own.shape
+def load_kernel(left_ref, right_ref, left_own, left_other, right, sems):
+    rows = left_own.shape[1]
     core = lax.axis_index("rep")
     own = pl.multiple_of(core * rows, rows)
     other = pl.multiple_of((core ^ 1) * rows, rows)
+    mine = left_ref.at[:, pl.ds(own, rows)]
     copies = [
-        pltpu.make_async_copy(wave_ref.at[0], wave_own, sems.at[0]),
-        pltpu.make_async_copy(
-            left_ref.at[:, pl.ds(own, rows), pl.ds(own, rows)], left_own, sems.at[1]
-        ),
-        pltpu.make_async_copy(
-            left_ref.at[:, pl.ds(own, rows), pl.ds(other, rows)], left_other, sems.at[2]
-        ),
-        pltpu.make_async_copy(right_ref, right, sems.at[3]),
+        pltpu.make_async_copy(mine.at[:, :, pl.ds(own, rows)], left_own, sems.at[0]),
+        pltpu.make_async_copy(mine.at[:, :, pl.ds(other, rows)], left_other, sems.at[1]),
+        pltpu.make_async_copy(right_ref, right, sems.at[2]),
     ]
     for copy in copies:
         copy.start()
-    copies[0].wait()
-    live = live_cells(sizes_ref, lax.axis_index("sec"), own, rows, columns)
-    wave_own[...] = masked(wave_own[...], live)
-    for copy in copies[1:]:
+    for copy in copies:
         copy.wait()
 
 
 def first_kernel(sectors, *refs):
-    sizes_ref, pairs_ref, weights_ref, left_own, left_other, right, own, arrived = refs[:8]
-    other, *shares = refs[8:-1]
+    sizes_ref, pairs_ref, weights_ref, left_own, left_other, right, wave, arrived = refs[:8]
+    own, other, *parts = refs[8:-1]
     held = refs[-1]
     rows, columns = own.shape
-    share = shares[0].shape[0]
+    share = parts[0].shape[1]
     sector = lax.axis_index("sec")
     core = lax.axis_index("rep")
     place = lax.axis_index("ops")
+    live = live_cells(sizes_ref, sector, core * rows, rows, columns)
+    own[...] = masked(wave[0], live)
     live = live_cells(sizes_ref, sector, (core ^ 1) * rows, rows, columns)
     other[...] = masked(arrived[0], live)
     totals = [None] * sectors
@@ -92,15 +83,37 @@
     for step in range(sectors):
         live = live_cells(sizes_ref, sector ^ step, core * rows, rows, columns)
         held[step] = jnp.where(live, totals[step], 0.0)
-    for index, out in enumerate(shares):
-        along, across = index // sectors, index % sectors
-        start = pl.multiple_of((place ^ along) * share, share)
-        out[...] = held[across, pl.ds(start, share), :].astype(out.dtype)
-
-
-def sum_kernel(own_ref, *refs):
+    for index, out in enumerate(parts):
+        first = 2 * (index // sectors)
+        for step in range(out.shape[0]):
+            start = pl.multiple_of((place ^ (first + step)) * share, share)
+            out[step] = held[index % sectors, pl.ds(start, share), :].astype(out.dtype)
+
+
+def far_kernel(sectors, *refs):
+    far, near = refs[:sectors], refs[sectors : 2 * sectors - 1]
+    sums, handed = refs[2 * sectors - 1 : -(sectors - 1)], refs[-(sectors - 1) :]
+    for step, out in enumerate(sums):
+        total = far[0][step]
+        for part in far[1:]:
+            total = total + part[step].astype(jnp.float32)
+        out[...] = total.astype(out.dtype)
+    for part, out in zip(near, handed):
+        out[...] = part[...]
+
+
+def near_kernel(*refs):
+    parts, (kept, given) = refs[:-2], refs[-2:]
+    total = parts[0][...]
+    for part in parts[1:]:
+        total = total + part[...].astype(jnp.float32)
+    kept[...] = total[0]
+    given[...] = total[1].astype(given.dtype)
+
+
+def sum_kernel(count, own_ref, *refs):
     total = own_ref[...]
-    for piece in refs[:-1]:
+    for piece in refs[:count]:
         total = total + piece[...].astype(jnp.float32)
     refs[-1][...] = total.astype(refs[-1].dtype)
 
@@ -111,7 +124,7 @@
     share = pieces[0].shape[0]
     sector = lax.axis_index("sec")
     place = lax.axis_index("ops")
-    for index, piece in enumerate(pieces):
+    for index, piece in enumerate(reversed(pieces)):
         along, across = index // sectors, index % sectors
         start = pl.multiple_of((place ^ along) * share, share)
         half[sector ^ across, pl.ds(start, share), :] = piece[...]
@@ -193,7 +206,7 @@
     place = lax.axis_index("ops")
     scale = jnp.broadcast_to(factors[0][:1, :1], (share, columns))
     shift = jnp.broadcast_to(factors[1][:1, :1], (share, columns))
-    for step, piece in enumerate(pieces):
+    for step, piece in enumerate(reversed(pieces)):
         start = pl.multiple_of((place ^ step) * share, share)
         sigma = sigma_own[sector, pl.ds(start, share), :].astype(jnp.float32)
         out[0, pl.ds(start, share), :] = scale * piece[...].astype(jnp.float32) - shift * sigma
@@ -229,64 +242,92 @@
     def shape(*dims, dtype=bf16):
         return jax.ShapeDtypeStruct(dims, dtype)
 
-    def call(kernel, name, out_shape, in_specs, *operands, scratch=()):
+    def call(kernel, name, out_shape, in_specs, *operands, scratch=(), vmem=16):
         return pl.pallas_call(
             kernel,
             out_shape=out_shape,
             in_specs=list(in_specs) + [inside] * (len(operands) - len(in_specs)),
             out_specs=jax.tree.map(lambda _: inside, out_shape),
             scratch_shapes=list(scratch),
-            compiler_params=pltpu.CompilerParams(vmem_limit_bytes=vmem_bytes),
+            compiler_params=pltpu.CompilerParams(vmem_limit_bytes=vmem * mebibyte),
             name=name,
         )(*operands)
 
-    def share_shapes(count):
-        return [shape(share, columns, dtype=f32)] + [shape(share, columns)] * (count - 1)
-
+    def summed(name, own, *pieces, after=()):
+        count = len(pieces)
+        return call(
+            lambda *refs: sum_kernel(count, *refs),
+            name,
+            shape(share, columns),
+            [],
+            own,
+            *pieces,
+            *after,
+        )
+
+    def parts(count):
+        return [shape(count, share, columns, dtype=f32)] + [shape(count, share, columns)] * (
+            sectors - 1
+        )
+
+    def across(values):
+        return [partner(value, {"sec": step}) for step, value in enumerate(values, 1)]
+
+    farthest_first = list(reversed(range(ops_count)))
+    far_steps = farthest_first[:-2]
     arrived = partner(wavefunction, {"rep": 1})
-    left_own, left_other, right, wave_own = call(
+    left_own, left_other, right = call(
         load_kernel,
         "load_operators",
         [
             shape(terms, rows, rows),
             shape(terms, rows, side - rows),
             shape(*right_blocks.shape),
-            shape(rows, columns),
         ],
-        [smem] + [outside] * 3,
-        sector_sizes,
+        [outside] * 2,
         left_blocks,
         right_blocks,
-        wavefunction,
-        scratch=[pltpu.SemaphoreType.DMA((4,))],
-    )
-    operators = (sector_sizes, sector_pairs, pair_weights, left_own, left_other, right)
-
-    wave_other, *shares = call(
+        scratch=[pltpu.SemaphoreType.DMA((3,))],
+        vmem=49,
+    )
+    pairs = jnp.swapaxes(sector_pairs, 1, 2)
+    operators = (sector_sizes, pairs, pair_weights, left_own, left_other, right)
+
+    wave_own, wave_other, *rest = call(
         lambda *refs: first_kernel(sectors, *refs),
         "first_sigma_terms",
-        [shape(rows, columns)] + share_shapes(ops_count * sectors),
+        [shape(rows, columns)] * 2 + parts(2) + parts(ops_count - 2),
         [smem] * 3,
         *operators,
-        wave_own,
+        wavefunction,
         arrived,
         scratch=[pltpu.VMEM((sectors, rows, columns), f32)],
     )
-    received = [
-        partner(shares[index], {"ops": index // sectors, "sec": index % sectors})
-        for index in reversed(range(1, ops_count * sectors))
-    ]
-    first_share = call(
-        sum_kernel, "sum_first_sigma", shape(share, columns), [], shares[0], *received
-    )
-    along = [None] * ops_count
-    for step in reversed(range(ops_count)):
-        along[step] = partner(first_share, {"ops": step})
-    pieces = [
-        partner(along[step], {"sec": across})
-        for step in range(ops_count)
-        for across in range(sectors)
-    ]
+    near, far = rest[:sectors], rest[sectors:]
+    sums = call(
+        lambda *refs: far_kernel(sectors, *refs),
+        "sum_far_shares",
+        [shape(share, columns)] * (ops_count - 2) + parts(2)[1:],
+        [],
+        far[0],
+        *across(far[1:]),
+        *near[1:],
+    )
+    far_sums, handed = sums[: ops_count - 2], sums[ops_count - 2 :]
+    kept, given = call(
+        near_kernel,
+        "sum_near_shares",
+        [shape(share, columns, dtype=f32), shape(share, columns)],
+        [],
+        near[0],
+        *across(handed),
+    )
+    received = [partner(far_sums[step - 2], {"ops": step}) for step in far_steps]
+    first_share = summed("sum_first_sigma", kept, *received, partner(given, {"ops": 1}))
+    pieces = []
+    for step in farthest_first:
+        along = partner(first_share, {"ops": step})
+        pieces += [partner(along, {"sec": i}) for i in reversed(range(sectors))]
     sigma_own = call(
         join_halves_kernel, "join_first_sigma", shape(sectors, rows, columns), [], *pieces
     )
@@ -295,14 +336,14 @@
     shares = call(
         second_kernel,
         "second_sigma_terms",
-        share_shapes(ops_count),
+        [shape(share, columns, dtype=f32)] + [shape(share, columns)] * (ops_count - 1),
         [smem] * 3,
         *operators,
         sigma_own,
         sigma_other,
         scratch=[pltpu.VMEM((rows, columns), f32)],
     )
-    received = [partner(shares[step], {"ops": step}) for step in reversed(range(1, ops_count))]
+    received = [partner(shares[step], {"ops": step}) for step in farthest_first[:-1]]
     sums = call(
         sums_kernel,
         "sums_for_rayleigh",
@@ -313,6 +354,7 @@
         sigma_own,
         sigma_other,
     )
+    second_share = summed("sum_second_sigma", shares[0], *received, after=(sums,))
     second_wave, factors = call(
         wave_kernel,
         "second_wave",
@@ -323,12 +365,6 @@
         sigma_own,
         *[partner(sums, {"sec": step}) for step in range(sectors)],
     )
-    second_share = call(
-        sum_kernel, "sum_second_sigma", shape(share, columns), [], shares[0], *received
-    )
-    pieces = [None] * ops_count
-    for step in reversed(range(ops_count)):
-        pieces[step] = partner(second_share, {"ops": step})
     second_sigma = call(
         join_kernel,
         "join_second_sigma",
@@ -336,7 +372,7 @@
         [],
         factors,
         sigma_own,
-        *pieces,
+        *[partner(second_share, {"ops": step}) for step in farthest_first],
     )
     return (second_wave, second_sigma)
 

time: 67.6 us -> 61.5 us (0.910)
  local copies, waits for them, and re-layouts: 5.6 us -> 0.02 us
  starting transfers between devices: 30 us -> 28 us
  waiting for transfers between devices: 21.4 us -> 22.3 us
    unnamed x13 -> x8, local copies, waits for them, and re-layouts: 5.6 us -> 0.02 us
    ppermute x23 -> x21, starting transfers between devices: 30 us -> 28 us  [partner(): return lax.ppermute(value, axes, pairs)]
    ppermute x23 -> x21, waiting for transfers between devices: 21.4 us -> 22.3 us  [partner(): return lax.ppermute(value, axes, pairs)]
    pallas_call x9 -> x11, Pallas kernels: 9.6 us -> 10.2 us  [call(): pl.pallas_call(kernel, out_shape=out_shape, in_specs=list(in_specs) + [in...]
  transfers between devices with their start and end apart: 23 -> 21, of which waited for: 12 -> 13; matrix products, arithmetic and copies ran while one was open for 1% -> 0% of each run, Pallas kernels for 4% -> 6%
where the time goes in v5:
time: 61.5 us; the launch traced here: 61.3 us
  starting transfers between devices  28 us (46%)
  waiting for transfers between devices  22.3 us (36%)
  Pallas kernels  10.2 us (17%)
  between operations  0.79 us (1%)
    ppermute x21, starting transfers between devices, partner(): return lax.ppermute(value, axes, pairs)  28 us
    ppermute x21, waiting for transfers between devices, partner(): return lax.ppermute(value, axes, pairs)  22.3 us
    pallas_call x11, Pallas kernels, call(): pl.pallas_call(kernel, out_shape=out_shape, in_specs=list(in_specs) + [in...  10.2 us
  transfers between devices with their start and end apart: 21, of which 13 were waited for; matrix products, arithmetic and copies ran while one was open for 0% of the time, Pallas kernels for 6%

profile of v5, /device:TPU:0, one launch (start us, length us, event | category | flops | bytes accessed | tf_op | source)
XLA Modules:
  0.0 61.3 jit_solution(16999413751184061514)
XLA Ops:
  0.6 0.0 copy-start
  0.6 0.0 copy-start.2
  0.7 0.0 copy-start.1
  0.7 0.0 copy-start.3
  0.7 0.5 collective-permute-start
  1.2 2.0 %load_operators.1 = (bf16[4,256,256]{2,1,0:T(8,128)(2,1)S(1)}, bf16[4,256,256]{2,1,0:T(8,128)(2,1)S(1)}, bf16[4,512,512]{2,1,0:T(8,128)(2,1)S(1)}) custom-call(bf16[4,512,512]{2,1,0:T(8,128)(2,1)} %left_ref.1, bf16[4,512,512]{2,1,0:T(8,128)(2,1)} %right_ref.1), custom_call_target="tpu_custom_call" | custom-call | tf_op jit(solution)/shard_map/load_operators/pallas_call | solution.py:246
  3.2 0.0 collective-permute-done.refs_7_
  3.2 0.0 copy-done
  3.2 0.0 copy-done.2
  3.2 0.0 copy-done.1
  3.2 0.0 copy-done.3
  3.2 2.5 %first_sigma_terms.1 = (bf16[256,512]{1,0:T(8,128)(2,1)S(1)}, bf16[256,512]{1,0:T(8,128)(2,1)S(1)}, f32[2,64,512]{2,1,0:T(8,128)S(1)}, bf16[2,64,512]{2,1,0:T(8,...) custom-call(s32[2,2]{1,0:T(2,128)S(1)} %copy-done.2, s32[4,2,8]{2,1,0:T(2,128)S(1)} %bitcast.1, ...), custom_call_target="tpu_custom_call" | custom-call | tf_op jit(solution)/shard_map/first_sigma_terms/pallas_call | solution.py:246
  5.7 2.6 %collective-permute-start.1 = (bf16[2,64,512]{2,1,0:T(8,128)(2,1)S(1)}, bf16[2,64,512]{2,1,0:T(8,128)(2,1)S(1)}, u32[]{:S(2)}, u32[]{:S(2)}) collective-permute-start(bf16[2,64,512]{2,1,0:T(8,128)(2,1)S(1)} %get-tuple-element.28), channel_id=1, source_target_pairs={{2,0},{0,2},{3,1},{1,3},{6,4},{4,6},{7,5},{5,7},{10,8},{8,10},{11,... | collective-permute-start | bytes 393224 | tf_op jit(solution)/shard_map/ppermute | solution.py:228
  8.3 4.1 %collective-permute-done.1.refs_1_ = bf16[2,64,512]{2,1,0:T(8,128)(2,1)S(1)} collective-permute-done((bf16[2,64,512]{2,1,0:T(8,128)(2,1)S(1)}, bf16[2,64,512]{2,1,0:T(8,128)(2,1)S(1)}, u32[]{:S(2)}, u32[]{:S(2)}) %collective-permute-start.1) | collective-permute-done | bytes 131104 | tf_op jit(solution)/shard_map/ppermute | solution.py:228
  12.5 1.8 %collective-permute-start.2 = (bf16[2,64,512]{2,1,0:T(8,128)(2,1)S(1)}, bf16[2,64,512]{2,1,0:T(8,128)(2,1)S(1)}, u32[]{:S(2)}, u32[]{:S(2)}) collective-permute-start(bf16[2,64,512]{2,1,0:T(8,128)(2,1)S(1)} %get-tuple-element.30), channel_id=1, source_target_pairs={{2,0},{0,2},{3,1},{1,3},{6,4},{4,6},{7,5},{5,7},{10,8},{8,10},{11,... | collective-permute-start | bytes 393224 | tf_op jit(solution)/shard_map/ppermute | solution.py:228
  14.3 3.6 %collective-permute-start.3 = (bf16[64,512]{1,0:T(8,128)(2,1)S(1)}, bf16[64,512]{1,0:T(8,128)(2,1)S(1)}, u32[]{:S(2)}, u32[]{:S(2)}) collective-permute-start(bf16[64,512]{1,0:T(8,128)(2,1)S(1)} %get-tuple-element.32), channel_id=1, source_target_pairs={{12,0},{8,4},{4,8},{0,12},{13,1},{9,5},{5,9},{1,13},{14,2},{10,6},... | collective-permute-start | bytes 196616 | tf_op jit(solution)/shard_map/ppermute | solution.py:228
  17.9 0.0 collective-permute-start.4
  17.9 0.0 collective-permute-done.2.refs_1_
  17.9 1.6 %collective-permute-start.5 = (bf16[64,512]{1,0:T(8,128)(2,1)S(1)}, bf16[64,512]{1,0:T(8,128)(2,1)S(1)}, u32[]{:S(2)}, u32[]{:S(2)}) collective-permute-start(bf16[64,512]{1,0:T(8,128)(2,1)S(1)} %get-tuple-element.34), channel_id=1, source_target_pairs={{4,0},{0,4},{12,8},{8,12},{5,1},{1,5},{13,9},{9,13},{6,2},{2,6},{1... | collective-permute-start | bytes 196616 | tf_op jit(solution)/shard_map/ppermute | solution.py:228
  19.6 1.5 %collective-permute-done.3.refs_1_ = bf16[64,512]{1,0:T(8,128)(2,1)S(1)} collective-permute-done((bf16[64,512]{1,0:T(8,128)(2,1)S(1)}, bf16[64,512]{1,0:T(8,128)(2,1)S(1)}, u32[]{:S(2)}, u32[]{:S(2)}) %collective-permute-start.3) | collective-permute-done | bytes 65568 | tf_op jit(solution)/shard_map/ppermute | solution.py:228
  21.0 2.1 %collective-permute-done.4.refs_2_ = bf16[64,512]{1,0:T(8,128)(2,1)S(1)} collective-permute-done((bf16[64,512]{1,0:T(8,128)(2,1)S(1)}, bf16[64,512]{1,0:T(8,128)(2,1)S(1)}, u32[]{:S(2)}, u32[]{:S(2)}) %collective-permute-start.4) | collective-permute-done | bytes 65568 | tf_op jit(solution)/shard_map/ppermute | solution.py:228
  23.2 0.2 collective-permute-done.5.refs_3_
  23.4 3.1 %collective-permute-start.6 = (bf16[64,512]{1,0:T(8,128)(2,1)S(1)}, bf16[64,512]{1,0:T(8,128)(2,1)S(1)}, u32[]{:S(2)}, u32[]{:S(2)}) collective-permute-start(bf16[64,512]{1,0:T(8,128)(2,1)S(1)} %sum_first_sigma.1.refs_7_), channel_id=1, source_target_pairs={{12,0},{8,4},{4,8},{0,12},{13,1},{9,5},{5,9},{1,13},{14,2},{10,6},... | collective-permute-start | bytes 196616 | tf_op jit(solution)/shard_map/ppermute | solution.py:228
  26.4 0.0 collective-permute-start.8
  26.4 1.4 %collective-permute-start.10 = (bf16[64,512]{1,0:T(8,128)(2,1)S(1)}, bf16[64,512]{1,0:T(8,128)(2,1)S(1)}, u32[]{:S(2)}, u32[]{:S(2)}) collective-permute-start(bf16[64,512]{1,0:T(8,128)(2,1)S(1)} %sum_first_sigma.1.refs_7_), channel_id=1, source_target_pairs={{4,0},{0,4},{12,8},{8,12},{5,1},{1,5},{13,9},{9,13},{6,2},{2,6},{1... | collective-permute-start | bytes 196616 | tf_op jit(solution)/shard_map/ppermute | solution.py:228
  27.8 1.0 %collective-permute-start.12 = (bf16[64,512]{1,0:T(8,128)(2,1)S(1)}, bf16[64,512]{1,0:T(8,128)(2,1)S(1)}, u32[]{:S(2)}, u32[]{:S(2)}) collective-permute-start(bf16[64,512]{1,0:T(8,128)(2,1)S(1)} %sum_first_sigma.1.refs_7_), channel_id=1, source_target_pairs={{2,0},{0,2},{3,1},{1,3},{6,4},{4,6},{7,5},{5,7},{10,8},{8,10},{11,... | collective-permute-start | bytes 196616 | tf_op jit(solution)/shard_map/ppermute | solution.py:228
  28.8 1.3 %collective-permute-done.6.refs_1_ = bf16[64,512]{1,0:T(8,128)(2,1)S(1)} collective-permute-done((bf16[64,512]{1,0:T(8,128)(2,1)S(1)}, bf16[64,512]{1,0:T(8,128)(2,1)S(1)}, u32[]{:S(2)}, u32[]{:S(2)}) %collective-permute-start.6) | collective-permute-done | bytes 65568 | tf_op jit(solution)/shard_map/ppermute | solution.py:228
  30.2 0.6 collective-permute-start.7
  30.7 0.9 %collective-permute-done.8.refs_3_ = bf16[64,512]{1,0:T(8,128)(2,1)S(1)} collective-permute-done((bf16[64,512]{1,0:T(8,128)(2,1)S(1)}, bf16[64,512]{1,0:T(8,128)(2,1)S(1)}, u32[]{:S(2)}, u32[]{:S(2)}) %collective-permute-start.8) | collective-permute-done | bytes 65568 | tf_op jit(solution)/shard_map/ppermute | solution.py:228
  31.6 1.0 %collective-permute-start.9 = (bf16[64,512]{1,0:T(8,128)(2,1)S(1)}, bf16[64,512]{1,0:T(8,128)(2,1)S(1)}, u32[]{:S(2)}, u32[]{:S(2)}) collective-permute-start(bf16[64,512]{1,0:T(8,128)(2,1)S(1)} %collective-permute-done.8.refs_3_), channel_id=1, source_target_pairs={{2,0},{0,2},{3,1},{1,3},{6,4},{4,6},{7,5},{5,7},{10,8},{8,10},{11,... | collective-permute-start | bytes 196616 | tf_op jit(solution)/shard_map/ppermute | solution.py:228
  32.6 0.0 collective-permute-done.10.refs_5_
  32.6 1.0 %collective-permute-start.11 = (bf16[64,512]{1,0:T(8,128)(2,1)S(1)}, bf16[64,512]{1,0:T(8,128)(2,1)S(1)}, u32[]{:S(2)}, u32[]{:S(2)}) collective-permute-start(bf16[64,512]{1,0:T(8,128)(2,1)S(1)} %collective-permute-done.10.refs_5_), channel_id=1, source_target_pairs={{2,0},{0,2},{3,1},{1,3},{6,4},{4,6},{7,5},{5,7},{10,8},{8,10},{11,... | collective-permute-start | bytes 196616 | tf_op jit(solution)/shard_map/ppermute | solution.py:228
  33.7 0.0 collective-permute-done.12.refs_6_
  33.7 1.5 %collective-permute-done.7.refs_0_ = bf16[64,512]{1,0:T(8,128)(2,1)S(1)} collective-permute-done((bf16[64,512]{1,0:T(8,128)(2,1)S(1)}, bf16[64,512]{1,0:T(8,128)(2,1)S(1)}, u32[]{:S(2)}, u32[]{:S(2)}) %collective-permute-start.7) | collective-permute-done | bytes 65568 | tf_op jit(solution)/shard_map/ppermute | solution.py:228
  35.1 1.3 %collective-permute-done.9.refs_2_ = bf16[64,512]{1,0:T(8,128)(2,1)S(1)} collective-permute-done((bf16[64,512]{1,0:T(8,128)(2,1)S(1)}, bf16[64,512]{1,0:T(8,128)(2,1)S(1)}, u32[]{:S(2)}, u32[]{:S(2)}) %collective-permute-start.9) | collective-permute-done | bytes 65568 | tf_op jit(solution)/shard_map/ppermute | solution.py:228
  36.5 0.7 %collective-permute-done.11.refs_4_ = bf16[64,512]{1,0:T(8,128)(2,1)S(1)} collective-permute-done((bf16[64,512]{1,0:T(8,128)(2,1)S(1)}, bf16[64,512]{1,0:T(8,128)(2,1)S(1)}, u32[]{:S(2)}, u32[]{:S(2)}) %collective-permute-start.11) | collective-permute-done | bytes 65568 | tf_op jit(solution)/shard_map/ppermute | solution.py:228
  37.2 0.1 collective-permute-start.13
  37.3 1.9 %collective-permute-done.13.sigma_other.other = bf16[2,256,512]{2,1,0:T(8,128)(2,1)S(1)} collective-permute-done((bf16[2,256,512]{2,1,0:T(8,128)(2,1)S(1)}, bf16[2,256,512]{2,1,0:T(8,128)(2,1)S(1)}, u32[]{:S(2)}, u32[]{:S(2)}) %collective-permute-start.13) | collective-permute-done | bytes 524320 | tf_op jit(solution)/shard_map/ppermute | solution.py:228
  39.2 2.7 %second_sigma_terms.1 = (f32[64,512]{1,0:T(8,128)S(1)}, bf16[64,512]{1,0:T(8,128)(2,1)S(1)}, bf16[64,512]{1,0:T(8,128)(2,1)S(1)}, bf16[64,512]{1,0:T(8,128)(2,1)S(1)}) custom-call(s32[2,2]{1,0:T(2,128)S(1)} %copy-done.2, s32[4,2,8]{2,1,0:T(2,128)S(1)} %bitcast.2, f32[4,8]{1,0:T(4,128)S(1)} %copy-done.3, ...), custom_call_target="tpu_custom_call" | custom-call | tf_op jit(solution)/shard_map/second_sigma_terms/pallas_call | solution.py:246
  41.9 2.0 %collective-permute-start.15 = (bf16[64,512]{1,0:T(8,128)(2,1)S(1)}, bf16[64,512]{1,0:T(8,128)(2,1)S(1)}, u32[]{:S(2)}, u32[]{:S(2)}) collective-permute-start(bf16[64,512]{1,0:T(8,128)(2,1)S(1)} %get-tuple-element.39), channel_id=1, source_target_pairs={{12,0},{8,4},{4,8},{0,12},{13,1},{9,5},{5,9},{1,13},{14,2},{10,6},... | collective-permute-start | bytes 196616 | tf_op jit(solution)/shard_map/ppermute | solution.py:228
  43.9 0.1 collective-permute-start.16
  44.1 2.3 %collective-permute-start.17 = (bf16[64,512]{1,0:T(8,128)(2,1)S(1)}, bf16[64,512]{1,0:T(8,128)(2,1)S(1)}, u32[]{:S(2)}, u32[]{:S(2)}) collective-permute-start(bf16[64,512]{1,0:T(8,128)(2,1)S(1)} %get-tuple-element.41), channel_id=1, source_target_pairs={{4,0},{0,4},{12,8},{8,12},{5,1},{1,5},{13,9},{9,13},{6,2},{2,6},{1... | collective-permute-start | bytes 196616 | tf_op jit(solution)/shard_map/ppermute | solution.py:228
  46.4 0.5 sums_for_rayleigh.1.refs_0_.refs_4_
  46.9 1.9 %collective-permute-done.15.refs_1_ = bf16[64,512]{1,0:T(8,128)(2,1)S(1)} collective-permute-done((bf16[64,512]{1,0:T(8,128)(2,1)S(1)}, bf16[64,512]{1,0:T(8,128)(2,1)S(1)}, u32[]{:S(2)}, u32[]{:S(2)}) %collective-permute-start.15) | collective-permute-done | bytes 65568 | tf_op jit(solution)/shard_map/ppermute | solution.py:228
  48.7 2.0 %collective-permute-done.16.refs_2_ = bf16[64,512]{1,0:T(8,128)(2,1)S(1)} collective-permute-done((bf16[64,512]{1,0:T(8,128)(2,1)S(1)}, bf16[64,512]{1,0:T(8,128)(2,1)S(1)}, u32[]{:S(2)}, u32[]{:S(2)}) %collective-permute-start.16) | collective-permute-done | bytes 65568 | tf_op jit(solution)/shard_map/ppermute | solution.py:228
  50.7 0.0 collective-permute-done.17.refs_3_
  50.8 2.0 %collective-permute-start.18 = (bf16[64,512]{1,0:T(8,128)(2,1)S(1)}, bf16[64,512]{1,0:T(8,128)(2,1)S(1)}, u32[]{:S(2)}, u32[]{:S(2)}) collective-permute-start(bf16[64,512]{1,0:T(8,128)(2,1)S(1)} %sum_second_sigma.1.refs_3_), channel_id=1, source_target_pairs={{12,0},{8,4},{4,8},{0,12},{13,1},{9,5},{5,9},{1,13},{14,2},{10,6},... | collective-permute-start | bytes 196616 | tf_op jit(solution)/shard_map/ppermute | solution.py:228
  52.8 0.0 collective-permute-start.19
  52.8 2.4 %collective-permute-start.20 = (bf16[64,512]{1,0:T(8,128)(2,1)S(1)}, bf16[64,512]{1,0:T(8,128)(2,1)S(1)}, u32[]{:S(2)}, u32[]{:S(2)}) collective-permute-start(bf16[64,512]{1,0:T(8,128)(2,1)S(1)} %sum_second_sigma.1.refs_3_), channel_id=1, source_target_pairs={{4,0},{0,4},{12,8},{8,12},{5,1},{1,5},{13,9},{9,13},{6,2},{2,6},{1... | collective-permute-start | bytes 196616 | tf_op jit(solution)/shard_map/ppermute | solution.py:228
  55.2 0.8 %collective-permute-start.14 = (f32[3,8,128]{2,1,0:T(8,128)S(1)}, f32[3,8,128]{2,1,0:T(8,128)S(1)}, u32[]{:S(2)}, u32[]{:S(2)}) collective-permute-start(f32[3,8,128]{2,1,0:T(8,128)S(1)} %sums_for_rayleigh.1.refs_0_.refs_4_), channel_id=1, source_target_pairs={{2,0},{0,2},{3,1},{1,3},{6,4},{4,6},{7,5},{5,7},{10,8},{8,10},{11,... | collective-permute-start | bytes 36872 | tf_op jit(solution)/shard_map/ppermute | solution.py:228
  56.0 2.9 %collective-permute-done.14.refs_1_ = f32[3,8,128]{2,1,0:T(8,128)S(1)} collective-permute-done((f32[3,8,128]{2,1,0:T(8,128)S(1)}, f32[3,8,128]{2,1,0:T(8,128)S(1)}, u32[]{:S(2)}, u32[]{:S(2)}) %collective-permute-start.14) | collective-permute-done | bytes 12320 | tf_op jit(solution)/shard_map/ppermute | solution.py:228
  58.9 1.4 %second_wave.1 = (bf16[1,256,512]{2,1,0:T(8,128)(2,1)}, f32[2,8,128]{2,1,0:T(8,128)S(1)}) custom-call(s32[2,2]{1,0:T(2,128)S(1)} %copy-done.2, bf16[256,512]{1,0:T(8,128)(2,1)S(1)} %get-tuple-element.25.wave_own, bf16[2,256,512]{2,1,0:T(8,128)(2,1)S(1)} %join_first_sigma.1.sigma_own.own, f32[3,8,128]{2,1,0:T(8,128)S(1)} %sums_for_rayleigh.1.refs_0_.refs_4_, ...), custom_call_target="tpu_custom_call" | custom-call | tf_op jit(solution)/shard_map/second_wave/pallas_call | solution.py:246
  60.4 0.0 collective-permute-done.18.refs_0_
  60.4 0.0 collective-permute-done.19.refs_1_
  60.4 0.0 collective-permute-done.20.refs_2_
  60.4 0.9 %join_second_sigma.1 = f32[1,256,512]{2,1,0:T(8,128)} custom-call(f32[2,8,128]{2,1,0:T(8,128)S(1)} %get-tuple-element.37.factors, bf16[2,256,512]{2,1,0:T(8,128)(2,1)S(1)} %join_first_sigma.1.sigma_own.own, bf16[64,512]{1,0:T(8,128)(2,1)S(1)} %collective-permute-done.18.refs_0_, bf16[64,512]{1,0:T(8,128)(2,1)S(1)} %collective-permute-done.19.refs_1_, ...), custom_call_target="tpu_custom_call" | custom-call | tf_op jit(solution)/shard_map/join_second_sigma/pallas_call | solution.py:246
  (5 shorter events, 0.2 us)
Async XLA Ops:
  0.6 2.5 %copy-start = (bf16[1,256,512]{2,1,0:T(8,128)(2,1)S(1)}, bf16[1,256,512]{2,1,0:T(8,128)(2,1)}, u32[]{:S(2)}) copy-start(bf16[1,256,512]{2,1,0:T(8,128)(2,1)} %refs_6_.1) | copy-start | bytes 786436
  0.6 2.5 %copy-start.2 = (s32[2,2]{1,0:T(2,128)S(1)}, s32[2,2]{1,0:T(2,128)}, u32[]{:S(2)}) copy-start(s32[2,2]{1,0:T(2,128)} %sizes_ref.3) | copy-start | bytes 52
  0.7 2.5 %copy-start.1 = (s32[4,8,2]{1,2,0:T(2,128)S(1)}, s32[4,8,2]{1,2,0:T(2,128)}, u32[]{:S(2)}) copy-start(s32[4,8,2]{1,2,0:T(2,128)} %param.10) | copy-start | bytes 772
  0.7 2.5 %copy-start.3 = (f32[4,8]{1,0:T(4,128)S(1)}, f32[4,8]{1,0:T(4,128)}, u32[]{:S(2)}) copy-start(f32[4,8]{1,0:T(4,128)} %weights_ref.1) | copy-start | bytes 388
  0.7 2.5 %collective-permute-start = (bf16[1,256,512]{2,1,0:T(8,128)(2,1)}, bf16[1,256,512]{2,1,0:T(8,128)(2,1)S(1)}, u32[]{:S(2)}, u32[]{:S(2)}) collective-permute-start(bf16[1,256,512]{2,1,0:T(8,128)(2,1)} %refs_6_.1), channel_id=1, source_target_pairs={{1,0},{0,1},{3,2},{2,3},{5,4},{4,5},{7,6},{6,7},{9,8},{8,9},{11,10... | collective-permute-start | bytes 786440 | tf_op jit(solution)/shard_map/ppermute | solution.py:228
  5.7 6.7 %collective-permute-start.1 = (bf16[2,64,512]{2,1,0:T(8,128)(2,1)S(1)}, bf16[2,64,512]{2,1,0:T(8,128)(2,1)S(1)}, u32[]{:S(2)}, u32[]{:S(2)}) collective-permute-start(bf16[2,64,512]{2,1,0:T(8,128)(2,1)S(1)} %get-tuple-element.28), channel_id=1, source_target_pairs={{2,0},{0,2},{3,1},{1,3},{6,4},{4,6},{7,5},{5,7},{10,8},{8,10},{11,... | collective-permute-start | bytes 393224 | tf_op jit(solution)/shard_map/ppermute | solution.py:228
  12.5 5.4 %collective-permute-start.2 = (bf16[2,64,512]{2,1,0:T(8,128)(2,1)S(1)}, bf16[2,64,512]{2,1,0:T(8,128)(2,1)S(1)}, u32[]{:S(2)}, u32[]{:S(2)}) collective-permute-start(bf16[2,64,512]{2,1,0:T(8,128)(2,1)S(1)} %get-tuple-element.30), channel_id=1, source_target_pairs={{2,0},{0,2},{3,1},{1,3},{6,4},{4,6},{7,5},{5,7},{10,8},{8,10},{11,... | collective-permute-start | bytes 393224 | tf_op jit(solution)/shard_map/ppermute | solution.py:228
  14.3 6.7 %collective-permute-start.3 = (bf16[64,512]{1,0:T(8,128)(2,1)S(1)}, bf16[64,512]{1,0:T(8,128)(2,1)S(1)}, u32[]{:S(2)}, u32[]{:S(2)}) collective-permute-start(bf16[64,512]{1,0:T(8,128)(2,1)S(1)} %get-tuple-element.32), channel_id=1, source_target_pairs={{12,0},{8,4},{4,8},{0,12},{13,1},{9,5},{5,9},{1,13},{14,2},{10,6},... | collective-permute-start | bytes 196616 | tf_op jit(solution)/shard_map/ppermute | solution.py:228
  17.9 5.2 %collective-permute-start.4 = (bf16[64,512]{1,0:T(8,128)(2,1)S(1)}, bf16[64,512]{1,0:T(8,128)(2,1)S(1)}, u32[]{:S(2)}, u32[]{:S(2)}) collective-permute-start(bf16[64,512]{1,0:T(8,128)(2,1)S(1)} %get-tuple-element.33), channel_id=1, source_target_pairs={{8,0},{12,4},{0,8},{4,12},{9,1},{13,5},{1,9},{5,13},{10,2},{14,6},... | collective-permute-start | bytes 196616 | tf_op jit(solution)/shard_map/ppermute | solution.py:228
  17.9 5.4 %collective-permute-start.5 = (bf16[64,512]{1,0:T(8,128)(2,1)S(1)}, bf16[64,512]{1,0:T(8,128)(2,1)S(1)}, u32[]{:S(2)}, u32[]{:S(2)}) collective-permute-start(bf16[64,512]{1,0:T(8,128)(2,1)S(1)} %get-tuple-element.34), channel_id=1, source_target_pairs={{4,0},{0,4},{12,8},{8,12},{5,1},{1,5},{13,9},{9,13},{6,2},{2,6},{1... | collective-permute-start | bytes 196616 | tf_op jit(solution)/shard_map/ppermute | solution.py:228
  23.4 6.8 %collective-permute-start.6 = (bf16[64,512]{1,0:T(8,128)(2,1)S(1)}, bf16[64,512]{1,0:T(8,128)(2,1)S(1)}, u32[]{:S(2)}, u32[]{:S(2)}) collective-permute-start(bf16[64,512]{1,0:T(8,128)(2,1)S(1)} %sum_first_sigma.1.refs_7_), channel_id=1, source_target_pairs={{12,0},{8,4},{4,8},{0,12},{13,1},{9,5},{5,9},{1,13},{14,2},{10,6},... | collective-permute-start | bytes 196616 | tf_op jit(solution)/shard_map/ppermute | solution.py:228
  26.4 5.2 %collective-permute-start.8 = (bf16[64,512]{1,0:T(8,128)(2,1)S(1)}, bf16[64,512]{1,0:T(8,128)(2,1)S(1)}, u32[]{:S(2)}, u32[]{:S(2)}) collective-permute-start(bf16[64,512]{1,0:T(8,128)(2,1)S(1)} %sum_first_sigma.1.refs_7_), channel_id=1, source_target_pairs={{8,0},{12,4},{0,8},{4,12},{9,1},{13,5},{1,9},{5,13},{10,2},{14,6},... | collective-permute-start | bytes 196616 | tf_op jit(solution)/shard_map/ppermute | solution.py:228
  26.4 6.2 %collective-permute-start.10 = (bf16[64,512]{1,0:T(8,128)(2,1)S(1)}, bf16[64,512]{1,0:T(8,128)(2,1)S(1)}, u32[]{:S(2)}, u32[]{:S(2)}) collective-permute-start(bf16[64,512]{1,0:T(8,128)(2,1)S(1)} %sum_first_sigma.1.refs_7_), channel_id=1, source_target_pairs={{4,0},{0,4},{12,8},{8,12},{5,1},{1,5},{13,9},{9,13},{6,2},{2,6},{1... | collective-permute-start | bytes 196616 | tf_op jit(solution)/shard_map/ppermute | solution.py:228
  27.8 5.9 %collective-permute-start.12 = (bf16[64,512]{1,0:T(8,128)(2,1)S(1)}, bf16[64,512]{1,0:T(8,128)(2,1)S(1)}, u32[]{:S(2)}, u32[]{:S(2)}) collective-permute-start(bf16[64,512]{1,0:T(8,128)(2,1)S(1)} %sum_first_sigma.1.refs_7_), channel_id=1, source_target_pairs={{2,0},{0,2},{3,1},{1,3},{6,4},{4,6},{7,5},{5,7},{10,8},{8,10},{11,... | collective-permute-start | bytes 196616 | tf_op jit(solution)/shard_map/ppermute | solution.py:228
  30.2 5.0 %collective-permute-start.7 = (bf16[64,512]{1,0:T(8,128)(2,1)S(1)}, bf16[64,512]{1,0:T(8,128)(2,1)S(1)}, u32[]{:S(2)}, u32[]{:S(2)}) collective-permute-start(bf16[64,512]{1,0:T(8,128)(2,1)S(1)} %collective-permute-done.6.refs_1_), channel_id=1, source_target_pairs={{2,0},{0,2},{3,1},{1,3},{6,4},{4,6},{7,5},{5,7},{10,8},{8,10},{11,... | collective-permute-start | bytes 196616 | tf_op jit(solution)/shard_map/ppermute | solution.py:228
  31.6 4.8 %collective-permute-start.9 = (bf16[64,512]{1,0:T(8,128)(2,1)S(1)}, bf16[64,512]{1,0:T(8,128)(2,1)S(1)}, u32[]{:S(2)}, u32[]{:S(2)}) collective-permute-start(bf16[64,512]{1,0:T(8,128)(2,1)S(1)} %collective-permute-done.8.refs_3_), channel_id=1, source_target_pairs={{2,0},{0,2},{3,1},{1,3},{6,4},{4,6},{7,5},{5,7},{10,8},{8,10},{11,... | collective-permute-start | bytes 196616 | tf_op jit(solution)/shard_map/ppermute | solution.py:228
  32.6 4.5 %collective-permute-start.11 = (bf16[64,512]{1,0:T(8,128)(2,1)S(1)}, bf16[64,512]{1,0:T(8,128)(2,1)S(1)}, u32[]{:S(2)}, u32[]{:S(2)}) collective-permute-start(bf16[64,512]{1,0:T(8,128)(2,1)S(1)} %collective-permute-done.10.refs_5_), channel_id=1, source_target_pairs={{2,0},{0,2},{3,1},{1,3},{6,4},{4,6},{7,5},{5,7},{10,8},{8,10},{11,... | collective-permute-start | bytes 196616 | tf_op jit(solution)/shard_map/ppermute | solution.py:228
  37.2 2.0 %collective-permute-start.13 = (bf16[2,256,512]{2,1,0:T(8,128)(2,1)S(1)}, bf16[2,256,512]{2,1,0:T(8,128)(2,1)S(1)}, u32[]{:S(2)}, u32[]{:S(2)}) collective-permute-start(bf16[2,256,512]{2,1,0:T(8,128)(2,1)S(1)} %join_first_sigma.1.sigma_own.own), channel_id=1, source_target_pairs={{1,0},{0,1},{3,2},{2,3},{5,4},{4,5},{7,6},{6,7},{9,8},{8,9},{11,10... | collective-permute-start | bytes 1572872 | tf_op jit(solution)/shard_map/ppermute | solution.py:228
  41.9 6.8 %collective-permute-start.15 = (bf16[64,512]{1,0:T(8,128)(2,1)S(1)}, bf16[64,512]{1,0:T(8,128)(2,1)S(1)}, u32[]{:S(2)}, u32[]{:S(2)}) collective-permute-start(bf16[64,512]{1,0:T(8,128)(2,1)S(1)} %get-tuple-element.39), channel_id=1, source_target_pairs={{12,0},{8,4},{4,8},{0,12},{13,1},{9,5},{5,9},{1,13},{14,2},{10,6},... | collective-permute-start | bytes 196616 | tf_op jit(solution)/shard_map/ppermute | solution.py:228
  43.9 6.8 %collective-permute-start.16 = (bf16[64,512]{1,0:T(8,128)(2,1)S(1)}, bf16[64,512]{1,0:T(8,128)(2,1)S(1)}, u32[]{:S(2)}, u32[]{:S(2)}) collective-permute-start(bf16[64,512]{1,0:T(8,128)(2,1)S(1)} %get-tuple-element.40), channel_id=1, source_target_pairs={{8,0},{12,4},{0,8},{4,12},{9,1},{13,5},{1,9},{5,13},{10,2},{14,6},... | collective-permute-start | bytes 196616 | tf_op jit(solution)/shard_map/ppermute | solution.py:228
  44.1 6.7 %collective-permute-start.17 = (bf16[64,512]{1,0:T(8,128)(2,1)S(1)}, bf16[64,512]{1,0:T(8,128)(2,1)S(1)}, u32[]{:S(2)}, u32[]{:S(2)}) collective-permute-start(bf16[64,512]{1,0:T(8,128)(2,1)S(1)} %get-tuple-element.41), channel_id=1, source_target_pairs={{4,0},{0,4},{12,8},{8,12},{5,1},{1,5},{13,9},{9,13},{6,2},{2,6},{1... | collective-permute-start | bytes 196616 | tf_op jit(solution)/shard_map/ppermute | solution.py:228
  50.8 9.6 %collective-permute-start.18 = (bf16[64,512]{1,0:T(8,128)(2,1)S(1)}, bf16[64,512]{1,0:T(8,128)(2,1)S(1)}, u32[]{:S(2)}, u32[]{:S(2)}) collective-permute-start(bf16[64,512]{1,0:T(8,128)(2,1)S(1)} %sum_second_sigma.1.refs_3_), channel_id=1, source_target_pairs={{12,0},{8,4},{4,8},{0,12},{13,1},{9,5},{5,9},{1,13},{14,2},{10,6},... | collective-permute-start | bytes 196616 | tf_op jit(solution)/shard_map/ppermute | solution.py:228
  52.8 7.6 %collective-permute-start.19 = (bf16[64,512]{1,0:T(8,128)(2,1)S(1)}, bf16[64,512]{1,0:T(8,128)(2,1)S(1)}, u32[]{:S(2)}, u32[]{:S(2)}) collective-permute-start(bf16[64,512]{1,0:T(8,128)(2,1)S(1)} %sum_second_sigma.1.refs_3_), channel_id=1, source_target_pairs={{8,0},{12,4},{0,8},{4,12},{9,1},{13,5},{1,9},{5,13},{10,2},{14,6},... | collective-permute-start | bytes 196616 | tf_op jit(solution)/shard_map/ppermute | solution.py:228
  52.8 7.6 %collective-permute-start.20 = (bf16[64,512]{1,0:T(8,128)(2,1)S(1)}, bf16[64,512]{1,0:T(8,128)(2,1)S(1)}, u32[]{:S(2)}, u32[]{:S(2)}) collective-permute-start(bf16[64,512]{1,0:T(8,128)(2,1)S(1)} %sum_second_sigma.1.refs_3_), channel_id=1, source_target_pairs={{4,0},{0,4},{12,8},{8,12},{5,1},{1,5},{13,9},{9,13},{6,2},{2,6},{1... | collective-permute-start | bytes 196616 | tf_op jit(solution)/shard_map/ppermute | solution.py:228
  55.2 3.7 %collective-permute-start.14 = (f32[3,8,128]{2,1,0:T(8,128)S(1)}, f32[3,8,128]{2,1,0:T(8,128)S(1)}, u32[]{:S(2)}, u32[]{:S(2)}) collective-permute-start(f32[3,8,128]{2,1,0:T(8,128)S(1)} %sums_for_rayleigh.1.refs_0_.refs_4_), channel_id=1, source_target_pairs={{2,0},{0,2},{3,1},{1,3},{6,4},{4,6},{7,5},{5,7},{10,8},{8,10},{11,... | collective-permute-start | bytes 36872 | tf_op jit(solution)/shard_map/ppermute | solution.py:228

commit v6 on v5

--- a/solution.py
+++ b/solution.py
@@ -59,12 +59,13 @@
         copy.wait()
 
 
-def first_kernel(sectors, *refs):
+def first_kernel(shares, *refs):
     sizes_ref, pairs_ref, weights_ref, left_own, left_other, right, wave, arrived = refs[:8]
     own, other, *parts = refs[8:-1]
     held = refs[-1]
     rows, columns = own.shape
-    share = parts[0].shape[1]
+    share = parts[0].shape[0]
+    sectors = held.shape[0]
     sector = lax.axis_index("sec")
     core = lax.axis_index("rep")
     place = lax.axis_index("ops")
@@ -83,32 +84,9 @@
     for step in range(sectors):
         live = live_cells(sizes_ref, sector ^ step, core * rows, rows, columns)
         held[step] = jnp.where(live, totals[step], 0.0)
-    for index, out in enumerate(parts):
-        first = 2 * (index // sectors)
-        for step in range(out.shape[0]):
-            start = pl.multiple_of((place ^ (first + step)) * share, share)
-            out[step] = held[index % sectors, pl.ds(start, share), :].astype(out.dtype)
-
-
-def far_kernel(sectors, *refs):
-    far, near = refs[:sectors], refs[sectors : 2 * sectors - 1]
-    sums, handed = refs[2 * sectors - 1 : -(sectors - 1)], refs[-(sectors - 1) :]
-    for step, out in enumerate(sums):
-        total = far[0][step]
-        for part in far[1:]:
-            total = total + part[step].astype(jnp.float32)
-        out[...] = total.astype(out.dtype)
-    for part, out in zip(near, handed):
-        out[...] = part[...]
-
-
-def near_kernel(*refs):
-    parts, (kept, given) = refs[:-2], refs[-2:]
-    total = parts[0][...]
-    for part in parts[1:]:
-        total = total + part[...].astype(jnp.float32)
-    kept[...] = total[0]
-    given[...] = total[1].astype(given.dtype)
+    for (along, across), out in zip(shares, parts):
+        start = pl.multiple_of((place ^ along) * share, share)
+        out[...] = held[across, pl.ds(start, share), :].astype(out.dtype)
 
 
 def sum_kernel(count, own_ref, *refs):
@@ -118,34 +96,38 @@
     refs[-1][...] = total.astype(refs[-1].dtype)
 
 
-def join_halves_kernel(*refs):
+def place_kernel(spots, *refs):
     pieces, half = refs[:-1], refs[-1]
-    sectors = half.shape[0]
     share = pieces[0].shape[0]
-    sector = lax.axis_index("sec")
     place = lax.axis_index("ops")
-    for index, piece in enumerate(reversed(pieces)):
-        along, across = index // sectors, index % sectors
+    for (along, index), piece in zip(spots, pieces):
         start = pl.multiple_of((place ^ along) * share, share)
-        half[sector ^ across, pl.ds(start, share), :] = piece[...]
+        half[index, pl.ds(start, share), :] = piece[...]
+
+
+def left_kernel(left_own, left_other, own, other, out):
+    for term in range(out.shape[0]):
+        out[term] = left_times(left_own, left_other, term, own[0], other[0])
 
 
 def second_kernel(
-    sizes_ref, pairs_ref, weights_ref, left_own, left_other, right, own, other, *refs
+    sizes_ref, pairs_ref, weights_ref, left_own, left_other, right, products, own, other, *refs
 ):
     shares, held = refs[:-1], refs[-1]
-    sectors, rows, columns = own.shape
+    rows, columns = own.shape[1:]
     share = shares[0].shape[0]
     target = lax.axis_index("sec")
     core = lax.axis_index("rep")
     place = lax.axis_index("ops")
     total = None
     for term in range(right.shape[0]):
-        combined = None
-        for source in range(sectors):
-            weight = mixing_scalar(pairs_ref, weights_ref, term, target, source)
-            part = weight * left_times(left_own, left_other, term, own[source], other[source])
-            combined = part if combined is None else combined + part
+        weight = mixing_scalar(pairs_ref, weights_ref, term, target, target)
+        combined = weight * products[term]
+        for step in range(own.shape[0]):
+            weight = mixing_scalar(pairs_ref, weights_ref, term, target, target ^ (step + 1))
+            combined = combined + weight * left_times(
+                left_own, left_other, term, own[step], other[step]
+            )
         part = times_right(combined, right, term)
         total = part if total is None else total + part
     live = live_cells(sizes_ref, target, core * rows, rows, columns)
@@ -156,7 +138,6 @@
 
 
 def sums_kernel(wave_own, wave_other, sigma_own, sigma_other, out):
-    sector = lax.axis_index("sec")
     step, columns = 16, wave_own.shape[1]
     sums = (jnp.zeros((step, columns), jnp.float32),) * 3
     for wave, sigma in ((wave_own, sigma_own), (wave_other, sigma_other)):
@@ -164,7 +145,7 @@
         def add_rows(block, carry):
             start = pl.multiple_of(block * step, step)
             w = wave[pl.ds(start, step), :].astype(jnp.float32)
-            s = sigma[sector, pl.ds(start, step), :].astype(jnp.float32)
+            s = sigma[0, pl.ds(start, step), :].astype(jnp.float32)
             return (carry[0] + w * s, carry[1] + w * w, carry[2] + s * s)
 
         sums = lax.fori_loop(0, wave.shape[0] // step, add_rows, sums, unroll=2)
@@ -194,7 +175,7 @@
     factors[1] = rayleigh * scale
     sigma_factor = jnp.broadcast_to(scale[:1, :1], (rows, columns))
     wave_factor = jnp.broadcast_to((rayleigh * scale)[:1, :1], (rows, columns))
-    sigma = sigma_own[lax.axis_index("sec")].astype(jnp.float32)
+    sigma = sigma_own[0].astype(jnp.float32)
     wave = wave_own[...].astype(jnp.float32)
     second[0] = (sigma_factor * sigma - wave_factor * wave).astype(second.dtype)
 
@@ -202,13 +183,12 @@
 def join_kernel(factors, sigma_own, *refs):
     pieces, out = refs[:-1], refs[-1]
     share, columns = pieces[0].shape
-    sector = lax.axis_index("sec")
     place = lax.axis_index("ops")
     scale = jnp.broadcast_to(factors[0][:1, :1], (share, columns))
     shift = jnp.broadcast_to(factors[1][:1, :1], (share, columns))
     for step, piece in enumerate(reversed(pieces)):
         start = pl.multiple_of((place ^ step) * share, share)
-        sigma = sigma_own[sector, pl.ds(start, share), :].astype(jnp.float32)
+        sigma = sigma_own[0, pl.ds(start, share), :].astype(jnp.float32)
         out[0, pl.ds(start, share), :] = scale * piece[...].astype(jnp.float32) - shift * sigma
 
 
@@ -264,14 +244,6 @@
             *pieces,
             *after,
         )
-
-    def parts(count):
-        return [shape(count, share, columns, dtype=f32)] + [shape(count, share, columns)] * (
-            sectors - 1
-        )
-
-    def across(values):
-        return [partner(value, {"sec": step}) for step, value in enumerate(values, 1)]
 
     farthest_first = list(reversed(range(ops_count)))
     far_steps = farthest_first[:-2]
@@ -293,54 +265,77 @@
     pairs = jnp.swapaxes(sector_pairs, 1, 2)
     operators = (sector_sizes, pairs, pair_weights, left_own, left_other, right)
 
+    spots = [(along, across) for along in farthest_first for across in range(sectors)]
     wave_own, wave_other, *rest = call(
-        lambda *refs: first_kernel(sectors, *refs),
+        lambda *refs: first_kernel(spots, *refs),
         "first_sigma_terms",
-        [shape(rows, columns)] * 2 + parts(2) + parts(ops_count - 2),
+        [shape(rows, columns)] * 2
+        + [
+            shape(share, columns, dtype=f32 if across == 0 and along != 1 else bf16)
+            for along, across in spots
+        ],
         [smem] * 3,
         *operators,
         wavefunction,
         arrived,
         scratch=[pltpu.VMEM((sectors, rows, columns), f32)],
     )
-    near, far = rest[:sectors], rest[sectors:]
-    sums = call(
-        lambda *refs: far_kernel(sectors, *refs),
-        "sum_far_shares",
-        [shape(share, columns)] * (ops_count - 2) + parts(2)[1:],
-        [],
-        far[0],
-        *across(far[1:]),
-        *near[1:],
-    )
-    far_sums, handed = sums[: ops_count - 2], sums[ops_count - 2 :]
-    kept, given = call(
-        near_kernel,
-        "sum_near_shares",
-        [shape(share, columns, dtype=f32), shape(share, columns)],
-        [],
-        near[0],
-        *across(handed),
-    )
-    received = [partner(far_sums[step - 2], {"ops": step}) for step in far_steps]
-    first_share = summed("sum_first_sigma", kept, *received, partner(given, {"ops": 1}))
-    pieces = []
-    for step in farthest_first:
-        along = partner(first_share, {"ops": step})
-        pieces += [partner(along, {"sec": i}) for i in reversed(range(sectors))]
+    rest = dict(zip(spots, rest))
+    received = []
+    for along in far_steps:
+        parts = [partner(rest[along, across], {"sec": across}) for across in range(sectors)]
+        received.append(partner(summed("sum_far_share", *parts), {"ops": along}))
+    received += [
+        partner(rest[along, across], {"ops": along, "sec": across})
+        for along in (1, 0)
+        for across in range(sectors)
+        if along or across
+    ]
+    first_share = summed("sum_first_sigma", rest[0, 0], *received)
+    along_ops = {along: partner(first_share, {"ops": along}) for along in farthest_first}
     sigma_own = call(
-        join_halves_kernel, "join_first_sigma", shape(sectors, rows, columns), [], *pieces
+        lambda *refs: place_kernel([(along, 0) for along in farthest_first], *refs),
+        "place_own_sector",
+        shape(1, rows, columns),
+        [],
+        *along_ops.values(),
     )
     sigma_other = partner(sigma_own, {"rep": 1})
-
+    spots = [(along, across) for along in farthest_first for across in range(1, sectors)]
+    pieces = [
+        partner(first_share, {"ops": along, "sec": across})
+        if along < 2
+        else partner(along_ops[along], {"sec": across})
+        for along, across in spots
+    ]
+    across_own = call(
+        lambda *refs: place_kernel([(along, across - 1) for along, across in spots], *refs),
+        "place_other_sectors",
+        shape(sectors - 1, rows, columns),
+        [],
+        *pieces,
+    )
+    across_other = partner(across_own, {"rep": 1})
+
+    products = call(
+        left_kernel,
+        "left_products",
+        shape(terms, rows, columns, dtype=f32),
+        [],
+        left_own,
+        left_other,
+        sigma_own,
+        sigma_other,
+    )
     shares = call(
         second_kernel,
         "second_sigma_terms",
         [shape(share, columns, dtype=f32)] + [shape(share, columns)] * (ops_count - 1),
         [smem] * 3,
         *operators,
-        sigma_own,
-        sigma_other,
+        products,
+        across_own,
+        across_other,
         scratch=[pltpu.VMEM((rows, columns), f32)],
     )
     received = [partner(shares[step], {"ops": step}) for step in farthest_first[:-1]]
@@ -354,7 +349,8 @@
         sigma_own,
         sigma_other,
     )
-    second_share = summed("sum_second_sigma", shares[0], *received, after=(sums,))
+    sums = [partner(sums, {"sec": step}) for step in range(sectors)]
+    second_share = summed("sum_second_sigma", shares[0], *received, after=sums)
     second_wave, factors = call(
         wave_kernel,
         "second_wave",
@@ -363,7 +359,7 @@
         sector_sizes,
         wave_own,
         sigma_own,
-        *[partner(sums, {"sec": step}) for step in range(sectors)],
+        *sums,
     )
     second_sigma = call(
         join_kernel,

time: 61.5 us -> 58 us (0.943)
  waiting for transfers between devices: 22.3 us -> 16.6 us
  starting transfers between devices: 28 us -> 30.1 us
    ppermute x21 -> x24, waiting for transfers between devices: 22.3 us -> 16.6 us  [partner(): return lax.ppermute(value, axes, pairs)]
    ppermute x21 -> x24, starting transfers between devices: 28 us -> 30.1 us  [partner(): return lax.ppermute(value, axes, pairs)]
    pallas_call x11 -> x13, Pallas kernels: 10.2 us -> 10.4 us  [call(): pl.pallas_call(kernel, out_shape=out_shape, in_specs=list(in_specs) + [in...]
  transfers between devices with their start and end apart: 21 -> 24, of which waited for: 13 -> 12; matrix products, arithmetic and copies ran while one was open for 0% -> 0% of each run, Pallas kernels for 6% -> 8%
where the time goes in v6:
time: 58 us; the launch traced here: 57.9 us
  starting transfers between devices  30.1 us (52%)
  waiting for transfers between devices  16.6 us (29%)
  Pallas kernels  10.4 us (18%)
  between operations  0.84 us (1%)
    ppermute x24, starting transfers between devices, partner(): return lax.ppermute(value, axes, pairs)  30.1 us
    ppermute x24, waiting for transfers between devices, partner(): return lax.ppermute(value, axes, pairs)  16.6 us
    pallas_call x13, Pallas kernels, call(): pl.pallas_call(kernel, out_shape=out_shape, in_specs=list(in_specs) + [in...  10.4 us
  transfers between devices with their start and end apart: 24, of which 12 were waited for; matrix products, arithmetic and copies ran while one was open for 0% of the time, Pallas kernels for 8%

profile of v6, /device:TPU:0, one launch (start us, length us, event | category | flops | bytes accessed | tf_op | source)
XLA Modules:
  0.0 57.9 jit_solution(8794509693276566262)
XLA Ops:
  0.6 0.0 copy-start
  0.6 0.0 copy-start.2
  0.7 0.0 copy-start.3
  0.7 0.0 copy-start.1
  0.7 0.5 collective-permute-start
  1.2 2.0 %load_operators.1 = (bf16[4,256,256]{2,1,0:T(8,128)(2,1)S(1)}, bf16[4,256,256]{2,1,0:T(8,128)(2,1)S(1)}, bf16[4,512,512]{2,1,0:T(8,128)(2,1)S(1)}) custom-call(bf16[4,512,512]{2,1,0:T(8,128)(2,1)} %left_ref.1, bf16[4,512,512]{2,1,0:T(8,128)(2,1)} %right_ref.1), custom_call_target="tpu_custom_call" | custom-call | tf_op jit(solution)/shard_map/load_operators/pallas_call | solution.py:226
  3.2 0.0 collective-permute-done.refs_7_
  3.2 0.0 copy-done
  3.2 0.0 copy-done.2
  3.2 0.0 copy-done.3
  3.2 0.0 copy-done.1
  3.2 2.5 %first_sigma_terms.1 = (bf16[256,512]{1,0:T(8,128)(2,1)S(1)}, bf16[256,512]{1,0:T(8,128)(2,1)S(1)}, f32[64,512]{1,0:T(8,128)S(1)}, bf16[64,512]{1,0:T(8,128)(2,1...) custom-call(s32[2,2]{1,0:T(2,128)S(1)} %copy-done.2, ...), custom_call_target="tpu_custom_call" | custom-call | tf_op jit(solution)/shard_map/first_sigma_terms/pallas_call | solution.py:226
  5.7 2.6 %collective-permute-start.1 = (bf16[64,512]{1,0:T(8,128)(2,1)S(1)}, bf16[64,512]{1,0:T(8,128)(2,1)S(1)}, u32[]{:S(2)}, u32[]{:S(2)}) collective-permute-start(bf16[64,512]{1,0:T(8,128)(2,1)S(1)} %get-tuple-element.27), channel_id=1, source_target_pairs={{2,0},{0,2},{3,1},{1,3},{6,4},{4,6},{7,5},{5,7},{10,8},{8,10},{11,... | collective-permute-start | bytes 196616 | tf_op jit(solution)/shard_map/ppermute | solution.py:208
  8.3 0.1 collective-permute-start.3
  8.4 2.0 %collective-permute-start.5 = (bf16[64,512]{1,0:T(8,128)(2,1)S(1)}, bf16[64,512]{1,0:T(8,128)(2,1)S(1)}, u32[]{:S(2)}, u32[]{:S(2)}) collective-permute-start(bf16[64,512]{1,0:T(8,128)(2,1)S(1)} %get-tuple-element.30), channel_id=1, source_target_pairs={{4,0},{0,4},{12,8},{8,12},{5,1},{1,5},{13,9},{9,13},{6,2},{2,6},{1... | collective-permute-start | bytes 196616 | tf_op jit(solution)/shard_map/ppermute | solution.py:208
  10.4 1.4 %collective-permute-start.6 = (bf16[64,512]{1,0:T(8,128)(2,1)S(1)}, bf16[64,512]{1,0:T(8,128)(2,1)S(1)}, u32[]{:S(2)}, u32[]{:S(2)}) collective-permute-start(bf16[64,512]{1,0:T(8,128)(2,1)S(1)} %get-tuple-element.31), channel_id=1, source_target_pairs={{6,0},{4,2},{2,4},{0,6},{14,8},{12,10},{10,12},{8,14},{7,1},{5,3},... | collective-permute-start | bytes 196616 | tf_op jit(solution)/shard_map/ppermute | solution.py:208
  11.8 0.1 collective-permute-start.7
  11.9 0.0 collective-permute-done.1.refs_1_
  11.9 4.1 %collective-permute-start.2 = (bf16[64,512]{1,0:T(8,128)(2,1)S(1)}, bf16[64,512]{1,0:T(8,128)(2,1)S(1)}, u32[]{:S(2)}, u32[]{:S(2)}) collective-permute-start(bf16[64,512]{1,0:T(8,128)(2,1)S(1)} %sum_far_share.2), channel_id=1, source_target_pairs={{12,0},{8,4},{4,8},{0,12},{13,1},{9,5},{5,9},{1,13},{14,2},{10,6},... | collective-permute-start | bytes 196616 | tf_op jit(solution)/shard_map/ppermute | solution.py:208
  16.0 0.0 collective-permute-done.3.refs_1_
  16.1 0.1 collective-permute-start.4
  16.1 0.0 collective-permute-done.5.refs_3_
  16.1 0.0 collective-permute-done.6.refs_4_
  16.2 0.3 collective-permute-done.7.refs_5_
  16.5 2.7 %collective-permute-done.2.refs_1_ = bf16[64,512]{1,0:T(8,128)(2,1)S(1)} collective-permute-done((bf16[64,512]{1,0:T(8,128)(2,1)S(1)}, bf16[64,512]{1,0:T(8,128)(2,1)S(1)}, u32[]{:S(2)}, u32[]{:S(2)}) %collective-permute-start.2) | collective-permute-done | bytes 65568 | tf_op jit(solution)/shard_map/ppermute | solution.py:208
  19.1 2.1 %collective-permute-done.4.refs_2_ = bf16[64,512]{1,0:T(8,128)(2,1)S(1)} collective-permute-done((bf16[64,512]{1,0:T(8,128)(2,1)S(1)}, bf16[64,512]{1,0:T(8,128)(2,1)S(1)}, u32[]{:S(2)}, u32[]{:S(2)}) %collective-permute-start.4) | collective-permute-done | bytes 65568 | tf_op jit(solution)/shard_map/ppermute | solution.py:208
  21.3 0.1 sum_first_sigma.1.refs_3_
  21.3 1.6 %collective-permute-start.9 = (bf16[64,512]{1,0:T(8,128)(2,1)S(1)}, bf16[64,512]{1,0:T(8,128)(2,1)S(1)}, u32[]{:S(2)}, u32[]{:S(2)}) collective-permute-start(bf16[64,512]{1,0:T(8,128)(2,1)S(1)} %sum_first_sigma.1.refs_3_), channel_id=1, source_target_pairs={{8,0},{12,4},{0,8},{4,12},{9,1},{13,5},{1,9},{5,13},{10,2},{14,6},... | collective-permute-start | bytes 196616 | tf_op jit(solution)/shard_map/ppermute | solution.py:208
  22.9 1.7 %collective-permute-start.8 = (bf16[64,512]{1,0:T(8,128)(2,1)S(1)}, bf16[64,512]{1,0:T(8,128)(2,1)S(1)}, u32[]{:S(2)}, u32[]{:S(2)}) collective-permute-start(bf16[64,512]{1,0:T(8,128)(2,1)S(1)} %sum_first_sigma.1.refs_3_), channel_id=1, source_target_pairs={{12,0},{8,4},{4,8},{0,12},{13,1},{9,5},{5,9},{1,13},{14,2},{10,6},... | collective-permute-start | bytes 196616 | tf_op jit(solution)/shard_map/ppermute | solution.py:208
  24.6 0.5 collective-permute-start.10
  25.1 1.5 %collective-permute-start.16 = (bf16[64,512]{1,0:T(8,128)(2,1)S(1)}, bf16[64,512]{1,0:T(8,128)(2,1)S(1)}, u32[]{:S(2)}, u32[]{:S(2)}) collective-permute-start(bf16[64,512]{1,0:T(8,128)(2,1)S(1)} %sum_first_sigma.1.refs_3_), channel_id=1, source_target_pairs={{2,0},{0,2},{3,1},{1,3},{6,4},{4,6},{7,5},{5,7},{10,8},{8,10},{11,... | collective-permute-start | bytes 196616 | tf_op jit(solution)/shard_map/ppermute | solution.py:208
  26.6 1.5 %collective-permute-start.15 = (bf16[64,512]{1,0:T(8,128)(2,1)S(1)}, bf16[64,512]{1,0:T(8,128)(2,1)S(1)}, u32[]{:S(2)}, u32[]{:S(2)}) collective-permute-start(bf16[64,512]{1,0:T(8,128)(2,1)S(1)} %sum_first_sigma.1.refs_3_), channel_id=1, source_target_pairs={{6,0},{4,2},{2,4},{0,6},{14,8},{12,10},{10,12},{8,14},{7,1},{5,3},... | collective-permute-start | bytes 196616 | tf_op jit(solution)/shard_map/ppermute | solution.py:208
  28.1 0.1 collective-permute-done.9.refs_1_
  28.1 2.6 %collective-permute-start.14 = (bf16[64,512]{1,0:T(8,128)(2,1)S(1)}, bf16[64,512]{1,0:T(8,128)(2,1)S(1)}, u32[]{:S(2)}, u32[]{:S(2)}) collective-permute-start(bf16[64,512]{1,0:T(8,128)(2,1)S(1)} %collective-permute-done.9.refs_1_), channel_id=1, source_target_pairs={{2,0},{0,2},{3,1},{1,3},{6,4},{4,6},{7,5},{5,7},{10,8},{8,10},{11,... | collective-permute-start | bytes 196616 | tf_op jit(solution)/shard_map/ppermute | solution.py:208
  30.8 0.0 collective-permute-done.8.refs_0_
  30.8 0.0 collective-permute-start.13
  30.8 0.0 collective-permute-done.10.refs_2_
  30.8 0.1 collective-permute-start.11
  30.9 0.0 collective-permute-done.16.refs_3_
  30.9 1.1 %collective-permute-done.15.refs_2_ = bf16[64,512]{1,0:T(8,128)(2,1)S(1)} collective-permute-done((bf16[64,512]{1,0:T(8,128)(2,1)S(1)}, bf16[64,512]{1,0:T(8,128)(2,1)S(1)}, u32[]{:S(2)}, u32[]{:S(2)}) %collective-permute-start.15) | collective-permute-done | bytes 65568 | tf_op jit(solution)/shard_map/ppermute | solution.py:208
  32.0 1.3 %collective-permute-done.14.refs_1_ = bf16[64,512]{1,0:T(8,128)(2,1)S(1)} collective-permute-done((bf16[64,512]{1,0:T(8,128)(2,1)S(1)}, bf16[64,512]{1,0:T(8,128)(2,1)S(1)}, u32[]{:S(2)}, u32[]{:S(2)}) %collective-permute-start.14) | collective-permute-done | bytes 65568 | tf_op jit(solution)/shard_map/ppermute | solution.py:208
  33.3 1.7 %collective-permute-done.13.refs_0_ = bf16[64,512]{1,0:T(8,128)(2,1)S(1)} collective-permute-done((bf16[64,512]{1,0:T(8,128)(2,1)S(1)}, bf16[64,512]{1,0:T(8,128)(2,1)S(1)}, u32[]{:S(2)}, u32[]{:S(2)}) %collective-permute-start.13) | collective-permute-done | bytes 65568 | tf_op jit(solution)/shard_map/ppermute | solution.py:208
  35.1 0.1 collective-permute-start.17
  35.1 0.0 collective-permute-done.11.sigma_other.other
  35.1 0.7 %left_products.1.products = f32[4,256,512]{2,1,0:T(8,128)S(1)} custom-call(bf16[4,256,256]{2,1,0:T(8,128)(2,1)S(1)} %get-tuple-element.21.refs_3_.left_own, bf16[4,256,256]{2,1,0:T(8,128)(2,1)S(1)} %get-tuple-element.22.refs_4_.left_other, bf16[1,256,512]{2,1,0:T(8,128)(2,1)S(1)} %place_own_sector.1.sigma_own.own, ...), custom_call_target="tpu_custom_call" | custom-call | tf_op jit(solution)/shard_map/left_products/pallas_call | solution.py:226
  35.9 0.8 %collective-permute-done.17.other = bf16[1,256,512]{2,1,0:T(8,128)(2,1)S(1)} collective-permute-done((bf16[1,256,512]{2,1,0:T(8,128)(2,1)S(1)}, bf16[1,256,512]{2,1,0:T(8,128)(2,1)S(1)}, u32[]{:S(2)}, u32[]{:S(2)}) %collective-permute-start.17) | collective-permute-done | bytes 262176 | tf_op jit(solution)/shard_map/ppermute | solution.py:208
  36.7 2.2 %second_sigma_terms.1 = (f32[64,512]{1,0:T(8,128)S(1)}, bf16[64,512]{1,0:T(8,128)(2,1)S(1)}, bf16[64,512]{1,0:T(8,128)(2,1)S(1)}, bf16[64,512]{1,0:T(8,128)(2,1)S(1)}) custom-call(s32[2,2]{1,0:T(2,128)S(1)} %copy-done.2, s32[4,2,8]{2,1,0:T(2,128)S(1)} %bitcast.2, f32[4,8]{1,0:T(4,128)S(1)} %copy-done.3, ...), custom_call_target="tpu_custom_call" | custom-call | tf_op jit(solution)/shard_map/second_sigma_terms/pallas_call | solution.py:226
  38.8 2.5 %collective-permute-start.18 = (bf16[64,512]{1,0:T(8,128)(2,1)S(1)}, bf16[64,512]{1,0:T(8,128)(2,1)S(1)}, u32[]{:S(2)}, u32[]{:S(2)}) collective-permute-start(bf16[64,512]{1,0:T(8,128)(2,1)S(1)} %get-tuple-element.37), channel_id=1, source_target_pairs={{12,0},{8,4},{4,8},{0,12},{13,1},{9,5},{5,9},{1,13},{14,2},{10,6},... | collective-permute-start | bytes 196616 | tf_op jit(solution)/shard_map/ppermute | solution.py:208
  41.4 0.0 collective-permute-start.19
  41.4 1.9 %collective-permute-start.20 = (bf16[64,512]{1,0:T(8,128)(2,1)S(1)}, bf16[64,512]{1,0:T(8,128)(2,1)S(1)}, u32[]{:S(2)}, u32[]{:S(2)}) collective-permute-start(bf16[64,512]{1,0:T(8,128)(2,1)S(1)} %get-tuple-element.39), channel_id=1, source_target_pairs={{4,0},{0,4},{12,8},{8,12},{5,1},{1,5},{13,9},{9,13},{6,2},{2,6},{1... | collective-permute-start | bytes 196616 | tf_op jit(solution)/shard_map/ppermute | solution.py:208
  43.3 0.5 sums_for_rayleigh.1.refs_0_.refs_4_
  43.8 0.8 %collective-permute-start.12 = (f32[3,8,128]{2,1,0:T(8,128)S(1)}, f32[3,8,128]{2,1,0:T(8,128)S(1)}, u32[]{:S(2)}, u32[]{:S(2)}) collective-permute-start(f32[3,8,128]{2,1,0:T(8,128)S(1)} %sums_for_rayleigh.1.refs_0_.refs_4_), channel_id=1, source_target_pairs={{2,0},{0,2},{3,1},{1,3},{6,4},{4,6},{7,5},{5,7},{10,8},{8,10},{11,... | collective-permute-start | bytes 36872 | tf_op jit(solution)/shard_map/ppermute | solution.py:208
  44.6 3.0 %collective-permute-done.12.refs_1_.refs_5_ = f32[3,8,128]{2,1,0:T(8,128)S(1)} collective-permute-done((f32[3,8,128]{2,1,0:T(8,128)S(1)}, f32[3,8,128]{2,1,0:T(8,128)S(1)}, u32[]{:S(2)}, u32[]{:S(2)}) %collective-permute-start.12) | collective-permute-done | bytes 12320 | tf_op jit(solution)/shard_map/ppermute | solution.py:208
  47.6 0.0 collective-permute-done.18.refs_1_
  47.6 0.1 collective-permute-done.19.refs_2_
  47.6 0.0 collective-permute-done.20.refs_3_
  47.7 0.8 %collective-permute-start.23 = (bf16[64,512]{1,0:T(8,128)(2,1)S(1)}, bf16[64,512]{1,0:T(8,128)(2,1)S(1)}, u32[]{:S(2)}, u32[]{:S(2)}) collective-permute-start(bf16[64,512]{1,0:T(8,128)(2,1)S(1)} %sum_second_sigma.1.refs_3_), channel_id=1, source_target_pairs={{4,0},{0,4},{12,8},{8,12},{5,1},{1,5},{13,9},{9,13},{6,2},{2,6},{1... | collective-permute-start | bytes 196616 | tf_op jit(solution)/shard_map/ppermute | solution.py:208
  48.5 2.3 %collective-permute-start.22 = (bf16[64,512]{1,0:T(8,128)(2,1)S(1)}, bf16[64,512]{1,0:T(8,128)(2,1)S(1)}, u32[]{:S(2)}, u32[]{:S(2)}) collective-permute-start(bf16[64,512]{1,0:T(8,128)(2,1)S(1)} %sum_second_sigma.1.refs_3_), channel_id=1, source_target_pairs={{8,0},{12,4},{0,8},{4,12},{9,1},{13,5},{1,9},{5,13},{10,2},{14,6},... | collective-permute-start | bytes 196616 | tf_op jit(solution)/shard_map/ppermute | solution.py:208
  50.8 1.3 %collective-permute-start.21 = (bf16[64,512]{1,0:T(8,128)(2,1)S(1)}, bf16[64,512]{1,0:T(8,128)(2,1)S(1)}, u32[]{:S(2)}, u32[]{:S(2)}) collective-permute-start(bf16[64,512]{1,0:T(8,128)(2,1)S(1)} %sum_second_sigma.1.refs_3_), channel_id=1, source_target_pairs={{12,0},{8,4},{4,8},{0,12},{13,1},{9,5},{5,9},{1,13},{14,2},{10,6},... | collective-permute-start | bytes 196616 | tf_op jit(solution)/shard_map/ppermute | solution.py:208
  52.1 1.4 %second_wave.1 = (bf16[1,256,512]{2,1,0:T(8,128)(2,1)}, f32[2,8,128]{2,1,0:T(8,128)S(1)}) custom-call(s32[2,2]{1,0:T(2,128)S(1)} %copy-done.2, bf16[256,512]{1,0:T(8,128)(2,1)S(1)} %get-tuple-element.24.wave_own, bf16[1,256,512]{2,1,0:T(8,128)(2,1)S(1)} %place_own_sector.1.sigma_own.own, f32[3,8,128]{2,1,0:T(8,128)S(1)} %sums_for_rayleigh.1.refs_0_.refs_4_, ...), custom_call_target="tpu_custom_call" | custom-call | tf_op jit(solution)/shard_map/second_wave/pallas_call | solution.py:226
  53.6 0.0 collective-permute-done.23.refs_2_
  53.6 2.4 %collective-permute-done.22.refs_1_ = bf16[64,512]{1,0:T(8,128)(2,1)S(1)} collective-permute-done((bf16[64,512]{1,0:T(8,128)(2,1)S(1)}, bf16[64,512]{1,0:T(8,128)(2,1)S(1)}, u32[]{:S(2)}, u32[]{:S(2)}) %collective-permute-start.22) | collective-permute-done | bytes 65568 | tf_op jit(solution)/shard_map/ppermute | solution.py:208
  56.0 0.9 %collective-permute-done.21.refs_0_ = bf16[64,512]{1,0:T(8,128)(2,1)S(1)} collective-permute-done((bf16[64,512]{1,0:T(8,128)(2,1)S(1)}, bf16[64,512]{1,0:T(8,128)(2,1)S(1)}, u32[]{:S(2)}, u32[]{:S(2)}) %collective-permute-start.21) | collective-permute-done | bytes 65568 | tf_op jit(solution)/shard_map/ppermute | solution.py:208
  57.0 0.9 %join_second_sigma.1 = f32[1,256,512]{2,1,0:T(8,128)} custom-call(f32[2,8,128]{2,1,0:T(8,128)S(1)} %get-tuple-element.35.factors, bf16[1,256,512]{2,1,0:T(8,128)(2,1)S(1)} %place_own_sector.1.sigma_own.own, bf16[64,512]{1,0:T(8,128)(2,1)S(1)} %collective-permute-done.21.refs_0_, bf16[64,512]{1,0:T(8,128)(2,1)S(1)} %collective-permute-done.22.refs_1_, ...), custom_call_target="tpu_custom_call" | custom-call | tf_op jit(solution)/shard_map/join_second_sigma/pallas_call | solution.py:226
  (5 shorter events, 0.1 us)
Async XLA Ops:
  0.6 2.5 %copy-start = (bf16[1,256,512]{2,1,0:T(8,128)(2,1)S(1)}, bf16[1,256,512]{2,1,0:T(8,128)(2,1)}, u32[]{:S(2)}) copy-start(bf16[1,256,512]{2,1,0:T(8,128)(2,1)} %refs_6_.1) | copy-start | bytes 786436
  0.6 2.5 %copy-start.2 = (s32[2,2]{1,0:T(2,128)S(1)}, s32[2,2]{1,0:T(2,128)}, u32[]{:S(2)}) copy-start(s32[2,2]{1,0:T(2,128)} %sizes_ref.3) | copy-start | bytes 52
  0.7 2.5 %copy-start.3 = (f32[4,8]{1,0:T(4,128)S(1)}, f32[4,8]{1,0:T(4,128)}, u32[]{:S(2)}) copy-start(f32[4,8]{1,0:T(4,128)} %weights_ref.1) | copy-start | bytes 388
  0.7 2.5 %copy-start.1 = (s32[4,8,2]{1,2,0:T(2,128)S(1)}, s32[4,8,2]{1,2,0:T(2,128)}, u32[]{:S(2)}) copy-start(s32[4,8,2]{1,2,0:T(2,128)} %param.10) | copy-start | bytes 772
  0.7 2.5 %collective-permute-start = (bf16[1,256,512]{2,1,0:T(8,128)(2,1)}, bf16[1,256,512]{2,1,0:T(8,128)(2,1)S(1)}, u32[]{:S(2)}, u32[]{:S(2)}) collective-permute-start(bf16[1,256,512]{2,1,0:T(8,128)(2,1)} %refs_6_.1), channel_id=1, source_target_pairs={{1,0},{0,1},{3,2},{2,3},{5,4},{4,5},{7,6},{6,7},{9,8},{8,9},{11,10... | collective-permute-start | bytes 786440 | tf_op jit(solution)/shard_map/ppermute | solution.py:208
  5.7 6.2 %collective-permute-start.1 = (bf16[64,512]{1,0:T(8,128)(2,1)S(1)}, bf16[64,512]{1,0:T(8,128)(2,1)S(1)}, u32[]{:S(2)}, u32[]{:S(2)}) collective-permute-start(bf16[64,512]{1,0:T(8,128)(2,1)S(1)} %get-tuple-element.27), channel_id=1, source_target_pairs={{2,0},{0,2},{3,1},{1,3},{6,4},{4,6},{7,5},{5,7},{10,8},{8,10},{11,... | collective-permute-start | bytes 196616 | tf_op jit(solution)/shard_map/ppermute | solution.py:208
  8.3 7.7 %collective-permute-start.3 = (bf16[64,512]{1,0:T(8,128)(2,1)S(1)}, bf16[64,512]{1,0:T(8,128)(2,1)S(1)}, u32[]{:S(2)}, u32[]{:S(2)}) collective-permute-start(bf16[64,512]{1,0:T(8,128)(2,1)S(1)} %get-tuple-element.29), channel_id=1, source_target_pairs={{2,0},{0,2},{3,1},{1,3},{6,4},{4,6},{7,5},{5,7},{10,8},{8,10},{11,... | collective-permute-start | bytes 196616 | tf_op jit(solution)/shard_map/ppermute | solution.py:208
  8.4 7.8 %collective-permute-start.5 = (bf16[64,512]{1,0:T(8,128)(2,1)S(1)}, bf16[64,512]{1,0:T(8,128)(2,1)S(1)}, u32[]{:S(2)}, u32[]{:S(2)}) collective-permute-start(bf16[64,512]{1,0:T(8,128)(2,1)S(1)} %get-tuple-element.30), channel_id=1, source_target_pairs={{4,0},{0,4},{12,8},{8,12},{5,1},{1,5},{13,9},{9,13},{6,2},{2,6},{1... | collective-permute-start | bytes 196616 | tf_op jit(solution)/shard_map/ppermute | solution.py:208
  10.4 5.7 %collective-permute-start.6 = (bf16[64,512]{1,0:T(8,128)(2,1)S(1)}, bf16[64,512]{1,0:T(8,128)(2,1)S(1)}, u32[]{:S(2)}, u32[]{:S(2)}) collective-permute-start(bf16[64,512]{1,0:T(8,128)(2,1)S(1)} %get-tuple-element.31), channel_id=1, source_target_pairs={{6,0},{4,2},{2,4},{0,6},{14,8},{12,10},{10,12},{8,14},{7,1},{5,3},... | collective-permute-start | bytes 196616 | tf_op jit(solution)/shard_map/ppermute | solution.py:208
  11.8 4.7 %collective-permute-start.7 = (bf16[64,512]{1,0:T(8,128)(2,1)S(1)}, bf16[64,512]{1,0:T(8,128)(2,1)S(1)}, u32[]{:S(2)}, u32[]{:S(2)}) collective-permute-start(bf16[64,512]{1,0:T(8,128)(2,1)S(1)} %get-tuple-element.32), channel_id=1, source_target_pairs={{2,0},{0,2},{3,1},{1,3},{6,4},{4,6},{7,5},{5,7},{10,8},{8,10},{11,... | collective-permute-start | bytes 196616 | tf_op jit(solution)/shard_map/ppermute | solution.py:208
  11.9 7.2 %collective-permute-start.2 = (bf16[64,512]{1,0:T(8,128)(2,1)S(1)}, bf16[64,512]{1,0:T(8,128)(2,1)S(1)}, u32[]{:S(2)}, u32[]{:S(2)}) collective-permute-start(bf16[64,512]{1,0:T(8,128)(2,1)S(1)} %sum_far_share.2), channel_id=1, source_target_pairs={{12,0},{8,4},{4,8},{0,12},{13,1},{9,5},{5,9},{1,13},{14,2},{10,6},... | collective-permute-start | bytes 196616 | tf_op jit(solution)/shard_map/ppermute | solution.py:208
  16.1 5.2 %collective-permute-start.4 = (bf16[64,512]{1,0:T(8,128)(2,1)S(1)}, bf16[64,512]{1,0:T(8,128)(2,1)S(1)}, u32[]{:S(2)}, u32[]{:S(2)}) collective-permute-start(bf16[64,512]{1,0:T(8,128)(2,1)S(1)} %sum_far_share.3), channel_id=1, source_target_pairs={{8,0},{12,4},{0,8},{4,12},{9,1},{13,5},{1,9},{5,13},{10,2},{14,6},... | collective-permute-start | bytes 196616 | tf_op jit(solution)/shard_map/ppermute | solution.py:208
  21.3 6.8 %collective-permute-start.9 = (bf16[64,512]{1,0:T(8,128)(2,1)S(1)}, bf16[64,512]{1,0:T(8,128)(2,1)S(1)}, u32[]{:S(2)}, u32[]{:S(2)}) collective-permute-start(bf16[64,512]{1,0:T(8,128)(2,1)S(1)} %sum_first_sigma.1.refs_3_), channel_id=1, source_target_pairs={{8,0},{12,4},{0,8},{4,12},{9,1},{13,5},{1,9},{5,13},{10,2},{14,6},... | collective-permute-start | bytes 196616 | tf_op jit(solution)/shard_map/ppermute | solution.py:208
  22.9 7.9 %collective-permute-start.8 = (bf16[64,512]{1,0:T(8,128)(2,1)S(1)}, bf16[64,512]{1,0:T(8,128)(2,1)S(1)}, u32[]{:S(2)}, u32[]{:S(2)}) collective-permute-start(bf16[64,512]{1,0:T(8,128)(2,1)S(1)} %sum_first_sigma.1.refs_3_), channel_id=1, source_target_pairs={{12,0},{8,4},{4,8},{0,12},{13,1},{9,5},{5,9},{1,13},{14,2},{10,6},... | collective-permute-start | bytes 196616 | tf_op jit(solution)/shard_map/ppermute | solution.py:208
  24.6 6.2 %collective-permute-start.10 = (bf16[64,512]{1,0:T(8,128)(2,1)S(1)}, bf16[64,512]{1,0:T(8,128)(2,1)S(1)}, u32[]{:S(2)}, u32[]{:S(2)}) collective-permute-start(bf16[64,512]{1,0:T(8,128)(2,1)S(1)} %sum_first_sigma.1.refs_3_), channel_id=1, source_target_pairs={{4,0},{0,4},{12,8},{8,12},{5,1},{1,5},{13,9},{9,13},{6,2},{2,6},{1... | collective-permute-start | bytes 196616 | tf_op jit(solution)/shard_map/ppermute | solution.py:208
  25.1 5.8 %collective-permute-start.16 = (bf16[64,512]{1,0:T(8,128)(2,1)S(1)}, bf16[64,512]{1,0:T(8,128)(2,1)S(1)}, u32[]{:S(2)}, u32[]{:S(2)}) collective-permute-start(bf16[64,512]{1,0:T(8,128)(2,1)S(1)} %sum_first_sigma.1.refs_3_), channel_id=1, source_target_pairs={{2,0},{0,2},{3,1},{1,3},{6,4},{4,6},{7,5},{5,7},{10,8},{8,10},{11,... | collective-permute-start | bytes 196616 | tf_op jit(solution)/shard_map/ppermute | solution.py:208
  26.6 5.4 %collective-permute-start.15 = (bf16[64,512]{1,0:T(8,128)(2,1)S(1)}, bf16[64,512]{1,0:T(8,128)(2,1)S(1)}, u32[]{:S(2)}, u32[]{:S(2)}) collective-permute-start(bf16[64,512]{1,0:T(8,128)(2,1)S(1)} %sum_first_sigma.1.refs_3_), channel_id=1, source_target_pairs={{6,0},{4,2},{2,4},{0,6},{14,8},{12,10},{10,12},{8,14},{7,1},{5,3},... | collective-permute-start | bytes 196616 | tf_op jit(solution)/shard_map/ppermute | solution.py:208
  28.1 5.2 %collective-permute-start.14 = (bf16[64,512]{1,0:T(8,128)(2,1)S(1)}, bf16[64,512]{1,0:T(8,128)(2,1)S(1)}, u32[]{:S(2)}, u32[]{:S(2)}) collective-permute-start(bf16[64,512]{1,0:T(8,128)(2,1)S(1)} %collective-permute-done.9.refs_1_), channel_id=1, source_target_pairs={{2,0},{0,2},{3,1},{1,3},{6,4},{4,6},{7,5},{5,7},{10,8},{8,10},{11,... | collective-permute-start | bytes 196616 | tf_op jit(solution)/shard_map/ppermute | solution.py:208
  30.8 4.3 %collective-permute-start.13 = (bf16[64,512]{1,0:T(8,128)(2,1)S(1)}, bf16[64,512]{1,0:T(8,128)(2,1)S(1)}, u32[]{:S(2)}, u32[]{:S(2)}) collective-permute-start(bf16[64,512]{1,0:T(8,128)(2,1)S(1)} %collective-permute-done.8.refs_0_), channel_id=1, source_target_pairs={{2,0},{0,2},{3,1},{1,3},{6,4},{4,6},{7,5},{5,7},{10,8},{8,10},{11,... | collective-permute-start | bytes 196616 | tf_op jit(solution)/shard_map/ppermute | solution.py:208
  30.8 4.3 %collective-permute-start.11 = (bf16[1,256,512]{2,1,0:T(8,128)(2,1)S(1)}, bf16[1,256,512]{2,1,0:T(8,128)(2,1)S(1)}, u32[]{:S(2)}, u32[]{:S(2)}) collective-permute-start(bf16[1,256,512]{2,1,0:T(8,128)(2,1)S(1)} %place_own_sector.1.sigma_own.own), channel_id=1, source_target_pairs={{1,0},{0,1},{3,2},{2,3},{5,4},{4,5},{7,6},{6,7},{9,8},{8,9},{11,10... | collective-permute-start | bytes 786440 | tf_op jit(solution)/shard_map/ppermute | solution.py:208
  35.1 1.6 %collective-permute-start.17 = (bf16[1,256,512]{2,1,0:T(8,128)(2,1)S(1)}, bf16[1,256,512]{2,1,0:T(8,128)(2,1)S(1)}, u32[]{:S(2)}, u32[]{:S(2)}) collective-permute-start(bf16[1,256,512]{2,1,0:T(8,128)(2,1)S(1)} %place_other_sectors.1.own), channel_id=1, source_target_pairs={{1,0},{0,1},{3,2},{2,3},{5,4},{4,5},{7,6},{6,7},{9,8},{8,9},{11,10... | collective-permute-start | bytes 786440 | tf_op jit(solution)/shard_map/ppermute | solution.py:208
  38.8 8.7 %collective-permute-start.18 = (bf16[64,512]{1,0:T(8,128)(2,1)S(1)}, bf16[64,512]{1,0:T(8,128)(2,1)S(1)}, u32[]{:S(2)}, u32[]{:S(2)}) collective-permute-start(bf16[64,512]{1,0:T(8,128)(2,1)S(1)} %get-tuple-element.37), channel_id=1, source_target_pairs={{12,0},{8,4},{4,8},{0,12},{13,1},{9,5},{5,9},{1,13},{14,2},{10,6},... | collective-permute-start | bytes 196616 | tf_op jit(solution)/shard_map/ppermute | solution.py:208
  41.4 6.3 %collective-permute-start.19 = (bf16[64,512]{1,0:T(8,128)(2,1)S(1)}, bf16[64,512]{1,0:T(8,128)(2,1)S(1)}, u32[]{:S(2)}, u32[]{:S(2)}) collective-permute-start(bf16[64,512]{1,0:T(8,128)(2,1)S(1)} %get-tuple-element.38), channel_id=1, source_target_pairs={{8,0},{12,4},{0,8},{4,12},{9,1},{13,5},{1,9},{5,13},{10,2},{14,6},... | collective-permute-start | bytes 196616 | tf_op jit(solution)/shard_map/ppermute | solution.py:208
  41.4 6.3 %collective-permute-start.20 = (bf16[64,512]{1,0:T(8,128)(2,1)S(1)}, bf16[64,512]{1,0:T(8,128)(2,1)S(1)}, u32[]{:S(2)}, u32[]{:S(2)}) collective-permute-start(bf16[64,512]{1,0:T(8,128)(2,1)S(1)} %get-tuple-element.39), channel_id=1, source_target_pairs={{4,0},{0,4},{12,8},{8,12},{5,1},{1,5},{13,9},{9,13},{6,2},{2,6},{1... | collective-permute-start | bytes 196616 | tf_op jit(solution)/shard_map/ppermute | solution.py:208
  43.8 3.8 %collective-permute-start.12 = (f32[3,8,128]{2,1,0:T(8,128)S(1)}, f32[3,8,128]{2,1,0:T(8,128)S(1)}, u32[]{:S(2)}, u32[]{:S(2)}) collective-permute-start(f32[3,8,128]{2,1,0:T(8,128)S(1)} %sums_for_rayleigh.1.refs_0_.refs_4_), channel_id=1, source_target_pairs={{2,0},{0,2},{3,1},{1,3},{6,4},{4,6},{7,5},{5,7},{10,8},{8,10},{11,... | collective-permute-start | bytes 36872 | tf_op jit(solution)/shard_map/ppermute | solution.py:208
  47.7 5.9 %collective-permute-start.23 = (bf16[64,512]{1,0:T(8,128)(2,1)S(1)}, bf16[64,512]{1,0:T(8,128)(2,1)S(1)}, u32[]{:S(2)}, u32[]{:S(2)}) collective-permute-start(bf16[64,512]{1,0:T(8,128)(2,1)S(1)} %sum_second_sigma.1.refs_3_), channel_id=1, source_target_pairs={{4,0},{0,4},{12,8},{8,12},{5,1},{1,5},{13,9},{9,13},{6,2},{2,6},{1... | collective-permute-start | bytes 196616 | tf_op jit(solution)/shard_map/ppermute | solution.py:208
  48.5 7.5 %collective-permute-start.22 = (bf16[64,512]{1,0:T(8,128)(2,1)S(1)}, bf16[64,512]{1,0:T(8,128)(2,1)S(1)}, u32[]{:S(2)}, u32[]{:S(2)}) collective-permute-start(bf16[64,512]{1,0:T(8,128)(2,1)S(1)} %sum_second_sigma.1.refs_3_), channel_id=1, source_target_pairs={{8,0},{12,4},{0,8},{4,12},{9,1},{13,5},{1,9},{5,13},{10,2},{14,6},... | collective-permute-start | bytes 196616 | tf_op jit(solution)/shard_map/ppermute | solution.py:208
  50.8 6.2 %collective-permute-start.21 = (bf16[64,512]{1,0:T(8,128)(2,1)S(1)}, bf16[64,512]{1,0:T(8,128)(2,1)S(1)}, u32[]{:S(2)}, u32[]{:S(2)}) collective-permute-start(bf16[64,512]{1,0:T(8,128)(2,1)S(1)} %sum_second_sigma.1.refs_3_), channel_id=1, source_target_pairs={{12,0},{8,4},{4,8},{0,12},{13,1},{9,5},{5,9},{1,13},{14,2},{10,6},... | collective-permute-start | bytes 196616 | tf_op jit(solution)/shard_map/ppermute | solution.py:208

commit v7 on v6

--- a/solution.py
+++ b/solution.py
@@ -42,17 +42,14 @@
     )
 
 
-def load_kernel(left_ref, right_ref, left_own, left_other, right, sems):
+def load_kernel(left_ref, left_own, left_other, sems):
     rows = left_own.shape[1]
     core = lax.axis_index("rep")
-    own = pl.multiple_of(core * rows, rows)
-    other = pl.multiple_of((core ^ 1) * rows, rows)
-    mine = left_ref.at[:, pl.ds(own, rows)]
-    copies = [
-        pltpu.make_async_copy(mine.at[:, :, pl.ds(own, rows)], left_own, sems.at[0]),
-        pltpu.make_async_copy(mine.at[:, :, pl.ds(other, rows)], left_other, sems.at[1]),
-        pltpu.make_async_copy(right_ref, right, sems.at[2]),
-    ]
+    copies = []
+    for index, (half, place) in enumerate(((left_own, core), (left_other, core ^ 1))):
+        mine = pl.ds(pl.multiple_of(core * rows, rows), rows)
+        columns = pl.ds(pl.multiple_of(place * rows, rows), rows)
+        copies.append(pltpu.make_async_copy(left_ref.at[:, mine, columns], half, sems.at[index]))
     for copy in copies:
         copy.start()
     for copy in copies:
@@ -60,11 +57,17 @@
 
 
 def first_kernel(shares, *refs):
-    sizes_ref, pairs_ref, weights_ref, left_own, left_other, right, wave, arrived = refs[:8]
-    own, other, *parts = refs[8:-1]
-    held = refs[-1]
+    sizes_ref, pairs_ref, weights_ref, left_own, left_other, right_ref, wave, arrived = refs[:8]
+    right, own, other, *parts = refs[8:-2]
+    held, sems = refs[-2:]
     rows, columns = own.shape
-    share = parts[0].shape[0]
+    share = parts[0].shape[-2]
+    copies = [
+        pltpu.make_async_copy(right_ref.at[term], right.at[term], sems.at[term])
+        for term in range(right.shape[0])
+    ]
+    for copy in copies:
+        copy.start()
     sectors = held.shape[0]
     sector = lax.axis_index("sec")
     core = lax.axis_index("rep")
@@ -76,6 +79,7 @@
     totals = [None] * sectors
     for term in range(right.shape[0]):
         product = left_times(left_own, left_other, term, own[...], other[...])
+        copies[term].wait()
         product = times_right(product, right, term)
         for step in range(sectors):
             weight = mixing_scalar(pairs_ref, weights_ref, term, sector ^ step, sector)
@@ -84,25 +88,26 @@
     for step in range(sectors):
         live = live_cells(sizes_ref, sector ^ step, core * rows, rows, columns)
         held[step] = jnp.where(live, totals[step], 0.0)
-    for (along, across), out in zip(shares, parts):
-        start = pl.multiple_of((place ^ along) * share, share)
-        out[...] = held[across, pl.ds(start, share), :].astype(out.dtype)
-
-
-def sum_kernel(count, own_ref, *refs):
-    total = own_ref[...]
-    for piece in refs[:count]:
-        total = total + piece[...].astype(jnp.float32)
-    refs[-1][...] = total.astype(refs[-1].dtype)
+    for (steps, across), out in zip(shares, parts):
+        for index, along in enumerate(steps):
+            start = pl.multiple_of((place ^ along) * share, share)
+            out[index] = held[across, pl.ds(start, share), :].astype(out.dtype)
+
+
+def sum_kernel(indices, *refs):
+    total = refs[0][indices[0]].astype(jnp.float32)
+    for index, piece in zip(indices[1:], refs[1:]):
+        total = total + piece[index].astype(jnp.float32)
+    refs[-1][0] = total.astype(refs[-1].dtype)
 
 
 def place_kernel(spots, *refs):
     pieces, half = refs[:-1], refs[-1]
-    share = pieces[0].shape[0]
+    share = pieces[0].shape[1]
     place = lax.axis_index("ops")
     for (along, index), piece in zip(spots, pieces):
         start = pl.multiple_of((place ^ along) * share, share)
-        half[index, pl.ds(start, share), :] = piece[...]
+        half[index, pl.ds(start, share), :] = piece[0]
 
 
 def left_kernel(left_own, left_other, own, other, out):
@@ -115,7 +120,7 @@
 ):
     shares, held = refs[:-1], refs[-1]
     rows, columns = own.shape[1:]
-    share = shares[0].shape[0]
+    share = shares[0].shape[1]
     target = lax.axis_index("sec")
     core = lax.axis_index("rep")
     place = lax.axis_index("ops")
@@ -134,7 +139,7 @@
     held[...] = jnp.where(live, total, 0.0)
     for step, out in enumerate(shares):
         start = pl.multiple_of((place ^ step) * share, share)
-        out[...] = held[pl.ds(start, share), :].astype(out.dtype)
+        out[0] = held[pl.ds(start, share), :].astype(out.dtype)
 
 
 def sums_kernel(wave_own, wave_other, sigma_own, sigma_other, out):
@@ -181,15 +186,20 @@
 
 
 def join_kernel(factors, sigma_own, *refs):
-    pieces, out = refs[:-1], refs[-1]
-    share, columns = pieces[0].shape
+    pieces, (out, held, sems) = refs[:-3], refs[-3:]
+    _, share, columns = pieces[0].shape
     place = lax.axis_index("ops")
     scale = jnp.broadcast_to(factors[0][:1, :1], (share, columns))
     shift = jnp.broadcast_to(factors[1][:1, :1], (share, columns))
-    for step, piece in enumerate(reversed(pieces)):
-        start = pl.multiple_of((place ^ step) * share, share)
-        sigma = sigma_own[0, pl.ds(start, share), :].astype(jnp.float32)
-        out[0, pl.ds(start, share), :] = scale * piece[...].astype(jnp.float32) - shift * sigma
+    copies = []
+    for step, piece in enumerate(pieces):
+        rows = pl.ds(pl.multiple_of((place ^ step) * share, share), share)
+        moved = shift * sigma_own[0, rows, :].astype(jnp.float32)
+        held[step] = scale * piece[0].astype(jnp.float32) - moved
+        copies.append(pltpu.make_async_copy(held.at[step], out.at[0, rows], sems.at[step]))
+        copies[-1].start()
+    for copy in copies:
+        copy.wait()
 
 
 def partner(value, steps):
@@ -222,76 +232,78 @@
     def shape(*dims, dtype=bf16):
         return jax.ShapeDtypeStruct(dims, dtype)
 
-    def call(kernel, name, out_shape, in_specs, *operands, scratch=(), vmem=16):
+    def call(kernel, name, out_shape, in_specs, *operands, scratch=(), vmem=16, out=inside):
         return pl.pallas_call(
             kernel,
             out_shape=out_shape,
             in_specs=list(in_specs) + [inside] * (len(operands) - len(in_specs)),
-            out_specs=jax.tree.map(lambda _: inside, out_shape),
+            out_specs=jax.tree.map(lambda _: out, out_shape),
             scratch_shapes=list(scratch),
             compiler_params=pltpu.CompilerParams(vmem_limit_bytes=vmem * mebibyte),
             name=name,
         )(*operands)
 
-    def summed(name, own, *pieces, after=()):
-        count = len(pieces)
+    def summed(name, *pieces, after=()):
+        pieces = [piece if isinstance(piece, tuple) else (piece, 0) for piece in pieces]
+        arrays, indices = zip(*pieces)
         return call(
-            lambda *refs: sum_kernel(count, *refs),
+            lambda *refs: sum_kernel(indices, *refs),
             name,
-            shape(share, columns),
+            shape(1, share, columns),
             [],
-            own,
-            *pieces,
+            *arrays,
             *after,
         )
 
     farthest_first = list(reversed(range(ops_count)))
-    far_steps = farthest_first[:-2]
     arrived = partner(wavefunction, {"rep": 1})
-    left_own, left_other, right = call(
+    left_own, left_other = call(
         load_kernel,
         "load_operators",
-        [
-            shape(terms, rows, rows),
-            shape(terms, rows, side - rows),
-            shape(*right_blocks.shape),
-        ],
-        [outside] * 2,
+        [shape(terms, rows, rows), shape(terms, rows, side - rows)],
+        [outside],
         left_blocks,
-        right_blocks,
-        scratch=[pltpu.SemaphoreType.DMA((3,))],
-        vmem=49,
+        scratch=[pltpu.SemaphoreType.DMA((2,))],
+        vmem=51,
     )
     pairs = jnp.swapaxes(sector_pairs, 1, 2)
-    operators = (sector_sizes, pairs, pair_weights, left_own, left_other, right)
-
-    spots = [(along, across) for along in farthest_first for across in range(sectors)]
-    wave_own, wave_other, *rest = call(
+    scalars = (sector_sizes, pairs, pair_weights)
+
+    far = ops_count - 1
+    direct = [(along,) for along in farthest_first[1:-1]]
+    spots = [((far, 0), across) for across in range(sectors)]
+    spots += [(along, across) for along in direct for across in range(sectors)]
+    right, wave_own, wave_other, *rest = call(
         lambda *refs: first_kernel(spots, *refs),
         "first_sigma_terms",
-        [shape(rows, columns)] * 2
+        [shape(*right_blocks.shape), shape(rows, columns), shape(rows, columns)]
         + [
-            shape(share, columns, dtype=f32 if across == 0 and along != 1 else bf16)
+            shape(len(along), share, columns, dtype=f32 if along == (far, 0) and across == 0 else bf16)
             for along, across in spots
         ],
-        [smem] * 3,
-        *operators,
+        [smem] * 3 + [inside] * 2 + [outside],
+        *scalars,
+        left_own,
+        left_other,
+        right_blocks,
         wavefunction,
         arrived,
-        scratch=[pltpu.VMEM((sectors, rows, columns), f32)],
-    )
+        scratch=[
+            pltpu.VMEM((sectors, rows, columns), f32),
+            pltpu.SemaphoreType.DMA((terms,)),
+        ],
+        vmem=49,
+    )
+    operators = scalars + (left_own, left_other, right)
     rest = dict(zip(spots, rest))
-    received = []
-    for along in far_steps:
-        parts = [partner(rest[along, across], {"sec": across}) for across in range(sectors)]
-        received.append(partner(summed("sum_far_share", *parts), {"ops": along}))
+    met = [partner(rest[(far, 0), across], {"sec": across}) for across in range(sectors)]
+    received = [partner(summed("sum_far_share", *met), {"ops": far})]
     received += [
-        partner(rest[along, across], {"ops": along, "sec": across})
-        for along in (1, 0)
+        partner(rest[along, across], {"ops": along[0], "sec": across})
+        for along in direct
         for across in range(sectors)
-        if along or across
     ]
-    first_share = summed("sum_first_sigma", rest[0, 0], *received)
+    first_share = summed("sum_first_sigma", *[(piece, 1) for piece in met], *received)
     along_ops = {along: partner(first_share, {"ops": along}) for along in farthest_first}
     sigma_own = call(
         lambda *refs: place_kernel([(along, 0) for along in farthest_first], *refs),
@@ -330,7 +342,7 @@
     shares = call(
         second_kernel,
         "second_sigma_terms",
-        [shape(share, columns, dtype=f32)] + [shape(share, columns)] * (ops_count - 1),
+        [shape(1, share, columns, dtype=f32)] + [shape(1, share, columns)] * (ops_count - 1),
         [smem] * 3,
         *operators,
         products,
@@ -368,7 +380,12 @@
         [],
         factors,
         sigma_own,
-        *[partner(second_share, {"ops": step}) for step in farthest_first],
+        *[partner(second_share, {"ops": step}) for step in range(ops_count)],
+        scratch=[
+            pltpu.VMEM((ops_count, share, columns), f32),
+            pltpu.SemaphoreType.DMA((ops_count,)),
+        ],
+        out=outside,
     )
     return (second_wave, second_sigma)
 

time: 58 us -> 56.8 us (0.979)
  waiting for transfers between devices: 16.6 us -> 12.9 us
  starting transfers between devices: 30.1 us -> 32.1 us
    ppermute x24 -> x23, waiting for transfers between devices: 16.6 us -> 12.9 us  [partner(): return lax.ppermute(value, axes, pairs)]
    ppermute x24 -> x23, starting transfers between devices: 30.1 us -> 32.1 us  [partner(): return lax.ppermute(value, axes, pairs)]
    pallas_call x13 -> x12, Pallas kernels: 10.4 us -> 10.8 us  [call(): pl.pallas_call(kernel, out_shape=out_shape, in_specs=list(in_specs) + [in...]
  transfers between devices with their start and end apart: 24 -> 23, of which waited for: 12 -> 13; matrix products, arithmetic and copies ran while one was open for 0% -> 0% of each run, Pallas kernels for 8% -> 7%
where the time goes in v7:
time: 56.8 us; the launch traced here: 56.6 us
  starting transfers between devices  32.1 us (57%)
  waiting for transfers between devices  12.9 us (23%)
  Pallas kernels  10.8 us (19%)
  between operations  0.78 us (1%)
    ppermute x23, starting transfers between devices, partner(): return lax.ppermute(value, axes, pairs)  32.1 us
    ppermute x23, waiting for transfers between devices, partner(): return lax.ppermute(value, axes, pairs)  12.9 us
    pallas_call x12, Pallas kernels, call(): pl.pallas_call(kernel, out_shape=out_shape, in_specs=list(in_specs) + [in...  10.8 us
  transfers between devices with their start and end apart: 23, of which 13 were waited for; matrix products, arithmetic and copies ran while one was open for 0% of the time, Pallas kernels for 7%

profile of v7, /device:TPU:0, one launch (start us, length us, event | category | flops | bytes accessed | tf_op | source)
XLA Modules:
  0.0 56.6 jit_solution(17297697788114496303)
XLA Ops:
  0.6 0.0 copy-start
  0.6 0.0 copy-start.2
  0.7 0.0 copy-start.3
  0.7 0.0 copy-start.1
  0.7 0.5 collective-permute-start
  1.2 1.2 %load_operators.1 = (bf16[4,256,256]{2,1,0:T(8,128)(2,1)S(1)}, bf16[4,256,256]{2,1,0:T(8,128)(2,1)S(1)}) custom-call(bf16[4,512,512]{2,1,0:T(8,128)(2,1)} %left_ref.1), custom_call_target="tpu_custom_call" | custom-call | tf_op jit(solution)/shard_map/load_operators/pallas_call | solution.py:236
  2.4 0.1 collective-permute-done.refs_7_
  2.6 0.0 copy-done
  2.6 0.0 copy-done.2
  2.6 0.0 copy-done.3
  2.6 0.0 copy-done.1
  2.6 3.7 %first_sigma_terms.1 = (bf16[4,512,512]{2,1,0:T(8,128)(2,1)S(1)}, bf16[256,512]{1,0:T(8,128)(2,1)S(1)}, bf16[256,512]{1,0:T(8,128)(2,1)S(1)}, f32[2,64,512]{2,1,...) custom-call(s32[2,2]{1,0:T(2,128)S(1)} %copy-done.2, ...), custom_call_target="tpu_custom_call" | custom-call | tf_op jit(solution)/shard_map/first_sigma_terms/pallas_call | solution.py:236
  6.3 2.9 %collective-permute-start.1 = (bf16[2,64,512]{2,1,0:T(8,128)(2,1)S(1)}, bf16[2,64,512]{2,1,0:T(8,128)(2,1)S(1)}, u32[]{:S(2)}, u32[]{:S(2)}) collective-permute-start(bf16[2,64,512]{2,1,0:T(8,128)(2,1)S(1)} %get-tuple-element.23), channel_id=1, source_target_pairs={{2,0},{0,2},{3,1},{1,3},{6,4},{4,6},{7,5},{5,7},{10,8},{8,10},{11,... | collective-permute-start | bytes 393224 | tf_op jit(solution)/shard_map/ppermute | solution.py:218
  9.2 2.6 %collective-permute-start.3 = (bf16[1,64,512]{2,1,0:T(8,128)(2,1)S(1)}, bf16[1,64,512]{2,1,0:T(8,128)(2,1)S(1)}, u32[]{:S(2)}, u32[]{:S(2)}) collective-permute-start(bf16[1,64,512]{2,1,0:T(8,128)(2,1)S(1)} %get-tuple-element.24), channel_id=1, source_target_pairs={{8,0},{12,4},{0,8},{4,12},{9,1},{13,5},{1,9},{5,13},{10,2},{14,6},... | collective-permute-start | bytes 196616 | tf_op jit(solution)/shard_map/ppermute | solution.py:218
  11.8 0.0 collective-permute-start.4
  11.8 1.9 %collective-permute-start.5 = (bf16[1,64,512]{2,1,0:T(8,128)(2,1)S(1)}, bf16[1,64,512]{2,1,0:T(8,128)(2,1)S(1)}, u32[]{:S(2)}, u32[]{:S(2)}) collective-permute-start(bf16[1,64,512]{2,1,0:T(8,128)(2,1)S(1)} %get-tuple-element.26), channel_id=1, source_target_pairs={{4,0},{0,4},{12,8},{8,12},{5,1},{1,5},{13,9},{9,13},{6,2},{2,6},{1... | collective-permute-start | bytes 196616 | tf_op jit(solution)/shard_map/ppermute | solution.py:218
  13.7 1.4 %collective-permute-start.6 = (bf16[1,64,512]{2,1,0:T(8,128)(2,1)S(1)}, bf16[1,64,512]{2,1,0:T(8,128)(2,1)S(1)}, u32[]{:S(2)}, u32[]{:S(2)}) collective-permute-start(bf16[1,64,512]{2,1,0:T(8,128)(2,1)S(1)} %get-tuple-element.27), channel_id=1, source_target_pairs={{6,0},{4,2},{2,4},{0,6},{14,8},{12,10},{10,12},{8,14},{7,1},{5,3},... | collective-permute-start | bytes 196616 | tf_op jit(solution)/shard_map/ppermute | solution.py:218
  15.1 0.0 collective-permute-done.1.refs_1_
  15.1 3.7 %collective-permute-start.2 = (bf16[1,64,512]{2,1,0:T(8,128)(2,1)S(1)}, bf16[1,64,512]{2,1,0:T(8,128)(2,1)S(1)}, u32[]{:S(2)}, u32[]{:S(2)}) collective-permute-start(bf16[1,64,512]{2,1,0:T(8,128)(2,1)S(1)} %sum_far_share.1), channel_id=1, source_target_pairs={{12,0},{8,4},{4,8},{0,12},{13,1},{9,5},{5,9},{1,13},{14,2},{10,6},... | collective-permute-start | bytes 196616 | tf_op jit(solution)/shard_map/ppermute | solution.py:218
  18.8 0.0 collective-permute-done.3.refs_3_
  18.8 0.8 %collective-permute-done.4.refs_4_ = bf16[1,64,512]{2,1,0:T(8,128)(2,1)S(1)} collective-permute-done((bf16[1,64,512]{2,1,0:T(8,128)(2,1)S(1)}, bf16[1,64,512]{2,1,0:T(8,128)(2,1)S(1)}, u32[]{:S(2)}, u32[]{:S(2)}) %collective-permute-start.4) | collective-permute-done | bytes 65568 | tf_op jit(solution)/shard_map/ppermute | solution.py:218
  19.6 0.0 collective-permute-done.5.refs_5_
  19.6 0.0 collective-permute-done.6.refs_6_
  19.6 2.0 %collective-permute-done.2.refs_2_ = bf16[1,64,512]{2,1,0:T(8,128)(2,1)S(1)} collective-permute-done((bf16[1,64,512]{2,1,0:T(8,128)(2,1)S(1)}, bf16[1,64,512]{2,1,0:T(8,128)(2,1)S(1)}, u32[]{:S(2)}, u32[]{:S(2)}) %collective-permute-start.2) | collective-permute-done | bytes 65568 | tf_op jit(solution)/shard_map/ppermute | solution.py:218
  21.6 0.1 sum_first_sigma.1.refs_3_
  21.7 1.4 %collective-permute-start.8 = (bf16[1,64,512]{2,1,0:T(8,128)(2,1)S(1)}, bf16[1,64,512]{2,1,0:T(8,128)(2,1)S(1)}, u32[]{:S(2)}, u32[]{:S(2)}) collective-permute-start(bf16[1,64,512]{2,1,0:T(8,128)(2,1)S(1)} %sum_first_sigma.1.refs_3_), channel_id=1, source_target_pairs={{8,0},{12,4},{0,8},{4,12},{9,1},{13,5},{1,9},{5,13},{10,2},{14,6},... | collective-permute-start | bytes 196616 | tf_op jit(solution)/shard_map/ppermute | solution.py:218
  23.1 2.3 %collective-permute-start.7 = (bf16[1,64,512]{2,1,0:T(8,128)(2,1)S(1)}, bf16[1,64,512]{2,1,0:T(8,128)(2,1)S(1)}, u32[]{:S(2)}, u32[]{:S(2)}) collective-permute-start(bf16[1,64,512]{2,1,0:T(8,128)(2,1)S(1)} %sum_first_sigma.1.refs_3_), channel_id=1, source_target_pairs={{12,0},{8,4},{4,8},{0,12},{13,1},{9,5},{5,9},{1,13},{14,2},{10,6},... | collective-permute-start | bytes 196616 | tf_op jit(solution)/shard_map/ppermute | solution.py:218
  25.4 0.5 collective-permute-start.9
  25.9 0.7 %collective-permute-start.15 = (bf16[1,64,512]{2,1,0:T(8,128)(2,1)S(1)}, bf16[1,64,512]{2,1,0:T(8,128)(2,1)S(1)}, u32[]{:S(2)}, u32[]{:S(2)}) collective-permute-start(bf16[1,64,512]{2,1,0:T(8,128)(2,1)S(1)} %sum_first_sigma.1.refs_3_), channel_id=1, source_target_pairs={{2,0},{0,2},{3,1},{1,3},{6,4},{4,6},{7,5},{5,7},{10,8},{8,10},{11,... | collective-permute-start | bytes 196616 | tf_op jit(solution)/shard_map/ppermute | solution.py:218
  26.6 2.3 %collective-permute-start.14 = (bf16[1,64,512]{2,1,0:T(8,128)(2,1)S(1)}, bf16[1,64,512]{2,1,0:T(8,128)(2,1)S(1)}, u32[]{:S(2)}, u32[]{:S(2)}) collective-permute-start(bf16[1,64,512]{2,1,0:T(8,128)(2,1)S(1)} %sum_first_sigma.1.refs_3_), channel_id=1, source_target_pairs={{6,0},{4,2},{2,4},{0,6},{14,8},{12,10},{10,12},{8,14},{7,1},{5,3},... | collective-permute-start | bytes 196616 | tf_op jit(solution)/shard_map/ppermute | solution.py:218
  28.9 0.1 collective-permute-done.8.refs_1_
  29.0 0.4 collective-permute-start.13
  29.4 0.4 collective-permute-done.7.refs_0_
  29.8 1.2 %collective-permute-start.12 = (bf16[1,64,512]{2,1,0:T(8,128)(2,1)S(1)}, bf16[1,64,512]{2,1,0:T(8,128)(2,1)S(1)}, u32[]{:S(2)}, u32[]{:S(2)}) collective-permute-start(bf16[1,64,512]{2,1,0:T(8,128)(2,1)S(1)} %collective-permute-done.7.refs_0_), channel_id=1, source_target_pairs={{2,0},{0,2},{3,1},{1,3},{6,4},{4,6},{7,5},{5,7},{10,8},{8,10},{11,... | collective-permute-start | bytes 196616 | tf_op jit(solution)/shard_map/ppermute | solution.py:218
  31.1 0.0 collective-permute-done.9.refs_2_
  31.1 0.1 collective-permute-start.10
  31.2 0.0 collective-permute-done.15.refs_3_
  31.2 0.7 %collective-permute-done.14.refs_2_ = bf16[1,64,512]{2,1,0:T(8,128)(2,1)S(1)} collective-permute-done((bf16[1,64,512]{2,1,0:T(8,128)(2,1)S(1)}, bf16[1,64,512]{2,1,0:T(8,128)(2,1)S(1)}, u32[]{:S(2)}, u32[]{:S(2)}) %collective-permute-start.14) | collective-permute-done | bytes 65568 | tf_op jit(solution)/shard_map/ppermute | solution.py:218
  31.9 1.4 %collective-permute-done.13.refs_1_ = bf16[1,64,512]{2,1,0:T(8,128)(2,1)S(1)} collective-permute-done((bf16[1,64,512]{2,1,0:T(8,128)(2,1)S(1)}, bf16[1,64,512]{2,1,0:T(8,128)(2,1)S(1)}, u32[]{:S(2)}, u32[]{:S(2)}) %collective-permute-start.13) | collective-permute-done | bytes 65568 | tf_op jit(solution)/shard_map/ppermute | solution.py:218
  33.3 0.8 %collective-permute-done.12.refs_0_ = bf16[1,64,512]{2,1,0:T(8,128)(2,1)S(1)} collective-permute-done((bf16[1,64,512]{2,1,0:T(8,128)(2,1)S(1)}, bf16[1,64,512]{2,1,0:T(8,128)(2,1)S(1)}, u32[]{:S(2)}, u32[]{:S(2)}) %collective-permute-start.12) | collective-permute-done | bytes 65568 | tf_op jit(solution)/shard_map/ppermute | solution.py:218
  34.1 0.1 collective-permute-start.16
  34.2 0.0 collective-permute-done.10.sigma_other.other
  34.2 0.7 %left_products.1.products = f32[4,256,512]{2,1,0:T(8,128)S(1)} custom-call(bf16[4,256,256]{2,1,0:T(8,128)(2,1)S(1)} %get-tuple-element.19.refs_3_.left_own, bf16[4,256,256]{2,1,0:T(8,128)(2,1)S(1)} %get-tuple-element.20.refs_4_.left_other, bf16[1,256,512]{2,1,0:T(8,128)(2,1)S(1)} %place_own_sector.1.sigma_own.own, ...), custom_call_target="tpu_custom_call" | custom-call | tf_op jit(solution)/shard_map/left_products/pallas_call | solution.py:236
  34.9 0.8 %collective-permute-done.16.other = bf16[1,256,512]{2,1,0:T(8,128)(2,1)S(1)} collective-permute-done((bf16[1,256,512]{2,1,0:T(8,128)(2,1)S(1)}, bf16[1,256,512]{2,1,0:T(8,128)(2,1)S(1)}, u32[]{:S(2)}, u32[]{:S(2)}) %collective-permute-start.16) | collective-permute-done | bytes 262176 | tf_op jit(solution)/shard_map/ppermute | solution.py:218
  35.7 2.2 %second_sigma_terms.1 = (f32[1,64,512]{2,1,0:T(8,128)S(1)}, bf16[1,64,512]{2,1,0:T(8,128)(2,1)S(1)}, bf16[1,64,512]{2,1,0:T(8,128)(2,1)S(1)}, bf16[1,64,512]{2,1,0:T(8,128)(2,1)S(1)}) custom-call(s32[2,2]{1,0:T(2,128)S(1)} %copy-done.2, s32[4,2,8]{2,1,0:T(2,128)S(1)} %bitcast.2, f32[4,8]{1,0:T(4,128)S(1)} %copy-done.3, ...), custom_call_target="tpu_custom_call" | custom-call | tf_op jit(solution)/shard_map/second_sigma_terms/pallas_call | solution.py:236
  37.9 2.8 %collective-permute-start.17 = (bf16[1,64,512]{2,1,0:T(8,128)(2,1)S(1)}, bf16[1,64,512]{2,1,0:T(8,128)(2,1)S(1)}, u32[]{:S(2)}, u32[]{:S(2)}) collective-permute-start(bf16[1,64,512]{2,1,0:T(8,128)(2,1)S(1)} %get-tuple-element.33), channel_id=1, source_target_pairs={{12,0},{8,4},{4,8},{0,12},{13,1},{9,5},{5,9},{1,13},{14,2},{10,6},... | collective-permute-start | bytes 196616 | tf_op jit(solution)/shard_map/ppermute | solution.py:218
  40.7 0.0 collective-permute-start.18
  40.7 1.6 %collective-permute-start.19 = (bf16[1,64,512]{2,1,0:T(8,128)(2,1)S(1)}, bf16[1,64,512]{2,1,0:T(8,128)(2,1)S(1)}, u32[]{:S(2)}, u32[]{:S(2)}) collective-permute-start(bf16[1,64,512]{2,1,0:T(8,128)(2,1)S(1)} %get-tuple-element.35), channel_id=1, source_target_pairs={{4,0},{0,4},{12,8},{8,12},{5,1},{1,5},{13,9},{9,13},{6,2},{2,6},{1... | collective-permute-start | bytes 196616 | tf_op jit(solution)/shard_map/ppermute | solution.py:218
  42.4 0.5 sums_for_rayleigh.1.refs_0_.refs_4_
  42.9 1.3 %collective-permute-start.11 = (f32[3,8,128]{2,1,0:T(8,128)S(1)}, f32[3,8,128]{2,1,0:T(8,128)S(1)}, u32[]{:S(2)}, u32[]{:S(2)}) collective-permute-start(f32[3,8,128]{2,1,0:T(8,128)S(1)} %sums_for_rayleigh.1.refs_0_.refs_4_), channel_id=1, source_target_pairs={{2,0},{0,2},{3,1},{1,3},{6,4},{4,6},{7,5},{5,7},{10,8},{8,10},{11,... | collective-permute-start | bytes 36872 | tf_op jit(solution)/shard_map/ppermute | solution.py:218
  44.2 2.5 %collective-permute-done.11.refs_1_.refs_5_ = f32[3,8,128]{2,1,0:T(8,128)S(1)} collective-permute-done((f32[3,8,128]{2,1,0:T(8,128)S(1)}, f32[3,8,128]{2,1,0:T(8,128)S(1)}, u32[]{:S(2)}, u32[]{:S(2)}) %collective-permute-start.11) | collective-permute-done | bytes 12320 | tf_op jit(solution)/shard_map/ppermute | solution.py:218
  46.6 0.0 collective-permute-done.17.refs_1_
  46.6 0.2 collective-permute-done.18.refs_2_
  46.8 0.0 collective-permute-done.19.refs_3_
  46.9 2.6 %collective-permute-start.22 = (bf16[1,64,512]{2,1,0:T(8,128)(2,1)S(1)}, bf16[1,64,512]{2,1,0:T(8,128)(2,1)S(1)}, u32[]{:S(2)}, u32[]{:S(2)}) collective-permute-start(bf16[1,64,512]{2,1,0:T(8,128)(2,1)S(1)} %sum_second_sigma.1.refs_0_), channel_id=1, source_target_pairs={{12,0},{8,4},{4,8},{0,12},{13,1},{9,5},{5,9},{1,13},{14,2},{10,6},... | collective-permute-start | bytes 196616 | tf_op jit(solution)/shard_map/ppermute | solution.py:218
  49.5 0.0 collective-permute-start.21
  49.5 1.8 %collective-permute-start.20 = (bf16[1,64,512]{2,1,0:T(8,128)(2,1)S(1)}, bf16[1,64,512]{2,1,0:T(8,128)(2,1)S(1)}, u32[]{:S(2)}, u32[]{:S(2)}) collective-permute-start(bf16[1,64,512]{2,1,0:T(8,128)(2,1)S(1)} %sum_second_sigma.1.refs_0_), channel_id=1, source_target_pairs={{4,0},{0,4},{12,8},{8,12},{5,1},{1,5},{13,9},{9,13},{6,2},{2,6},{1... | collective-permute-start | bytes 196616 | tf_op jit(solution)/shard_map/ppermute | solution.py:218
  51.3 1.4 %second_wave.1 = (bf16[1,256,512]{2,1,0:T(8,128)(2,1)}, f32[2,8,128]{2,1,0:T(8,128)S(1)}) custom-call(s32[2,2]{1,0:T(2,128)S(1)} %copy-done.2, bf16[256,512]{1,0:T(8,128)(2,1)S(1)} %get-tuple-element.21.wave_own, bf16[1,256,512]{2,1,0:T(8,128)(2,1)S(1)} %place_own_sector.1.sigma_own.own, f32[3,8,128]{2,1,0:T(8,128)S(1)} %sums_for_rayleigh.1.refs_0_.refs_4_, ...), custom_call_target="tpu_custom_call" | custom-call | tf_op jit(solution)/shard_map/second_wave/pallas_call | solution.py:236
  52.8 0.8 %collective-permute-done.22.refs_3_ = bf16[1,64,512]{2,1,0:T(8,128)(2,1)S(1)} collective-permute-done((bf16[1,64,512]{2,1,0:T(8,128)(2,1)S(1)}, bf16[1,64,512]{2,1,0:T(8,128)(2,1)S(1)}, u32[]{:S(2)}, u32[]{:S(2)}) %collective-permute-start.22) | collective-permute-done | bytes 65568 | tf_op jit(solution)/shard_map/ppermute | solution.py:218
  53.6 2.1 %collective-permute-done.21.refs_2_ = bf16[1,64,512]{2,1,0:T(8,128)(2,1)S(1)} collective-permute-done((bf16[1,64,512]{2,1,0:T(8,128)(2,1)S(1)}, bf16[1,64,512]{2,1,0:T(8,128)(2,1)S(1)}, u32[]{:S(2)}, u32[]{:S(2)}) %collective-permute-start.21) | collective-permute-done | bytes 65568 | tf_op jit(solution)/shard_map/ppermute | solution.py:218
  55.7 0.0 collective-permute-done.20.refs_1_
  55.7 0.9 %join_second_sigma.1 = f32[1,256,512]{2,1,0:T(8,128)} custom-call(f32[2,8,128]{2,1,0:T(8,128)S(1)} %get-tuple-element.30.factors, bf16[1,256,512]{2,1,0:T(8,128)(2,1)S(1)} %place_own_sector.1.sigma_own.own, bf16[1,64,512]{2,1,0:T(8,128)(2,1)S(1)} %sum_second_sigma.1.refs_0_, bf16[1,64,512]{2,1,0:T(8,128)(2,1)S(1)} %collective-permute-done.20.refs_1_, ...), custom_call_target="tpu_custom_call" | custom-call | tf_op jit(solution)/shard_map/join_second_sigma/pallas_call | solution.py:236
  (4 shorter events, 0.1 us)
Async XLA Ops:
  0.6 1.9 %copy-start = (bf16[1,256,512]{2,1,0:T(8,128)(2,1)S(1)}, bf16[1,256,512]{2,1,0:T(8,128)(2,1)}, u32[]{:S(2)}) copy-start(bf16[1,256,512]{2,1,0:T(8,128)(2,1)} %refs_6_.1) | copy-start | bytes 786436
  0.6 1.9 %copy-start.2 = (s32[2,2]{1,0:T(2,128)S(1)}, s32[2,2]{1,0:T(2,128)}, u32[]{:S(2)}) copy-start(s32[2,2]{1,0:T(2,128)} %sizes_ref.3) | copy-start | bytes 52
  0.7 1.9 %copy-start.3 = (f32[4,8]{1,0:T(4,128)S(1)}, f32[4,8]{1,0:T(4,128)}, u32[]{:S(2)}) copy-start(f32[4,8]{1,0:T(4,128)} %weights_ref.1) | copy-start | bytes 388
  0.7 1.9 %copy-start.1 = (s32[4,8,2]{1,2,0:T(2,128)S(1)}, s32[4,8,2]{1,2,0:T(2,128)}, u32[]{:S(2)}) copy-start(s32[4,8,2]{1,2,0:T(2,128)} %param.10) | copy-start | bytes 772
  0.7 1.9 %collective-permute-start = (bf16[1,256,512]{2,1,0:T(8,128)(2,1)}, bf16[1,256,512]{2,1,0:T(8,128)(2,1)S(1)}, u32[]{:S(2)}, u32[]{:S(2)}) collective-permute-start(bf16[1,256,512]{2,1,0:T(8,128)(2,1)} %refs_6_.1), channel_id=1, source_target_pairs={{1,0},{0,1},{3,2},{2,3},{5,4},{4,5},{7,6},{6,7},{9,8},{8,9},{11,10... | collective-permute-start | bytes 786440 | tf_op jit(solution)/shard_map/ppermute | solution.py:218
  6.3 8.8 %collective-permute-start.1 = (bf16[2,64,512]{2,1,0:T(8,128)(2,1)S(1)}, bf16[2,64,512]{2,1,0:T(8,128)(2,1)S(1)}, u32[]{:S(2)}, u32[]{:S(2)}) collective-permute-start(bf16[2,64,512]{2,1,0:T(8,128)(2,1)S(1)} %get-tuple-element.23), channel_id=1, source_target_pairs={{2,0},{0,2},{3,1},{1,3},{6,4},{4,6},{7,5},{5,7},{10,8},{8,10},{11,... | collective-permute-start | bytes 393224 | tf_op jit(solution)/shard_map/ppermute | solution.py:218
  9.2 9.6 %collective-permute-start.3 = (bf16[1,64,512]{2,1,0:T(8,128)(2,1)S(1)}, bf16[1,64,512]{2,1,0:T(8,128)(2,1)S(1)}, u32[]{:S(2)}, u32[]{:S(2)}) collective-permute-start(bf16[1,64,512]{2,1,0:T(8,128)(2,1)S(1)} %get-tuple-element.24), channel_id=1, source_target_pairs={{8,0},{12,4},{0,8},{4,12},{9,1},{13,5},{1,9},{5,13},{10,2},{14,6},... | collective-permute-start | bytes 196616 | tf_op jit(solution)/shard_map/ppermute | solution.py:218
  11.8 7.8 %collective-permute-start.4 = (bf16[1,64,512]{2,1,0:T(8,128)(2,1)S(1)}, bf16[1,64,512]{2,1,0:T(8,128)(2,1)S(1)}, u32[]{:S(2)}, u32[]{:S(2)}) collective-permute-start(bf16[1,64,512]{2,1,0:T(8,128)(2,1)S(1)} %get-tuple-element.25), channel_id=1, source_target_pairs={{10,0},{8,2},{14,4},{12,6},{2,8},{0,10},{6,12},{4,14},{11,1},{9,3}... | collective-permute-start | bytes 196616 | tf_op jit(solution)/shard_map/ppermute | solution.py:218
  11.8 7.8 %collective-permute-start.5 = (bf16[1,64,512]{2,1,0:T(8,128)(2,1)S(1)}, bf16[1,64,512]{2,1,0:T(8,128)(2,1)S(1)}, u32[]{:S(2)}, u32[]{:S(2)}) collective-permute-start(bf16[1,64,512]{2,1,0:T(8,128)(2,1)S(1)} %get-tuple-element.26), channel_id=1, source_target_pairs={{4,0},{0,4},{12,8},{8,12},{5,1},{1,5},{13,9},{9,13},{6,2},{2,6},{1... | collective-permute-start | bytes 196616 | tf_op jit(solution)/shard_map/ppermute | solution.py:218
  13.7 5.9 %collective-permute-start.6 = (bf16[1,64,512]{2,1,0:T(8,128)(2,1)S(1)}, bf16[1,64,512]{2,1,0:T(8,128)(2,1)S(1)}, u32[]{:S(2)}, u32[]{:S(2)}) collective-permute-start(bf16[1,64,512]{2,1,0:T(8,128)(2,1)S(1)} %get-tuple-element.27), channel_id=1, source_target_pairs={{6,0},{4,2},{2,4},{0,6},{14,8},{12,10},{10,12},{8,14},{7,1},{5,3},... | collective-permute-start | bytes 196616 | tf_op jit(solution)/shard_map/ppermute | solution.py:218
  15.1 6.5 %collective-permute-start.2 = (bf16[1,64,512]{2,1,0:T(8,128)(2,1)S(1)}, bf16[1,64,512]{2,1,0:T(8,128)(2,1)S(1)}, u32[]{:S(2)}, u32[]{:S(2)}) collective-permute-start(bf16[1,64,512]{2,1,0:T(8,128)(2,1)S(1)} %sum_far_share.1), channel_id=1, source_target_pairs={{12,0},{8,4},{4,8},{0,12},{13,1},{9,5},{5,9},{1,13},{14,2},{10,6},... | collective-permute-start | bytes 196616 | tf_op jit(solution)/shard_map/ppermute | solution.py:218
  21.7 7.3 %collective-permute-start.8 = (bf16[1,64,512]{2,1,0:T(8,128)(2,1)S(1)}, bf16[1,64,512]{2,1,0:T(8,128)(2,1)S(1)}, u32[]{:S(2)}, u32[]{:S(2)}) collective-permute-start(bf16[1,64,512]{2,1,0:T(8,128)(2,1)S(1)} %sum_first_sigma.1.refs_3_), channel_id=1, source_target_pairs={{8,0},{12,4},{0,8},{4,12},{9,1},{13,5},{1,9},{5,13},{10,2},{14,6},... | collective-permute-start | bytes 196616 | tf_op jit(solution)/shard_map/ppermute | solution.py:218
  23.1 6.8 %collective-permute-start.7 = (bf16[1,64,512]{2,1,0:T(8,128)(2,1)S(1)}, bf16[1,64,512]{2,1,0:T(8,128)(2,1)S(1)}, u32[]{:S(2)}, u32[]{:S(2)}) collective-permute-start(bf16[1,64,512]{2,1,0:T(8,128)(2,1)S(1)} %sum_first_sigma.1.refs_3_), channel_id=1, source_target_pairs={{12,0},{8,4},{4,8},{0,12},{13,1},{9,5},{5,9},{1,13},{14,2},{10,6},... | collective-permute-start | bytes 196616 | tf_op jit(solution)/shard_map/ppermute | solution.py:218
  25.4 5.7 %collective-permute-start.9 = (bf16[1,64,512]{2,1,0:T(8,128)(2,1)S(1)}, bf16[1,64,512]{2,1,0:T(8,128)(2,1)S(1)}, u32[]{:S(2)}, u32[]{:S(2)}) collective-permute-start(bf16[1,64,512]{2,1,0:T(8,128)(2,1)S(1)} %sum_first_sigma.1.refs_3_), channel_id=1, source_target_pairs={{4,0},{0,4},{12,8},{8,12},{5,1},{1,5},{13,9},{9,13},{6,2},{2,6},{1... | collective-permute-start | bytes 196616 | tf_op jit(solution)/shard_map/ppermute | solution.py:218
  25.9 5.3 %collective-permute-start.15 = (bf16[1,64,512]{2,1,0:T(8,128)(2,1)S(1)}, bf16[1,64,512]{2,1,0:T(8,128)(2,1)S(1)}, u32[]{:S(2)}, u32[]{:S(2)}) collective-permute-start(bf16[1,64,512]{2,1,0:T(8,128)(2,1)S(1)} %sum_first_sigma.1.refs_3_), channel_id=1, source_target_pairs={{2,0},{0,2},{3,1},{1,3},{6,4},{4,6},{7,5},{5,7},{10,8},{8,10},{11,... | collective-permute-start | bytes 196616 | tf_op jit(solution)/shard_map/ppermute | solution.py:218
  26.6 5.3 %collective-permute-start.14 = (bf16[1,64,512]{2,1,0:T(8,128)(2,1)S(1)}, bf16[1,64,512]{2,1,0:T(8,128)(2,1)S(1)}, u32[]{:S(2)}, u32[]{:S(2)}) collective-permute-start(bf16[1,64,512]{2,1,0:T(8,128)(2,1)S(1)} %sum_first_sigma.1.refs_3_), channel_id=1, source_target_pairs={{6,0},{4,2},{2,4},{0,6},{14,8},{12,10},{10,12},{8,14},{7,1},{5,3},... | collective-permute-start | bytes 196616 | tf_op jit(solution)/shard_map/ppermute | solution.py:218
  29.0 4.3 %collective-permute-start.13 = (bf16[1,64,512]{2,1,0:T(8,128)(2,1)S(1)}, bf16[1,64,512]{2,1,0:T(8,128)(2,1)S(1)}, u32[]{:S(2)}, u32[]{:S(2)}) collective-permute-start(bf16[1,64,512]{2,1,0:T(8,128)(2,1)S(1)} %collective-permute-done.8.refs_1_), channel_id=1, source_target_pairs={{2,0},{0,2},{3,1},{1,3},{6,4},{4,6},{7,5},{5,7},{10,8},{8,10},{11,... | collective-permute-start | bytes 196616 | tf_op jit(solution)/shard_map/ppermute | solution.py:218
  29.8 4.3 %collective-permute-start.12 = (bf16[1,64,512]{2,1,0:T(8,128)(2,1)S(1)}, bf16[1,64,512]{2,1,0:T(8,128)(2,1)S(1)}, u32[]{:S(2)}, u32[]{:S(2)}) collective-permute-start(bf16[1,64,512]{2,1,0:T(8,128)(2,1)S(1)} %collective-permute-done.7.refs_0_), channel_id=1, source_target_pairs={{2,0},{0,2},{3,1},{1,3},{6,4},{4,6},{7,5},{5,7},{10,8},{8,10},{11,... | collective-permute-start | bytes 196616 | tf_op jit(solution)/shard_map/ppermute | solution.py:218
  31.1 3.1 %collective-permute-start.10 = (bf16[1,256,512]{2,1,0:T(8,128)(2,1)S(1)}, bf16[1,256,512]{2,1,0:T(8,128)(2,1)S(1)}, u32[]{:S(2)}, u32[]{:S(2)}) collective-permute-start(bf16[1,256,512]{2,1,0:T(8,128)(2,1)S(1)} %place_own_sector.1.sigma_own.own), channel_id=1, source_target_pairs={{1,0},{0,1},{3,2},{2,3},{5,4},{4,5},{7,6},{6,7},{9,8},{8,9},{11,10... | collective-permute-start | bytes 786440 | tf_op jit(solution)/shard_map/ppermute | solution.py:218
  34.1 1.6 %collective-permute-start.16 = (bf16[1,256,512]{2,1,0:T(8,128)(2,1)S(1)}, bf16[1,256,512]{2,1,0:T(8,128)(2,1)S(1)}, u32[]{:S(2)}, u32[]{:S(2)}) collective-permute-start(bf16[1,256,512]{2,1,0:T(8,128)(2,1)S(1)} %place_other_sectors.1.own), channel_id=1, source_target_pairs={{1,0},{0,1},{3,2},{2,3},{5,4},{4,5},{7,6},{6,7},{9,8},{8,9},{11,10... | collective-permute-start | bytes 786440 | tf_op jit(solution)/shard_map/ppermute | solution.py:218
  37.9 8.7 %collective-permute-start.17 = (bf16[1,64,512]{2,1,0:T(8,128)(2,1)S(1)}, bf16[1,64,512]{2,1,0:T(8,128)(2,1)S(1)}, u32[]{:S(2)}, u32[]{:S(2)}) collective-permute-start(bf16[1,64,512]{2,1,0:T(8,128)(2,1)S(1)} %get-tuple-element.33), channel_id=1, source_target_pairs={{12,0},{8,4},{4,8},{0,12},{13,1},{9,5},{5,9},{1,13},{14,2},{10,6},... | collective-permute-start | bytes 196616 | tf_op jit(solution)/shard_map/ppermute | solution.py:218
  40.7 6.1 %collective-permute-start.18 = (bf16[1,64,512]{2,1,0:T(8,128)(2,1)S(1)}, bf16[1,64,512]{2,1,0:T(8,128)(2,1)S(1)}, u32[]{:S(2)}, u32[]{:S(2)}) collective-permute-start(bf16[1,64,512]{2,1,0:T(8,128)(2,1)S(1)} %get-tuple-element.34), channel_id=1, source_target_pairs={{8,0},{12,4},{0,8},{4,12},{9,1},{13,5},{1,9},{5,13},{10,2},{14,6},... | collective-permute-start | bytes 196616 | tf_op jit(solution)/shard_map/ppermute | solution.py:218
  40.7 6.1 %collective-permute-start.19 = (bf16[1,64,512]{2,1,0:T(8,128)(2,1)S(1)}, bf16[1,64,512]{2,1,0:T(8,128)(2,1)S(1)}, u32[]{:S(2)}, u32[]{:S(2)}) collective-permute-start(bf16[1,64,512]{2,1,0:T(8,128)(2,1)S(1)} %get-tuple-element.35), channel_id=1, source_target_pairs={{4,0},{0,4},{12,8},{8,12},{5,1},{1,5},{13,9},{9,13},{6,2},{2,6},{1... | collective-permute-start | bytes 196616 | tf_op jit(solution)/shard_map/ppermute | solution.py:218
  42.9 3.8 %collective-permute-start.11 = (f32[3,8,128]{2,1,0:T(8,128)S(1)}, f32[3,8,128]{2,1,0:T(8,128)S(1)}, u32[]{:S(2)}, u32[]{:S(2)}) collective-permute-start(f32[3,8,128]{2,1,0:T(8,128)S(1)} %sums_for_rayleigh.1.refs_0_.refs_4_), channel_id=1, source_target_pairs={{2,0},{0,2},{3,1},{1,3},{6,4},{4,6},{7,5},{5,7},{10,8},{8,10},{11,... | collective-permute-start | bytes 36872 | tf_op jit(solution)/shard_map/ppermute | solution.py:218
  46.9 6.7 %collective-permute-start.22 = (bf16[1,64,512]{2,1,0:T(8,128)(2,1)S(1)}, bf16[1,64,512]{2,1,0:T(8,128)(2,1)S(1)}, u32[]{:S(2)}, u32[]{:S(2)}) collective-permute-start(bf16[1,64,512]{2,1,0:T(8,128)(2,1)S(1)} %sum_second_sigma.1.refs_0_), channel_id=1, source_target_pairs={{12,0},{8,4},{4,8},{0,12},{13,1},{9,5},{5,9},{1,13},{14,2},{10,6},... | collective-permute-start | bytes 196616 | tf_op jit(solution)/shard_map/ppermute | solution.py:218
  49.5 6.2 %collective-permute-start.21 = (bf16[1,64,512]{2,1,0:T(8,128)(2,1)S(1)}, bf16[1,64,512]{2,1,0:T(8,128)(2,1)S(1)}, u32[]{:S(2)}, u32[]{:S(2)}) collective-permute-start(bf16[1,64,512]{2,1,0:T(8,128)(2,1)S(1)} %sum_second_sigma.1.refs_0_), channel_id=1, source_target_pairs={{8,0},{12,4},{0,8},{4,12},{9,1},{13,5},{1,9},{5,13},{10,2},{14,6},... | collective-permute-start | bytes 196616 | tf_op jit(solution)/shard_map/ppermute | solution.py:218
  49.5 6.2 %collective-permute-start.20 = (bf16[1,64,512]{2,1,0:T(8,128)(2,1)S(1)}, bf16[1,64,512]{2,1,0:T(8,128)(2,1)S(1)}, u32[]{:S(2)}, u32[]{:S(2)}) collective-permute-start(bf16[1,64,512]{2,1,0:T(8,128)(2,1)S(1)} %sum_second_sigma.1.refs_0_), channel_id=1, source_target_pairs={{4,0},{0,4},{12,8},{8,12},{5,1},{1,5},{13,9},{9,13},{6,2},{2,6},{1... | collective-permute-start | bytes 196616 | tf_op jit(solution)/shard_map/ppermute | solution.py:218

commit v8 on v7

--- a/solution.py
+++ b/solution.py
@@ -33,16 +33,16 @@
     )
 
 
-def times_right(values, right, term):
+def times_right(values, right):
     return lax.dot_general(
         values.astype(jnp.bfloat16),
-        right[term],
+        right,
         (((1,), (1,)), ((), ())),
         preferred_element_type=jnp.float32,
     )
 
 
-def load_kernel(left_ref, left_own, left_other, sems):
+def load_kernel(left_ref, right_ref, left_own, left_other, right, sems):
     rows = left_own.shape[1]
     core = lax.axis_index("rep")
     copies = []
@@ -50,6 +50,8 @@
         mine = pl.ds(pl.multiple_of(core * rows, rows), rows)
         columns = pl.ds(pl.multiple_of(place * rows, rows), rows)
         copies.append(pltpu.make_async_copy(left_ref.at[:, mine, columns], half, sems.at[index]))
+    loaded = right_ref.at[pl.ds(0, right.shape[0])]
+    copies.append(pltpu.make_async_copy(loaded, right, sems.at[2]))
     for copy in copies:
         copy.start()
     for copy in copies:
@@ -57,13 +59,14 @@
 
 
 def first_kernel(shares, *refs):
-    sizes_ref, pairs_ref, weights_ref, left_own, left_other, right_ref, wave, arrived = refs[:8]
-    right, own, other, *parts = refs[8:-2]
+    sizes_ref, pairs_ref, weights_ref, left_own, left_other, loaded, right_ref = refs[:7]
+    wave, arrived, right, own, other, *parts = refs[7:-2]
     held, sems = refs[-2:]
+    early = loaded.shape[0]
     rows, columns = own.shape
     share = parts[0].shape[-2]
     copies = [
-        pltpu.make_async_copy(right_ref.at[term], right.at[term], sems.at[term])
+        pltpu.make_async_copy(right_ref.at[early + term], right.at[term], sems.at[term])
         for term in range(right.shape[0])
     ]
     for copy in copies:
@@ -77,10 +80,13 @@
     live = live_cells(sizes_ref, sector, (core ^ 1) * rows, rows, columns)
     other[...] = masked(arrived[0], live)
     totals = [None] * sectors
-    for term in range(right.shape[0]):
+    for term in range(left_own.shape[0]):
         product = left_times(left_own, left_other, term, own[...], other[...])
-        copies[term].wait()
-        product = times_right(product, right, term)
+        if term < early:
+            product = times_right(product, loaded[term])
+        else:
+            copies[term - early].wait()
+            product = times_right(product, right[term - early])
         for step in range(sectors):
             weight = mixing_scalar(pairs_ref, weights_ref, term, sector ^ step, sector)
             part = weight * product
@@ -94,11 +100,14 @@
             out[index] = held[across, pl.ds(start, share), :].astype(out.dtype)
 
 
-def sum_kernel(indices, *refs):
+def sum_kernel(indices, handed, *refs):
     total = refs[0][indices[0]].astype(jnp.float32)
     for index, piece in zip(indices[1:], refs[1:]):
         total = total + piece[index].astype(jnp.float32)
-    refs[-1][0] = total.astype(refs[-1].dtype)
+    out, *copies = refs[len(refs) - handed - 1 :]
+    out[0] = total.astype(out.dtype)
+    for array, copy in zip(refs[len(indices) :], copies):
+        copy[...] = array[...]
 
 
 def place_kernel(spots, *refs):
@@ -110,35 +119,46 @@
         half[index, pl.ds(start, share), :] = piece[0]
 
 
-def left_kernel(left_own, left_other, own, other, out):
+def left_kernel(pairs_ref, weights_ref, left_own, left_other, own, other, across_own, out):
+    target = lax.axis_index("sec")
     for term in range(out.shape[0]):
-        out[term] = left_times(left_own, left_other, term, own[0], other[0])
-
-
-def second_kernel(
-    sizes_ref, pairs_ref, weights_ref, left_own, left_other, right, products, own, other, *refs
-):
-    shares, held = refs[:-1], refs[-1]
-    rows, columns = own.shape[1:]
+        weight = mixing_scalar(pairs_ref, weights_ref, term, target, target)
+        total = weight * left_times(left_own, left_other, term, own[0], other[0])
+        for step in range(across_own.shape[0]):
+            weight = mixing_scalar(pairs_ref, weights_ref, term, target, target ^ (step + 1))
+            total = total + weight * jnp.dot(
+                left_own[term], across_own[step], preferred_element_type=jnp.float32
+            )
+        out[term] = total
+
+
+def second_kernel(side, steps, *refs):
+    sizes_ref, pairs_ref, weights_ref, left_other, loaded, right, products, across = refs[:8]
+    shares, held = refs[8:-1], refs[-1]
+    half, columns = held.shape
     share = shares[0].shape[1]
     target = lax.axis_index("sec")
-    core = lax.axis_index("rep")
     place = lax.axis_index("ops")
+    count = lax.axis_size("ops") // 2
+    first = pl.multiple_of(((place // count) ^ side) * half, half)
+    mine = pl.ds(first, half)
     total = None
-    for term in range(right.shape[0]):
-        weight = mixing_scalar(pairs_ref, weights_ref, term, target, target)
-        combined = weight * products[term]
-        for step in range(own.shape[0]):
+    for term in range(products.shape[0]):
+        combined = products[term, mine, :]
+        for step in range(across.shape[0]):
             weight = mixing_scalar(pairs_ref, weights_ref, term, target, target ^ (step + 1))
-            combined = combined + weight * left_times(
-                left_own, left_other, term, own[step], other[step]
+            combined = combined + weight * jnp.dot(
+                left_other[term, mine, :], across[step], preferred_element_type=jnp.float32
             )
-        part = times_right(combined, right, term)
+        early = loaded.shape[0]
+        block = loaded[term] if term < early else right[term - early]
+        part = times_right(combined, block)
         total = part if total is None else total + part
-    live = live_cells(sizes_ref, target, core * rows, rows, columns)
+    row_start = lax.axis_index("rep") * (2 * half) + first
+    live = live_cells(sizes_ref, target, row_start, half, columns)
     held[...] = jnp.where(live, total, 0.0)
-    for step, out in enumerate(shares):
-        start = pl.multiple_of((place ^ step) * share, share)
+    for step, out in zip(steps, shares):
+        start = pl.multiple_of((place ^ step) % count * share, share)
         out[0] = held[pl.ds(start, share), :].astype(out.dtype)
 
 
@@ -192,7 +212,7 @@
     scale = jnp.broadcast_to(factors[0][:1, :1], (share, columns))
     shift = jnp.broadcast_to(factors[1][:1, :1], (share, columns))
     copies = []
-    for step, piece in enumerate(pieces):
+    for step, piece in zip(reversed(range(len(pieces))), pieces):
         rows = pl.ds(pl.multiple_of((place ^ step) * share, share), share)
         moved = shift * sigma_own[0, rows, :].astype(jnp.float32)
         held[step] = scale * piece[0].astype(jnp.float32) - moved
@@ -243,27 +263,35 @@
             name=name,
         )(*operands)
 
-    def summed(name, *pieces, after=()):
+    def summed(name, *pieces, after=(), handed=()):
         pieces = [piece if isinstance(piece, tuple) else (piece, 0) for piece in pieces]
         arrays, indices = zip(*pieces)
-        return call(
-            lambda *refs: sum_kernel(indices, *refs),
+        sums = call(
+            lambda *refs: sum_kernel(indices, len(handed), *refs),
             name,
-            shape(1, share, columns),
+            [shape(1, share, columns)] * (1 + len(handed)),
             [],
             *arrays,
+            *handed,
             *after,
         )
+        return sums if handed else sums[0]
 
     farthest_first = list(reversed(range(ops_count)))
     arrived = partner(wavefunction, {"rep": 1})
-    left_own, left_other = call(
+    early = terms // 2
+    left_own, left_other, loaded = call(
         load_kernel,
         "load_operators",
-        [shape(terms, rows, rows), shape(terms, rows, side - rows)],
-        [outside],
+        [
+            shape(terms, rows, rows),
+            shape(terms, rows, side - rows),
+            shape(early, *right_blocks.shape[1:]),
+        ],
+        [outside] * 2,
         left_blocks,
-        scratch=[pltpu.SemaphoreType.DMA((2,))],
+        right_blocks,
+        scratch=[pltpu.SemaphoreType.DMA((3,))],
         vmem=51,
     )
     pairs = jnp.swapaxes(sector_pairs, 1, 2)
@@ -276,28 +304,31 @@
     right, wave_own, wave_other, *rest = call(
         lambda *refs: first_kernel(spots, *refs),
         "first_sigma_terms",
-        [shape(*right_blocks.shape), shape(rows, columns), shape(rows, columns)]
+        [shape(terms - early, *right_blocks.shape[1:]), shape(rows, columns), shape(rows, columns)]
         + [
             shape(len(along), share, columns, dtype=f32 if along == (far, 0) and across == 0 else bf16)
             for along, across in spots
         ],
-        [smem] * 3 + [inside] * 2 + [outside],
+        [smem] * 3 + [inside] * 3 + [outside],
         *scalars,
         left_own,
         left_other,
+        loaded,
         right_blocks,
         wavefunction,
         arrived,
         scratch=[
             pltpu.VMEM((sectors, rows, columns), f32),
-            pltpu.SemaphoreType.DMA((terms,)),
+            pltpu.SemaphoreType.DMA((terms - early,)),
         ],
         vmem=49,
     )
-    operators = scalars + (left_own, left_other, right)
     rest = dict(zip(spots, rest))
     met = [partner(rest[(far, 0), across], {"sec": across}) for across in range(sectors)]
-    received = [partner(summed("sum_far_share", *met), {"ops": far})]
+    diagonal = [((1,), across) for across in range(1, sectors)]
+    far_sum, *handed = summed("sum_far_share", *met, handed=[rest[spot] for spot in diagonal])
+    rest.update(zip(diagonal, handed))
+    received = [partner(far_sum, {"ops": far})]
     received += [
         partner(rest[along, across], {"ops": along[0], "sec": across})
         for along in direct
@@ -333,23 +364,30 @@
         left_kernel,
         "left_products",
         shape(terms, rows, columns, dtype=f32),
-        [],
+        [smem] * 2,
+        *scalars[1:],
         left_own,
         left_other,
         sigma_own,
         sigma_other,
-    )
-    shares = call(
-        second_kernel,
-        "second_sigma_terms",
-        [shape(1, share, columns, dtype=f32)] + [shape(1, share, columns)] * (ops_count - 1),
-        [smem] * 3,
-        *operators,
-        products,
         across_own,
-        across_other,
-        scratch=[pltpu.VMEM((rows, columns), f32)],
-    )
+    )
+    shares = []
+    for side, steps in ((1, farthest_first[: ops_count // 2]), (0, farthest_first[ops_count // 2 :])):
+        shares += call(
+            lambda *refs, side=side, steps=steps: second_kernel(side, steps, *refs),
+            "second_sigma_far" if side else "second_sigma_near",
+            [shape(1, share, columns, dtype=bf16 if step else f32) for step in steps],
+            [smem] * 3,
+            *scalars,
+            left_other,
+            loaded,
+            right,
+            products,
+            across_other,
+            scratch=[pltpu.VMEM((rows // 2, columns), f32)],
+        )
+    shares = dict(zip(farthest_first, shares))
     received = [partner(shares[step], {"ops": step}) for step in farthest_first[:-1]]
     sums = call(
         sums_kernel,
@@ -380,7 +418,7 @@
         [],
         factors,
         sigma_own,
-        *[partner(second_share, {"ops": step}) for step in range(ops_count)],
+        *[partner(second_share, {"ops": step}) for step in farthest_first],
         scratch=[
             pltpu.VMEM((ops_count, share, columns), f32),
             pltpu.SemaphoreType.DMA((ops_count,)),

time: 56.8 us -> 58.9 us (1.037)
  Pallas kernels: 10.8 us -> 13.3 us
  starting transfers between devices: 32.1 us -> 30.4 us
  waiting for transfers between devices: 12.9 us -> 14.1 us
    pallas_call x12 -> x13, Pallas kernels: 10.8 us -> 13.3 us  [call(): pl.pallas_call(kernel, out_shape=out_shape, in_specs=list(in_specs) + [in...]
    ppermute x23, starting transfers between devices: 32.1 us -> 30.4 us  [partner(): return lax.ppermute(value, axes, pairs)]
    ppermute x23, waiting for transfers between devices: 12.9 us -> 14.1 us  [partner(): return lax.ppermute(value, axes, pairs)]
  transfers between devices with their start and end apart: 23 -> 23, of which waited for: 13 -> 11; matrix products, arithmetic and copies ran while one was open for 0% -> 0% of each run, Pallas kernels for 7% -> 12%
where the time goes in v8:
time: 58.9 us; the launch traced here: 58.7 us
  starting transfers between devices  30.4 us (52%)
  waiting for transfers between devices  14.1 us (24%)
  Pallas kernels  13.3 us (23%)
  between operations  0.82 us (1%)
    ppermute x23, starting transfers between devices, partner(): return lax.ppermute(value, axes, pairs)  30.4 us
    ppermute x23, waiting for transfers between devices, partner(): return lax.ppermute(value, axes, pairs)  14.1 us
    pallas_call x13, Pallas kernels, call(): pl.pallas_call(kernel, out_shape=out_shape, in_specs=list(in_specs) + [in...  13.3 us
  transfers between devices with their start and end apart: 23, of which 11 were waited for; matrix products, arithmetic and copies ran while one was open for 0% of the time, Pallas kernels for 12%

profile of v8, /device:TPU:0, one launch (start us, length us, event | category | flops | bytes accessed | tf_op | source)
XLA Modules:
  0.0 58.7 jit_solution(9959128749607633410)
XLA Ops:
  0.6 0.0 copy-start
  0.6 0.0 copy-start.3
  0.7 0.0 copy-start.1
  0.7 0.0 copy-start.2
  0.7 0.5 collective-permute-start
  1.2 1.6 %load_operators.1 = (bf16[4,256,256]{2,1,0:T(8,128)(2,1)S(1)}, bf16[4,256,256]{2,1,0:T(8,128)(2,1)S(1)}, bf16[2,512,512]{2,1,0:T(8,128)(2,1)S(1)}) custom-call(bf16[4,512,512]{2,1,0:T(8,128)(2,1)} %left_ref.1, bf16[4,512,512]{2,1,0:T(8,128)(2,1)} %refs_6_.1), custom_call_target="tpu_custom_call" | custom-call | tf_op jit(solution)/shard_map/load_operators/pallas_call | solution.py:256
  2.8 0.0 collective-permute-done.refs_8_
  2.8 0.0 copy-done
  2.8 0.0 copy-done.3
  2.8 0.0 copy-done.1
  2.8 0.0 copy-done.2
  2.8 3.5 %first_sigma_terms.1 = (bf16[2,512,512]{2,1,0:T(8,128)(2,1)S(1)}, bf16[256,512]{1,0:T(8,128)(2,1)S(1)}, bf16[256,512]{1,0:T(8,128)(2,1)S(1)}, f32[2,64,512]{2,1,...) custom-call(s32[2,2]{1,0:T(2,128)S(1)} %copy-done.3, ...), custom_call_target="tpu_custom_call" | custom-call | tf_op jit(solution)/shard_map/first_sigma_terms/pallas_call | solution.py:256
  6.4 2.7 %collective-permute-start.1 = (bf16[2,64,512]{2,1,0:T(8,128)(2,1)S(1)}, bf16[2,64,512]{2,1,0:T(8,128)(2,1)S(1)}, u32[]{:S(2)}, u32[]{:S(2)}) collective-permute-start(bf16[2,64,512]{2,1,0:T(8,128)(2,1)S(1)} %get-tuple-element.27), channel_id=1, source_target_pairs={{2,0},{0,2},{3,1},{1,3},{6,4},{4,6},{7,5},{5,7},{10,8},{8,10},{11,... | collective-permute-start | bytes 393224 | tf_op jit(solution)/shard_map/ppermute | solution.py:238
  9.1 2.6 %collective-permute-start.3 = (bf16[1,64,512]{2,1,0:T(8,128)(2,1)S(1)}, bf16[1,64,512]{2,1,0:T(8,128)(2,1)S(1)}, u32[]{:S(2)}, u32[]{:S(2)}) collective-permute-start(bf16[1,64,512]{2,1,0:T(8,128)(2,1)S(1)} %get-tuple-element.30), channel_id=1, source_target_pairs={{8,0},{12,4},{0,8},{4,12},{9,1},{13,5},{1,9},{5,13},{10,2},{14,6},... | collective-permute-start | bytes 196616 | tf_op jit(solution)/shard_map/ppermute | solution.py:238
  11.7 0.0 collective-permute-start.4
  11.7 1.9 %collective-permute-start.5 = (bf16[1,64,512]{2,1,0:T(8,128)(2,1)S(1)}, bf16[1,64,512]{2,1,0:T(8,128)(2,1)S(1)}, u32[]{:S(2)}, u32[]{:S(2)}) collective-permute-start(bf16[1,64,512]{2,1,0:T(8,128)(2,1)S(1)} %get-tuple-element.32), channel_id=1, source_target_pairs={{4,0},{0,4},{12,8},{8,12},{5,1},{1,5},{13,9},{9,13},{6,2},{2,6},{1... | collective-permute-start | bytes 196616 | tf_op jit(solution)/shard_map/ppermute | solution.py:238
  13.5 0.0 collective-permute-done.1.refs_1_
  13.6 3.5 %collective-permute-start.2 = (bf16[1,64,512]{2,1,0:T(8,128)(2,1)S(1)}, bf16[1,64,512]{2,1,0:T(8,128)(2,1)S(1)}, u32[]{:S(2)}, u32[]{:S(2)}) collective-permute-start(bf16[1,64,512]{2,1,0:T(8,128)(2,1)S(1)} %get-tuple-element.29), channel_id=1, source_target_pairs={{12,0},{8,4},{4,8},{0,12},{13,1},{9,5},{5,9},{1,13},{14,2},{10,6},... | collective-permute-start | bytes 196616 | tf_op jit(solution)/shard_map/ppermute | solution.py:238
  17.0 0.7 %collective-permute-start.6 = (bf16[1,64,512]{2,1,0:T(8,128)(2,1)S(1)}, bf16[1,64,512]{2,1,0:T(8,128)(2,1)S(1)}, u32[]{:S(2)}, u32[]{:S(2)}) collective-permute-start(bf16[1,64,512]{2,1,0:T(8,128)(2,1)S(1)} %get-tuple-element.33), channel_id=1, source_target_pairs={{6,0},{4,2},{2,4},{0,6},{14,8},{12,10},{10,12},{8,14},{7,1},{5,3},... | collective-permute-start | bytes 196616 | tf_op jit(solution)/shard_map/ppermute | solution.py:238
  17.7 0.0 collective-permute-done.3.refs_3_
  17.7 2.6 %collective-permute-done.4.refs_4_ = bf16[1,64,512]{2,1,0:T(8,128)(2,1)S(1)} collective-permute-done((bf16[1,64,512]{2,1,0:T(8,128)(2,1)S(1)}, bf16[1,64,512]{2,1,0:T(8,128)(2,1)S(1)}, u32[]{:S(2)}, u32[]{:S(2)}) %collective-permute-start.4) | collective-permute-done | bytes 65568 | tf_op jit(solution)/shard_map/ppermute | solution.py:238
  20.3 0.0 collective-permute-done.5.refs_5_
  20.3 0.6 %collective-permute-done.2.refs_2_ = bf16[1,64,512]{2,1,0:T(8,128)(2,1)S(1)} collective-permute-done((bf16[1,64,512]{2,1,0:T(8,128)(2,1)S(1)}, bf16[1,64,512]{2,1,0:T(8,128)(2,1)S(1)}, u32[]{:S(2)}, u32[]{:S(2)}) %collective-permute-start.2) | collective-permute-done | bytes 65568 | tf_op jit(solution)/shard_map/ppermute | solution.py:238
  21.0 1.5 %collective-permute-done.6.refs_6_ = bf16[1,64,512]{2,1,0:T(8,128)(2,1)S(1)} collective-permute-done((bf16[1,64,512]{2,1,0:T(8,128)(2,1)S(1)}, bf16[1,64,512]{2,1,0:T(8,128)(2,1)S(1)}, u32[]{:S(2)}, u32[]{:S(2)}) %collective-permute-start.6) | collective-permute-done | bytes 65568 | tf_op jit(solution)/shard_map/ppermute | solution.py:238
  22.5 0.1 sum_first_sigma.1.refs_3_
  22.6 3.0 %collective-permute-start.7 = (bf16[1,64,512]{2,1,0:T(8,128)(2,1)S(1)}, bf16[1,64,512]{2,1,0:T(8,128)(2,1)S(1)}, u32[]{:S(2)}, u32[]{:S(2)}) collective-permute-start(bf16[1,64,512]{2,1,0:T(8,128)(2,1)S(1)} %sum_first_sigma.1.refs_3_), channel_id=1, source_target_pairs={{12,0},{8,4},{4,8},{0,12},{13,1},{9,5},{5,9},{1,13},{14,2},{10,6},... | collective-permute-start | bytes 196616 | tf_op jit(solution)/shard_map/ppermute | solution.py:238
  25.5 0.0 collective-permute-start.8
  25.5 1.5 %collective-permute-start.9 = (bf16[1,64,512]{2,1,0:T(8,128)(2,1)S(1)}, bf16[1,64,512]{2,1,0:T(8,128)(2,1)S(1)}, u32[]{:S(2)}, u32[]{:S(2)}) collective-permute-start(bf16[1,64,512]{2,1,0:T(8,128)(2,1)S(1)} %sum_first_sigma.1.refs_3_), channel_id=1, source_target_pairs={{4,0},{0,4},{12,8},{8,12},{5,1},{1,5},{13,9},{9,13},{6,2},{2,6},{1... | collective-permute-start | bytes 196616 | tf_op jit(solution)/shard_map/ppermute | solution.py:238
  27.0 1.0 %collective-permute-start.14 = (bf16[1,64,512]{2,1,0:T(8,128)(2,1)S(1)}, bf16[1,64,512]{2,1,0:T(8,128)(2,1)S(1)}, u32[]{:S(2)}, u32[]{:S(2)}) collective-permute-start(bf16[1,64,512]{2,1,0:T(8,128)(2,1)S(1)} %sum_first_sigma.1.refs_3_), channel_id=1, source_target_pairs={{6,0},{4,2},{2,4},{0,6},{14,8},{12,10},{10,12},{8,14},{7,1},{5,3},... | collective-permute-start | bytes 196616 | tf_op jit(solution)/shard_map/ppermute | solution.py:238
  28.0 1.1 %collective-permute-start.15 = (bf16[1,64,512]{2,1,0:T(8,128)(2,1)S(1)}, bf16[1,64,512]{2,1,0:T(8,128)(2,1)S(1)}, u32[]{:S(2)}, u32[]{:S(2)}) collective-permute-start(bf16[1,64,512]{2,1,0:T(8,128)(2,1)S(1)} %sum_first_sigma.1.refs_3_), channel_id=1, source_target_pairs={{2,0},{0,2},{3,1},{1,3},{6,4},{4,6},{7,5},{5,7},{10,8},{8,10},{11,... | collective-permute-start | bytes 196616 | tf_op jit(solution)/shard_map/ppermute | solution.py:238
  29.0 0.0 collective-permute-done.7.refs_0_
  29.0 1.0 %collective-permute-start.12 = (bf16[1,64,512]{2,1,0:T(8,128)(2,1)S(1)}, bf16[1,64,512]{2,1,0:T(8,128)(2,1)S(1)}, u32[]{:S(2)}, u32[]{:S(2)}) collective-permute-start(bf16[1,64,512]{2,1,0:T(8,128)(2,1)S(1)} %collective-permute-done.7.refs_0_), channel_id=1, source_target_pairs={{2,0},{0,2},{3,1},{1,3},{6,4},{4,6},{7,5},{5,7},{10,8},{8,10},{11,... | collective-permute-start | bytes 196616 | tf_op jit(solution)/shard_map/ppermute | solution.py:238
  30.0 0.9 %collective-permute-done.8.refs_1_ = bf16[1,64,512]{2,1,0:T(8,128)(2,1)S(1)} collective-permute-done((bf16[1,64,512]{2,1,0:T(8,128)(2,1)S(1)}, bf16[1,64,512]{2,1,0:T(8,128)(2,1)S(1)}, u32[]{:S(2)}, u32[]{:S(2)}) %collective-permute-start.8) | collective-permute-done | bytes 65568 | tf_op jit(solution)/shard_map/ppermute | solution.py:238
  30.9 1.1 %collective-permute-start.13 = (bf16[1,64,512]{2,1,0:T(8,128)(2,1)S(1)}, bf16[1,64,512]{2,1,0:T(8,128)(2,1)S(1)}, u32[]{:S(2)}, u32[]{:S(2)}) collective-permute-start(bf16[1,64,512]{2,1,0:T(8,128)(2,1)S(1)} %collective-permute-done.8.refs_1_), channel_id=1, source_target_pairs={{2,0},{0,2},{3,1},{1,3},{6,4},{4,6},{7,5},{5,7},{10,8},{8,10},{11,... | collective-permute-start | bytes 196616 | tf_op jit(solution)/shard_map/ppermute | solution.py:238
  32.0 0.0 collective-permute-done.9.refs_2_
  32.0 0.1 collective-permute-start.10
  32.1 1.0 %collective-permute-done.14.refs_2_ = bf16[1,64,512]{2,1,0:T(8,128)(2,1)S(1)} collective-permute-done((bf16[1,64,512]{2,1,0:T(8,128)(2,1)S(1)}, bf16[1,64,512]{2,1,0:T(8,128)(2,1)S(1)}, u32[]{:S(2)}, u32[]{:S(2)}) %collective-permute-start.14) | collective-permute-done | bytes 65568 | tf_op jit(solution)/shard_map/ppermute | solution.py:238
  33.1 0.4 collective-permute-done.15.refs_3_
  33.5 1.2 %collective-permute-done.12.refs_0_ = bf16[1,64,512]{2,1,0:T(8,128)(2,1)S(1)} collective-permute-done((bf16[1,64,512]{2,1,0:T(8,128)(2,1)S(1)}, bf16[1,64,512]{2,1,0:T(8,128)(2,1)S(1)}, u32[]{:S(2)}, u32[]{:S(2)}) %collective-permute-start.12) | collective-permute-done | bytes 65568 | tf_op jit(solution)/shard_map/ppermute | solution.py:238
  34.8 0.7 %collective-permute-done.13.refs_1_ = bf16[1,64,512]{2,1,0:T(8,128)(2,1)S(1)} collective-permute-done((bf16[1,64,512]{2,1,0:T(8,128)(2,1)S(1)}, bf16[1,64,512]{2,1,0:T(8,128)(2,1)S(1)}, u32[]{:S(2)}, u32[]{:S(2)}) %collective-permute-start.13) | collective-permute-done | bytes 65568 | tf_op jit(solution)/shard_map/ppermute | solution.py:238
  35.5 0.1 collective-permute-start.16
  35.6 0.0 collective-permute-done.10.sigma_other.other
  35.6 1.6 %left_products.1.refs_6_ = f32[4,256,512]{2,1,0:T(8,128)S(1)} custom-call(s32[4,2,8]{2,1,0:T(2,128)S(1)} %bitcast.2, f32[4,8]{1,0:T(4,128)S(1)} %copy-done.2, bf16[4,256,256]{2,1,0:T(8,128)(2,1)S(1)} %get-tuple-element.22.refs_3_.left_own, bf16[4,256,256]{2,1,0:T(8,128)(2,1)S(1)} %get-tuple-element.23.refs_4_.left_other.refs_3_, ...), custom_call_target="tpu_custom_call" | custom-call | tf_op jit(solution)/shard_map/left_products/pallas_call | solution.py:256
  37.2 0.0 collective-permute-done.16.refs_7_
  37.2 1.8 %second_sigma_far.1 = (bf16[1,64,512]{2,1,0:T(8,128)(2,1)S(1)}, bf16[1,64,512]{2,1,0:T(8,128)(2,1)S(1)}) custom-call(s32[2,2]{1,0:T(2,128)S(1)} %copy-done.3, s32[4,2,8]{2,1,0:T(2,128)S(1)} %bitcast.3, f32[4,8]{1,0:T(4,128)S(1)} %copy-done.2, bf16[4,256,256]{2,1,0:T(8,128)(2,1)S(1)} %get-tuple-element.23.refs_4_.left_other.refs_3_, ...), custom_call_target="tpu_custom_call" | custom-call | tf_op jit(solution)/shard_map/second_sigma_far/pallas_call | solution.py:256
  39.0 2.3 %collective-permute-start.17 = (bf16[1,64,512]{2,1,0:T(8,128)(2,1)S(1)}, bf16[1,64,512]{2,1,0:T(8,128)(2,1)S(1)}, u32[]{:S(2)}, u32[]{:S(2)}) collective-permute-start(bf16[1,64,512]{2,1,0:T(8,128)(2,1)S(1)} %get-tuple-element.39), channel_id=1, source_target_pairs={{12,0},{8,4},{4,8},{0,12},{13,1},{9,5},{5,9},{1,13},{14,2},{10,6},... | collective-permute-start | bytes 196616 | tf_op jit(solution)/shard_map/ppermute | solution.py:238
  41.3 0.0 collective-permute-start.18
  41.3 1.8 %second_sigma_near.1 = (bf16[1,64,512]{2,1,0:T(8,128)(2,1)S(1)}, f32[1,64,512]{2,1,0:T(8,128)S(1)}) custom-call(s32[2,2]{1,0:T(2,128)S(1)} %copy-done.3, s32[4,2,8]{2,1,0:T(2,128)S(1)} %bitcast.4, f32[4,8]{1,0:T(4,128)S(1)} %copy-done.2, bf16[4,256,256]{2,1,0:T(8,128)(2,1)S(1)} %get-tuple-element.23.refs_4_.left_other.refs_3_, ...), custom_call_target="tpu_custom_call" | custom-call | tf_op jit(solution)/shard_map/second_sigma_near/pallas_call | solution.py:256
  43.1 2.2 %collective-permute-start.19 = (bf16[1,64,512]{2,1,0:T(8,128)(2,1)S(1)}, bf16[1,64,512]{2,1,0:T(8,128)(2,1)S(1)}, u32[]{:S(2)}, u32[]{:S(2)}) collective-permute-start(bf16[1,64,512]{2,1,0:T(8,128)(2,1)S(1)} %get-tuple-element.41), channel_id=1, source_target_pairs={{4,0},{0,4},{12,8},{8,12},{5,1},{1,5},{13,9},{9,13},{6,2},{2,6},{1... | collective-permute-start | bytes 196616 | tf_op jit(solution)/shard_map/ppermute | solution.py:238
  45.4 0.5 sums_for_rayleigh.1.refs_0_.refs_4_
  45.9 0.9 %collective-permute-start.11 = (f32[3,8,128]{2,1,0:T(8,128)S(1)}, f32[3,8,128]{2,1,0:T(8,128)S(1)}, u32[]{:S(2)}, u32[]{:S(2)}) collective-permute-start(f32[3,8,128]{2,1,0:T(8,128)S(1)} %sums_for_rayleigh.1.refs_0_.refs_4_), channel_id=1, source_target_pairs={{2,0},{0,2},{3,1},{1,3},{6,4},{4,6},{7,5},{5,7},{10,8},{8,10},{11,... | collective-permute-start | bytes 36872 | tf_op jit(solution)/shard_map/ppermute | solution.py:238
  46.7 2.9 %collective-permute-done.11.refs_1_.refs_5_ = f32[3,8,128]{2,1,0:T(8,128)S(1)} collective-permute-done((f32[3,8,128]{2,1,0:T(8,128)S(1)}, f32[3,8,128]{2,1,0:T(8,128)S(1)}, u32[]{:S(2)}, u32[]{:S(2)}) %collective-permute-start.11) | collective-permute-done | bytes 12320 | tf_op jit(solution)/shard_map/ppermute | solution.py:238
  49.6 0.0 collective-permute-done.17.refs_1_
  49.6 0.0 collective-permute-done.18.refs_2_
  49.6 0.0 collective-permute-done.19.refs_3_
  49.7 2.3 %collective-permute-start.20 = (bf16[1,64,512]{2,1,0:T(8,128)(2,1)S(1)}, bf16[1,64,512]{2,1,0:T(8,128)(2,1)S(1)}, u32[]{:S(2)}, u32[]{:S(2)}) collective-permute-start(bf16[1,64,512]{2,1,0:T(8,128)(2,1)S(1)} %sum_second_sigma.1.refs_3_), channel_id=1, source_target_pairs={{12,0},{8,4},{4,8},{0,12},{13,1},{9,5},{5,9},{1,13},{14,2},{10,6},... | collective-permute-start | bytes 196616 | tf_op jit(solution)/shard_map/ppermute | solution.py:238
  52.0 0.0 collective-permute-start.21
  52.0 2.2 %collective-permute-start.22 = (bf16[1,64,512]{2,1,0:T(8,128)(2,1)S(1)}, bf16[1,64,512]{2,1,0:T(8,128)(2,1)S(1)}, u32[]{:S(2)}, u32[]{:S(2)}) collective-permute-start(bf16[1,64,512]{2,1,0:T(8,128)(2,1)S(1)} %sum_second_sigma.1.refs_3_), channel_id=1, source_target_pairs={{4,0},{0,4},{12,8},{8,12},{5,1},{1,5},{13,9},{9,13},{6,2},{2,6},{1... | collective-permute-start | bytes 196616 | tf_op jit(solution)/shard_map/ppermute | solution.py:238
  54.1 1.4 %second_wave.1 = (bf16[1,256,512]{2,1,0:T(8,128)(2,1)}, f32[2,8,128]{2,1,0:T(8,128)S(1)}) custom-call(s32[2,2]{1,0:T(2,128)S(1)} %copy-done.3, bf16[256,512]{1,0:T(8,128)(2,1)S(1)} %get-tuple-element.25.wave_own, bf16[1,256,512]{2,1,0:T(8,128)(2,1)S(1)} %place_own_sector.1.sigma_own.own, f32[3,8,128]{2,1,0:T(8,128)S(1)} %sums_for_rayleigh.1.refs_0_.refs_4_, ...), custom_call_target="tpu_custom_call" | custom-call | tf_op jit(solution)/shard_map/second_wave/pallas_call | solution.py:256
  55.6 0.9 %collective-permute-done.20.refs_0_ = bf16[1,64,512]{2,1,0:T(8,128)(2,1)S(1)} collective-permute-done((bf16[1,64,512]{2,1,0:T(8,128)(2,1)S(1)}, bf16[1,64,512]{2,1,0:T(8,128)(2,1)S(1)}, u32[]{:S(2)}, u32[]{:S(2)}) %collective-permute-start.20) | collective-permute-done | bytes 65568 | tf_op jit(solution)/shard_map/ppermute | solution.py:238
  56.5 1.4 %collective-permute-done.21.refs_1_ = bf16[1,64,512]{2,1,0:T(8,128)(2,1)S(1)} collective-permute-done((bf16[1,64,512]{2,1,0:T(8,128)(2,1)S(1)}, bf16[1,64,512]{2,1,0:T(8,128)(2,1)S(1)}, u32[]{:S(2)}, u32[]{:S(2)}) %collective-permute-start.21) | collective-permute-done | bytes 65568 | tf_op jit(solution)/shard_map/ppermute | solution.py:238
  57.9 0.0 collective-permute-done.22.refs_2_
  57.9 0.9 %join_second_sigma.1 = f32[1,256,512]{2,1,0:T(8,128)} custom-call(f32[2,8,128]{2,1,0:T(8,128)S(1)} %get-tuple-element.36.factors, bf16[1,256,512]{2,1,0:T(8,128)(2,1)S(1)} %place_own_sector.1.sigma_own.own, bf16[1,64,512]{2,1,0:T(8,128)(2,1)S(1)} %collective-permute-done.20.refs_0_, bf16[1,64,512]{2,1,0:T(8,128)(2,1)S(1)} %collective-permute-done.21.refs_1_, ...), custom_call_target="tpu_custom_call" | custom-call | tf_op jit(solution)/shard_map/join_second_sigma/pallas_call | solution.py:256
  (4 shorter events, 0.1 us)
Async XLA Ops:
  0.6 2.2 %copy-start = (bf16[1,256,512]{2,1,0:T(8,128)(2,1)S(1)}, bf16[1,256,512]{2,1,0:T(8,128)(2,1)}, u32[]{:S(2)}) copy-start(bf16[1,256,512]{2,1,0:T(8,128)(2,1)} %refs_7_.1) | copy-start | bytes 786436
  0.6 2.2 %copy-start.3 = (s32[2,2]{1,0:T(2,128)S(1)}, s32[2,2]{1,0:T(2,128)}, u32[]{:S(2)}) copy-start(s32[2,2]{1,0:T(2,128)} %refs_0_.5) | copy-start | bytes 52
  0.7 2.2 %copy-start.1 = (s32[4,8,2]{1,2,0:T(2,128)S(1)}, s32[4,8,2]{1,2,0:T(2,128)}, u32[]{:S(2)}) copy-start(s32[4,8,2]{1,2,0:T(2,128)} %param.10) | copy-start | bytes 772
  0.7 2.2 %copy-start.2 = (f32[4,8]{1,0:T(4,128)S(1)}, f32[4,8]{1,0:T(4,128)}, u32[]{:S(2)}) copy-start(f32[4,8]{1,0:T(4,128)} %refs_2_.5) | copy-start | bytes 388
  0.7 2.1 %collective-permute-start = (bf16[1,256,512]{2,1,0:T(8,128)(2,1)}, bf16[1,256,512]{2,1,0:T(8,128)(2,1)S(1)}, u32[]{:S(2)}, u32[]{:S(2)}) collective-permute-start(bf16[1,256,512]{2,1,0:T(8,128)(2,1)} %refs_7_.1), channel_id=1, source_target_pairs={{1,0},{0,1},{3,2},{2,3},{5,4},{4,5},{7,6},{6,7},{9,8},{8,9},{11,10... | collective-permute-start | bytes 786440 | tf_op jit(solution)/shard_map/ppermute | solution.py:238
  6.4 7.2 %collective-permute-start.1 = (bf16[2,64,512]{2,1,0:T(8,128)(2,1)S(1)}, bf16[2,64,512]{2,1,0:T(8,128)(2,1)S(1)}, u32[]{:S(2)}, u32[]{:S(2)}) collective-permute-start(bf16[2,64,512]{2,1,0:T(8,128)(2,1)S(1)} %get-tuple-element.27), channel_id=1, source_target_pairs={{2,0},{0,2},{3,1},{1,3},{6,4},{4,6},{7,5},{5,7},{10,8},{8,10},{11,... | collective-permute-start | bytes 393224 | tf_op jit(solution)/shard_map/ppermute | solution.py:238
  9.1 8.7 %collective-permute-start.3 = (bf16[1,64,512]{2,1,0:T(8,128)(2,1)S(1)}, bf16[1,64,512]{2,1,0:T(8,128)(2,1)S(1)}, u32[]{:S(2)}, u32[]{:S(2)}) collective-permute-start(bf16[1,64,512]{2,1,0:T(8,128)(2,1)S(1)} %get-tuple-element.30), channel_id=1, source_target_pairs={{8,0},{12,4},{0,8},{4,12},{9,1},{13,5},{1,9},{5,13},{10,2},{14,6},... | collective-permute-start | bytes 196616 | tf_op jit(solution)/shard_map/ppermute | solution.py:238
  11.7 8.7 %collective-permute-start.4 = (bf16[1,64,512]{2,1,0:T(8,128)(2,1)S(1)}, bf16[1,64,512]{2,1,0:T(8,128)(2,1)S(1)}, u32[]{:S(2)}, u32[]{:S(2)}) collective-permute-start(bf16[1,64,512]{2,1,0:T(8,128)(2,1)S(1)} %get-tuple-element.31), channel_id=1, source_target_pairs={{10,0},{8,2},{14,4},{12,6},{2,8},{0,10},{6,12},{4,14},{11,1},{9,3}... | collective-permute-start | bytes 196616 | tf_op jit(solution)/shard_map/ppermute | solution.py:238
  11.7 8.7 %collective-permute-start.5 = (bf16[1,64,512]{2,1,0:T(8,128)(2,1)S(1)}, bf16[1,64,512]{2,1,0:T(8,128)(2,1)S(1)}, u32[]{:S(2)}, u32[]{:S(2)}) collective-permute-start(bf16[1,64,512]{2,1,0:T(8,128)(2,1)S(1)} %get-tuple-element.32), channel_id=1, source_target_pairs={{4,0},{0,4},{12,8},{8,12},{5,1},{1,5},{13,9},{9,13},{6,2},{2,6},{1... | collective-permute-start | bytes 196616 | tf_op jit(solution)/shard_map/ppermute | solution.py:238
  13.6 7.4 %collective-permute-start.2 = (bf16[1,64,512]{2,1,0:T(8,128)(2,1)S(1)}, bf16[1,64,512]{2,1,0:T(8,128)(2,1)S(1)}, u32[]{:S(2)}, u32[]{:S(2)}) collective-permute-start(bf16[1,64,512]{2,1,0:T(8,128)(2,1)S(1)} %get-tuple-element.29), channel_id=1, source_target_pairs={{12,0},{8,4},{4,8},{0,12},{13,1},{9,5},{5,9},{1,13},{14,2},{10,6},... | collective-permute-start | bytes 196616 | tf_op jit(solution)/shard_map/ppermute | solution.py:238
  17.0 5.5 %collective-permute-start.6 = (bf16[1,64,512]{2,1,0:T(8,128)(2,1)S(1)}, bf16[1,64,512]{2,1,0:T(8,128)(2,1)S(1)}, u32[]{:S(2)}, u32[]{:S(2)}) collective-permute-start(bf16[1,64,512]{2,1,0:T(8,128)(2,1)S(1)} %get-tuple-element.33), channel_id=1, source_target_pairs={{6,0},{4,2},{2,4},{0,6},{14,8},{12,10},{10,12},{8,14},{7,1},{5,3},... | collective-permute-start | bytes 196616 | tf_op jit(solution)/shard_map/ppermute | solution.py:238
  22.6 6.5 %collective-permute-start.7 = (bf16[1,64,512]{2,1,0:T(8,128)(2,1)S(1)}, bf16[1,64,512]{2,1,0:T(8,128)(2,1)S(1)}, u32[]{:S(2)}, u32[]{:S(2)}) collective-permute-start(bf16[1,64,512]{2,1,0:T(8,128)(2,1)S(1)} %sum_first_sigma.1.refs_3_), channel_id=1, source_target_pairs={{12,0},{8,4},{4,8},{0,12},{13,1},{9,5},{5,9},{1,13},{14,2},{10,6},... | collective-permute-start | bytes 196616 | tf_op jit(solution)/shard_map/ppermute | solution.py:238
  25.5 5.4 %collective-permute-start.8 = (bf16[1,64,512]{2,1,0:T(8,128)(2,1)S(1)}, bf16[1,64,512]{2,1,0:T(8,128)(2,1)S(1)}, u32[]{:S(2)}, u32[]{:S(2)}) collective-permute-start(bf16[1,64,512]{2,1,0:T(8,128)(2,1)S(1)} %sum_first_sigma.1.refs_3_), channel_id=1, source_target_pairs={{8,0},{12,4},{0,8},{4,12},{9,1},{13,5},{1,9},{5,13},{10,2},{14,6},... | collective-permute-start | bytes 196616 | tf_op jit(solution)/shard_map/ppermute | solution.py:238
  25.5 6.5 %collective-permute-start.9 = (bf16[1,64,512]{2,1,0:T(8,128)(2,1)S(1)}, bf16[1,64,512]{2,1,0:T(8,128)(2,1)S(1)}, u32[]{:S(2)}, u32[]{:S(2)}) collective-permute-start(bf16[1,64,512]{2,1,0:T(8,128)(2,1)S(1)} %sum_first_sigma.1.refs_3_), channel_id=1, source_target_pairs={{4,0},{0,4},{12,8},{8,12},{5,1},{1,5},{13,9},{9,13},{6,2},{2,6},{1... | collective-permute-start | bytes 196616 | tf_op jit(solution)/shard_map/ppermute | solution.py:238
  27.0 6.1 %collective-permute-start.14 = (bf16[1,64,512]{2,1,0:T(8,128)(2,1)S(1)}, bf16[1,64,512]{2,1,0:T(8,128)(2,1)S(1)}, u32[]{:S(2)}, u32[]{:S(2)}) collective-permute-start(bf16[1,64,512]{2,1,0:T(8,128)(2,1)S(1)} %sum_first_sigma.1.refs_3_), channel_id=1, source_target_pairs={{6,0},{4,2},{2,4},{0,6},{14,8},{12,10},{10,12},{8,14},{7,1},{5,3},... | collective-permute-start | bytes 196616 | tf_op jit(solution)/shard_map/ppermute | solution.py:238
  28.0 5.5 %collective-permute-start.15 = (bf16[1,64,512]{2,1,0:T(8,128)(2,1)S(1)}, bf16[1,64,512]{2,1,0:T(8,128)(2,1)S(1)}, u32[]{:S(2)}, u32[]{:S(2)}) collective-permute-start(bf16[1,64,512]{2,1,0:T(8,128)(2,1)S(1)} %sum_first_sigma.1.refs_3_), channel_id=1, source_target_pairs={{2,0},{0,2},{3,1},{1,3},{6,4},{4,6},{7,5},{5,7},{10,8},{8,10},{11,... | collective-permute-start | bytes 196616 | tf_op jit(solution)/shard_map/ppermute | solution.py:238
  29.0 5.7 %collective-permute-start.12 = (bf16[1,64,512]{2,1,0:T(8,128)(2,1)S(1)}, bf16[1,64,512]{2,1,0:T(8,128)(2,1)S(1)}, u32[]{:S(2)}, u32[]{:S(2)}) collective-permute-start(bf16[1,64,512]{2,1,0:T(8,128)(2,1)S(1)} %collective-permute-done.7.refs_0_), channel_id=1, source_target_pairs={{2,0},{0,2},{3,1},{1,3},{6,4},{4,6},{7,5},{5,7},{10,8},{8,10},{11,... | collective-permute-start | bytes 196616 | tf_op jit(solution)/shard_map/ppermute | solution.py:238
  30.9 4.6 %collective-permute-start.13 = (bf16[1,64,512]{2,1,0:T(8,128)(2,1)S(1)}, bf16[1,64,512]{2,1,0:T(8,128)(2,1)S(1)}, u32[]{:S(2)}, u32[]{:S(2)}) collective-permute-start(bf16[1,64,512]{2,1,0:T(8,128)(2,1)S(1)} %collective-permute-done.8.refs_1_), channel_id=1, source_target_pairs={{2,0},{0,2},{3,1},{1,3},{6,4},{4,6},{7,5},{5,7},{10,8},{8,10},{11,... | collective-permute-start | bytes 196616 | tf_op jit(solution)/shard_map/ppermute | solution.py:238
  32.0 3.5 %collective-permute-start.10 = (bf16[1,256,512]{2,1,0:T(8,128)(2,1)S(1)}, bf16[1,256,512]{2,1,0:T(8,128)(2,1)S(1)}, u32[]{:S(2)}, u32[]{:S(2)}) collective-permute-start(bf16[1,256,512]{2,1,0:T(8,128)(2,1)S(1)} %place_own_sector.1.sigma_own.own), channel_id=1, source_target_pairs={{1,0},{0,1},{3,2},{2,3},{5,4},{4,5},{7,6},{6,7},{9,8},{8,9},{11,10... | collective-permute-start | bytes 786440 | tf_op jit(solution)/shard_map/ppermute | solution.py:238
  35.5 1.7 %collective-permute-start.16 = (bf16[1,256,512]{2,1,0:T(8,128)(2,1)S(1)}, bf16[1,256,512]{2,1,0:T(8,128)(2,1)S(1)}, u32[]{:S(2)}, u32[]{:S(2)}) collective-permute-start(bf16[1,256,512]{2,1,0:T(8,128)(2,1)S(1)} %place_other_sectors.1.across_own), channel_id=1, source_target_pairs={{1,0},{0,1},{3,2},{2,3},{5,4},{4,5},{7,6},{6,7},{9,8},{8,9},{11,10... | collective-permute-start | bytes 786440 | tf_op jit(solution)/shard_map/ppermute | solution.py:238
  39.0 10.6 %collective-permute-start.17 = (bf16[1,64,512]{2,1,0:T(8,128)(2,1)S(1)}, bf16[1,64,512]{2,1,0:T(8,128)(2,1)S(1)}, u32[]{:S(2)}, u32[]{:S(2)}) collective-permute-start(bf16[1,64,512]{2,1,0:T(8,128)(2,1)S(1)} %get-tuple-element.39), channel_id=1, source_target_pairs={{12,0},{8,4},{4,8},{0,12},{13,1},{9,5},{5,9},{1,13},{14,2},{10,6},... | collective-permute-start | bytes 196616 | tf_op jit(solution)/shard_map/ppermute | solution.py:238
  41.3 8.3 %collective-permute-start.18 = (bf16[1,64,512]{2,1,0:T(8,128)(2,1)S(1)}, bf16[1,64,512]{2,1,0:T(8,128)(2,1)S(1)}, u32[]{:S(2)}, u32[]{:S(2)}) collective-permute-start(bf16[1,64,512]{2,1,0:T(8,128)(2,1)S(1)} %get-tuple-element.40), channel_id=1, source_target_pairs={{8,0},{12,4},{0,8},{4,12},{9,1},{13,5},{1,9},{5,13},{10,2},{14,6},... | collective-permute-start | bytes 196616 | tf_op jit(solution)/shard_map/ppermute | solution.py:238
  43.1 6.5 %collective-permute-start.19 = (bf16[1,64,512]{2,1,0:T(8,128)(2,1)S(1)}, bf16[1,64,512]{2,1,0:T(8,128)(2,1)S(1)}, u32[]{:S(2)}, u32[]{:S(2)}) collective-permute-start(bf16[1,64,512]{2,1,0:T(8,128)(2,1)S(1)} %get-tuple-element.41), channel_id=1, source_target_pairs={{4,0},{0,4},{12,8},{8,12},{5,1},{1,5},{13,9},{9,13},{6,2},{2,6},{1... | collective-permute-start | bytes 196616 | tf_op jit(solution)/shard_map/ppermute | solution.py:238
  45.9 3.8 %collective-permute-start.11 = (f32[3,8,128]{2,1,0:T(8,128)S(1)}, f32[3,8,128]{2,1,0:T(8,128)S(1)}, u32[]{:S(2)}, u32[]{:S(2)}) collective-permute-start(f32[3,8,128]{2,1,0:T(8,128)S(1)} %sums_for_rayleigh.1.refs_0_.refs_4_), channel_id=1, source_target_pairs={{2,0},{0,2},{3,1},{1,3},{6,4},{4,6},{7,5},{5,7},{10,8},{8,10},{11,... | collective-permute-start | bytes 36872 | tf_op jit(solution)/shard_map/ppermute | solution.py:238
  49.7 6.8 %collective-permute-start.20 = (bf16[1,64,512]{2,1,0:T(8,128)(2,1)S(1)}, bf16[1,64,512]{2,1,0:T(8,128)(2,1)S(1)}, u32[]{:S(2)}, u32[]{:S(2)}) collective-permute-start(bf16[1,64,512]{2,1,0:T(8,128)(2,1)S(1)} %sum_second_sigma.1.refs_3_), channel_id=1, source_target_pairs={{12,0},{8,4},{4,8},{0,12},{13,1},{9,5},{5,9},{1,13},{14,2},{10,6},... | collective-permute-start | bytes 196616 | tf_op jit(solution)/shard_map/ppermute | solution.py:238
  52.0 5.9 %collective-permute-start.21 = (bf16[1,64,512]{2,1,0:T(8,128)(2,1)S(1)}, bf16[1,64,512]{2,1,0:T(8,128)(2,1)S(1)}, u32[]{:S(2)}, u32[]{:S(2)}) collective-permute-start(bf16[1,64,512]{2,1,0:T(8,128)(2,1)S(1)} %sum_second_sigma.1.refs_3_), channel_id=1, source_target_pairs={{8,0},{12,4},{0,8},{4,12},{9,1},{13,5},{1,9},{5,13},{10,2},{14,6},... | collective-permute-start | bytes 196616 | tf_op jit(solution)/shard_map/ppermute | solution.py:238
  52.0 5.9 %collective-permute-start.22 = (bf16[1,64,512]{2,1,0:T(8,128)(2,1)S(1)}, bf16[1,64,512]{2,1,0:T(8,128)(2,1)S(1)}, u32[]{:S(2)}, u32[]{:S(2)}) collective-permute-start(bf16[1,64,512]{2,1,0:T(8,128)(2,1)S(1)} %sum_second_sigma.1.refs_3_), channel_id=1, source_target_pairs={{4,0},{0,4},{12,8},{8,12},{5,1},{1,5},{13,9},{9,13},{6,2},{2,6},{1... | collective-permute-start | bytes 196616 | tf_op jit(solution)/shard_map/ppermute | solution.py:238

commit v9 on v7

--- a/solution.py
+++ b/solution.py
@@ -27,10 +27,14 @@
     return jnp.where(live, values.astype(jnp.float32), 0.0).astype(values.dtype)
 
 
-def left_times(left_own, left_other, term, own, other):
-    return jnp.dot(left_own[term], own, preferred_element_type=jnp.float32) + jnp.dot(
-        left_other[term], other, preferred_element_type=jnp.float32
-    )
+def left_times(left_own, left_other, own, other):
+    terms, rows, depth = left_own.shape
+    product = jnp.dot(
+        left_own[...].reshape(terms * rows, depth), own, preferred_element_type=jnp.float32
+    ) + jnp.dot(
+        left_other[...].reshape(terms * rows, depth), other, preferred_element_type=jnp.float32
+    )
+    return product.reshape(terms, rows, -1)
 
 
 def times_right(values, right, term):
@@ -42,7 +46,7 @@
     )
 
 
-def load_kernel(left_ref, left_own, left_other, sems):
+def load_kernel(left_ref, right_ref, left_own, left_other, right, sems):
     rows = left_own.shape[1]
     core = lax.axis_index("rep")
     copies = []
@@ -50,6 +54,7 @@
         mine = pl.ds(pl.multiple_of(core * rows, rows), rows)
         columns = pl.ds(pl.multiple_of(place * rows, rows), rows)
         copies.append(pltpu.make_async_copy(left_ref.at[:, mine, columns], half, sems.at[index]))
+    copies.append(pltpu.make_async_copy(right_ref, right, sems.at[2]))
     for copy in copies:
         copy.start()
     for copy in copies:
@@ -57,17 +62,11 @@
 
 
 def first_kernel(shares, *refs):
-    sizes_ref, pairs_ref, weights_ref, left_own, left_other, right_ref, wave, arrived = refs[:8]
-    right, own, other, *parts = refs[8:-2]
-    held, sems = refs[-2:]
+    sizes_ref, pairs_ref, weights_ref, left_own, left_other, right, wave, arrived = refs[:8]
+    own, other, *parts = refs[8:-1]
+    held = refs[-1]
     rows, columns = own.shape
     share = parts[0].shape[-2]
-    copies = [
-        pltpu.make_async_copy(right_ref.at[term], right.at[term], sems.at[term])
-        for term in range(right.shape[0])
-    ]
-    for copy in copies:
-        copy.start()
     sectors = held.shape[0]
     sector = lax.axis_index("sec")
     core = lax.axis_index("rep")
@@ -77,10 +76,9 @@
     live = live_cells(sizes_ref, sector, (core ^ 1) * rows, rows, columns)
     other[...] = masked(arrived[0], live)
     totals = [None] * sectors
+    products = left_times(left_own, left_other, own[...], other[...])
     for term in range(right.shape[0]):
-        product = left_times(left_own, left_other, term, own[...], other[...])
-        copies[term].wait()
-        product = times_right(product, right, term)
+        product = times_right(products[term], right, term)
         for step in range(sectors):
             weight = mixing_scalar(pairs_ref, weights_ref, term, sector ^ step, sector)
             part = weight * product
@@ -111,8 +109,7 @@
 
 
 def left_kernel(left_own, left_other, own, other, out):
-    for term in range(out.shape[0]):
-        out[term] = left_times(left_own, left_other, term, own[0], other[0])
+    out[...] = left_times(left_own, left_other, own[0], other[0])
 
 
 def second_kernel(
@@ -125,14 +122,15 @@
     core = lax.axis_index("rep")
     place = lax.axis_index("ops")
     total = None
+    across = [
+        left_times(left_own, left_other, own[step], other[step]) for step in range(own.shape[0])
+    ]
     for term in range(right.shape[0]):
         weight = mixing_scalar(pairs_ref, weights_ref, term, target, target)
         combined = weight * products[term]
-        for step in range(own.shape[0]):
-            weight = mixing_scalar(pairs_ref, weights_ref, term, target, target ^ (step + 1))
-            combined = combined + weight * left_times(
-                left_own, left_other, term, own[step], other[step]
-            )
+        for step, part in enumerate(across, 1):
+            weight = mixing_scalar(pairs_ref, weights_ref, term, target, target ^ step)
+            combined = combined + weight * part[term]
         part = times_right(combined, right, term)
         total = part if total is None else total + part
     live = live_cells(sizes_ref, target, core * rows, rows, columns)
@@ -257,44 +255,41 @@
 
     farthest_first = list(reversed(range(ops_count)))
     arrived = partner(wavefunction, {"rep": 1})
-    left_own, left_other = call(
+    left_own, left_other, right = call(
         load_kernel,
         "load_operators",
-        [shape(terms, rows, rows), shape(terms, rows, side - rows)],
-        [outside],
+        [
+            shape(terms, rows, rows),
+            shape(terms, rows, side - rows),
+            shape(*right_blocks.shape),
+        ],
+        [outside] * 2,
         left_blocks,
-        scratch=[pltpu.SemaphoreType.DMA((2,))],
-        vmem=51,
+        right_blocks,
+        scratch=[pltpu.SemaphoreType.DMA((3,))],
+        vmem=49,
     )
     pairs = jnp.swapaxes(sector_pairs, 1, 2)
-    scalars = (sector_sizes, pairs, pair_weights)
+    operators = (sector_sizes, pairs, pair_weights, left_own, left_other, right)
 
     far = ops_count - 1
     direct = [(along,) for along in farthest_first[1:-1]]
     spots = [((far, 0), across) for across in range(sectors)]
     spots += [(along, across) for along in direct for across in range(sectors)]
-    right, wave_own, wave_other, *rest = call(
+    wave_own, wave_other, *rest = call(
         lambda *refs: first_kernel(spots, *refs),
         "first_sigma_terms",
-        [shape(*right_blocks.shape), shape(rows, columns), shape(rows, columns)]
+        [shape(rows, columns)] * 2
         + [
             shape(len(along), share, columns, dtype=f32 if along == (far, 0) and across == 0 else bf16)
             for along, across in spots
         ],
-        [smem] * 3 + [inside] * 2 + [outside],
-        *scalars,
-        left_own,
-        left_other,
-        right_blocks,
+        [smem] * 3,
+        *operators,
         wavefunction,
         arrived,
-        scratch=[
-            pltpu.VMEM((sectors, rows, columns), f32),
-            pltpu.SemaphoreType.DMA((terms,)),
-        ],
-        vmem=49,
-    )
-    operators = scalars + (left_own, left_other, right)
+        scratch=[pltpu.VMEM((sectors, rows, columns), f32)],
+    )
     rest = dict(zip(spots, rest))
     met = [partner(rest[(far, 0), across], {"sec": across}) for across in range(sectors)]
     received = [partner(summed("sum_far_share", *met), {"ops": far})]

time: 56.8 us -> 56.3 us (level)
  Pallas kernels: 10.8 us -> 9.81 us
  waiting for transfers between devices: 12.9 us -> 13.5 us
    pallas_call x12, Pallas kernels: 10.8 us -> 9.81 us  [call(): pl.pallas_call(kernel, out_shape=out_shape, in_specs=list(in_specs) + [in...]
    ppermute x23, waiting for transfers between devices: 12.9 us -> 13.5 us  [partner(): return lax.ppermute(value, axes, pairs)]
  transfers between devices with their start and end apart: 23 -> 23, of which waited for: 13 -> 11; matrix products, arithmetic and copies ran while one was open for 0% -> 0% of each run, Pallas kernels for 7% -> 8%
where the time goes in v9:
time: 56.3 us; the launch traced here: 56.1 us
  starting transfers between devices  32 us (57%)
  waiting for transfers between devices  13.5 us (24%)
  Pallas kernels  9.81 us (17%)
  between operations  0.81 us (1%)
    ppermute x23, starting transfers between devices, partner(): return lax.ppermute(value, axes, pairs)  32 us
    ppermute x23, waiting for transfers between devices, partner(): return lax.ppermute(value, axes, pairs)  13.5 us
    pallas_call x12, Pallas kernels, call(): pl.pallas_call(kernel, out_shape=out_shape, in_specs=list(in_specs) + [in...  9.81 us
  transfers between devices with their start and end apart: 23, of which 11 were waited for; matrix products, arithmetic and copies ran while one was open for 0% of the time, Pallas kernels for 8%

profile of v9, /device:TPU:0, one launch (start us, length us, event | category | flops | bytes accessed | tf_op | source)
XLA Modules:
  0.0 56.1 jit_solution(2400321750853582122)
XLA Ops:
  0.6 0.0 copy-start
  0.6 0.0 copy-start.2
  0.7 0.0 copy-start.3
  0.7 0.0 copy-start.1
  0.7 0.5 collective-permute-start
  1.2 2.0 %load_operators.1 = (bf16[4,256,256]{2,1,0:T(8,128)(2,1)S(1)}, bf16[4,256,256]{2,1,0:T(8,128)(2,1)S(1)}, bf16[4,512,512]{2,1,0:T(8,128)(2,1)S(1)}) custom-call(bf16[4,512,512]{2,1,0:T(8,128)(2,1)} %left_ref.1, bf16[4,512,512]{2,1,0:T(8,128)(2,1)} %right_ref.1), custom_call_target="tpu_custom_call" | custom-call | tf_op jit(solution)/shard_map/load_operators/pallas_call | solution.py:234
  3.2 0.0 collective-permute-done.refs_7_
  3.2 0.0 copy-done
  3.2 0.0 copy-done.2
  3.2 0.0 copy-done.3
  3.2 0.0 copy-done.1
  3.2 2.2 %first_sigma_terms.1 = (bf16[256,512]{1,0:T(8,128)(2,1)S(1)}, bf16[256,512]{1,0:T(8,128)(2,1)S(1)}, f32[2,64,512]{2,1,0:T(8,128)S(1)}, bf16[2,64,512]{2,1,0:T(8,...) custom-call(s32[2,2]{1,0:T(2,128)S(1)} %copy-done.2, ...), custom_call_target="tpu_custom_call" | custom-call | tf_op jit(solution)/shard_map/first_sigma_terms/pallas_call | solution.py:234
  5.4 2.6 %collective-permute-start.1 = (bf16[2,64,512]{2,1,0:T(8,128)(2,1)S(1)}, bf16[2,64,512]{2,1,0:T(8,128)(2,1)S(1)}, u32[]{:S(2)}, u32[]{:S(2)}) collective-permute-start(bf16[2,64,512]{2,1,0:T(8,128)(2,1)S(1)} %get-tuple-element.24), channel_id=1, source_target_pairs={{2,0},{0,2},{3,1},{1,3},{6,4},{4,6},{7,5},{5,7},{10,8},{8,10},{11,... | collective-permute-start | bytes 393224 | tf_op jit(solution)/shard_map/ppermute | solution.py:216
  8.0 2.6 %collective-permute-start.3 = (bf16[1,64,512]{2,1,0:T(8,128)(2,1)S(1)}, bf16[1,64,512]{2,1,0:T(8,128)(2,1)S(1)}, u32[]{:S(2)}, u32[]{:S(2)}) collective-permute-start(bf16[1,64,512]{2,1,0:T(8,128)(2,1)S(1)} %get-tuple-element.25), channel_id=1, source_target_pairs={{8,0},{12,4},{0,8},{4,12},{9,1},{13,5},{1,9},{5,13},{10,2},{14,6},... | collective-permute-start | bytes 196616 | tf_op jit(solution)/shard_map/ppermute | solution.py:216
  10.6 0.0 collective-permute-start.4
  10.6 1.9 %collective-permute-start.5 = (bf16[1,64,512]{2,1,0:T(8,128)(2,1)S(1)}, bf16[1,64,512]{2,1,0:T(8,128)(2,1)S(1)}, u32[]{:S(2)}, u32[]{:S(2)}) collective-permute-start(bf16[1,64,512]{2,1,0:T(8,128)(2,1)S(1)} %get-tuple-element.27), channel_id=1, source_target_pairs={{4,0},{0,4},{12,8},{8,12},{5,1},{1,5},{13,9},{9,13},{6,2},{2,6},{1... | collective-permute-start | bytes 196616 | tf_op jit(solution)/shard_map/ppermute | solution.py:216
  12.5 1.4 %collective-permute-start.6 = (bf16[1,64,512]{2,1,0:T(8,128)(2,1)S(1)}, bf16[1,64,512]{2,1,0:T(8,128)(2,1)S(1)}, u32[]{:S(2)}, u32[]{:S(2)}) collective-permute-start(bf16[1,64,512]{2,1,0:T(8,128)(2,1)S(1)} %get-tuple-element.28), channel_id=1, source_target_pairs={{6,0},{4,2},{2,4},{0,6},{14,8},{12,10},{10,12},{8,14},{7,1},{5,3},... | collective-permute-start | bytes 196616 | tf_op jit(solution)/shard_map/ppermute | solution.py:216
  13.8 0.0 collective-permute-done.1.refs_1_
  13.9 3.7 %collective-permute-start.2 = (bf16[1,64,512]{2,1,0:T(8,128)(2,1)S(1)}, bf16[1,64,512]{2,1,0:T(8,128)(2,1)S(1)}, u32[]{:S(2)}, u32[]{:S(2)}) collective-permute-start(bf16[1,64,512]{2,1,0:T(8,128)(2,1)S(1)} %sum_far_share.1), channel_id=1, source_target_pairs={{12,0},{8,4},{4,8},{0,12},{13,1},{9,5},{5,9},{1,13},{14,2},{10,6},... | collective-permute-start | bytes 196616 | tf_op jit(solution)/shard_map/ppermute | solution.py:216
  17.5 0.0 collective-permute-done.3.refs_3_
  17.5 1.1 %collective-permute-done.4.refs_4_ = bf16[1,64,512]{2,1,0:T(8,128)(2,1)S(1)} collective-permute-done((bf16[1,64,512]{2,1,0:T(8,128)(2,1)S(1)}, bf16[1,64,512]{2,1,0:T(8,128)(2,1)S(1)}, u32[]{:S(2)}, u32[]{:S(2)}) %collective-permute-start.4) | collective-permute-done | bytes 65568 | tf_op jit(solution)/shard_map/ppermute | solution.py:216
  18.6 0.0 collective-permute-done.5.refs_5_
  18.6 0.0 collective-permute-done.6.refs_6_
  18.6 2.0 %collective-permute-done.2.refs_2_ = bf16[1,64,512]{2,1,0:T(8,128)(2,1)S(1)} collective-permute-done((bf16[1,64,512]{2,1,0:T(8,128)(2,1)S(1)}, bf16[1,64,512]{2,1,0:T(8,128)(2,1)S(1)}, u32[]{:S(2)}, u32[]{:S(2)}) %collective-permute-start.2) | collective-permute-done | bytes 65568 | tf_op jit(solution)/shard_map/ppermute | solution.py:216
  20.6 0.1 sum_first_sigma.1.refs_3_
  20.7 1.5 %collective-permute-start.8 = (bf16[1,64,512]{2,1,0:T(8,128)(2,1)S(1)}, bf16[1,64,512]{2,1,0:T(8,128)(2,1)S(1)}, u32[]{:S(2)}, u32[]{:S(2)}) collective-permute-start(bf16[1,64,512]{2,1,0:T(8,128)(2,1)S(1)} %sum_first_sigma.1.refs_3_), channel_id=1, source_target_pairs={{8,0},{12,4},{0,8},{4,12},{9,1},{13,5},{1,9},{5,13},{10,2},{14,6},... | collective-permute-start | bytes 196616 | tf_op jit(solution)/shard_map/ppermute | solution.py:216
  22.2 2.5 %collective-permute-start.7 = (bf16[1,64,512]{2,1,0:T(8,128)(2,1)S(1)}, bf16[1,64,512]{2,1,0:T(8,128)(2,1)S(1)}, u32[]{:S(2)}, u32[]{:S(2)}) collective-permute-start(bf16[1,64,512]{2,1,0:T(8,128)(2,1)S(1)} %sum_first_sigma.1.refs_3_), channel_id=1, source_target_pairs={{12,0},{8,4},{4,8},{0,12},{13,1},{9,5},{5,9},{1,13},{14,2},{10,6},... | collective-permute-start | bytes 196616 | tf_op jit(solution)/shard_map/ppermute | solution.py:216
  24.7 0.5 collective-permute-start.9
  25.2 0.8 %collective-permute-start.15 = (bf16[1,64,512]{2,1,0:T(8,128)(2,1)S(1)}, bf16[1,64,512]{2,1,0:T(8,128)(2,1)S(1)}, u32[]{:S(2)}, u32[]{:S(2)}) collective-permute-start(bf16[1,64,512]{2,1,0:T(8,128)(2,1)S(1)} %sum_first_sigma.1.refs_3_), channel_id=1, source_target_pairs={{2,0},{0,2},{3,1},{1,3},{6,4},{4,6},{7,5},{5,7},{10,8},{8,10},{11,... | collective-permute-start | bytes 196616 | tf_op jit(solution)/shard_map/ppermute | solution.py:216
  26.0 2.2 %collective-permute-start.14 = (bf16[1,64,512]{2,1,0:T(8,128)(2,1)S(1)}, bf16[1,64,512]{2,1,0:T(8,128)(2,1)S(1)}, u32[]{:S(2)}, u32[]{:S(2)}) collective-permute-start(bf16[1,64,512]{2,1,0:T(8,128)(2,1)S(1)} %sum_first_sigma.1.refs_3_), channel_id=1, source_target_pairs={{6,0},{4,2},{2,4},{0,6},{14,8},{12,10},{10,12},{8,14},{7,1},{5,3},... | collective-permute-start | bytes 196616 | tf_op jit(solution)/shard_map/ppermute | solution.py:216
  28.2 0.3 collective-permute-done.8.refs_1_
  28.5 1.3 %collective-permute-start.13 = (bf16[1,64,512]{2,1,0:T(8,128)(2,1)S(1)}, bf16[1,64,512]{2,1,0:T(8,128)(2,1)S(1)}, u32[]{:S(2)}, u32[]{:S(2)}) collective-permute-start(bf16[1,64,512]{2,1,0:T(8,128)(2,1)S(1)} %collective-permute-done.8.refs_1_), channel_id=1, source_target_pairs={{2,0},{0,2},{3,1},{1,3},{6,4},{4,6},{7,5},{5,7},{10,8},{8,10},{11,... | collective-permute-start | bytes 196616 | tf_op jit(solution)/shard_map/ppermute | solution.py:216
  29.8 0.0 collective-permute-done.7.refs_0_
  29.9 0.7 %collective-permute-start.12 = (bf16[1,64,512]{2,1,0:T(8,128)(2,1)S(1)}, bf16[1,64,512]{2,1,0:T(8,128)(2,1)S(1)}, u32[]{:S(2)}, u32[]{:S(2)}) collective-permute-start(bf16[1,64,512]{2,1,0:T(8,128)(2,1)S(1)} %collective-permute-done.7.refs_0_), channel_id=1, source_target_pairs={{2,0},{0,2},{3,1},{1,3},{6,4},{4,6},{7,5},{5,7},{10,8},{8,10},{11,... | collective-permute-start | bytes 196616 | tf_op jit(solution)/shard_map/ppermute | solution.py:216
  30.6 0.0 collective-permute-done.9.refs_2_
  30.6 0.1 collective-permute-start.10
  30.7 0.0 collective-permute-done.15.refs_3_
  30.7 0.6 %collective-permute-done.14.refs_2_ = bf16[1,64,512]{2,1,0:T(8,128)(2,1)S(1)} collective-permute-done((bf16[1,64,512]{2,1,0:T(8,128)(2,1)S(1)}, bf16[1,64,512]{2,1,0:T(8,128)(2,1)S(1)}, u32[]{:S(2)}, u32[]{:S(2)}) %collective-permute-start.14) | collective-permute-done | bytes 65568 | tf_op jit(solution)/shard_map/ppermute | solution.py:216
  31.3 1.5 %collective-permute-done.13.refs_1_ = bf16[1,64,512]{2,1,0:T(8,128)(2,1)S(1)} collective-permute-done((bf16[1,64,512]{2,1,0:T(8,128)(2,1)S(1)}, bf16[1,64,512]{2,1,0:T(8,128)(2,1)S(1)}, u32[]{:S(2)}, u32[]{:S(2)}) %collective-permute-start.13) | collective-permute-done | bytes 65568 | tf_op jit(solution)/shard_map/ppermute | solution.py:216
  32.8 1.3 %collective-permute-done.12.refs_0_ = bf16[1,64,512]{2,1,0:T(8,128)(2,1)S(1)} collective-permute-done((bf16[1,64,512]{2,1,0:T(8,128)(2,1)S(1)}, bf16[1,64,512]{2,1,0:T(8,128)(2,1)S(1)}, u32[]{:S(2)}, u32[]{:S(2)}) %collective-permute-start.12) | collective-permute-done | bytes 65568 | tf_op jit(solution)/shard_map/ppermute | solution.py:216
  34.2 0.1 collective-permute-start.16
  34.2 0.0 collective-permute-done.10.sigma_other.other
  34.2 0.7 %left_products.1.products = f32[4,256,512]{2,1,0:T(8,128)S(1)} custom-call(bf16[4,256,256]{2,1,0:T(8,128)(2,1)S(1)} %get-tuple-element.19.refs_3_.left_own, bf16[4,256,256]{2,1,0:T(8,128)(2,1)S(1)} %get-tuple-element.20.refs_4_.left_other, bf16[1,256,512]{2,1,0:T(8,128)(2,1)S(1)} %place_own_sector.1.sigma_own.own, ...), custom_call_target="tpu_custom_call" | custom-call | tf_op jit(solution)/shard_map/left_products/pallas_call | solution.py:234
  34.9 0.8 %collective-permute-done.16.other = bf16[1,256,512]{2,1,0:T(8,128)(2,1)S(1)} collective-permute-done((bf16[1,256,512]{2,1,0:T(8,128)(2,1)S(1)}, bf16[1,256,512]{2,1,0:T(8,128)(2,1)S(1)}, u32[]{:S(2)}, u32[]{:S(2)}) %collective-permute-start.16) | collective-permute-done | bytes 262176 | tf_op jit(solution)/shard_map/ppermute | solution.py:216
  35.8 2.0 %second_sigma_terms.1 = (f32[1,64,512]{2,1,0:T(8,128)S(1)}, bf16[1,64,512]{2,1,0:T(8,128)(2,1)S(1)}, bf16[1,64,512]{2,1,0:T(8,128)(2,1)S(1)}, bf16[1,64,512]{2,1,0:T(8,128)(2,1)S(1)}) custom-call(s32[2,2]{1,0:T(2,128)S(1)} %copy-done.2, s32[4,2,8]{2,1,0:T(2,128)S(1)} %bitcast.2, f32[4,8]{1,0:T(4,128)S(1)} %copy-done.3, ...), custom_call_target="tpu_custom_call" | custom-call | tf_op jit(solution)/shard_map/second_sigma_terms/pallas_call | solution.py:234
  37.7 2.5 %collective-permute-start.17 = (bf16[1,64,512]{2,1,0:T(8,128)(2,1)S(1)}, bf16[1,64,512]{2,1,0:T(8,128)(2,1)S(1)}, u32[]{:S(2)}, u32[]{:S(2)}) collective-permute-start(bf16[1,64,512]{2,1,0:T(8,128)(2,1)S(1)} %get-tuple-element.33), channel_id=1, source_target_pairs={{12,0},{8,4},{4,8},{0,12},{13,1},{9,5},{5,9},{1,13},{14,2},{10,6},... | collective-permute-start | bytes 196616 | tf_op jit(solution)/shard_map/ppermute | solution.py:216
  40.2 0.0 collective-permute-start.18
  40.2 2.0 %collective-permute-start.19 = (bf16[1,64,512]{2,1,0:T(8,128)(2,1)S(1)}, bf16[1,64,512]{2,1,0:T(8,128)(2,1)S(1)}, u32[]{:S(2)}, u32[]{:S(2)}) collective-permute-start(bf16[1,64,512]{2,1,0:T(8,128)(2,1)S(1)} %get-tuple-element.35), channel_id=1, source_target_pairs={{4,0},{0,4},{12,8},{8,12},{5,1},{1,5},{13,9},{9,13},{6,2},{2,6},{1... | collective-permute-start | bytes 196616 | tf_op jit(solution)/shard_map/ppermute | solution.py:216
  42.2 0.5 sums_for_rayleigh.1.refs_0_.refs_4_
  42.7 0.8 %collective-permute-start.11 = (f32[3,8,128]{2,1,0:T(8,128)S(1)}, f32[3,8,128]{2,1,0:T(8,128)S(1)}, u32[]{:S(2)}, u32[]{:S(2)}) collective-permute-start(f32[3,8,128]{2,1,0:T(8,128)S(1)} %sums_for_rayleigh.1.refs_0_.refs_4_), channel_id=1, source_target_pairs={{2,0},{0,2},{3,1},{1,3},{6,4},{4,6},{7,5},{5,7},{10,8},{8,10},{11,... | collective-permute-start | bytes 36872 | tf_op jit(solution)/shard_map/ppermute | solution.py:216
  43.5 3.0 %collective-permute-done.11.refs_1_.refs_5_ = f32[3,8,128]{2,1,0:T(8,128)S(1)} collective-permute-done((f32[3,8,128]{2,1,0:T(8,128)S(1)}, f32[3,8,128]{2,1,0:T(8,128)S(1)}, u32[]{:S(2)}, u32[]{:S(2)}) %collective-permute-start.11) | collective-permute-done | bytes 12320 | tf_op jit(solution)/shard_map/ppermute | solution.py:216
  46.5 0.0 collective-permute-done.17.refs_1_
  46.5 0.1 collective-permute-done.18.refs_2_
  46.5 0.0 collective-permute-done.19.refs_3_
  46.6 2.5 %collective-permute-start.22 = (bf16[1,64,512]{2,1,0:T(8,128)(2,1)S(1)}, bf16[1,64,512]{2,1,0:T(8,128)(2,1)S(1)}, u32[]{:S(2)}, u32[]{:S(2)}) collective-permute-start(bf16[1,64,512]{2,1,0:T(8,128)(2,1)S(1)} %sum_second_sigma.1.refs_0_), channel_id=1, source_target_pairs={{12,0},{8,4},{4,8},{0,12},{13,1},{9,5},{5,9},{1,13},{14,2},{10,6},... | collective-permute-start | bytes 196616 | tf_op jit(solution)/shard_map/ppermute | solution.py:216
  49.0 0.0 collective-permute-start.21
  49.0 2.0 %collective-permute-start.20 = (bf16[1,64,512]{2,1,0:T(8,128)(2,1)S(1)}, bf16[1,64,512]{2,1,0:T(8,128)(2,1)S(1)}, u32[]{:S(2)}, u32[]{:S(2)}) collective-permute-start(bf16[1,64,512]{2,1,0:T(8,128)(2,1)S(1)} %sum_second_sigma.1.refs_0_), channel_id=1, source_target_pairs={{4,0},{0,4},{12,8},{8,12},{5,1},{1,5},{13,9},{9,13},{6,2},{2,6},{1... | collective-permute-start | bytes 196616 | tf_op jit(solution)/shard_map/ppermute | solution.py:216
  51.0 1.4 %second_wave.1 = (bf16[1,256,512]{2,1,0:T(8,128)(2,1)}, f32[2,8,128]{2,1,0:T(8,128)S(1)}) custom-call(s32[2,2]{1,0:T(2,128)S(1)} %copy-done.2, bf16[256,512]{1,0:T(8,128)(2,1)S(1)} %get-tuple-element.22.wave_own, bf16[1,256,512]{2,1,0:T(8,128)(2,1)S(1)} %place_own_sector.1.sigma_own.own, f32[3,8,128]{2,1,0:T(8,128)S(1)} %sums_for_rayleigh.1.refs_0_.refs_4_, ...), custom_call_target="tpu_custom_call" | custom-call | tf_op jit(solution)/shard_map/second_wave/pallas_call | solution.py:234
  52.5 0.8 %collective-permute-done.22.refs_3_ = bf16[1,64,512]{2,1,0:T(8,128)(2,1)S(1)} collective-permute-done((bf16[1,64,512]{2,1,0:T(8,128)(2,1)S(1)}, bf16[1,64,512]{2,1,0:T(8,128)(2,1)S(1)}, u32[]{:S(2)}, u32[]{:S(2)}) %collective-permute-start.22) | collective-permute-done | bytes 65568 | tf_op jit(solution)/shard_map/ppermute | solution.py:216
  53.3 2.0 %collective-permute-done.21.refs_2_ = bf16[1,64,512]{2,1,0:T(8,128)(2,1)S(1)} collective-permute-done((bf16[1,64,512]{2,1,0:T(8,128)(2,1)S(1)}, bf16[1,64,512]{2,1,0:T(8,128)(2,1)S(1)}, u32[]{:S(2)}, u32[]{:S(2)}) %collective-permute-start.21) | collective-permute-done | bytes 65568 | tf_op jit(solution)/shard_map/ppermute | solution.py:216
  55.3 0.0 collective-permute-done.20.refs_1_
  55.3 0.9 %join_second_sigma.1 = f32[1,256,512]{2,1,0:T(8,128)} custom-call(f32[2,8,128]{2,1,0:T(8,128)S(1)} %get-tuple-element.31.factors, bf16[1,256,512]{2,1,0:T(8,128)(2,1)S(1)} %place_own_sector.1.sigma_own.own, bf16[1,64,512]{2,1,0:T(8,128)(2,1)S(1)} %sum_second_sigma.1.refs_0_, bf16[1,64,512]{2,1,0:T(8,128)(2,1)S(1)} %collective-permute-done.20.refs_1_, ...), custom_call_target="tpu_custom_call" | custom-call | tf_op jit(solution)/shard_map/join_second_sigma/pallas_call | solution.py:234
  (4 shorter events, 0.1 us)
Async XLA Ops:
  0.6 2.5 %copy-start = (bf16[1,256,512]{2,1,0:T(8,128)(2,1)S(1)}, bf16[1,256,512]{2,1,0:T(8,128)(2,1)}, u32[]{:S(2)}) copy-start(bf16[1,256,512]{2,1,0:T(8,128)(2,1)} %refs_6_.1) | copy-start | bytes 786436
  0.6 2.5 %copy-start.2 = (s32[2,2]{1,0:T(2,128)S(1)}, s32[2,2]{1,0:T(2,128)}, u32[]{:S(2)}) copy-start(s32[2,2]{1,0:T(2,128)} %sizes_ref.3) | copy-start | bytes 52
  0.7 2.5 %copy-start.3 = (f32[4,8]{1,0:T(4,128)S(1)}, f32[4,8]{1,0:T(4,128)}, u32[]{:S(2)}) copy-start(f32[4,8]{1,0:T(4,128)} %weights_ref.1) | copy-start | bytes 388
  0.7 2.5 %copy-start.1 = (s32[4,8,2]{1,2,0:T(2,128)S(1)}, s32[4,8,2]{1,2,0:T(2,128)}, u32[]{:S(2)}) copy-start(s32[4,8,2]{1,2,0:T(2,128)} %param.10) | copy-start | bytes 772
  0.7 2.5 %collective-permute-start = (bf16[1,256,512]{2,1,0:T(8,128)(2,1)}, bf16[1,256,512]{2,1,0:T(8,128)(2,1)S(1)}, u32[]{:S(2)}, u32[]{:S(2)}) collective-permute-start(bf16[1,256,512]{2,1,0:T(8,128)(2,1)} %refs_6_.1), channel_id=1, source_target_pairs={{1,0},{0,1},{3,2},{2,3},{5,4},{4,5},{7,6},{6,7},{9,8},{8,9},{11,10... | collective-permute-start | bytes 786440 | tf_op jit(solution)/shard_map/ppermute | solution.py:216
  5.4 8.4 %collective-permute-start.1 = (bf16[2,64,512]{2,1,0:T(8,128)(2,1)S(1)}, bf16[2,64,512]{2,1,0:T(8,128)(2,1)S(1)}, u32[]{:S(2)}, u32[]{:S(2)}) collective-permute-start(bf16[2,64,512]{2,1,0:T(8,128)(2,1)S(1)} %get-tuple-element.24), channel_id=1, source_target_pairs={{2,0},{0,2},{3,1},{1,3},{6,4},{4,6},{7,5},{5,7},{10,8},{8,10},{11,... | collective-permute-start | bytes 393224 | tf_op jit(solution)/shard_map/ppermute | solution.py:216
  8.0 9.6 %collective-permute-start.3 = (bf16[1,64,512]{2,1,0:T(8,128)(2,1)S(1)}, bf16[1,64,512]{2,1,0:T(8,128)(2,1)S(1)}, u32[]{:S(2)}, u32[]{:S(2)}) collective-permute-start(bf16[1,64,512]{2,1,0:T(8,128)(2,1)S(1)} %get-tuple-element.25), channel_id=1, source_target_pairs={{8,0},{12,4},{0,8},{4,12},{9,1},{13,5},{1,9},{5,13},{10,2},{14,6},... | collective-permute-start | bytes 196616 | tf_op jit(solution)/shard_map/ppermute | solution.py:216
  10.6 8.1 %collective-permute-start.4 = (bf16[1,64,512]{2,1,0:T(8,128)(2,1)S(1)}, bf16[1,64,512]{2,1,0:T(8,128)(2,1)S(1)}, u32[]{:S(2)}, u32[]{:S(2)}) collective-permute-start(bf16[1,64,512]{2,1,0:T(8,128)(2,1)S(1)} %get-tuple-element.26), channel_id=1, source_target_pairs={{10,0},{8,2},{14,4},{12,6},{2,8},{0,10},{6,12},{4,14},{11,1},{9,3}... | collective-permute-start | bytes 196616 | tf_op jit(solution)/shard_map/ppermute | solution.py:216
  10.6 8.1 %collective-permute-start.5 = (bf16[1,64,512]{2,1,0:T(8,128)(2,1)S(1)}, bf16[1,64,512]{2,1,0:T(8,128)(2,1)S(1)}, u32[]{:S(2)}, u32[]{:S(2)}) collective-permute-start(bf16[1,64,512]{2,1,0:T(8,128)(2,1)S(1)} %get-tuple-element.27), channel_id=1, source_target_pairs={{4,0},{0,4},{12,8},{8,12},{5,1},{1,5},{13,9},{9,13},{6,2},{2,6},{1... | collective-permute-start | bytes 196616 | tf_op jit(solution)/shard_map/ppermute | solution.py:216
  12.5 6.2 %collective-permute-start.6 = (bf16[1,64,512]{2,1,0:T(8,128)(2,1)S(1)}, bf16[1,64,512]{2,1,0:T(8,128)(2,1)S(1)}, u32[]{:S(2)}, u32[]{:S(2)}) collective-permute-start(bf16[1,64,512]{2,1,0:T(8,128)(2,1)S(1)} %get-tuple-element.28), channel_id=1, source_target_pairs={{6,0},{4,2},{2,4},{0,6},{14,8},{12,10},{10,12},{8,14},{7,1},{5,3},... | collective-permute-start | bytes 196616 | tf_op jit(solution)/shard_map/ppermute | solution.py:216
  13.9 6.7 %collective-permute-start.2 = (bf16[1,64,512]{2,1,0:T(8,128)(2,1)S(1)}, bf16[1,64,512]{2,1,0:T(8,128)(2,1)S(1)}, u32[]{:S(2)}, u32[]{:S(2)}) collective-permute-start(bf16[1,64,512]{2,1,0:T(8,128)(2,1)S(1)} %sum_far_share.1), channel_id=1, source_target_pairs={{12,0},{8,4},{4,8},{0,12},{13,1},{9,5},{5,9},{1,13},{14,2},{10,6},... | collective-permute-start | bytes 196616 | tf_op jit(solution)/shard_map/ppermute | solution.py:216
  20.7 7.9 %collective-permute-start.8 = (bf16[1,64,512]{2,1,0:T(8,128)(2,1)S(1)}, bf16[1,64,512]{2,1,0:T(8,128)(2,1)S(1)}, u32[]{:S(2)}, u32[]{:S(2)}) collective-permute-start(bf16[1,64,512]{2,1,0:T(8,128)(2,1)S(1)} %sum_first_sigma.1.refs_3_), channel_id=1, source_target_pairs={{8,0},{12,4},{0,8},{4,12},{9,1},{13,5},{1,9},{5,13},{10,2},{14,6},... | collective-permute-start | bytes 196616 | tf_op jit(solution)/shard_map/ppermute | solution.py:216
  22.2 7.7 %collective-permute-start.7 = (bf16[1,64,512]{2,1,0:T(8,128)(2,1)S(1)}, bf16[1,64,512]{2,1,0:T(8,128)(2,1)S(1)}, u32[]{:S(2)}, u32[]{:S(2)}) collective-permute-start(bf16[1,64,512]{2,1,0:T(8,128)(2,1)S(1)} %sum_first_sigma.1.refs_3_), channel_id=1, source_target_pairs={{12,0},{8,4},{4,8},{0,12},{13,1},{9,5},{5,9},{1,13},{14,2},{10,6},... | collective-permute-start | bytes 196616 | tf_op jit(solution)/shard_map/ppermute | solution.py:216
  24.7 5.8 %collective-permute-start.9 = (bf16[1,64,512]{2,1,0:T(8,128)(2,1)S(1)}, bf16[1,64,512]{2,1,0:T(8,128)(2,1)S(1)}, u32[]{:S(2)}, u32[]{:S(2)}) collective-permute-start(bf16[1,64,512]{2,1,0:T(8,128)(2,1)S(1)} %sum_first_sigma.1.refs_3_), channel_id=1, source_target_pairs={{4,0},{0,4},{12,8},{8,12},{5,1},{1,5},{13,9},{9,13},{6,2},{2,6},{1... | collective-permute-start | bytes 196616 | tf_op jit(solution)/shard_map/ppermute | solution.py:216
  25.2 5.5 %collective-permute-start.15 = (bf16[1,64,512]{2,1,0:T(8,128)(2,1)S(1)}, bf16[1,64,512]{2,1,0:T(8,128)(2,1)S(1)}, u32[]{:S(2)}, u32[]{:S(2)}) collective-permute-start(bf16[1,64,512]{2,1,0:T(8,128)(2,1)S(1)} %sum_first_sigma.1.refs_3_), channel_id=1, source_target_pairs={{2,0},{0,2},{3,1},{1,3},{6,4},{4,6},{7,5},{5,7},{10,8},{8,10},{11,... | collective-permute-start | bytes 196616 | tf_op jit(solution)/shard_map/ppermute | solution.py:216
  26.0 5.3 %collective-permute-start.14 = (bf16[1,64,512]{2,1,0:T(8,128)(2,1)S(1)}, bf16[1,64,512]{2,1,0:T(8,128)(2,1)S(1)}, u32[]{:S(2)}, u32[]{:S(2)}) collective-permute-start(bf16[1,64,512]{2,1,0:T(8,128)(2,1)S(1)} %sum_first_sigma.1.refs_3_), channel_id=1, source_target_pairs={{6,0},{4,2},{2,4},{0,6},{14,8},{12,10},{10,12},{8,14},{7,1},{5,3},... | collective-permute-start | bytes 196616 | tf_op jit(solution)/shard_map/ppermute | solution.py:216
  28.5 4.3 %collective-permute-start.13 = (bf16[1,64,512]{2,1,0:T(8,128)(2,1)S(1)}, bf16[1,64,512]{2,1,0:T(8,128)(2,1)S(1)}, u32[]{:S(2)}, u32[]{:S(2)}) collective-permute-start(bf16[1,64,512]{2,1,0:T(8,128)(2,1)S(1)} %collective-permute-done.8.refs_1_), channel_id=1, source_target_pairs={{2,0},{0,2},{3,1},{1,3},{6,4},{4,6},{7,5},{5,7},{10,8},{8,10},{11,... | collective-permute-start | bytes 196616 | tf_op jit(solution)/shard_map/ppermute | solution.py:216
  29.9 4.3 %collective-permute-start.12 = (bf16[1,64,512]{2,1,0:T(8,128)(2,1)S(1)}, bf16[1,64,512]{2,1,0:T(8,128)(2,1)S(1)}, u32[]{:S(2)}, u32[]{:S(2)}) collective-permute-start(bf16[1,64,512]{2,1,0:T(8,128)(2,1)S(1)} %collective-permute-done.7.refs_0_), channel_id=1, source_target_pairs={{2,0},{0,2},{3,1},{1,3},{6,4},{4,6},{7,5},{5,7},{10,8},{8,10},{11,... | collective-permute-start | bytes 196616 | tf_op jit(solution)/shard_map/ppermute | solution.py:216
  30.6 3.6 %collective-permute-start.10 = (bf16[1,256,512]{2,1,0:T(8,128)(2,1)S(1)}, bf16[1,256,512]{2,1,0:T(8,128)(2,1)S(1)}, u32[]{:S(2)}, u32[]{:S(2)}) collective-permute-start(bf16[1,256,512]{2,1,0:T(8,128)(2,1)S(1)} %place_own_sector.1.sigma_own.own), channel_id=1, source_target_pairs={{1,0},{0,1},{3,2},{2,3},{5,4},{4,5},{7,6},{6,7},{9,8},{8,9},{11,10... | collective-permute-start | bytes 786440 | tf_op jit(solution)/shard_map/ppermute | solution.py:216
  34.2 1.6 %collective-permute-start.16 = (bf16[1,256,512]{2,1,0:T(8,128)(2,1)S(1)}, bf16[1,256,512]{2,1,0:T(8,128)(2,1)S(1)}, u32[]{:S(2)}, u32[]{:S(2)}) collective-permute-start(bf16[1,256,512]{2,1,0:T(8,128)(2,1)S(1)} %place_other_sectors.1.own), channel_id=1, source_target_pairs={{1,0},{0,1},{3,2},{2,3},{5,4},{4,5},{7,6},{6,7},{9,8},{8,9},{11,10... | collective-permute-start | bytes 786440 | tf_op jit(solution)/shard_map/ppermute | solution.py:216
  37.7 8.7 %collective-permute-start.17 = (bf16[1,64,512]{2,1,0:T(8,128)(2,1)S(1)}, bf16[1,64,512]{2,1,0:T(8,128)(2,1)S(1)}, u32[]{:S(2)}, u32[]{:S(2)}) collective-permute-start(bf16[1,64,512]{2,1,0:T(8,128)(2,1)S(1)} %get-tuple-element.33), channel_id=1, source_target_pairs={{12,0},{8,4},{4,8},{0,12},{13,1},{9,5},{5,9},{1,13},{14,2},{10,6},... | collective-permute-start | bytes 196616 | tf_op jit(solution)/shard_map/ppermute | solution.py:216
  40.2 6.3 %collective-permute-start.18 = (bf16[1,64,512]{2,1,0:T(8,128)(2,1)S(1)}, bf16[1,64,512]{2,1,0:T(8,128)(2,1)S(1)}, u32[]{:S(2)}, u32[]{:S(2)}) collective-permute-start(bf16[1,64,512]{2,1,0:T(8,128)(2,1)S(1)} %get-tuple-element.34), channel_id=1, source_target_pairs={{8,0},{12,4},{0,8},{4,12},{9,1},{13,5},{1,9},{5,13},{10,2},{14,6},... | collective-permute-start | bytes 196616 | tf_op jit(solution)/shard_map/ppermute | solution.py:216
  40.2 6.3 %collective-permute-start.19 = (bf16[1,64,512]{2,1,0:T(8,128)(2,1)S(1)}, bf16[1,64,512]{2,1,0:T(8,128)(2,1)S(1)}, u32[]{:S(2)}, u32[]{:S(2)}) collective-permute-start(bf16[1,64,512]{2,1,0:T(8,128)(2,1)S(1)} %get-tuple-element.35), channel_id=1, source_target_pairs={{4,0},{0,4},{12,8},{8,12},{5,1},{1,5},{13,9},{9,13},{6,2},{2,6},{1... | collective-permute-start | bytes 196616 | tf_op jit(solution)/shard_map/ppermute | solution.py:216
  42.7 3.8 %collective-permute-start.11 = (f32[3,8,128]{2,1,0:T(8,128)S(1)}, f32[3,8,128]{2,1,0:T(8,128)S(1)}, u32[]{:S(2)}, u32[]{:S(2)}) collective-permute-start(f32[3,8,128]{2,1,0:T(8,128)S(1)} %sums_for_rayleigh.1.refs_0_.refs_4_), channel_id=1, source_target_pairs={{2,0},{0,2},{3,1},{1,3},{6,4},{4,6},{7,5},{5,7},{10,8},{8,10},{11,... | collective-permute-start | bytes 36872 | tf_op jit(solution)/shard_map/ppermute | solution.py:216
  46.6 6.7 %collective-permute-start.22 = (bf16[1,64,512]{2,1,0:T(8,128)(2,1)S(1)}, bf16[1,64,512]{2,1,0:T(8,128)(2,1)S(1)}, u32[]{:S(2)}, u32[]{:S(2)}) collective-permute-start(bf16[1,64,512]{2,1,0:T(8,128)(2,1)S(1)} %sum_second_sigma.1.refs_0_), channel_id=1, source_target_pairs={{12,0},{8,4},{4,8},{0,12},{13,1},{9,5},{5,9},{1,13},{14,2},{10,6},... | collective-permute-start | bytes 196616 | tf_op jit(solution)/shard_map/ppermute | solution.py:216
  49.0 6.2 %collective-permute-start.21 = (bf16[1,64,512]{2,1,0:T(8,128)(2,1)S(1)}, bf16[1,64,512]{2,1,0:T(8,128)(2,1)S(1)}, u32[]{:S(2)}, u32[]{:S(2)}) collective-permute-start(bf16[1,64,512]{2,1,0:T(8,128)(2,1)S(1)} %sum_second_sigma.1.refs_0_), channel_id=1, source_target_pairs={{8,0},{12,4},{0,8},{4,12},{9,1},{13,5},{1,9},{5,13},{10,2},{14,6},... | collective-permute-start | bytes 196616 | tf_op jit(solution)/shard_map/ppermute | solution.py:216
  49.0 6.2 %collective-permute-start.20 = (bf16[1,64,512]{2,1,0:T(8,128)(2,1)S(1)}, bf16[1,64,512]{2,1,0:T(8,128)(2,1)S(1)}, u32[]{:S(2)}, u32[]{:S(2)}) collective-permute-start(bf16[1,64,512]{2,1,0:T(8,128)(2,1)S(1)} %sum_second_sigma.1.refs_0_), channel_id=1, source_target_pairs={{4,0},{0,4},{12,8},{8,12},{5,1},{1,5},{13,9},{9,13},{6,2},{2,6},{1... | collective-permute-start | bytes 196616 | tf_op jit(solution)/shard_map/ppermute | solution.py:216

commit v10 on v9

--- a/solution.py
+++ b/solution.py
@@ -27,14 +27,14 @@
     return jnp.where(live, values.astype(jnp.float32), 0.0).astype(values.dtype)
 
 
-def left_times(left_own, left_other, own, other):
-    terms, rows, depth = left_own.shape
-    product = jnp.dot(
-        left_own[...].reshape(terms * rows, depth), own, preferred_element_type=jnp.float32
-    ) + jnp.dot(
-        left_other[...].reshape(terms * rows, depth), other, preferred_element_type=jnp.float32
-    )
-    return product.reshape(terms, rows, -1)
+def left_times(lefts, blocks):
+    total = None
+    for left, block in zip(lefts, blocks):
+        terms, rows, depth = left.shape
+        stacked = left[...].reshape(terms * rows, depth)
+        part = jnp.dot(stacked, block, preferred_element_type=jnp.float32)
+        total = part if total is None else total + part
+    return total.reshape(terms, rows, -1)
 
 
 def times_right(values, right, term):
@@ -76,7 +76,7 @@
     live = live_cells(sizes_ref, sector, (core ^ 1) * rows, rows, columns)
     other[...] = masked(arrived[0], live)
     totals = [None] * sectors
-    products = left_times(left_own, left_other, own[...], other[...])
+    products = left_times((left_own, left_other), (own[...], other[...]))
     for term in range(right.shape[0]):
         product = times_right(products[term], right, term)
         for step in range(sectors):
@@ -108,29 +108,29 @@
         half[index, pl.ds(start, share), :] = piece[0]
 
 
-def left_kernel(left_own, left_other, own, other, out):
-    out[...] = left_times(left_own, left_other, own[0], other[0])
+def left_kernel(left_own, left_other, own, other, across_own, out, across_out):
+    out[...] = left_times((left_own, left_other), (own[0], other[0]))
+    for step in range(across_own.shape[0]):
+        across_out[step] = left_times((left_own,), (across_own[step],))
 
 
 def second_kernel(
-    sizes_ref, pairs_ref, weights_ref, left_own, left_other, right, products, own, other, *refs
+    sizes_ref, pairs_ref, weights_ref, left_other, right, products, across_products, other, *refs
 ):
     shares, held = refs[:-1], refs[-1]
-    rows, columns = own.shape[1:]
+    rows, columns = products.shape[1:]
     share = shares[0].shape[1]
     target = lax.axis_index("sec")
     core = lax.axis_index("rep")
     place = lax.axis_index("ops")
     total = None
-    across = [
-        left_times(left_own, left_other, own[step], other[step]) for step in range(own.shape[0])
-    ]
+    across = [left_times((left_other,), (other[step],)) for step in range(other.shape[0])]
     for term in range(right.shape[0]):
         weight = mixing_scalar(pairs_ref, weights_ref, term, target, target)
         combined = weight * products[term]
         for step, part in enumerate(across, 1):
             weight = mixing_scalar(pairs_ref, weights_ref, term, target, target ^ step)
-            combined = combined + weight * part[term]
+            combined = combined + weight * (across_products[step - 1, term] + part[term])
         part = times_right(combined, right, term)
         total = part if total is None else total + part
     live = live_cells(sizes_ref, target, core * rows, rows, columns)
@@ -190,7 +190,7 @@
     scale = jnp.broadcast_to(factors[0][:1, :1], (share, columns))
     shift = jnp.broadcast_to(factors[1][:1, :1], (share, columns))
     copies = []
-    for step, piece in enumerate(pieces):
+    for step, piece in zip(reversed(range(len(pieces))), pieces):
         rows = pl.ds(pl.multiple_of((place ^ step) * share, share), share)
         moved = shift * sigma_own[0, rows, :].astype(jnp.float32)
         held[step] = scale * piece[0].astype(jnp.float32) - moved
@@ -270,7 +270,7 @@
         vmem=49,
     )
     pairs = jnp.swapaxes(sector_pairs, 1, 2)
-    operators = (sector_sizes, pairs, pair_weights, left_own, left_other, right)
+    scalars = (sector_sizes, pairs, pair_weights)
 
     far = ops_count - 1
     direct = [(along,) for along in farthest_first[1:-1]]
@@ -285,7 +285,10 @@
             for along, across in spots
         ],
         [smem] * 3,
-        *operators,
+        *scalars,
+        left_own,
+        left_other,
+        right,
         wavefunction,
         arrived,
         scratch=[pltpu.VMEM((sectors, rows, columns), f32)],
@@ -299,49 +302,57 @@
         for across in range(sectors)
     ]
     first_share = summed("sum_first_sigma", *[(piece, 1) for piece in met], *received)
-    along_ops = {along: partner(first_share, {"ops": along}) for along in farthest_first}
+    crossed = {
+        along: partner(first_share, {"ops": along}) for along in farthest_first if along % 2 == 0
+    }
+    pieces = {
+        (along, across): partner(crossed[along // 2 * 2], {"ops": along % 2, "sec": across})
+        for along in farthest_first
+        for across in range(sectors)
+    }
     sigma_own = call(
         lambda *refs: place_kernel([(along, 0) for along in farthest_first], *refs),
         "place_own_sector",
         shape(1, rows, columns),
         [],
-        *along_ops.values(),
+        *[pieces[along, 0] for along in farthest_first],
+        *[pieces[spot] for spot in pieces if spot[0] < 2 and spot[1]],
     )
     sigma_other = partner(sigma_own, {"rep": 1})
     spots = [(along, across) for along in farthest_first for across in range(1, sectors)]
-    pieces = [
-        partner(first_share, {"ops": along, "sec": across})
-        if along < 2
-        else partner(along_ops[along], {"sec": across})
-        for along, across in spots
-    ]
     across_own = call(
         lambda *refs: place_kernel([(along, across - 1) for along, across in spots], *refs),
         "place_other_sectors",
         shape(sectors - 1, rows, columns),
         [],
-        *pieces,
+        *[pieces[spot] for spot in spots],
     )
     across_other = partner(across_own, {"rep": 1})
 
-    products = call(
+    products, across_products = call(
         left_kernel,
         "left_products",
-        shape(terms, rows, columns, dtype=f32),
+        [
+            shape(terms, rows, columns, dtype=f32),
+            shape(sectors - 1, terms, rows, columns, dtype=f32),
+        ],
         [],
         left_own,
         left_other,
         sigma_own,
         sigma_other,
+        across_own,
     )
     shares = call(
         second_kernel,
         "second_sigma_terms",
         [shape(1, share, columns, dtype=f32)] + [shape(1, share, columns)] * (ops_count - 1),
         [smem] * 3,
-        *operators,
+        *scalars,
+        left_other,
+        right,
         products,
-        across_own,
+        across_products,
         across_other,
         scratch=[pltpu.VMEM((rows, columns), f32)],
     )
@@ -375,7 +386,7 @@
         [],
         factors,
         sigma_own,
-        *[partner(second_share, {"ops": step}) for step in range(ops_count)],
+        *[partner(second_share, {"ops": step}) for step in farthest_first],
         scratch=[
             pltpu.VMEM((ops_count, share, columns), f32),
             pltpu.SemaphoreType.DMA((ops_count,)),

time: 56.3 us -> 56.6 us (level)
  transfers between devices with their start and end apart: 23 -> 23, of which waited for: 11 -> 11; matrix products, arithmetic and copies ran while one was open for 0% -> 0% of each run, Pallas kernels for 8% -> 9%
where the time goes in v10:
time: 56.6 us; the launch traced here: 56.5 us
  starting transfers between devices  31.8 us (56%)
  waiting for transfers between devices  13.9 us (25%)
  Pallas kernels  9.98 us (18%)
  between operations  0.8 us (1%)
    ppermute x23, starting transfers between devices, partner(): return lax.ppermute(value, axes, pairs)  31.8 us
    ppermute x23, waiting for transfers between devices, partner(): return lax.ppermute(value, axes, pairs)  13.9 us
    pallas_call x12, Pallas kernels, call(): pl.pallas_call(kernel, out_shape=out_shape, in_specs=list(in_specs) + [in...  9.98 us
  transfers between devices with their start and end apart: 23, of which 11 were waited for; matrix products, arithmetic and copies ran while one was open for 0% of the time, Pallas kernels for 9%

profile of v10, /device:TPU:0, one launch (start us, length us, event | category | flops | bytes accessed | tf_op | source)
XLA Modules:
  0.0 56.5 jit_solution(12110153041537004404)
XLA Ops:
  0.6 0.0 copy-start
  0.6 0.0 copy-start.2
  0.7 0.0 copy-start.1
  0.7 0.0 copy-start.3
  0.7 0.5 collective-permute-start
  1.2 2.0 %load_operators.1 = (bf16[4,256,256]{2,1,0:T(8,128)(2,1)S(1)}, bf16[4,256,256]{2,1,0:T(8,128)(2,1)S(1)}, bf16[4,512,512]{2,1,0:T(8,128)(2,1)S(1)}) custom-call(bf16[4,512,512]{2,1,0:T(8,128)(2,1)} %left_ref.1, bf16[4,512,512]{2,1,0:T(8,128)(2,1)} %right_ref.1), custom_call_target="tpu_custom_call" | custom-call | tf_op jit(solution)/shard_map/load_operators/pallas_call | solution.py:234
  3.2 0.0 collective-permute-done.refs_7_
  3.2 0.0 copy-done
  3.2 0.0 copy-done.2
  3.2 0.0 copy-done.1
  3.2 0.0 copy-done.3
  3.2 2.2 %first_sigma_terms.1 = (bf16[256,512]{1,0:T(8,128)(2,1)S(1)}, bf16[256,512]{1,0:T(8,128)(2,1)S(1)}, f32[2,64,512]{2,1,0:T(8,128)S(1)}, bf16[2,64,512]{2,1,0:T(8,...) custom-call(s32[2,2]{1,0:T(2,128)S(1)} %copy-done.2, ...), custom_call_target="tpu_custom_call" | custom-call | tf_op jit(solution)/shard_map/first_sigma_terms/pallas_call | solution.py:234
  5.4 2.6 %collective-permute-start.1 = (bf16[2,64,512]{2,1,0:T(8,128)(2,1)S(1)}, bf16[2,64,512]{2,1,0:T(8,128)(2,1)S(1)}, u32[]{:S(2)}, u32[]{:S(2)}) collective-permute-start(bf16[2,64,512]{2,1,0:T(8,128)(2,1)S(1)} %get-tuple-element.26), channel_id=1, source_target_pairs={{2,0},{0,2},{3,1},{1,3},{6,4},{4,6},{7,5},{5,7},{10,8},{8,10},{11,... | collective-permute-start | bytes 393224 | tf_op jit(solution)/shard_map/ppermute | solution.py:216
  8.0 2.6 %collective-permute-start.3 = (bf16[1,64,512]{2,1,0:T(8,128)(2,1)S(1)}, bf16[1,64,512]{2,1,0:T(8,128)(2,1)S(1)}, u32[]{:S(2)}, u32[]{:S(2)}) collective-permute-start(bf16[1,64,512]{2,1,0:T(8,128)(2,1)S(1)} %get-tuple-element.27), channel_id=1, source_target_pairs={{8,0},{12,4},{0,8},{4,12},{9,1},{13,5},{1,9},{5,13},{10,2},{14,6},... | collective-permute-start | bytes 196616 | tf_op jit(solution)/shard_map/ppermute | solution.py:216
  10.6 0.0 collective-permute-start.4
  10.6 1.9 %collective-permute-start.5 = (bf16[1,64,512]{2,1,0:T(8,128)(2,1)S(1)}, bf16[1,64,512]{2,1,0:T(8,128)(2,1)S(1)}, u32[]{:S(2)}, u32[]{:S(2)}) collective-permute-start(bf16[1,64,512]{2,1,0:T(8,128)(2,1)S(1)} %get-tuple-element.29), channel_id=1, source_target_pairs={{4,0},{0,4},{12,8},{8,12},{5,1},{1,5},{13,9},{9,13},{6,2},{2,6},{1... | collective-permute-start | bytes 196616 | tf_op jit(solution)/shard_map/ppermute | solution.py:216
  12.5 1.4 %collective-permute-start.6 = (bf16[1,64,512]{2,1,0:T(8,128)(2,1)S(1)}, bf16[1,64,512]{2,1,0:T(8,128)(2,1)S(1)}, u32[]{:S(2)}, u32[]{:S(2)}) collective-permute-start(bf16[1,64,512]{2,1,0:T(8,128)(2,1)S(1)} %get-tuple-element.30), channel_id=1, source_target_pairs={{6,0},{4,2},{2,4},{0,6},{14,8},{12,10},{10,12},{8,14},{7,1},{5,3},... | collective-permute-start | bytes 196616 | tf_op jit(solution)/shard_map/ppermute | solution.py:216
  13.8 0.0 collective-permute-done.1.refs_1_
  13.9 3.7 %collective-permute-start.2 = (bf16[1,64,512]{2,1,0:T(8,128)(2,1)S(1)}, bf16[1,64,512]{2,1,0:T(8,128)(2,1)S(1)}, u32[]{:S(2)}, u32[]{:S(2)}) collective-permute-start(bf16[1,64,512]{2,1,0:T(8,128)(2,1)S(1)} %sum_far_share.1), channel_id=1, source_target_pairs={{12,0},{8,4},{4,8},{0,12},{13,1},{9,5},{5,9},{1,13},{14,2},{10,6},... | collective-permute-start | bytes 196616 | tf_op jit(solution)/shard_map/ppermute | solution.py:216
  17.5 0.0 collective-permute-done.3.refs_3_
  17.5 1.1 %collective-permute-done.4.refs_4_ = bf16[1,64,512]{2,1,0:T(8,128)(2,1)S(1)} collective-permute-done((bf16[1,64,512]{2,1,0:T(8,128)(2,1)S(1)}, bf16[1,64,512]{2,1,0:T(8,128)(2,1)S(1)}, u32[]{:S(2)}, u32[]{:S(2)}) %collective-permute-start.4) | collective-permute-done | bytes 65568 | tf_op jit(solution)/shard_map/ppermute | solution.py:216
  18.6 0.0 collective-permute-done.5.refs_5_
  18.6 0.0 collective-permute-done.6.refs_6_
  18.6 2.0 %collective-permute-done.2.refs_2_ = bf16[1,64,512]{2,1,0:T(8,128)(2,1)S(1)} collective-permute-done((bf16[1,64,512]{2,1,0:T(8,128)(2,1)S(1)}, bf16[1,64,512]{2,1,0:T(8,128)(2,1)S(1)}, u32[]{:S(2)}, u32[]{:S(2)}) %collective-permute-start.2) | collective-permute-done | bytes 65568 | tf_op jit(solution)/shard_map/ppermute | solution.py:216
  20.6 0.1 sum_first_sigma.1.refs_3_
  20.7 1.5 %collective-permute-start.7 = (bf16[1,64,512]{2,1,0:T(8,128)(2,1)S(1)}, bf16[1,64,512]{2,1,0:T(8,128)(2,1)S(1)}, u32[]{:S(2)}, u32[]{:S(2)}) collective-permute-start(bf16[1,64,512]{2,1,0:T(8,128)(2,1)S(1)} %sum_first_sigma.1.refs_3_), channel_id=1, source_target_pairs={{8,0},{12,4},{0,8},{4,12},{9,1},{13,5},{1,9},{5,13},{10,2},{14,6},... | collective-permute-start | bytes 196616 | tf_op jit(solution)/shard_map/ppermute | solution.py:216
  22.2 3.0 %collective-permute-start.9 = (bf16[1,64,512]{2,1,0:T(8,128)(2,1)S(1)}, bf16[1,64,512]{2,1,0:T(8,128)(2,1)S(1)}, u32[]{:S(2)}, u32[]{:S(2)}) collective-permute-start(bf16[1,64,512]{2,1,0:T(8,128)(2,1)S(1)} %sum_first_sigma.1.refs_3_), channel_id=1, source_target_pairs={{4,0},{0,4},{12,8},{8,12},{5,1},{1,5},{13,9},{9,13},{6,2},{2,6},{1... | collective-permute-start | bytes 196616 | tf_op jit(solution)/shard_map/ppermute | solution.py:216
  25.2 0.2 collective-permute-start.10
  25.4 1.2 %collective-permute-start.11 = (bf16[1,64,512]{2,1,0:T(8,128)(2,1)S(1)}, bf16[1,64,512]{2,1,0:T(8,128)(2,1)S(1)}, u32[]{:S(2)}, u32[]{:S(2)}) collective-permute-start(bf16[1,64,512]{2,1,0:T(8,128)(2,1)S(1)} %sum_first_sigma.1.refs_3_), channel_id=1, source_target_pairs={{2,0},{0,2},{3,1},{1,3},{6,4},{4,6},{7,5},{5,7},{10,8},{8,10},{11,... | collective-permute-start | bytes 196616 | tf_op jit(solution)/shard_map/ppermute | solution.py:216
  26.7 0.0 collective-permute-done.7.refs_1_
  26.7 2.0 %collective-permute-start.8 = (bf16[1,64,512]{2,1,0:T(8,128)(2,1)S(1)}, bf16[1,64,512]{2,1,0:T(8,128)(2,1)S(1)}, u32[]{:S(2)}, u32[]{:S(2)}) collective-permute-start(bf16[1,64,512]{2,1,0:T(8,128)(2,1)S(1)} %collective-permute-done.7.refs_1_), channel_id=1, source_target_pairs={{4,0},{0,4},{12,8},{8,12},{5,1},{1,5},{13,9},{9,13},{6,2},{2,6},{1... | collective-permute-start | bytes 196616 | tf_op jit(solution)/shard_map/ppermute | solution.py:216
  28.7 1.0 %collective-permute-start.14 = (bf16[1,64,512]{2,1,0:T(8,128)(2,1)S(1)}, bf16[1,64,512]{2,1,0:T(8,128)(2,1)S(1)}, u32[]{:S(2)}, u32[]{:S(2)}) collective-permute-start(bf16[1,64,512]{2,1,0:T(8,128)(2,1)S(1)} %collective-permute-done.7.refs_1_), channel_id=1, source_target_pairs={{6,0},{4,2},{2,4},{0,6},{14,8},{12,10},{10,12},{8,14},{7,1},{5,3},... | collective-permute-start | bytes 196616 | tf_op jit(solution)/shard_map/ppermute | solution.py:216
  29.7 0.0 collective-permute-done.9.refs_2_
  29.7 0.5 collective-permute-start.15
  30.2 0.4 collective-permute-done.10.refs_4_.refs_2_
  30.6 0.9 %collective-permute-done.11.refs_5_.refs_3_ = bf16[1,64,512]{2,1,0:T(8,128)(2,1)S(1)} collective-permute-done((bf16[1,64,512]{2,1,0:T(8,128)(2,1)S(1)}, bf16[1,64,512]{2,1,0:T(8,128)(2,1)S(1)}, u32[]{:S(2)}, u32[]{:S(2)}) %collective-permute-start.11) | collective-permute-done | bytes 65568 | tf_op jit(solution)/shard_map/ppermute | solution.py:216
  31.5 0.0 collective-permute-done.8.refs_0_
  31.5 0.1 collective-permute-start.12
  31.6 2.3 %collective-permute-done.14.refs_0_ = bf16[1,64,512]{2,1,0:T(8,128)(2,1)S(1)} collective-permute-done((bf16[1,64,512]{2,1,0:T(8,128)(2,1)S(1)}, bf16[1,64,512]{2,1,0:T(8,128)(2,1)S(1)}, u32[]{:S(2)}, u32[]{:S(2)}) %collective-permute-start.14) | collective-permute-done | bytes 65568 | tf_op jit(solution)/shard_map/ppermute | solution.py:216
  33.9 0.6 %collective-permute-done.15.refs_1_ = bf16[1,64,512]{2,1,0:T(8,128)(2,1)S(1)} collective-permute-done((bf16[1,64,512]{2,1,0:T(8,128)(2,1)S(1)}, bf16[1,64,512]{2,1,0:T(8,128)(2,1)S(1)}, u32[]{:S(2)}, u32[]{:S(2)}) %collective-permute-start.15) | collective-permute-done | bytes 65568 | tf_op jit(solution)/shard_map/ppermute | solution.py:216
  34.6 0.1 collective-permute-start.16
  34.7 0.0 collective-permute-done.12.sigma_other.other
  34.7 1.0 %left_products.1 = (f32[4,256,512]{2,1,0:T(8,128)S(1)}, f32[1,4,256,512]{3,2,1,0:T(8,128)S(1)}) custom-call(bf16[4,256,256]{2,1,0:T(8,128)(2,1)S(1)} %get-tuple-element.21.refs_3_.left_own, bf16[4,256,256]{2,1,0:T(8,128)(2,1)S(1)} %get-tuple-element.22.refs_4_.left_other, bf16[1,256,512]{2,1,0:T(8,128)(2,1)S(1)} %place_own_sector.1.sigma_own.own, ...), custom_call_target="tpu_custom_call" | custom-call | tf_op jit(solution)/shard_map/left_products/pallas_call | solution.py:234
  35.7 0.5 collective-permute-done.16.other
  36.2 1.9 %second_sigma_terms.1 = (f32[1,64,512]{2,1,0:T(8,128)S(1)}, bf16[1,64,512]{2,1,0:T(8,128)(2,1)S(1)}, bf16[1,64,512]{2,1,0:T(8,128)(2,1)S(1)}, bf16[1,64,512]{2,1,0:T(8,128)(2,1)S(1)}) custom-call(s32[2,2]{1,0:T(2,128)S(1)} %copy-done.2, s32[4,2,8]{2,1,0:T(2,128)S(1)} %bitcast.2, f32[4,8]{1,0:T(4,128)S(1)} %copy-done.3, ...), custom_call_target="tpu_custom_call" | custom-call | tf_op jit(solution)/shard_map/second_sigma_terms/pallas_call | solution.py:234
  38.1 1.9 %collective-permute-start.17 = (bf16[1,64,512]{2,1,0:T(8,128)(2,1)S(1)}, bf16[1,64,512]{2,1,0:T(8,128)(2,1)S(1)}, u32[]{:S(2)}, u32[]{:S(2)}) collective-permute-start(bf16[1,64,512]{2,1,0:T(8,128)(2,1)S(1)} %get-tuple-element.37), channel_id=1, source_target_pairs={{12,0},{8,4},{4,8},{0,12},{13,1},{9,5},{5,9},{1,13},{14,2},{10,6},... | collective-permute-start | bytes 196616 | tf_op jit(solution)/shard_map/ppermute | solution.py:216
  40.0 0.2 collective-permute-start.18
  40.2 2.3 %collective-permute-start.19 = (bf16[1,64,512]{2,1,0:T(8,128)(2,1)S(1)}, bf16[1,64,512]{2,1,0:T(8,128)(2,1)S(1)}, u32[]{:S(2)}, u32[]{:S(2)}) collective-permute-start(bf16[1,64,512]{2,1,0:T(8,128)(2,1)S(1)} %get-tuple-element.39), channel_id=1, source_target_pairs={{4,0},{0,4},{12,8},{8,12},{5,1},{1,5},{13,9},{9,13},{6,2},{2,6},{1... | collective-permute-start | bytes 196616 | tf_op jit(solution)/shard_map/ppermute | solution.py:216
  42.5 0.5 sums_for_rayleigh.1.refs_0_.refs_4_
  43.0 0.6 %collective-permute-start.13 = (f32[3,8,128]{2,1,0:T(8,128)S(1)}, f32[3,8,128]{2,1,0:T(8,128)S(1)}, u32[]{:S(2)}, u32[]{:S(2)}) collective-permute-start(f32[3,8,128]{2,1,0:T(8,128)S(1)} %sums_for_rayleigh.1.refs_0_.refs_4_), channel_id=1, source_target_pairs={{2,0},{0,2},{3,1},{1,3},{6,4},{4,6},{7,5},{5,7},{10,8},{8,10},{11,... | collective-permute-start | bytes 36872 | tf_op jit(solution)/shard_map/ppermute | solution.py:216
  43.7 3.1 %collective-permute-done.13.refs_1_.refs_5_ = f32[3,8,128]{2,1,0:T(8,128)S(1)} collective-permute-done((f32[3,8,128]{2,1,0:T(8,128)S(1)}, f32[3,8,128]{2,1,0:T(8,128)S(1)}, u32[]{:S(2)}, u32[]{:S(2)}) %collective-permute-start.13) | collective-permute-done | bytes 12320 | tf_op jit(solution)/shard_map/ppermute | solution.py:216
  46.8 0.0 collective-permute-done.17.refs_1_
  46.8 0.1 collective-permute-done.18.refs_2_
  46.9 0.0 collective-permute-done.19.refs_3_
  46.9 1.9 %collective-permute-start.20 = (bf16[1,64,512]{2,1,0:T(8,128)(2,1)S(1)}, bf16[1,64,512]{2,1,0:T(8,128)(2,1)S(1)}, u32[]{:S(2)}, u32[]{:S(2)}) collective-permute-start(bf16[1,64,512]{2,1,0:T(8,128)(2,1)S(1)} %sum_second_sigma.1.refs_3_), channel_id=1, source_target_pairs={{12,0},{8,4},{4,8},{0,12},{13,1},{9,5},{5,9},{1,13},{14,2},{10,6},... | collective-permute-start | bytes 196616 | tf_op jit(solution)/shard_map/ppermute | solution.py:216
  48.9 0.0 collective-permute-start.21
  48.9 2.5 %collective-permute-start.22 = (bf16[1,64,512]{2,1,0:T(8,128)(2,1)S(1)}, bf16[1,64,512]{2,1,0:T(8,128)(2,1)S(1)}, u32[]{:S(2)}, u32[]{:S(2)}) collective-permute-start(bf16[1,64,512]{2,1,0:T(8,128)(2,1)S(1)} %sum_second_sigma.1.refs_3_), channel_id=1, source_target_pairs={{4,0},{0,4},{12,8},{8,12},{5,1},{1,5},{13,9},{9,13},{6,2},{2,6},{1... | collective-permute-start | bytes 196616 | tf_op jit(solution)/shard_map/ppermute | solution.py:216
  51.4 1.4 %second_wave.1 = (bf16[1,256,512]{2,1,0:T(8,128)(2,1)}, f32[2,8,128]{2,1,0:T(8,128)S(1)}) custom-call(s32[2,2]{1,0:T(2,128)S(1)} %copy-done.2, bf16[256,512]{1,0:T(8,128)(2,1)S(1)} %get-tuple-element.24.wave_own, bf16[1,256,512]{2,1,0:T(8,128)(2,1)S(1)} %place_own_sector.1.sigma_own.own, f32[3,8,128]{2,1,0:T(8,128)S(1)} %sums_for_rayleigh.1.refs_0_.refs_4_, ...), custom_call_target="tpu_custom_call" | custom-call | tf_op jit(solution)/shard_map/second_wave/pallas_call | solution.py:234
  52.8 1.0 %collective-permute-done.20.refs_0_ = bf16[1,64,512]{2,1,0:T(8,128)(2,1)S(1)} collective-permute-done((bf16[1,64,512]{2,1,0:T(8,128)(2,1)S(1)}, bf16[1,64,512]{2,1,0:T(8,128)(2,1)S(1)}, u32[]{:S(2)}, u32[]{:S(2)}) %collective-permute-start.20) | collective-permute-done | bytes 65568 | tf_op jit(solution)/shard_map/ppermute | solution.py:216
  53.8 1.8 %collective-permute-done.21.refs_1_ = bf16[1,64,512]{2,1,0:T(8,128)(2,1)S(1)} collective-permute-done((bf16[1,64,512]{2,1,0:T(8,128)(2,1)S(1)}, bf16[1,64,512]{2,1,0:T(8,128)(2,1)S(1)}, u32[]{:S(2)}, u32[]{:S(2)}) %collective-permute-start.21) | collective-permute-done | bytes 65568 | tf_op jit(solution)/shard_map/ppermute | solution.py:216
  55.6 0.0 collective-permute-done.22.refs_2_
  55.6 0.9 %join_second_sigma.1 = f32[1,256,512]{2,1,0:T(8,128)} custom-call(f32[2,8,128]{2,1,0:T(8,128)S(1)} %get-tuple-element.33.factors, bf16[1,256,512]{2,1,0:T(8,128)(2,1)S(1)} %place_own_sector.1.sigma_own.own, bf16[1,64,512]{2,1,0:T(8,128)(2,1)S(1)} %collective-permute-done.20.refs_0_, bf16[1,64,512]{2,1,0:T(8,128)(2,1)S(1)} %collective-permute-done.21.refs_1_, ...), custom_call_target="tpu_custom_call" | custom-call | tf_op jit(solution)/shard_map/join_second_sigma/pallas_call | solution.py:234
  (4 shorter events, 0.1 us)
Async XLA Ops:
  0.6 2.5 %copy-start = (bf16[1,256,512]{2,1,0:T(8,128)(2,1)S(1)}, bf16[1,256,512]{2,1,0:T(8,128)(2,1)}, u32[]{:S(2)}) copy-start(bf16[1,256,512]{2,1,0:T(8,128)(2,1)} %refs_6_.1) | copy-start | bytes 786436
  0.6 2.5 %copy-start.2 = (s32[2,2]{1,0:T(2,128)S(1)}, s32[2,2]{1,0:T(2,128)}, u32[]{:S(2)}) copy-start(s32[2,2]{1,0:T(2,128)} %sizes_ref.3) | copy-start | bytes 52
  0.7 2.5 %copy-start.1 = (s32[4,8,2]{1,2,0:T(2,128)S(1)}, s32[4,8,2]{1,2,0:T(2,128)}, u32[]{:S(2)}) copy-start(s32[4,8,2]{1,2,0:T(2,128)} %param.10) | copy-start | bytes 772
  0.7 2.5 %copy-start.3 = (f32[4,8]{1,0:T(4,128)S(1)}, f32[4,8]{1,0:T(4,128)}, u32[]{:S(2)}) copy-start(f32[4,8]{1,0:T(4,128)} %weights_ref.1) | copy-start | bytes 388
  0.7 2.5 %collective-permute-start = (bf16[1,256,512]{2,1,0:T(8,128)(2,1)}, bf16[1,256,512]{2,1,0:T(8,128)(2,1)S(1)}, u32[]{:S(2)}, u32[]{:S(2)}) collective-permute-start(bf16[1,256,512]{2,1,0:T(8,128)(2,1)} %refs_6_.1), channel_id=1, source_target_pairs={{1,0},{0,1},{3,2},{2,3},{5,4},{4,5},{7,6},{6,7},{9,8},{8,9},{11,10... | collective-permute-start | bytes 786440 | tf_op jit(solution)/shard_map/ppermute | solution.py:216
  5.4 8.4 %collective-permute-start.1 = (bf16[2,64,512]{2,1,0:T(8,128)(2,1)S(1)}, bf16[2,64,512]{2,1,0:T(8,128)(2,1)S(1)}, u32[]{:S(2)}, u32[]{:S(2)}) collective-permute-start(bf16[2,64,512]{2,1,0:T(8,128)(2,1)S(1)} %get-tuple-element.26), channel_id=1, source_target_pairs={{2,0},{0,2},{3,1},{1,3},{6,4},{4,6},{7,5},{5,7},{10,8},{8,10},{11,... | collective-permute-start | bytes 393224 | tf_op jit(solution)/shard_map/ppermute | solution.py:216
  8.0 9.6 %collective-permute-start.3 = (bf16[1,64,512]{2,1,0:T(8,128)(2,1)S(1)}, bf16[1,64,512]{2,1,0:T(8,128)(2,1)S(1)}, u32[]{:S(2)}, u32[]{:S(2)}) collective-permute-start(bf16[1,64,512]{2,1,0:T(8,128)(2,1)S(1)} %get-tuple-element.27), channel_id=1, source_target_pairs={{8,0},{12,4},{0,8},{4,12},{9,1},{13,5},{1,9},{5,13},{10,2},{14,6},... | collective-permute-start | bytes 196616 | tf_op jit(solution)/shard_map/ppermute | solution.py:216
  10.6 8.1 %collective-permute-start.4 = (bf16[1,64,512]{2,1,0:T(8,128)(2,1)S(1)}, bf16[1,64,512]{2,1,0:T(8,128)(2,1)S(1)}, u32[]{:S(2)}, u32[]{:S(2)}) collective-permute-start(bf16[1,64,512]{2,1,0:T(8,128)(2,1)S(1)} %get-tuple-element.28), channel_id=1, source_target_pairs={{10,0},{8,2},{14,4},{12,6},{2,8},{0,10},{6,12},{4,14},{11,1},{9,3}... | collective-permute-start | bytes 196616 | tf_op jit(solution)/shard_map/ppermute | solution.py:216
  10.6 8.1 %collective-permute-start.5 = (bf16[1,64,512]{2,1,0:T(8,128)(2,1)S(1)}, bf16[1,64,512]{2,1,0:T(8,128)(2,1)S(1)}, u32[]{:S(2)}, u32[]{:S(2)}) collective-permute-start(bf16[1,64,512]{2,1,0:T(8,128)(2,1)S(1)} %get-tuple-element.29), channel_id=1, source_target_pairs={{4,0},{0,4},{12,8},{8,12},{5,1},{1,5},{13,9},{9,13},{6,2},{2,6},{1... | collective-permute-start | bytes 196616 | tf_op jit(solution)/shard_map/ppermute | solution.py:216
  12.5 6.2 %collective-permute-start.6 = (bf16[1,64,512]{2,1,0:T(8,128)(2,1)S(1)}, bf16[1,64,512]{2,1,0:T(8,128)(2,1)S(1)}, u32[]{:S(2)}, u32[]{:S(2)}) collective-permute-start(bf16[1,64,512]{2,1,0:T(8,128)(2,1)S(1)} %get-tuple-element.30), channel_id=1, source_target_pairs={{6,0},{4,2},{2,4},{0,6},{14,8},{12,10},{10,12},{8,14},{7,1},{5,3},... | collective-permute-start | bytes 196616 | tf_op jit(solution)/shard_map/ppermute | solution.py:216
  13.9 6.7 %collective-permute-start.2 = (bf16[1,64,512]{2,1,0:T(8,128)(2,1)S(1)}, bf16[1,64,512]{2,1,0:T(8,128)(2,1)S(1)}, u32[]{:S(2)}, u32[]{:S(2)}) collective-permute-start(bf16[1,64,512]{2,1,0:T(8,128)(2,1)S(1)} %sum_far_share.1), channel_id=1, source_target_pairs={{12,0},{8,4},{4,8},{0,12},{13,1},{9,5},{5,9},{1,13},{14,2},{10,6},... | collective-permute-start | bytes 196616 | tf_op jit(solution)/shard_map/ppermute | solution.py:216
  20.7 6.0 %collective-permute-start.7 = (bf16[1,64,512]{2,1,0:T(8,128)(2,1)S(1)}, bf16[1,64,512]{2,1,0:T(8,128)(2,1)S(1)}, u32[]{:S(2)}, u32[]{:S(2)}) collective-permute-start(bf16[1,64,512]{2,1,0:T(8,128)(2,1)S(1)} %sum_first_sigma.1.refs_3_), channel_id=1, source_target_pairs={{8,0},{12,4},{0,8},{4,12},{9,1},{13,5},{1,9},{5,13},{10,2},{14,6},... | collective-permute-start | bytes 196616 | tf_op jit(solution)/shard_map/ppermute | solution.py:216
  22.2 7.5 %collective-permute-start.9 = (bf16[1,64,512]{2,1,0:T(8,128)(2,1)S(1)}, bf16[1,64,512]{2,1,0:T(8,128)(2,1)S(1)}, u32[]{:S(2)}, u32[]{:S(2)}) collective-permute-start(bf16[1,64,512]{2,1,0:T(8,128)(2,1)S(1)} %sum_first_sigma.1.refs_3_), channel_id=1, source_target_pairs={{4,0},{0,4},{12,8},{8,12},{5,1},{1,5},{13,9},{9,13},{6,2},{2,6},{1... | collective-permute-start | bytes 196616 | tf_op jit(solution)/shard_map/ppermute | solution.py:216
  25.2 5.4 %collective-permute-start.10 = (bf16[1,64,512]{2,1,0:T(8,128)(2,1)S(1)}, bf16[1,64,512]{2,1,0:T(8,128)(2,1)S(1)}, u32[]{:S(2)}, u32[]{:S(2)}) collective-permute-start(bf16[1,64,512]{2,1,0:T(8,128)(2,1)S(1)} %sum_first_sigma.1.refs_3_), channel_id=1, source_target_pairs={{6,0},{4,2},{2,4},{0,6},{14,8},{12,10},{10,12},{8,14},{7,1},{5,3},... | collective-permute-start | bytes 196616 | tf_op jit(solution)/shard_map/ppermute | solution.py:216
  25.4 6.0 %collective-permute-start.11 = (bf16[1,64,512]{2,1,0:T(8,128)(2,1)S(1)}, bf16[1,64,512]{2,1,0:T(8,128)(2,1)S(1)}, u32[]{:S(2)}, u32[]{:S(2)}) collective-permute-start(bf16[1,64,512]{2,1,0:T(8,128)(2,1)S(1)} %sum_first_sigma.1.refs_3_), channel_id=1, source_target_pairs={{2,0},{0,2},{3,1},{1,3},{6,4},{4,6},{7,5},{5,7},{10,8},{8,10},{11,... | collective-permute-start | bytes 196616 | tf_op jit(solution)/shard_map/ppermute | solution.py:216
  26.7 4.8 %collective-permute-start.8 = (bf16[1,64,512]{2,1,0:T(8,128)(2,1)S(1)}, bf16[1,64,512]{2,1,0:T(8,128)(2,1)S(1)}, u32[]{:S(2)}, u32[]{:S(2)}) collective-permute-start(bf16[1,64,512]{2,1,0:T(8,128)(2,1)S(1)} %collective-permute-done.7.refs_1_), channel_id=1, source_target_pairs={{4,0},{0,4},{12,8},{8,12},{5,1},{1,5},{13,9},{9,13},{6,2},{2,6},{1... | collective-permute-start | bytes 196616 | tf_op jit(solution)/shard_map/ppermute | solution.py:216
  28.7 5.2 %collective-permute-start.14 = (bf16[1,64,512]{2,1,0:T(8,128)(2,1)S(1)}, bf16[1,64,512]{2,1,0:T(8,128)(2,1)S(1)}, u32[]{:S(2)}, u32[]{:S(2)}) collective-permute-start(bf16[1,64,512]{2,1,0:T(8,128)(2,1)S(1)} %collective-permute-done.7.refs_1_), channel_id=1, source_target_pairs={{6,0},{4,2},{2,4},{0,6},{14,8},{12,10},{10,12},{8,14},{7,1},{5,3},... | collective-permute-start | bytes 196616 | tf_op jit(solution)/shard_map/ppermute | solution.py:216
  29.7 4.9 %collective-permute-start.15 = (bf16[1,64,512]{2,1,0:T(8,128)(2,1)S(1)}, bf16[1,64,512]{2,1,0:T(8,128)(2,1)S(1)}, u32[]{:S(2)}, u32[]{:S(2)}) collective-permute-start(bf16[1,64,512]{2,1,0:T(8,128)(2,1)S(1)} %collective-permute-done.7.refs_1_), channel_id=1, source_target_pairs={{2,0},{0,2},{3,1},{1,3},{6,4},{4,6},{7,5},{5,7},{10,8},{8,10},{11,... | collective-permute-start | bytes 196616 | tf_op jit(solution)/shard_map/ppermute | solution.py:216
  31.5 3.2 %collective-permute-start.12 = (bf16[1,256,512]{2,1,0:T(8,128)(2,1)S(1)}, bf16[1,256,512]{2,1,0:T(8,128)(2,1)S(1)}, u32[]{:S(2)}, u32[]{:S(2)}) collective-permute-start(bf16[1,256,512]{2,1,0:T(8,128)(2,1)S(1)} %place_own_sector.1.sigma_own.own), channel_id=1, source_target_pairs={{1,0},{0,1},{3,2},{2,3},{5,4},{4,5},{7,6},{6,7},{9,8},{8,9},{11,10... | collective-permute-start | bytes 786440 | tf_op jit(solution)/shard_map/ppermute | solution.py:216
  34.6 1.6 %collective-permute-start.16 = (bf16[1,256,512]{2,1,0:T(8,128)(2,1)S(1)}, bf16[1,256,512]{2,1,0:T(8,128)(2,1)S(1)}, u32[]{:S(2)}, u32[]{:S(2)}) collective-permute-start(bf16[1,256,512]{2,1,0:T(8,128)(2,1)S(1)} %place_other_sectors.1.across_own), channel_id=1, source_target_pairs={{1,0},{0,1},{3,2},{2,3},{5,4},{4,5},{7,6},{6,7},{9,8},{8,9},{11,10... | collective-permute-start | bytes 786440 | tf_op jit(solution)/shard_map/ppermute | solution.py:216
  38.1 8.7 %collective-permute-start.17 = (bf16[1,64,512]{2,1,0:T(8,128)(2,1)S(1)}, bf16[1,64,512]{2,1,0:T(8,128)(2,1)S(1)}, u32[]{:S(2)}, u32[]{:S(2)}) collective-permute-start(bf16[1,64,512]{2,1,0:T(8,128)(2,1)S(1)} %get-tuple-element.37), channel_id=1, source_target_pairs={{12,0},{8,4},{4,8},{0,12},{13,1},{9,5},{5,9},{1,13},{14,2},{10,6},... | collective-permute-start | bytes 196616 | tf_op jit(solution)/shard_map/ppermute | solution.py:216
  40.0 6.9 %collective-permute-start.18 = (bf16[1,64,512]{2,1,0:T(8,128)(2,1)S(1)}, bf16[1,64,512]{2,1,0:T(8,128)(2,1)S(1)}, u32[]{:S(2)}, u32[]{:S(2)}) collective-permute-start(bf16[1,64,512]{2,1,0:T(8,128)(2,1)S(1)} %get-tuple-element.38), channel_id=1, source_target_pairs={{8,0},{12,4},{0,8},{4,12},{9,1},{13,5},{1,9},{5,13},{10,2},{14,6},... | collective-permute-start | bytes 196616 | tf_op jit(solution)/shard_map/ppermute | solution.py:216
  40.2 6.6 %collective-permute-start.19 = (bf16[1,64,512]{2,1,0:T(8,128)(2,1)S(1)}, bf16[1,64,512]{2,1,0:T(8,128)(2,1)S(1)}, u32[]{:S(2)}, u32[]{:S(2)}) collective-permute-start(bf16[1,64,512]{2,1,0:T(8,128)(2,1)S(1)} %get-tuple-element.39), channel_id=1, source_target_pairs={{4,0},{0,4},{12,8},{8,12},{5,1},{1,5},{13,9},{9,13},{6,2},{2,6},{1... | collective-permute-start | bytes 196616 | tf_op jit(solution)/shard_map/ppermute | solution.py:216
  43.0 3.8 %collective-permute-start.13 = (f32[3,8,128]{2,1,0:T(8,128)S(1)}, f32[3,8,128]{2,1,0:T(8,128)S(1)}, u32[]{:S(2)}, u32[]{:S(2)}) collective-permute-start(f32[3,8,128]{2,1,0:T(8,128)S(1)} %sums_for_rayleigh.1.refs_0_.refs_4_), channel_id=1, source_target_pairs={{2,0},{0,2},{3,1},{1,3},{6,4},{4,6},{7,5},{5,7},{10,8},{8,10},{11,... | collective-permute-start | bytes 36872 | tf_op jit(solution)/shard_map/ppermute | solution.py:216
  46.9 6.9 %collective-permute-start.20 = (bf16[1,64,512]{2,1,0:T(8,128)(2,1)S(1)}, bf16[1,64,512]{2,1,0:T(8,128)(2,1)S(1)}, u32[]{:S(2)}, u32[]{:S(2)}) collective-permute-start(bf16[1,64,512]{2,1,0:T(8,128)(2,1)S(1)} %sum_second_sigma.1.refs_3_), channel_id=1, source_target_pairs={{12,0},{8,4},{4,8},{0,12},{13,1},{9,5},{5,9},{1,13},{14,2},{10,6},... | collective-permute-start | bytes 196616 | tf_op jit(solution)/shard_map/ppermute | solution.py:216
  48.9 6.8 %collective-permute-start.21 = (bf16[1,64,512]{2,1,0:T(8,128)(2,1)S(1)}, bf16[1,64,512]{2,1,0:T(8,128)(2,1)S(1)}, u32[]{:S(2)}, u32[]{:S(2)}) collective-permute-start(bf16[1,64,512]{2,1,0:T(8,128)(2,1)S(1)} %sum_second_sigma.1.refs_3_), channel_id=1, source_target_pairs={{8,0},{12,4},{0,8},{4,12},{9,1},{13,5},{1,9},{5,13},{10,2},{14,6},... | collective-permute-start | bytes 196616 | tf_op jit(solution)/shard_map/ppermute | solution.py:216
  48.9 6.8 %collective-permute-start.22 = (bf16[1,64,512]{2,1,0:T(8,128)(2,1)S(1)}, bf16[1,64,512]{2,1,0:T(8,128)(2,1)S(1)}, u32[]{:S(2)}, u32[]{:S(2)}) collective-permute-start(bf16[1,64,512]{2,1,0:T(8,128)(2,1)S(1)} %sum_second_sigma.1.refs_3_), channel_id=1, source_target_pairs={{4,0},{0,4},{12,8},{8,12},{5,1},{1,5},{13,9},{9,13},{6,2},{2,6},{1... | collective-permute-start | bytes 196616 | tf_op jit(solution)/shard_map/ppermute | solution.py:216

commit v11 on v10

--- a/solution.py
+++ b/solution.py
@@ -75,17 +75,19 @@
     own[...] = masked(wave[0], live)
     live = live_cells(sizes_ref, sector, (core ^ 1) * rows, rows, columns)
     other[...] = masked(arrived[0], live)
-    totals = [None] * sectors
     products = left_times((left_own, left_other), (own[...], other[...]))
+    total = None
     for term in range(right.shape[0]):
-        product = times_right(products[term], right, term)
-        for step in range(sectors):
-            weight = mixing_scalar(pairs_ref, weights_ref, term, sector ^ step, sector)
-            part = weight * product
-            totals[step] = part if totals[step] is None else totals[step] + part
+        scaled = [
+            mixing_scalar(pairs_ref, weights_ref, term, sector ^ step, sector) * products[term]
+            for step in range(sectors)
+        ]
+        stacked = jnp.concatenate([part.astype(jnp.bfloat16) for part in scaled], axis=0)
+        part = times_right(stacked, right, term)
+        total = part if total is None else total + part
     for step in range(sectors):
         live = live_cells(sizes_ref, sector ^ step, core * rows, rows, columns)
-        held[step] = jnp.where(live, totals[step], 0.0)
+        held[step] = jnp.where(live, total[step * rows : (step + 1) * rows], 0.0)
     for (steps, across), out in zip(shares, parts):
         for index, along in enumerate(steps):
             start = pl.multiple_of((place ^ along) * share, share)
@@ -114,27 +116,35 @@
         across_out[step] = left_times((left_own,), (across_own[step],))
 
 
-def second_kernel(
-    sizes_ref, pairs_ref, weights_ref, left_other, right, products, across_products, other, *refs
-):
+def tables_kernel(sizes_ref, pairs_ref, weights_ref, _, mixing, live):
+    target = lax.axis_index("sec")
+    for term in range(mixing.shape[0]):
+        for step in range(mixing.shape[1]):
+            weight = mixing_scalar(pairs_ref, weights_ref, term, target, target ^ step)
+            mixing[term, step] = jnp.full(mixing.shape[2:], weight, jnp.float32)
+    rows, columns = live.shape
+    cells = live_cells(sizes_ref, target, lax.axis_index("rep") * rows, rows, columns)
+    live[...] = jnp.where(cells, 1.0, 0.0)
+
+
+def second_kernel(mixing, live, left_other, right, products, across_products, other, *refs):
     shares, held = refs[:-1], refs[-1]
     rows, columns = products.shape[1:]
     share = shares[0].shape[1]
-    target = lax.axis_index("sec")
-    core = lax.axis_index("rep")
     place = lax.axis_index("ops")
     total = None
     across = [left_times((left_other,), (other[step],)) for step in range(other.shape[0])]
     for term in range(right.shape[0]):
-        weight = mixing_scalar(pairs_ref, weights_ref, term, target, target)
-        combined = weight * products[term]
-        for step, part in enumerate(across, 1):
-            weight = mixing_scalar(pairs_ref, weights_ref, term, target, target ^ step)
-            combined = combined + weight * (across_products[step - 1, term] + part[term])
+        weights = [
+            jnp.broadcast_to(mixing[term, step][:1, :1], (rows, columns))
+            for step in range(len(across) + 1)
+        ]
+        combined = weights[0] * products[term]
+        for step, part in enumerate(across):
+            combined = combined + weights[step + 1] * (across_products[step, term] + part[term])
         part = times_right(combined, right, term)
         total = part if total is None else total + part
-    live = live_cells(sizes_ref, target, core * rows, rows, columns)
-    held[...] = jnp.where(live, total, 0.0)
+    held[...] = total * live[...]
     for step, out in enumerate(shares):
         start = pl.multiple_of((place ^ step) * share, share)
         out[0] = held[pl.ds(start, share), :].astype(out.dtype)
@@ -294,6 +304,14 @@
         scratch=[pltpu.VMEM((sectors, rows, columns), f32)],
     )
     rest = dict(zip(spots, rest))
+    mixing, live = call(
+        tables_kernel,
+        "tables_for_second_sigma",
+        [shape(terms, sectors, 8, 128, dtype=f32), shape(rows, columns, dtype=f32)],
+        [smem] * 3,
+        *scalars,
+        wave_own,
+    )
     met = [partner(rest[(far, 0), across], {"sec": across}) for across in range(sectors)]
     received = [partner(summed("sum_far_share", *met), {"ops": far})]
     received += [
@@ -301,31 +319,29 @@
         for along in direct
         for across in range(sectors)
     ]
-    first_share = summed("sum_first_sigma", *[(piece, 1) for piece in met], *received)
-    crossed = {
-        along: partner(first_share, {"ops": along}) for along in farthest_first if along % 2 == 0
-    }
-    pieces = {
-        (along, across): partner(crossed[along // 2 * 2], {"ops": along % 2, "sec": across})
-        for along in farthest_first
-        for across in range(sectors)
-    }
+    first_share = summed("sum_first_sigma", *[(piece, 1) for piece in met], *received, after=(mixing,))
+    along_ops = {along: partner(first_share, {"ops": along}) for along in farthest_first}
     sigma_own = call(
         lambda *refs: place_kernel([(along, 0) for along in farthest_first], *refs),
         "place_own_sector",
         shape(1, rows, columns),
         [],
-        *[pieces[along, 0] for along in farthest_first],
-        *[pieces[spot] for spot in pieces if spot[0] < 2 and spot[1]],
+        *along_ops.values(),
     )
     sigma_other = partner(sigma_own, {"rep": 1})
     spots = [(along, across) for along in farthest_first for across in range(1, sectors)]
+    pieces = [
+        partner(first_share, {"ops": along, "sec": across})
+        if along < 2
+        else partner(along_ops[along], {"sec": across})
+        for along, across in spots
+    ]
     across_own = call(
         lambda *refs: place_kernel([(along, across - 1) for along, across in spots], *refs),
         "place_other_sectors",
         shape(sectors - 1, rows, columns),
         [],
-        *[pieces[spot] for spot in spots],
+        *pieces,
     )
     across_other = partner(across_own, {"rep": 1})
 
@@ -347,8 +363,9 @@
         second_kernel,
         "second_sigma_terms",
         [shape(1, share, columns, dtype=f32)] + [shape(1, share, columns)] * (ops_count - 1),
-        [smem] * 3,
-        *scalars,
+        [],
+        mixing,
+        live,
         left_other,
         right,
         products,

time: 56.6 us -> 56 us (0.989)
  waiting for transfers between devices: 13.9 us -> 12.7 us
    ppermute x23, waiting for transfers between devices: 13.9 us -> 12.7 us  [partner(): return lax.ppermute(value, axes, pairs)]
    pallas_call x12 -> x13, Pallas kernels: 9.98 us -> 10.4 us  [call(): pl.pallas_call(kernel, out_shape=out_shape, in_specs=list(in_specs) + [in...]
  transfers between devices with their start and end apart: 23 -> 23, of which waited for: 11 -> 12; matrix products, arithmetic and copies ran while one was open for 0% -> 0% of each run, Pallas kernels for 9% -> 10%
where the time goes in v11:
time: 56 us; the launch traced here: 55.8 us
  starting transfers between devices  31.8 us (57%)
  waiting for transfers between devices  12.7 us (23%)
  Pallas kernels  10.4 us (19%)
  between operations  0.82 us (1%)
    ppermute x23, starting transfers between devices, partner(): return lax.ppermute(value, axes, pairs)  31.8 us
    ppermute x23, waiting for transfers between devices, partner(): return lax.ppermute(value, axes, pairs)  12.7 us
    pallas_call x13, Pallas kernels, call(): pl.pallas_call(kernel, out_shape=out_shape, in_specs=list(in_specs) + [in...  10.4 us
  transfers between devices with their start and end apart: 23, of which 12 were waited for; matrix products, arithmetic and copies ran while one was open for 0% of the time, Pallas kernels for 10%

profile of v11, /device:TPU:0, one launch (start us, length us, event | category | flops | bytes accessed | tf_op | source)
XLA Modules:
  0.0 55.8 jit_solution(13900475313820846743)
XLA Ops:
  0.6 0.0 copy-start
  0.6 0.0 copy-start.2
  0.7 0.0 copy-start.1
  0.7 0.0 copy-start.3
  0.7 0.5 collective-permute-start
  1.2 2.0 %load_operators.1 = (bf16[4,256,256]{2,1,0:T(8,128)(2,1)S(1)}, bf16[4,256,256]{2,1,0:T(8,128)(2,1)S(1)}, bf16[4,512,512]{2,1,0:T(8,128)(2,1)S(1)}) custom-call(bf16[4,512,512]{2,1,0:T(8,128)(2,1)} %left_ref.1, bf16[4,512,512]{2,1,0:T(8,128)(2,1)} %right_ref.1), custom_call_target="tpu_custom_call" | custom-call | tf_op jit(solution)/shard_map/load_operators/pallas_call | solution.py:244
  3.2 0.0 collective-permute-done.refs_7_
  3.2 0.0 copy-done
  3.2 0.0 copy-done.2
  3.2 0.0 copy-done.1
  3.2 0.0 copy-done.3
  3.2 2.6 %first_sigma_terms.1 = (bf16[256,512]{1,0:T(8,128)(2,1)S(1)}, bf16[256,512]{1,0:T(8,128)(2,1)S(1)}, f32[2,64,512]{2,1,0:T(8,128)S(1)}, bf16[2,64,512]{2,1,0:T(8,...) custom-call(s32[2,2]{1,0:T(2,128)S(1)} %copy-done.2, ...), custom_call_target="tpu_custom_call" | custom-call | tf_op jit(solution)/shard_map/first_sigma_terms/pallas_call | solution.py:244
  5.8 2.6 %collective-permute-start.1 = (bf16[2,64,512]{2,1,0:T(8,128)(2,1)S(1)}, bf16[2,64,512]{2,1,0:T(8,128)(2,1)S(1)}, u32[]{:S(2)}, u32[]{:S(2)}) collective-permute-start(bf16[2,64,512]{2,1,0:T(8,128)(2,1)S(1)} %get-tuple-element.28), channel_id=1, source_target_pairs={{2,0},{0,2},{3,1},{1,3},{6,4},{4,6},{7,5},{5,7},{10,8},{8,10},{11,... | collective-permute-start | bytes 393224 | tf_op jit(solution)/shard_map/ppermute | solution.py:226
  8.4 2.6 %collective-permute-start.3 = (bf16[1,64,512]{2,1,0:T(8,128)(2,1)S(1)}, bf16[1,64,512]{2,1,0:T(8,128)(2,1)S(1)}, u32[]{:S(2)}, u32[]{:S(2)}) collective-permute-start(bf16[1,64,512]{2,1,0:T(8,128)(2,1)S(1)} %get-tuple-element.29), channel_id=1, source_target_pairs={{8,0},{12,4},{0,8},{4,12},{9,1},{13,5},{1,9},{5,13},{10,2},{14,6},... | collective-permute-start | bytes 196616 | tf_op jit(solution)/shard_map/ppermute | solution.py:226
  11.0 0.0 collective-permute-start.4
  11.0 1.9 %collective-permute-start.5 = (bf16[1,64,512]{2,1,0:T(8,128)(2,1)S(1)}, bf16[1,64,512]{2,1,0:T(8,128)(2,1)S(1)}, u32[]{:S(2)}, u32[]{:S(2)}) collective-permute-start(bf16[1,64,512]{2,1,0:T(8,128)(2,1)S(1)} %get-tuple-element.31), channel_id=1, source_target_pairs={{4,0},{0,4},{12,8},{8,12},{5,1},{1,5},{13,9},{9,13},{6,2},{2,6},{1... | collective-permute-start | bytes 196616 | tf_op jit(solution)/shard_map/ppermute | solution.py:226
  12.9 1.4 %collective-permute-start.6 = (bf16[1,64,512]{2,1,0:T(8,128)(2,1)S(1)}, bf16[1,64,512]{2,1,0:T(8,128)(2,1)S(1)}, u32[]{:S(2)}, u32[]{:S(2)}) collective-permute-start(bf16[1,64,512]{2,1,0:T(8,128)(2,1)S(1)} %get-tuple-element.32), channel_id=1, source_target_pairs={{6,0},{4,2},{2,4},{0,6},{14,8},{12,10},{10,12},{8,14},{7,1},{5,3},... | collective-permute-start | bytes 196616 | tf_op jit(solution)/shard_map/ppermute | solution.py:226
  14.2 0.0 collective-permute-done.1.refs_1_
  14.3 3.7 %collective-permute-start.2 = (bf16[1,64,512]{2,1,0:T(8,128)(2,1)S(1)}, bf16[1,64,512]{2,1,0:T(8,128)(2,1)S(1)}, u32[]{:S(2)}, u32[]{:S(2)}) collective-permute-start(bf16[1,64,512]{2,1,0:T(8,128)(2,1)S(1)} %sum_far_share.1), channel_id=1, source_target_pairs={{12,0},{8,4},{4,8},{0,12},{13,1},{9,5},{5,9},{1,13},{14,2},{10,6},... | collective-permute-start | bytes 196616 | tf_op jit(solution)/shard_map/ppermute | solution.py:226
  17.9 0.8 %tables_for_second_sigma.1 = (f32[4,2,8,128]{3,2,1,0:T(8,128)S(1)}, f32[256,512]{1,0:T(8,128)S(1)}) custom-call(s32[2,2]{1,0:T(2,128)S(1)} %copy-done.2, s32[4,2,8]{2,1,0:T(2,128)S(1)} %bitcast.2, f32[4,8]{1,0:T(4,128)S(1)} %copy-done.3, bf16[256,512]{1,0:T(8,128)(2,1)S(1)} %get-tuple-element.26._.wave_own), custom_call_target="tpu_custom_call" | custom-call | tf_op jit(solution)/shard_map/tables_for_second_sigma/pallas_call | solution.py:244
  18.7 0.0 collective-permute-done.3.refs_3_
  18.8 0.3 collective-permute-done.4.refs_4_
  19.0 0.0 collective-permute-done.5.refs_5_
  19.0 0.0 collective-permute-done.6.refs_6_
  19.0 2.0 %collective-permute-done.2.refs_2_ = bf16[1,64,512]{2,1,0:T(8,128)(2,1)S(1)} collective-permute-done((bf16[1,64,512]{2,1,0:T(8,128)(2,1)S(1)}, bf16[1,64,512]{2,1,0:T(8,128)(2,1)S(1)}, u32[]{:S(2)}, u32[]{:S(2)}) %collective-permute-start.2) | collective-permute-done | bytes 65568 | tf_op jit(solution)/shard_map/ppermute | solution.py:226
  21.0 0.1 sum_first_sigma.1.refs_3_
  21.1 4.0 %collective-permute-start.7 = (bf16[1,64,512]{2,1,0:T(8,128)(2,1)S(1)}, bf16[1,64,512]{2,1,0:T(8,128)(2,1)S(1)}, u32[]{:S(2)}, u32[]{:S(2)}) collective-permute-start(bf16[1,64,512]{2,1,0:T(8,128)(2,1)S(1)} %sum_first_sigma.1.refs_3_), channel_id=1, source_target_pairs={{12,0},{8,4},{4,8},{0,12},{13,1},{9,5},{5,9},{1,13},{14,2},{10,6},... | collective-permute-start | bytes 196616 | tf_op jit(solution)/shard_map/ppermute | solution.py:226
  25.0 0.0 collective-permute-start.8
  25.1 0.6 %collective-permute-start.9 = (bf16[1,64,512]{2,1,0:T(8,128)(2,1)S(1)}, bf16[1,64,512]{2,1,0:T(8,128)(2,1)S(1)}, u32[]{:S(2)}, u32[]{:S(2)}) collective-permute-start(bf16[1,64,512]{2,1,0:T(8,128)(2,1)S(1)} %sum_first_sigma.1.refs_3_), channel_id=1, source_target_pairs={{4,0},{0,4},{12,8},{8,12},{5,1},{1,5},{13,9},{9,13},{6,2},{2,6},{1... | collective-permute-start | bytes 196616 | tf_op jit(solution)/shard_map/ppermute | solution.py:226
  25.7 1.6 %collective-permute-start.14 = (bf16[1,64,512]{2,1,0:T(8,128)(2,1)S(1)}, bf16[1,64,512]{2,1,0:T(8,128)(2,1)S(1)}, u32[]{:S(2)}, u32[]{:S(2)}) collective-permute-start(bf16[1,64,512]{2,1,0:T(8,128)(2,1)S(1)} %sum_first_sigma.1.refs_3_), channel_id=1, source_target_pairs={{6,0},{4,2},{2,4},{0,6},{14,8},{12,10},{10,12},{8,14},{7,1},{5,3},... | collective-permute-start | bytes 196616 | tf_op jit(solution)/shard_map/ppermute | solution.py:226
  27.3 1.2 %collective-permute-start.15 = (bf16[1,64,512]{2,1,0:T(8,128)(2,1)S(1)}, bf16[1,64,512]{2,1,0:T(8,128)(2,1)S(1)}, u32[]{:S(2)}, u32[]{:S(2)}) collective-permute-start(bf16[1,64,512]{2,1,0:T(8,128)(2,1)S(1)} %sum_first_sigma.1.refs_3_), channel_id=1, source_target_pairs={{2,0},{0,2},{3,1},{1,3},{6,4},{4,6},{7,5},{5,7},{10,8},{8,10},{11,... | collective-permute-start | bytes 196616 | tf_op jit(solution)/shard_map/ppermute | solution.py:226
  28.5 0.0 collective-permute-done.7.refs_0_
  28.5 0.8 %collective-permute-start.12 = (bf16[1,64,512]{2,1,0:T(8,128)(2,1)S(1)}, bf16[1,64,512]{2,1,0:T(8,128)(2,1)S(1)}, u32[]{:S(2)}, u32[]{:S(2)}) collective-permute-start(bf16[1,64,512]{2,1,0:T(8,128)(2,1)S(1)} %collective-permute-done.7.refs_0_), channel_id=1, source_target_pairs={{2,0},{0,2},{3,1},{1,3},{6,4},{4,6},{7,5},{5,7},{10,8},{8,10},{11,... | collective-permute-start | bytes 196616 | tf_op jit(solution)/shard_map/ppermute | solution.py:226
  29.3 1.0 %collective-permute-done.8.refs_1_ = bf16[1,64,512]{2,1,0:T(8,128)(2,1)S(1)} collective-permute-done((bf16[1,64,512]{2,1,0:T(8,128)(2,1)S(1)}, bf16[1,64,512]{2,1,0:T(8,128)(2,1)S(1)}, u32[]{:S(2)}, u32[]{:S(2)}) %collective-permute-start.8) | collective-permute-done | bytes 65568 | tf_op jit(solution)/shard_map/ppermute | solution.py:226
  30.3 0.8 %collective-permute-start.13 = (bf16[1,64,512]{2,1,0:T(8,128)(2,1)S(1)}, bf16[1,64,512]{2,1,0:T(8,128)(2,1)S(1)}, u32[]{:S(2)}, u32[]{:S(2)}) collective-permute-start(bf16[1,64,512]{2,1,0:T(8,128)(2,1)S(1)} %collective-permute-done.8.refs_1_), channel_id=1, source_target_pairs={{2,0},{0,2},{3,1},{1,3},{6,4},{4,6},{7,5},{5,7},{10,8},{8,10},{11,... | collective-permute-start | bytes 196616 | tf_op jit(solution)/shard_map/ppermute | solution.py:226
  31.1 0.0 collective-permute-done.9.refs_2_
  31.1 0.1 collective-permute-start.10
  31.2 0.1 collective-permute-done.14.refs_2_
  31.3 1.3 %collective-permute-done.15.refs_3_ = bf16[1,64,512]{2,1,0:T(8,128)(2,1)S(1)} collective-permute-done((bf16[1,64,512]{2,1,0:T(8,128)(2,1)S(1)}, bf16[1,64,512]{2,1,0:T(8,128)(2,1)S(1)}, u32[]{:S(2)}, u32[]{:S(2)}) %collective-permute-start.15) | collective-permute-done | bytes 65568 | tf_op jit(solution)/shard_map/ppermute | solution.py:226
  32.7 0.7 %collective-permute-done.12.refs_0_ = bf16[1,64,512]{2,1,0:T(8,128)(2,1)S(1)} collective-permute-done((bf16[1,64,512]{2,1,0:T(8,128)(2,1)S(1)}, bf16[1,64,512]{2,1,0:T(8,128)(2,1)S(1)}, u32[]{:S(2)}, u32[]{:S(2)}) %collective-permute-start.12) | collective-permute-done | bytes 65568 | tf_op jit(solution)/shard_map/ppermute | solution.py:226
  33.4 1.2 %collective-permute-done.13.refs_1_ = bf16[1,64,512]{2,1,0:T(8,128)(2,1)S(1)} collective-permute-done((bf16[1,64,512]{2,1,0:T(8,128)(2,1)S(1)}, bf16[1,64,512]{2,1,0:T(8,128)(2,1)S(1)}, u32[]{:S(2)}, u32[]{:S(2)}) %collective-permute-start.13) | collective-permute-done | bytes 65568 | tf_op jit(solution)/shard_map/ppermute | solution.py:226
  34.6 0.1 collective-permute-start.16
  34.7 0.0 collective-permute-done.10.sigma_other.other
  34.7 1.0 %left_products.1 = (f32[4,256,512]{2,1,0:T(8,128)S(1)}, f32[1,4,256,512]{3,2,1,0:T(8,128)S(1)}) custom-call(bf16[4,256,256]{2,1,0:T(8,128)(2,1)S(1)} %get-tuple-element.23.refs_3_.left_own, bf16[4,256,256]{2,1,0:T(8,128)(2,1)S(1)} %get-tuple-element.24.refs_4_.left_other, bf16[1,256,512]{2,1,0:T(8,128)(2,1)S(1)} %place_own_sector.1.sigma_own.own, ...), custom_call_target="tpu_custom_call" | custom-call | tf_op jit(solution)/shard_map/left_products/pallas_call | solution.py:244
  35.7 0.5 collective-permute-done.16.other
  36.2 1.1 %second_sigma_terms.1 = (f32[1,64,512]{2,1,0:T(8,128)S(1)}, bf16[1,64,512]{2,1,0:T(8,128)(2,1)S(1)}, bf16[1,64,512]{2,1,0:T(8,128)(2,1)S(1)}, bf16[1,64,512]{2,1,0:T(8,128)(2,1)S(1)}) custom-call(f32[4,2,8,128]{3,2,1,0:T(8,128)S(1)} %get-tuple-element.33.refs_7_.mixing, f32[256,512]{1,0:T(8,128)S(1)} %get-tuple-element.37.live, ...), custom_call_target="tpu_custom_call" | custom-call | tf_op jit(solution)/shard_map/second_sigma_terms/pallas_call | solution.py:244
  37.3 2.4 %collective-permute-start.17 = (bf16[1,64,512]{2,1,0:T(8,128)(2,1)S(1)}, bf16[1,64,512]{2,1,0:T(8,128)(2,1)S(1)}, u32[]{:S(2)}, u32[]{:S(2)}) collective-permute-start(bf16[1,64,512]{2,1,0:T(8,128)(2,1)S(1)} %get-tuple-element.41), channel_id=1, source_target_pairs={{12,0},{8,4},{4,8},{0,12},{13,1},{9,5},{5,9},{1,13},{14,2},{10,6},... | collective-permute-start | bytes 196616 | tf_op jit(solution)/shard_map/ppermute | solution.py:226
  39.7 0.0 collective-permute-start.18
  39.7 2.1 %collective-permute-start.19 = (bf16[1,64,512]{2,1,0:T(8,128)(2,1)S(1)}, bf16[1,64,512]{2,1,0:T(8,128)(2,1)S(1)}, u32[]{:S(2)}, u32[]{:S(2)}) collective-permute-start(bf16[1,64,512]{2,1,0:T(8,128)(2,1)S(1)} %get-tuple-element.43), channel_id=1, source_target_pairs={{4,0},{0,4},{12,8},{8,12},{5,1},{1,5},{13,9},{9,13},{6,2},{2,6},{1... | collective-permute-start | bytes 196616 | tf_op jit(solution)/shard_map/ppermute | solution.py:226
  41.8 0.5 sums_for_rayleigh.1.refs_0_.refs_4_
  42.3 1.1 %collective-permute-start.11 = (f32[3,8,128]{2,1,0:T(8,128)S(1)}, f32[3,8,128]{2,1,0:T(8,128)S(1)}, u32[]{:S(2)}, u32[]{:S(2)}) collective-permute-start(f32[3,8,128]{2,1,0:T(8,128)S(1)} %sums_for_rayleigh.1.refs_0_.refs_4_), channel_id=1, source_target_pairs={{2,0},{0,2},{3,1},{1,3},{6,4},{4,6},{7,5},{5,7},{10,8},{8,10},{11,... | collective-permute-start | bytes 36872 | tf_op jit(solution)/shard_map/ppermute | solution.py:226
  43.4 2.7 %collective-permute-done.11.refs_1_.refs_5_ = f32[3,8,128]{2,1,0:T(8,128)S(1)} collective-permute-done((f32[3,8,128]{2,1,0:T(8,128)S(1)}, f32[3,8,128]{2,1,0:T(8,128)S(1)}, u32[]{:S(2)}, u32[]{:S(2)}) %collective-permute-start.11) | collective-permute-done | bytes 12320 | tf_op jit(solution)/shard_map/ppermute | solution.py:226
  46.1 0.0 collective-permute-done.17.refs_1_
  46.1 0.2 collective-permute-done.18.refs_2_
  46.2 0.0 collective-permute-done.19.refs_3_
  46.3 2.6 %collective-permute-start.20 = (bf16[1,64,512]{2,1,0:T(8,128)(2,1)S(1)}, bf16[1,64,512]{2,1,0:T(8,128)(2,1)S(1)}, u32[]{:S(2)}, u32[]{:S(2)}) collective-permute-start(bf16[1,64,512]{2,1,0:T(8,128)(2,1)S(1)} %sum_second_sigma.1.refs_3_), channel_id=1, source_target_pairs={{12,0},{8,4},{4,8},{0,12},{13,1},{9,5},{5,9},{1,13},{14,2},{10,6},... | collective-permute-start | bytes 196616 | tf_op jit(solution)/shard_map/ppermute | solution.py:226
  48.8 0.0 collective-permute-start.21
  48.8 1.9 %collective-permute-start.22 = (bf16[1,64,512]{2,1,0:T(8,128)(2,1)S(1)}, bf16[1,64,512]{2,1,0:T(8,128)(2,1)S(1)}, u32[]{:S(2)}, u32[]{:S(2)}) collective-permute-start(bf16[1,64,512]{2,1,0:T(8,128)(2,1)S(1)} %sum_second_sigma.1.refs_3_), channel_id=1, source_target_pairs={{4,0},{0,4},{12,8},{8,12},{5,1},{1,5},{13,9},{9,13},{6,2},{2,6},{1... | collective-permute-start | bytes 196616 | tf_op jit(solution)/shard_map/ppermute | solution.py:226
  50.7 1.4 %second_wave.1 = (bf16[1,256,512]{2,1,0:T(8,128)(2,1)}, f32[2,8,128]{2,1,0:T(8,128)S(1)}) custom-call(s32[2,2]{1,0:T(2,128)S(1)} %copy-done.2, bf16[256,512]{1,0:T(8,128)(2,1)S(1)} %get-tuple-element.26._.wave_own, bf16[1,256,512]{2,1,0:T(8,128)(2,1)S(1)} %place_own_sector.1.sigma_own.own, f32[3,8,128]{2,1,0:T(8,128)S(1)} %sums_for_rayleigh.1.refs_0_.refs_4_, ...), custom_call_target="tpu_custom_call" | custom-call | tf_op jit(solution)/shard_map/second_wave/pallas_call | solution.py:244
  52.2 0.8 %collective-permute-done.20.refs_0_ = bf16[1,64,512]{2,1,0:T(8,128)(2,1)S(1)} collective-permute-done((bf16[1,64,512]{2,1,0:T(8,128)(2,1)S(1)}, bf16[1,64,512]{2,1,0:T(8,128)(2,1)S(1)}, u32[]{:S(2)}, u32[]{:S(2)}) %collective-permute-start.20) | collective-permute-done | bytes 65568 | tf_op jit(solution)/shard_map/ppermute | solution.py:226
  53.0 2.0 %collective-permute-done.21.refs_1_ = bf16[1,64,512]{2,1,0:T(8,128)(2,1)S(1)} collective-permute-done((bf16[1,64,512]{2,1,0:T(8,128)(2,1)S(1)}, bf16[1,64,512]{2,1,0:T(8,128)(2,1)S(1)}, u32[]{:S(2)}, u32[]{:S(2)}) %collective-permute-start.21) | collective-permute-done | bytes 65568 | tf_op jit(solution)/shard_map/ppermute | solution.py:226
  54.9 0.0 collective-permute-done.22.refs_2_
  54.9 0.9 %join_second_sigma.1 = f32[1,256,512]{2,1,0:T(8,128)} custom-call(f32[2,8,128]{2,1,0:T(8,128)S(1)} %get-tuple-element.36.factors, bf16[1,256,512]{2,1,0:T(8,128)(2,1)S(1)} %place_own_sector.1.sigma_own.own, bf16[1,64,512]{2,1,0:T(8,128)(2,1)S(1)} %collective-permute-done.20.refs_0_, bf16[1,64,512]{2,1,0:T(8,128)(2,1)S(1)} %collective-permute-done.21.refs_1_, ...), custom_call_target="tpu_custom_call" | custom-call | tf_op jit(solution)/shard_map/join_second_sigma/pallas_call | solution.py:244
  (4 shorter events, 0.1 us)
Async XLA Ops:
  0.6 2.5 %copy-start = (bf16[1,256,512]{2,1,0:T(8,128)(2,1)S(1)}, bf16[1,256,512]{2,1,0:T(8,128)(2,1)}, u32[]{:S(2)}) copy-start(bf16[1,256,512]{2,1,0:T(8,128)(2,1)} %refs_6_.1) | copy-start | bytes 786436
  0.6 2.5 %copy-start.2 = (s32[2,2]{1,0:T(2,128)S(1)}, s32[2,2]{1,0:T(2,128)}, u32[]{:S(2)}) copy-start(s32[2,2]{1,0:T(2,128)} %sizes_ref.3) | copy-start | bytes 52
  0.7 2.5 %copy-start.1 = (s32[4,8,2]{1,2,0:T(2,128)S(1)}, s32[4,8,2]{1,2,0:T(2,128)}, u32[]{:S(2)}) copy-start(s32[4,8,2]{1,2,0:T(2,128)} %param.10) | copy-start | bytes 772
  0.7 2.5 %copy-start.3 = (f32[4,8]{1,0:T(4,128)S(1)}, f32[4,8]{1,0:T(4,128)}, u32[]{:S(2)}) copy-start(f32[4,8]{1,0:T(4,128)} %weights_ref.1) | copy-start | bytes 388
  0.7 2.5 %collective-permute-start = (bf16[1,256,512]{2,1,0:T(8,128)(2,1)}, bf16[1,256,512]{2,1,0:T(8,128)(2,1)S(1)}, u32[]{:S(2)}, u32[]{:S(2)}) collective-permute-start(bf16[1,256,512]{2,1,0:T(8,128)(2,1)} %refs_6_.1), channel_id=1, source_target_pairs={{1,0},{0,1},{3,2},{2,3},{5,4},{4,5},{7,6},{6,7},{9,8},{8,9},{11,10... | collective-permute-start | bytes 786440 | tf_op jit(solution)/shard_map/ppermute | solution.py:226
  5.8 8.4 %collective-permute-start.1 = (bf16[2,64,512]{2,1,0:T(8,128)(2,1)S(1)}, bf16[2,64,512]{2,1,0:T(8,128)(2,1)S(1)}, u32[]{:S(2)}, u32[]{:S(2)}) collective-permute-start(bf16[2,64,512]{2,1,0:T(8,128)(2,1)S(1)} %get-tuple-element.28), channel_id=1, source_target_pairs={{2,0},{0,2},{3,1},{1,3},{6,4},{4,6},{7,5},{5,7},{10,8},{8,10},{11,... | collective-permute-start | bytes 393224 | tf_op jit(solution)/shard_map/ppermute | solution.py:226
  8.4 10.4 %collective-permute-start.3 = (bf16[1,64,512]{2,1,0:T(8,128)(2,1)S(1)}, bf16[1,64,512]{2,1,0:T(8,128)(2,1)S(1)}, u32[]{:S(2)}, u32[]{:S(2)}) collective-permute-start(bf16[1,64,512]{2,1,0:T(8,128)(2,1)S(1)} %get-tuple-element.29), channel_id=1, source_target_pairs={{8,0},{12,4},{0,8},{4,12},{9,1},{13,5},{1,9},{5,13},{10,2},{14,6},... | collective-permute-start | bytes 196616 | tf_op jit(solution)/shard_map/ppermute | solution.py:226
  11.0 8.0 %collective-permute-start.4 = (bf16[1,64,512]{2,1,0:T(8,128)(2,1)S(1)}, bf16[1,64,512]{2,1,0:T(8,128)(2,1)S(1)}, u32[]{:S(2)}, u32[]{:S(2)}) collective-permute-start(bf16[1,64,512]{2,1,0:T(8,128)(2,1)S(1)} %get-tuple-element.30), channel_id=1, source_target_pairs={{10,0},{8,2},{14,4},{12,6},{2,8},{0,10},{6,12},{4,14},{11,1},{9,3}... | collective-permute-start | bytes 196616 | tf_op jit(solution)/shard_map/ppermute | solution.py:226
  11.0 8.0 %collective-permute-start.5 = (bf16[1,64,512]{2,1,0:T(8,128)(2,1)S(1)}, bf16[1,64,512]{2,1,0:T(8,128)(2,1)S(1)}, u32[]{:S(2)}, u32[]{:S(2)}) collective-permute-start(bf16[1,64,512]{2,1,0:T(8,128)(2,1)S(1)} %get-tuple-element.31), channel_id=1, source_target_pairs={{4,0},{0,4},{12,8},{8,12},{5,1},{1,5},{13,9},{9,13},{6,2},{2,6},{1... | collective-permute-start | bytes 196616 | tf_op jit(solution)/shard_map/ppermute | solution.py:226
  12.9 6.2 %collective-permute-start.6 = (bf16[1,64,512]{2,1,0:T(8,128)(2,1)S(1)}, bf16[1,64,512]{2,1,0:T(8,128)(2,1)S(1)}, u32[]{:S(2)}, u32[]{:S(2)}) collective-permute-start(bf16[1,64,512]{2,1,0:T(8,128)(2,1)S(1)} %get-tuple-element.32), channel_id=1, source_target_pairs={{6,0},{4,2},{2,4},{0,6},{14,8},{12,10},{10,12},{8,14},{7,1},{5,3},... | collective-permute-start | bytes 196616 | tf_op jit(solution)/shard_map/ppermute | solution.py:226
  14.3 6.7 %collective-permute-start.2 = (bf16[1,64,512]{2,1,0:T(8,128)(2,1)S(1)}, bf16[1,64,512]{2,1,0:T(8,128)(2,1)S(1)}, u32[]{:S(2)}, u32[]{:S(2)}) collective-permute-start(bf16[1,64,512]{2,1,0:T(8,128)(2,1)S(1)} %sum_far_share.1), channel_id=1, source_target_pairs={{12,0},{8,4},{4,8},{0,12},{13,1},{9,5},{5,9},{1,13},{14,2},{10,6},... | collective-permute-start | bytes 196616 | tf_op jit(solution)/shard_map/ppermute | solution.py:226
  21.1 7.5 %collective-permute-start.7 = (bf16[1,64,512]{2,1,0:T(8,128)(2,1)S(1)}, bf16[1,64,512]{2,1,0:T(8,128)(2,1)S(1)}, u32[]{:S(2)}, u32[]{:S(2)}) collective-permute-start(bf16[1,64,512]{2,1,0:T(8,128)(2,1)S(1)} %sum_first_sigma.1.refs_3_), channel_id=1, source_target_pairs={{12,0},{8,4},{4,8},{0,12},{13,1},{9,5},{5,9},{1,13},{14,2},{10,6},... | collective-permute-start | bytes 196616 | tf_op jit(solution)/shard_map/ppermute | solution.py:226
  25.0 5.3 %collective-permute-start.8 = (bf16[1,64,512]{2,1,0:T(8,128)(2,1)S(1)}, bf16[1,64,512]{2,1,0:T(8,128)(2,1)S(1)}, u32[]{:S(2)}, u32[]{:S(2)}) collective-permute-start(bf16[1,64,512]{2,1,0:T(8,128)(2,1)S(1)} %sum_first_sigma.1.refs_3_), channel_id=1, source_target_pairs={{8,0},{12,4},{0,8},{4,12},{9,1},{13,5},{1,9},{5,13},{10,2},{14,6},... | collective-permute-start | bytes 196616 | tf_op jit(solution)/shard_map/ppermute | solution.py:226
  25.1 6.1 %collective-permute-start.9 = (bf16[1,64,512]{2,1,0:T(8,128)(2,1)S(1)}, bf16[1,64,512]{2,1,0:T(8,128)(2,1)S(1)}, u32[]{:S(2)}, u32[]{:S(2)}) collective-permute-start(bf16[1,64,512]{2,1,0:T(8,128)(2,1)S(1)} %sum_first_sigma.1.refs_3_), channel_id=1, source_target_pairs={{4,0},{0,4},{12,8},{8,12},{5,1},{1,5},{13,9},{9,13},{6,2},{2,6},{1... | collective-permute-start | bytes 196616 | tf_op jit(solution)/shard_map/ppermute | solution.py:226
  25.7 5.6 %collective-permute-start.14 = (bf16[1,64,512]{2,1,0:T(8,128)(2,1)S(1)}, bf16[1,64,512]{2,1,0:T(8,128)(2,1)S(1)}, u32[]{:S(2)}, u32[]{:S(2)}) collective-permute-start(bf16[1,64,512]{2,1,0:T(8,128)(2,1)S(1)} %sum_first_sigma.1.refs_3_), channel_id=1, source_target_pairs={{6,0},{4,2},{2,4},{0,6},{14,8},{12,10},{10,12},{8,14},{7,1},{5,3},... | collective-permute-start | bytes 196616 | tf_op jit(solution)/shard_map/ppermute | solution.py:226
  27.3 5.4 %collective-permute-start.15 = (bf16[1,64,512]{2,1,0:T(8,128)(2,1)S(1)}, bf16[1,64,512]{2,1,0:T(8,128)(2,1)S(1)}, u32[]{:S(2)}, u32[]{:S(2)}) collective-permute-start(bf16[1,64,512]{2,1,0:T(8,128)(2,1)S(1)} %sum_first_sigma.1.refs_3_), channel_id=1, source_target_pairs={{2,0},{0,2},{3,1},{1,3},{6,4},{4,6},{7,5},{5,7},{10,8},{8,10},{11,... | collective-permute-start | bytes 196616 | tf_op jit(solution)/shard_map/ppermute | solution.py:226
  28.5 4.9 %collective-permute-start.12 = (bf16[1,64,512]{2,1,0:T(8,128)(2,1)S(1)}, bf16[1,64,512]{2,1,0:T(8,128)(2,1)S(1)}, u32[]{:S(2)}, u32[]{:S(2)}) collective-permute-start(bf16[1,64,512]{2,1,0:T(8,128)(2,1)S(1)} %collective-permute-done.7.refs_0_), channel_id=1, source_target_pairs={{2,0},{0,2},{3,1},{1,3},{6,4},{4,6},{7,5},{5,7},{10,8},{8,10},{11,... | collective-permute-start | bytes 196616 | tf_op jit(solution)/shard_map/ppermute | solution.py:226
  30.3 4.3 %collective-permute-start.13 = (bf16[1,64,512]{2,1,0:T(8,128)(2,1)S(1)}, bf16[1,64,512]{2,1,0:T(8,128)(2,1)S(1)}, u32[]{:S(2)}, u32[]{:S(2)}) collective-permute-start(bf16[1,64,512]{2,1,0:T(8,128)(2,1)S(1)} %collective-permute-done.8.refs_1_), channel_id=1, source_target_pairs={{2,0},{0,2},{3,1},{1,3},{6,4},{4,6},{7,5},{5,7},{10,8},{8,10},{11,... | collective-permute-start | bytes 196616 | tf_op jit(solution)/shard_map/ppermute | solution.py:226
  31.1 3.5 %collective-permute-start.10 = (bf16[1,256,512]{2,1,0:T(8,128)(2,1)S(1)}, bf16[1,256,512]{2,1,0:T(8,128)(2,1)S(1)}, u32[]{:S(2)}, u32[]{:S(2)}) collective-permute-start(bf16[1,256,512]{2,1,0:T(8,128)(2,1)S(1)} %place_own_sector.1.sigma_own.own), channel_id=1, source_target_pairs={{1,0},{0,1},{3,2},{2,3},{5,4},{4,5},{7,6},{6,7},{9,8},{8,9},{11,10... | collective-permute-start | bytes 786440 | tf_op jit(solution)/shard_map/ppermute | solution.py:226
  34.6 1.6 %collective-permute-start.16 = (bf16[1,256,512]{2,1,0:T(8,128)(2,1)S(1)}, bf16[1,256,512]{2,1,0:T(8,128)(2,1)S(1)}, u32[]{:S(2)}, u32[]{:S(2)}) collective-permute-start(bf16[1,256,512]{2,1,0:T(8,128)(2,1)S(1)} %place_other_sectors.1.across_own), channel_id=1, source_target_pairs={{1,0},{0,1},{3,2},{2,3},{5,4},{4,5},{7,6},{6,7},{9,8},{8,9},{11,10... | collective-permute-start | bytes 786440 | tf_op jit(solution)/shard_map/ppermute | solution.py:226
  37.3 8.7 %collective-permute-start.17 = (bf16[1,64,512]{2,1,0:T(8,128)(2,1)S(1)}, bf16[1,64,512]{2,1,0:T(8,128)(2,1)S(1)}, u32[]{:S(2)}, u32[]{:S(2)}) collective-permute-start(bf16[1,64,512]{2,1,0:T(8,128)(2,1)S(1)} %get-tuple-element.41), channel_id=1, source_target_pairs={{12,0},{8,4},{4,8},{0,12},{13,1},{9,5},{5,9},{1,13},{14,2},{10,6},... | collective-permute-start | bytes 196616 | tf_op jit(solution)/shard_map/ppermute | solution.py:226
  39.7 6.5 %collective-permute-start.18 = (bf16[1,64,512]{2,1,0:T(8,128)(2,1)S(1)}, bf16[1,64,512]{2,1,0:T(8,128)(2,1)S(1)}, u32[]{:S(2)}, u32[]{:S(2)}) collective-permute-start(bf16[1,64,512]{2,1,0:T(8,128)(2,1)S(1)} %get-tuple-element.42), channel_id=1, source_target_pairs={{8,0},{12,4},{0,8},{4,12},{9,1},{13,5},{1,9},{5,13},{10,2},{14,6},... | collective-permute-start | bytes 196616 | tf_op jit(solution)/shard_map/ppermute | solution.py:226
  39.7 6.5 %collective-permute-start.19 = (bf16[1,64,512]{2,1,0:T(8,128)(2,1)S(1)}, bf16[1,64,512]{2,1,0:T(8,128)(2,1)S(1)}, u32[]{:S(2)}, u32[]{:S(2)}) collective-permute-start(bf16[1,64,512]{2,1,0:T(8,128)(2,1)S(1)} %get-tuple-element.43), channel_id=1, source_target_pairs={{4,0},{0,4},{12,8},{8,12},{5,1},{1,5},{13,9},{9,13},{6,2},{2,6},{1... | collective-permute-start | bytes 196616 | tf_op jit(solution)/shard_map/ppermute | solution.py:226
  42.3 3.8 %collective-permute-start.11 = (f32[3,8,128]{2,1,0:T(8,128)S(1)}, f32[3,8,128]{2,1,0:T(8,128)S(1)}, u32[]{:S(2)}, u32[]{:S(2)}) collective-permute-start(f32[3,8,128]{2,1,0:T(8,128)S(1)} %sums_for_rayleigh.1.refs_0_.refs_4_), channel_id=1, source_target_pairs={{2,0},{0,2},{3,1},{1,3},{6,4},{4,6},{7,5},{5,7},{10,8},{8,10},{11,... | collective-permute-start | bytes 36872 | tf_op jit(solution)/shard_map/ppermute | solution.py:226
  46.3 6.7 %collective-permute-start.20 = (bf16[1,64,512]{2,1,0:T(8,128)(2,1)S(1)}, bf16[1,64,512]{2,1,0:T(8,128)(2,1)S(1)}, u32[]{:S(2)}, u32[]{:S(2)}) collective-permute-start(bf16[1,64,512]{2,1,0:T(8,128)(2,1)S(1)} %sum_second_sigma.1.refs_3_), channel_id=1, source_target_pairs={{12,0},{8,4},{4,8},{0,12},{13,1},{9,5},{5,9},{1,13},{14,2},{10,6},... | collective-permute-start | bytes 196616 | tf_op jit(solution)/shard_map/ppermute | solution.py:226
  48.8 6.1 %collective-permute-start.21 = (bf16[1,64,512]{2,1,0:T(8,128)(2,1)S(1)}, bf16[1,64,512]{2,1,0:T(8,128)(2,1)S(1)}, u32[]{:S(2)}, u32[]{:S(2)}) collective-permute-start(bf16[1,64,512]{2,1,0:T(8,128)(2,1)S(1)} %sum_second_sigma.1.refs_3_), channel_id=1, source_target_pairs={{8,0},{12,4},{0,8},{4,12},{9,1},{13,5},{1,9},{5,13},{10,2},{14,6},... | collective-permute-start | bytes 196616 | tf_op jit(solution)/shard_map/ppermute | solution.py:226
  48.8 6.1 %collective-permute-start.22 = (bf16[1,64,512]{2,1,0:T(8,128)(2,1)S(1)}, bf16[1,64,512]{2,1,0:T(8,128)(2,1)S(1)}, u32[]{:S(2)}, u32[]{:S(2)}) collective-permute-start(bf16[1,64,512]{2,1,0:T(8,128)(2,1)S(1)} %sum_second_sigma.1.refs_3_), channel_id=1, source_target_pairs={{4,0},{0,4},{12,8},{8,12},{5,1},{1,5},{13,9},{9,13},{6,2},{2,6},{1... | collective-permute-start | bytes 196616 | tf_op jit(solution)/shard_map/ppermute | solution.py:226

commit v12 on v11

--- a/solution.py
+++ b/solution.py
@@ -46,7 +46,7 @@
     )
 
 
-def load_kernel(left_ref, right_ref, left_own, left_other, right, sems):
+def load_kernel(left_ref, left_own, left_other, sems):
     rows = left_own.shape[1]
     core = lax.axis_index("rep")
     copies = []
@@ -54,40 +54,47 @@
         mine = pl.ds(pl.multiple_of(core * rows, rows), rows)
         columns = pl.ds(pl.multiple_of(place * rows, rows), rows)
         copies.append(pltpu.make_async_copy(left_ref.at[:, mine, columns], half, sems.at[index]))
-    copies.append(pltpu.make_async_copy(right_ref, right, sems.at[2]))
     for copy in copies:
         copy.start()
     for copy in copies:
         copy.wait()
 
 
+def first_tables_kernel(sizes_ref, pairs_ref, weights_ref, wave, _, own, mixing, live):
+    rows, columns = own.shape
+    sector = lax.axis_index("sec")
+    start = lax.axis_index("rep") * rows
+    for term in range(mixing.shape[0]):
+        for step in range(mixing.shape[1]):
+            weight = mixing_scalar(pairs_ref, weights_ref, term, sector ^ step, sector)
+            mixing[term, step] = jnp.full(mixing.shape[2:], weight, jnp.float32)
+    for step in range(live.shape[0] - 1):
+        cells = live_cells(sizes_ref, sector ^ step, start, rows, columns)
+        live[step] = jnp.where(cells, 1.0, 0.0)
+    own[...] = (wave[0].astype(jnp.float32) * live[0]).astype(own.dtype)
+    start = (lax.axis_index("rep") ^ 1) * rows
+    cells = live_cells(sizes_ref, sector, start, rows, columns)
+    live[live.shape[0] - 1] = jnp.where(cells, 1.0, 0.0)
+
+
 def first_kernel(shares, *refs):
-    sizes_ref, pairs_ref, weights_ref, left_own, left_other, right, wave, arrived = refs[:8]
-    own, other, *parts = refs[8:-1]
+    mixing, live, left_own, left_other, right, own, arrived = refs[:7]
+    other, *parts = refs[7:-1]
     held = refs[-1]
     rows, columns = own.shape
     share = parts[0].shape[-2]
     sectors = held.shape[0]
-    sector = lax.axis_index("sec")
-    core = lax.axis_index("rep")
     place = lax.axis_index("ops")
-    live = live_cells(sizes_ref, sector, core * rows, rows, columns)
-    own[...] = masked(wave[0], live)
-    live = live_cells(sizes_ref, sector, (core ^ 1) * rows, rows, columns)
-    other[...] = masked(arrived[0], live)
+    other[...] = (arrived[0].astype(jnp.float32) * live[sectors]).astype(other.dtype)
     products = left_times((left_own, left_other), (own[...], other[...]))
-    total = None
+    totals = [None] * sectors
     for term in range(right.shape[0]):
-        scaled = [
-            mixing_scalar(pairs_ref, weights_ref, term, sector ^ step, sector) * products[term]
-            for step in range(sectors)
-        ]
-        stacked = jnp.concatenate([part.astype(jnp.bfloat16) for part in scaled], axis=0)
-        part = times_right(stacked, right, term)
-        total = part if total is None else total + part
+        product = times_right(products[term], right, term)
+        for step in range(sectors):
+            part = jnp.broadcast_to(mixing[term, step][:1, :1], (rows, columns)) * product
+            totals[step] = part if totals[step] is None else totals[step] + part
     for step in range(sectors):
-        live = live_cells(sizes_ref, sector ^ step, core * rows, rows, columns)
-        held[step] = jnp.where(live, total[step * rows : (step + 1) * rows], 0.0)
+        held[step] = totals[step] * live[step]
     for (steps, across), out in zip(shares, parts):
         for index, along in enumerate(steps):
             start = pl.multiple_of((place ^ along) * share, share)
@@ -265,20 +272,16 @@
 
     farthest_first = list(reversed(range(ops_count)))
     arrived = partner(wavefunction, {"rep": 1})
-    left_own, left_other, right = call(
+    left_own, left_other = call(
         load_kernel,
         "load_operators",
-        [
-            shape(terms, rows, rows),
-            shape(terms, rows, side - rows),
-            shape(*right_blocks.shape),
-        ],
-        [outside] * 2,
+        [shape(terms, rows, rows), shape(terms, rows, side - rows)],
+        [outside],
         left_blocks,
-        right_blocks,
-        scratch=[pltpu.SemaphoreType.DMA((3,))],
-        vmem=49,
-    )
+        scratch=[pltpu.SemaphoreType.DMA((2,))],
+        vmem=51,
+    )
+    right = right_blocks
     pairs = jnp.swapaxes(sector_pairs, 1, 2)
     scalars = (sector_sizes, pairs, pair_weights)
 
@@ -286,20 +289,34 @@
     direct = [(along,) for along in farthest_first[1:-1]]
     spots = [((far, 0), across) for across in range(sectors)]
     spots += [(along, across) for along in direct for across in range(sectors)]
-    wave_own, wave_other, *rest = call(
+    wave_own, mixing, live = call(
+        first_tables_kernel,
+        "tables_for_first_sigma",
+        [
+            shape(rows, columns),
+            shape(terms, sectors, 8, 128, dtype=f32),
+            shape(sectors + 1, rows, columns, dtype=f32),
+        ],
+        [smem] * 3,
+        *scalars,
+        wavefunction,
+        left_own,
+    )
+    wave_other, *rest = call(
         lambda *refs: first_kernel(spots, *refs),
         "first_sigma_terms",
-        [shape(rows, columns)] * 2
+        [shape(rows, columns)]
         + [
             shape(len(along), share, columns, dtype=f32 if along == (far, 0) and across == 0 else bf16)
             for along, across in spots
         ],
-        [smem] * 3,
-        *scalars,
+        [],
+        mixing,
+        live,
         left_own,
         left_other,
         right,
-        wavefunction,
+        wave_own,
         arrived,
         scratch=[pltpu.VMEM((sectors, rows, columns), f32)],
     )
@@ -310,7 +327,7 @@
         [shape(terms, sectors, 8, 128, dtype=f32), shape(rows, columns, dtype=f32)],
         [smem] * 3,
         *scalars,
-        wave_own,
+        wave_other,
     )
     met = [partner(rest[(far, 0), across], {"sec": across}) for across in range(sectors)]
     received = [partner(summed("sum_far_share", *met), {"ops": far})]

time: 56 us -> 54.9 us (0.980)
  starting transfers between devices: 31.8 us -> 30.6 us
  waiting for transfers between devices: 12.7 us -> 13.6 us
  Pallas kernels: 10.4 us -> 9.75 us
    ppermute x23, starting transfers between devices: 31.8 us -> 30.6 us  [partner(): return lax.ppermute(value, axes, pairs)]
    ppermute x23, waiting for transfers between devices: 12.7 us -> 13.6 us  [partner(): return lax.ppermute(value, axes, pairs)]
    pallas_call x13 -> x14, Pallas kernels: 10.4 us -> 9.75 us  [call(): pl.pallas_call(kernel, out_shape=out_shape, in_specs=list(in_specs) + [in...]
  transfers between devices with their start and end apart: 23 -> 23, of which waited for: 12 -> 12; matrix products, arithmetic and copies ran while one was open for 0% -> 0% of each run, Pallas kernels for 10% -> 11%
where the time goes in v12:
time: 54.9 us; the launch traced here: 54.8 us
  starting transfers between devices  30.6 us (56%)
  waiting for transfers between devices  13.6 us (25%)
  Pallas kernels  9.75 us (18%)
  between operations  0.84 us (2%)
    ppermute x23, starting transfers between devices, partner(): return lax.ppermute(value, axes, pairs)  30.6 us
    ppermute x23, waiting for transfers between devices, partner(): return lax.ppermute(value, axes, pairs)  13.6 us
    pallas_call x14, Pallas kernels, call(): pl.pallas_call(kernel, out_shape=out_shape, in_specs=list(in_specs) + [in...  9.75 us
  transfers between devices with their start and end apart: 23, of which 12 were waited for; matrix products, arithmetic and copies ran while one was open for 0% of the time, Pallas kernels for 11%

profile of v12, /device:TPU:0, one launch (start us, length us, event | category | flops | bytes accessed | tf_op | source)
XLA Modules:
  0.0 54.8 jit_solution(5665782342729597395)
XLA Ops:
  0.6 0.0 copy-start.1
  0.6 0.0 copy-start.3
  0.7 0.0 copy-start.2
  0.7 0.0 copy-start.4
  0.7 0.0 copy-start
  0.7 0.5 collective-permute-start
  1.2 1.4 %load_operators.1 = (bf16[4,256,256]{2,1,0:T(8,128)(2,1)S(1)}, bf16[4,256,256]{2,1,0:T(8,128)(2,1)S(1)}) custom-call(bf16[4,512,512]{2,1,0:T(8,128)(2,1)} %left_ref.1), custom_call_target="tpu_custom_call" | custom-call | tf_op jit(solution)/shard_map/load_operators/pallas_call | solution.py:251
  2.6 0.0 copy-done.1
  2.6 0.0 copy-done.3
  2.7 0.0 copy-done.2
  2.7 1.0 %tables_for_first_sigma.1 = (bf16[256,512]{1,0:T(8,128)(2,1)S(1)}, f32[4,2,8,128]{3,2,1,0:T(8,128)S(1)}, f32[3,256,512]{2,1,0:T(8,128)S(1)}) custom-call(s32[2,2]{1,0:T(2,128)S(1)} %copy-done.3, s32[4,2,8]{2,1,0:T(2,128)S(1)} %bitcast.1, f32[4,8]{1,0:T(4,128)S(1)} %copy-done.4, bf16[1,256,512]{2,1,0:T(8,128)(2,1)S(1)} %copy-done.1, ...), custom_call_target="tpu_custom_call" | custom-call | tf_op jit(solution)/shard_map/tables_for_first_sigma/pallas_call | solution.py:251
  3.6 0.0 collective-permute-done.refs_6_
  3.7 1.5 %first_sigma_terms.1 = (bf16[256,512]{1,0:T(8,128)(2,1)S(1)}, f32[2,64,512]{2,1,0:T(8,128)S(1)}, bf16[2,64,512]{2,1,0:T(8,128)(2,1)S(1)}, bf16[1,64,512]{2,1,0:T...) custom-call(f32[4,2,8,128]{3,2,1,0:T(8,128)S(1)} %get-tuple-element., ...), custom_call_target="tpu_custom_call" | custom-call | tf_op jit(solution)/shard_map/first_sigma_terms/pallas_call | solution.py:251
  5.2 2.5 %collective-permute-start.1 = (bf16[2,64,512]{2,1,0:T(8,128)(2,1)S(1)}, bf16[2,64,512]{2,1,0:T(8,128)(2,1)S(1)}, u32[]{:S(2)}, u32[]{:S(2)}) collective-permute-start(bf16[2,64,512]{2,1,0:T(8,128)(2,1)S(1)} %get-tuple-element.30), channel_id=1, source_target_pairs={{2,0},{0,2},{3,1},{1,3},{6,4},{4,6},{7,5},{5,7},{10,8},{8,10},{11,... | collective-permute-start | bytes 393224 | tf_op jit(solution)/shard_map/ppermute | solution.py:233
  7.7 2.6 %collective-permute-start.3 = (bf16[1,64,512]{2,1,0:T(8,128)(2,1)S(1)}, bf16[1,64,512]{2,1,0:T(8,128)(2,1)S(1)}, u32[]{:S(2)}, u32[]{:S(2)}) collective-permute-start(bf16[1,64,512]{2,1,0:T(8,128)(2,1)S(1)} %get-tuple-element.31), channel_id=1, source_target_pairs={{8,0},{12,4},{0,8},{4,12},{9,1},{13,5},{1,9},{5,13},{10,2},{14,6},... | collective-permute-start | bytes 196616 | tf_op jit(solution)/shard_map/ppermute | solution.py:233
  10.3 0.0 collective-permute-start.4
  10.3 1.9 %collective-permute-start.5 = (bf16[1,64,512]{2,1,0:T(8,128)(2,1)S(1)}, bf16[1,64,512]{2,1,0:T(8,128)(2,1)S(1)}, u32[]{:S(2)}, u32[]{:S(2)}) collective-permute-start(bf16[1,64,512]{2,1,0:T(8,128)(2,1)S(1)} %get-tuple-element.33), channel_id=1, source_target_pairs={{4,0},{0,4},{12,8},{8,12},{5,1},{1,5},{13,9},{9,13},{6,2},{2,6},{1... | collective-permute-start | bytes 196616 | tf_op jit(solution)/shard_map/ppermute | solution.py:233
  12.2 1.4 %collective-permute-start.6 = (bf16[1,64,512]{2,1,0:T(8,128)(2,1)S(1)}, bf16[1,64,512]{2,1,0:T(8,128)(2,1)S(1)}, u32[]{:S(2)}, u32[]{:S(2)}) collective-permute-start(bf16[1,64,512]{2,1,0:T(8,128)(2,1)S(1)} %get-tuple-element.34), channel_id=1, source_target_pairs={{6,0},{4,2},{2,4},{0,6},{14,8},{12,10},{10,12},{8,14},{7,1},{5,3},... | collective-permute-start | bytes 196616 | tf_op jit(solution)/shard_map/ppermute | solution.py:233
  13.5 0.0 collective-permute-done.1.refs_1_
  13.6 3.7 %collective-permute-start.2 = (bf16[1,64,512]{2,1,0:T(8,128)(2,1)S(1)}, bf16[1,64,512]{2,1,0:T(8,128)(2,1)S(1)}, u32[]{:S(2)}, u32[]{:S(2)}) collective-permute-start(bf16[1,64,512]{2,1,0:T(8,128)(2,1)S(1)} %sum_far_share.1), channel_id=1, source_target_pairs={{12,0},{8,4},{4,8},{0,12},{13,1},{9,5},{5,9},{1,13},{14,2},{10,6},... | collective-permute-start | bytes 196616 | tf_op jit(solution)/shard_map/ppermute | solution.py:233
  17.2 0.8 %tables_for_second_sigma.1 = (f32[4,2,8,128]{3,2,1,0:T(8,128)S(1)}, f32[256,512]{1,0:T(8,128)S(1)}) custom-call(s32[2,2]{1,0:T(2,128)S(1)} %copy-done.3, s32[4,2,8]{2,1,0:T(2,128)S(1)} %bitcast.2, f32[4,8]{1,0:T(4,128)S(1)} %copy-done.4, bf16[256,512]{1,0:T(8,128)(2,1)S(1)} %get-tuple-element.35._.wave_other), custom_call_target="tpu_custom_call" | custom-call | tf_op jit(solution)/shard_map/tables_for_second_sigma/pallas_call | solution.py:251
  18.0 0.0 collective-permute-done.3.refs_3_
  18.1 0.2 collective-permute-done.4.refs_4_
  18.2 0.0 collective-permute-done.5.refs_5_
  18.2 0.0 collective-permute-done.6.refs_6_
  18.2 1.9 %collective-permute-done.2.refs_2_ = bf16[1,64,512]{2,1,0:T(8,128)(2,1)S(1)} collective-permute-done((bf16[1,64,512]{2,1,0:T(8,128)(2,1)S(1)}, bf16[1,64,512]{2,1,0:T(8,128)(2,1)S(1)}, u32[]{:S(2)}, u32[]{:S(2)}) %collective-permute-start.2) | collective-permute-done | bytes 65568 | tf_op jit(solution)/shard_map/ppermute | solution.py:233
  20.1 0.1 sum_first_sigma.1.refs_3_
  20.2 3.9 %collective-permute-start.7 = (bf16[1,64,512]{2,1,0:T(8,128)(2,1)S(1)}, bf16[1,64,512]{2,1,0:T(8,128)(2,1)S(1)}, u32[]{:S(2)}, u32[]{:S(2)}) collective-permute-start(bf16[1,64,512]{2,1,0:T(8,128)(2,1)S(1)} %sum_first_sigma.1.refs_3_), channel_id=1, source_target_pairs={{12,0},{8,4},{4,8},{0,12},{13,1},{9,5},{5,9},{1,13},{14,2},{10,6},... | collective-permute-start | bytes 196616 | tf_op jit(solution)/shard_map/ppermute | solution.py:233
  24.1 0.0 collective-permute-start.8
  24.1 0.6 %collective-permute-start.9 = (bf16[1,64,512]{2,1,0:T(8,128)(2,1)S(1)}, bf16[1,64,512]{2,1,0:T(8,128)(2,1)S(1)}, u32[]{:S(2)}, u32[]{:S(2)}) collective-permute-start(bf16[1,64,512]{2,1,0:T(8,128)(2,1)S(1)} %sum_first_sigma.1.refs_3_), channel_id=1, source_target_pairs={{4,0},{0,4},{12,8},{8,12},{5,1},{1,5},{13,9},{9,13},{6,2},{2,6},{1... | collective-permute-start | bytes 196616 | tf_op jit(solution)/shard_map/ppermute | solution.py:233
  24.7 0.9 %collective-permute-start.14 = (bf16[1,64,512]{2,1,0:T(8,128)(2,1)S(1)}, bf16[1,64,512]{2,1,0:T(8,128)(2,1)S(1)}, u32[]{:S(2)}, u32[]{:S(2)}) collective-permute-start(bf16[1,64,512]{2,1,0:T(8,128)(2,1)S(1)} %sum_first_sigma.1.refs_3_), channel_id=1, source_target_pairs={{6,0},{4,2},{2,4},{0,6},{14,8},{12,10},{10,12},{8,14},{7,1},{5,3},... | collective-permute-start | bytes 196616 | tf_op jit(solution)/shard_map/ppermute | solution.py:233
  25.7 1.9 %collective-permute-start.15 = (bf16[1,64,512]{2,1,0:T(8,128)(2,1)S(1)}, bf16[1,64,512]{2,1,0:T(8,128)(2,1)S(1)}, u32[]{:S(2)}, u32[]{:S(2)}) collective-permute-start(bf16[1,64,512]{2,1,0:T(8,128)(2,1)S(1)} %sum_first_sigma.1.refs_3_), channel_id=1, source_target_pairs={{2,0},{0,2},{3,1},{1,3},{6,4},{4,6},{7,5},{5,7},{10,8},{8,10},{11,... | collective-permute-start | bytes 196616 | tf_op jit(solution)/shard_map/ppermute | solution.py:233
  27.6 0.0 collective-permute-done.7.refs_0_
  27.6 0.5 collective-permute-start.12
  28.0 1.2 %collective-permute-done.8.refs_1_ = bf16[1,64,512]{2,1,0:T(8,128)(2,1)S(1)} collective-permute-done((bf16[1,64,512]{2,1,0:T(8,128)(2,1)S(1)}, bf16[1,64,512]{2,1,0:T(8,128)(2,1)S(1)}, u32[]{:S(2)}, u32[]{:S(2)}) %collective-permute-start.8) | collective-permute-done | bytes 65568 | tf_op jit(solution)/shard_map/ppermute | solution.py:233
  29.3 0.4 collective-permute-start.13
  29.7 0.0 collective-permute-done.9.refs_2_
  29.7 0.1 collective-permute-start.10
  29.8 0.6 %collective-permute-done.14.refs_2_ = bf16[1,64,512]{2,1,0:T(8,128)(2,1)S(1)} collective-permute-done((bf16[1,64,512]{2,1,0:T(8,128)(2,1)S(1)}, bf16[1,64,512]{2,1,0:T(8,128)(2,1)S(1)}, u32[]{:S(2)}, u32[]{:S(2)}) %collective-permute-start.14) | collective-permute-done | bytes 65568 | tf_op jit(solution)/shard_map/ppermute | solution.py:233
  30.4 0.8 %collective-permute-done.15.refs_3_ = bf16[1,64,512]{2,1,0:T(8,128)(2,1)S(1)} collective-permute-done((bf16[1,64,512]{2,1,0:T(8,128)(2,1)S(1)}, bf16[1,64,512]{2,1,0:T(8,128)(2,1)S(1)}, u32[]{:S(2)}, u32[]{:S(2)}) %collective-permute-start.15) | collective-permute-done | bytes 65568 | tf_op jit(solution)/shard_map/ppermute | solution.py:233
  31.1 1.0 %collective-permute-done.12.refs_0_ = bf16[1,64,512]{2,1,0:T(8,128)(2,1)S(1)} collective-permute-done((bf16[1,64,512]{2,1,0:T(8,128)(2,1)S(1)}, bf16[1,64,512]{2,1,0:T(8,128)(2,1)S(1)}, u32[]{:S(2)}, u32[]{:S(2)}) %collective-permute-start.12) | collective-permute-done | bytes 65568 | tf_op jit(solution)/shard_map/ppermute | solution.py:233
  32.2 1.4 %collective-permute-done.13.refs_1_ = bf16[1,64,512]{2,1,0:T(8,128)(2,1)S(1)} collective-permute-done((bf16[1,64,512]{2,1,0:T(8,128)(2,1)S(1)}, bf16[1,64,512]{2,1,0:T(8,128)(2,1)S(1)}, u32[]{:S(2)}, u32[]{:S(2)}) %collective-permute-start.13) | collective-permute-done | bytes 65568 | tf_op jit(solution)/shard_map/ppermute | solution.py:233
  33.6 0.1 collective-permute-start.16
  33.6 0.0 collective-permute-done.10.sigma_other.other
  33.7 1.0 %left_products.1 = (f32[4,256,512]{2,1,0:T(8,128)S(1)}, f32[1,4,256,512]{3,2,1,0:T(8,128)S(1)}) custom-call(bf16[4,256,256]{2,1,0:T(8,128)(2,1)S(1)} %get-tuple-element.24._.refs_2_.left_own, bf16[4,256,256]{2,1,0:T(8,128)(2,1)S(1)} %get-tuple-element.28.refs_3_.left_other, bf16[1,256,512]{2,1,0:T(8,128)(2,1)S(1)} %place_own_sector.1.sigma_own.own, ...), custom_call_target="tpu_custom_call" | custom-call | tf_op jit(solution)/shard_map/left_products/pallas_call | solution.py:251
  34.6 0.5 collective-permute-done.16.other
  35.2 1.1 %second_sigma_terms.1 = (f32[1,64,512]{2,1,0:T(8,128)S(1)}, bf16[1,64,512]{2,1,0:T(8,128)(2,1)S(1)}, bf16[1,64,512]{2,1,0:T(8,128)(2,1)S(1)}, bf16[1,64,512]{2,1,0:T(8,128)(2,1)S(1)}) custom-call(f32[4,2,8,128]{3,2,1,0:T(8,128)S(1)} %get-tuple-element.36.refs_7_.mixing, f32[256,512]{1,0:T(8,128)S(1)} %get-tuple-element.39.live, ...), custom_call_target="tpu_custom_call" | custom-call | tf_op jit(solution)/shard_map/second_sigma_terms/pallas_call | solution.py:251
  36.3 2.0 %collective-permute-start.17 = (bf16[1,64,512]{2,1,0:T(8,128)(2,1)S(1)}, bf16[1,64,512]{2,1,0:T(8,128)(2,1)S(1)}, u32[]{:S(2)}, u32[]{:S(2)}) collective-permute-start(bf16[1,64,512]{2,1,0:T(8,128)(2,1)S(1)} %get-tuple-element.43), channel_id=1, source_target_pairs={{12,0},{8,4},{4,8},{0,12},{13,1},{9,5},{5,9},{1,13},{14,2},{10,6},... | collective-permute-start | bytes 196616 | tf_op jit(solution)/shard_map/ppermute | solution.py:233
  38.3 0.1 collective-permute-start.18
  38.4 2.4 %collective-permute-start.19 = (bf16[1,64,512]{2,1,0:T(8,128)(2,1)S(1)}, bf16[1,64,512]{2,1,0:T(8,128)(2,1)S(1)}, u32[]{:S(2)}, u32[]{:S(2)}) collective-permute-start(bf16[1,64,512]{2,1,0:T(8,128)(2,1)S(1)} %get-tuple-element.45), channel_id=1, source_target_pairs={{4,0},{0,4},{12,8},{8,12},{5,1},{1,5},{13,9},{9,13},{6,2},{2,6},{1... | collective-permute-start | bytes 196616 | tf_op jit(solution)/shard_map/ppermute | solution.py:233
  40.7 0.5 sums_for_rayleigh.1.refs_0_.refs_4_
  41.2 0.7 %collective-permute-start.11 = (f32[3,8,128]{2,1,0:T(8,128)S(1)}, f32[3,8,128]{2,1,0:T(8,128)S(1)}, u32[]{:S(2)}, u32[]{:S(2)}) collective-permute-start(f32[3,8,128]{2,1,0:T(8,128)S(1)} %sums_for_rayleigh.1.refs_0_.refs_4_), channel_id=1, source_target_pairs={{2,0},{0,2},{3,1},{1,3},{6,4},{4,6},{7,5},{5,7},{10,8},{8,10},{11,... | collective-permute-start | bytes 36872 | tf_op jit(solution)/shard_map/ppermute | solution.py:233
  42.0 3.0 %collective-permute-done.11.refs_1_.refs_5_ = f32[3,8,128]{2,1,0:T(8,128)S(1)} collective-permute-done((f32[3,8,128]{2,1,0:T(8,128)S(1)}, f32[3,8,128]{2,1,0:T(8,128)S(1)}, u32[]{:S(2)}, u32[]{:S(2)}) %collective-permute-start.11) | collective-permute-done | bytes 12320 | tf_op jit(solution)/shard_map/ppermute | solution.py:233
  45.0 0.0 collective-permute-done.17.refs_1_
  45.0 0.2 collective-permute-done.18.refs_2_
  45.2 0.0 collective-permute-done.19.refs_3_
  45.2 2.6 %collective-permute-start.20 = (bf16[1,64,512]{2,1,0:T(8,128)(2,1)S(1)}, bf16[1,64,512]{2,1,0:T(8,128)(2,1)S(1)}, u32[]{:S(2)}, u32[]{:S(2)}) collective-permute-start(bf16[1,64,512]{2,1,0:T(8,128)(2,1)S(1)} %sum_second_sigma.1.refs_3_), channel_id=1, source_target_pairs={{12,0},{8,4},{4,8},{0,12},{13,1},{9,5},{5,9},{1,13},{14,2},{10,6},... | collective-permute-start | bytes 196616 | tf_op jit(solution)/shard_map/ppermute | solution.py:233
  47.8 0.0 collective-permute-start.21
  47.8 1.9 %collective-permute-start.22 = (bf16[1,64,512]{2,1,0:T(8,128)(2,1)S(1)}, bf16[1,64,512]{2,1,0:T(8,128)(2,1)S(1)}, u32[]{:S(2)}, u32[]{:S(2)}) collective-permute-start(bf16[1,64,512]{2,1,0:T(8,128)(2,1)S(1)} %sum_second_sigma.1.refs_3_), channel_id=1, source_target_pairs={{4,0},{0,4},{12,8},{8,12},{5,1},{1,5},{13,9},{9,13},{6,2},{2,6},{1... | collective-permute-start | bytes 196616 | tf_op jit(solution)/shard_map/ppermute | solution.py:233
  49.7 1.4 %second_wave.1 = (bf16[1,256,512]{2,1,0:T(8,128)(2,1)}, f32[2,8,128]{2,1,0:T(8,128)S(1)}) custom-call(s32[2,2]{1,0:T(2,128)S(1)} %copy-done.3, bf16[256,512]{1,0:T(8,128)(2,1)S(1)} %get-tuple-element.25.refs_5_.wave_own, bf16[1,256,512]{2,1,0:T(8,128)(2,1)S(1)} %place_own_sector.1.sigma_own.own, f32[3,8,128]{2,1,0:T(8,128)S(1)} %sums_for_rayleigh.1.refs_0_.refs_4_, ...), custom_call_target="tpu_custom_call" | custom-call | tf_op jit(solution)/shard_map/second_wave/pallas_call | solution.py:251
  51.1 0.8 %collective-permute-done.20.refs_0_ = bf16[1,64,512]{2,1,0:T(8,128)(2,1)S(1)} collective-permute-done((bf16[1,64,512]{2,1,0:T(8,128)(2,1)S(1)}, bf16[1,64,512]{2,1,0:T(8,128)(2,1)S(1)}, u32[]{:S(2)}, u32[]{:S(2)}) %collective-permute-start.20) | collective-permute-done | bytes 65568 | tf_op jit(solution)/shard_map/ppermute | solution.py:233
  51.9 2.0 %collective-permute-done.21.refs_1_ = bf16[1,64,512]{2,1,0:T(8,128)(2,1)S(1)} collective-permute-done((bf16[1,64,512]{2,1,0:T(8,128)(2,1)S(1)}, bf16[1,64,512]{2,1,0:T(8,128)(2,1)S(1)}, u32[]{:S(2)}, u32[]{:S(2)}) %collective-permute-start.21) | collective-permute-done | bytes 65568 | tf_op jit(solution)/shard_map/ppermute | solution.py:233
  53.9 0.0 collective-permute-done.22.refs_2_
  53.9 0.9 %join_second_sigma.1 = f32[1,256,512]{2,1,0:T(8,128)} custom-call(f32[2,8,128]{2,1,0:T(8,128)S(1)} %get-tuple-element.38.factors, bf16[1,256,512]{2,1,0:T(8,128)(2,1)S(1)} %place_own_sector.1.sigma_own.own, bf16[1,64,512]{2,1,0:T(8,128)(2,1)S(1)} %collective-permute-done.20.refs_0_, bf16[1,64,512]{2,1,0:T(8,128)(2,1)S(1)} %collective-permute-done.21.refs_1_, ...), custom_call_target="tpu_custom_call" | custom-call | tf_op jit(solution)/shard_map/join_second_sigma/pallas_call | solution.py:251
  (6 shorter events, 0.1 us)
Async XLA Ops:
  0.6 2.0 %copy-start.1 = (bf16[1,256,512]{2,1,0:T(8,128)(2,1)S(1)}, bf16[1,256,512]{2,1,0:T(8,128)(2,1)}, u32[]{:S(2)}) copy-start(bf16[1,256,512]{2,1,0:T(8,128)(2,1)} %wave.1) | copy-start | bytes 786436
  0.6 2.0 %copy-start.3 = (s32[2,2]{1,0:T(2,128)S(1)}, s32[2,2]{1,0:T(2,128)}, u32[]{:S(2)}) copy-start(s32[2,2]{1,0:T(2,128)} %sizes_ref.5) | copy-start | bytes 52
  0.7 2.0 %copy-start.2 = (s32[4,8,2]{1,2,0:T(2,128)S(1)}, s32[4,8,2]{1,2,0:T(2,128)}, u32[]{:S(2)}) copy-start(s32[4,8,2]{1,2,0:T(2,128)} %param.10) | copy-start | bytes 772
  0.7 2.0 %copy-start.4 = (f32[4,8]{1,0:T(4,128)S(1)}, f32[4,8]{1,0:T(4,128)}, u32[]{:S(2)}) copy-start(f32[4,8]{1,0:T(4,128)} %weights_ref.3) | copy-start | bytes 388
  0.7 3.0 %copy-start = (bf16[4,512,512]{2,1,0:T(8,128)(2,1)S(1)}, bf16[4,512,512]{2,1,0:T(8,128)(2,1)}, u32[]{:S(2)}) copy-start(bf16[4,512,512]{2,1,0:T(8,128)(2,1)} %right.1) | copy-start | bytes 6291460
  0.7 3.0 %collective-permute-start = (bf16[1,256,512]{2,1,0:T(8,128)(2,1)}, bf16[1,256,512]{2,1,0:T(8,128)(2,1)S(1)}, u32[]{:S(2)}, u32[]{:S(2)}) collective-permute-start(bf16[1,256,512]{2,1,0:T(8,128)(2,1)} %wave.1), channel_id=1, source_target_pairs={{1,0},{0,1},{3,2},{2,3},{5,4},{4,5},{7,6},{6,7},{9,8},{8,9},{11,10... | collective-permute-start | bytes 786440 | tf_op jit(solution)/shard_map/ppermute | solution.py:233
  5.2 8.4 %collective-permute-start.1 = (bf16[2,64,512]{2,1,0:T(8,128)(2,1)S(1)}, bf16[2,64,512]{2,1,0:T(8,128)(2,1)S(1)}, u32[]{:S(2)}, u32[]{:S(2)}) collective-permute-start(bf16[2,64,512]{2,1,0:T(8,128)(2,1)S(1)} %get-tuple-element.30), channel_id=1, source_target_pairs={{2,0},{0,2},{3,1},{1,3},{6,4},{4,6},{7,5},{5,7},{10,8},{8,10},{11,... | collective-permute-start | bytes 393224 | tf_op jit(solution)/shard_map/ppermute | solution.py:233
  7.7 10.4 %collective-permute-start.3 = (bf16[1,64,512]{2,1,0:T(8,128)(2,1)S(1)}, bf16[1,64,512]{2,1,0:T(8,128)(2,1)S(1)}, u32[]{:S(2)}, u32[]{:S(2)}) collective-permute-start(bf16[1,64,512]{2,1,0:T(8,128)(2,1)S(1)} %get-tuple-element.31), channel_id=1, source_target_pairs={{8,0},{12,4},{0,8},{4,12},{9,1},{13,5},{1,9},{5,13},{10,2},{14,6},... | collective-permute-start | bytes 196616 | tf_op jit(solution)/shard_map/ppermute | solution.py:233
  10.3 7.9 %collective-permute-start.4 = (bf16[1,64,512]{2,1,0:T(8,128)(2,1)S(1)}, bf16[1,64,512]{2,1,0:T(8,128)(2,1)S(1)}, u32[]{:S(2)}, u32[]{:S(2)}) collective-permute-start(bf16[1,64,512]{2,1,0:T(8,128)(2,1)S(1)} %get-tuple-element.32), channel_id=1, source_target_pairs={{10,0},{8,2},{14,4},{12,6},{2,8},{0,10},{6,12},{4,14},{11,1},{9,3}... | collective-permute-start | bytes 196616 | tf_op jit(solution)/shard_map/ppermute | solution.py:233
  10.3 7.9 %collective-permute-start.5 = (bf16[1,64,512]{2,1,0:T(8,128)(2,1)S(1)}, bf16[1,64,512]{2,1,0:T(8,128)(2,1)S(1)}, u32[]{:S(2)}, u32[]{:S(2)}) collective-permute-start(bf16[1,64,512]{2,1,0:T(8,128)(2,1)S(1)} %get-tuple-element.33), channel_id=1, source_target_pairs={{4,0},{0,4},{12,8},{8,12},{5,1},{1,5},{13,9},{9,13},{6,2},{2,6},{1... | collective-permute-start | bytes 196616 | tf_op jit(solution)/shard_map/ppermute | solution.py:233
  12.2 6.1 %collective-permute-start.6 = (bf16[1,64,512]{2,1,0:T(8,128)(2,1)S(1)}, bf16[1,64,512]{2,1,0:T(8,128)(2,1)S(1)}, u32[]{:S(2)}, u32[]{:S(2)}) collective-permute-start(bf16[1,64,512]{2,1,0:T(8,128)(2,1)S(1)} %get-tuple-element.34), channel_id=1, source_target_pairs={{6,0},{4,2},{2,4},{0,6},{14,8},{12,10},{10,12},{8,14},{7,1},{5,3},... | collective-permute-start | bytes 196616 | tf_op jit(solution)/shard_map/ppermute | solution.py:233
  13.6 6.6 %collective-permute-start.2 = (bf16[1,64,512]{2,1,0:T(8,128)(2,1)S(1)}, bf16[1,64,512]{2,1,0:T(8,128)(2,1)S(1)}, u32[]{:S(2)}, u32[]{:S(2)}) collective-permute-start(bf16[1,64,512]{2,1,0:T(8,128)(2,1)S(1)} %sum_far_share.1), channel_id=1, source_target_pairs={{12,0},{8,4},{4,8},{0,12},{13,1},{9,5},{5,9},{1,13},{14,2},{10,6},... | collective-permute-start | bytes 196616 | tf_op jit(solution)/shard_map/ppermute | solution.py:233
  20.2 7.4 %collective-permute-start.7 = (bf16[1,64,512]{2,1,0:T(8,128)(2,1)S(1)}, bf16[1,64,512]{2,1,0:T(8,128)(2,1)S(1)}, u32[]{:S(2)}, u32[]{:S(2)}) collective-permute-start(bf16[1,64,512]{2,1,0:T(8,128)(2,1)S(1)} %sum_first_sigma.1.refs_3_), channel_id=1, source_target_pairs={{12,0},{8,4},{4,8},{0,12},{13,1},{9,5},{5,9},{1,13},{14,2},{10,6},... | collective-permute-start | bytes 196616 | tf_op jit(solution)/shard_map/ppermute | solution.py:233
  24.1 5.2 %collective-permute-start.8 = (bf16[1,64,512]{2,1,0:T(8,128)(2,1)S(1)}, bf16[1,64,512]{2,1,0:T(8,128)(2,1)S(1)}, u32[]{:S(2)}, u32[]{:S(2)}) collective-permute-start(bf16[1,64,512]{2,1,0:T(8,128)(2,1)S(1)} %sum_first_sigma.1.refs_3_), channel_id=1, source_target_pairs={{8,0},{12,4},{0,8},{4,12},{9,1},{13,5},{1,9},{5,13},{10,2},{14,6},... | collective-permute-start | bytes 196616 | tf_op jit(solution)/shard_map/ppermute | solution.py:233
  24.1 5.6 %collective-permute-start.9 = (bf16[1,64,512]{2,1,0:T(8,128)(2,1)S(1)}, bf16[1,64,512]{2,1,0:T(8,128)(2,1)S(1)}, u32[]{:S(2)}, u32[]{:S(2)}) collective-permute-start(bf16[1,64,512]{2,1,0:T(8,128)(2,1)S(1)} %sum_first_sigma.1.refs_3_), channel_id=1, source_target_pairs={{4,0},{0,4},{12,8},{8,12},{5,1},{1,5},{13,9},{9,13},{6,2},{2,6},{1... | collective-permute-start | bytes 196616 | tf_op jit(solution)/shard_map/ppermute | solution.py:233
  24.7 5.6 %collective-permute-start.14 = (bf16[1,64,512]{2,1,0:T(8,128)(2,1)S(1)}, bf16[1,64,512]{2,1,0:T(8,128)(2,1)S(1)}, u32[]{:S(2)}, u32[]{:S(2)}) collective-permute-start(bf16[1,64,512]{2,1,0:T(8,128)(2,1)S(1)} %sum_first_sigma.1.refs_3_), channel_id=1, source_target_pairs={{6,0},{4,2},{2,4},{0,6},{14,8},{12,10},{10,12},{8,14},{7,1},{5,3},... | collective-permute-start | bytes 196616 | tf_op jit(solution)/shard_map/ppermute | solution.py:233
  25.7 5.4 %collective-permute-start.15 = (bf16[1,64,512]{2,1,0:T(8,128)(2,1)S(1)}, bf16[1,64,512]{2,1,0:T(8,128)(2,1)S(1)}, u32[]{:S(2)}, u32[]{:S(2)}) collective-permute-start(bf16[1,64,512]{2,1,0:T(8,128)(2,1)S(1)} %sum_first_sigma.1.refs_3_), channel_id=1, source_target_pairs={{2,0},{0,2},{3,1},{1,3},{6,4},{4,6},{7,5},{5,7},{10,8},{8,10},{11,... | collective-permute-start | bytes 196616 | tf_op jit(solution)/shard_map/ppermute | solution.py:233
  27.6 4.6 %collective-permute-start.12 = (bf16[1,64,512]{2,1,0:T(8,128)(2,1)S(1)}, bf16[1,64,512]{2,1,0:T(8,128)(2,1)S(1)}, u32[]{:S(2)}, u32[]{:S(2)}) collective-permute-start(bf16[1,64,512]{2,1,0:T(8,128)(2,1)S(1)} %collective-permute-done.7.refs_0_), channel_id=1, source_target_pairs={{2,0},{0,2},{3,1},{1,3},{6,4},{4,6},{7,5},{5,7},{10,8},{8,10},{11,... | collective-permute-start | bytes 196616 | tf_op jit(solution)/shard_map/ppermute | solution.py:233
  29.3 4.3 %collective-permute-start.13 = (bf16[1,64,512]{2,1,0:T(8,128)(2,1)S(1)}, bf16[1,64,512]{2,1,0:T(8,128)(2,1)S(1)}, u32[]{:S(2)}, u32[]{:S(2)}) collective-permute-start(bf16[1,64,512]{2,1,0:T(8,128)(2,1)S(1)} %collective-permute-done.8.refs_1_), channel_id=1, source_target_pairs={{2,0},{0,2},{3,1},{1,3},{6,4},{4,6},{7,5},{5,7},{10,8},{8,10},{11,... | collective-permute-start | bytes 196616 | tf_op jit(solution)/shard_map/ppermute | solution.py:233
  29.7 3.9 %collective-permute-start.10 = (bf16[1,256,512]{2,1,0:T(8,128)(2,1)S(1)}, bf16[1,256,512]{2,1,0:T(8,128)(2,1)S(1)}, u32[]{:S(2)}, u32[]{:S(2)}) collective-permute-start(bf16[1,256,512]{2,1,0:T(8,128)(2,1)S(1)} %place_own_sector.1.sigma_own.own), channel_id=1, source_target_pairs={{1,0},{0,1},{3,2},{2,3},{5,4},{4,5},{7,6},{6,7},{9,8},{8,9},{11,10... | collective-permute-start | bytes 786440 | tf_op jit(solution)/shard_map/ppermute | solution.py:233
  33.6 1.6 %collective-permute-start.16 = (bf16[1,256,512]{2,1,0:T(8,128)(2,1)S(1)}, bf16[1,256,512]{2,1,0:T(8,128)(2,1)S(1)}, u32[]{:S(2)}, u32[]{:S(2)}) collective-permute-start(bf16[1,256,512]{2,1,0:T(8,128)(2,1)S(1)} %place_other_sectors.1.across_own), channel_id=1, source_target_pairs={{1,0},{0,1},{3,2},{2,3},{5,4},{4,5},{7,6},{6,7},{9,8},{8,9},{11,10... | collective-permute-start | bytes 786440 | tf_op jit(solution)/shard_map/ppermute | solution.py:233
  36.3 8.7 %collective-permute-start.17 = (bf16[1,64,512]{2,1,0:T(8,128)(2,1)S(1)}, bf16[1,64,512]{2,1,0:T(8,128)(2,1)S(1)}, u32[]{:S(2)}, u32[]{:S(2)}) collective-permute-start(bf16[1,64,512]{2,1,0:T(8,128)(2,1)S(1)} %get-tuple-element.43), channel_id=1, source_target_pairs={{12,0},{8,4},{4,8},{0,12},{13,1},{9,5},{5,9},{1,13},{14,2},{10,6},... | collective-permute-start | bytes 196616 | tf_op jit(solution)/shard_map/ppermute | solution.py:233
  38.3 6.9 %collective-permute-start.18 = (bf16[1,64,512]{2,1,0:T(8,128)(2,1)S(1)}, bf16[1,64,512]{2,1,0:T(8,128)(2,1)S(1)}, u32[]{:S(2)}, u32[]{:S(2)}) collective-permute-start(bf16[1,64,512]{2,1,0:T(8,128)(2,1)S(1)} %get-tuple-element.44), channel_id=1, source_target_pairs={{8,0},{12,4},{0,8},{4,12},{9,1},{13,5},{1,9},{5,13},{10,2},{14,6},... | collective-permute-start | bytes 196616 | tf_op jit(solution)/shard_map/ppermute | solution.py:233
  38.4 6.8 %collective-permute-start.19 = (bf16[1,64,512]{2,1,0:T(8,128)(2,1)S(1)}, bf16[1,64,512]{2,1,0:T(8,128)(2,1)S(1)}, u32[]{:S(2)}, u32[]{:S(2)}) collective-permute-start(bf16[1,64,512]{2,1,0:T(8,128)(2,1)S(1)} %get-tuple-element.45), channel_id=1, source_target_pairs={{4,0},{0,4},{12,8},{8,12},{5,1},{1,5},{13,9},{9,13},{6,2},{2,6},{1... | collective-permute-start | bytes 196616 | tf_op jit(solution)/shard_map/ppermute | solution.py:233
  41.2 3.8 %collective-permute-start.11 = (f32[3,8,128]{2,1,0:T(8,128)S(1)}, f32[3,8,128]{2,1,0:T(8,128)S(1)}, u32[]{:S(2)}, u32[]{:S(2)}) collective-permute-start(f32[3,8,128]{2,1,0:T(8,128)S(1)} %sums_for_rayleigh.1.refs_0_.refs_4_), channel_id=1, source_target_pairs={{2,0},{0,2},{3,1},{1,3},{6,4},{4,6},{7,5},{5,7},{10,8},{8,10},{11,... | collective-permute-start | bytes 36872 | tf_op jit(solution)/shard_map/ppermute | solution.py:233
  45.2 6.7 %collective-permute-start.20 = (bf16[1,64,512]{2,1,0:T(8,128)(2,1)S(1)}, bf16[1,64,512]{2,1,0:T(8,128)(2,1)S(1)}, u32[]{:S(2)}, u32[]{:S(2)}) collective-permute-start(bf16[1,64,512]{2,1,0:T(8,128)(2,1)S(1)} %sum_second_sigma.1.refs_3_), channel_id=1, source_target_pairs={{12,0},{8,4},{4,8},{0,12},{13,1},{9,5},{5,9},{1,13},{14,2},{10,6},... | collective-permute-start | bytes 196616 | tf_op jit(solution)/shard_map/ppermute | solution.py:233
  47.8 6.1 %collective-permute-start.21 = (bf16[1,64,512]{2,1,0:T(8,128)(2,1)S(1)}, bf16[1,64,512]{2,1,0:T(8,128)(2,1)S(1)}, u32[]{:S(2)}, u32[]{:S(2)}) collective-permute-start(bf16[1,64,512]{2,1,0:T(8,128)(2,1)S(1)} %sum_second_sigma.1.refs_3_), channel_id=1, source_target_pairs={{8,0},{12,4},{0,8},{4,12},{9,1},{13,5},{1,9},{5,13},{10,2},{14,6},... | collective-permute-start | bytes 196616 | tf_op jit(solution)/shard_map/ppermute | solution.py:233
  47.8 6.1 %collective-permute-start.22 = (bf16[1,64,512]{2,1,0:T(8,128)(2,1)S(1)}, bf16[1,64,512]{2,1,0:T(8,128)(2,1)S(1)}, u32[]{:S(2)}, u32[]{:S(2)}) collective-permute-start(bf16[1,64,512]{2,1,0:T(8,128)(2,1)S(1)} %sum_second_sigma.1.refs_3_), channel_id=1, source_target_pairs={{4,0},{0,4},{12,8},{8,12},{5,1},{1,5},{13,9},{9,13},{6,2},{2,6},{1... | collective-permute-start | bytes 196616 | tf_op jit(solution)/shard_map/ppermute | solution.py:233

commit v13 on v12

--- a/solution.py
+++ b/solution.py
@@ -331,11 +331,9 @@
     )
     met = [partner(rest[(far, 0), across], {"sec": across}) for across in range(sectors)]
     received = [partner(summed("sum_far_share", *met), {"ops": far})]
-    received += [
-        partner(rest[along, across], {"ops": along[0], "sec": across})
-        for along in direct
-        for across in range(sectors)
-    ]
+    nearest = ((1,), 0)
+    order = [nearest] + [spot for spot in rest if spot[0] in direct and spot != nearest]
+    received += [partner(rest[spot], {"ops": spot[0][0], "sec": spot[1]}) for spot in order]
     first_share = summed("sum_first_sigma", *[(piece, 1) for piece in met], *received, after=(mixing,))
     along_ops = {along: partner(first_share, {"ops": along}) for along in farthest_first}
     sigma_own = call(

time: 54.9 us -> 54.7 us (level)
  starting transfers between devices: 30.6 us -> 29.7 us
  waiting for transfers between devices: 13.6 us -> 14.2 us
    ppermute x23, starting transfers between devices: 30.6 us -> 29.7 us  [partner(): return lax.ppermute(value, axes, pairs)]
    ppermute x23, waiting for transfers between devices: 13.6 us -> 14.2 us  [partner(): return lax.ppermute(value, axes, pairs)]
where the time goes in v13:
time: 54.7 us; the launch traced here: 54.6 us
  starting transfers between devices  29.7 us (54%)
  waiting for transfers between devices  14.2 us (26%)
  Pallas kernels  9.76 us (18%)
  between operations  0.85 us (2%)
    ppermute x23, starting transfers between devices, partner(): return lax.ppermute(value, axes, pairs)  29.7 us
    ppermute x23, waiting for transfers between devices, partner(): return lax.ppermute(value, axes, pairs)  14.2 us
    pallas_call x14, Pallas kernels, call(): pl.pallas_call(kernel, out_shape=out_shape, in_specs=list(in_specs) + [in...  9.76 us
  transfers between devices with their start and end apart: 23, of which 12 were waited for; matrix products, arithmetic and copies ran while one was open for 0% of the time, Pallas kernels for 11%

profile of v13, /device:TPU:0, one launch (start us, length us, event | category | flops | bytes accessed | tf_op | source)
XLA Modules:
  0.0 54.6 jit_solution(6748452826462548940)
XLA Ops:
  0.6 0.0 copy-start.1
  0.6 0.0 copy-start.3
  0.7 0.0 copy-start.2
  0.7 0.0 copy-start.4
  0.7 0.0 copy-start
  0.7 0.5 collective-permute-start
  1.2 1.4 %load_operators.1 = (bf16[4,256,256]{2,1,0:T(8,128)(2,1)S(1)}, bf16[4,256,256]{2,1,0:T(8,128)(2,1)S(1)}) custom-call(bf16[4,512,512]{2,1,0:T(8,128)(2,1)} %left_ref.1), custom_call_target="tpu_custom_call" | custom-call | tf_op jit(solution)/shard_map/load_operators/pallas_call | solution.py:251
  2.6 0.0 copy-done.1
  2.6 0.0 copy-done.3
  2.7 0.0 copy-done.2
  2.7 1.0 %tables_for_first_sigma.1 = (bf16[256,512]{1,0:T(8,128)(2,1)S(1)}, f32[4,2,8,128]{3,2,1,0:T(8,128)S(1)}, f32[3,256,512]{2,1,0:T(8,128)S(1)}) custom-call(s32[2,2]{1,0:T(2,128)S(1)} %copy-done.3, s32[4,2,8]{2,1,0:T(2,128)S(1)} %bitcast.1, f32[4,8]{1,0:T(4,128)S(1)} %copy-done.4, bf16[1,256,512]{2,1,0:T(8,128)(2,1)S(1)} %copy-done.1, ...), custom_call_target="tpu_custom_call" | custom-call | tf_op jit(solution)/shard_map/tables_for_first_sigma/pallas_call | solution.py:251
  3.6 0.0 collective-permute-done.refs_6_
  3.7 1.5 %first_sigma_terms.1 = (bf16[256,512]{1,0:T(8,128)(2,1)S(1)}, f32[2,64,512]{2,1,0:T(8,128)S(1)}, bf16[2,64,512]{2,1,0:T(8,128)(2,1)S(1)}, bf16[1,64,512]{2,1,0:T...) custom-call(f32[4,2,8,128]{3,2,1,0:T(8,128)S(1)} %get-tuple-element., ...), custom_call_target="tpu_custom_call" | custom-call | tf_op jit(solution)/shard_map/first_sigma_terms/pallas_call | solution.py:251
  5.2 2.5 %collective-permute-start.1 = (bf16[2,64,512]{2,1,0:T(8,128)(2,1)S(1)}, bf16[2,64,512]{2,1,0:T(8,128)(2,1)S(1)}, u32[]{:S(2)}, u32[]{:S(2)}) collective-permute-start(bf16[2,64,512]{2,1,0:T(8,128)(2,1)S(1)} %get-tuple-element.30), channel_id=1, source_target_pairs={{2,0},{0,2},{3,1},{1,3},{6,4},{4,6},{7,5},{5,7},{10,8},{8,10},{11,... | collective-permute-start | bytes 393224 | tf_op jit(solution)/shard_map/ppermute | solution.py:233
  7.7 1.6 %collective-permute-start.3 = (bf16[1,64,512]{2,1,0:T(8,128)(2,1)S(1)}, bf16[1,64,512]{2,1,0:T(8,128)(2,1)S(1)}, u32[]{:S(2)}, u32[]{:S(2)}) collective-permute-start(bf16[1,64,512]{2,1,0:T(8,128)(2,1)S(1)} %get-tuple-element.31), channel_id=1, source_target_pairs={{4,0},{0,4},{12,8},{8,12},{5,1},{1,5},{13,9},{9,13},{6,2},{2,6},{1... | collective-permute-start | bytes 196616 | tf_op jit(solution)/shard_map/ppermute | solution.py:233
  9.3 2.6 %collective-permute-start.4 = (bf16[1,64,512]{2,1,0:T(8,128)(2,1)S(1)}, bf16[1,64,512]{2,1,0:T(8,128)(2,1)S(1)}, u32[]{:S(2)}, u32[]{:S(2)}) collective-permute-start(bf16[1,64,512]{2,1,0:T(8,128)(2,1)S(1)} %get-tuple-element.32), channel_id=1, source_target_pairs={{8,0},{12,4},{0,8},{4,12},{9,1},{13,5},{1,9},{5,13},{10,2},{14,6},... | collective-permute-start | bytes 196616 | tf_op jit(solution)/shard_map/ppermute | solution.py:233
  11.9 0.3 collective-permute-start.5
  12.2 1.4 %collective-permute-start.6 = (bf16[1,64,512]{2,1,0:T(8,128)(2,1)S(1)}, bf16[1,64,512]{2,1,0:T(8,128)(2,1)S(1)}, u32[]{:S(2)}, u32[]{:S(2)}) collective-permute-start(bf16[1,64,512]{2,1,0:T(8,128)(2,1)S(1)} %get-tuple-element.34), channel_id=1, source_target_pairs={{6,0},{4,2},{2,4},{0,6},{14,8},{12,10},{10,12},{8,14},{7,1},{5,3},... | collective-permute-start | bytes 196616 | tf_op jit(solution)/shard_map/ppermute | solution.py:233
  13.5 0.0 collective-permute-done.1.refs_1_
  13.6 3.7 %collective-permute-start.2 = (bf16[1,64,512]{2,1,0:T(8,128)(2,1)S(1)}, bf16[1,64,512]{2,1,0:T(8,128)(2,1)S(1)}, u32[]{:S(2)}, u32[]{:S(2)}) collective-permute-start(bf16[1,64,512]{2,1,0:T(8,128)(2,1)S(1)} %sum_far_share.1), channel_id=1, source_target_pairs={{12,0},{8,4},{4,8},{0,12},{13,1},{9,5},{5,9},{1,13},{14,2},{10,6},... | collective-permute-start | bytes 196616 | tf_op jit(solution)/shard_map/ppermute | solution.py:233
  17.2 0.8 %tables_for_second_sigma.1 = (f32[4,2,8,128]{3,2,1,0:T(8,128)S(1)}, f32[256,512]{1,0:T(8,128)S(1)}) custom-call(s32[2,2]{1,0:T(2,128)S(1)} %copy-done.3, s32[4,2,8]{2,1,0:T(2,128)S(1)} %bitcast.2, f32[4,8]{1,0:T(4,128)S(1)} %copy-done.4, bf16[256,512]{1,0:T(8,128)(2,1)S(1)} %get-tuple-element.35._.wave_other), custom_call_target="tpu_custom_call" | custom-call | tf_op jit(solution)/shard_map/tables_for_second_sigma/pallas_call | solution.py:251
  18.0 0.0 collective-permute-done.3.refs_3_
  18.1 0.0 collective-permute-done.4.refs_4_
  18.1 2.5 %collective-permute-done.5.refs_5_ = bf16[1,64,512]{2,1,0:T(8,128)(2,1)S(1)} collective-permute-done((bf16[1,64,512]{2,1,0:T(8,128)(2,1)S(1)}, bf16[1,64,512]{2,1,0:T(8,128)(2,1)S(1)}, u32[]{:S(2)}, u32[]{:S(2)}) %collective-permute-start.5) | collective-permute-done | bytes 65568 | tf_op jit(solution)/shard_map/ppermute | solution.py:233
  20.5 0.0 collective-permute-done.6.refs_6_
  20.5 0.0 collective-permute-done.2.refs_2_
  20.6 0.1 sum_first_sigma.1.refs_3_
  20.6 2.9 %collective-permute-start.7 = (bf16[1,64,512]{2,1,0:T(8,128)(2,1)S(1)}, bf16[1,64,512]{2,1,0:T(8,128)(2,1)S(1)}, u32[]{:S(2)}, u32[]{:S(2)}) collective-permute-start(bf16[1,64,512]{2,1,0:T(8,128)(2,1)S(1)} %sum_first_sigma.1.refs_3_), channel_id=1, source_target_pairs={{12,0},{8,4},{4,8},{0,12},{13,1},{9,5},{5,9},{1,13},{14,2},{10,6},... | collective-permute-start | bytes 196616 | tf_op jit(solution)/shard_map/ppermute | solution.py:233
  23.5 0.0 collective-permute-start.8
  23.5 1.5 %collective-permute-start.9 = (bf16[1,64,512]{2,1,0:T(8,128)(2,1)S(1)}, bf16[1,64,512]{2,1,0:T(8,128)(2,1)S(1)}, u32[]{:S(2)}, u32[]{:S(2)}) collective-permute-start(bf16[1,64,512]{2,1,0:T(8,128)(2,1)S(1)} %sum_first_sigma.1.refs_3_), channel_id=1, source_target_pairs={{4,0},{0,4},{12,8},{8,12},{5,1},{1,5},{13,9},{9,13},{6,2},{2,6},{1... | collective-permute-start | bytes 196616 | tf_op jit(solution)/shard_map/ppermute | solution.py:233
  25.1 0.5 collective-permute-start.14
  25.5 1.5 %collective-permute-start.15 = (bf16[1,64,512]{2,1,0:T(8,128)(2,1)S(1)}, bf16[1,64,512]{2,1,0:T(8,128)(2,1)S(1)}, u32[]{:S(2)}, u32[]{:S(2)}) collective-permute-start(bf16[1,64,512]{2,1,0:T(8,128)(2,1)S(1)} %sum_first_sigma.1.refs_3_), channel_id=1, source_target_pairs={{2,0},{0,2},{3,1},{1,3},{6,4},{4,6},{7,5},{5,7},{10,8},{8,10},{11,... | collective-permute-start | bytes 196616 | tf_op jit(solution)/shard_map/ppermute | solution.py:233
  27.0 0.4 collective-permute-done.7.refs_0_
  27.5 0.2 collective-permute-start.12
  27.7 1.4 %collective-permute-done.8.refs_1_ = bf16[1,64,512]{2,1,0:T(8,128)(2,1)S(1)} collective-permute-done((bf16[1,64,512]{2,1,0:T(8,128)(2,1)S(1)}, bf16[1,64,512]{2,1,0:T(8,128)(2,1)S(1)}, u32[]{:S(2)}, u32[]{:S(2)}) %collective-permute-start.8) | collective-permute-done | bytes 65568 | tf_op jit(solution)/shard_map/ppermute | solution.py:233
  29.1 0.7 %collective-permute-start.13 = (bf16[1,64,512]{2,1,0:T(8,128)(2,1)S(1)}, bf16[1,64,512]{2,1,0:T(8,128)(2,1)S(1)}, u32[]{:S(2)}, u32[]{:S(2)}) collective-permute-start(bf16[1,64,512]{2,1,0:T(8,128)(2,1)S(1)} %collective-permute-done.8.refs_1_), channel_id=1, source_target_pairs={{2,0},{0,2},{3,1},{1,3},{6,4},{4,6},{7,5},{5,7},{10,8},{8,10},{11,... | collective-permute-start | bytes 196616 | tf_op jit(solution)/shard_map/ppermute | solution.py:233
  29.8 0.0 collective-permute-done.9.refs_2_
  29.9 0.1 collective-permute-start.10
  29.9 0.4 collective-permute-done.14.refs_2_
  30.3 0.3 collective-permute-done.15.refs_3_
  30.7 1.2 %collective-permute-done.12.refs_0_ = bf16[1,64,512]{2,1,0:T(8,128)(2,1)S(1)} collective-permute-done((bf16[1,64,512]{2,1,0:T(8,128)(2,1)S(1)}, bf16[1,64,512]{2,1,0:T(8,128)(2,1)S(1)}, u32[]{:S(2)}, u32[]{:S(2)}) %collective-permute-start.12) | collective-permute-done | bytes 65568 | tf_op jit(solution)/shard_map/ppermute | solution.py:233
  31.9 1.5 %collective-permute-done.13.refs_1_ = bf16[1,64,512]{2,1,0:T(8,128)(2,1)S(1)} collective-permute-done((bf16[1,64,512]{2,1,0:T(8,128)(2,1)S(1)}, bf16[1,64,512]{2,1,0:T(8,128)(2,1)S(1)}, u32[]{:S(2)}, u32[]{:S(2)}) %collective-permute-start.13) | collective-permute-done | bytes 65568 | tf_op jit(solution)/shard_map/ppermute | solution.py:233
  33.4 0.1 collective-permute-start.16
  33.5 0.0 collective-permute-done.10.sigma_other.other
  33.5 1.0 %left_products.1 = (f32[4,256,512]{2,1,0:T(8,128)S(1)}, f32[1,4,256,512]{3,2,1,0:T(8,128)S(1)}) custom-call(bf16[4,256,256]{2,1,0:T(8,128)(2,1)S(1)} %get-tuple-element.24._.refs_2_.left_own, bf16[4,256,256]{2,1,0:T(8,128)(2,1)S(1)} %get-tuple-element.28.refs_3_.left_other, bf16[1,256,512]{2,1,0:T(8,128)(2,1)S(1)} %place_own_sector.1.sigma_own.own, ...), custom_call_target="tpu_custom_call" | custom-call | tf_op jit(solution)/shard_map/left_products/pallas_call | solution.py:251
  34.5 0.5 collective-permute-done.16.other
  35.0 1.1 %second_sigma_terms.1 = (f32[1,64,512]{2,1,0:T(8,128)S(1)}, bf16[1,64,512]{2,1,0:T(8,128)(2,1)S(1)}, bf16[1,64,512]{2,1,0:T(8,128)(2,1)S(1)}, bf16[1,64,512]{2,1,0:T(8,128)(2,1)S(1)}) custom-call(f32[4,2,8,128]{3,2,1,0:T(8,128)S(1)} %get-tuple-element.36.refs_7_.mixing, f32[256,512]{1,0:T(8,128)S(1)} %get-tuple-element.39.live, ...), custom_call_target="tpu_custom_call" | custom-call | tf_op jit(solution)/shard_map/second_sigma_terms/pallas_call | solution.py:251
  36.2 2.0 %collective-permute-start.17 = (bf16[1,64,512]{2,1,0:T(8,128)(2,1)S(1)}, bf16[1,64,512]{2,1,0:T(8,128)(2,1)S(1)}, u32[]{:S(2)}, u32[]{:S(2)}) collective-permute-start(bf16[1,64,512]{2,1,0:T(8,128)(2,1)S(1)} %get-tuple-element.43), channel_id=1, source_target_pairs={{12,0},{8,4},{4,8},{0,12},{13,1},{9,5},{5,9},{1,13},{14,2},{10,6},... | collective-permute-start | bytes 196616 | tf_op jit(solution)/shard_map/ppermute | solution.py:233
  38.2 0.0 collective-permute-start.18
  38.2 2.4 %collective-permute-start.19 = (bf16[1,64,512]{2,1,0:T(8,128)(2,1)S(1)}, bf16[1,64,512]{2,1,0:T(8,128)(2,1)S(1)}, u32[]{:S(2)}, u32[]{:S(2)}) collective-permute-start(bf16[1,64,512]{2,1,0:T(8,128)(2,1)S(1)} %get-tuple-element.45), channel_id=1, source_target_pairs={{4,0},{0,4},{12,8},{8,12},{5,1},{1,5},{13,9},{9,13},{6,2},{2,6},{1... | collective-permute-start | bytes 196616 | tf_op jit(solution)/shard_map/ppermute | solution.py:233
  40.6 0.5 sums_for_rayleigh.1.refs_0_.refs_4_
  41.1 0.8 %collective-permute-start.11 = (f32[3,8,128]{2,1,0:T(8,128)S(1)}, f32[3,8,128]{2,1,0:T(8,128)S(1)}, u32[]{:S(2)}, u32[]{:S(2)}) collective-permute-start(f32[3,8,128]{2,1,0:T(8,128)S(1)} %sums_for_rayleigh.1.refs_0_.refs_4_), channel_id=1, source_target_pairs={{2,0},{0,2},{3,1},{1,3},{6,4},{4,6},{7,5},{5,7},{10,8},{8,10},{11,... | collective-permute-start | bytes 36872 | tf_op jit(solution)/shard_map/ppermute | solution.py:233
  41.9 3.0 %collective-permute-done.11.refs_1_.refs_5_ = f32[3,8,128]{2,1,0:T(8,128)S(1)} collective-permute-done((f32[3,8,128]{2,1,0:T(8,128)S(1)}, f32[3,8,128]{2,1,0:T(8,128)S(1)}, u32[]{:S(2)}, u32[]{:S(2)}) %collective-permute-start.11) | collective-permute-done | bytes 12320 | tf_op jit(solution)/shard_map/ppermute | solution.py:233
  44.9 0.0 collective-permute-done.17.refs_1_
  44.9 0.1 collective-permute-done.18.refs_2_
  45.0 0.0 collective-permute-done.19.refs_3_
  45.0 2.2 %collective-permute-start.20 = (bf16[1,64,512]{2,1,0:T(8,128)(2,1)S(1)}, bf16[1,64,512]{2,1,0:T(8,128)(2,1)S(1)}, u32[]{:S(2)}, u32[]{:S(2)}) collective-permute-start(bf16[1,64,512]{2,1,0:T(8,128)(2,1)S(1)} %sum_second_sigma.1.refs_3_), channel_id=1, source_target_pairs={{12,0},{8,4},{4,8},{0,12},{13,1},{9,5},{5,9},{1,13},{14,2},{10,6},... | collective-permute-start | bytes 196616 | tf_op jit(solution)/shard_map/ppermute | solution.py:233
  47.2 0.0 collective-permute-start.21
  47.2 2.2 %collective-permute-start.22 = (bf16[1,64,512]{2,1,0:T(8,128)(2,1)S(1)}, bf16[1,64,512]{2,1,0:T(8,128)(2,1)S(1)}, u32[]{:S(2)}, u32[]{:S(2)}) collective-permute-start(bf16[1,64,512]{2,1,0:T(8,128)(2,1)S(1)} %sum_second_sigma.1.refs_3_), channel_id=1, source_target_pairs={{4,0},{0,4},{12,8},{8,12},{5,1},{1,5},{13,9},{9,13},{6,2},{2,6},{1... | collective-permute-start | bytes 196616 | tf_op jit(solution)/shard_map/ppermute | solution.py:233
  49.5 1.4 %second_wave.1 = (bf16[1,256,512]{2,1,0:T(8,128)(2,1)}, f32[2,8,128]{2,1,0:T(8,128)S(1)}) custom-call(s32[2,2]{1,0:T(2,128)S(1)} %copy-done.3, bf16[256,512]{1,0:T(8,128)(2,1)S(1)} %get-tuple-element.25.refs_5_.wave_own, bf16[1,256,512]{2,1,0:T(8,128)(2,1)S(1)} %place_own_sector.1.sigma_own.own, f32[3,8,128]{2,1,0:T(8,128)S(1)} %sums_for_rayleigh.1.refs_0_.refs_4_, ...), custom_call_target="tpu_custom_call" | custom-call | tf_op jit(solution)/shard_map/second_wave/pallas_call | solution.py:251
  50.9 0.8 %collective-permute-done.20.refs_0_ = bf16[1,64,512]{2,1,0:T(8,128)(2,1)S(1)} collective-permute-done((bf16[1,64,512]{2,1,0:T(8,128)(2,1)S(1)}, bf16[1,64,512]{2,1,0:T(8,128)(2,1)S(1)}, u32[]{:S(2)}, u32[]{:S(2)}) %collective-permute-start.20) | collective-permute-done | bytes 65568 | tf_op jit(solution)/shard_map/ppermute | solution.py:233
  51.7 2.0 %collective-permute-done.21.refs_1_ = bf16[1,64,512]{2,1,0:T(8,128)(2,1)S(1)} collective-permute-done((bf16[1,64,512]{2,1,0:T(8,128)(2,1)S(1)}, bf16[1,64,512]{2,1,0:T(8,128)(2,1)S(1)}, u32[]{:S(2)}, u32[]{:S(2)}) %collective-permute-start.21) | collective-permute-done | bytes 65568 | tf_op jit(solution)/shard_map/ppermute | solution.py:233
  53.7 0.0 collective-permute-done.22.refs_2_
  53.7 0.9 %join_second_sigma.1 = f32[1,256,512]{2,1,0:T(8,128)} custom-call(f32[2,8,128]{2,1,0:T(8,128)S(1)} %get-tuple-element.38.factors, bf16[1,256,512]{2,1,0:T(8,128)(2,1)S(1)} %place_own_sector.1.sigma_own.own, bf16[1,64,512]{2,1,0:T(8,128)(2,1)S(1)} %collective-permute-done.20.refs_0_, bf16[1,64,512]{2,1,0:T(8,128)(2,1)S(1)} %collective-permute-done.21.refs_1_, ...), custom_call_target="tpu_custom_call" | custom-call | tf_op jit(solution)/shard_map/join_second_sigma/pallas_call | solution.py:251
  (6 shorter events, 0.1 us)
Async XLA Ops:
  0.6 2.0 %copy-start.1 = (bf16[1,256,512]{2,1,0:T(8,128)(2,1)S(1)}, bf16[1,256,512]{2,1,0:T(8,128)(2,1)}, u32[]{:S(2)}) copy-start(bf16[1,256,512]{2,1,0:T(8,128)(2,1)} %wave.1) | copy-start | bytes 786436
  0.6 2.0 %copy-start.3 = (s32[2,2]{1,0:T(2,128)S(1)}, s32[2,2]{1,0:T(2,128)}, u32[]{:S(2)}) copy-start(s32[2,2]{1,0:T(2,128)} %sizes_ref.5) | copy-start | bytes 52
  0.7 2.0 %copy-start.2 = (s32[4,8,2]{1,2,0:T(2,128)S(1)}, s32[4,8,2]{1,2,0:T(2,128)}, u32[]{:S(2)}) copy-start(s32[4,8,2]{1,2,0:T(2,128)} %param.10) | copy-start | bytes 772
  0.7 2.0 %copy-start.4 = (f32[4,8]{1,0:T(4,128)S(1)}, f32[4,8]{1,0:T(4,128)}, u32[]{:S(2)}) copy-start(f32[4,8]{1,0:T(4,128)} %weights_ref.3) | copy-start | bytes 388
  0.7 3.0 %copy-start = (bf16[4,512,512]{2,1,0:T(8,128)(2,1)S(1)}, bf16[4,512,512]{2,1,0:T(8,128)(2,1)}, u32[]{:S(2)}) copy-start(bf16[4,512,512]{2,1,0:T(8,128)(2,1)} %right.1) | copy-start | bytes 6291460
  0.7 3.0 %collective-permute-start = (bf16[1,256,512]{2,1,0:T(8,128)(2,1)}, bf16[1,256,512]{2,1,0:T(8,128)(2,1)S(1)}, u32[]{:S(2)}, u32[]{:S(2)}) collective-permute-start(bf16[1,256,512]{2,1,0:T(8,128)(2,1)} %wave.1), channel_id=1, source_target_pairs={{1,0},{0,1},{3,2},{2,3},{5,4},{4,5},{7,6},{6,7},{9,8},{8,9},{11,10... | collective-permute-start | bytes 786440 | tf_op jit(solution)/shard_map/ppermute | solution.py:233
  5.2 8.4 %collective-permute-start.1 = (bf16[2,64,512]{2,1,0:T(8,128)(2,1)S(1)}, bf16[2,64,512]{2,1,0:T(8,128)(2,1)S(1)}, u32[]{:S(2)}, u32[]{:S(2)}) collective-permute-start(bf16[2,64,512]{2,1,0:T(8,128)(2,1)S(1)} %get-tuple-element.30), channel_id=1, source_target_pairs={{2,0},{0,2},{3,1},{1,3},{6,4},{4,6},{7,5},{5,7},{10,8},{8,10},{11,... | collective-permute-start | bytes 393224 | tf_op jit(solution)/shard_map/ppermute | solution.py:233
  7.7 10.4 %collective-permute-start.3 = (bf16[1,64,512]{2,1,0:T(8,128)(2,1)S(1)}, bf16[1,64,512]{2,1,0:T(8,128)(2,1)S(1)}, u32[]{:S(2)}, u32[]{:S(2)}) collective-permute-start(bf16[1,64,512]{2,1,0:T(8,128)(2,1)S(1)} %get-tuple-element.31), channel_id=1, source_target_pairs={{4,0},{0,4},{12,8},{8,12},{5,1},{1,5},{13,9},{9,13},{6,2},{2,6},{1... | collective-permute-start | bytes 196616 | tf_op jit(solution)/shard_map/ppermute | solution.py:233
  9.3 8.8 %collective-permute-start.4 = (bf16[1,64,512]{2,1,0:T(8,128)(2,1)S(1)}, bf16[1,64,512]{2,1,0:T(8,128)(2,1)S(1)}, u32[]{:S(2)}, u32[]{:S(2)}) collective-permute-start(bf16[1,64,512]{2,1,0:T(8,128)(2,1)S(1)} %get-tuple-element.32), channel_id=1, source_target_pairs={{8,0},{12,4},{0,8},{4,12},{9,1},{13,5},{1,9},{5,13},{10,2},{14,6},... | collective-permute-start | bytes 196616 | tf_op jit(solution)/shard_map/ppermute | solution.py:233
  11.9 8.7 %collective-permute-start.5 = (bf16[1,64,512]{2,1,0:T(8,128)(2,1)S(1)}, bf16[1,64,512]{2,1,0:T(8,128)(2,1)S(1)}, u32[]{:S(2)}, u32[]{:S(2)}) collective-permute-start(bf16[1,64,512]{2,1,0:T(8,128)(2,1)S(1)} %get-tuple-element.33), channel_id=1, source_target_pairs={{10,0},{8,2},{14,4},{12,6},{2,8},{0,10},{6,12},{4,14},{11,1},{9,3}... | collective-permute-start | bytes 196616 | tf_op jit(solution)/shard_map/ppermute | solution.py:233
  12.2 8.4 %collective-permute-start.6 = (bf16[1,64,512]{2,1,0:T(8,128)(2,1)S(1)}, bf16[1,64,512]{2,1,0:T(8,128)(2,1)S(1)}, u32[]{:S(2)}, u32[]{:S(2)}) collective-permute-start(bf16[1,64,512]{2,1,0:T(8,128)(2,1)S(1)} %get-tuple-element.34), channel_id=1, source_target_pairs={{6,0},{4,2},{2,4},{0,6},{14,8},{12,10},{10,12},{8,14},{7,1},{5,3},... | collective-permute-start | bytes 196616 | tf_op jit(solution)/shard_map/ppermute | solution.py:233
  13.6 7.0 %collective-permute-start.2 = (bf16[1,64,512]{2,1,0:T(8,128)(2,1)S(1)}, bf16[1,64,512]{2,1,0:T(8,128)(2,1)S(1)}, u32[]{:S(2)}, u32[]{:S(2)}) collective-permute-start(bf16[1,64,512]{2,1,0:T(8,128)(2,1)S(1)} %sum_far_share.1), channel_id=1, source_target_pairs={{12,0},{8,4},{4,8},{0,12},{13,1},{9,5},{5,9},{1,13},{14,2},{10,6},... | collective-permute-start | bytes 196616 | tf_op jit(solution)/shard_map/ppermute | solution.py:233
  20.6 6.8 %collective-permute-start.7 = (bf16[1,64,512]{2,1,0:T(8,128)(2,1)S(1)}, bf16[1,64,512]{2,1,0:T(8,128)(2,1)S(1)}, u32[]{:S(2)}, u32[]{:S(2)}) collective-permute-start(bf16[1,64,512]{2,1,0:T(8,128)(2,1)S(1)} %sum_first_sigma.1.refs_3_), channel_id=1, source_target_pairs={{12,0},{8,4},{4,8},{0,12},{13,1},{9,5},{5,9},{1,13},{14,2},{10,6},... | collective-permute-start | bytes 196616 | tf_op jit(solution)/shard_map/ppermute | solution.py:233
  23.5 5.6 %collective-permute-start.8 = (bf16[1,64,512]{2,1,0:T(8,128)(2,1)S(1)}, bf16[1,64,512]{2,1,0:T(8,128)(2,1)S(1)}, u32[]{:S(2)}, u32[]{:S(2)}) collective-permute-start(bf16[1,64,512]{2,1,0:T(8,128)(2,1)S(1)} %sum_first_sigma.1.refs_3_), channel_id=1, source_target_pairs={{8,0},{12,4},{0,8},{4,12},{9,1},{13,5},{1,9},{5,13},{10,2},{14,6},... | collective-permute-start | bytes 196616 | tf_op jit(solution)/shard_map/ppermute | solution.py:233
  23.5 6.3 %collective-permute-start.9 = (bf16[1,64,512]{2,1,0:T(8,128)(2,1)S(1)}, bf16[1,64,512]{2,1,0:T(8,128)(2,1)S(1)}, u32[]{:S(2)}, u32[]{:S(2)}) collective-permute-start(bf16[1,64,512]{2,1,0:T(8,128)(2,1)S(1)} %sum_first_sigma.1.refs_3_), channel_id=1, source_target_pairs={{4,0},{0,4},{12,8},{8,12},{5,1},{1,5},{13,9},{9,13},{6,2},{2,6},{1... | collective-permute-start | bytes 196616 | tf_op jit(solution)/shard_map/ppermute | solution.py:233
  25.1 5.3 %collective-permute-start.14 = (bf16[1,64,512]{2,1,0:T(8,128)(2,1)S(1)}, bf16[1,64,512]{2,1,0:T(8,128)(2,1)S(1)}, u32[]{:S(2)}, u32[]{:S(2)}) collective-permute-start(bf16[1,64,512]{2,1,0:T(8,128)(2,1)S(1)} %sum_first_sigma.1.refs_3_), channel_id=1, source_target_pairs={{6,0},{4,2},{2,4},{0,6},{14,8},{12,10},{10,12},{8,14},{7,1},{5,3},... | collective-permute-start | bytes 196616 | tf_op jit(solution)/shard_map/ppermute | solution.py:233
  25.5 5.1 %collective-permute-start.15 = (bf16[1,64,512]{2,1,0:T(8,128)(2,1)S(1)}, bf16[1,64,512]{2,1,0:T(8,128)(2,1)S(1)}, u32[]{:S(2)}, u32[]{:S(2)}) collective-permute-start(bf16[1,64,512]{2,1,0:T(8,128)(2,1)S(1)} %sum_first_sigma.1.refs_3_), channel_id=1, source_target_pairs={{2,0},{0,2},{3,1},{1,3},{6,4},{4,6},{7,5},{5,7},{10,8},{8,10},{11,... | collective-permute-start | bytes 196616 | tf_op jit(solution)/shard_map/ppermute | solution.py:233
  27.5 4.5 %collective-permute-start.12 = (bf16[1,64,512]{2,1,0:T(8,128)(2,1)S(1)}, bf16[1,64,512]{2,1,0:T(8,128)(2,1)S(1)}, u32[]{:S(2)}, u32[]{:S(2)}) collective-permute-start(bf16[1,64,512]{2,1,0:T(8,128)(2,1)S(1)} %collective-permute-done.7.refs_0_), channel_id=1, source_target_pairs={{2,0},{0,2},{3,1},{1,3},{6,4},{4,6},{7,5},{5,7},{10,8},{8,10},{11,... | collective-permute-start | bytes 196616 | tf_op jit(solution)/shard_map/ppermute | solution.py:233
  29.1 4.3 %collective-permute-start.13 = (bf16[1,64,512]{2,1,0:T(8,128)(2,1)S(1)}, bf16[1,64,512]{2,1,0:T(8,128)(2,1)S(1)}, u32[]{:S(2)}, u32[]{:S(2)}) collective-permute-start(bf16[1,64,512]{2,1,0:T(8,128)(2,1)S(1)} %collective-permute-done.8.refs_1_), channel_id=1, source_target_pairs={{2,0},{0,2},{3,1},{1,3},{6,4},{4,6},{7,5},{5,7},{10,8},{8,10},{11,... | collective-permute-start | bytes 196616 | tf_op jit(solution)/shard_map/ppermute | solution.py:233
  29.9 3.7 %collective-permute-start.10 = (bf16[1,256,512]{2,1,0:T(8,128)(2,1)S(1)}, bf16[1,256,512]{2,1,0:T(8,128)(2,1)S(1)}, u32[]{:S(2)}, u32[]{:S(2)}) collective-permute-start(bf16[1,256,512]{2,1,0:T(8,128)(2,1)S(1)} %place_own_sector.1.sigma_own.own), channel_id=1, source_target_pairs={{1,0},{0,1},{3,2},{2,3},{5,4},{4,5},{7,6},{6,7},{9,8},{8,9},{11,10... | collective-permute-start | bytes 786440 | tf_op jit(solution)/shard_map/ppermute | solution.py:233
  33.4 1.6 %collective-permute-start.16 = (bf16[1,256,512]{2,1,0:T(8,128)(2,1)S(1)}, bf16[1,256,512]{2,1,0:T(8,128)(2,1)S(1)}, u32[]{:S(2)}, u32[]{:S(2)}) collective-permute-start(bf16[1,256,512]{2,1,0:T(8,128)(2,1)S(1)} %place_other_sectors.1.across_own), channel_id=1, source_target_pairs={{1,0},{0,1},{3,2},{2,3},{5,4},{4,5},{7,6},{6,7},{9,8},{8,9},{11,10... | collective-permute-start | bytes 786440 | tf_op jit(solution)/shard_map/ppermute | solution.py:233
  36.2 8.7 %collective-permute-start.17 = (bf16[1,64,512]{2,1,0:T(8,128)(2,1)S(1)}, bf16[1,64,512]{2,1,0:T(8,128)(2,1)S(1)}, u32[]{:S(2)}, u32[]{:S(2)}) collective-permute-start(bf16[1,64,512]{2,1,0:T(8,128)(2,1)S(1)} %get-tuple-element.43), channel_id=1, source_target_pairs={{12,0},{8,4},{4,8},{0,12},{13,1},{9,5},{5,9},{1,13},{14,2},{10,6},... | collective-permute-start | bytes 196616 | tf_op jit(solution)/shard_map/ppermute | solution.py:233
  38.2 6.8 %collective-permute-start.18 = (bf16[1,64,512]{2,1,0:T(8,128)(2,1)S(1)}, bf16[1,64,512]{2,1,0:T(8,128)(2,1)S(1)}, u32[]{:S(2)}, u32[]{:S(2)}) collective-permute-start(bf16[1,64,512]{2,1,0:T(8,128)(2,1)S(1)} %get-tuple-element.44), channel_id=1, source_target_pairs={{8,0},{12,4},{0,8},{4,12},{9,1},{13,5},{1,9},{5,13},{10,2},{14,6},... | collective-permute-start | bytes 196616 | tf_op jit(solution)/shard_map/ppermute | solution.py:233
  38.2 6.8 %collective-permute-start.19 = (bf16[1,64,512]{2,1,0:T(8,128)(2,1)S(1)}, bf16[1,64,512]{2,1,0:T(8,128)(2,1)S(1)}, u32[]{:S(2)}, u32[]{:S(2)}) collective-permute-start(bf16[1,64,512]{2,1,0:T(8,128)(2,1)S(1)} %get-tuple-element.45), channel_id=1, source_target_pairs={{4,0},{0,4},{12,8},{8,12},{5,1},{1,5},{13,9},{9,13},{6,2},{2,6},{1... | collective-permute-start | bytes 196616 | tf_op jit(solution)/shard_map/ppermute | solution.py:233
  41.1 3.8 %collective-permute-start.11 = (f32[3,8,128]{2,1,0:T(8,128)S(1)}, f32[3,8,128]{2,1,0:T(8,128)S(1)}, u32[]{:S(2)}, u32[]{:S(2)}) collective-permute-start(f32[3,8,128]{2,1,0:T(8,128)S(1)} %sums_for_rayleigh.1.refs_0_.refs_4_), channel_id=1, source_target_pairs={{2,0},{0,2},{3,1},{1,3},{6,4},{4,6},{7,5},{5,7},{10,8},{8,10},{11,... | collective-permute-start | bytes 36872 | tf_op jit(solution)/shard_map/ppermute | solution.py:233
  45.0 6.7 %collective-permute-start.20 = (bf16[1,64,512]{2,1,0:T(8,128)(2,1)S(1)}, bf16[1,64,512]{2,1,0:T(8,128)(2,1)S(1)}, u32[]{:S(2)}, u32[]{:S(2)}) collective-permute-start(bf16[1,64,512]{2,1,0:T(8,128)(2,1)S(1)} %sum_second_sigma.1.refs_3_), channel_id=1, source_target_pairs={{12,0},{8,4},{4,8},{0,12},{13,1},{9,5},{5,9},{1,13},{14,2},{10,6},... | collective-permute-start | bytes 196616 | tf_op jit(solution)/shard_map/ppermute | solution.py:233
  47.2 6.5 %collective-permute-start.21 = (bf16[1,64,512]{2,1,0:T(8,128)(2,1)S(1)}, bf16[1,64,512]{2,1,0:T(8,128)(2,1)S(1)}, u32[]{:S(2)}, u32[]{:S(2)}) collective-permute-start(bf16[1,64,512]{2,1,0:T(8,128)(2,1)S(1)} %sum_second_sigma.1.refs_3_), channel_id=1, source_target_pairs={{8,0},{12,4},{0,8},{4,12},{9,1},{13,5},{1,9},{5,13},{10,2},{14,6},... | collective-permute-start | bytes 196616 | tf_op jit(solution)/shard_map/ppermute | solution.py:233
  47.2 6.5 %collective-permute-start.22 = (bf16[1,64,512]{2,1,0:T(8,128)(2,1)S(1)}, bf16[1,64,512]{2,1,0:T(8,128)(2,1)S(1)}, u32[]{:S(2)}, u32[]{:S(2)}) collective-permute-start(bf16[1,64,512]{2,1,0:T(8,128)(2,1)S(1)} %sum_second_sigma.1.refs_3_), channel_id=1, source_target_pairs={{4,0},{0,4},{12,8},{8,12},{5,1},{1,5},{13,9},{9,13},{6,2},{2,6},{1... | collective-permute-start | bytes 196616 | tf_op jit(solution)/shard_map/ppermute | solution.py:233

commit v14 on v13

--- a/solution.py
+++ b/solution.py
@@ -60,41 +60,49 @@
         copy.wait()
 
 
-def first_tables_kernel(sizes_ref, pairs_ref, weights_ref, wave, _, own, mixing, live):
+def live_rows(sizes, sector, row_start, rows, columns):
+    bounds = sizes[pl.ds(sector, 1), :]
+    row = row_start + lax.broadcasted_iota(jnp.int32, (rows, columns), 0)
+    column = lax.broadcasted_iota(jnp.int32, (rows, columns), 1)
+    inside = (row < bounds[:, 0:1]) & (column < bounds[:, 1:2])
+    return jnp.where(inside, 1.0, 0.0)
+
+
+def first_tables_kernel(sizes, pairs, weights, wave, _, own, mixing):
     rows, columns = own.shape
     sector = lax.axis_index("sec")
-    start = lax.axis_index("rep") * rows
-    for term in range(mixing.shape[0]):
-        for step in range(mixing.shape[1]):
-            weight = mixing_scalar(pairs_ref, weights_ref, term, sector ^ step, sector)
-            mixing[term, step] = jnp.full(mixing.shape[2:], weight, jnp.float32)
-    for step in range(live.shape[0] - 1):
-        cells = live_cells(sizes_ref, sector ^ step, start, rows, columns)
-        live[step] = jnp.where(cells, 1.0, 0.0)
-    own[...] = (wave[0].astype(jnp.float32) * live[0]).astype(own.dtype)
-    start = (lax.axis_index("rep") ^ 1) * rows
-    cells = live_cells(sizes_ref, sector, start, rows, columns)
-    live[live.shape[0] - 1] = jnp.where(cells, 1.0, 0.0)
+    live = live_rows(sizes, sector, lax.axis_index("rep") * rows, rows, columns)
+    own[...] = (wave[0].astype(jnp.float32) * live).astype(own.dtype)
+    source, target = pairs[:, 0, :], pairs[:, 1, :]
+    for step in range(mixing.shape[0]):
+        hits = (source == sector) & (target == (sector ^ step))
+        total = jnp.sum(jnp.where(hits, weights[...], 0.0), axis=1, keepdims=True)
+        mixing[step] = jnp.broadcast_to(total, mixing.shape[1:])
 
 
 def first_kernel(shares, *refs):
-    mixing, live, left_own, left_other, right, own, arrived = refs[:7]
+    sizes, mixing, left_own, left_other, right, own, arrived = refs[:7]
     other, *parts = refs[7:-1]
     held = refs[-1]
     rows, columns = own.shape
     share = parts[0].shape[-2]
     sectors = held.shape[0]
+    sector = lax.axis_index("sec")
+    core = lax.axis_index("rep")
     place = lax.axis_index("ops")
-    other[...] = (arrived[0].astype(jnp.float32) * live[sectors]).astype(other.dtype)
+    live = live_rows(sizes, sector, (core ^ 1) * rows, rows, columns)
+    other[...] = (arrived[0].astype(jnp.float32) * live).astype(other.dtype)
     products = left_times((left_own, left_other), (own[...], other[...]))
     totals = [None] * sectors
     for term in range(right.shape[0]):
         product = times_right(products[term], right, term)
         for step in range(sectors):
-            part = jnp.broadcast_to(mixing[term, step][:1, :1], (rows, columns)) * product
+            weight = jnp.broadcast_to(mixing[step][term : term + 1, :1], (rows, columns))
+            part = weight * product
             totals[step] = part if totals[step] is None else totals[step] + part
     for step in range(sectors):
-        held[step] = totals[step] * live[step]
+        live = live_rows(sizes, sector ^ step, core * rows, rows, columns)
+        held[step] = totals[step] * live
     for (steps, across), out in zip(shares, parts):
         for index, along in enumerate(steps):
             start = pl.multiple_of((place ^ along) * share, share)
@@ -289,15 +297,11 @@
     direct = [(along,) for along in farthest_first[1:-1]]
     spots = [((far, 0), across) for across in range(sectors)]
     spots += [(along, across) for along in direct for across in range(sectors)]
-    wave_own, mixing, live = call(
+    wave_own, mixing = call(
         first_tables_kernel,
         "tables_for_first_sigma",
-        [
-            shape(rows, columns),
-            shape(terms, sectors, 8, 128, dtype=f32),
-            shape(sectors + 1, rows, columns, dtype=f32),
-        ],
-        [smem] * 3,
+        [shape(rows, columns), shape(sectors, terms, 128, dtype=f32)],
+        [],
         *scalars,
         wavefunction,
         left_own,
@@ -311,8 +315,8 @@
             for along, across in spots
         ],
         [],
+        sector_sizes,
         mixing,
-        live,
         left_own,
         left_other,
         right,

time: 54.7 us -> 54.2 us (level)
  Pallas kernels: 9.76 us -> 9.18 us
    pallas_call x14, Pallas kernels: 9.76 us -> 9.18 us  [call(): pl.pallas_call(kernel, out_shape=out_shape, in_specs=list(in_specs) + [in...]
  transfers between devices with their start and end apart: 23 -> 23, of which waited for: 12 -> 12; matrix products, arithmetic and copies ran while one was open for 0% -> 0% of each run, Pallas kernels for 11% -> 10%
where the time goes in v14:
time: 54.2 us; the launch traced here: 54.1 us
  starting transfers between devices  30.2 us (56%)
  waiting for transfers between devices  13.9 us (26%)
  Pallas kernels  9.18 us (17%)
  between operations  0.85 us (2%)
    ppermute x23, starting transfers between devices, partner(): return lax.ppermute(value, axes, pairs)  30.2 us
    ppermute x23, waiting for transfers between devices, partner(): return lax.ppermute(value, axes, pairs)  13.9 us
    pallas_call x14, Pallas kernels, call(): pl.pallas_call(kernel, out_shape=out_shape, in_specs=list(in_specs) + [in...  9.18 us
  transfers between devices with their start and end apart: 23, of which 12 were waited for; matrix products, arithmetic and copies ran while one was open for 0% of the time, Pallas kernels for 10%

profile of v14, /device:TPU:0, one launch (start us, length us, event | category | flops | bytes accessed | tf_op | source)
XLA Modules:
  0.0 54.1 jit_solution(16411060833203575879)
XLA Ops:
  0.6 0.0 copy-start.1
  0.6 0.0 copy-start.3
  0.7 0.0 copy-start.2
  0.7 0.0 copy-start.4
  0.7 0.0 copy-start
  0.7 0.5 collective-permute-start
  1.2 1.4 %load_operators.1 = (bf16[4,256,256]{2,1,0:T(8,128)(2,1)S(1)}, bf16[4,256,256]{2,1,0:T(8,128)(2,1)S(1)}) custom-call(bf16[4,512,512]{2,1,0:T(8,128)(2,1)} %left_ref.1), custom_call_target="tpu_custom_call" | custom-call | tf_op jit(solution)/shard_map/load_operators/pallas_call | solution.py:259
  2.6 0.0 copy-done.1
  2.6 0.0 copy-done.3
  2.7 0.0 copy-done.2
  2.7 0.2 tables_for_first_sigma.1
  2.9 0.0 collective-permute-done.refs_6_
  2.9 1.7 %first_sigma_terms.1 = (bf16[256,512]{1,0:T(8,128)(2,1)S(1)}, f32[2,64,512]{2,1,0:T(8,128)S(1)}, bf16[2,64,512]{2,1,0:T(8,128)(2,1)S(1)}, bf16[1,64,512]{2,1,0:T...) custom-call(s32[2,2]{1,0:T(2,128)S(1)} %copy-done.3, ...), custom_call_target="tpu_custom_call" | custom-call | tf_op jit(solution)/shard_map/first_sigma_terms/pallas_call | solution.py:259
  4.6 2.8 %collective-permute-start.1 = (bf16[2,64,512]{2,1,0:T(8,128)(2,1)S(1)}, bf16[2,64,512]{2,1,0:T(8,128)(2,1)S(1)}, u32[]{:S(2)}, u32[]{:S(2)}) collective-permute-start(bf16[2,64,512]{2,1,0:T(8,128)(2,1)S(1)} %get-tuple-element.28), channel_id=1, source_target_pairs={{2,0},{0,2},{3,1},{1,3},{6,4},{4,6},{7,5},{5,7},{10,8},{8,10},{11,... | collective-permute-start | bytes 393224 | tf_op jit(solution)/shard_map/ppermute | solution.py:241
  7.4 1.6 %collective-permute-start.3 = (bf16[1,64,512]{2,1,0:T(8,128)(2,1)S(1)}, bf16[1,64,512]{2,1,0:T(8,128)(2,1)S(1)}, u32[]{:S(2)}, u32[]{:S(2)}) collective-permute-start(bf16[1,64,512]{2,1,0:T(8,128)(2,1)S(1)} %get-tuple-element.29), channel_id=1, source_target_pairs={{4,0},{0,4},{12,8},{8,12},{5,1},{1,5},{13,9},{9,13},{6,2},{2,6},{1... | collective-permute-start | bytes 196616 | tf_op jit(solution)/shard_map/ppermute | solution.py:241
  9.0 2.6 %collective-permute-start.4 = (bf16[1,64,512]{2,1,0:T(8,128)(2,1)S(1)}, bf16[1,64,512]{2,1,0:T(8,128)(2,1)S(1)}, u32[]{:S(2)}, u32[]{:S(2)}) collective-permute-start(bf16[1,64,512]{2,1,0:T(8,128)(2,1)S(1)} %get-tuple-element.30), channel_id=1, source_target_pairs={{8,0},{12,4},{0,8},{4,12},{9,1},{13,5},{1,9},{5,13},{10,2},{14,6},... | collective-permute-start | bytes 196616 | tf_op jit(solution)/shard_map/ppermute | solution.py:241
  11.5 0.3 collective-permute-start.5
  11.8 1.4 %collective-permute-start.6 = (bf16[1,64,512]{2,1,0:T(8,128)(2,1)S(1)}, bf16[1,64,512]{2,1,0:T(8,128)(2,1)S(1)}, u32[]{:S(2)}, u32[]{:S(2)}) collective-permute-start(bf16[1,64,512]{2,1,0:T(8,128)(2,1)S(1)} %get-tuple-element.32), channel_id=1, source_target_pairs={{6,0},{4,2},{2,4},{0,6},{14,8},{12,10},{10,12},{8,14},{7,1},{5,3},... | collective-permute-start | bytes 196616 | tf_op jit(solution)/shard_map/ppermute | solution.py:241
  13.2 0.0 collective-permute-done.1.refs_1_
  13.3 3.7 %collective-permute-start.2 = (bf16[1,64,512]{2,1,0:T(8,128)(2,1)S(1)}, bf16[1,64,512]{2,1,0:T(8,128)(2,1)S(1)}, u32[]{:S(2)}, u32[]{:S(2)}) collective-permute-start(bf16[1,64,512]{2,1,0:T(8,128)(2,1)S(1)} %sum_far_share.1), channel_id=1, source_target_pairs={{12,0},{8,4},{4,8},{0,12},{13,1},{9,5},{5,9},{1,13},{14,2},{10,6},... | collective-permute-start | bytes 196616 | tf_op jit(solution)/shard_map/ppermute | solution.py:241
  16.9 0.8 %tables_for_second_sigma.1 = (f32[4,2,8,128]{3,2,1,0:T(8,128)S(1)}, f32[256,512]{1,0:T(8,128)S(1)}) custom-call(s32[2,2]{1,0:T(2,128)S(1)} %copy-done.3, s32[4,2,8]{2,1,0:T(2,128)S(1)} %bitcast.2, f32[4,8]{1,0:T(4,128)S(1)} %copy-done.4, bf16[256,512]{1,0:T(8,128)(2,1)S(1)} %get-tuple-element.33._.wave_other), custom_call_target="tpu_custom_call" | custom-call | tf_op jit(solution)/shard_map/tables_for_second_sigma/pallas_call | solution.py:259
  17.7 0.0 collective-permute-done.3.refs_3_
  17.7 0.0 collective-permute-done.4.refs_4_
  17.8 2.2 %collective-permute-done.5.refs_5_ = bf16[1,64,512]{2,1,0:T(8,128)(2,1)S(1)} collective-permute-done((bf16[1,64,512]{2,1,0:T(8,128)(2,1)S(1)}, bf16[1,64,512]{2,1,0:T(8,128)(2,1)S(1)}, u32[]{:S(2)}, u32[]{:S(2)}) %collective-permute-start.5) | collective-permute-done | bytes 65568 | tf_op jit(solution)/shard_map/ppermute | solution.py:241
  20.0 0.0 collective-permute-done.6.refs_6_
  20.0 0.0 collective-permute-done.2.refs_2_
  20.0 0.1 sum_first_sigma.1.refs_3_
  20.0 3.1 %collective-permute-start.7 = (bf16[1,64,512]{2,1,0:T(8,128)(2,1)S(1)}, bf16[1,64,512]{2,1,0:T(8,128)(2,1)S(1)}, u32[]{:S(2)}, u32[]{:S(2)}) collective-permute-start(bf16[1,64,512]{2,1,0:T(8,128)(2,1)S(1)} %sum_first_sigma.1.refs_3_), channel_id=1, source_target_pairs={{12,0},{8,4},{4,8},{0,12},{13,1},{9,5},{5,9},{1,13},{14,2},{10,6},... | collective-permute-start | bytes 196616 | tf_op jit(solution)/shard_map/ppermute | solution.py:241
  23.1 0.0 collective-permute-start.8
  23.1 1.4 %collective-permute-start.9 = (bf16[1,64,512]{2,1,0:T(8,128)(2,1)S(1)}, bf16[1,64,512]{2,1,0:T(8,128)(2,1)S(1)}, u32[]{:S(2)}, u32[]{:S(2)}) collective-permute-start(bf16[1,64,512]{2,1,0:T(8,128)(2,1)S(1)} %sum_first_sigma.1.refs_3_), channel_id=1, source_target_pairs={{4,0},{0,4},{12,8},{8,12},{5,1},{1,5},{13,9},{9,13},{6,2},{2,6},{1... | collective-permute-start | bytes 196616 | tf_op jit(solution)/shard_map/ppermute | solution.py:241
  24.5 0.7 %collective-permute-start.14 = (bf16[1,64,512]{2,1,0:T(8,128)(2,1)S(1)}, bf16[1,64,512]{2,1,0:T(8,128)(2,1)S(1)}, u32[]{:S(2)}, u32[]{:S(2)}) collective-permute-start(bf16[1,64,512]{2,1,0:T(8,128)(2,1)S(1)} %sum_first_sigma.1.refs_3_), channel_id=1, source_target_pairs={{6,0},{4,2},{2,4},{0,6},{14,8},{12,10},{10,12},{8,14},{7,1},{5,3},... | collective-permute-start | bytes 196616 | tf_op jit(solution)/shard_map/ppermute | solution.py:241
  25.2 1.4 %collective-permute-start.15 = (bf16[1,64,512]{2,1,0:T(8,128)(2,1)S(1)}, bf16[1,64,512]{2,1,0:T(8,128)(2,1)S(1)}, u32[]{:S(2)}, u32[]{:S(2)}) collective-permute-start(bf16[1,64,512]{2,1,0:T(8,128)(2,1)S(1)} %sum_first_sigma.1.refs_3_), channel_id=1, source_target_pairs={{2,0},{0,2},{3,1},{1,3},{6,4},{4,6},{7,5},{5,7},{10,8},{8,10},{11,... | collective-permute-start | bytes 196616 | tf_op jit(solution)/shard_map/ppermute | solution.py:241
  26.6 0.3 collective-permute-done.7.refs_0_
  26.9 0.5 collective-permute-start.12
  27.4 1.2 %collective-permute-done.8.refs_1_ = bf16[1,64,512]{2,1,0:T(8,128)(2,1)S(1)} collective-permute-done((bf16[1,64,512]{2,1,0:T(8,128)(2,1)S(1)}, bf16[1,64,512]{2,1,0:T(8,128)(2,1)S(1)}, u32[]{:S(2)}, u32[]{:S(2)}) %collective-permute-start.8) | collective-permute-done | bytes 65568 | tf_op jit(solution)/shard_map/ppermute | solution.py:241
  28.6 0.6 %collective-permute-start.13 = (bf16[1,64,512]{2,1,0:T(8,128)(2,1)S(1)}, bf16[1,64,512]{2,1,0:T(8,128)(2,1)S(1)}, u32[]{:S(2)}, u32[]{:S(2)}) collective-permute-start(bf16[1,64,512]{2,1,0:T(8,128)(2,1)S(1)} %collective-permute-done.8.refs_1_), channel_id=1, source_target_pairs={{2,0},{0,2},{3,1},{1,3},{6,4},{4,6},{7,5},{5,7},{10,8},{8,10},{11,... | collective-permute-start | bytes 196616 | tf_op jit(solution)/shard_map/ppermute | solution.py:241
  29.2 0.0 collective-permute-done.9.refs_2_
  29.2 0.1 collective-permute-start.10
  29.3 0.5 collective-permute-done.14.refs_2_
  29.8 0.8 %collective-permute-done.15.refs_3_ = bf16[1,64,512]{2,1,0:T(8,128)(2,1)S(1)} collective-permute-done((bf16[1,64,512]{2,1,0:T(8,128)(2,1)S(1)}, bf16[1,64,512]{2,1,0:T(8,128)(2,1)S(1)}, u32[]{:S(2)}, u32[]{:S(2)}) %collective-permute-start.15) | collective-permute-done | bytes 65568 | tf_op jit(solution)/shard_map/ppermute | solution.py:241
  30.6 1.0 %collective-permute-done.12.refs_0_ = bf16[1,64,512]{2,1,0:T(8,128)(2,1)S(1)} collective-permute-done((bf16[1,64,512]{2,1,0:T(8,128)(2,1)S(1)}, bf16[1,64,512]{2,1,0:T(8,128)(2,1)S(1)}, u32[]{:S(2)}, u32[]{:S(2)}) %collective-permute-start.12) | collective-permute-done | bytes 65568 | tf_op jit(solution)/shard_map/ppermute | solution.py:241
  31.6 1.3 %collective-permute-done.13.refs_1_ = bf16[1,64,512]{2,1,0:T(8,128)(2,1)S(1)} collective-permute-done((bf16[1,64,512]{2,1,0:T(8,128)(2,1)S(1)}, bf16[1,64,512]{2,1,0:T(8,128)(2,1)S(1)}, u32[]{:S(2)}, u32[]{:S(2)}) %collective-permute-start.13) | collective-permute-done | bytes 65568 | tf_op jit(solution)/shard_map/ppermute | solution.py:241
  32.9 0.1 collective-permute-start.16
  33.0 0.0 collective-permute-done.10.sigma_other.other
  33.0 1.0 %left_products.1 = (f32[4,256,512]{2,1,0:T(8,128)S(1)}, f32[1,4,256,512]{3,2,1,0:T(8,128)S(1)}) custom-call(bf16[4,256,256]{2,1,0:T(8,128)(2,1)S(1)} %get-tuple-element.23._.refs_2_.left_own, bf16[4,256,256]{2,1,0:T(8,128)(2,1)S(1)} %get-tuple-element.26.refs_3_.left_other, bf16[1,256,512]{2,1,0:T(8,128)(2,1)S(1)} %place_own_sector.1.sigma_own.own, ...), custom_call_target="tpu_custom_call" | custom-call | tf_op jit(solution)/shard_map/left_products/pallas_call | solution.py:259
  34.0 0.5 collective-permute-done.16.other
  34.5 1.1 %second_sigma_terms.1 = (f32[1,64,512]{2,1,0:T(8,128)S(1)}, bf16[1,64,512]{2,1,0:T(8,128)(2,1)S(1)}, bf16[1,64,512]{2,1,0:T(8,128)(2,1)S(1)}, bf16[1,64,512]{2,1,0:T(8,128)(2,1)S(1)}) custom-call(f32[4,2,8,128]{3,2,1,0:T(8,128)S(1)} %get-tuple-element.34.refs_7_.mixing, f32[256,512]{1,0:T(8,128)S(1)} %get-tuple-element.37.live, ...), custom_call_target="tpu_custom_call" | custom-call | tf_op jit(solution)/shard_map/second_sigma_terms/pallas_call | solution.py:259
  35.7 1.9 %collective-permute-start.17 = (bf16[1,64,512]{2,1,0:T(8,128)(2,1)S(1)}, bf16[1,64,512]{2,1,0:T(8,128)(2,1)S(1)}, u32[]{:S(2)}, u32[]{:S(2)}) collective-permute-start(bf16[1,64,512]{2,1,0:T(8,128)(2,1)S(1)} %get-tuple-element.41), channel_id=1, source_target_pairs={{12,0},{8,4},{4,8},{0,12},{13,1},{9,5},{5,9},{1,13},{14,2},{10,6},... | collective-permute-start | bytes 196616 | tf_op jit(solution)/shard_map/ppermute | solution.py:241
  37.6 0.0 collective-permute-start.18
  37.6 2.5 %collective-permute-start.19 = (bf16[1,64,512]{2,1,0:T(8,128)(2,1)S(1)}, bf16[1,64,512]{2,1,0:T(8,128)(2,1)S(1)}, u32[]{:S(2)}, u32[]{:S(2)}) collective-permute-start(bf16[1,64,512]{2,1,0:T(8,128)(2,1)S(1)} %get-tuple-element.43), channel_id=1, source_target_pairs={{4,0},{0,4},{12,8},{8,12},{5,1},{1,5},{13,9},{9,13},{6,2},{2,6},{1... | collective-permute-start | bytes 196616 | tf_op jit(solution)/shard_map/ppermute | solution.py:241
  40.1 0.5 sums_for_rayleigh.1.refs_0_.refs_4_
  40.6 0.6 %collective-permute-start.11 = (f32[3,8,128]{2,1,0:T(8,128)S(1)}, f32[3,8,128]{2,1,0:T(8,128)S(1)}, u32[]{:S(2)}, u32[]{:S(2)}) collective-permute-start(f32[3,8,128]{2,1,0:T(8,128)S(1)} %sums_for_rayleigh.1.refs_0_.refs_4_), channel_id=1, source_target_pairs={{2,0},{0,2},{3,1},{1,3},{6,4},{4,6},{7,5},{5,7},{10,8},{8,10},{11,... | collective-permute-start | bytes 36872 | tf_op jit(solution)/shard_map/ppermute | solution.py:241
  41.2 3.1 %collective-permute-done.11.refs_1_.refs_5_ = f32[3,8,128]{2,1,0:T(8,128)S(1)} collective-permute-done((f32[3,8,128]{2,1,0:T(8,128)S(1)}, f32[3,8,128]{2,1,0:T(8,128)S(1)}, u32[]{:S(2)}, u32[]{:S(2)}) %collective-permute-start.11) | collective-permute-done | bytes 12320 | tf_op jit(solution)/shard_map/ppermute | solution.py:241
  44.4 0.0 collective-permute-done.17.refs_1_
  44.4 0.1 collective-permute-done.18.refs_2_
  44.5 0.0 collective-permute-done.19.refs_3_
  44.5 2.3 %collective-permute-start.20 = (bf16[1,64,512]{2,1,0:T(8,128)(2,1)S(1)}, bf16[1,64,512]{2,1,0:T(8,128)(2,1)S(1)}, u32[]{:S(2)}, u32[]{:S(2)}) collective-permute-start(bf16[1,64,512]{2,1,0:T(8,128)(2,1)S(1)} %sum_second_sigma.1.refs_3_), channel_id=1, source_target_pairs={{12,0},{8,4},{4,8},{0,12},{13,1},{9,5},{5,9},{1,13},{14,2},{10,6},... | collective-permute-start | bytes 196616 | tf_op jit(solution)/shard_map/ppermute | solution.py:241
  46.8 0.0 collective-permute-start.21
  46.8 2.1 %collective-permute-start.22 = (bf16[1,64,512]{2,1,0:T(8,128)(2,1)S(1)}, bf16[1,64,512]{2,1,0:T(8,128)(2,1)S(1)}, u32[]{:S(2)}, u32[]{:S(2)}) collective-permute-start(bf16[1,64,512]{2,1,0:T(8,128)(2,1)S(1)} %sum_second_sigma.1.refs_3_), channel_id=1, source_target_pairs={{4,0},{0,4},{12,8},{8,12},{5,1},{1,5},{13,9},{9,13},{6,2},{2,6},{1... | collective-permute-start | bytes 196616 | tf_op jit(solution)/shard_map/ppermute | solution.py:241
  49.0 1.4 %second_wave.1 = (bf16[1,256,512]{2,1,0:T(8,128)(2,1)}, f32[2,8,128]{2,1,0:T(8,128)S(1)}) custom-call(s32[2,2]{1,0:T(2,128)S(1)} %copy-done.3, bf16[256,512]{1,0:T(8,128)(2,1)S(1)} %get-tuple-element.24.refs_5_.wave_own, bf16[1,256,512]{2,1,0:T(8,128)(2,1)S(1)} %place_own_sector.1.sigma_own.own, f32[3,8,128]{2,1,0:T(8,128)S(1)} %sums_for_rayleigh.1.refs_0_.refs_4_, ...), custom_call_target="tpu_custom_call" | custom-call | tf_op jit(solution)/shard_map/second_wave/pallas_call | solution.py:259
  50.4 0.8 %collective-permute-done.20.refs_0_ = bf16[1,64,512]{2,1,0:T(8,128)(2,1)S(1)} collective-permute-done((bf16[1,64,512]{2,1,0:T(8,128)(2,1)S(1)}, bf16[1,64,512]{2,1,0:T(8,128)(2,1)S(1)}, u32[]{:S(2)}, u32[]{:S(2)}) %collective-permute-start.20) | collective-permute-done | bytes 65568 | tf_op jit(solution)/shard_map/ppermute | solution.py:241
  51.2 2.0 %collective-permute-done.21.refs_1_ = bf16[1,64,512]{2,1,0:T(8,128)(2,1)S(1)} collective-permute-done((bf16[1,64,512]{2,1,0:T(8,128)(2,1)S(1)}, bf16[1,64,512]{2,1,0:T(8,128)(2,1)S(1)}, u32[]{:S(2)}, u32[]{:S(2)}) %collective-permute-start.21) | collective-permute-done | bytes 65568 | tf_op jit(solution)/shard_map/ppermute | solution.py:241
  53.2 0.0 collective-permute-done.22.refs_2_
  53.2 0.9 %join_second_sigma.1 = f32[1,256,512]{2,1,0:T(8,128)} custom-call(f32[2,8,128]{2,1,0:T(8,128)S(1)} %get-tuple-element.36.factors, bf16[1,256,512]{2,1,0:T(8,128)(2,1)S(1)} %place_own_sector.1.sigma_own.own, bf16[1,64,512]{2,1,0:T(8,128)(2,1)S(1)} %collective-permute-done.20.refs_0_, bf16[1,64,512]{2,1,0:T(8,128)(2,1)S(1)} %collective-permute-done.21.refs_1_, ...), custom_call_target="tpu_custom_call" | custom-call | tf_op jit(solution)/shard_map/join_second_sigma/pallas_call | solution.py:259
  (6 shorter events, 0.1 us)
Async XLA Ops:
  0.6 2.0 %copy-start.1 = (bf16[1,256,512]{2,1,0:T(8,128)(2,1)S(1)}, bf16[1,256,512]{2,1,0:T(8,128)(2,1)}, u32[]{:S(2)}) copy-start(bf16[1,256,512]{2,1,0:T(8,128)(2,1)} %wave.1) | copy-start | bytes 786436
  0.6 2.0 %copy-start.3 = (s32[2,2]{1,0:T(2,128)S(1)}, s32[2,2]{1,0:T(2,128)}, u32[]{:S(2)}) copy-start(s32[2,2]{1,0:T(2,128)} %sizes_ref.3) | copy-start | bytes 52
  0.7 2.0 %copy-start.2 = (s32[4,8,2]{1,2,0:T(2,128)S(1)}, s32[4,8,2]{1,2,0:T(2,128)}, u32[]{:S(2)}) copy-start(s32[4,8,2]{1,2,0:T(2,128)} %param.10) | copy-start | bytes 772
  0.7 2.0 %copy-start.4 = (f32[4,8]{1,0:T(4,128)S(1)}, f32[4,8]{1,0:T(4,128)}, u32[]{:S(2)}) copy-start(f32[4,8]{1,0:T(4,128)} %weights_ref.1) | copy-start | bytes 388
  0.7 2.2 %copy-start = (bf16[4,512,512]{2,1,0:T(8,128)(2,1)S(1)}, bf16[4,512,512]{2,1,0:T(8,128)(2,1)}, u32[]{:S(2)}) copy-start(bf16[4,512,512]{2,1,0:T(8,128)(2,1)} %right.1) | copy-start | bytes 6291460
  0.7 2.2 %collective-permute-start = (bf16[1,256,512]{2,1,0:T(8,128)(2,1)}, bf16[1,256,512]{2,1,0:T(8,128)(2,1)S(1)}, u32[]{:S(2)}, u32[]{:S(2)}) collective-permute-start(bf16[1,256,512]{2,1,0:T(8,128)(2,1)} %wave.1), channel_id=1, source_target_pairs={{1,0},{0,1},{3,2},{2,3},{5,4},{4,5},{7,6},{6,7},{9,8},{8,9},{11,10... | collective-permute-start | bytes 786440 | tf_op jit(solution)/shard_map/ppermute | solution.py:241
  4.6 8.7 %collective-permute-start.1 = (bf16[2,64,512]{2,1,0:T(8,128)(2,1)S(1)}, bf16[2,64,512]{2,1,0:T(8,128)(2,1)S(1)}, u32[]{:S(2)}, u32[]{:S(2)}) collective-permute-start(bf16[2,64,512]{2,1,0:T(8,128)(2,1)S(1)} %get-tuple-element.28), channel_id=1, source_target_pairs={{2,0},{0,2},{3,1},{1,3},{6,4},{4,6},{7,5},{5,7},{10,8},{8,10},{11,... | collective-permute-start | bytes 393224 | tf_op jit(solution)/shard_map/ppermute | solution.py:241
  7.4 10.4 %collective-permute-start.3 = (bf16[1,64,512]{2,1,0:T(8,128)(2,1)S(1)}, bf16[1,64,512]{2,1,0:T(8,128)(2,1)S(1)}, u32[]{:S(2)}, u32[]{:S(2)}) collective-permute-start(bf16[1,64,512]{2,1,0:T(8,128)(2,1)S(1)} %get-tuple-element.29), channel_id=1, source_target_pairs={{4,0},{0,4},{12,8},{8,12},{5,1},{1,5},{13,9},{9,13},{6,2},{2,6},{1... | collective-permute-start | bytes 196616 | tf_op jit(solution)/shard_map/ppermute | solution.py:241
  9.0 8.8 %collective-permute-start.4 = (bf16[1,64,512]{2,1,0:T(8,128)(2,1)S(1)}, bf16[1,64,512]{2,1,0:T(8,128)(2,1)S(1)}, u32[]{:S(2)}, u32[]{:S(2)}) collective-permute-start(bf16[1,64,512]{2,1,0:T(8,128)(2,1)S(1)} %get-tuple-element.30), channel_id=1, source_target_pairs={{8,0},{12,4},{0,8},{4,12},{9,1},{13,5},{1,9},{5,13},{10,2},{14,6},... | collective-permute-start | bytes 196616 | tf_op jit(solution)/shard_map/ppermute | solution.py:241
  11.5 8.4 %collective-permute-start.5 = (bf16[1,64,512]{2,1,0:T(8,128)(2,1)S(1)}, bf16[1,64,512]{2,1,0:T(8,128)(2,1)S(1)}, u32[]{:S(2)}, u32[]{:S(2)}) collective-permute-start(bf16[1,64,512]{2,1,0:T(8,128)(2,1)S(1)} %get-tuple-element.31), channel_id=1, source_target_pairs={{10,0},{8,2},{14,4},{12,6},{2,8},{0,10},{6,12},{4,14},{11,1},{9,3}... | collective-permute-start | bytes 196616 | tf_op jit(solution)/shard_map/ppermute | solution.py:241
  11.8 8.1 %collective-permute-start.6 = (bf16[1,64,512]{2,1,0:T(8,128)(2,1)S(1)}, bf16[1,64,512]{2,1,0:T(8,128)(2,1)S(1)}, u32[]{:S(2)}, u32[]{:S(2)}) collective-permute-start(bf16[1,64,512]{2,1,0:T(8,128)(2,1)S(1)} %get-tuple-element.32), channel_id=1, source_target_pairs={{6,0},{4,2},{2,4},{0,6},{14,8},{12,10},{10,12},{8,14},{7,1},{5,3},... | collective-permute-start | bytes 196616 | tf_op jit(solution)/shard_map/ppermute | solution.py:241
  13.3 6.7 %collective-permute-start.2 = (bf16[1,64,512]{2,1,0:T(8,128)(2,1)S(1)}, bf16[1,64,512]{2,1,0:T(8,128)(2,1)S(1)}, u32[]{:S(2)}, u32[]{:S(2)}) collective-permute-start(bf16[1,64,512]{2,1,0:T(8,128)(2,1)S(1)} %sum_far_share.1), channel_id=1, source_target_pairs={{12,0},{8,4},{4,8},{0,12},{13,1},{9,5},{5,9},{1,13},{14,2},{10,6},... | collective-permute-start | bytes 196616 | tf_op jit(solution)/shard_map/ppermute | solution.py:241
  20.0 6.8 %collective-permute-start.7 = (bf16[1,64,512]{2,1,0:T(8,128)(2,1)S(1)}, bf16[1,64,512]{2,1,0:T(8,128)(2,1)S(1)}, u32[]{:S(2)}, u32[]{:S(2)}) collective-permute-start(bf16[1,64,512]{2,1,0:T(8,128)(2,1)S(1)} %sum_first_sigma.1.refs_3_), channel_id=1, source_target_pairs={{12,0},{8,4},{4,8},{0,12},{13,1},{9,5},{5,9},{1,13},{14,2},{10,6},... | collective-permute-start | bytes 196616 | tf_op jit(solution)/shard_map/ppermute | solution.py:241
  23.1 5.5 %collective-permute-start.8 = (bf16[1,64,512]{2,1,0:T(8,128)(2,1)S(1)}, bf16[1,64,512]{2,1,0:T(8,128)(2,1)S(1)}, u32[]{:S(2)}, u32[]{:S(2)}) collective-permute-start(bf16[1,64,512]{2,1,0:T(8,128)(2,1)S(1)} %sum_first_sigma.1.refs_3_), channel_id=1, source_target_pairs={{8,0},{12,4},{0,8},{4,12},{9,1},{13,5},{1,9},{5,13},{10,2},{14,6},... | collective-permute-start | bytes 196616 | tf_op jit(solution)/shard_map/ppermute | solution.py:241
  23.1 6.1 %collective-permute-start.9 = (bf16[1,64,512]{2,1,0:T(8,128)(2,1)S(1)}, bf16[1,64,512]{2,1,0:T(8,128)(2,1)S(1)}, u32[]{:S(2)}, u32[]{:S(2)}) collective-permute-start(bf16[1,64,512]{2,1,0:T(8,128)(2,1)S(1)} %sum_first_sigma.1.refs_3_), channel_id=1, source_target_pairs={{4,0},{0,4},{12,8},{8,12},{5,1},{1,5},{13,9},{9,13},{6,2},{2,6},{1... | collective-permute-start | bytes 196616 | tf_op jit(solution)/shard_map/ppermute | solution.py:241
  24.5 5.3 %collective-permute-start.14 = (bf16[1,64,512]{2,1,0:T(8,128)(2,1)S(1)}, bf16[1,64,512]{2,1,0:T(8,128)(2,1)S(1)}, u32[]{:S(2)}, u32[]{:S(2)}) collective-permute-start(bf16[1,64,512]{2,1,0:T(8,128)(2,1)S(1)} %sum_first_sigma.1.refs_3_), channel_id=1, source_target_pairs={{6,0},{4,2},{2,4},{0,6},{14,8},{12,10},{10,12},{8,14},{7,1},{5,3},... | collective-permute-start | bytes 196616 | tf_op jit(solution)/shard_map/ppermute | solution.py:241
  25.2 5.4 %collective-permute-start.15 = (bf16[1,64,512]{2,1,0:T(8,128)(2,1)S(1)}, bf16[1,64,512]{2,1,0:T(8,128)(2,1)S(1)}, u32[]{:S(2)}, u32[]{:S(2)}) collective-permute-start(bf16[1,64,512]{2,1,0:T(8,128)(2,1)S(1)} %sum_first_sigma.1.refs_3_), channel_id=1, source_target_pairs={{2,0},{0,2},{3,1},{1,3},{6,4},{4,6},{7,5},{5,7},{10,8},{8,10},{11,... | collective-permute-start | bytes 196616 | tf_op jit(solution)/shard_map/ppermute | solution.py:241
  26.9 4.7 %collective-permute-start.12 = (bf16[1,64,512]{2,1,0:T(8,128)(2,1)S(1)}, bf16[1,64,512]{2,1,0:T(8,128)(2,1)S(1)}, u32[]{:S(2)}, u32[]{:S(2)}) collective-permute-start(bf16[1,64,512]{2,1,0:T(8,128)(2,1)S(1)} %collective-permute-done.7.refs_0_), channel_id=1, source_target_pairs={{2,0},{0,2},{3,1},{1,3},{6,4},{4,6},{7,5},{5,7},{10,8},{8,10},{11,... | collective-permute-start | bytes 196616 | tf_op jit(solution)/shard_map/ppermute | solution.py:241
  28.6 4.3 %collective-permute-start.13 = (bf16[1,64,512]{2,1,0:T(8,128)(2,1)S(1)}, bf16[1,64,512]{2,1,0:T(8,128)(2,1)S(1)}, u32[]{:S(2)}, u32[]{:S(2)}) collective-permute-start(bf16[1,64,512]{2,1,0:T(8,128)(2,1)S(1)} %collective-permute-done.8.refs_1_), channel_id=1, source_target_pairs={{2,0},{0,2},{3,1},{1,3},{6,4},{4,6},{7,5},{5,7},{10,8},{8,10},{11,... | collective-permute-start | bytes 196616 | tf_op jit(solution)/shard_map/ppermute | solution.py:241
  29.2 3.8 %collective-permute-start.10 = (bf16[1,256,512]{2,1,0:T(8,128)(2,1)S(1)}, bf16[1,256,512]{2,1,0:T(8,128)(2,1)S(1)}, u32[]{:S(2)}, u32[]{:S(2)}) collective-permute-start(bf16[1,256,512]{2,1,0:T(8,128)(2,1)S(1)} %place_own_sector.1.sigma_own.own), channel_id=1, source_target_pairs={{1,0},{0,1},{3,2},{2,3},{5,4},{4,5},{7,6},{6,7},{9,8},{8,9},{11,10... | collective-permute-start | bytes 786440 | tf_op jit(solution)/shard_map/ppermute | solution.py:241
  32.9 1.6 %collective-permute-start.16 = (bf16[1,256,512]{2,1,0:T(8,128)(2,1)S(1)}, bf16[1,256,512]{2,1,0:T(8,128)(2,1)S(1)}, u32[]{:S(2)}, u32[]{:S(2)}) collective-permute-start(bf16[1,256,512]{2,1,0:T(8,128)(2,1)S(1)} %place_other_sectors.1.across_own), channel_id=1, source_target_pairs={{1,0},{0,1},{3,2},{2,3},{5,4},{4,5},{7,6},{6,7},{9,8},{8,9},{11,10... | collective-permute-start | bytes 786440 | tf_op jit(solution)/shard_map/ppermute | solution.py:241
  35.7 8.7 %collective-permute-start.17 = (bf16[1,64,512]{2,1,0:T(8,128)(2,1)S(1)}, bf16[1,64,512]{2,1,0:T(8,128)(2,1)S(1)}, u32[]{:S(2)}, u32[]{:S(2)}) collective-permute-start(bf16[1,64,512]{2,1,0:T(8,128)(2,1)S(1)} %get-tuple-element.41), channel_id=1, source_target_pairs={{12,0},{8,4},{4,8},{0,12},{13,1},{9,5},{5,9},{1,13},{14,2},{10,6},... | collective-permute-start | bytes 196616 | tf_op jit(solution)/shard_map/ppermute | solution.py:241
  37.6 6.9 %collective-permute-start.18 = (bf16[1,64,512]{2,1,0:T(8,128)(2,1)S(1)}, bf16[1,64,512]{2,1,0:T(8,128)(2,1)S(1)}, u32[]{:S(2)}, u32[]{:S(2)}) collective-permute-start(bf16[1,64,512]{2,1,0:T(8,128)(2,1)S(1)} %get-tuple-element.42), channel_id=1, source_target_pairs={{8,0},{12,4},{0,8},{4,12},{9,1},{13,5},{1,9},{5,13},{10,2},{14,6},... | collective-permute-start | bytes 196616 | tf_op jit(solution)/shard_map/ppermute | solution.py:241
  37.6 6.9 %collective-permute-start.19 = (bf16[1,64,512]{2,1,0:T(8,128)(2,1)S(1)}, bf16[1,64,512]{2,1,0:T(8,128)(2,1)S(1)}, u32[]{:S(2)}, u32[]{:S(2)}) collective-permute-start(bf16[1,64,512]{2,1,0:T(8,128)(2,1)S(1)} %get-tuple-element.43), channel_id=1, source_target_pairs={{4,0},{0,4},{12,8},{8,12},{5,1},{1,5},{13,9},{9,13},{6,2},{2,6},{1... | collective-permute-start | bytes 196616 | tf_op jit(solution)/shard_map/ppermute | solution.py:241
  40.6 3.8 %collective-permute-start.11 = (f32[3,8,128]{2,1,0:T(8,128)S(1)}, f32[3,8,128]{2,1,0:T(8,128)S(1)}, u32[]{:S(2)}, u32[]{:S(2)}) collective-permute-start(f32[3,8,128]{2,1,0:T(8,128)S(1)} %sums_for_rayleigh.1.refs_0_.refs_4_), channel_id=1, source_target_pairs={{2,0},{0,2},{3,1},{1,3},{6,4},{4,6},{7,5},{5,7},{10,8},{8,10},{11,... | collective-permute-start | bytes 36872 | tf_op jit(solution)/shard_map/ppermute | solution.py:241
  44.5 6.7 %collective-permute-start.20 = (bf16[1,64,512]{2,1,0:T(8,128)(2,1)S(1)}, bf16[1,64,512]{2,1,0:T(8,128)(2,1)S(1)}, u32[]{:S(2)}, u32[]{:S(2)}) collective-permute-start(bf16[1,64,512]{2,1,0:T(8,128)(2,1)S(1)} %sum_second_sigma.1.refs_3_), channel_id=1, source_target_pairs={{12,0},{8,4},{4,8},{0,12},{13,1},{9,5},{5,9},{1,13},{14,2},{10,6},... | collective-permute-start | bytes 196616 | tf_op jit(solution)/shard_map/ppermute | solution.py:241
  46.8 6.4 %collective-permute-start.21 = (bf16[1,64,512]{2,1,0:T(8,128)(2,1)S(1)}, bf16[1,64,512]{2,1,0:T(8,128)(2,1)S(1)}, u32[]{:S(2)}, u32[]{:S(2)}) collective-permute-start(bf16[1,64,512]{2,1,0:T(8,128)(2,1)S(1)} %sum_second_sigma.1.refs_3_), channel_id=1, source_target_pairs={{8,0},{12,4},{0,8},{4,12},{9,1},{13,5},{1,9},{5,13},{10,2},{14,6},... | collective-permute-start | bytes 196616 | tf_op jit(solution)/shard_map/ppermute | solution.py:241
  46.8 6.4 %collective-permute-start.22 = (bf16[1,64,512]{2,1,0:T(8,128)(2,1)S(1)}, bf16[1,64,512]{2,1,0:T(8,128)(2,1)S(1)}, u32[]{:S(2)}, u32[]{:S(2)}) collective-permute-start(bf16[1,64,512]{2,1,0:T(8,128)(2,1)S(1)} %sum_second_sigma.1.refs_3_), channel_id=1, source_target_pairs={{4,0},{0,4},{12,8},{8,12},{5,1},{1,5},{13,9},{9,13},{6,2},{2,6},{1... | collective-permute-start | bytes 196616 | tf_op jit(solution)/shard_map/ppermute | solution.py:241

commit v15 on v14

--- a/solution.py
+++ b/solution.py
@@ -294,9 +294,8 @@
     scalars = (sector_sizes, pairs, pair_weights)
 
     far = ops_count - 1
-    direct = [(along,) for along in farthest_first[1:-1]]
-    spots = [((far, 0), across) for across in range(sectors)]
-    spots += [(along, across) for along in direct for across in range(sectors)]
+    groups = [(far, 0), (1,)] + [(along,) for along in farthest_first[1:-2]]
+    spots = [(along, across) for along in groups for across in range(sectors)]
     wave_own, mixing = call(
         first_tables_kernel,
         "tables_for_first_sigma",
@@ -311,7 +310,7 @@
         "first_sigma_terms",
         [shape(rows, columns)]
         + [
-            shape(len(along), share, columns, dtype=f32 if along == (far, 0) and across == 0 else bf16)
+            shape(len(along), share, columns, dtype=f32 if along in groups[:2] and across == 0 else bf16)
             for along, across in spots
         ],
         [],
@@ -333,12 +332,21 @@
         *scalars,
         wave_other,
     )
-    met = [partner(rest[(far, 0), across], {"sec": across}) for across in range(sectors)]
-    received = [partner(summed("sum_far_share", *met), {"ops": far})]
-    nearest = ((1,), 0)
-    order = [nearest] + [spot for spot in rest if spot[0] in direct and spot != nearest]
-    received += [partner(rest[spot], {"ops": spot[0][0], "sec": spot[1]}) for spot in order]
-    first_share = summed("sum_first_sigma", *[(piece, 1) for piece in met], *received, after=(mixing,))
+    met = {
+        along: [partner(rest[along, across], {"sec": across}) for across in range(sectors)]
+        for along in groups[:2]
+    }
+    far_sum = summed("sum_far_share", *met[far, 0])
+    received = [partner(far_sum, {"ops": far})]
+    received += [
+        partner(rest[along, across], {"ops": along[0], "sec": across})
+        for along in groups[2:]
+        for across in range(sectors)
+    ]
+    near_sum = summed("sum_near_share", *met[1,], after=(far_sum,))
+    received.append(partner(near_sum, {"ops": 1}))
+    kept = [(piece, 1) for piece in met[far, 0]]
+    first_share = summed("sum_first_sigma", *kept, *received, after=(mixing,))
     along_ops = {along: partner(first_share, {"ops": along}) for along in farthest_first}
     sigma_own = call(
         lambda *refs: place_kernel([(along, 0) for along in farthest_first], *refs),

time: 54.2 us -> 54.7 us (level)
  starting transfers between devices: 30.2 us -> 31.6 us
  waiting for transfers between devices: 13.9 us -> 12.9 us
    ppermute x23, starting transfers between devices: 30.2 us -> 31.6 us  [partner(): return lax.ppermute(value, axes, pairs)]
    ppermute x23, waiting for transfers between devices: 13.9 us -> 12.9 us  [partner(): return lax.ppermute(value, axes, pairs)]
    pallas_call x14 -> x15, Pallas kernels: 9.18 us -> 9.2 us  [call(): pl.pallas_call(kernel, out_shape=out_shape, in_specs=list(in_specs) + [in...]
where the time goes in v15:
time: 54.7 us; the launch traced here: 54.5 us
  starting transfers between devices  31.6 us (58%)
  waiting for transfers between devices  12.9 us (24%)
  Pallas kernels  9.2 us (17%)
  between operations  0.85 us (2%)
    ppermute x23, starting transfers between devices, partner(): return lax.ppermute(value, axes, pairs)  31.6 us
    ppermute x23, waiting for transfers between devices, partner(): return lax.ppermute(value, axes, pairs)  12.9 us
    pallas_call x15, Pallas kernels, call(): pl.pallas_call(kernel, out_shape=out_shape, in_specs=list(in_specs) + [in...  9.2 us
  transfers between devices with their start and end apart: 23, of which 12 were waited for; matrix products, arithmetic and copies ran while one was open for 0% of the time, Pallas kernels for 10%

profile of v15, /device:TPU:0, one launch (start us, length us, event | category | flops | bytes accessed | tf_op | source)
XLA Modules:
  0.0 54.5 jit_solution(4140753424987716893)
XLA Ops:
  0.6 0.0 copy-start.1
  0.6 0.0 copy-start.3
  0.7 0.0 copy-start.2
  0.7 0.0 copy-start.4
  0.7 0.5 collective-permute-start
  1.2 1.4 %load_operators.1 = (bf16[4,256,256]{2,1,0:T(8,128)(2,1)S(1)}, bf16[4,256,256]{2,1,0:T(8,128)(2,1)S(1)}) custom-call(bf16[4,512,512]{2,1,0:T(8,128)(2,1)} %left_ref.1), custom_call_target="tpu_custom_call" | custom-call | tf_op jit(solution)/shard_map/load_operators/pallas_call | solution.py:259
  2.6 0.0 copy-done.1
  2.6 0.0 copy-done.3
  2.7 0.0 copy-done.2
  2.7 0.0 copy-done.4
  2.7 0.2 tables_for_first_sigma.1
  2.9 0.0 collective-permute-done.refs_6_
  2.9 1.7 %first_sigma_terms.1 = (bf16[256,512]{1,0:T(8,128)(2,1)S(1)}, f32[2,64,512]{2,1,0:T(8,128)S(1)}, bf16[2,64,512]{2,1,0:T(8,128)(2,1)S(1)}, f32[1,64,512]{2,1,0:T(...) custom-call(s32[2,2]{1,0:T(2,128)S(1)} %copy-done.3, ...), custom_call_target="tpu_custom_call" | custom-call | tf_op jit(solution)/shard_map/first_sigma_terms/pallas_call | solution.py:259
  4.6 2.8 %collective-permute-start.1 = (bf16[2,64,512]{2,1,0:T(8,128)(2,1)S(1)}, bf16[2,64,512]{2,1,0:T(8,128)(2,1)S(1)}, u32[]{:S(2)}, u32[]{:S(2)}) collective-permute-start(bf16[2,64,512]{2,1,0:T(8,128)(2,1)S(1)} %get-tuple-element.28), channel_id=1, source_target_pairs={{2,0},{0,2},{3,1},{1,3},{6,4},{4,6},{7,5},{5,7},{10,8},{8,10},{11,... | collective-permute-start | bytes 393224 | tf_op jit(solution)/shard_map/ppermute | solution.py:241
  7.4 0.1 collective-permute-start.5
  7.5 3.0 %collective-permute-start.3 = (bf16[1,64,512]{2,1,0:T(8,128)(2,1)S(1)}, bf16[1,64,512]{2,1,0:T(8,128)(2,1)S(1)}, u32[]{:S(2)}, u32[]{:S(2)}) collective-permute-start(bf16[1,64,512]{2,1,0:T(8,128)(2,1)S(1)} %get-tuple-element.29), channel_id=1, source_target_pairs={{8,0},{12,4},{0,8},{4,12},{9,1},{13,5},{1,9},{5,13},{10,2},{14,6},... | collective-permute-start | bytes 196616 | tf_op jit(solution)/shard_map/ppermute | solution.py:241
  10.5 1.3 %collective-permute-start.4 = (bf16[1,64,512]{2,1,0:T(8,128)(2,1)S(1)}, bf16[1,64,512]{2,1,0:T(8,128)(2,1)S(1)}, u32[]{:S(2)}, u32[]{:S(2)}) collective-permute-start(bf16[1,64,512]{2,1,0:T(8,128)(2,1)S(1)} %get-tuple-element.30), channel_id=1, source_target_pairs={{10,0},{8,2},{14,4},{12,6},{2,8},{0,10},{6,12},{4,14},{11,1},{9,3}... | collective-permute-start | bytes 196616 | tf_op jit(solution)/shard_map/ppermute | solution.py:241
  11.8 0.0 collective-permute-done.1.refs_1_
  11.8 4.0 %collective-permute-start.2 = (bf16[1,64,512]{2,1,0:T(8,128)(2,1)S(1)}, bf16[1,64,512]{2,1,0:T(8,128)(2,1)S(1)}, u32[]{:S(2)}, u32[]{:S(2)}) collective-permute-start(bf16[1,64,512]{2,1,0:T(8,128)(2,1)S(1)} %sum_far_share.1.refs_2_), channel_id=1, source_target_pairs={{12,0},{8,4},{4,8},{0,12},{13,1},{9,5},{5,9},{1,13},{14,2},{10,6},... | collective-permute-start | bytes 196616 | tf_op jit(solution)/shard_map/ppermute | solution.py:241
  15.8 0.0 collective-permute-done.5.refs_1_
  15.8 0.1 collective-permute-start.6
  15.9 0.8 %tables_for_second_sigma.1 = (f32[4,2,8,128]{3,2,1,0:T(8,128)S(1)}, f32[256,512]{1,0:T(8,128)S(1)}) custom-call(s32[2,2]{1,0:T(2,128)S(1)} %copy-done.3, s32[4,2,8]{2,1,0:T(2,128)S(1)} %bitcast.2, f32[4,8]{1,0:T(4,128)S(1)} %copy-done.4, bf16[256,512]{1,0:T(8,128)(2,1)S(1)} %get-tuple-element.33._.wave_other), custom_call_target="tpu_custom_call" | custom-call | tf_op jit(solution)/shard_map/tables_for_second_sigma/pallas_call | solution.py:259
  16.7 0.0 collective-permute-done.3.refs_3_
  16.7 2.7 %collective-permute-done.4.refs_4_ = bf16[1,64,512]{2,1,0:T(8,128)(2,1)S(1)} collective-permute-done((bf16[1,64,512]{2,1,0:T(8,128)(2,1)S(1)}, bf16[1,64,512]{2,1,0:T(8,128)(2,1)S(1)}, u32[]{:S(2)}, u32[]{:S(2)}) %collective-permute-start.4) | collective-permute-done | bytes 65568 | tf_op jit(solution)/shard_map/ppermute | solution.py:241
  19.4 0.0 collective-permute-done.2.refs_2_
  19.4 0.7 %collective-permute-done.6.refs_5_ = bf16[1,64,512]{2,1,0:T(8,128)(2,1)S(1)} collective-permute-done((bf16[1,64,512]{2,1,0:T(8,128)(2,1)S(1)}, bf16[1,64,512]{2,1,0:T(8,128)(2,1)S(1)}, u32[]{:S(2)}, u32[]{:S(2)}) %collective-permute-start.6) | collective-permute-done | bytes 65568 | tf_op jit(solution)/shard_map/ppermute | solution.py:241
  20.1 0.1 sum_first_sigma.1.refs_3_
  20.2 2.8 %collective-permute-start.7 = (bf16[1,64,512]{2,1,0:T(8,128)(2,1)S(1)}, bf16[1,64,512]{2,1,0:T(8,128)(2,1)S(1)}, u32[]{:S(2)}, u32[]{:S(2)}) collective-permute-start(bf16[1,64,512]{2,1,0:T(8,128)(2,1)S(1)} %sum_first_sigma.1.refs_3_), channel_id=1, source_target_pairs={{12,0},{8,4},{4,8},{0,12},{13,1},{9,5},{5,9},{1,13},{14,2},{10,6},... | collective-permute-start | bytes 196616 | tf_op jit(solution)/shard_map/ppermute | solution.py:241
  23.0 0.0 collective-permute-start.8
  23.0 1.7 %collective-permute-start.9 = (bf16[1,64,512]{2,1,0:T(8,128)(2,1)S(1)}, bf16[1,64,512]{2,1,0:T(8,128)(2,1)S(1)}, u32[]{:S(2)}, u32[]{:S(2)}) collective-permute-start(bf16[1,64,512]{2,1,0:T(8,128)(2,1)S(1)} %sum_first_sigma.1.refs_3_), channel_id=1, source_target_pairs={{4,0},{0,4},{12,8},{8,12},{5,1},{1,5},{13,9},{9,13},{6,2},{2,6},{1... | collective-permute-start | bytes 196616 | tf_op jit(solution)/shard_map/ppermute | solution.py:241
  24.6 1.3 %collective-permute-start.14 = (bf16[1,64,512]{2,1,0:T(8,128)(2,1)S(1)}, bf16[1,64,512]{2,1,0:T(8,128)(2,1)S(1)}, u32[]{:S(2)}, u32[]{:S(2)}) collective-permute-start(bf16[1,64,512]{2,1,0:T(8,128)(2,1)S(1)} %sum_first_sigma.1.refs_3_), channel_id=1, source_target_pairs={{6,0},{4,2},{2,4},{0,6},{14,8},{12,10},{10,12},{8,14},{7,1},{5,3},... | collective-permute-start | bytes 196616 | tf_op jit(solution)/shard_map/ppermute | solution.py:241
  25.9 0.6 %collective-permute-start.15 = (bf16[1,64,512]{2,1,0:T(8,128)(2,1)S(1)}, bf16[1,64,512]{2,1,0:T(8,128)(2,1)S(1)}, u32[]{:S(2)}, u32[]{:S(2)}) collective-permute-start(bf16[1,64,512]{2,1,0:T(8,128)(2,1)S(1)} %sum_first_sigma.1.refs_3_), channel_id=1, source_target_pairs={{2,0},{0,2},{3,1},{1,3},{6,4},{4,6},{7,5},{5,7},{10,8},{8,10},{11,... | collective-permute-start | bytes 196616 | tf_op jit(solution)/shard_map/ppermute | solution.py:241
  26.5 0.2 collective-permute-done.7.refs_0_
  26.7 1.6 %collective-permute-start.12 = (bf16[1,64,512]{2,1,0:T(8,128)(2,1)S(1)}, bf16[1,64,512]{2,1,0:T(8,128)(2,1)S(1)}, u32[]{:S(2)}, u32[]{:S(2)}) collective-permute-start(bf16[1,64,512]{2,1,0:T(8,128)(2,1)S(1)} %collective-permute-done.7.refs_0_), channel_id=1, source_target_pairs={{2,0},{0,2},{3,1},{1,3},{6,4},{4,6},{7,5},{5,7},{10,8},{8,10},{11,... | collective-permute-start | bytes 196616 | tf_op jit(solution)/shard_map/ppermute | solution.py:241
  28.3 0.6 %collective-permute-done.8.refs_1_ = bf16[1,64,512]{2,1,0:T(8,128)(2,1)S(1)} collective-permute-done((bf16[1,64,512]{2,1,0:T(8,128)(2,1)S(1)}, bf16[1,64,512]{2,1,0:T(8,128)(2,1)S(1)}, u32[]{:S(2)}, u32[]{:S(2)}) %collective-permute-start.8) | collective-permute-done | bytes 65568 | tf_op jit(solution)/shard_map/ppermute | solution.py:241
  28.8 1.5 %collective-permute-start.13 = (bf16[1,64,512]{2,1,0:T(8,128)(2,1)S(1)}, bf16[1,64,512]{2,1,0:T(8,128)(2,1)S(1)}, u32[]{:S(2)}, u32[]{:S(2)}) collective-permute-start(bf16[1,64,512]{2,1,0:T(8,128)(2,1)S(1)} %collective-permute-done.8.refs_1_), channel_id=1, source_target_pairs={{2,0},{0,2},{3,1},{1,3},{6,4},{4,6},{7,5},{5,7},{10,8},{8,10},{11,... | collective-permute-start | bytes 196616 | tf_op jit(solution)/shard_map/ppermute | solution.py:241
  30.3 0.0 collective-permute-done.9.refs_2_
  30.4 0.1 collective-permute-start.10
  30.5 0.8 %collective-permute-done.14.refs_2_ = bf16[1,64,512]{2,1,0:T(8,128)(2,1)S(1)} collective-permute-done((bf16[1,64,512]{2,1,0:T(8,128)(2,1)S(1)}, bf16[1,64,512]{2,1,0:T(8,128)(2,1)S(1)}, u32[]{:S(2)}, u32[]{:S(2)}) %collective-permute-start.14) | collective-permute-done | bytes 65568 | tf_op jit(solution)/shard_map/ppermute | solution.py:241
  31.2 0.0 collective-permute-done.15.refs_3_
  31.2 1.0 %collective-permute-done.12.refs_0_ = bf16[1,64,512]{2,1,0:T(8,128)(2,1)S(1)} collective-permute-done((bf16[1,64,512]{2,1,0:T(8,128)(2,1)S(1)}, bf16[1,64,512]{2,1,0:T(8,128)(2,1)S(1)}, u32[]{:S(2)}, u32[]{:S(2)}) %collective-permute-start.12) | collective-permute-done | bytes 65568 | tf_op jit(solution)/shard_map/ppermute | solution.py:241
  32.3 1.0 %collective-permute-done.13.refs_1_ = bf16[1,64,512]{2,1,0:T(8,128)(2,1)S(1)} collective-permute-done((bf16[1,64,512]{2,1,0:T(8,128)(2,1)S(1)}, bf16[1,64,512]{2,1,0:T(8,128)(2,1)S(1)}, u32[]{:S(2)}, u32[]{:S(2)}) %collective-permute-start.13) | collective-permute-done | bytes 65568 | tf_op jit(solution)/shard_map/ppermute | solution.py:241
  33.3 0.1 collective-permute-start.16
  33.4 0.0 collective-permute-done.10.sigma_other.other
  33.4 1.0 %left_products.1 = (f32[4,256,512]{2,1,0:T(8,128)S(1)}, f32[1,4,256,512]{3,2,1,0:T(8,128)S(1)}) custom-call(bf16[4,256,256]{2,1,0:T(8,128)(2,1)S(1)} %get-tuple-element.23._.refs_2_.left_own, bf16[4,256,256]{2,1,0:T(8,128)(2,1)S(1)} %get-tuple-element.26.refs_3_.left_other, bf16[1,256,512]{2,1,0:T(8,128)(2,1)S(1)} %place_own_sector.1.sigma_own.own, ...), custom_call_target="tpu_custom_call" | custom-call | tf_op jit(solution)/shard_map/left_products/pallas_call | solution.py:259
  34.4 0.5 collective-permute-done.16.other
  34.9 1.1 %second_sigma_terms.1 = (f32[1,64,512]{2,1,0:T(8,128)S(1)}, bf16[1,64,512]{2,1,0:T(8,128)(2,1)S(1)}, bf16[1,64,512]{2,1,0:T(8,128)(2,1)S(1)}, bf16[1,64,512]{2,1,0:T(8,128)(2,1)S(1)}) custom-call(f32[4,2,8,128]{3,2,1,0:T(8,128)S(1)} %get-tuple-element.34.refs_6_.mixing, f32[256,512]{1,0:T(8,128)S(1)} %get-tuple-element.37.live, ...), custom_call_target="tpu_custom_call" | custom-call | tf_op jit(solution)/shard_map/second_sigma_terms/pallas_call | solution.py:259
  36.0 2.5 %collective-permute-start.17 = (bf16[1,64,512]{2,1,0:T(8,128)(2,1)S(1)}, bf16[1,64,512]{2,1,0:T(8,128)(2,1)S(1)}, u32[]{:S(2)}, u32[]{:S(2)}) collective-permute-start(bf16[1,64,512]{2,1,0:T(8,128)(2,1)S(1)} %get-tuple-element.41), channel_id=1, source_target_pairs={{12,0},{8,4},{4,8},{0,12},{13,1},{9,5},{5,9},{1,13},{14,2},{10,6},... | collective-permute-start | bytes 196616 | tf_op jit(solution)/shard_map/ppermute | solution.py:241
  38.6 0.0 collective-permute-start.18
  38.6 1.9 %collective-permute-start.19 = (bf16[1,64,512]{2,1,0:T(8,128)(2,1)S(1)}, bf16[1,64,512]{2,1,0:T(8,128)(2,1)S(1)}, u32[]{:S(2)}, u32[]{:S(2)}) collective-permute-start(bf16[1,64,512]{2,1,0:T(8,128)(2,1)S(1)} %get-tuple-element.43), channel_id=1, source_target_pairs={{4,0},{0,4},{12,8},{8,12},{5,1},{1,5},{13,9},{9,13},{6,2},{2,6},{1... | collective-permute-start | bytes 196616 | tf_op jit(solution)/shard_map/ppermute | solution.py:241
  40.5 0.5 sums_for_rayleigh.1.refs_0_.refs_4_
  41.0 1.4 %collective-permute-start.11 = (f32[3,8,128]{2,1,0:T(8,128)S(1)}, f32[3,8,128]{2,1,0:T(8,128)S(1)}, u32[]{:S(2)}, u32[]{:S(2)}) collective-permute-start(f32[3,8,128]{2,1,0:T(8,128)S(1)} %sums_for_rayleigh.1.refs_0_.refs_4_), channel_id=1, source_target_pairs={{2,0},{0,2},{3,1},{1,3},{6,4},{4,6},{7,5},{5,7},{10,8},{8,10},{11,... | collective-permute-start | bytes 36872 | tf_op jit(solution)/shard_map/ppermute | solution.py:241
  42.4 2.4 %collective-permute-done.11.refs_1_.refs_5_ = f32[3,8,128]{2,1,0:T(8,128)S(1)} collective-permute-done((f32[3,8,128]{2,1,0:T(8,128)S(1)}, f32[3,8,128]{2,1,0:T(8,128)S(1)}, u32[]{:S(2)}, u32[]{:S(2)}) %collective-permute-start.11) | collective-permute-done | bytes 12320 | tf_op jit(solution)/shard_map/ppermute | solution.py:241
  44.8 0.0 collective-permute-done.17.refs_1_
  44.8 0.2 collective-permute-done.18.refs_2_
  44.9 0.0 collective-permute-done.19.refs_3_
  45.0 2.6 %collective-permute-start.20 = (bf16[1,64,512]{2,1,0:T(8,128)(2,1)S(1)}, bf16[1,64,512]{2,1,0:T(8,128)(2,1)S(1)}, u32[]{:S(2)}, u32[]{:S(2)}) collective-permute-start(bf16[1,64,512]{2,1,0:T(8,128)(2,1)S(1)} %sum_second_sigma.1.refs_3_), channel_id=1, source_target_pairs={{12,0},{8,4},{4,8},{0,12},{13,1},{9,5},{5,9},{1,13},{14,2},{10,6},... | collective-permute-start | bytes 196616 | tf_op jit(solution)/shard_map/ppermute | solution.py:241
  47.6 0.0 collective-permute-start.21
  47.6 1.9 %collective-permute-start.22 = (bf16[1,64,512]{2,1,0:T(8,128)(2,1)S(1)}, bf16[1,64,512]{2,1,0:T(8,128)(2,1)S(1)}, u32[]{:S(2)}, u32[]{:S(2)}) collective-permute-start(bf16[1,64,512]{2,1,0:T(8,128)(2,1)S(1)} %sum_second_sigma.1.refs_3_), channel_id=1, source_target_pairs={{4,0},{0,4},{12,8},{8,12},{5,1},{1,5},{13,9},{9,13},{6,2},{2,6},{1... | collective-permute-start | bytes 196616 | tf_op jit(solution)/shard_map/ppermute | solution.py:241
  49.4 1.4 %second_wave.1 = (bf16[1,256,512]{2,1,0:T(8,128)(2,1)}, f32[2,8,128]{2,1,0:T(8,128)S(1)}) custom-call(s32[2,2]{1,0:T(2,128)S(1)} %copy-done.3, bf16[256,512]{1,0:T(8,128)(2,1)S(1)} %get-tuple-element.24.refs_5_.wave_own, bf16[1,256,512]{2,1,0:T(8,128)(2,1)S(1)} %place_own_sector.1.sigma_own.own, f32[3,8,128]{2,1,0:T(8,128)S(1)} %sums_for_rayleigh.1.refs_0_.refs_4_, ...), custom_call_target="tpu_custom_call" | custom-call | tf_op jit(solution)/shard_map/second_wave/pallas_call | solution.py:259
  50.9 0.8 %collective-permute-done.20.refs_0_ = bf16[1,64,512]{2,1,0:T(8,128)(2,1)S(1)} collective-permute-done((bf16[1,64,512]{2,1,0:T(8,128)(2,1)S(1)}, bf16[1,64,512]{2,1,0:T(8,128)(2,1)S(1)}, u32[]{:S(2)}, u32[]{:S(2)}) %collective-permute-start.20) | collective-permute-done | bytes 65568 | tf_op jit(solution)/shard_map/ppermute | solution.py:241
  51.7 2.0 %collective-permute-done.21.refs_1_ = bf16[1,64,512]{2,1,0:T(8,128)(2,1)S(1)} collective-permute-done((bf16[1,64,512]{2,1,0:T(8,128)(2,1)S(1)}, bf16[1,64,512]{2,1,0:T(8,128)(2,1)S(1)}, u32[]{:S(2)}, u32[]{:S(2)}) %collective-permute-start.21) | collective-permute-done | bytes 65568 | tf_op jit(solution)/shard_map/ppermute | solution.py:241
  53.7 0.0 collective-permute-done.22.refs_2_
  53.7 0.9 %join_second_sigma.1 = f32[1,256,512]{2,1,0:T(8,128)} custom-call(f32[2,8,128]{2,1,0:T(8,128)S(1)} %get-tuple-element.36.factors, bf16[1,256,512]{2,1,0:T(8,128)(2,1)S(1)} %place_own_sector.1.sigma_own.own, bf16[1,64,512]{2,1,0:T(8,128)(2,1)S(1)} %collective-permute-done.20.refs_0_, bf16[1,64,512]{2,1,0:T(8,128)(2,1)S(1)} %collective-permute-done.21.refs_1_, ...), custom_call_target="tpu_custom_call" | custom-call | tf_op jit(solution)/shard_map/join_second_sigma/pallas_call | solution.py:259
  (7 shorter events, 0.1 us)
Async XLA Ops:
  0.6 2.0 %copy-start.1 = (bf16[1,256,512]{2,1,0:T(8,128)(2,1)S(1)}, bf16[1,256,512]{2,1,0:T(8,128)(2,1)}, u32[]{:S(2)}) copy-start(bf16[1,256,512]{2,1,0:T(8,128)(2,1)} %wave.1) | copy-start | bytes 786436
  0.6 2.0 %copy-start.3 = (s32[2,2]{1,0:T(2,128)S(1)}, s32[2,2]{1,0:T(2,128)}, u32[]{:S(2)}) copy-start(s32[2,2]{1,0:T(2,128)} %sizes_ref.3) | copy-start | bytes 52
  0.7 2.0 %copy-start.2 = (s32[4,8,2]{1,2,0:T(2,128)S(1)}, s32[4,8,2]{1,2,0:T(2,128)}, u32[]{:S(2)}) copy-start(s32[4,8,2]{1,2,0:T(2,128)} %param.10) | copy-start | bytes 772
  0.7 2.0 %copy-start.4 = (f32[4,8]{1,0:T(4,128)S(1)}, f32[4,8]{1,0:T(4,128)}, u32[]{:S(2)}) copy-start(f32[4,8]{1,0:T(4,128)} %weights_ref.1) | copy-start | bytes 388
  0.7 2.2 %copy-start = (bf16[4,512,512]{2,1,0:T(8,128)(2,1)S(1)}, bf16[4,512,512]{2,1,0:T(8,128)(2,1)}, u32[]{:S(2)}) copy-start(bf16[4,512,512]{2,1,0:T(8,128)(2,1)} %right.1) | copy-start | bytes 6291460
  0.7 2.2 %collective-permute-start = (bf16[1,256,512]{2,1,0:T(8,128)(2,1)}, bf16[1,256,512]{2,1,0:T(8,128)(2,1)S(1)}, u32[]{:S(2)}, u32[]{:S(2)}) collective-permute-start(bf16[1,256,512]{2,1,0:T(8,128)(2,1)} %wave.1), channel_id=1, source_target_pairs={{1,0},{0,1},{3,2},{2,3},{5,4},{4,5},{7,6},{6,7},{9,8},{8,9},{11,10... | collective-permute-start | bytes 786440 | tf_op jit(solution)/shard_map/ppermute | solution.py:241
  4.6 7.2 %collective-permute-start.1 = (bf16[2,64,512]{2,1,0:T(8,128)(2,1)S(1)}, bf16[2,64,512]{2,1,0:T(8,128)(2,1)S(1)}, u32[]{:S(2)}, u32[]{:S(2)}) collective-permute-start(bf16[2,64,512]{2,1,0:T(8,128)(2,1)S(1)} %get-tuple-element.28), channel_id=1, source_target_pairs={{2,0},{0,2},{3,1},{1,3},{6,4},{4,6},{7,5},{5,7},{10,8},{8,10},{11,... | collective-permute-start | bytes 393224 | tf_op jit(solution)/shard_map/ppermute | solution.py:241
  7.4 8.4 %collective-permute-start.5 = (bf16[1,64,512]{2,1,0:T(8,128)(2,1)S(1)}, bf16[1,64,512]{2,1,0:T(8,128)(2,1)S(1)}, u32[]{:S(2)}, u32[]{:S(2)}) collective-permute-start(bf16[1,64,512]{2,1,0:T(8,128)(2,1)S(1)} %get-tuple-element.32), channel_id=1, source_target_pairs={{2,0},{0,2},{3,1},{1,3},{6,4},{4,6},{7,5},{5,7},{10,8},{8,10},{11,... | collective-permute-start | bytes 196616 | tf_op jit(solution)/shard_map/ppermute | solution.py:241
  7.5 9.2 %collective-permute-start.3 = (bf16[1,64,512]{2,1,0:T(8,128)(2,1)S(1)}, bf16[1,64,512]{2,1,0:T(8,128)(2,1)S(1)}, u32[]{:S(2)}, u32[]{:S(2)}) collective-permute-start(bf16[1,64,512]{2,1,0:T(8,128)(2,1)S(1)} %get-tuple-element.29), channel_id=1, source_target_pairs={{8,0},{12,4},{0,8},{4,12},{9,1},{13,5},{1,9},{5,13},{10,2},{14,6},... | collective-permute-start | bytes 196616 | tf_op jit(solution)/shard_map/ppermute | solution.py:241
  10.5 8.9 %collective-permute-start.4 = (bf16[1,64,512]{2,1,0:T(8,128)(2,1)S(1)}, bf16[1,64,512]{2,1,0:T(8,128)(2,1)S(1)}, u32[]{:S(2)}, u32[]{:S(2)}) collective-permute-start(bf16[1,64,512]{2,1,0:T(8,128)(2,1)S(1)} %get-tuple-element.30), channel_id=1, source_target_pairs={{10,0},{8,2},{14,4},{12,6},{2,8},{0,10},{6,12},{4,14},{11,1},{9,3}... | collective-permute-start | bytes 196616 | tf_op jit(solution)/shard_map/ppermute | solution.py:241
  11.8 7.6 %collective-permute-start.2 = (bf16[1,64,512]{2,1,0:T(8,128)(2,1)S(1)}, bf16[1,64,512]{2,1,0:T(8,128)(2,1)S(1)}, u32[]{:S(2)}, u32[]{:S(2)}) collective-permute-start(bf16[1,64,512]{2,1,0:T(8,128)(2,1)S(1)} %sum_far_share.1.refs_2_), channel_id=1, source_target_pairs={{12,0},{8,4},{4,8},{0,12},{13,1},{9,5},{5,9},{1,13},{14,2},{10,6},... | collective-permute-start | bytes 196616 | tf_op jit(solution)/shard_map/ppermute | solution.py:241
  15.8 4.3 %collective-permute-start.6 = (bf16[1,64,512]{2,1,0:T(8,128)(2,1)S(1)}, bf16[1,64,512]{2,1,0:T(8,128)(2,1)S(1)}, u32[]{:S(2)}, u32[]{:S(2)}) collective-permute-start(bf16[1,64,512]{2,1,0:T(8,128)(2,1)S(1)} %sum_near_share.1), channel_id=1, source_target_pairs={{4,0},{0,4},{12,8},{8,12},{5,1},{1,5},{13,9},{9,13},{6,2},{2,6},{1... | collective-permute-start | bytes 196616 | tf_op jit(solution)/shard_map/ppermute | solution.py:241
  20.2 6.5 %collective-permute-start.7 = (bf16[1,64,512]{2,1,0:T(8,128)(2,1)S(1)}, bf16[1,64,512]{2,1,0:T(8,128)(2,1)S(1)}, u32[]{:S(2)}, u32[]{:S(2)}) collective-permute-start(bf16[1,64,512]{2,1,0:T(8,128)(2,1)S(1)} %sum_first_sigma.1.refs_3_), channel_id=1, source_target_pairs={{12,0},{8,4},{4,8},{0,12},{13,1},{9,5},{5,9},{1,13},{14,2},{10,6},... | collective-permute-start | bytes 196616 | tf_op jit(solution)/shard_map/ppermute | solution.py:241
  23.0 5.9 %collective-permute-start.8 = (bf16[1,64,512]{2,1,0:T(8,128)(2,1)S(1)}, bf16[1,64,512]{2,1,0:T(8,128)(2,1)S(1)}, u32[]{:S(2)}, u32[]{:S(2)}) collective-permute-start(bf16[1,64,512]{2,1,0:T(8,128)(2,1)S(1)} %sum_first_sigma.1.refs_3_), channel_id=1, source_target_pairs={{8,0},{12,4},{0,8},{4,12},{9,1},{13,5},{1,9},{5,13},{10,2},{14,6},... | collective-permute-start | bytes 196616 | tf_op jit(solution)/shard_map/ppermute | solution.py:241
  23.0 7.4 %collective-permute-start.9 = (bf16[1,64,512]{2,1,0:T(8,128)(2,1)S(1)}, bf16[1,64,512]{2,1,0:T(8,128)(2,1)S(1)}, u32[]{:S(2)}, u32[]{:S(2)}) collective-permute-start(bf16[1,64,512]{2,1,0:T(8,128)(2,1)S(1)} %sum_first_sigma.1.refs_3_), channel_id=1, source_target_pairs={{4,0},{0,4},{12,8},{8,12},{5,1},{1,5},{13,9},{9,13},{6,2},{2,6},{1... | collective-permute-start | bytes 196616 | tf_op jit(solution)/shard_map/ppermute | solution.py:241
  24.6 6.6 %collective-permute-start.14 = (bf16[1,64,512]{2,1,0:T(8,128)(2,1)S(1)}, bf16[1,64,512]{2,1,0:T(8,128)(2,1)S(1)}, u32[]{:S(2)}, u32[]{:S(2)}) collective-permute-start(bf16[1,64,512]{2,1,0:T(8,128)(2,1)S(1)} %sum_first_sigma.1.refs_3_), channel_id=1, source_target_pairs={{6,0},{4,2},{2,4},{0,6},{14,8},{12,10},{10,12},{8,14},{7,1},{5,3},... | collective-permute-start | bytes 196616 | tf_op jit(solution)/shard_map/ppermute | solution.py:241
  25.9 5.3 %collective-permute-start.15 = (bf16[1,64,512]{2,1,0:T(8,128)(2,1)S(1)}, bf16[1,64,512]{2,1,0:T(8,128)(2,1)S(1)}, u32[]{:S(2)}, u32[]{:S(2)}) collective-permute-start(bf16[1,64,512]{2,1,0:T(8,128)(2,1)S(1)} %sum_first_sigma.1.refs_3_), channel_id=1, source_target_pairs={{2,0},{0,2},{3,1},{1,3},{6,4},{4,6},{7,5},{5,7},{10,8},{8,10},{11,... | collective-permute-start | bytes 196616 | tf_op jit(solution)/shard_map/ppermute | solution.py:241
  26.7 5.6 %collective-permute-start.12 = (bf16[1,64,512]{2,1,0:T(8,128)(2,1)S(1)}, bf16[1,64,512]{2,1,0:T(8,128)(2,1)S(1)}, u32[]{:S(2)}, u32[]{:S(2)}) collective-permute-start(bf16[1,64,512]{2,1,0:T(8,128)(2,1)S(1)} %collective-permute-done.7.refs_0_), channel_id=1, source_target_pairs={{2,0},{0,2},{3,1},{1,3},{6,4},{4,6},{7,5},{5,7},{10,8},{8,10},{11,... | collective-permute-start | bytes 196616 | tf_op jit(solution)/shard_map/ppermute | solution.py:241
  28.8 4.4 %collective-permute-start.13 = (bf16[1,64,512]{2,1,0:T(8,128)(2,1)S(1)}, bf16[1,64,512]{2,1,0:T(8,128)(2,1)S(1)}, u32[]{:S(2)}, u32[]{:S(2)}) collective-permute-start(bf16[1,64,512]{2,1,0:T(8,128)(2,1)S(1)} %collective-permute-done.8.refs_1_), channel_id=1, source_target_pairs={{2,0},{0,2},{3,1},{1,3},{6,4},{4,6},{7,5},{5,7},{10,8},{8,10},{11,... | collective-permute-start | bytes 196616 | tf_op jit(solution)/shard_map/ppermute | solution.py:241
  30.4 3.0 %collective-permute-start.10 = (bf16[1,256,512]{2,1,0:T(8,128)(2,1)S(1)}, bf16[1,256,512]{2,1,0:T(8,128)(2,1)S(1)}, u32[]{:S(2)}, u32[]{:S(2)}) collective-permute-start(bf16[1,256,512]{2,1,0:T(8,128)(2,1)S(1)} %place_own_sector.1.sigma_own.own), channel_id=1, source_target_pairs={{1,0},{0,1},{3,2},{2,3},{5,4},{4,5},{7,6},{6,7},{9,8},{8,9},{11,10... | collective-permute-start | bytes 786440 | tf_op jit(solution)/shard_map/ppermute | solution.py:241
  33.3 1.6 %collective-permute-start.16 = (bf16[1,256,512]{2,1,0:T(8,128)(2,1)S(1)}, bf16[1,256,512]{2,1,0:T(8,128)(2,1)S(1)}, u32[]{:S(2)}, u32[]{:S(2)}) collective-permute-start(bf16[1,256,512]{2,1,0:T(8,128)(2,1)S(1)} %place_other_sectors.1.across_own), channel_id=1, source_target_pairs={{1,0},{0,1},{3,2},{2,3},{5,4},{4,5},{7,6},{6,7},{9,8},{8,9},{11,10... | collective-permute-start | bytes 786440 | tf_op jit(solution)/shard_map/ppermute | solution.py:241
  36.0 8.7 %collective-permute-start.17 = (bf16[1,64,512]{2,1,0:T(8,128)(2,1)S(1)}, bf16[1,64,512]{2,1,0:T(8,128)(2,1)S(1)}, u32[]{:S(2)}, u32[]{:S(2)}) collective-permute-start(bf16[1,64,512]{2,1,0:T(8,128)(2,1)S(1)} %get-tuple-element.41), channel_id=1, source_target_pairs={{12,0},{8,4},{4,8},{0,12},{13,1},{9,5},{5,9},{1,13},{14,2},{10,6},... | collective-permute-start | bytes 196616 | tf_op jit(solution)/shard_map/ppermute | solution.py:241
  38.6 6.4 %collective-permute-start.18 = (bf16[1,64,512]{2,1,0:T(8,128)(2,1)S(1)}, bf16[1,64,512]{2,1,0:T(8,128)(2,1)S(1)}, u32[]{:S(2)}, u32[]{:S(2)}) collective-permute-start(bf16[1,64,512]{2,1,0:T(8,128)(2,1)S(1)} %get-tuple-element.42), channel_id=1, source_target_pairs={{8,0},{12,4},{0,8},{4,12},{9,1},{13,5},{1,9},{5,13},{10,2},{14,6},... | collective-permute-start | bytes 196616 | tf_op jit(solution)/shard_map/ppermute | solution.py:241
  38.6 6.4 %collective-permute-start.19 = (bf16[1,64,512]{2,1,0:T(8,128)(2,1)S(1)}, bf16[1,64,512]{2,1,0:T(8,128)(2,1)S(1)}, u32[]{:S(2)}, u32[]{:S(2)}) collective-permute-start(bf16[1,64,512]{2,1,0:T(8,128)(2,1)S(1)} %get-tuple-element.43), channel_id=1, source_target_pairs={{4,0},{0,4},{12,8},{8,12},{5,1},{1,5},{13,9},{9,13},{6,2},{2,6},{1... | collective-permute-start | bytes 196616 | tf_op jit(solution)/shard_map/ppermute | solution.py:241
  41.0 3.8 %collective-permute-start.11 = (f32[3,8,128]{2,1,0:T(8,128)S(1)}, f32[3,8,128]{2,1,0:T(8,128)S(1)}, u32[]{:S(2)}, u32[]{:S(2)}) collective-permute-start(f32[3,8,128]{2,1,0:T(8,128)S(1)} %sums_for_rayleigh.1.refs_0_.refs_4_), channel_id=1, source_target_pairs={{2,0},{0,2},{3,1},{1,3},{6,4},{4,6},{7,5},{5,7},{10,8},{8,10},{11,... | collective-permute-start | bytes 36872 | tf_op jit(solution)/shard_map/ppermute | solution.py:241
  45.0 6.7 %collective-permute-start.20 = (bf16[1,64,512]{2,1,0:T(8,128)(2,1)S(1)}, bf16[1,64,512]{2,1,0:T(8,128)(2,1)S(1)}, u32[]{:S(2)}, u32[]{:S(2)}) collective-permute-start(bf16[1,64,512]{2,1,0:T(8,128)(2,1)S(1)} %sum_second_sigma.1.refs_3_), channel_id=1, source_target_pairs={{12,0},{8,4},{4,8},{0,12},{13,1},{9,5},{5,9},{1,13},{14,2},{10,6},... | collective-permute-start | bytes 196616 | tf_op jit(solution)/shard_map/ppermute | solution.py:241
  47.6 6.1 %collective-permute-start.21 = (bf16[1,64,512]{2,1,0:T(8,128)(2,1)S(1)}, bf16[1,64,512]{2,1,0:T(8,128)(2,1)S(1)}, u32[]{:S(2)}, u32[]{:S(2)}) collective-permute-start(bf16[1,64,512]{2,1,0:T(8,128)(2,1)S(1)} %sum_second_sigma.1.refs_3_), channel_id=1, source_target_pairs={{8,0},{12,4},{0,8},{4,12},{9,1},{13,5},{1,9},{5,13},{10,2},{14,6},... | collective-permute-start | bytes 196616 | tf_op jit(solution)/shard_map/ppermute | solution.py:241
  47.6 6.1 %collective-permute-start.22 = (bf16[1,64,512]{2,1,0:T(8,128)(2,1)S(1)}, bf16[1,64,512]{2,1,0:T(8,128)(2,1)S(1)}, u32[]{:S(2)}, u32[]{:S(2)}) collective-permute-start(bf16[1,64,512]{2,1,0:T(8,128)(2,1)S(1)} %sum_second_sigma.1.refs_3_), channel_id=1, source_target_pairs={{4,0},{0,4},{12,8},{8,12},{5,1},{1,5},{13,9},{9,13},{6,2},{2,6},{1... | collective-permute-start | bytes 196616 | tf_op jit(solution)/shard_map/ppermute | solution.py:241

commit v16 on v14

--- a/solution.py
+++ b/solution.py
@@ -208,14 +208,14 @@
     second[0] = (sigma_factor * sigma - wave_factor * wave).astype(second.dtype)
 
 
-def join_kernel(factors, sigma_own, *refs):
+def join_kernel(order, factors, sigma_own, *refs):
     pieces, (out, held, sems) = refs[:-3], refs[-3:]
     _, share, columns = pieces[0].shape
     place = lax.axis_index("ops")
     scale = jnp.broadcast_to(factors[0][:1, :1], (share, columns))
     shift = jnp.broadcast_to(factors[1][:1, :1], (share, columns))
     copies = []
-    for step, piece in zip(reversed(range(len(pieces))), pieces):
+    for step, piece in zip(order, pieces):
         rows = pl.ds(pl.multiple_of((place ^ step) * share, share), share)
         moved = shift * sigma_own[0, rows, :].astype(jnp.float32)
         held[step] = scale * piece[0].astype(jnp.float32) - moved
@@ -279,6 +279,7 @@
         )
 
     farthest_first = list(reversed(range(ops_count)))
+    send_order = farthest_first[1:2] + farthest_first[:1] + farthest_first[2:]
     arrived = partner(wavefunction, {"rep": 1})
     left_own, left_other = call(
         load_kernel,
@@ -339,16 +340,16 @@
     order = [nearest] + [spot for spot in rest if spot[0] in direct and spot != nearest]
     received += [partner(rest[spot], {"ops": spot[0][0], "sec": spot[1]}) for spot in order]
     first_share = summed("sum_first_sigma", *[(piece, 1) for piece in met], *received, after=(mixing,))
-    along_ops = {along: partner(first_share, {"ops": along}) for along in farthest_first}
+    along_ops = {along: partner(first_share, {"ops": along}) for along in send_order}
     sigma_own = call(
-        lambda *refs: place_kernel([(along, 0) for along in farthest_first], *refs),
+        lambda *refs: place_kernel([(along, 0) for along in send_order], *refs),
         "place_own_sector",
         shape(1, rows, columns),
         [],
         *along_ops.values(),
     )
     sigma_other = partner(sigma_own, {"rep": 1})
-    spots = [(along, across) for along in farthest_first for across in range(1, sectors)]
+    spots = [(along, across) for along in send_order for across in range(1, sectors)]
     pieces = [
         partner(first_share, {"ops": along, "sec": across})
         if along < 2
@@ -392,7 +393,7 @@
         across_other,
         scratch=[pltpu.VMEM((rows, columns), f32)],
     )
-    received = [partner(shares[step], {"ops": step}) for step in farthest_first[:-1]]
+    received = [partner(shares[step], {"ops": step}) for step in send_order[:-1]]
     sums = call(
         sums_kernel,
         "sums_for_rayleigh",
@@ -416,13 +417,13 @@
         *sums,
     )
     second_sigma = call(
-        join_kernel,
+        lambda *refs: join_kernel(send_order, *refs),
         "join_second_sigma",
         shape(1, rows, columns, dtype=f32),
         [],
         factors,
         sigma_own,
-        *[partner(second_share, {"ops": step}) for step in farthest_first],
+        *[partner(second_share, {"ops": step}) for step in send_order],
         scratch=[
             pltpu.VMEM((ops_count, share, columns), f32),
             pltpu.SemaphoreType.DMA((ops_count,)),

time: 54.2 us -> 54 us (level)
  no operation moved by 1% of the time
where the time goes in v16:
time: 54 us; the launch traced here: 53.9 us
  starting transfers between devices  30.2 us (56%)
  waiting for transfers between devices  13.6 us (25%)
  Pallas kernels  9.18 us (17%)
  between operations  0.85 us (2%)
    ppermute x23, starting transfers between devices, partner(): return lax.ppermute(value, axes, pairs)  30.2 us
    ppermute x23, waiting for transfers between devices, partner(): return lax.ppermute(value, axes, pairs)  13.6 us
    pallas_call x14, Pallas kernels, call(): pl.pallas_call(kernel, out_shape=out_shape, in_specs=list(in_specs) + [in...  9.18 us
  transfers between devices with their start and end apart: 23, of which 12 were waited for; matrix products, arithmetic and copies ran while one was open for 0% of the time, Pallas kernels for 10%

profile of v16, /device:TPU:0, one launch (start us, length us, event | category | flops | bytes accessed | tf_op | source)
XLA Modules:
  0.0 53.9 jit_solution(9174776938612635251)
XLA Ops:
  0.6 0.0 copy-start.1
  0.6 0.0 copy-start.3
  0.7 0.0 copy-start.2
  0.7 0.0 copy-start.4
  0.7 0.0 copy-start
  0.7 0.5 collective-permute-start
  1.2 1.4 %load_operators.1 = (bf16[4,256,256]{2,1,0:T(8,128)(2,1)S(1)}, bf16[4,256,256]{2,1,0:T(8,128)(2,1)S(1)}) custom-call(bf16[4,512,512]{2,1,0:T(8,128)(2,1)} %left_ref.1), custom_call_target="tpu_custom_call" | custom-call | tf_op jit(solution)/shard_map/load_operators/pallas_call | solution.py:259
  2.6 0.0 copy-done.1
  2.6 0.0 copy-done.3
  2.7 0.0 copy-done.2
  2.7 0.2 tables_for_first_sigma.1
  2.9 0.0 collective-permute-done.refs_6_
  2.9 1.7 %first_sigma_terms.1 = (bf16[256,512]{1,0:T(8,128)(2,1)S(1)}, f32[2,64,512]{2,1,0:T(8,128)S(1)}, bf16[2,64,512]{2,1,0:T(8,128)(2,1)S(1)}, bf16[1,64,512]{2,1,0:T...) custom-call(s32[2,2]{1,0:T(2,128)S(1)} %copy-done.3, ...), custom_call_target="tpu_custom_call" | custom-call | tf_op jit(solution)/shard_map/first_sigma_terms/pallas_call | solution.py:259
  4.6 2.8 %collective-permute-start.1 = (bf16[2,64,512]{2,1,0:T(8,128)(2,1)S(1)}, bf16[2,64,512]{2,1,0:T(8,128)(2,1)S(1)}, u32[]{:S(2)}, u32[]{:S(2)}) collective-permute-start(bf16[2,64,512]{2,1,0:T(8,128)(2,1)S(1)} %get-tuple-element.28), channel_id=1, source_target_pairs={{2,0},{0,2},{3,1},{1,3},{6,4},{4,6},{7,5},{5,7},{10,8},{8,10},{11,... | collective-permute-start | bytes 393224 | tf_op jit(solution)/shard_map/ppermute | solution.py:241
  7.4 1.6 %collective-permute-start.3 = (bf16[1,64,512]{2,1,0:T(8,128)(2,1)S(1)}, bf16[1,64,512]{2,1,0:T(8,128)(2,1)S(1)}, u32[]{:S(2)}, u32[]{:S(2)}) collective-permute-start(bf16[1,64,512]{2,1,0:T(8,128)(2,1)S(1)} %get-tuple-element.29), channel_id=1, source_target_pairs={{4,0},{0,4},{12,8},{8,12},{5,1},{1,5},{13,9},{9,13},{6,2},{2,6},{1... | collective-permute-start | bytes 196616 | tf_op jit(solution)/shard_map/ppermute | solution.py:241
  9.0 2.6 %collective-permute-start.4 = (bf16[1,64,512]{2,1,0:T(8,128)(2,1)S(1)}, bf16[1,64,512]{2,1,0:T(8,128)(2,1)S(1)}, u32[]{:S(2)}, u32[]{:S(2)}) collective-permute-start(bf16[1,64,512]{2,1,0:T(8,128)(2,1)S(1)} %get-tuple-element.30), channel_id=1, source_target_pairs={{8,0},{12,4},{0,8},{4,12},{9,1},{13,5},{1,9},{5,13},{10,2},{14,6},... | collective-permute-start | bytes 196616 | tf_op jit(solution)/shard_map/ppermute | solution.py:241
  11.5 0.3 collective-permute-start.5
  11.8 1.4 %collective-permute-start.6 = (bf16[1,64,512]{2,1,0:T(8,128)(2,1)S(1)}, bf16[1,64,512]{2,1,0:T(8,128)(2,1)S(1)}, u32[]{:S(2)}, u32[]{:S(2)}) collective-permute-start(bf16[1,64,512]{2,1,0:T(8,128)(2,1)S(1)} %get-tuple-element.32), channel_id=1, source_target_pairs={{6,0},{4,2},{2,4},{0,6},{14,8},{12,10},{10,12},{8,14},{7,1},{5,3},... | collective-permute-start | bytes 196616 | tf_op jit(solution)/shard_map/ppermute | solution.py:241
  13.2 0.0 collective-permute-done.1.refs_1_
  13.3 3.7 %collective-permute-start.2 = (bf16[1,64,512]{2,1,0:T(8,128)(2,1)S(1)}, bf16[1,64,512]{2,1,0:T(8,128)(2,1)S(1)}, u32[]{:S(2)}, u32[]{:S(2)}) collective-permute-start(bf16[1,64,512]{2,1,0:T(8,128)(2,1)S(1)} %sum_far_share.1), channel_id=1, source_target_pairs={{12,0},{8,4},{4,8},{0,12},{13,1},{9,5},{5,9},{1,13},{14,2},{10,6},... | collective-permute-start | bytes 196616 | tf_op jit(solution)/shard_map/ppermute | solution.py:241
  16.9 0.8 %tables_for_second_sigma.1 = (f32[4,2,8,128]{3,2,1,0:T(8,128)S(1)}, f32[256,512]{1,0:T(8,128)S(1)}) custom-call(s32[2,2]{1,0:T(2,128)S(1)} %copy-done.3, s32[4,2,8]{2,1,0:T(2,128)S(1)} %bitcast.2, f32[4,8]{1,0:T(4,128)S(1)} %copy-done.4, bf16[256,512]{1,0:T(8,128)(2,1)S(1)} %get-tuple-element.33._.wave_other), custom_call_target="tpu_custom_call" | custom-call | tf_op jit(solution)/shard_map/tables_for_second_sigma/pallas_call | solution.py:259
  17.7 0.0 collective-permute-done.3.refs_3_
  17.7 0.0 collective-permute-done.4.refs_4_
  17.8 2.2 %collective-permute-done.5.refs_5_ = bf16[1,64,512]{2,1,0:T(8,128)(2,1)S(1)} collective-permute-done((bf16[1,64,512]{2,1,0:T(8,128)(2,1)S(1)}, bf16[1,64,512]{2,1,0:T(8,128)(2,1)S(1)}, u32[]{:S(2)}, u32[]{:S(2)}) %collective-permute-start.5) | collective-permute-done | bytes 65568 | tf_op jit(solution)/shard_map/ppermute | solution.py:241
  20.0 0.0 collective-permute-done.6.refs_6_
  20.0 0.0 collective-permute-done.2.refs_2_
  20.0 0.1 sum_first_sigma.1.refs_3_
  20.0 1.3 %collective-permute-start.7 = (bf16[1,64,512]{2,1,0:T(8,128)(2,1)S(1)}, bf16[1,64,512]{2,1,0:T(8,128)(2,1)S(1)}, u32[]{:S(2)}, u32[]{:S(2)}) collective-permute-start(bf16[1,64,512]{2,1,0:T(8,128)(2,1)S(1)} %sum_first_sigma.1.refs_3_), channel_id=1, source_target_pairs={{8,0},{12,4},{0,8},{4,12},{9,1},{13,5},{1,9},{5,13},{10,2},{14,6},... | collective-permute-start | bytes 196616 | tf_op jit(solution)/shard_map/ppermute | solution.py:241
  21.4 2.1 %collective-permute-start.8 = (bf16[1,64,512]{2,1,0:T(8,128)(2,1)S(1)}, bf16[1,64,512]{2,1,0:T(8,128)(2,1)S(1)}, u32[]{:S(2)}, u32[]{:S(2)}) collective-permute-start(bf16[1,64,512]{2,1,0:T(8,128)(2,1)S(1)} %sum_first_sigma.1.refs_3_), channel_id=1, source_target_pairs={{12,0},{8,4},{4,8},{0,12},{13,1},{9,5},{5,9},{1,13},{14,2},{10,6},... | collective-permute-start | bytes 196616 | tf_op jit(solution)/shard_map/ppermute | solution.py:241
  23.5 0.2 collective-permute-start.9
  23.7 2.1 %collective-permute-start.14 = (bf16[1,64,512]{2,1,0:T(8,128)(2,1)S(1)}, bf16[1,64,512]{2,1,0:T(8,128)(2,1)S(1)}, u32[]{:S(2)}, u32[]{:S(2)}) collective-permute-start(bf16[1,64,512]{2,1,0:T(8,128)(2,1)S(1)} %sum_first_sigma.1.refs_3_), channel_id=1, source_target_pairs={{6,0},{4,2},{2,4},{0,6},{14,8},{12,10},{10,12},{8,14},{7,1},{5,3},... | collective-permute-start | bytes 196616 | tf_op jit(solution)/shard_map/ppermute | solution.py:241
  25.8 1.2 %collective-permute-start.15 = (bf16[1,64,512]{2,1,0:T(8,128)(2,1)S(1)}, bf16[1,64,512]{2,1,0:T(8,128)(2,1)S(1)}, u32[]{:S(2)}, u32[]{:S(2)}) collective-permute-start(bf16[1,64,512]{2,1,0:T(8,128)(2,1)S(1)} %sum_first_sigma.1.refs_3_), channel_id=1, source_target_pairs={{2,0},{0,2},{3,1},{1,3},{6,4},{4,6},{7,5},{5,7},{10,8},{8,10},{11,... | collective-permute-start | bytes 196616 | tf_op jit(solution)/shard_map/ppermute | solution.py:241
  27.0 0.0 collective-permute-done.7.refs_0_
  27.0 0.8 %collective-permute-start.12 = (bf16[1,64,512]{2,1,0:T(8,128)(2,1)S(1)}, bf16[1,64,512]{2,1,0:T(8,128)(2,1)S(1)}, u32[]{:S(2)}, u32[]{:S(2)}) collective-permute-start(bf16[1,64,512]{2,1,0:T(8,128)(2,1)S(1)} %collective-permute-done.7.refs_0_), channel_id=1, source_target_pairs={{2,0},{0,2},{3,1},{1,3},{6,4},{4,6},{7,5},{5,7},{10,8},{8,10},{11,... | collective-permute-start | bytes 196616 | tf_op jit(solution)/shard_map/ppermute | solution.py:241
  27.8 0.2 collective-permute-done.8.refs_1_
  28.0 1.1 %collective-permute-start.13 = (bf16[1,64,512]{2,1,0:T(8,128)(2,1)S(1)}, bf16[1,64,512]{2,1,0:T(8,128)(2,1)S(1)}, u32[]{:S(2)}, u32[]{:S(2)}) collective-permute-start(bf16[1,64,512]{2,1,0:T(8,128)(2,1)S(1)} %collective-permute-done.8.refs_1_), channel_id=1, source_target_pairs={{2,0},{0,2},{3,1},{1,3},{6,4},{4,6},{7,5},{5,7},{10,8},{8,10},{11,... | collective-permute-start | bytes 196616 | tf_op jit(solution)/shard_map/ppermute | solution.py:241
  29.1 0.0 collective-permute-done.9.refs_2_
  29.2 0.1 collective-permute-start.10
  29.2 0.3 collective-permute-done.14.refs_2_
  29.5 1.1 %collective-permute-done.15.refs_3_ = bf16[1,64,512]{2,1,0:T(8,128)(2,1)S(1)} collective-permute-done((bf16[1,64,512]{2,1,0:T(8,128)(2,1)S(1)}, bf16[1,64,512]{2,1,0:T(8,128)(2,1)S(1)}, u32[]{:S(2)}, u32[]{:S(2)}) %collective-permute-start.15) | collective-permute-done | bytes 65568 | tf_op jit(solution)/shard_map/ppermute | solution.py:241
  30.6 0.7 %collective-permute-done.12.refs_0_ = bf16[1,64,512]{2,1,0:T(8,128)(2,1)S(1)} collective-permute-done((bf16[1,64,512]{2,1,0:T(8,128)(2,1)S(1)}, bf16[1,64,512]{2,1,0:T(8,128)(2,1)S(1)}, u32[]{:S(2)}, u32[]{:S(2)}) %collective-permute-start.12) | collective-permute-done | bytes 65568 | tf_op jit(solution)/shard_map/ppermute | solution.py:241
  31.3 0.9 %collective-permute-done.13.refs_1_ = bf16[1,64,512]{2,1,0:T(8,128)(2,1)S(1)} collective-permute-done((bf16[1,64,512]{2,1,0:T(8,128)(2,1)S(1)}, bf16[1,64,512]{2,1,0:T(8,128)(2,1)S(1)}, u32[]{:S(2)}, u32[]{:S(2)}) %collective-permute-start.13) | collective-permute-done | bytes 65568 | tf_op jit(solution)/shard_map/ppermute | solution.py:241
  32.3 0.1 collective-permute-start.16
  32.4 0.0 collective-permute-done.10.sigma_other.other
  32.4 1.0 %left_products.1 = (f32[4,256,512]{2,1,0:T(8,128)S(1)}, f32[1,4,256,512]{3,2,1,0:T(8,128)S(1)}) custom-call(bf16[4,256,256]{2,1,0:T(8,128)(2,1)S(1)} %get-tuple-element.23._.refs_2_.left_own, bf16[4,256,256]{2,1,0:T(8,128)(2,1)S(1)} %get-tuple-element.26.refs_3_.left_other, bf16[1,256,512]{2,1,0:T(8,128)(2,1)S(1)} %place_own_sector.1.sigma_own.own.refs_1_, ...), custom_call_target="tpu_custom_call" | custom-call | tf_op jit(solution)/shard_map/left_products/pallas_call | solution.py:259
  33.3 0.5 collective-permute-done.16.other
  33.9 1.1 %second_sigma_terms.1 = (f32[1,64,512]{2,1,0:T(8,128)S(1)}, bf16[1,64,512]{2,1,0:T(8,128)(2,1)S(1)}, bf16[1,64,512]{2,1,0:T(8,128)(2,1)S(1)}, bf16[1,64,512]{2,1,0:T(8,128)(2,1)S(1)}) custom-call(f32[4,2,8,128]{3,2,1,0:T(8,128)S(1)} %get-tuple-element.34.refs_7_.mixing, f32[256,512]{1,0:T(8,128)S(1)} %get-tuple-element.37.live, ...), custom_call_target="tpu_custom_call" | custom-call | tf_op jit(solution)/shard_map/second_sigma_terms/pallas_call | solution.py:259
  35.0 1.4 %collective-permute-start.17 = (bf16[1,64,512]{2,1,0:T(8,128)(2,1)S(1)}, bf16[1,64,512]{2,1,0:T(8,128)(2,1)S(1)}, u32[]{:S(2)}, u32[]{:S(2)}) collective-permute-start(bf16[1,64,512]{2,1,0:T(8,128)(2,1)S(1)} %get-tuple-element.41), channel_id=1, source_target_pairs={{8,0},{12,4},{0,8},{4,12},{9,1},{13,5},{1,9},{5,13},{10,2},{14,6},... | collective-permute-start | bytes 196616 | tf_op jit(solution)/shard_map/ppermute | solution.py:241
  36.4 1.8 %collective-permute-start.18 = (bf16[1,64,512]{2,1,0:T(8,128)(2,1)S(1)}, bf16[1,64,512]{2,1,0:T(8,128)(2,1)S(1)}, u32[]{:S(2)}, u32[]{:S(2)}) collective-permute-start(bf16[1,64,512]{2,1,0:T(8,128)(2,1)S(1)} %get-tuple-element.42), channel_id=1, source_target_pairs={{12,0},{8,4},{4,8},{0,12},{13,1},{9,5},{5,9},{1,13},{14,2},{10,6},... | collective-permute-start | bytes 196616 | tf_op jit(solution)/shard_map/ppermute | solution.py:241
  38.2 0.4 collective-permute-start.19
  38.6 0.5 sums_for_rayleigh.1.refs_0_.refs_4_
  39.1 1.2 %collective-permute-start.11 = (f32[3,8,128]{2,1,0:T(8,128)S(1)}, f32[3,8,128]{2,1,0:T(8,128)S(1)}, u32[]{:S(2)}, u32[]{:S(2)}) collective-permute-start(f32[3,8,128]{2,1,0:T(8,128)S(1)} %sums_for_rayleigh.1.refs_0_.refs_4_), channel_id=1, source_target_pairs={{2,0},{0,2},{3,1},{1,3},{6,4},{4,6},{7,5},{5,7},{10,8},{8,10},{11,... | collective-permute-start | bytes 36872 | tf_op jit(solution)/shard_map/ppermute | solution.py:241
  40.3 2.5 %collective-permute-done.11.refs_1_.refs_5_ = f32[3,8,128]{2,1,0:T(8,128)S(1)} collective-permute-done((f32[3,8,128]{2,1,0:T(8,128)S(1)}, f32[3,8,128]{2,1,0:T(8,128)S(1)}, u32[]{:S(2)}, u32[]{:S(2)}) %collective-permute-start.11) | collective-permute-done | bytes 12320 | tf_op jit(solution)/shard_map/ppermute | solution.py:241
  42.8 0.4 collective-permute-done.17.refs_1_
  43.3 0.0 collective-permute-done.18.refs_2_
  43.3 1.0 %collective-permute-done.19.refs_3_ = bf16[1,64,512]{2,1,0:T(8,128)(2,1)S(1)} collective-permute-done((bf16[1,64,512]{2,1,0:T(8,128)(2,1)S(1)}, bf16[1,64,512]{2,1,0:T(8,128)(2,1)S(1)}, u32[]{:S(2)}, u32[]{:S(2)}) %collective-permute-start.19) | collective-permute-done | bytes 65568 | tf_op jit(solution)/shard_map/ppermute | solution.py:241
  44.3 1.5 %collective-permute-start.20 = (bf16[1,64,512]{2,1,0:T(8,128)(2,1)S(1)}, bf16[1,64,512]{2,1,0:T(8,128)(2,1)S(1)}, u32[]{:S(2)}, u32[]{:S(2)}) collective-permute-start(bf16[1,64,512]{2,1,0:T(8,128)(2,1)S(1)} %sum_second_sigma.1.refs_5_), channel_id=1, source_target_pairs={{8,0},{12,4},{0,8},{4,12},{9,1},{13,5},{1,9},{5,13},{10,2},{14,6},... | collective-permute-start | bytes 196616 | tf_op jit(solution)/shard_map/ppermute | solution.py:241
  45.8 1.6 %collective-permute-start.21 = (bf16[1,64,512]{2,1,0:T(8,128)(2,1)S(1)}, bf16[1,64,512]{2,1,0:T(8,128)(2,1)S(1)}, u32[]{:S(2)}, u32[]{:S(2)}) collective-permute-start(bf16[1,64,512]{2,1,0:T(8,128)(2,1)S(1)} %sum_second_sigma.1.refs_5_), channel_id=1, source_target_pairs={{12,0},{8,4},{4,8},{0,12},{13,1},{9,5},{5,9},{1,13},{14,2},{10,6},... | collective-permute-start | bytes 196616 | tf_op jit(solution)/shard_map/ppermute | solution.py:241
  47.4 0.4 collective-permute-start.22
  47.8 1.4 %second_wave.1 = (bf16[1,256,512]{2,1,0:T(8,128)(2,1)}, f32[2,8,128]{2,1,0:T(8,128)S(1)}) custom-call(s32[2,2]{1,0:T(2,128)S(1)} %copy-done.3, bf16[256,512]{1,0:T(8,128)(2,1)S(1)} %get-tuple-element.24.refs_5_.wave_own, bf16[1,256,512]{2,1,0:T(8,128)(2,1)S(1)} %place_own_sector.1.sigma_own.own.refs_1_, f32[3,8,128]{2,1,0:T(8,128)S(1)} %sums_for_rayleigh.1.refs_0_.refs_4_, ...), custom_call_target="tpu_custom_call" | custom-call | tf_op jit(solution)/shard_map/second_wave/pallas_call | solution.py:259
  49.3 3.1 %collective-permute-done.20.refs_2_ = bf16[1,64,512]{2,1,0:T(8,128)(2,1)S(1)} collective-permute-done((bf16[1,64,512]{2,1,0:T(8,128)(2,1)S(1)}, bf16[1,64,512]{2,1,0:T(8,128)(2,1)S(1)}, u32[]{:S(2)}, u32[]{:S(2)}) %collective-permute-start.20) | collective-permute-done | bytes 65568 | tf_op jit(solution)/shard_map/ppermute | solution.py:241
  52.4 0.0 collective-permute-done.21.refs_3_
  52.4 0.6 %collective-permute-done.22.refs_4_ = bf16[1,64,512]{2,1,0:T(8,128)(2,1)S(1)} collective-permute-done((bf16[1,64,512]{2,1,0:T(8,128)(2,1)S(1)}, bf16[1,64,512]{2,1,0:T(8,128)(2,1)S(1)}, u32[]{:S(2)}, u32[]{:S(2)}) %collective-permute-start.22) | collective-permute-done | bytes 65568 | tf_op jit(solution)/shard_map/ppermute | solution.py:241
  53.0 0.9 %join_second_sigma.1 = f32[1,256,512]{2,1,0:T(8,128)} custom-call(f32[2,8,128]{2,1,0:T(8,128)S(1)} %get-tuple-element.36.refs_0_, bf16[1,256,512]{2,1,0:T(8,128)(2,1)S(1)} %place_own_sector.1.sigma_own.own.refs_1_, bf16[1,64,512]{2,1,0:T(8,128)(2,1)S(1)} %collective-permute-done.20.refs_2_, bf16[1,64,512]{2,1,0:T(8,128)(2,1)S(1)} %collective-permute-done.21.refs_3_, ...), custom_call_target="tpu_custom_call" | custom-call | tf_op jit(solution)/shard_map/join_second_sigma/pallas_call | solution.py:259
  (6 shorter events, 0.1 us)
Async XLA Ops:
  0.6 2.0 %copy-start.1 = (bf16[1,256,512]{2,1,0:T(8,128)(2,1)S(1)}, bf16[1,256,512]{2,1,0:T(8,128)(2,1)}, u32[]{:S(2)}) copy-start(bf16[1,256,512]{2,1,0:T(8,128)(2,1)} %wave.1) | copy-start | bytes 786436
  0.6 2.0 %copy-start.3 = (s32[2,2]{1,0:T(2,128)S(1)}, s32[2,2]{1,0:T(2,128)}, u32[]{:S(2)}) copy-start(s32[2,2]{1,0:T(2,128)} %sizes_ref.3) | copy-start | bytes 52
  0.7 2.0 %copy-start.2 = (s32[4,8,2]{1,2,0:T(2,128)S(1)}, s32[4,8,2]{1,2,0:T(2,128)}, u32[]{:S(2)}) copy-start(s32[4,8,2]{1,2,0:T(2,128)} %param.10) | copy-start | bytes 772
  0.7 2.0 %copy-start.4 = (f32[4,8]{1,0:T(4,128)S(1)}, f32[4,8]{1,0:T(4,128)}, u32[]{:S(2)}) copy-start(f32[4,8]{1,0:T(4,128)} %weights_ref.1) | copy-start | bytes 388
  0.7 2.2 %copy-start = (bf16[4,512,512]{2,1,0:T(8,128)(2,1)S(1)}, bf16[4,512,512]{2,1,0:T(8,128)(2,1)}, u32[]{:S(2)}) copy-start(bf16[4,512,512]{2,1,0:T(8,128)(2,1)} %right.1) | copy-start | bytes 6291460
  0.7 2.2 %collective-permute-start = (bf16[1,256,512]{2,1,0:T(8,128)(2,1)}, bf16[1,256,512]{2,1,0:T(8,128)(2,1)S(1)}, u32[]{:S(2)}, u32[]{:S(2)}) collective-permute-start(bf16[1,256,512]{2,1,0:T(8,128)(2,1)} %wave.1), channel_id=1, source_target_pairs={{1,0},{0,1},{3,2},{2,3},{5,4},{4,5},{7,6},{6,7},{9,8},{8,9},{11,10... | collective-permute-start | bytes 786440 | tf_op jit(solution)/shard_map/ppermute | solution.py:241
  4.6 8.7 %collective-permute-start.1 = (bf16[2,64,512]{2,1,0:T(8,128)(2,1)S(1)}, bf16[2,64,512]{2,1,0:T(8,128)(2,1)S(1)}, u32[]{:S(2)}, u32[]{:S(2)}) collective-permute-start(bf16[2,64,512]{2,1,0:T(8,128)(2,1)S(1)} %get-tuple-element.28), channel_id=1, source_target_pairs={{2,0},{0,2},{3,1},{1,3},{6,4},{4,6},{7,5},{5,7},{10,8},{8,10},{11,... | collective-permute-start | bytes 393224 | tf_op jit(solution)/shard_map/ppermute | solution.py:241
  7.4 10.4 %collective-permute-start.3 = (bf16[1,64,512]{2,1,0:T(8,128)(2,1)S(1)}, bf16[1,64,512]{2,1,0:T(8,128)(2,1)S(1)}, u32[]{:S(2)}, u32[]{:S(2)}) collective-permute-start(bf16[1,64,512]{2,1,0:T(8,128)(2,1)S(1)} %get-tuple-element.29), channel_id=1, source_target_pairs={{4,0},{0,4},{12,8},{8,12},{5,1},{1,5},{13,9},{9,13},{6,2},{2,6},{1... | collective-permute-start | bytes 196616 | tf_op jit(solution)/shard_map/ppermute | solution.py:241
  9.0 8.8 %collective-permute-start.4 = (bf16[1,64,512]{2,1,0:T(8,128)(2,1)S(1)}, bf16[1,64,512]{2,1,0:T(8,128)(2,1)S(1)}, u32[]{:S(2)}, u32[]{:S(2)}) collective-permute-start(bf16[1,64,512]{2,1,0:T(8,128)(2,1)S(1)} %get-tuple-element.30), channel_id=1, source_target_pairs={{8,0},{12,4},{0,8},{4,12},{9,1},{13,5},{1,9},{5,13},{10,2},{14,6},... | collective-permute-start | bytes 196616 | tf_op jit(solution)/shard_map/ppermute | solution.py:241
  11.5 8.4 %collective-permute-start.5 = (bf16[1,64,512]{2,1,0:T(8,128)(2,1)S(1)}, bf16[1,64,512]{2,1,0:T(8,128)(2,1)S(1)}, u32[]{:S(2)}, u32[]{:S(2)}) collective-permute-start(bf16[1,64,512]{2,1,0:T(8,128)(2,1)S(1)} %get-tuple-element.31), channel_id=1, source_target_pairs={{10,0},{8,2},{14,4},{12,6},{2,8},{0,10},{6,12},{4,14},{11,1},{9,3}... | collective-permute-start | bytes 196616 | tf_op jit(solution)/shard_map/ppermute | solution.py:241
  11.8 8.1 %collective-permute-start.6 = (bf16[1,64,512]{2,1,0:T(8,128)(2,1)S(1)}, bf16[1,64,512]{2,1,0:T(8,128)(2,1)S(1)}, u32[]{:S(2)}, u32[]{:S(2)}) collective-permute-start(bf16[1,64,512]{2,1,0:T(8,128)(2,1)S(1)} %get-tuple-element.32), channel_id=1, source_target_pairs={{6,0},{4,2},{2,4},{0,6},{14,8},{12,10},{10,12},{8,14},{7,1},{5,3},... | collective-permute-start | bytes 196616 | tf_op jit(solution)/shard_map/ppermute | solution.py:241
  13.3 6.7 %collective-permute-start.2 = (bf16[1,64,512]{2,1,0:T(8,128)(2,1)S(1)}, bf16[1,64,512]{2,1,0:T(8,128)(2,1)S(1)}, u32[]{:S(2)}, u32[]{:S(2)}) collective-permute-start(bf16[1,64,512]{2,1,0:T(8,128)(2,1)S(1)} %sum_far_share.1), channel_id=1, source_target_pairs={{12,0},{8,4},{4,8},{0,12},{13,1},{9,5},{5,9},{1,13},{14,2},{10,6},... | collective-permute-start | bytes 196616 | tf_op jit(solution)/shard_map/ppermute | solution.py:241
  20.0 6.9 %collective-permute-start.7 = (bf16[1,64,512]{2,1,0:T(8,128)(2,1)S(1)}, bf16[1,64,512]{2,1,0:T(8,128)(2,1)S(1)}, u32[]{:S(2)}, u32[]{:S(2)}) collective-permute-start(bf16[1,64,512]{2,1,0:T(8,128)(2,1)S(1)} %sum_first_sigma.1.refs_3_), channel_id=1, source_target_pairs={{8,0},{12,4},{0,8},{4,12},{9,1},{13,5},{1,9},{5,13},{10,2},{14,6},... | collective-permute-start | bytes 196616 | tf_op jit(solution)/shard_map/ppermute | solution.py:241
  21.4 6.6 %collective-permute-start.8 = (bf16[1,64,512]{2,1,0:T(8,128)(2,1)S(1)}, bf16[1,64,512]{2,1,0:T(8,128)(2,1)S(1)}, u32[]{:S(2)}, u32[]{:S(2)}) collective-permute-start(bf16[1,64,512]{2,1,0:T(8,128)(2,1)S(1)} %sum_first_sigma.1.refs_3_), channel_id=1, source_target_pairs={{12,0},{8,4},{4,8},{0,12},{13,1},{9,5},{5,9},{1,13},{14,2},{10,6},... | collective-permute-start | bytes 196616 | tf_op jit(solution)/shard_map/ppermute | solution.py:241
  23.5 5.6 %collective-permute-start.9 = (bf16[1,64,512]{2,1,0:T(8,128)(2,1)S(1)}, bf16[1,64,512]{2,1,0:T(8,128)(2,1)S(1)}, u32[]{:S(2)}, u32[]{:S(2)}) collective-permute-start(bf16[1,64,512]{2,1,0:T(8,128)(2,1)S(1)} %sum_first_sigma.1.refs_3_), channel_id=1, source_target_pairs={{4,0},{0,4},{12,8},{8,12},{5,1},{1,5},{13,9},{9,13},{6,2},{2,6},{1... | collective-permute-start | bytes 196616 | tf_op jit(solution)/shard_map/ppermute | solution.py:241
  23.7 5.8 %collective-permute-start.14 = (bf16[1,64,512]{2,1,0:T(8,128)(2,1)S(1)}, bf16[1,64,512]{2,1,0:T(8,128)(2,1)S(1)}, u32[]{:S(2)}, u32[]{:S(2)}) collective-permute-start(bf16[1,64,512]{2,1,0:T(8,128)(2,1)S(1)} %sum_first_sigma.1.refs_3_), channel_id=1, source_target_pairs={{6,0},{4,2},{2,4},{0,6},{14,8},{12,10},{10,12},{8,14},{7,1},{5,3},... | collective-permute-start | bytes 196616 | tf_op jit(solution)/shard_map/ppermute | solution.py:241
  25.8 4.9 %collective-permute-start.15 = (bf16[1,64,512]{2,1,0:T(8,128)(2,1)S(1)}, bf16[1,64,512]{2,1,0:T(8,128)(2,1)S(1)}, u32[]{:S(2)}, u32[]{:S(2)}) collective-permute-start(bf16[1,64,512]{2,1,0:T(8,128)(2,1)S(1)} %sum_first_sigma.1.refs_3_), channel_id=1, source_target_pairs={{2,0},{0,2},{3,1},{1,3},{6,4},{4,6},{7,5},{5,7},{10,8},{8,10},{11,... | collective-permute-start | bytes 196616 | tf_op jit(solution)/shard_map/ppermute | solution.py:241
  27.0 4.3 %collective-permute-start.12 = (bf16[1,64,512]{2,1,0:T(8,128)(2,1)S(1)}, bf16[1,64,512]{2,1,0:T(8,128)(2,1)S(1)}, u32[]{:S(2)}, u32[]{:S(2)}) collective-permute-start(bf16[1,64,512]{2,1,0:T(8,128)(2,1)S(1)} %collective-permute-done.7.refs_0_), channel_id=1, source_target_pairs={{2,0},{0,2},{3,1},{1,3},{6,4},{4,6},{7,5},{5,7},{10,8},{8,10},{11,... | collective-permute-start | bytes 196616 | tf_op jit(solution)/shard_map/ppermute | solution.py:241
  28.0 4.3 %collective-permute-start.13 = (bf16[1,64,512]{2,1,0:T(8,128)(2,1)S(1)}, bf16[1,64,512]{2,1,0:T(8,128)(2,1)S(1)}, u32[]{:S(2)}, u32[]{:S(2)}) collective-permute-start(bf16[1,64,512]{2,1,0:T(8,128)(2,1)S(1)} %collective-permute-done.8.refs_1_), channel_id=1, source_target_pairs={{2,0},{0,2},{3,1},{1,3},{6,4},{4,6},{7,5},{5,7},{10,8},{8,10},{11,... | collective-permute-start | bytes 196616 | tf_op jit(solution)/shard_map/ppermute | solution.py:241
  29.2 3.2 %collective-permute-start.10 = (bf16[1,256,512]{2,1,0:T(8,128)(2,1)S(1)}, bf16[1,256,512]{2,1,0:T(8,128)(2,1)S(1)}, u32[]{:S(2)}, u32[]{:S(2)}) collective-permute-start(bf16[1,256,512]{2,1,0:T(8,128)(2,1)S(1)} %place_own_sector.1.sigma_own.own.refs_1_), channel_id=1, source_target_pairs={{1,0},{0,1},{3,2},{2,3},{5,4},{4,5},{7,6},{6,7},{9,8},{8,9},{11,10... | collective-permute-start | bytes 786440 | tf_op jit(solution)/shard_map/ppermute | solution.py:241
  32.3 1.6 %collective-permute-start.16 = (bf16[1,256,512]{2,1,0:T(8,128)(2,1)S(1)}, bf16[1,256,512]{2,1,0:T(8,128)(2,1)S(1)}, u32[]{:S(2)}, u32[]{:S(2)}) collective-permute-start(bf16[1,256,512]{2,1,0:T(8,128)(2,1)S(1)} %place_other_sectors.1.across_own), channel_id=1, source_target_pairs={{1,0},{0,1},{3,2},{2,3},{5,4},{4,5},{7,6},{6,7},{9,8},{8,9},{11,10... | collective-permute-start | bytes 786440 | tf_op jit(solution)/shard_map/ppermute | solution.py:241
  35.0 8.2 %collective-permute-start.17 = (bf16[1,64,512]{2,1,0:T(8,128)(2,1)S(1)}, bf16[1,64,512]{2,1,0:T(8,128)(2,1)S(1)}, u32[]{:S(2)}, u32[]{:S(2)}) collective-permute-start(bf16[1,64,512]{2,1,0:T(8,128)(2,1)S(1)} %get-tuple-element.41), channel_id=1, source_target_pairs={{8,0},{12,4},{0,8},{4,12},{9,1},{13,5},{1,9},{5,13},{10,2},{14,6},... | collective-permute-start | bytes 196616 | tf_op jit(solution)/shard_map/ppermute | solution.py:241
  36.4 6.8 %collective-permute-start.18 = (bf16[1,64,512]{2,1,0:T(8,128)(2,1)S(1)}, bf16[1,64,512]{2,1,0:T(8,128)(2,1)S(1)}, u32[]{:S(2)}, u32[]{:S(2)}) collective-permute-start(bf16[1,64,512]{2,1,0:T(8,128)(2,1)S(1)} %get-tuple-element.42), channel_id=1, source_target_pairs={{12,0},{8,4},{4,8},{0,12},{13,1},{9,5},{5,9},{1,13},{14,2},{10,6},... | collective-permute-start | bytes 196616 | tf_op jit(solution)/shard_map/ppermute | solution.py:241
  38.2 6.0 %collective-permute-start.19 = (bf16[1,64,512]{2,1,0:T(8,128)(2,1)S(1)}, bf16[1,64,512]{2,1,0:T(8,128)(2,1)S(1)}, u32[]{:S(2)}, u32[]{:S(2)}) collective-permute-start(bf16[1,64,512]{2,1,0:T(8,128)(2,1)S(1)} %get-tuple-element.43), channel_id=1, source_target_pairs={{4,0},{0,4},{12,8},{8,12},{5,1},{1,5},{13,9},{9,13},{6,2},{2,6},{1... | collective-permute-start | bytes 196616 | tf_op jit(solution)/shard_map/ppermute | solution.py:241
  39.1 3.8 %collective-permute-start.11 = (f32[3,8,128]{2,1,0:T(8,128)S(1)}, f32[3,8,128]{2,1,0:T(8,128)S(1)}, u32[]{:S(2)}, u32[]{:S(2)}) collective-permute-start(f32[3,8,128]{2,1,0:T(8,128)S(1)} %sums_for_rayleigh.1.refs_0_.refs_4_), channel_id=1, source_target_pairs={{2,0},{0,2},{3,1},{1,3},{6,4},{4,6},{7,5},{5,7},{10,8},{8,10},{11,... | collective-permute-start | bytes 36872 | tf_op jit(solution)/shard_map/ppermute | solution.py:241
  44.3 8.1 %collective-permute-start.20 = (bf16[1,64,512]{2,1,0:T(8,128)(2,1)S(1)}, bf16[1,64,512]{2,1,0:T(8,128)(2,1)S(1)}, u32[]{:S(2)}, u32[]{:S(2)}) collective-permute-start(bf16[1,64,512]{2,1,0:T(8,128)(2,1)S(1)} %sum_second_sigma.1.refs_5_), channel_id=1, source_target_pairs={{8,0},{12,4},{0,8},{4,12},{9,1},{13,5},{1,9},{5,13},{10,2},{14,6},... | collective-permute-start | bytes 196616 | tf_op jit(solution)/shard_map/ppermute | solution.py:241
  45.8 6.6 %collective-permute-start.21 = (bf16[1,64,512]{2,1,0:T(8,128)(2,1)S(1)}, bf16[1,64,512]{2,1,0:T(8,128)(2,1)S(1)}, u32[]{:S(2)}, u32[]{:S(2)}) collective-permute-start(bf16[1,64,512]{2,1,0:T(8,128)(2,1)S(1)} %sum_second_sigma.1.refs_5_), channel_id=1, source_target_pairs={{12,0},{8,4},{4,8},{0,12},{13,1},{9,5},{5,9},{1,13},{14,2},{10,6},... | collective-permute-start | bytes 196616 | tf_op jit(solution)/shard_map/ppermute | solution.py:241
  47.4 5.6 %collective-permute-start.22 = (bf16[1,64,512]{2,1,0:T(8,128)(2,1)S(1)}, bf16[1,64,512]{2,1,0:T(8,128)(2,1)S(1)}, u32[]{:S(2)}, u32[]{:S(2)}) collective-permute-start(bf16[1,64,512]{2,1,0:T(8,128)(2,1)S(1)} %sum_second_sigma.1.refs_5_), channel_id=1, source_target_pairs={{4,0},{0,4},{12,8},{8,12},{5,1},{1,5},{13,9},{9,13},{6,2},{2,6},{1... | collective-permute-start | bytes 196616 | tf_op jit(solution)/shard_map/ppermute | solution.py:241

commit v17 on v16

--- a/solution.py
+++ b/solution.py
@@ -393,7 +393,7 @@
         across_other,
         scratch=[pltpu.VMEM((rows, columns), f32)],
     )
-    received = [partner(shares[step], {"ops": step}) for step in send_order[:-1]]
+    received = [partner(shares[step], {"ops": step}) for step in farthest_first[:-1]]
     sums = call(
         sums_kernel,
         "sums_for_rayleigh",
@@ -417,13 +417,13 @@
         *sums,
     )
     second_sigma = call(
-        lambda *refs: join_kernel(send_order, *refs),
+        lambda *refs: join_kernel(farthest_first, *refs),
         "join_second_sigma",
         shape(1, rows, columns, dtype=f32),
         [],
         factors,
         sigma_own,
-        *[partner(second_share, {"ops": step}) for step in send_order],
+        *[partner(second_share, {"ops": step}) for step in farthest_first],
         scratch=[
             pltpu.VMEM((ops_count, share, columns), f32),
             pltpu.SemaphoreType.DMA((ops_count,)),

time: 54 us -> 53.6 us (level)
  waiting for transfers between devices: 13.6 us -> 11.4 us
  starting transfers between devices: 30.2 us -> 32 us
    ppermute x23, waiting for transfers between devices: 13.6 us -> 11.4 us  [partner(): return lax.ppermute(value, axes, pairs)]
    ppermute x23, starting transfers between devices: 30.2 us -> 32 us  [partner(): return lax.ppermute(value, axes, pairs)]
  transfers between devices with their start and end apart: 23 -> 23, of which waited for: 12 -> 11; matrix products, arithmetic and copies ran while one was open for 0% -> 0% of each run, Pallas kernels for 10% -> 10%
where the time goes in v17:
time: 53.6 us; the launch traced here: 53.4 us
  starting transfers between devices  32 us (60%)
  waiting for transfers between devices  11.4 us (21%)
  Pallas kernels  9.18 us (17%)
  between operations  0.85 us (2%)
    ppermute x23, starting transfers between devices, partner(): return lax.ppermute(value, axes, pairs)  32 us
    ppermute x23, waiting for transfers between devices, partner(): return lax.ppermute(value, axes, pairs)  11.4 us
    pallas_call x14, Pallas kernels, call(): pl.pallas_call(kernel, out_shape=out_shape, in_specs=list(in_specs) + [in...  9.18 us
  transfers between devices with their start and end apart: 23, of which 11 were waited for; matrix products, arithmetic and copies ran while one was open for 0% of the time, Pallas kernels for 10%

profile of v17, /device:TPU:0, one launch (start us, length us, event | category | flops | bytes accessed | tf_op | source)
XLA Modules:
  0.0 53.4 jit_solution(3544533943586117917)
XLA Ops:
  0.6 0.0 copy-start.1
  0.6 0.0 copy-start.3
  0.7 0.0 copy-start.2
  0.7 0.0 copy-start.4
  0.7 0.0 copy-start
  0.7 0.5 collective-permute-start
  1.2 1.4 %load_operators.1 = (bf16[4,256,256]{2,1,0:T(8,128)(2,1)S(1)}, bf16[4,256,256]{2,1,0:T(8,128)(2,1)S(1)}) custom-call(bf16[4,512,512]{2,1,0:T(8,128)(2,1)} %left_ref.1), custom_call_target="tpu_custom_call" | custom-call | tf_op jit(solution)/shard_map/load_operators/pallas_call | solution.py:259
  2.6 0.0 copy-done.1
  2.6 0.0 copy-done.3
  2.7 0.0 copy-done.2
  2.7 0.2 tables_for_first_sigma.1
  2.9 0.0 collective-permute-done.refs_6_
  2.9 1.7 %first_sigma_terms.1 = (bf16[256,512]{1,0:T(8,128)(2,1)S(1)}, f32[2,64,512]{2,1,0:T(8,128)S(1)}, bf16[2,64,512]{2,1,0:T(8,128)(2,1)S(1)}, bf16[1,64,512]{2,1,0:T...) custom-call(s32[2,2]{1,0:T(2,128)S(1)} %copy-done.3, ...), custom_call_target="tpu_custom_call" | custom-call | tf_op jit(solution)/shard_map/first_sigma_terms/pallas_call | solution.py:259
  4.6 2.8 %collective-permute-start.1 = (bf16[2,64,512]{2,1,0:T(8,128)(2,1)S(1)}, bf16[2,64,512]{2,1,0:T(8,128)(2,1)S(1)}, u32[]{:S(2)}, u32[]{:S(2)}) collective-permute-start(bf16[2,64,512]{2,1,0:T(8,128)(2,1)S(1)} %get-tuple-element.28), channel_id=1, source_target_pairs={{2,0},{0,2},{3,1},{1,3},{6,4},{4,6},{7,5},{5,7},{10,8},{8,10},{11,... | collective-permute-start | bytes 393224 | tf_op jit(solution)/shard_map/ppermute | solution.py:241
  7.4 1.6 %collective-permute-start.3 = (bf16[1,64,512]{2,1,0:T(8,128)(2,1)S(1)}, bf16[1,64,512]{2,1,0:T(8,128)(2,1)S(1)}, u32[]{:S(2)}, u32[]{:S(2)}) collective-permute-start(bf16[1,64,512]{2,1,0:T(8,128)(2,1)S(1)} %get-tuple-element.29), channel_id=1, source_target_pairs={{4,0},{0,4},{12,8},{8,12},{5,1},{1,5},{13,9},{9,13},{6,2},{2,6},{1... | collective-permute-start | bytes 196616 | tf_op jit(solution)/shard_map/ppermute | solution.py:241
  9.0 2.6 %collective-permute-start.4 = (bf16[1,64,512]{2,1,0:T(8,128)(2,1)S(1)}, bf16[1,64,512]{2,1,0:T(8,128)(2,1)S(1)}, u32[]{:S(2)}, u32[]{:S(2)}) collective-permute-start(bf16[1,64,512]{2,1,0:T(8,128)(2,1)S(1)} %get-tuple-element.30), channel_id=1, source_target_pairs={{8,0},{12,4},{0,8},{4,12},{9,1},{13,5},{1,9},{5,13},{10,2},{14,6},... | collective-permute-start | bytes 196616 | tf_op jit(solution)/shard_map/ppermute | solution.py:241
  11.5 0.3 collective-permute-start.5
  11.8 1.4 %collective-permute-start.6 = (bf16[1,64,512]{2,1,0:T(8,128)(2,1)S(1)}, bf16[1,64,512]{2,1,0:T(8,128)(2,1)S(1)}, u32[]{:S(2)}, u32[]{:S(2)}) collective-permute-start(bf16[1,64,512]{2,1,0:T(8,128)(2,1)S(1)} %get-tuple-element.32), channel_id=1, source_target_pairs={{6,0},{4,2},{2,4},{0,6},{14,8},{12,10},{10,12},{8,14},{7,1},{5,3},... | collective-permute-start | bytes 196616 | tf_op jit(solution)/shard_map/ppermute | solution.py:241
  13.2 0.0 collective-permute-done.1.refs_1_
  13.3 3.7 %collective-permute-start.2 = (bf16[1,64,512]{2,1,0:T(8,128)(2,1)S(1)}, bf16[1,64,512]{2,1,0:T(8,128)(2,1)S(1)}, u32[]{:S(2)}, u32[]{:S(2)}) collective-permute-start(bf16[1,64,512]{2,1,0:T(8,128)(2,1)S(1)} %sum_far_share.1), channel_id=1, source_target_pairs={{12,0},{8,4},{4,8},{0,12},{13,1},{9,5},{5,9},{1,13},{14,2},{10,6},... | collective-permute-start | bytes 196616 | tf_op jit(solution)/shard_map/ppermute | solution.py:241
  16.9 0.8 %tables_for_second_sigma.1 = (f32[4,2,8,128]{3,2,1,0:T(8,128)S(1)}, f32[256,512]{1,0:T(8,128)S(1)}) custom-call(s32[2,2]{1,0:T(2,128)S(1)} %copy-done.3, s32[4,2,8]{2,1,0:T(2,128)S(1)} %bitcast.2, f32[4,8]{1,0:T(4,128)S(1)} %copy-done.4, bf16[256,512]{1,0:T(8,128)(2,1)S(1)} %get-tuple-element.33._.wave_other), custom_call_target="tpu_custom_call" | custom-call | tf_op jit(solution)/shard_map/tables_for_second_sigma/pallas_call | solution.py:259
  17.7 0.0 collective-permute-done.3.refs_3_
  17.7 0.0 collective-permute-done.4.refs_4_
  17.8 2.2 %collective-permute-done.5.refs_5_ = bf16[1,64,512]{2,1,0:T(8,128)(2,1)S(1)} collective-permute-done((bf16[1,64,512]{2,1,0:T(8,128)(2,1)S(1)}, bf16[1,64,512]{2,1,0:T(8,128)(2,1)S(1)}, u32[]{:S(2)}, u32[]{:S(2)}) %collective-permute-start.5) | collective-permute-done | bytes 65568 | tf_op jit(solution)/shard_map/ppermute | solution.py:241
  20.0 0.0 collective-permute-done.6.refs_6_
  20.0 0.0 collective-permute-done.2.refs_2_
  20.0 0.1 sum_first_sigma.1.refs_3_
  20.0 1.3 %collective-permute-start.7 = (bf16[1,64,512]{2,1,0:T(8,128)(2,1)S(1)}, bf16[1,64,512]{2,1,0:T(8,128)(2,1)S(1)}, u32[]{:S(2)}, u32[]{:S(2)}) collective-permute-start(bf16[1,64,512]{2,1,0:T(8,128)(2,1)S(1)} %sum_first_sigma.1.refs_3_), channel_id=1, source_target_pairs={{8,0},{12,4},{0,8},{4,12},{9,1},{13,5},{1,9},{5,13},{10,2},{14,6},... | collective-permute-start | bytes 196616 | tf_op jit(solution)/shard_map/ppermute | solution.py:241
  21.4 2.1 %collective-permute-start.8 = (bf16[1,64,512]{2,1,0:T(8,128)(2,1)S(1)}, bf16[1,64,512]{2,1,0:T(8,128)(2,1)S(1)}, u32[]{:S(2)}, u32[]{:S(2)}) collective-permute-start(bf16[1,64,512]{2,1,0:T(8,128)(2,1)S(1)} %sum_first_sigma.1.refs_3_), channel_id=1, source_target_pairs={{12,0},{8,4},{4,8},{0,12},{13,1},{9,5},{5,9},{1,13},{14,2},{10,6},... | collective-permute-start | bytes 196616 | tf_op jit(solution)/shard_map/ppermute | solution.py:241
  23.5 0.2 collective-permute-start.9
  23.7 2.1 %collective-permute-start.14 = (bf16[1,64,512]{2,1,0:T(8,128)(2,1)S(1)}, bf16[1,64,512]{2,1,0:T(8,128)(2,1)S(1)}, u32[]{:S(2)}, u32[]{:S(2)}) collective-permute-start(bf16[1,64,512]{2,1,0:T(8,128)(2,1)S(1)} %sum_first_sigma.1.refs_3_), channel_id=1, source_target_pairs={{6,0},{4,2},{2,4},{0,6},{14,8},{12,10},{10,12},{8,14},{7,1},{5,3},... | collective-permute-start | bytes 196616 | tf_op jit(solution)/shard_map/ppermute | solution.py:241
  25.8 1.2 %collective-permute-start.15 = (bf16[1,64,512]{2,1,0:T(8,128)(2,1)S(1)}, bf16[1,64,512]{2,1,0:T(8,128)(2,1)S(1)}, u32[]{:S(2)}, u32[]{:S(2)}) collective-permute-start(bf16[1,64,512]{2,1,0:T(8,128)(2,1)S(1)} %sum_first_sigma.1.refs_3_), channel_id=1, source_target_pairs={{2,0},{0,2},{3,1},{1,3},{6,4},{4,6},{7,5},{5,7},{10,8},{8,10},{11,... | collective-permute-start | bytes 196616 | tf_op jit(solution)/shard_map/ppermute | solution.py:241
  27.0 0.0 collective-permute-done.7.refs_0_
  27.0 0.8 %collective-permute-start.12 = (bf16[1,64,512]{2,1,0:T(8,128)(2,1)S(1)}, bf16[1,64,512]{2,1,0:T(8,128)(2,1)S(1)}, u32[]{:S(2)}, u32[]{:S(2)}) collective-permute-start(bf16[1,64,512]{2,1,0:T(8,128)(2,1)S(1)} %collective-permute-done.7.refs_0_), channel_id=1, source_target_pairs={{2,0},{0,2},{3,1},{1,3},{6,4},{4,6},{7,5},{5,7},{10,8},{8,10},{11,... | collective-permute-start | bytes 196616 | tf_op jit(solution)/shard_map/ppermute | solution.py:241
  27.8 0.2 collective-permute-done.8.refs_1_
  28.0 1.1 %collective-permute-start.13 = (bf16[1,64,512]{2,1,0:T(8,128)(2,1)S(1)}, bf16[1,64,512]{2,1,0:T(8,128)(2,1)S(1)}, u32[]{:S(2)}, u32[]{:S(2)}) collective-permute-start(bf16[1,64,512]{2,1,0:T(8,128)(2,1)S(1)} %collective-permute-done.8.refs_1_), channel_id=1, source_target_pairs={{2,0},{0,2},{3,1},{1,3},{6,4},{4,6},{7,5},{5,7},{10,8},{8,10},{11,... | collective-permute-start | bytes 196616 | tf_op jit(solution)/shard_map/ppermute | solution.py:241
  29.1 0.0 collective-permute-done.9.refs_2_
  29.2 0.1 collective-permute-start.10
  29.2 0.3 collective-permute-done.14.refs_2_
  29.5 1.1 %collective-permute-done.15.refs_3_ = bf16[1,64,512]{2,1,0:T(8,128)(2,1)S(1)} collective-permute-done((bf16[1,64,512]{2,1,0:T(8,128)(2,1)S(1)}, bf16[1,64,512]{2,1,0:T(8,128)(2,1)S(1)}, u32[]{:S(2)}, u32[]{:S(2)}) %collective-permute-start.15) | collective-permute-done | bytes 65568 | tf_op jit(solution)/shard_map/ppermute | solution.py:241
  30.6 0.7 %collective-permute-done.12.refs_0_ = bf16[1,64,512]{2,1,0:T(8,128)(2,1)S(1)} collective-permute-done((bf16[1,64,512]{2,1,0:T(8,128)(2,1)S(1)}, bf16[1,64,512]{2,1,0:T(8,128)(2,1)S(1)}, u32[]{:S(2)}, u32[]{:S(2)}) %collective-permute-start.12) | collective-permute-done | bytes 65568 | tf_op jit(solution)/shard_map/ppermute | solution.py:241
  31.3 0.9 %collective-permute-done.13.refs_1_ = bf16[1,64,512]{2,1,0:T(8,128)(2,1)S(1)} collective-permute-done((bf16[1,64,512]{2,1,0:T(8,128)(2,1)S(1)}, bf16[1,64,512]{2,1,0:T(8,128)(2,1)S(1)}, u32[]{:S(2)}, u32[]{:S(2)}) %collective-permute-start.13) | collective-permute-done | bytes 65568 | tf_op jit(solution)/shard_map/ppermute | solution.py:241
  32.3 0.1 collective-permute-start.16
  32.4 0.0 collective-permute-done.10.sigma_other.other
  32.4 1.0 %left_products.1 = (f32[4,256,512]{2,1,0:T(8,128)S(1)}, f32[1,4,256,512]{3,2,1,0:T(8,128)S(1)}) custom-call(bf16[4,256,256]{2,1,0:T(8,128)(2,1)S(1)} %get-tuple-element.23._.refs_2_.left_own, bf16[4,256,256]{2,1,0:T(8,128)(2,1)S(1)} %get-tuple-element.26.refs_3_.left_other, bf16[1,256,512]{2,1,0:T(8,128)(2,1)S(1)} %place_own_sector.1.sigma_own.own.refs_1_, ...), custom_call_target="tpu_custom_call" | custom-call | tf_op jit(solution)/shard_map/left_products/pallas_call | solution.py:259
  33.3 0.5 collective-permute-done.16.other
  33.9 1.1 %second_sigma_terms.1 = (f32[1,64,512]{2,1,0:T(8,128)S(1)}, bf16[1,64,512]{2,1,0:T(8,128)(2,1)S(1)}, bf16[1,64,512]{2,1,0:T(8,128)(2,1)S(1)}, bf16[1,64,512]{2,1,0:T(8,128)(2,1)S(1)}) custom-call(f32[4,2,8,128]{3,2,1,0:T(8,128)S(1)} %get-tuple-element.34.refs_7_.mixing, f32[256,512]{1,0:T(8,128)S(1)} %get-tuple-element.37.live, ...), custom_call_target="tpu_custom_call" | custom-call | tf_op jit(solution)/shard_map/second_sigma_terms/pallas_call | solution.py:259
  35.0 2.4 %collective-permute-start.17 = (bf16[1,64,512]{2,1,0:T(8,128)(2,1)S(1)}, bf16[1,64,512]{2,1,0:T(8,128)(2,1)S(1)}, u32[]{:S(2)}, u32[]{:S(2)}) collective-permute-start(bf16[1,64,512]{2,1,0:T(8,128)(2,1)S(1)} %get-tuple-element.41), channel_id=1, source_target_pairs={{12,0},{8,4},{4,8},{0,12},{13,1},{9,5},{5,9},{1,13},{14,2},{10,6},... | collective-permute-start | bytes 196616 | tf_op jit(solution)/shard_map/ppermute | solution.py:241
  37.4 0.0 collective-permute-start.18
  37.4 2.1 %collective-permute-start.19 = (bf16[1,64,512]{2,1,0:T(8,128)(2,1)S(1)}, bf16[1,64,512]{2,1,0:T(8,128)(2,1)S(1)}, u32[]{:S(2)}, u32[]{:S(2)}) collective-permute-start(bf16[1,64,512]{2,1,0:T(8,128)(2,1)S(1)} %get-tuple-element.43), channel_id=1, source_target_pairs={{4,0},{0,4},{12,8},{8,12},{5,1},{1,5},{13,9},{9,13},{6,2},{2,6},{1... | collective-permute-start | bytes 196616 | tf_op jit(solution)/shard_map/ppermute | solution.py:241
  39.5 0.5 sums_for_rayleigh.1.refs_0_.refs_4_
  40.0 1.2 %collective-permute-start.11 = (f32[3,8,128]{2,1,0:T(8,128)S(1)}, f32[3,8,128]{2,1,0:T(8,128)S(1)}, u32[]{:S(2)}, u32[]{:S(2)}) collective-permute-start(f32[3,8,128]{2,1,0:T(8,128)S(1)} %sums_for_rayleigh.1.refs_0_.refs_4_), channel_id=1, source_target_pairs={{2,0},{0,2},{3,1},{1,3},{6,4},{4,6},{7,5},{5,7},{10,8},{8,10},{11,... | collective-permute-start | bytes 36872 | tf_op jit(solution)/shard_map/ppermute | solution.py:241
  41.2 2.5 %collective-permute-done.11.refs_1_.refs_5_ = f32[3,8,128]{2,1,0:T(8,128)S(1)} collective-permute-done((f32[3,8,128]{2,1,0:T(8,128)S(1)}, f32[3,8,128]{2,1,0:T(8,128)S(1)}, u32[]{:S(2)}, u32[]{:S(2)}) %collective-permute-start.11) | collective-permute-done | bytes 12320 | tf_op jit(solution)/shard_map/ppermute | solution.py:241
  43.7 0.0 collective-permute-done.17.refs_1_
  43.7 0.1 collective-permute-done.18.refs_2_
  43.8 0.0 collective-permute-done.19.refs_3_
  43.8 2.4 %collective-permute-start.20 = (bf16[1,64,512]{2,1,0:T(8,128)(2,1)S(1)}, bf16[1,64,512]{2,1,0:T(8,128)(2,1)S(1)}, u32[]{:S(2)}, u32[]{:S(2)}) collective-permute-start(bf16[1,64,512]{2,1,0:T(8,128)(2,1)S(1)} %sum_second_sigma.1.refs_5_), channel_id=1, source_target_pairs={{12,0},{8,4},{4,8},{0,12},{13,1},{9,5},{5,9},{1,13},{14,2},{10,6},... | collective-permute-start | bytes 196616 | tf_op jit(solution)/shard_map/ppermute | solution.py:241
  46.2 0.0 collective-permute-start.21
  46.2 2.1 %collective-permute-start.22 = (bf16[1,64,512]{2,1,0:T(8,128)(2,1)S(1)}, bf16[1,64,512]{2,1,0:T(8,128)(2,1)S(1)}, u32[]{:S(2)}, u32[]{:S(2)}) collective-permute-start(bf16[1,64,512]{2,1,0:T(8,128)(2,1)S(1)} %sum_second_sigma.1.refs_5_), channel_id=1, source_target_pairs={{4,0},{0,4},{12,8},{8,12},{5,1},{1,5},{13,9},{9,13},{6,2},{2,6},{1... | collective-permute-start | bytes 196616 | tf_op jit(solution)/shard_map/ppermute | solution.py:241
  48.3 1.4 %second_wave.1 = (bf16[1,256,512]{2,1,0:T(8,128)(2,1)}, f32[2,8,128]{2,1,0:T(8,128)S(1)}) custom-call(s32[2,2]{1,0:T(2,128)S(1)} %copy-done.3, bf16[256,512]{1,0:T(8,128)(2,1)S(1)} %get-tuple-element.24.refs_5_.wave_own, bf16[1,256,512]{2,1,0:T(8,128)(2,1)S(1)} %place_own_sector.1.sigma_own.own.refs_1_, f32[3,8,128]{2,1,0:T(8,128)S(1)} %sums_for_rayleigh.1.refs_0_.refs_4_, ...), custom_call_target="tpu_custom_call" | custom-call | tf_op jit(solution)/shard_map/second_wave/pallas_call | solution.py:259
  49.7 0.8 %collective-permute-done.20.refs_2_ = bf16[1,64,512]{2,1,0:T(8,128)(2,1)S(1)} collective-permute-done((bf16[1,64,512]{2,1,0:T(8,128)(2,1)S(1)}, bf16[1,64,512]{2,1,0:T(8,128)(2,1)S(1)}, u32[]{:S(2)}, u32[]{:S(2)}) %collective-permute-start.20) | collective-permute-done | bytes 65568 | tf_op jit(solution)/shard_map/ppermute | solution.py:241
  50.6 2.0 %collective-permute-done.21.refs_3_ = bf16[1,64,512]{2,1,0:T(8,128)(2,1)S(1)} collective-permute-done((bf16[1,64,512]{2,1,0:T(8,128)(2,1)S(1)}, bf16[1,64,512]{2,1,0:T(8,128)(2,1)S(1)}, u32[]{:S(2)}, u32[]{:S(2)}) %collective-permute-start.21) | collective-permute-done | bytes 65568 | tf_op jit(solution)/shard_map/ppermute | solution.py:241
  52.5 0.0 collective-permute-done.22.refs_4_
  52.5 0.9 %join_second_sigma.1 = f32[1,256,512]{2,1,0:T(8,128)} custom-call(f32[2,8,128]{2,1,0:T(8,128)S(1)} %get-tuple-element.36.refs_0_, bf16[1,256,512]{2,1,0:T(8,128)(2,1)S(1)} %place_own_sector.1.sigma_own.own.refs_1_, bf16[1,64,512]{2,1,0:T(8,128)(2,1)S(1)} %collective-permute-done.20.refs_2_, bf16[1,64,512]{2,1,0:T(8,128)(2,1)S(1)} %collective-permute-done.21.refs_3_, ...), custom_call_target="tpu_custom_call" | custom-call | tf_op jit(solution)/shard_map/join_second_sigma/pallas_call | solution.py:259
  (6 shorter events, 0.1 us)
Async XLA Ops:
  0.6 2.0 %copy-start.1 = (bf16[1,256,512]{2,1,0:T(8,128)(2,1)S(1)}, bf16[1,256,512]{2,1,0:T(8,128)(2,1)}, u32[]{:S(2)}) copy-start(bf16[1,256,512]{2,1,0:T(8,128)(2,1)} %wave.1) | copy-start | bytes 786436
  0.6 2.0 %copy-start.3 = (s32[2,2]{1,0:T(2,128)S(1)}, s32[2,2]{1,0:T(2,128)}, u32[]{:S(2)}) copy-start(s32[2,2]{1,0:T(2,128)} %sizes_ref.3) | copy-start | bytes 52
  0.7 2.0 %copy-start.2 = (s32[4,8,2]{1,2,0:T(2,128)S(1)}, s32[4,8,2]{1,2,0:T(2,128)}, u32[]{:S(2)}) copy-start(s32[4,8,2]{1,2,0:T(2,128)} %param.10) | copy-start | bytes 772
  0.7 2.0 %copy-start.4 = (f32[4,8]{1,0:T(4,128)S(1)}, f32[4,8]{1,0:T(4,128)}, u32[]{:S(2)}) copy-start(f32[4,8]{1,0:T(4,128)} %weights_ref.1) | copy-start | bytes 388
  0.7 2.2 %copy-start = (bf16[4,512,512]{2,1,0:T(8,128)(2,1)S(1)}, bf16[4,512,512]{2,1,0:T(8,128)(2,1)}, u32[]{:S(2)}) copy-start(bf16[4,512,512]{2,1,0:T(8,128)(2,1)} %right.1) | copy-start | bytes 6291460
  0.7 2.2 %collective-permute-start = (bf16[1,256,512]{2,1,0:T(8,128)(2,1)}, bf16[1,256,512]{2,1,0:T(8,128)(2,1)S(1)}, u32[]{:S(2)}, u32[]{:S(2)}) collective-permute-start(bf16[1,256,512]{2,1,0:T(8,128)(2,1)} %wave.1), channel_id=1, source_target_pairs={{1,0},{0,1},{3,2},{2,3},{5,4},{4,5},{7,6},{6,7},{9,8},{8,9},{11,10... | collective-permute-start | bytes 786440 | tf_op jit(solution)/shard_map/ppermute | solution.py:241
  4.6 8.7 %collective-permute-start.1 = (bf16[2,64,512]{2,1,0:T(8,128)(2,1)S(1)}, bf16[2,64,512]{2,1,0:T(8,128)(2,1)S(1)}, u32[]{:S(2)}, u32[]{:S(2)}) collective-permute-start(bf16[2,64,512]{2,1,0:T(8,128)(2,1)S(1)} %get-tuple-element.28), channel_id=1, source_target_pairs={{2,0},{0,2},{3,1},{1,3},{6,4},{4,6},{7,5},{5,7},{10,8},{8,10},{11,... | collective-permute-start | bytes 393224 | tf_op jit(solution)/shard_map/ppermute | solution.py:241
  7.4 10.4 %collective-permute-start.3 = (bf16[1,64,512]{2,1,0:T(8,128)(2,1)S(1)}, bf16[1,64,512]{2,1,0:T(8,128)(2,1)S(1)}, u32[]{:S(2)}, u32[]{:S(2)}) collective-permute-start(bf16[1,64,512]{2,1,0:T(8,128)(2,1)S(1)} %get-tuple-element.29), channel_id=1, source_target_pairs={{4,0},{0,4},{12,8},{8,12},{5,1},{1,5},{13,9},{9,13},{6,2},{2,6},{1... | collective-permute-start | bytes 196616 | tf_op jit(solution)/shard_map/ppermute | solution.py:241
  9.0 8.8 %collective-permute-start.4 = (bf16[1,64,512]{2,1,0:T(8,128)(2,1)S(1)}, bf16[1,64,512]{2,1,0:T(8,128)(2,1)S(1)}, u32[]{:S(2)}, u32[]{:S(2)}) collective-permute-start(bf16[1,64,512]{2,1,0:T(8,128)(2,1)S(1)} %get-tuple-element.30), channel_id=1, source_target_pairs={{8,0},{12,4},{0,8},{4,12},{9,1},{13,5},{1,9},{5,13},{10,2},{14,6},... | collective-permute-start | bytes 196616 | tf_op jit(solution)/shard_map/ppermute | solution.py:241
  11.5 8.4 %collective-permute-start.5 = (bf16[1,64,512]{2,1,0:T(8,128)(2,1)S(1)}, bf16[1,64,512]{2,1,0:T(8,128)(2,1)S(1)}, u32[]{:S(2)}, u32[]{:S(2)}) collective-permute-start(bf16[1,64,512]{2,1,0:T(8,128)(2,1)S(1)} %get-tuple-element.31), channel_id=1, source_target_pairs={{10,0},{8,2},{14,4},{12,6},{2,8},{0,10},{6,12},{4,14},{11,1},{9,3}... | collective-permute-start | bytes 196616 | tf_op jit(solution)/shard_map/ppermute | solution.py:241
  11.8 8.1 %collective-permute-start.6 = (bf16[1,64,512]{2,1,0:T(8,128)(2,1)S(1)}, bf16[1,64,512]{2,1,0:T(8,128)(2,1)S(1)}, u32[]{:S(2)}, u32[]{:S(2)}) collective-permute-start(bf16[1,64,512]{2,1,0:T(8,128)(2,1)S(1)} %get-tuple-element.32), channel_id=1, source_target_pairs={{6,0},{4,2},{2,4},{0,6},{14,8},{12,10},{10,12},{8,14},{7,1},{5,3},... | collective-permute-start | bytes 196616 | tf_op jit(solution)/shard_map/ppermute | solution.py:241
  13.3 6.7 %collective-permute-start.2 = (bf16[1,64,512]{2,1,0:T(8,128)(2,1)S(1)}, bf16[1,64,512]{2,1,0:T(8,128)(2,1)S(1)}, u32[]{:S(2)}, u32[]{:S(2)}) collective-permute-start(bf16[1,64,512]{2,1,0:T(8,128)(2,1)S(1)} %sum_far_share.1), channel_id=1, source_target_pairs={{12,0},{8,4},{4,8},{0,12},{13,1},{9,5},{5,9},{1,13},{14,2},{10,6},... | collective-permute-start | bytes 196616 | tf_op jit(solution)/shard_map/ppermute | solution.py:241
  20.0 6.9 %collective-permute-start.7 = (bf16[1,64,512]{2,1,0:T(8,128)(2,1)S(1)}, bf16[1,64,512]{2,1,0:T(8,128)(2,1)S(1)}, u32[]{:S(2)}, u32[]{:S(2)}) collective-permute-start(bf16[1,64,512]{2,1,0:T(8,128)(2,1)S(1)} %sum_first_sigma.1.refs_3_), channel_id=1, source_target_pairs={{8,0},{12,4},{0,8},{4,12},{9,1},{13,5},{1,9},{5,13},{10,2},{14,6},... | collective-permute-start | bytes 196616 | tf_op jit(solution)/shard_map/ppermute | solution.py:241
  21.4 6.6 %collective-permute-start.8 = (bf16[1,64,512]{2,1,0:T(8,128)(2,1)S(1)}, bf16[1,64,512]{2,1,0:T(8,128)(2,1)S(1)}, u32[]{:S(2)}, u32[]{:S(2)}) collective-permute-start(bf16[1,64,512]{2,1,0:T(8,128)(2,1)S(1)} %sum_first_sigma.1.refs_3_), channel_id=1, source_target_pairs={{12,0},{8,4},{4,8},{0,12},{13,1},{9,5},{5,9},{1,13},{14,2},{10,6},... | collective-permute-start | bytes 196616 | tf_op jit(solution)/shard_map/ppermute | solution.py:241
  23.5 5.6 %collective-permute-start.9 = (bf16[1,64,512]{2,1,0:T(8,128)(2,1)S(1)}, bf16[1,64,512]{2,1,0:T(8,128)(2,1)S(1)}, u32[]{:S(2)}, u32[]{:S(2)}) collective-permute-start(bf16[1,64,512]{2,1,0:T(8,128)(2,1)S(1)} %sum_first_sigma.1.refs_3_), channel_id=1, source_target_pairs={{4,0},{0,4},{12,8},{8,12},{5,1},{1,5},{13,9},{9,13},{6,2},{2,6},{1... | collective-permute-start | bytes 196616 | tf_op jit(solution)/shard_map/ppermute | solution.py:241
  23.7 5.8 %collective-permute-start.14 = (bf16[1,64,512]{2,1,0:T(8,128)(2,1)S(1)}, bf16[1,64,512]{2,1,0:T(8,128)(2,1)S(1)}, u32[]{:S(2)}, u32[]{:S(2)}) collective-permute-start(bf16[1,64,512]{2,1,0:T(8,128)(2,1)S(1)} %sum_first_sigma.1.refs_3_), channel_id=1, source_target_pairs={{6,0},{4,2},{2,4},{0,6},{14,8},{12,10},{10,12},{8,14},{7,1},{5,3},... | collective-permute-start | bytes 196616 | tf_op jit(solution)/shard_map/ppermute | solution.py:241
  25.8 4.9 %collective-permute-start.15 = (bf16[1,64,512]{2,1,0:T(8,128)(2,1)S(1)}, bf16[1,64,512]{2,1,0:T(8,128)(2,1)S(1)}, u32[]{:S(2)}, u32[]{:S(2)}) collective-permute-start(bf16[1,64,512]{2,1,0:T(8,128)(2,1)S(1)} %sum_first_sigma.1.refs_3_), channel_id=1, source_target_pairs={{2,0},{0,2},{3,1},{1,3},{6,4},{4,6},{7,5},{5,7},{10,8},{8,10},{11,... | collective-permute-start | bytes 196616 | tf_op jit(solution)/shard_map/ppermute | solution.py:241
  27.0 4.3 %collective-permute-start.12 = (bf16[1,64,512]{2,1,0:T(8,128)(2,1)S(1)}, bf16[1,64,512]{2,1,0:T(8,128)(2,1)S(1)}, u32[]{:S(2)}, u32[]{:S(2)}) collective-permute-start(bf16[1,64,512]{2,1,0:T(8,128)(2,1)S(1)} %collective-permute-done.7.refs_0_), channel_id=1, source_target_pairs={{2,0},{0,2},{3,1},{1,3},{6,4},{4,6},{7,5},{5,7},{10,8},{8,10},{11,... | collective-permute-start | bytes 196616 | tf_op jit(solution)/shard_map/ppermute | solution.py:241
  28.0 4.3 %collective-permute-start.13 = (bf16[1,64,512]{2,1,0:T(8,128)(2,1)S(1)}, bf16[1,64,512]{2,1,0:T(8,128)(2,1)S(1)}, u32[]{:S(2)}, u32[]{:S(2)}) collective-permute-start(bf16[1,64,512]{2,1,0:T(8,128)(2,1)S(1)} %collective-permute-done.8.refs_1_), channel_id=1, source_target_pairs={{2,0},{0,2},{3,1},{1,3},{6,4},{4,6},{7,5},{5,7},{10,8},{8,10},{11,... | collective-permute-start | bytes 196616 | tf_op jit(solution)/shard_map/ppermute | solution.py:241
  29.2 3.2 %collective-permute-start.10 = (bf16[1,256,512]{2,1,0:T(8,128)(2,1)S(1)}, bf16[1,256,512]{2,1,0:T(8,128)(2,1)S(1)}, u32[]{:S(2)}, u32[]{:S(2)}) collective-permute-start(bf16[1,256,512]{2,1,0:T(8,128)(2,1)S(1)} %place_own_sector.1.sigma_own.own.refs_1_), channel_id=1, source_target_pairs={{1,0},{0,1},{3,2},{2,3},{5,4},{4,5},{7,6},{6,7},{9,8},{8,9},{11,10... | collective-permute-start | bytes 786440 | tf_op jit(solution)/shard_map/ppermute | solution.py:241
  32.3 1.6 %collective-permute-start.16 = (bf16[1,256,512]{2,1,0:T(8,128)(2,1)S(1)}, bf16[1,256,512]{2,1,0:T(8,128)(2,1)S(1)}, u32[]{:S(2)}, u32[]{:S(2)}) collective-permute-start(bf16[1,256,512]{2,1,0:T(8,128)(2,1)S(1)} %place_other_sectors.1.across_own), channel_id=1, source_target_pairs={{1,0},{0,1},{3,2},{2,3},{5,4},{4,5},{7,6},{6,7},{9,8},{8,9},{11,10... | collective-permute-start | bytes 786440 | tf_op jit(solution)/shard_map/ppermute | solution.py:241
  35.0 8.7 %collective-permute-start.17 = (bf16[1,64,512]{2,1,0:T(8,128)(2,1)S(1)}, bf16[1,64,512]{2,1,0:T(8,128)(2,1)S(1)}, u32[]{:S(2)}, u32[]{:S(2)}) collective-permute-start(bf16[1,64,512]{2,1,0:T(8,128)(2,1)S(1)} %get-tuple-element.41), channel_id=1, source_target_pairs={{12,0},{8,4},{4,8},{0,12},{13,1},{9,5},{5,9},{1,13},{14,2},{10,6},... | collective-permute-start | bytes 196616 | tf_op jit(solution)/shard_map/ppermute | solution.py:241
  37.4 6.4 %collective-permute-start.18 = (bf16[1,64,512]{2,1,0:T(8,128)(2,1)S(1)}, bf16[1,64,512]{2,1,0:T(8,128)(2,1)S(1)}, u32[]{:S(2)}, u32[]{:S(2)}) collective-permute-start(bf16[1,64,512]{2,1,0:T(8,128)(2,1)S(1)} %get-tuple-element.42), channel_id=1, source_target_pairs={{8,0},{12,4},{0,8},{4,12},{9,1},{13,5},{1,9},{5,13},{10,2},{14,6},... | collective-permute-start | bytes 196616 | tf_op jit(solution)/shard_map/ppermute | solution.py:241
  37.4 6.4 %collective-permute-start.19 = (bf16[1,64,512]{2,1,0:T(8,128)(2,1)S(1)}, bf16[1,64,512]{2,1,0:T(8,128)(2,1)S(1)}, u32[]{:S(2)}, u32[]{:S(2)}) collective-permute-start(bf16[1,64,512]{2,1,0:T(8,128)(2,1)S(1)} %get-tuple-element.43), channel_id=1, source_target_pairs={{4,0},{0,4},{12,8},{8,12},{5,1},{1,5},{13,9},{9,13},{6,2},{2,6},{1... | collective-permute-start | bytes 196616 | tf_op jit(solution)/shard_map/ppermute | solution.py:241
  40.0 3.8 %collective-permute-start.11 = (f32[3,8,128]{2,1,0:T(8,128)S(1)}, f32[3,8,128]{2,1,0:T(8,128)S(1)}, u32[]{:S(2)}, u32[]{:S(2)}) collective-permute-start(f32[3,8,128]{2,1,0:T(8,128)S(1)} %sums_for_rayleigh.1.refs_0_.refs_4_), channel_id=1, source_target_pairs={{2,0},{0,2},{3,1},{1,3},{6,4},{4,6},{7,5},{5,7},{10,8},{8,10},{11,... | collective-permute-start | bytes 36872 | tf_op jit(solution)/shard_map/ppermute | solution.py:241
  43.8 6.7 %collective-permute-start.20 = (bf16[1,64,512]{2,1,0:T(8,128)(2,1)S(1)}, bf16[1,64,512]{2,1,0:T(8,128)(2,1)S(1)}, u32[]{:S(2)}, u32[]{:S(2)}) collective-permute-start(bf16[1,64,512]{2,1,0:T(8,128)(2,1)S(1)} %sum_second_sigma.1.refs_5_), channel_id=1, source_target_pairs={{12,0},{8,4},{4,8},{0,12},{13,1},{9,5},{5,9},{1,13},{14,2},{10,6},... | collective-permute-start | bytes 196616 | tf_op jit(solution)/shard_map/ppermute | solution.py:241
  46.2 6.3 %collective-permute-start.21 = (bf16[1,64,512]{2,1,0:T(8,128)(2,1)S(1)}, bf16[1,64,512]{2,1,0:T(8,128)(2,1)S(1)}, u32[]{:S(2)}, u32[]{:S(2)}) collective-permute-start(bf16[1,64,512]{2,1,0:T(8,128)(2,1)S(1)} %sum_second_sigma.1.refs_5_), channel_id=1, source_target_pairs={{8,0},{12,4},{0,8},{4,12},{9,1},{13,5},{1,9},{5,13},{10,2},{14,6},... | collective-permute-start | bytes 196616 | tf_op jit(solution)/shard_map/ppermute | solution.py:241
  46.2 6.3 %collective-permute-start.22 = (bf16[1,64,512]{2,1,0:T(8,128)(2,1)S(1)}, bf16[1,64,512]{2,1,0:T(8,128)(2,1)S(1)}, u32[]{:S(2)}, u32[]{:S(2)}) collective-permute-start(bf16[1,64,512]{2,1,0:T(8,128)(2,1)S(1)} %sum_second_sigma.1.refs_5_), channel_id=1, source_target_pairs={{4,0},{0,4},{12,8},{8,12},{5,1},{1,5},{13,9},{9,13},{6,2},{2,6},{1... | collective-permute-start | bytes 196616 | tf_op jit(solution)/shard_map/ppermute | solution.py:241

commit v18 on v17

--- a/solution.py
+++ b/solution.py
@@ -350,10 +350,15 @@
     )
     sigma_other = partner(sigma_own, {"rep": 1})
     spots = [(along, across) for along in send_order for across in range(1, sectors)]
+    beside = {across: partner(first_share, {"sec": across}) for across in range(1, sectors)}
+    handed = dict(along_ops)
+    handed[send_order[0]] = summed("hand_on", along_ops[send_order[0]], after=beside.values())
     pieces = [
-        partner(first_share, {"ops": along, "sec": across})
-        if along < 2
-        else partner(along_ops[along], {"sec": across})
+        beside[across]
+        if along == 0
+        else partner(first_share, {"ops": along, "sec": across})
+        if along == 1
+        else partner(handed[along], {"sec": across})
         for along, across in spots
     ]
     across_own = call(

time: 53.6 us -> 54.7 us (1.021)
  waiting for transfers between devices: 11.4 us -> 13.5 us
  starting transfers between devices: 32 us -> 30.9 us
    ppermute x23, waiting for transfers between devices: 11.4 us -> 13.5 us  [partner(): return lax.ppermute(value, axes, pairs)]
    ppermute x23, starting transfers between devices: 32 us -> 30.9 us  [partner(): return lax.ppermute(value, axes, pairs)]
    pallas_call x14 -> x15, Pallas kernels: 9.18 us -> 9.19 us  [call(): pl.pallas_call(kernel, out_shape=out_shape, in_specs=list(in_specs) + [in...]
  transfers between devices with their start and end apart: 23 -> 23, of which waited for: 11 -> 10; matrix products, arithmetic and copies ran while one was open for 0% -> 0% of each run, Pallas kernels for 10% -> 10%
where the time goes in v18:
time: 54.7 us; the launch traced here: 54.5 us
  starting transfers between devices  30.9 us (56%)
  waiting for transfers between devices  13.5 us (25%)
  Pallas kernels  9.19 us (17%)
  between operations  0.85 us (2%)
    ppermute x23, starting transfers between devices, partner(): return lax.ppermute(value, axes, pairs)  30.9 us
    ppermute x23, waiting for transfers between devices, partner(): return lax.ppermute(value, axes, pairs)  13.5 us
    pallas_call x15, Pallas kernels, call(): pl.pallas_call(kernel, out_shape=out_shape, in_specs=list(in_specs) + [in...  9.19 us
  transfers between devices with their start and end apart: 23, of which 10 were waited for; matrix products, arithmetic and copies ran while one was open for 0% of the time, Pallas kernels for 10%

profile of v18, /device:TPU:0, one launch (start us, length us, event | category | flops | bytes accessed | tf_op | source)
XLA Modules:
  0.0 54.5 jit_solution(4816018743809360040)
XLA Ops:
  0.6 0.0 copy-start.1
  0.6 0.0 copy-start.3
  0.7 0.0 copy-start.2
  0.7 0.0 copy-start.4
  0.7 0.5 collective-permute-start
  1.2 1.4 %load_operators.1 = (bf16[4,256,256]{2,1,0:T(8,128)(2,1)S(1)}, bf16[4,256,256]{2,1,0:T(8,128)(2,1)S(1)}) custom-call(bf16[4,512,512]{2,1,0:T(8,128)(2,1)} %left_ref.1), custom_call_target="tpu_custom_call" | custom-call | tf_op jit(solution)/shard_map/load_operators/pallas_call | solution.py:259
  2.6 0.0 copy-done.1
  2.6 0.0 copy-done.3
  2.7 0.0 copy-done.2
  2.7 0.0 copy-done.4
  2.7 0.2 tables_for_first_sigma.1
  2.9 0.0 collective-permute-done.refs_6_
  2.9 1.7 %first_sigma_terms.1 = (bf16[256,512]{1,0:T(8,128)(2,1)S(1)}, f32[2,64,512]{2,1,0:T(8,128)S(1)}, bf16[2,64,512]{2,1,0:T(8,128)(2,1)S(1)}, bf16[1,64,512]{2,1,0:T...) custom-call(s32[2,2]{1,0:T(2,128)S(1)} %copy-done.3, ...), custom_call_target="tpu_custom_call" | custom-call | tf_op jit(solution)/shard_map/first_sigma_terms/pallas_call | solution.py:259
  4.6 2.8 %collective-permute-start.1 = (bf16[2,64,512]{2,1,0:T(8,128)(2,1)S(1)}, bf16[2,64,512]{2,1,0:T(8,128)(2,1)S(1)}, u32[]{:S(2)}, u32[]{:S(2)}) collective-permute-start(bf16[2,64,512]{2,1,0:T(8,128)(2,1)S(1)} %get-tuple-element.28), channel_id=1, source_target_pairs={{2,0},{0,2},{3,1},{1,3},{6,4},{4,6},{7,5},{5,7},{10,8},{8,10},{11,... | collective-permute-start | bytes 393224 | tf_op jit(solution)/shard_map/ppermute | solution.py:241
  7.4 1.6 %collective-permute-start.3 = (bf16[1,64,512]{2,1,0:T(8,128)(2,1)S(1)}, bf16[1,64,512]{2,1,0:T(8,128)(2,1)S(1)}, u32[]{:S(2)}, u32[]{:S(2)}) collective-permute-start(bf16[1,64,512]{2,1,0:T(8,128)(2,1)S(1)} %get-tuple-element.29), channel_id=1, source_target_pairs={{4,0},{0,4},{12,8},{8,12},{5,1},{1,5},{13,9},{9,13},{6,2},{2,6},{1... | collective-permute-start | bytes 196616 | tf_op jit(solution)/shard_map/ppermute | solution.py:241
  9.0 2.6 %collective-permute-start.4 = (bf16[1,64,512]{2,1,0:T(8,128)(2,1)S(1)}, bf16[1,64,512]{2,1,0:T(8,128)(2,1)S(1)}, u32[]{:S(2)}, u32[]{:S(2)}) collective-permute-start(bf16[1,64,512]{2,1,0:T(8,128)(2,1)S(1)} %get-tuple-element.30), channel_id=1, source_target_pairs={{8,0},{12,4},{0,8},{4,12},{9,1},{13,5},{1,9},{5,13},{10,2},{14,6},... | collective-permute-start | bytes 196616 | tf_op jit(solution)/shard_map/ppermute | solution.py:241
  11.5 0.3 collective-permute-start.5
  11.8 1.4 %collective-permute-start.6 = (bf16[1,64,512]{2,1,0:T(8,128)(2,1)S(1)}, bf16[1,64,512]{2,1,0:T(8,128)(2,1)S(1)}, u32[]{:S(2)}, u32[]{:S(2)}) collective-permute-start(bf16[1,64,512]{2,1,0:T(8,128)(2,1)S(1)} %get-tuple-element.32), channel_id=1, source_target_pairs={{6,0},{4,2},{2,4},{0,6},{14,8},{12,10},{10,12},{8,14},{7,1},{5,3},... | collective-permute-start | bytes 196616 | tf_op jit(solution)/shard_map/ppermute | solution.py:241
  13.2 0.0 collective-permute-done.1.refs_1_
  13.3 3.7 %collective-permute-start.2 = (bf16[1,64,512]{2,1,0:T(8,128)(2,1)S(1)}, bf16[1,64,512]{2,1,0:T(8,128)(2,1)S(1)}, u32[]{:S(2)}, u32[]{:S(2)}) collective-permute-start(bf16[1,64,512]{2,1,0:T(8,128)(2,1)S(1)} %sum_far_share.1), channel_id=1, source_target_pairs={{12,0},{8,4},{4,8},{0,12},{13,1},{9,5},{5,9},{1,13},{14,2},{10,6},... | collective-permute-start | bytes 196616 | tf_op jit(solution)/shard_map/ppermute | solution.py:241
  16.9 0.8 %tables_for_second_sigma.1 = (f32[4,2,8,128]{3,2,1,0:T(8,128)S(1)}, f32[256,512]{1,0:T(8,128)S(1)}) custom-call(s32[2,2]{1,0:T(2,128)S(1)} %copy-done.3, s32[4,2,8]{2,1,0:T(2,128)S(1)} %bitcast.2, f32[4,8]{1,0:T(4,128)S(1)} %copy-done.4, bf16[256,512]{1,0:T(8,128)(2,1)S(1)} %get-tuple-element.33._.wave_other), custom_call_target="tpu_custom_call" | custom-call | tf_op jit(solution)/shard_map/tables_for_second_sigma/pallas_call | solution.py:259
  17.7 0.0 collective-permute-done.3.refs_3_
  17.7 0.0 collective-permute-done.4.refs_4_
  17.8 2.2 %collective-permute-done.5.refs_5_ = bf16[1,64,512]{2,1,0:T(8,128)(2,1)S(1)} collective-permute-done((bf16[1,64,512]{2,1,0:T(8,128)(2,1)S(1)}, bf16[1,64,512]{2,1,0:T(8,128)(2,1)S(1)}, u32[]{:S(2)}, u32[]{:S(2)}) %collective-permute-start.5) | collective-permute-done | bytes 65568 | tf_op jit(solution)/shard_map/ppermute | solution.py:241
  20.0 0.0 collective-permute-done.6.refs_6_
  20.0 0.0 collective-permute-done.2.refs_2_
  20.0 0.1 sum_first_sigma.1.refs_3_
  20.0 1.3 %collective-permute-start.7 = (bf16[1,64,512]{2,1,0:T(8,128)(2,1)S(1)}, bf16[1,64,512]{2,1,0:T(8,128)(2,1)S(1)}, u32[]{:S(2)}, u32[]{:S(2)}) collective-permute-start(bf16[1,64,512]{2,1,0:T(8,128)(2,1)S(1)} %sum_first_sigma.1.refs_3_), channel_id=1, source_target_pairs={{8,0},{12,4},{0,8},{4,12},{9,1},{13,5},{1,9},{5,13},{10,2},{14,6},... | collective-permute-start | bytes 196616 | tf_op jit(solution)/shard_map/ppermute | solution.py:241
  21.4 1.5 %collective-permute-start.12 = (bf16[1,64,512]{2,1,0:T(8,128)(2,1)S(1)}, bf16[1,64,512]{2,1,0:T(8,128)(2,1)S(1)}, u32[]{:S(2)}, u32[]{:S(2)}) collective-permute-start(bf16[1,64,512]{2,1,0:T(8,128)(2,1)S(1)} %sum_first_sigma.1.refs_3_), channel_id=1, source_target_pairs={{2,0},{0,2},{3,1},{1,3},{6,4},{4,6},{7,5},{5,7},{10,8},{8,10},{11,... | collective-permute-start | bytes 196616 | tf_op jit(solution)/shard_map/ppermute | solution.py:241
  22.9 1.4 %collective-permute-start.8 = (bf16[1,64,512]{2,1,0:T(8,128)(2,1)S(1)}, bf16[1,64,512]{2,1,0:T(8,128)(2,1)S(1)}, u32[]{:S(2)}, u32[]{:S(2)}) collective-permute-start(bf16[1,64,512]{2,1,0:T(8,128)(2,1)S(1)} %sum_first_sigma.1.refs_3_), channel_id=1, source_target_pairs={{12,0},{8,4},{4,8},{0,12},{13,1},{9,5},{5,9},{1,13},{14,2},{10,6},... | collective-permute-start | bytes 196616 | tf_op jit(solution)/shard_map/ppermute | solution.py:241
  24.3 0.0 collective-permute-start.9
  24.3 2.7 %collective-permute-start.15 = (bf16[1,64,512]{2,1,0:T(8,128)(2,1)S(1)}, bf16[1,64,512]{2,1,0:T(8,128)(2,1)S(1)}, u32[]{:S(2)}, u32[]{:S(2)}) collective-permute-start(bf16[1,64,512]{2,1,0:T(8,128)(2,1)S(1)} %sum_first_sigma.1.refs_3_), channel_id=1, source_target_pairs={{6,0},{4,2},{2,4},{0,6},{14,8},{12,10},{10,12},{8,14},{7,1},{5,3},... | collective-permute-start | bytes 196616 | tf_op jit(solution)/shard_map/ppermute | solution.py:241
  27.0 0.0 collective-permute-done.7.refs_0_
  27.0 0.0 collective-permute-done.12.refs_1_.refs_3_
  27.0 0.9 %collective-permute-start.13 = (bf16[1,64,512]{2,1,0:T(8,128)(2,1)S(1)}, bf16[1,64,512]{2,1,0:T(8,128)(2,1)S(1)}, u32[]{:S(2)}, u32[]{:S(2)}) collective-permute-start(bf16[1,64,512]{2,1,0:T(8,128)(2,1)S(1)} %hand_on.1), channel_id=1, source_target_pairs={{2,0},{0,2},{3,1},{1,3},{6,4},{4,6},{7,5},{5,7},{10,8},{8,10},{11,... | collective-permute-start | bytes 196616 | tf_op jit(solution)/shard_map/ppermute | solution.py:241
  27.9 1.2 %collective-permute-done.8.refs_1_ = bf16[1,64,512]{2,1,0:T(8,128)(2,1)S(1)} collective-permute-done((bf16[1,64,512]{2,1,0:T(8,128)(2,1)S(1)}, bf16[1,64,512]{2,1,0:T(8,128)(2,1)S(1)}, u32[]{:S(2)}, u32[]{:S(2)}) %collective-permute-start.8) | collective-permute-done | bytes 65568 | tf_op jit(solution)/shard_map/ppermute | solution.py:241
  29.1 0.6 %collective-permute-start.14 = (bf16[1,64,512]{2,1,0:T(8,128)(2,1)S(1)}, bf16[1,64,512]{2,1,0:T(8,128)(2,1)S(1)}, u32[]{:S(2)}, u32[]{:S(2)}) collective-permute-start(bf16[1,64,512]{2,1,0:T(8,128)(2,1)S(1)} %collective-permute-done.8.refs_1_), channel_id=1, source_target_pairs={{2,0},{0,2},{3,1},{1,3},{6,4},{4,6},{7,5},{5,7},{10,8},{8,10},{11,... | collective-permute-start | bytes 196616 | tf_op jit(solution)/shard_map/ppermute | solution.py:241
  29.6 0.0 collective-permute-done.9.refs_2_
  29.7 0.1 collective-permute-start.10
  29.8 0.7 %collective-permute-done.15.refs_2_ = bf16[1,64,512]{2,1,0:T(8,128)(2,1)S(1)} collective-permute-done((bf16[1,64,512]{2,1,0:T(8,128)(2,1)S(1)}, bf16[1,64,512]{2,1,0:T(8,128)(2,1)S(1)}, u32[]{:S(2)}, u32[]{:S(2)}) %collective-permute-start.15) | collective-permute-done | bytes 65568 | tf_op jit(solution)/shard_map/ppermute | solution.py:241
  30.5 0.9 %collective-permute-done.13.refs_0_ = bf16[1,64,512]{2,1,0:T(8,128)(2,1)S(1)} collective-permute-done((bf16[1,64,512]{2,1,0:T(8,128)(2,1)S(1)}, bf16[1,64,512]{2,1,0:T(8,128)(2,1)S(1)}, u32[]{:S(2)}, u32[]{:S(2)}) %collective-permute-start.13) | collective-permute-done | bytes 65568 | tf_op jit(solution)/shard_map/ppermute | solution.py:241
  31.3 2.0 %collective-permute-done.14.refs_1_ = bf16[1,64,512]{2,1,0:T(8,128)(2,1)S(1)} collective-permute-done((bf16[1,64,512]{2,1,0:T(8,128)(2,1)S(1)}, bf16[1,64,512]{2,1,0:T(8,128)(2,1)S(1)}, u32[]{:S(2)}, u32[]{:S(2)}) %collective-permute-start.14) | collective-permute-done | bytes 65568 | tf_op jit(solution)/shard_map/ppermute | solution.py:241
  33.4 0.1 collective-permute-start.16
  33.5 0.0 collective-permute-done.10.sigma_other.other
  33.5 1.0 %left_products.1 = (f32[4,256,512]{2,1,0:T(8,128)S(1)}, f32[1,4,256,512]{3,2,1,0:T(8,128)S(1)}) custom-call(bf16[4,256,256]{2,1,0:T(8,128)(2,1)S(1)} %get-tuple-element.23._.refs_2_.left_own, bf16[4,256,256]{2,1,0:T(8,128)(2,1)S(1)} %get-tuple-element.26.refs_3_.left_other, bf16[1,256,512]{2,1,0:T(8,128)(2,1)S(1)} %place_own_sector.1.sigma_own.own.refs_1_, ...), custom_call_target="tpu_custom_call" | custom-call | tf_op jit(solution)/shard_map/left_products/pallas_call | solution.py:259
  34.5 0.5 collective-permute-done.16.other
  35.0 1.1 %second_sigma_terms.1 = (f32[1,64,512]{2,1,0:T(8,128)S(1)}, bf16[1,64,512]{2,1,0:T(8,128)(2,1)S(1)}, bf16[1,64,512]{2,1,0:T(8,128)(2,1)S(1)}, bf16[1,64,512]{2,1,0:T(8,128)(2,1)S(1)}) custom-call(f32[4,2,8,128]{3,2,1,0:T(8,128)S(1)} %get-tuple-element.34.refs_7_.mixing, f32[256,512]{1,0:T(8,128)S(1)} %get-tuple-element.37.live, ...), custom_call_target="tpu_custom_call" | custom-call | tf_op jit(solution)/shard_map/second_sigma_terms/pallas_call | solution.py:259
  36.1 1.8 %collective-permute-start.17 = (bf16[1,64,512]{2,1,0:T(8,128)(2,1)S(1)}, bf16[1,64,512]{2,1,0:T(8,128)(2,1)S(1)}, u32[]{:S(2)}, u32[]{:S(2)}) collective-permute-start(bf16[1,64,512]{2,1,0:T(8,128)(2,1)S(1)} %get-tuple-element.41), channel_id=1, source_target_pairs={{12,0},{8,4},{4,8},{0,12},{13,1},{9,5},{5,9},{1,13},{14,2},{10,6},... | collective-permute-start | bytes 196616 | tf_op jit(solution)/shard_map/ppermute | solution.py:241
  37.9 0.0 collective-permute-start.18
  37.9 2.6 %collective-permute-start.19 = (bf16[1,64,512]{2,1,0:T(8,128)(2,1)S(1)}, bf16[1,64,512]{2,1,0:T(8,128)(2,1)S(1)}, u32[]{:S(2)}, u32[]{:S(2)}) collective-permute-start(bf16[1,64,512]{2,1,0:T(8,128)(2,1)S(1)} %get-tuple-element.43), channel_id=1, source_target_pairs={{4,0},{0,4},{12,8},{8,12},{5,1},{1,5},{13,9},{9,13},{6,2},{2,6},{1... | collective-permute-start | bytes 196616 | tf_op jit(solution)/shard_map/ppermute | solution.py:241
  40.6 0.5 sums_for_rayleigh.1.refs_0_.refs_4_
  41.1 0.6 %collective-permute-start.11 = (f32[3,8,128]{2,1,0:T(8,128)S(1)}, f32[3,8,128]{2,1,0:T(8,128)S(1)}, u32[]{:S(2)}, u32[]{:S(2)}) collective-permute-start(f32[3,8,128]{2,1,0:T(8,128)S(1)} %sums_for_rayleigh.1.refs_0_.refs_4_), channel_id=1, source_target_pairs={{2,0},{0,2},{3,1},{1,3},{6,4},{4,6},{7,5},{5,7},{10,8},{8,10},{11,... | collective-permute-start | bytes 36872 | tf_op jit(solution)/shard_map/ppermute | solution.py:241
  41.7 3.1 %collective-permute-done.11.refs_1_.refs_5_ = f32[3,8,128]{2,1,0:T(8,128)S(1)} collective-permute-done((f32[3,8,128]{2,1,0:T(8,128)S(1)}, f32[3,8,128]{2,1,0:T(8,128)S(1)}, u32[]{:S(2)}, u32[]{:S(2)}) %collective-permute-start.11) | collective-permute-done | bytes 12320 | tf_op jit(solution)/shard_map/ppermute | solution.py:241
  44.8 0.0 collective-permute-done.17.refs_1_
  44.8 0.1 collective-permute-done.18.refs_2_
  44.9 0.0 collective-permute-done.19.refs_3_
  45.0 1.8 %collective-permute-start.20 = (bf16[1,64,512]{2,1,0:T(8,128)(2,1)S(1)}, bf16[1,64,512]{2,1,0:T(8,128)(2,1)S(1)}, u32[]{:S(2)}, u32[]{:S(2)}) collective-permute-start(bf16[1,64,512]{2,1,0:T(8,128)(2,1)S(1)} %sum_second_sigma.1.refs_5_), channel_id=1, source_target_pairs={{12,0},{8,4},{4,8},{0,12},{13,1},{9,5},{5,9},{1,13},{14,2},{10,6},... | collective-permute-start | bytes 196616 | tf_op jit(solution)/shard_map/ppermute | solution.py:241
  46.8 0.0 collective-permute-start.21
  46.8 2.6 %collective-permute-start.22 = (bf16[1,64,512]{2,1,0:T(8,128)(2,1)S(1)}, bf16[1,64,512]{2,1,0:T(8,128)(2,1)S(1)}, u32[]{:S(2)}, u32[]{:S(2)}) collective-permute-start(bf16[1,64,512]{2,1,0:T(8,128)(2,1)S(1)} %sum_second_sigma.1.refs_5_), channel_id=1, source_target_pairs={{4,0},{0,4},{12,8},{8,12},{5,1},{1,5},{13,9},{9,13},{6,2},{2,6},{1... | collective-permute-start | bytes 196616 | tf_op jit(solution)/shard_map/ppermute | solution.py:241
  49.4 1.4 %second_wave.1 = (bf16[1,256,512]{2,1,0:T(8,128)(2,1)}, f32[2,8,128]{2,1,0:T(8,128)S(1)}) custom-call(s32[2,2]{1,0:T(2,128)S(1)} %copy-done.3, bf16[256,512]{1,0:T(8,128)(2,1)S(1)} %get-tuple-element.24.refs_5_.wave_own, bf16[1,256,512]{2,1,0:T(8,128)(2,1)S(1)} %place_own_sector.1.sigma_own.own.refs_1_, f32[3,8,128]{2,1,0:T(8,128)S(1)} %sums_for_rayleigh.1.refs_0_.refs_4_, ...), custom_call_target="tpu_custom_call" | custom-call | tf_op jit(solution)/shard_map/second_wave/pallas_call | solution.py:259
  50.9 1.0 %collective-permute-done.20.refs_2_ = bf16[1,64,512]{2,1,0:T(8,128)(2,1)S(1)} collective-permute-done((bf16[1,64,512]{2,1,0:T(8,128)(2,1)S(1)}, bf16[1,64,512]{2,1,0:T(8,128)(2,1)S(1)}, u32[]{:S(2)}, u32[]{:S(2)}) %collective-permute-start.20) | collective-permute-done | bytes 65568 | tf_op jit(solution)/shard_map/ppermute | solution.py:241
  51.8 1.8 %collective-permute-done.21.refs_3_ = bf16[1,64,512]{2,1,0:T(8,128)(2,1)S(1)} collective-permute-done((bf16[1,64,512]{2,1,0:T(8,128)(2,1)S(1)}, bf16[1,64,512]{2,1,0:T(8,128)(2,1)S(1)}, u32[]{:S(2)}, u32[]{:S(2)}) %collective-permute-start.21) | collective-permute-done | bytes 65568 | tf_op jit(solution)/shard_map/ppermute | solution.py:241
  53.6 0.0 collective-permute-done.22.refs_4_
  53.6 0.9 %join_second_sigma.1 = f32[1,256,512]{2,1,0:T(8,128)} custom-call(f32[2,8,128]{2,1,0:T(8,128)S(1)} %get-tuple-element.36.refs_0_, bf16[1,256,512]{2,1,0:T(8,128)(2,1)S(1)} %place_own_sector.1.sigma_own.own.refs_1_, bf16[1,64,512]{2,1,0:T(8,128)(2,1)S(1)} %collective-permute-done.20.refs_2_, bf16[1,64,512]{2,1,0:T(8,128)(2,1)S(1)} %collective-permute-done.21.refs_3_, ...), custom_call_target="tpu_custom_call" | custom-call | tf_op jit(solution)/shard_map/join_second_sigma/pallas_call | solution.py:259
  (7 shorter events, 0.1 us)
Async XLA Ops:
  0.6 2.0 %copy-start.1 = (bf16[1,256,512]{2,1,0:T(8,128)(2,1)S(1)}, bf16[1,256,512]{2,1,0:T(8,128)(2,1)}, u32[]{:S(2)}) copy-start(bf16[1,256,512]{2,1,0:T(8,128)(2,1)} %wave.1) | copy-start | bytes 786436
  0.6 2.0 %copy-start.3 = (s32[2,2]{1,0:T(2,128)S(1)}, s32[2,2]{1,0:T(2,128)}, u32[]{:S(2)}) copy-start(s32[2,2]{1,0:T(2,128)} %sizes_ref.3) | copy-start | bytes 52
  0.7 2.0 %copy-start.2 = (s32[4,8,2]{1,2,0:T(2,128)S(1)}, s32[4,8,2]{1,2,0:T(2,128)}, u32[]{:S(2)}) copy-start(s32[4,8,2]{1,2,0:T(2,128)} %param.10) | copy-start | bytes 772
  0.7 2.0 %copy-start.4 = (f32[4,8]{1,0:T(4,128)S(1)}, f32[4,8]{1,0:T(4,128)}, u32[]{:S(2)}) copy-start(f32[4,8]{1,0:T(4,128)} %weights_ref.1) | copy-start | bytes 388
  0.7 2.2 %copy-start = (bf16[4,512,512]{2,1,0:T(8,128)(2,1)S(1)}, bf16[4,512,512]{2,1,0:T(8,128)(2,1)}, u32[]{:S(2)}) copy-start(bf16[4,512,512]{2,1,0:T(8,128)(2,1)} %right.1) | copy-start | bytes 6291460
  0.7 2.2 %collective-permute-start = (bf16[1,256,512]{2,1,0:T(8,128)(2,1)}, bf16[1,256,512]{2,1,0:T(8,128)(2,1)S(1)}, u32[]{:S(2)}, u32[]{:S(2)}) collective-permute-start(bf16[1,256,512]{2,1,0:T(8,128)(2,1)} %wave.1), channel_id=1, source_target_pairs={{1,0},{0,1},{3,2},{2,3},{5,4},{4,5},{7,6},{6,7},{9,8},{8,9},{11,10... | collective-permute-start | bytes 786440 | tf_op jit(solution)/shard_map/ppermute | solution.py:241
  4.6 8.7 %collective-permute-start.1 = (bf16[2,64,512]{2,1,0:T(8,128)(2,1)S(1)}, bf16[2,64,512]{2,1,0:T(8,128)(2,1)S(1)}, u32[]{:S(2)}, u32[]{:S(2)}) collective-permute-start(bf16[2,64,512]{2,1,0:T(8,128)(2,1)S(1)} %get-tuple-element.28), channel_id=1, source_target_pairs={{2,0},{0,2},{3,1},{1,3},{6,4},{4,6},{7,5},{5,7},{10,8},{8,10},{11,... | collective-permute-start | bytes 393224 | tf_op jit(solution)/shard_map/ppermute | solution.py:241
  7.4 10.4 %collective-permute-start.3 = (bf16[1,64,512]{2,1,0:T(8,128)(2,1)S(1)}, bf16[1,64,512]{2,1,0:T(8,128)(2,1)S(1)}, u32[]{:S(2)}, u32[]{:S(2)}) collective-permute-start(bf16[1,64,512]{2,1,0:T(8,128)(2,1)S(1)} %get-tuple-element.29), channel_id=1, source_target_pairs={{4,0},{0,4},{12,8},{8,12},{5,1},{1,5},{13,9},{9,13},{6,2},{2,6},{1... | collective-permute-start | bytes 196616 | tf_op jit(solution)/shard_map/ppermute | solution.py:241
  9.0 8.8 %collective-permute-start.4 = (bf16[1,64,512]{2,1,0:T(8,128)(2,1)S(1)}, bf16[1,64,512]{2,1,0:T(8,128)(2,1)S(1)}, u32[]{:S(2)}, u32[]{:S(2)}) collective-permute-start(bf16[1,64,512]{2,1,0:T(8,128)(2,1)S(1)} %get-tuple-element.30), channel_id=1, source_target_pairs={{8,0},{12,4},{0,8},{4,12},{9,1},{13,5},{1,9},{5,13},{10,2},{14,6},... | collective-permute-start | bytes 196616 | tf_op jit(solution)/shard_map/ppermute | solution.py:241
  11.5 8.4 %collective-permute-start.5 = (bf16[1,64,512]{2,1,0:T(8,128)(2,1)S(1)}, bf16[1,64,512]{2,1,0:T(8,128)(2,1)S(1)}, u32[]{:S(2)}, u32[]{:S(2)}) collective-permute-start(bf16[1,64,512]{2,1,0:T(8,128)(2,1)S(1)} %get-tuple-element.31), channel_id=1, source_target_pairs={{10,0},{8,2},{14,4},{12,6},{2,8},{0,10},{6,12},{4,14},{11,1},{9,3}... | collective-permute-start | bytes 196616 | tf_op jit(solution)/shard_map/ppermute | solution.py:241
  11.8 8.1 %collective-permute-start.6 = (bf16[1,64,512]{2,1,0:T(8,128)(2,1)S(1)}, bf16[1,64,512]{2,1,0:T(8,128)(2,1)S(1)}, u32[]{:S(2)}, u32[]{:S(2)}) collective-permute-start(bf16[1,64,512]{2,1,0:T(8,128)(2,1)S(1)} %get-tuple-element.32), channel_id=1, source_target_pairs={{6,0},{4,2},{2,4},{0,6},{14,8},{12,10},{10,12},{8,14},{7,1},{5,3},... | collective-permute-start | bytes 196616 | tf_op jit(solution)/shard_map/ppermute | solution.py:241
  13.3 6.7 %collective-permute-start.2 = (bf16[1,64,512]{2,1,0:T(8,128)(2,1)S(1)}, bf16[1,64,512]{2,1,0:T(8,128)(2,1)S(1)}, u32[]{:S(2)}, u32[]{:S(2)}) collective-permute-start(bf16[1,64,512]{2,1,0:T(8,128)(2,1)S(1)} %sum_far_share.1), channel_id=1, source_target_pairs={{12,0},{8,4},{4,8},{0,12},{13,1},{9,5},{5,9},{1,13},{14,2},{10,6},... | collective-permute-start | bytes 196616 | tf_op jit(solution)/shard_map/ppermute | solution.py:241
  20.0 6.9 %collective-permute-start.7 = (bf16[1,64,512]{2,1,0:T(8,128)(2,1)S(1)}, bf16[1,64,512]{2,1,0:T(8,128)(2,1)S(1)}, u32[]{:S(2)}, u32[]{:S(2)}) collective-permute-start(bf16[1,64,512]{2,1,0:T(8,128)(2,1)S(1)} %sum_first_sigma.1.refs_3_), channel_id=1, source_target_pairs={{8,0},{12,4},{0,8},{4,12},{9,1},{13,5},{1,9},{5,13},{10,2},{14,6},... | collective-permute-start | bytes 196616 | tf_op jit(solution)/shard_map/ppermute | solution.py:241
  21.4 5.6 %collective-permute-start.12 = (bf16[1,64,512]{2,1,0:T(8,128)(2,1)S(1)}, bf16[1,64,512]{2,1,0:T(8,128)(2,1)S(1)}, u32[]{:S(2)}, u32[]{:S(2)}) collective-permute-start(bf16[1,64,512]{2,1,0:T(8,128)(2,1)S(1)} %sum_first_sigma.1.refs_3_), channel_id=1, source_target_pairs={{2,0},{0,2},{3,1},{1,3},{6,4},{4,6},{7,5},{5,7},{10,8},{8,10},{11,... | collective-permute-start | bytes 196616 | tf_op jit(solution)/shard_map/ppermute | solution.py:241
  22.9 6.2 %collective-permute-start.8 = (bf16[1,64,512]{2,1,0:T(8,128)(2,1)S(1)}, bf16[1,64,512]{2,1,0:T(8,128)(2,1)S(1)}, u32[]{:S(2)}, u32[]{:S(2)}) collective-permute-start(bf16[1,64,512]{2,1,0:T(8,128)(2,1)S(1)} %sum_first_sigma.1.refs_3_), channel_id=1, source_target_pairs={{12,0},{8,4},{4,8},{0,12},{13,1},{9,5},{5,9},{1,13},{14,2},{10,6},... | collective-permute-start | bytes 196616 | tf_op jit(solution)/shard_map/ppermute | solution.py:241
  24.3 5.4 %collective-permute-start.9 = (bf16[1,64,512]{2,1,0:T(8,128)(2,1)S(1)}, bf16[1,64,512]{2,1,0:T(8,128)(2,1)S(1)}, u32[]{:S(2)}, u32[]{:S(2)}) collective-permute-start(bf16[1,64,512]{2,1,0:T(8,128)(2,1)S(1)} %sum_first_sigma.1.refs_3_), channel_id=1, source_target_pairs={{4,0},{0,4},{12,8},{8,12},{5,1},{1,5},{13,9},{9,13},{6,2},{2,6},{1... | collective-permute-start | bytes 196616 | tf_op jit(solution)/shard_map/ppermute | solution.py:241
  24.3 6.1 %collective-permute-start.15 = (bf16[1,64,512]{2,1,0:T(8,128)(2,1)S(1)}, bf16[1,64,512]{2,1,0:T(8,128)(2,1)S(1)}, u32[]{:S(2)}, u32[]{:S(2)}) collective-permute-start(bf16[1,64,512]{2,1,0:T(8,128)(2,1)S(1)} %sum_first_sigma.1.refs_3_), channel_id=1, source_target_pairs={{6,0},{4,2},{2,4},{0,6},{14,8},{12,10},{10,12},{8,14},{7,1},{5,3},... | collective-permute-start | bytes 196616 | tf_op jit(solution)/shard_map/ppermute | solution.py:241
  27.0 4.3 %collective-permute-start.13 = (bf16[1,64,512]{2,1,0:T(8,128)(2,1)S(1)}, bf16[1,64,512]{2,1,0:T(8,128)(2,1)S(1)}, u32[]{:S(2)}, u32[]{:S(2)}) collective-permute-start(bf16[1,64,512]{2,1,0:T(8,128)(2,1)S(1)} %hand_on.1), channel_id=1, source_target_pairs={{2,0},{0,2},{3,1},{1,3},{6,4},{4,6},{7,5},{5,7},{10,8},{8,10},{11,... | collective-permute-start | bytes 196616 | tf_op jit(solution)/shard_map/ppermute | solution.py:241
  29.1 4.3 %collective-permute-start.14 = (bf16[1,64,512]{2,1,0:T(8,128)(2,1)S(1)}, bf16[1,64,512]{2,1,0:T(8,128)(2,1)S(1)}, u32[]{:S(2)}, u32[]{:S(2)}) collective-permute-start(bf16[1,64,512]{2,1,0:T(8,128)(2,1)S(1)} %collective-permute-done.8.refs_1_), channel_id=1, source_target_pairs={{2,0},{0,2},{3,1},{1,3},{6,4},{4,6},{7,5},{5,7},{10,8},{8,10},{11,... | collective-permute-start | bytes 196616 | tf_op jit(solution)/shard_map/ppermute | solution.py:241
  29.7 3.8 %collective-permute-start.10 = (bf16[1,256,512]{2,1,0:T(8,128)(2,1)S(1)}, bf16[1,256,512]{2,1,0:T(8,128)(2,1)S(1)}, u32[]{:S(2)}, u32[]{:S(2)}) collective-permute-start(bf16[1,256,512]{2,1,0:T(8,128)(2,1)S(1)} %place_own_sector.1.sigma_own.own.refs_1_), channel_id=1, source_target_pairs={{1,0},{0,1},{3,2},{2,3},{5,4},{4,5},{7,6},{6,7},{9,8},{8,9},{11,10... | collective-permute-start | bytes 786440 | tf_op jit(solution)/shard_map/ppermute | solution.py:241
  33.4 1.6 %collective-permute-start.16 = (bf16[1,256,512]{2,1,0:T(8,128)(2,1)S(1)}, bf16[1,256,512]{2,1,0:T(8,128)(2,1)S(1)}, u32[]{:S(2)}, u32[]{:S(2)}) collective-permute-start(bf16[1,256,512]{2,1,0:T(8,128)(2,1)S(1)} %place_other_sectors.1.across_own), channel_id=1, source_target_pairs={{1,0},{0,1},{3,2},{2,3},{5,4},{4,5},{7,6},{6,7},{9,8},{8,9},{11,10... | collective-permute-start | bytes 786440 | tf_op jit(solution)/shard_map/ppermute | solution.py:241
  36.1 8.7 %collective-permute-start.17 = (bf16[1,64,512]{2,1,0:T(8,128)(2,1)S(1)}, bf16[1,64,512]{2,1,0:T(8,128)(2,1)S(1)}, u32[]{:S(2)}, u32[]{:S(2)}) collective-permute-start(bf16[1,64,512]{2,1,0:T(8,128)(2,1)S(1)} %get-tuple-element.41), channel_id=1, source_target_pairs={{12,0},{8,4},{4,8},{0,12},{13,1},{9,5},{5,9},{1,13},{14,2},{10,6},... | collective-permute-start | bytes 196616 | tf_op jit(solution)/shard_map/ppermute | solution.py:241
  37.9 7.0 %collective-permute-start.18 = (bf16[1,64,512]{2,1,0:T(8,128)(2,1)S(1)}, bf16[1,64,512]{2,1,0:T(8,128)(2,1)S(1)}, u32[]{:S(2)}, u32[]{:S(2)}) collective-permute-start(bf16[1,64,512]{2,1,0:T(8,128)(2,1)S(1)} %get-tuple-element.42), channel_id=1, source_target_pairs={{8,0},{12,4},{0,8},{4,12},{9,1},{13,5},{1,9},{5,13},{10,2},{14,6},... | collective-permute-start | bytes 196616 | tf_op jit(solution)/shard_map/ppermute | solution.py:241
  37.9 7.0 %collective-permute-start.19 = (bf16[1,64,512]{2,1,0:T(8,128)(2,1)S(1)}, bf16[1,64,512]{2,1,0:T(8,128)(2,1)S(1)}, u32[]{:S(2)}, u32[]{:S(2)}) collective-permute-start(bf16[1,64,512]{2,1,0:T(8,128)(2,1)S(1)} %get-tuple-element.43), channel_id=1, source_target_pairs={{4,0},{0,4},{12,8},{8,12},{5,1},{1,5},{13,9},{9,13},{6,2},{2,6},{1... | collective-permute-start | bytes 196616 | tf_op jit(solution)/shard_map/ppermute | solution.py:241
  41.1 3.8 %collective-permute-start.11 = (f32[3,8,128]{2,1,0:T(8,128)S(1)}, f32[3,8,128]{2,1,0:T(8,128)S(1)}, u32[]{:S(2)}, u32[]{:S(2)}) collective-permute-start(f32[3,8,128]{2,1,0:T(8,128)S(1)} %sums_for_rayleigh.1.refs_0_.refs_4_), channel_id=1, source_target_pairs={{2,0},{0,2},{3,1},{1,3},{6,4},{4,6},{7,5},{5,7},{10,8},{8,10},{11,... | collective-permute-start | bytes 36872 | tf_op jit(solution)/shard_map/ppermute | solution.py:241
  45.0 6.9 %collective-permute-start.20 = (bf16[1,64,512]{2,1,0:T(8,128)(2,1)S(1)}, bf16[1,64,512]{2,1,0:T(8,128)(2,1)S(1)}, u32[]{:S(2)}, u32[]{:S(2)}) collective-permute-start(bf16[1,64,512]{2,1,0:T(8,128)(2,1)S(1)} %sum_second_sigma.1.refs_5_), channel_id=1, source_target_pairs={{12,0},{8,4},{4,8},{0,12},{13,1},{9,5},{5,9},{1,13},{14,2},{10,6},... | collective-permute-start | bytes 196616 | tf_op jit(solution)/shard_map/ppermute | solution.py:241
  46.8 6.9 %collective-permute-start.21 = (bf16[1,64,512]{2,1,0:T(8,128)(2,1)S(1)}, bf16[1,64,512]{2,1,0:T(8,128)(2,1)S(1)}, u32[]{:S(2)}, u32[]{:S(2)}) collective-permute-start(bf16[1,64,512]{2,1,0:T(8,128)(2,1)S(1)} %sum_second_sigma.1.refs_5_), channel_id=1, source_target_pairs={{8,0},{12,4},{0,8},{4,12},{9,1},{13,5},{1,9},{5,13},{10,2},{14,6},... | collective-permute-start | bytes 196616 | tf_op jit(solution)/shard_map/ppermute | solution.py:241
  46.8 6.9 %collective-permute-start.22 = (bf16[1,64,512]{2,1,0:T(8,128)(2,1)S(1)}, bf16[1,64,512]{2,1,0:T(8,128)(2,1)S(1)}, u32[]{:S(2)}, u32[]{:S(2)}) collective-permute-start(bf16[1,64,512]{2,1,0:T(8,128)(2,1)S(1)} %sum_second_sigma.1.refs_5_), channel_id=1, source_target_pairs={{4,0},{0,4},{12,8},{8,12},{5,1},{1,5},{13,9},{9,13},{6,2},{2,6},{1... | collective-permute-start | bytes 196616 | tf_op jit(solution)/shard_map/ppermute | solution.py:241

commit v19 on v17

--- a/solution.py
+++ b/solution.py
@@ -101,18 +101,21 @@
             part = weight * product
             totals[step] = part if totals[step] is None else totals[step] + part
     for step in range(sectors):
-        live = live_rows(sizes, sector ^ step, core * rows, rows, columns)
-        held[step] = totals[step] * live
+        held[step] = totals[step]
     for (steps, across), out in zip(shares, parts):
         for index, along in enumerate(steps):
             start = pl.multiple_of((place ^ along) * share, share)
             out[index] = held[across, pl.ds(start, share), :].astype(out.dtype)
 
 
-def sum_kernel(indices, *refs):
+def sum_kernel(indices, masked, *refs):
     total = refs[0][indices[0]].astype(jnp.float32)
     for index, piece in zip(indices[1:], refs[1:]):
         total = total + piece[index].astype(jnp.float32)
+    if masked:
+        share = total.shape[0]
+        start = pl.multiple_of(lax.axis_index("ops") * share, share)
+        total = total * refs[len(indices)][pl.ds(start, share), :]
     refs[-1][0] = total.astype(refs[-1].dtype)
 
 
@@ -142,7 +145,7 @@
     live[...] = jnp.where(cells, 1.0, 0.0)
 
 
-def second_kernel(mixing, live, left_other, right, products, across_products, other, *refs):
+def second_kernel(mixing, left_other, right, products, across_products, other, *refs):
     shares, held = refs[:-1], refs[-1]
     rows, columns = products.shape[1:]
     share = shares[0].shape[1]
@@ -159,7 +162,7 @@
             combined = combined + weights[step + 1] * (across_products[step, term] + part[term])
         part = times_right(combined, right, term)
         total = part if total is None else total + part
-    held[...] = total * live[...]
+    held[...] = total
     for step, out in enumerate(shares):
         start = pl.multiple_of((place ^ step) * share, share)
         out[0] = held[pl.ds(start, share), :].astype(out.dtype)
@@ -266,15 +269,16 @@
             name=name,
         )(*operands)
 
-    def summed(name, *pieces, after=()):
+    def summed(name, *pieces, live=None, after=()):
         pieces = [piece if isinstance(piece, tuple) else (piece, 0) for piece in pieces]
         arrays, indices = zip(*pieces)
         return call(
-            lambda *refs: sum_kernel(indices, *refs),
+            lambda *refs: sum_kernel(indices, live is not None, *refs),
             name,
             shape(1, share, columns),
             [],
             *arrays,
+            *([] if live is None else [live]),
             *after,
         )
 
@@ -336,10 +340,10 @@
     )
     met = [partner(rest[(far, 0), across], {"sec": across}) for across in range(sectors)]
     received = [partner(summed("sum_far_share", *met), {"ops": far})]
-    nearest = ((1,), 0)
-    order = [nearest] + [spot for spot in rest if spot[0] in direct and spot != nearest]
+    first_two = [(direct[0], 0), (direct[-1], 0)]
+    order = first_two + [spot for spot in rest if spot[0] in direct and spot not in first_two]
     received += [partner(rest[spot], {"ops": spot[0][0], "sec": spot[1]}) for spot in order]
-    first_share = summed("sum_first_sigma", *[(piece, 1) for piece in met], *received, after=(mixing,))
+    first_share = summed("sum_first_sigma", *[(piece, 1) for piece in met], *received, live=live)
     along_ops = {along: partner(first_share, {"ops": along}) for along in send_order}
     sigma_own = call(
         lambda *refs: place_kernel([(along, 0) for along in send_order], *refs),
@@ -385,7 +389,6 @@
         [shape(1, share, columns, dtype=f32)] + [shape(1, share, columns)] * (ops_count - 1),
         [],
         mixing,
-        live,
         left_other,
         right,
         products,
@@ -405,7 +408,7 @@
         sigma_other,
     )
     sums = [partner(sums, {"sec": step}) for step in range(sectors)]
-    second_share = summed("sum_second_sigma", shares[0], *received, after=sums)
+    second_share = summed("sum_second_sigma", shares[0], *received, live=live, after=sums)
     second_wave, factors = call(
         wave_kernel,
         "second_wave",

time: 53.6 us -> 53.5 us (level)
  starting transfers between devices: 32 us -> 31.4 us
  waiting for transfers between devices: 11.4 us -> 12 us
    ppermute x23, starting transfers between devices: 32 us -> 31.4 us  [partner(): return lax.ppermute(value, axes, pairs)]
    ppermute x23, waiting for transfers between devices: 11.4 us -> 12 us  [partner(): return lax.ppermute(value, axes, pairs)]
  transfers between devices with their start and end apart: 23 -> 23, of which waited for: 11 -> 12; matrix products, arithmetic and copies ran while one was open for 0% -> 0% of each run, Pallas kernels for 10% -> 10%
where the time goes in v19:
time: 53.5 us; the launch traced here: 53.3 us
  starting transfers between devices  31.4 us (59%)
  waiting for transfers between devices  12 us (22%)
  Pallas kernels  9.11 us (17%)
  between operations  0.85 us (2%)
    ppermute x23, starting transfers between devices, partner(): return lax.ppermute(value, axes, pairs)  31.4 us
    ppermute x23, waiting for transfers between devices, partner(): return lax.ppermute(value, axes, pairs)  12 us
    pallas_call x14, Pallas kernels, call(): pl.pallas_call(kernel, out_shape=out_shape, in_specs=list(in_specs) + [in...  9.11 us
  transfers between devices with their start and end apart: 23, of which 12 were waited for; matrix products, arithmetic and copies ran while one was open for 0% of the time, Pallas kernels for 10%

profile of v19, /device:TPU:0, one launch (start us, length us, event | category | flops | bytes accessed | tf_op | source)
XLA Modules:
  0.0 53.3 jit_solution(6365629542447469499)
XLA Ops:
  0.6 0.0 copy-start.1
  0.6 0.0 copy-start.3
  0.7 0.0 copy-start.2
  0.7 0.0 copy-start.4
  0.7 0.5 collective-permute-start
  1.2 1.4 %load_operators.1 = (bf16[4,256,256]{2,1,0:T(8,128)(2,1)S(1)}, bf16[4,256,256]{2,1,0:T(8,128)(2,1)S(1)}) custom-call(bf16[4,512,512]{2,1,0:T(8,128)(2,1)} %left_ref.1), custom_call_target="tpu_custom_call" | custom-call | tf_op jit(solution)/shard_map/load_operators/pallas_call | solution.py:262
  2.6 0.0 copy-done.1
  2.6 0.0 copy-done.3
  2.7 0.0 copy-done.2
  2.7 0.0 copy-done.4
  2.7 0.2 tables_for_first_sigma.1
  2.9 0.0 collective-permute-done.refs_6_
  2.9 1.6 %first_sigma_terms.1 = (bf16[256,512]{1,0:T(8,128)(2,1)S(1)}, f32[2,64,512]{2,1,0:T(8,128)S(1)}, bf16[2,64,512]{2,1,0:T(8,128)(2,1)S(1)}, bf16[1,64,512]{2,1,0:T...) custom-call(s32[2,2]{1,0:T(2,128)S(1)} %copy-done.3, ...), custom_call_target="tpu_custom_call" | custom-call | tf_op jit(solution)/shard_map/first_sigma_terms/pallas_call | solution.py:262
  4.5 2.8 %collective-permute-start.1 = (bf16[2,64,512]{2,1,0:T(8,128)(2,1)S(1)}, bf16[2,64,512]{2,1,0:T(8,128)(2,1)S(1)}, u32[]{:S(2)}, u32[]{:S(2)}) collective-permute-start(bf16[2,64,512]{2,1,0:T(8,128)(2,1)S(1)} %get-tuple-element.28), channel_id=1, source_target_pairs={{2,0},{0,2},{3,1},{1,3},{6,4},{4,6},{7,5},{5,7},{10,8},{8,10},{11,... | collective-permute-start | bytes 393224 | tf_op jit(solution)/shard_map/ppermute | solution.py:244
  7.3 2.6 %collective-permute-start.3 = (bf16[1,64,512]{2,1,0:T(8,128)(2,1)S(1)}, bf16[1,64,512]{2,1,0:T(8,128)(2,1)S(1)}, u32[]{:S(2)}, u32[]{:S(2)}) collective-permute-start(bf16[1,64,512]{2,1,0:T(8,128)(2,1)S(1)} %get-tuple-element.29), channel_id=1, source_target_pairs={{8,0},{12,4},{0,8},{4,12},{9,1},{13,5},{1,9},{5,13},{10,2},{14,6},... | collective-permute-start | bytes 196616 | tf_op jit(solution)/shard_map/ppermute | solution.py:244
  9.9 1.6 %collective-permute-start.4 = (bf16[1,64,512]{2,1,0:T(8,128)(2,1)S(1)}, bf16[1,64,512]{2,1,0:T(8,128)(2,1)S(1)}, u32[]{:S(2)}, u32[]{:S(2)}) collective-permute-start(bf16[1,64,512]{2,1,0:T(8,128)(2,1)S(1)} %get-tuple-element.30), channel_id=1, source_target_pairs={{4,0},{0,4},{12,8},{8,12},{5,1},{1,5},{13,9},{9,13},{6,2},{2,6},{1... | collective-permute-start | bytes 196616 | tf_op jit(solution)/shard_map/ppermute | solution.py:244
  11.5 0.3 collective-permute-start.5
  11.8 1.4 %collective-permute-start.6 = (bf16[1,64,512]{2,1,0:T(8,128)(2,1)S(1)}, bf16[1,64,512]{2,1,0:T(8,128)(2,1)S(1)}, u32[]{:S(2)}, u32[]{:S(2)}) collective-permute-start(bf16[1,64,512]{2,1,0:T(8,128)(2,1)S(1)} %get-tuple-element.32), channel_id=1, source_target_pairs={{6,0},{4,2},{2,4},{0,6},{14,8},{12,10},{10,12},{8,14},{7,1},{5,3},... | collective-permute-start | bytes 196616 | tf_op jit(solution)/shard_map/ppermute | solution.py:244
  13.1 0.0 collective-permute-done.1.refs_1_
  13.2 3.7 %collective-permute-start.2 = (bf16[1,64,512]{2,1,0:T(8,128)(2,1)S(1)}, bf16[1,64,512]{2,1,0:T(8,128)(2,1)S(1)}, u32[]{:S(2)}, u32[]{:S(2)}) collective-permute-start(bf16[1,64,512]{2,1,0:T(8,128)(2,1)S(1)} %sum_far_share.1), channel_id=1, source_target_pairs={{12,0},{8,4},{4,8},{0,12},{13,1},{9,5},{5,9},{1,13},{14,2},{10,6},... | collective-permute-start | bytes 196616 | tf_op jit(solution)/shard_map/ppermute | solution.py:244
  16.8 0.8 %tables_for_second_sigma.1 = (f32[4,2,8,128]{3,2,1,0:T(8,128)S(1)}, f32[256,512]{1,0:T(8,128)S(1)}) custom-call(s32[2,2]{1,0:T(2,128)S(1)} %copy-done.3, s32[4,2,8]{2,1,0:T(2,128)S(1)} %bitcast.2, f32[4,8]{1,0:T(4,128)S(1)} %copy-done.4, bf16[256,512]{1,0:T(8,128)(2,1)S(1)} %get-tuple-element.33._.wave_other), custom_call_target="tpu_custom_call" | custom-call | tf_op jit(solution)/shard_map/tables_for_second_sigma/pallas_call | solution.py:262
  17.6 0.0 collective-permute-done.3.refs_3_
  17.7 0.0 collective-permute-done.4.refs_4_
  17.7 2.2 %collective-permute-done.5.refs_5_ = bf16[1,64,512]{2,1,0:T(8,128)(2,1)S(1)} collective-permute-done((bf16[1,64,512]{2,1,0:T(8,128)(2,1)S(1)}, bf16[1,64,512]{2,1,0:T(8,128)(2,1)S(1)}, u32[]{:S(2)}, u32[]{:S(2)}) %collective-permute-start.5) | collective-permute-done | bytes 65568 | tf_op jit(solution)/shard_map/ppermute | solution.py:244
  19.9 0.0 collective-permute-done.6.refs_6_
  19.9 0.0 collective-permute-done.2.refs_2_
  19.9 0.1 sum_first_sigma.1.refs_3_
  20.0 1.1 %collective-permute-start.7 = (bf16[1,64,512]{2,1,0:T(8,128)(2,1)S(1)}, bf16[1,64,512]{2,1,0:T(8,128)(2,1)S(1)}, u32[]{:S(2)}, u32[]{:S(2)}) collective-permute-start(bf16[1,64,512]{2,1,0:T(8,128)(2,1)S(1)} %sum_first_sigma.1.refs_3_), channel_id=1, source_target_pairs={{8,0},{12,4},{0,8},{4,12},{9,1},{13,5},{1,9},{5,13},{10,2},{14,6},... | collective-permute-start | bytes 196616 | tf_op jit(solution)/shard_map/ppermute | solution.py:244
  21.0 2.1 %collective-permute-start.8 = (bf16[1,64,512]{2,1,0:T(8,128)(2,1)S(1)}, bf16[1,64,512]{2,1,0:T(8,128)(2,1)S(1)}, u32[]{:S(2)}, u32[]{:S(2)}) collective-permute-start(bf16[1,64,512]{2,1,0:T(8,128)(2,1)S(1)} %sum_first_sigma.1.refs_3_), channel_id=1, source_target_pairs={{12,0},{8,4},{4,8},{0,12},{13,1},{9,5},{5,9},{1,13},{14,2},{10,6},... | collective-permute-start | bytes 196616 | tf_op jit(solution)/shard_map/ppermute | solution.py:244
  23.1 0.5 collective-permute-start.9
  23.6 2.1 %collective-permute-start.14 = (bf16[1,64,512]{2,1,0:T(8,128)(2,1)S(1)}, bf16[1,64,512]{2,1,0:T(8,128)(2,1)S(1)}, u32[]{:S(2)}, u32[]{:S(2)}) collective-permute-start(bf16[1,64,512]{2,1,0:T(8,128)(2,1)S(1)} %sum_first_sigma.1.refs_3_), channel_id=1, source_target_pairs={{6,0},{4,2},{2,4},{0,6},{14,8},{12,10},{10,12},{8,14},{7,1},{5,3},... | collective-permute-start | bytes 196616 | tf_op jit(solution)/shard_map/ppermute | solution.py:244
  25.7 0.9 %collective-permute-start.15 = (bf16[1,64,512]{2,1,0:T(8,128)(2,1)S(1)}, bf16[1,64,512]{2,1,0:T(8,128)(2,1)S(1)}, u32[]{:S(2)}, u32[]{:S(2)}) collective-permute-start(bf16[1,64,512]{2,1,0:T(8,128)(2,1)S(1)} %sum_first_sigma.1.refs_3_), channel_id=1, source_target_pairs={{2,0},{0,2},{3,1},{1,3},{6,4},{4,6},{7,5},{5,7},{10,8},{8,10},{11,... | collective-permute-start | bytes 196616 | tf_op jit(solution)/shard_map/ppermute | solution.py:244
  26.6 0.1 collective-permute-done.7.refs_0_
  26.7 1.0 %collective-permute-start.12 = (bf16[1,64,512]{2,1,0:T(8,128)(2,1)S(1)}, bf16[1,64,512]{2,1,0:T(8,128)(2,1)S(1)}, u32[]{:S(2)}, u32[]{:S(2)}) collective-permute-start(bf16[1,64,512]{2,1,0:T(8,128)(2,1)S(1)} %collective-permute-done.7.refs_0_), channel_id=1, source_target_pairs={{2,0},{0,2},{3,1},{1,3},{6,4},{4,6},{7,5},{5,7},{10,8},{8,10},{11,... | collective-permute-start | bytes 196616 | tf_op jit(solution)/shard_map/ppermute | solution.py:244
  27.7 0.2 collective-permute-done.8.refs_1_
  27.9 0.9 %collective-permute-start.13 = (bf16[1,64,512]{2,1,0:T(8,128)(2,1)S(1)}, bf16[1,64,512]{2,1,0:T(8,128)(2,1)S(1)}, u32[]{:S(2)}, u32[]{:S(2)}) collective-permute-start(bf16[1,64,512]{2,1,0:T(8,128)(2,1)S(1)} %collective-permute-done.8.refs_1_), channel_id=1, source_target_pairs={{2,0},{0,2},{3,1},{1,3},{6,4},{4,6},{7,5},{5,7},{10,8},{8,10},{11,... | collective-permute-start | bytes 196616 | tf_op jit(solution)/shard_map/ppermute | solution.py:244
  28.8 0.0 collective-permute-done.9.refs_2_
  28.8 0.1 collective-permute-start.10
  28.9 0.2 collective-permute-done.14.refs_2_
  29.0 1.4 %collective-permute-done.15.refs_3_ = bf16[1,64,512]{2,1,0:T(8,128)(2,1)S(1)} collective-permute-done((bf16[1,64,512]{2,1,0:T(8,128)(2,1)S(1)}, bf16[1,64,512]{2,1,0:T(8,128)(2,1)S(1)}, u32[]{:S(2)}, u32[]{:S(2)}) %collective-permute-start.15) | collective-permute-done | bytes 65568 | tf_op jit(solution)/shard_map/ppermute | solution.py:244
  30.4 0.7 %collective-permute-done.12.refs_0_ = bf16[1,64,512]{2,1,0:T(8,128)(2,1)S(1)} collective-permute-done((bf16[1,64,512]{2,1,0:T(8,128)(2,1)S(1)}, bf16[1,64,512]{2,1,0:T(8,128)(2,1)S(1)}, u32[]{:S(2)}, u32[]{:S(2)}) %collective-permute-start.12) | collective-permute-done | bytes 65568 | tf_op jit(solution)/shard_map/ppermute | solution.py:244
  31.1 1.0 %collective-permute-done.13.refs_1_ = bf16[1,64,512]{2,1,0:T(8,128)(2,1)S(1)} collective-permute-done((bf16[1,64,512]{2,1,0:T(8,128)(2,1)S(1)}, bf16[1,64,512]{2,1,0:T(8,128)(2,1)S(1)}, u32[]{:S(2)}, u32[]{:S(2)}) %collective-permute-start.13) | collective-permute-done | bytes 65568 | tf_op jit(solution)/shard_map/ppermute | solution.py:244
  32.2 0.1 collective-permute-start.16
  32.2 0.0 collective-permute-done.10.sigma_other.other
  32.3 1.0 %left_products.1 = (f32[4,256,512]{2,1,0:T(8,128)S(1)}, f32[1,4,256,512]{3,2,1,0:T(8,128)S(1)}) custom-call(bf16[4,256,256]{2,1,0:T(8,128)(2,1)S(1)} %get-tuple-element.23._.refs_2_.left_own, bf16[4,256,256]{2,1,0:T(8,128)(2,1)S(1)} %get-tuple-element.26.refs_3_.left_other, bf16[1,256,512]{2,1,0:T(8,128)(2,1)S(1)} %place_own_sector.1.sigma_own.own.refs_1_, ...), custom_call_target="tpu_custom_call" | custom-call | tf_op jit(solution)/shard_map/left_products/pallas_call | solution.py:262
  33.2 0.5 %collective-permute-done.16.other = bf16[1,256,512]{2,1,0:T(8,128)(2,1)S(1)} collective-permute-done((bf16[1,256,512]{2,1,0:T(8,128)(2,1)S(1)}, bf16[1,256,512]{2,1,0:T(8,128)(2,1)S(1)}, u32[]{:S(2)}, u32[]{:S(2)}) %collective-permute-start.16) | collective-permute-done | bytes 262176 | tf_op jit(solution)/shard_map/ppermute | solution.py:244
  33.8 1.1 %second_sigma_terms.1 = (f32[1,64,512]{2,1,0:T(8,128)S(1)}, bf16[1,64,512]{2,1,0:T(8,128)(2,1)S(1)}, bf16[1,64,512]{2,1,0:T(8,128)(2,1)S(1)}, bf16[1,64,512]{2,1,0:T(8,128)(2,1)S(1)}) custom-call(f32[4,2,8,128]{3,2,1,0:T(8,128)S(1)} %get-tuple-element.37.mixing, bf16[4,256,256]{2,1,0:T(8,128)(2,1)S(1)} %get-tuple-element.26.refs_3_.left_other, ...), custom_call_target="tpu_custom_call" | custom-call | tf_op jit(solution)/shard_map/second_sigma_terms/pallas_call | solution.py:262
  34.9 2.5 %collective-permute-start.17 = (bf16[1,64,512]{2,1,0:T(8,128)(2,1)S(1)}, bf16[1,64,512]{2,1,0:T(8,128)(2,1)S(1)}, u32[]{:S(2)}, u32[]{:S(2)}) collective-permute-start(bf16[1,64,512]{2,1,0:T(8,128)(2,1)S(1)} %get-tuple-element.41), channel_id=1, source_target_pairs={{12,0},{8,4},{4,8},{0,12},{13,1},{9,5},{5,9},{1,13},{14,2},{10,6},... | collective-permute-start | bytes 196616 | tf_op jit(solution)/shard_map/ppermute | solution.py:244
  37.4 0.0 collective-permute-start.18
  37.4 1.9 %collective-permute-start.19 = (bf16[1,64,512]{2,1,0:T(8,128)(2,1)S(1)}, bf16[1,64,512]{2,1,0:T(8,128)(2,1)S(1)}, u32[]{:S(2)}, u32[]{:S(2)}) collective-permute-start(bf16[1,64,512]{2,1,0:T(8,128)(2,1)S(1)} %get-tuple-element.43), channel_id=1, source_target_pairs={{4,0},{0,4},{12,8},{8,12},{5,1},{1,5},{13,9},{9,13},{6,2},{2,6},{1... | collective-permute-start | bytes 196616 | tf_op jit(solution)/shard_map/ppermute | solution.py:244
  39.4 0.5 sums_for_rayleigh.1.refs_0_.refs_5_
  39.9 1.0 %collective-permute-start.11 = (f32[3,8,128]{2,1,0:T(8,128)S(1)}, f32[3,8,128]{2,1,0:T(8,128)S(1)}, u32[]{:S(2)}, u32[]{:S(2)}) collective-permute-start(f32[3,8,128]{2,1,0:T(8,128)S(1)} %sums_for_rayleigh.1.refs_0_.refs_5_), channel_id=1, source_target_pairs={{2,0},{0,2},{3,1},{1,3},{6,4},{4,6},{7,5},{5,7},{10,8},{8,10},{11,... | collective-permute-start | bytes 36872 | tf_op jit(solution)/shard_map/ppermute | solution.py:244
  40.8 2.8 %collective-permute-done.11.refs_1_.refs_6_ = f32[3,8,128]{2,1,0:T(8,128)S(1)} collective-permute-done((f32[3,8,128]{2,1,0:T(8,128)S(1)}, f32[3,8,128]{2,1,0:T(8,128)S(1)}, u32[]{:S(2)}, u32[]{:S(2)}) %collective-permute-start.11) | collective-permute-done | bytes 12320 | tf_op jit(solution)/shard_map/ppermute | solution.py:244
  43.6 0.0 collective-permute-done.17.refs_1_
  43.6 0.1 collective-permute-done.18.refs_2_
  43.7 0.0 collective-permute-done.19.refs_3_
  43.7 2.5 %collective-permute-start.20 = (bf16[1,64,512]{2,1,0:T(8,128)(2,1)S(1)}, bf16[1,64,512]{2,1,0:T(8,128)(2,1)S(1)}, u32[]{:S(2)}, u32[]{:S(2)}) collective-permute-start(bf16[1,64,512]{2,1,0:T(8,128)(2,1)S(1)} %sum_second_sigma.1.refs_5_), channel_id=1, source_target_pairs={{12,0},{8,4},{4,8},{0,12},{13,1},{9,5},{5,9},{1,13},{14,2},{10,6},... | collective-permute-start | bytes 196616 | tf_op jit(solution)/shard_map/ppermute | solution.py:244
  46.3 0.0 collective-permute-start.21
  46.3 1.9 %collective-permute-start.22 = (bf16[1,64,512]{2,1,0:T(8,128)(2,1)S(1)}, bf16[1,64,512]{2,1,0:T(8,128)(2,1)S(1)}, u32[]{:S(2)}, u32[]{:S(2)}) collective-permute-start(bf16[1,64,512]{2,1,0:T(8,128)(2,1)S(1)} %sum_second_sigma.1.refs_5_), channel_id=1, source_target_pairs={{4,0},{0,4},{12,8},{8,12},{5,1},{1,5},{13,9},{9,13},{6,2},{2,6},{1... | collective-permute-start | bytes 196616 | tf_op jit(solution)/shard_map/ppermute | solution.py:244
  48.2 1.4 %second_wave.1 = (bf16[1,256,512]{2,1,0:T(8,128)(2,1)}, f32[2,8,128]{2,1,0:T(8,128)S(1)}) custom-call(s32[2,2]{1,0:T(2,128)S(1)} %copy-done.3, bf16[256,512]{1,0:T(8,128)(2,1)S(1)} %get-tuple-element.24.refs_5_.wave_own, bf16[1,256,512]{2,1,0:T(8,128)(2,1)S(1)} %place_own_sector.1.sigma_own.own.refs_1_, f32[3,8,128]{2,1,0:T(8,128)S(1)} %sums_for_rayleigh.1.refs_0_.refs_5_, ...), custom_call_target="tpu_custom_call" | custom-call | tf_op jit(solution)/shard_map/second_wave/pallas_call | solution.py:262
  49.6 0.8 %collective-permute-done.20.refs_2_ = bf16[1,64,512]{2,1,0:T(8,128)(2,1)S(1)} collective-permute-done((bf16[1,64,512]{2,1,0:T(8,128)(2,1)S(1)}, bf16[1,64,512]{2,1,0:T(8,128)(2,1)S(1)}, u32[]{:S(2)}, u32[]{:S(2)}) %collective-permute-start.20) | collective-permute-done | bytes 65568 | tf_op jit(solution)/shard_map/ppermute | solution.py:244
  50.4 2.0 %collective-permute-done.21.refs_3_ = bf16[1,64,512]{2,1,0:T(8,128)(2,1)S(1)} collective-permute-done((bf16[1,64,512]{2,1,0:T(8,128)(2,1)S(1)}, bf16[1,64,512]{2,1,0:T(8,128)(2,1)S(1)}, u32[]{:S(2)}, u32[]{:S(2)}) %collective-permute-start.21) | collective-permute-done | bytes 65568 | tf_op jit(solution)/shard_map/ppermute | solution.py:244
  52.4 0.0 collective-permute-done.22.refs_4_
  52.4 0.9 %join_second_sigma.1 = f32[1,256,512]{2,1,0:T(8,128)} custom-call(f32[2,8,128]{2,1,0:T(8,128)S(1)} %get-tuple-element.36.refs_0_, bf16[1,256,512]{2,1,0:T(8,128)(2,1)S(1)} %place_own_sector.1.sigma_own.own.refs_1_, bf16[1,64,512]{2,1,0:T(8,128)(2,1)S(1)} %collective-permute-done.20.refs_2_, bf16[1,64,512]{2,1,0:T(8,128)(2,1)S(1)} %collective-permute-done.21.refs_3_, ...), custom_call_target="tpu_custom_call" | custom-call | tf_op jit(solution)/shard_map/join_second_sigma/pallas_call | solution.py:262
  (6 shorter events, 0.1 us)
Async XLA Ops:
  0.6 2.0 %copy-start.1 = (bf16[1,256,512]{2,1,0:T(8,128)(2,1)S(1)}, bf16[1,256,512]{2,1,0:T(8,128)(2,1)}, u32[]{:S(2)}) copy-start(bf16[1,256,512]{2,1,0:T(8,128)(2,1)} %wave.1) | copy-start | bytes 786436
  0.6 2.0 %copy-start.3 = (s32[2,2]{1,0:T(2,128)S(1)}, s32[2,2]{1,0:T(2,128)}, u32[]{:S(2)}) copy-start(s32[2,2]{1,0:T(2,128)} %sizes_ref.3) | copy-start | bytes 52
  0.7 2.0 %copy-start.2 = (s32[4,8,2]{1,2,0:T(2,128)S(1)}, s32[4,8,2]{1,2,0:T(2,128)}, u32[]{:S(2)}) copy-start(s32[4,8,2]{1,2,0:T(2,128)} %param.10) | copy-start | bytes 772
  0.7 2.0 %copy-start.4 = (f32[4,8]{1,0:T(4,128)S(1)}, f32[4,8]{1,0:T(4,128)}, u32[]{:S(2)}) copy-start(f32[4,8]{1,0:T(4,128)} %weights_ref.1) | copy-start | bytes 388
  0.7 2.2 %copy-start = (bf16[4,512,512]{2,1,0:T(8,128)(2,1)S(1)}, bf16[4,512,512]{2,1,0:T(8,128)(2,1)}, u32[]{:S(2)}) copy-start(bf16[4,512,512]{2,1,0:T(8,128)(2,1)} %right.1) | copy-start | bytes 6291460
  0.7 2.2 %collective-permute-start = (bf16[1,256,512]{2,1,0:T(8,128)(2,1)}, bf16[1,256,512]{2,1,0:T(8,128)(2,1)S(1)}, u32[]{:S(2)}, u32[]{:S(2)}) collective-permute-start(bf16[1,256,512]{2,1,0:T(8,128)(2,1)} %wave.1), channel_id=1, source_target_pairs={{1,0},{0,1},{3,2},{2,3},{5,4},{4,5},{7,6},{6,7},{9,8},{8,9},{11,10... | collective-permute-start | bytes 786440 | tf_op jit(solution)/shard_map/ppermute | solution.py:244
  4.5 8.6 %collective-permute-start.1 = (bf16[2,64,512]{2,1,0:T(8,128)(2,1)S(1)}, bf16[2,64,512]{2,1,0:T(8,128)(2,1)S(1)}, u32[]{:S(2)}, u32[]{:S(2)}) collective-permute-start(bf16[2,64,512]{2,1,0:T(8,128)(2,1)S(1)} %get-tuple-element.28), channel_id=1, source_target_pairs={{2,0},{0,2},{3,1},{1,3},{6,4},{4,6},{7,5},{5,7},{10,8},{8,10},{11,... | collective-permute-start | bytes 393224 | tf_op jit(solution)/shard_map/ppermute | solution.py:244
  7.3 10.4 %collective-permute-start.3 = (bf16[1,64,512]{2,1,0:T(8,128)(2,1)S(1)}, bf16[1,64,512]{2,1,0:T(8,128)(2,1)S(1)}, u32[]{:S(2)}, u32[]{:S(2)}) collective-permute-start(bf16[1,64,512]{2,1,0:T(8,128)(2,1)S(1)} %get-tuple-element.29), channel_id=1, source_target_pairs={{8,0},{12,4},{0,8},{4,12},{9,1},{13,5},{1,9},{5,13},{10,2},{14,6},... | collective-permute-start | bytes 196616 | tf_op jit(solution)/shard_map/ppermute | solution.py:244
  9.9 7.8 %collective-permute-start.4 = (bf16[1,64,512]{2,1,0:T(8,128)(2,1)S(1)}, bf16[1,64,512]{2,1,0:T(8,128)(2,1)S(1)}, u32[]{:S(2)}, u32[]{:S(2)}) collective-permute-start(bf16[1,64,512]{2,1,0:T(8,128)(2,1)S(1)} %get-tuple-element.30), channel_id=1, source_target_pairs={{4,0},{0,4},{12,8},{8,12},{5,1},{1,5},{13,9},{9,13},{6,2},{2,6},{1... | collective-permute-start | bytes 196616 | tf_op jit(solution)/shard_map/ppermute | solution.py:244
  11.5 8.4 %collective-permute-start.5 = (bf16[1,64,512]{2,1,0:T(8,128)(2,1)S(1)}, bf16[1,64,512]{2,1,0:T(8,128)(2,1)S(1)}, u32[]{:S(2)}, u32[]{:S(2)}) collective-permute-start(bf16[1,64,512]{2,1,0:T(8,128)(2,1)S(1)} %get-tuple-element.31), channel_id=1, source_target_pairs={{10,0},{8,2},{14,4},{12,6},{2,8},{0,10},{6,12},{4,14},{11,1},{9,3}... | collective-permute-start | bytes 196616 | tf_op jit(solution)/shard_map/ppermute | solution.py:244
  11.8 8.1 %collective-permute-start.6 = (bf16[1,64,512]{2,1,0:T(8,128)(2,1)S(1)}, bf16[1,64,512]{2,1,0:T(8,128)(2,1)S(1)}, u32[]{:S(2)}, u32[]{:S(2)}) collective-permute-start(bf16[1,64,512]{2,1,0:T(8,128)(2,1)S(1)} %get-tuple-element.32), channel_id=1, source_target_pairs={{6,0},{4,2},{2,4},{0,6},{14,8},{12,10},{10,12},{8,14},{7,1},{5,3},... | collective-permute-start | bytes 196616 | tf_op jit(solution)/shard_map/ppermute | solution.py:244
  13.2 6.7 %collective-permute-start.2 = (bf16[1,64,512]{2,1,0:T(8,128)(2,1)S(1)}, bf16[1,64,512]{2,1,0:T(8,128)(2,1)S(1)}, u32[]{:S(2)}, u32[]{:S(2)}) collective-permute-start(bf16[1,64,512]{2,1,0:T(8,128)(2,1)S(1)} %sum_far_share.1), channel_id=1, source_target_pairs={{12,0},{8,4},{4,8},{0,12},{13,1},{9,5},{5,9},{1,13},{14,2},{10,6},... | collective-permute-start | bytes 196616 | tf_op jit(solution)/shard_map/ppermute | solution.py:244
  20.0 6.8 %collective-permute-start.7 = (bf16[1,64,512]{2,1,0:T(8,128)(2,1)S(1)}, bf16[1,64,512]{2,1,0:T(8,128)(2,1)S(1)}, u32[]{:S(2)}, u32[]{:S(2)}) collective-permute-start(bf16[1,64,512]{2,1,0:T(8,128)(2,1)S(1)} %sum_first_sigma.1.refs_3_), channel_id=1, source_target_pairs={{8,0},{12,4},{0,8},{4,12},{9,1},{13,5},{1,9},{5,13},{10,2},{14,6},... | collective-permute-start | bytes 196616 | tf_op jit(solution)/shard_map/ppermute | solution.py:244
  21.0 6.8 %collective-permute-start.8 = (bf16[1,64,512]{2,1,0:T(8,128)(2,1)S(1)}, bf16[1,64,512]{2,1,0:T(8,128)(2,1)S(1)}, u32[]{:S(2)}, u32[]{:S(2)}) collective-permute-start(bf16[1,64,512]{2,1,0:T(8,128)(2,1)S(1)} %sum_first_sigma.1.refs_3_), channel_id=1, source_target_pairs={{12,0},{8,4},{4,8},{0,12},{13,1},{9,5},{5,9},{1,13},{14,2},{10,6},... | collective-permute-start | bytes 196616 | tf_op jit(solution)/shard_map/ppermute | solution.py:244
  23.1 5.7 %collective-permute-start.9 = (bf16[1,64,512]{2,1,0:T(8,128)(2,1)S(1)}, bf16[1,64,512]{2,1,0:T(8,128)(2,1)S(1)}, u32[]{:S(2)}, u32[]{:S(2)}) collective-permute-start(bf16[1,64,512]{2,1,0:T(8,128)(2,1)S(1)} %sum_first_sigma.1.refs_3_), channel_id=1, source_target_pairs={{4,0},{0,4},{12,8},{8,12},{5,1},{1,5},{13,9},{9,13},{6,2},{2,6},{1... | collective-permute-start | bytes 196616 | tf_op jit(solution)/shard_map/ppermute | solution.py:244
  23.6 5.4 %collective-permute-start.14 = (bf16[1,64,512]{2,1,0:T(8,128)(2,1)S(1)}, bf16[1,64,512]{2,1,0:T(8,128)(2,1)S(1)}, u32[]{:S(2)}, u32[]{:S(2)}) collective-permute-start(bf16[1,64,512]{2,1,0:T(8,128)(2,1)S(1)} %sum_first_sigma.1.refs_3_), channel_id=1, source_target_pairs={{6,0},{4,2},{2,4},{0,6},{14,8},{12,10},{10,12},{8,14},{7,1},{5,3},... | collective-permute-start | bytes 196616 | tf_op jit(solution)/shard_map/ppermute | solution.py:244
  25.7 4.7 %collective-permute-start.15 = (bf16[1,64,512]{2,1,0:T(8,128)(2,1)S(1)}, bf16[1,64,512]{2,1,0:T(8,128)(2,1)S(1)}, u32[]{:S(2)}, u32[]{:S(2)}) collective-permute-start(bf16[1,64,512]{2,1,0:T(8,128)(2,1)S(1)} %sum_first_sigma.1.refs_3_), channel_id=1, source_target_pairs={{2,0},{0,2},{3,1},{1,3},{6,4},{4,6},{7,5},{5,7},{10,8},{8,10},{11,... | collective-permute-start | bytes 196616 | tf_op jit(solution)/shard_map/ppermute | solution.py:244
  26.7 4.4 %collective-permute-start.12 = (bf16[1,64,512]{2,1,0:T(8,128)(2,1)S(1)}, bf16[1,64,512]{2,1,0:T(8,128)(2,1)S(1)}, u32[]{:S(2)}, u32[]{:S(2)}) collective-permute-start(bf16[1,64,512]{2,1,0:T(8,128)(2,1)S(1)} %collective-permute-done.7.refs_0_), channel_id=1, source_target_pairs={{2,0},{0,2},{3,1},{1,3},{6,4},{4,6},{7,5},{5,7},{10,8},{8,10},{11,... | collective-permute-start | bytes 196616 | tf_op jit(solution)/shard_map/ppermute | solution.py:244
  27.9 4.3 %collective-permute-start.13 = (bf16[1,64,512]{2,1,0:T(8,128)(2,1)S(1)}, bf16[1,64,512]{2,1,0:T(8,128)(2,1)S(1)}, u32[]{:S(2)}, u32[]{:S(2)}) collective-permute-start(bf16[1,64,512]{2,1,0:T(8,128)(2,1)S(1)} %collective-permute-done.8.refs_1_), channel_id=1, source_target_pairs={{2,0},{0,2},{3,1},{1,3},{6,4},{4,6},{7,5},{5,7},{10,8},{8,10},{11,... | collective-permute-start | bytes 196616 | tf_op jit(solution)/shard_map/ppermute | solution.py:244
  28.8 3.4 %collective-permute-start.10 = (bf16[1,256,512]{2,1,0:T(8,128)(2,1)S(1)}, bf16[1,256,512]{2,1,0:T(8,128)(2,1)S(1)}, u32[]{:S(2)}, u32[]{:S(2)}) collective-permute-start(bf16[1,256,512]{2,1,0:T(8,128)(2,1)S(1)} %place_own_sector.1.sigma_own.own.refs_1_), channel_id=1, source_target_pairs={{1,0},{0,1},{3,2},{2,3},{5,4},{4,5},{7,6},{6,7},{9,8},{8,9},{11,10... | collective-permute-start | bytes 786440 | tf_op jit(solution)/shard_map/ppermute | solution.py:244
  32.2 1.6 %collective-permute-start.16 = (bf16[1,256,512]{2,1,0:T(8,128)(2,1)S(1)}, bf16[1,256,512]{2,1,0:T(8,128)(2,1)S(1)}, u32[]{:S(2)}, u32[]{:S(2)}) collective-permute-start(bf16[1,256,512]{2,1,0:T(8,128)(2,1)S(1)} %place_other_sectors.1.across_own), channel_id=1, source_target_pairs={{1,0},{0,1},{3,2},{2,3},{5,4},{4,5},{7,6},{6,7},{9,8},{8,9},{11,10... | collective-permute-start | bytes 786440 | tf_op jit(solution)/shard_map/ppermute | solution.py:244
  34.9 8.7 %collective-permute-start.17 = (bf16[1,64,512]{2,1,0:T(8,128)(2,1)S(1)}, bf16[1,64,512]{2,1,0:T(8,128)(2,1)S(1)}, u32[]{:S(2)}, u32[]{:S(2)}) collective-permute-start(bf16[1,64,512]{2,1,0:T(8,128)(2,1)S(1)} %get-tuple-element.41), channel_id=1, source_target_pairs={{12,0},{8,4},{4,8},{0,12},{13,1},{9,5},{5,9},{1,13},{14,2},{10,6},... | collective-permute-start | bytes 196616 | tf_op jit(solution)/shard_map/ppermute | solution.py:244
  37.4 6.3 %collective-permute-start.18 = (bf16[1,64,512]{2,1,0:T(8,128)(2,1)S(1)}, bf16[1,64,512]{2,1,0:T(8,128)(2,1)S(1)}, u32[]{:S(2)}, u32[]{:S(2)}) collective-permute-start(bf16[1,64,512]{2,1,0:T(8,128)(2,1)S(1)} %get-tuple-element.42), channel_id=1, source_target_pairs={{8,0},{12,4},{0,8},{4,12},{9,1},{13,5},{1,9},{5,13},{10,2},{14,6},... | collective-permute-start | bytes 196616 | tf_op jit(solution)/shard_map/ppermute | solution.py:244
  37.4 6.3 %collective-permute-start.19 = (bf16[1,64,512]{2,1,0:T(8,128)(2,1)S(1)}, bf16[1,64,512]{2,1,0:T(8,128)(2,1)S(1)}, u32[]{:S(2)}, u32[]{:S(2)}) collective-permute-start(bf16[1,64,512]{2,1,0:T(8,128)(2,1)S(1)} %get-tuple-element.43), channel_id=1, source_target_pairs={{4,0},{0,4},{12,8},{8,12},{5,1},{1,5},{13,9},{9,13},{6,2},{2,6},{1... | collective-permute-start | bytes 196616 | tf_op jit(solution)/shard_map/ppermute | solution.py:244
  39.9 3.8 %collective-permute-start.11 = (f32[3,8,128]{2,1,0:T(8,128)S(1)}, f32[3,8,128]{2,1,0:T(8,128)S(1)}, u32[]{:S(2)}, u32[]{:S(2)}) collective-permute-start(f32[3,8,128]{2,1,0:T(8,128)S(1)} %sums_for_rayleigh.1.refs_0_.refs_5_), channel_id=1, source_target_pairs={{2,0},{0,2},{3,1},{1,3},{6,4},{4,6},{7,5},{5,7},{10,8},{8,10},{11,... | collective-permute-start | bytes 36872 | tf_op jit(solution)/shard_map/ppermute | solution.py:244
  43.7 6.7 %collective-permute-start.20 = (bf16[1,64,512]{2,1,0:T(8,128)(2,1)S(1)}, bf16[1,64,512]{2,1,0:T(8,128)(2,1)S(1)}, u32[]{:S(2)}, u32[]{:S(2)}) collective-permute-start(bf16[1,64,512]{2,1,0:T(8,128)(2,1)S(1)} %sum_second_sigma.1.refs_5_), channel_id=1, source_target_pairs={{12,0},{8,4},{4,8},{0,12},{13,1},{9,5},{5,9},{1,13},{14,2},{10,6},... | collective-permute-start | bytes 196616 | tf_op jit(solution)/shard_map/ppermute | solution.py:244
  46.3 6.2 %collective-permute-start.21 = (bf16[1,64,512]{2,1,0:T(8,128)(2,1)S(1)}, bf16[1,64,512]{2,1,0:T(8,128)(2,1)S(1)}, u32[]{:S(2)}, u32[]{:S(2)}) collective-permute-start(bf16[1,64,512]{2,1,0:T(8,128)(2,1)S(1)} %sum_second_sigma.1.refs_5_), channel_id=1, source_target_pairs={{8,0},{12,4},{0,8},{4,12},{9,1},{13,5},{1,9},{5,13},{10,2},{14,6},... | collective-permute-start | bytes 196616 | tf_op jit(solution)/shard_map/ppermute | solution.py:244
  46.3 6.2 %collective-permute-start.22 = (bf16[1,64,512]{2,1,0:T(8,128)(2,1)S(1)}, bf16[1,64,512]{2,1,0:T(8,128)(2,1)S(1)}, u32[]{:S(2)}, u32[]{:S(2)}) collective-permute-start(bf16[1,64,512]{2,1,0:T(8,128)(2,1)S(1)} %sum_second_sigma.1.refs_5_), channel_id=1, source_target_pairs={{4,0},{0,4},{12,8},{8,12},{5,1},{1,5},{13,9},{9,13},{6,2},{2,6},{1... | collective-permute-start | bytes 196616 | tf_op jit(solution)/shard_map/ppermute | solution.py:244

commit v20 on v19

--- a/solution.py
+++ b/solution.py
@@ -345,27 +345,29 @@
     received += [partner(rest[spot], {"ops": spot[0][0], "sec": spot[1]}) for spot in order]
     first_share = summed("sum_first_sigma", *[(piece, 1) for piece in met], *received, live=live)
     along_ops = {along: partner(first_share, {"ops": along}) for along in send_order}
-    sigma_own = call(
-        lambda *refs: place_kernel([(along, 0) for along in send_order], *refs),
-        "place_own_sector",
-        shape(1, rows, columns),
-        [],
-        *along_ops.values(),
-    )
-    sigma_other = partner(sigma_own, {"rep": 1})
     spots = [(along, across) for along in send_order for across in range(1, sectors)]
-    pieces = [
-        partner(first_share, {"ops": along, "sec": across})
+    pieces = {
+        (along, across): partner(first_share, {"ops": along, "sec": across})
         if along < 2
         else partner(along_ops[along], {"sec": across})
         for along, across in spots
-    ]
+    }
+    ahead = [pieces[along, across] for along, across in spots if along < 2]
+    sigma_own = call(
+        lambda *refs: place_kernel([(along, 0) for along in send_order], *refs[len(ahead) :]),
+        "place_own_sector",
+        shape(1, rows, columns),
+        [],
+        *ahead,
+        *along_ops.values(),
+    )
+    sigma_other = partner(sigma_own, {"rep": 1})
     across_own = call(
         lambda *refs: place_kernel([(along, across - 1) for along, across in spots], *refs),
         "place_other_sectors",
         shape(sectors - 1, rows, columns),
         [],
-        *pieces,
+        *pieces.values(),
     )
     across_other = partner(across_own, {"rep": 1})
 

time: 53.5 us -> 53.4 us (level)
  transfers between devices with their start and end apart: 23 -> 23, of which waited for: 12 -> 10; matrix products, arithmetic and copies ran while one was open for 0% -> 0% of each run, Pallas kernels for 10% -> 10%
where the time goes in v20:
time: 53.4 us; the launch traced here: 53.2 us
  starting transfers between devices  31.7 us (59%)
  waiting for transfers between devices  11.5 us (22%)
  Pallas kernels  9.11 us (17%)
  between operations  0.85 us (2%)
    ppermute x23, starting transfers between devices, partner(): return lax.ppermute(value, axes, pairs)  31.7 us
    ppermute x23, waiting for transfers between devices, partner(): return lax.ppermute(value, axes, pairs)  11.5 us
    pallas_call x14, Pallas kernels, call(): pl.pallas_call(kernel, out_shape=out_shape, in_specs=list(in_specs) + [in...  9.11 us
  transfers between devices with their start and end apart: 23, of which 10 were waited for; matrix products, arithmetic and copies ran while one was open for 0% of the time, Pallas kernels for 10%

profile of v20, /device:TPU:0, one launch (start us, length us, event | category | flops | bytes accessed | tf_op | source)
XLA Modules:
  0.0 53.2 jit_solution(14306273327770416871)
XLA Ops:
  0.6 0.0 copy-start.1
  0.6 0.0 copy-start.3
  0.7 0.0 copy-start.2
  0.7 0.0 copy-start.4
  0.7 0.0 copy-start
  0.7 0.5 collective-permute-start
  1.2 1.4 %load_operators.1 = (bf16[4,256,256]{2,1,0:T(8,128)(2,1)S(1)}, bf16[4,256,256]{2,1,0:T(8,128)(2,1)S(1)}) custom-call(bf16[4,512,512]{2,1,0:T(8,128)(2,1)} %left_ref.1), custom_call_target="tpu_custom_call" | custom-call | tf_op jit(solution)/shard_map/load_operators/pallas_call | solution.py:262
  2.6 0.0 copy-done.1
  2.6 0.0 copy-done.3
  2.7 0.2 tables_for_first_sigma.1
  2.9 0.0 collective-permute-done.refs_6_
  2.9 0.0 copy-done
  2.9 1.6 %first_sigma_terms.1 = (bf16[256,512]{1,0:T(8,128)(2,1)S(1)}, f32[2,64,512]{2,1,0:T(8,128)S(1)}, bf16[2,64,512]{2,1,0:T(8,128)(2,1)S(1)}, bf16[1,64,512]{2,1,0:T...) custom-call(s32[2,2]{1,0:T(2,128)S(1)} %copy-done.3, ...), custom_call_target="tpu_custom_call" | custom-call | tf_op jit(solution)/shard_map/first_sigma_terms/pallas_call | solution.py:262
  4.5 2.8 %collective-permute-start.1 = (bf16[2,64,512]{2,1,0:T(8,128)(2,1)S(1)}, bf16[2,64,512]{2,1,0:T(8,128)(2,1)S(1)}, u32[]{:S(2)}, u32[]{:S(2)}) collective-permute-start(bf16[2,64,512]{2,1,0:T(8,128)(2,1)S(1)} %get-tuple-element.28), channel_id=1, source_target_pairs={{2,0},{0,2},{3,1},{1,3},{6,4},{4,6},{7,5},{5,7},{10,8},{8,10},{11,... | collective-permute-start | bytes 393224 | tf_op jit(solution)/shard_map/ppermute | solution.py:244
  7.3 2.6 %collective-permute-start.3 = (bf16[1,64,512]{2,1,0:T(8,128)(2,1)S(1)}, bf16[1,64,512]{2,1,0:T(8,128)(2,1)S(1)}, u32[]{:S(2)}, u32[]{:S(2)}) collective-permute-start(bf16[1,64,512]{2,1,0:T(8,128)(2,1)S(1)} %get-tuple-element.29), channel_id=1, source_target_pairs={{8,0},{12,4},{0,8},{4,12},{9,1},{13,5},{1,9},{5,13},{10,2},{14,6},... | collective-permute-start | bytes 196616 | tf_op jit(solution)/shard_map/ppermute | solution.py:244
  9.9 1.6 %collective-permute-start.4 = (bf16[1,64,512]{2,1,0:T(8,128)(2,1)S(1)}, bf16[1,64,512]{2,1,0:T(8,128)(2,1)S(1)}, u32[]{:S(2)}, u32[]{:S(2)}) collective-permute-start(bf16[1,64,512]{2,1,0:T(8,128)(2,1)S(1)} %get-tuple-element.30), channel_id=1, source_target_pairs={{4,0},{0,4},{12,8},{8,12},{5,1},{1,5},{13,9},{9,13},{6,2},{2,6},{1... | collective-permute-start | bytes 196616 | tf_op jit(solution)/shard_map/ppermute | solution.py:244
  11.5 0.3 collective-permute-start.5
  11.8 1.4 %collective-permute-start.6 = (bf16[1,64,512]{2,1,0:T(8,128)(2,1)S(1)}, bf16[1,64,512]{2,1,0:T(8,128)(2,1)S(1)}, u32[]{:S(2)}, u32[]{:S(2)}) collective-permute-start(bf16[1,64,512]{2,1,0:T(8,128)(2,1)S(1)} %get-tuple-element.32), channel_id=1, source_target_pairs={{6,0},{4,2},{2,4},{0,6},{14,8},{12,10},{10,12},{8,14},{7,1},{5,3},... | collective-permute-start | bytes 196616 | tf_op jit(solution)/shard_map/ppermute | solution.py:244
  13.1 0.0 collective-permute-done.1.refs_1_
  13.2 3.7 %collective-permute-start.2 = (bf16[1,64,512]{2,1,0:T(8,128)(2,1)S(1)}, bf16[1,64,512]{2,1,0:T(8,128)(2,1)S(1)}, u32[]{:S(2)}, u32[]{:S(2)}) collective-permute-start(bf16[1,64,512]{2,1,0:T(8,128)(2,1)S(1)} %sum_far_share.1), channel_id=1, source_target_pairs={{12,0},{8,4},{4,8},{0,12},{13,1},{9,5},{5,9},{1,13},{14,2},{10,6},... | collective-permute-start | bytes 196616 | tf_op jit(solution)/shard_map/ppermute | solution.py:244
  16.8 0.8 %tables_for_second_sigma.1 = (f32[4,2,8,128]{3,2,1,0:T(8,128)S(1)}, f32[256,512]{1,0:T(8,128)S(1)}) custom-call(s32[2,2]{1,0:T(2,128)S(1)} %copy-done.3, s32[4,2,8]{2,1,0:T(2,128)S(1)} %bitcast.2, f32[4,8]{1,0:T(4,128)S(1)} %copy-done.4, bf16[256,512]{1,0:T(8,128)(2,1)S(1)} %get-tuple-element.33._.wave_other), custom_call_target="tpu_custom_call" | custom-call | tf_op jit(solution)/shard_map/tables_for_second_sigma/pallas_call | solution.py:262
  17.6 0.0 collective-permute-done.3.refs_3_
  17.7 0.0 collective-permute-done.4.refs_4_
  17.7 2.2 %collective-permute-done.5.refs_5_ = bf16[1,64,512]{2,1,0:T(8,128)(2,1)S(1)} collective-permute-done((bf16[1,64,512]{2,1,0:T(8,128)(2,1)S(1)}, bf16[1,64,512]{2,1,0:T(8,128)(2,1)S(1)}, u32[]{:S(2)}, u32[]{:S(2)}) %collective-permute-start.5) | collective-permute-done | bytes 65568 | tf_op jit(solution)/shard_map/ppermute | solution.py:244
  19.9 0.0 collective-permute-done.6.refs_6_
  19.9 0.0 collective-permute-done.2.refs_2_
  19.9 0.1 sum_first_sigma.1.refs_5_
  20.0 1.1 %collective-permute-start.9 = (bf16[1,64,512]{2,1,0:T(8,128)(2,1)S(1)}, bf16[1,64,512]{2,1,0:T(8,128)(2,1)S(1)}, u32[]{:S(2)}, u32[]{:S(2)}) collective-permute-start(bf16[1,64,512]{2,1,0:T(8,128)(2,1)S(1)} %sum_first_sigma.1.refs_5_), channel_id=1, source_target_pairs={{8,0},{12,4},{0,8},{4,12},{9,1},{13,5},{1,9},{5,13},{10,2},{14,6},... | collective-permute-start | bytes 196616 | tf_op jit(solution)/shard_map/ppermute | solution.py:244
  21.0 2.1 %collective-permute-start.10 = (bf16[1,64,512]{2,1,0:T(8,128)(2,1)S(1)}, bf16[1,64,512]{2,1,0:T(8,128)(2,1)S(1)}, u32[]{:S(2)}, u32[]{:S(2)}) collective-permute-start(bf16[1,64,512]{2,1,0:T(8,128)(2,1)S(1)} %sum_first_sigma.1.refs_5_), channel_id=1, source_target_pairs={{12,0},{8,4},{4,8},{0,12},{13,1},{9,5},{5,9},{1,13},{14,2},{10,6},... | collective-permute-start | bytes 196616 | tf_op jit(solution)/shard_map/ppermute | solution.py:244
  23.1 0.5 collective-permute-start.7
  23.6 1.5 %collective-permute-start.8 = (bf16[1,64,512]{2,1,0:T(8,128)(2,1)S(1)}, bf16[1,64,512]{2,1,0:T(8,128)(2,1)S(1)}, u32[]{:S(2)}, u32[]{:S(2)}) collective-permute-start(bf16[1,64,512]{2,1,0:T(8,128)(2,1)S(1)} %sum_first_sigma.1.refs_5_), channel_id=1, source_target_pairs={{2,0},{0,2},{3,1},{1,3},{6,4},{4,6},{7,5},{5,7},{10,8},{8,10},{11,... | collective-permute-start | bytes 196616 | tf_op jit(solution)/shard_map/ppermute | solution.py:244
  25.1 1.5 %collective-permute-start.11 = (bf16[1,64,512]{2,1,0:T(8,128)(2,1)S(1)}, bf16[1,64,512]{2,1,0:T(8,128)(2,1)S(1)}, u32[]{:S(2)}, u32[]{:S(2)}) collective-permute-start(bf16[1,64,512]{2,1,0:T(8,128)(2,1)S(1)} %sum_first_sigma.1.refs_5_), channel_id=1, source_target_pairs={{4,0},{0,4},{12,8},{8,12},{5,1},{1,5},{13,9},{9,13},{6,2},{2,6},{1... | collective-permute-start | bytes 196616 | tf_op jit(solution)/shard_map/ppermute | solution.py:244
  26.6 0.2 collective-permute-done.9.refs_2_
  26.8 0.9 %collective-permute-start.14 = (bf16[1,64,512]{2,1,0:T(8,128)(2,1)S(1)}, bf16[1,64,512]{2,1,0:T(8,128)(2,1)S(1)}, u32[]{:S(2)}, u32[]{:S(2)}) collective-permute-start(bf16[1,64,512]{2,1,0:T(8,128)(2,1)S(1)} %collective-permute-done.9.refs_2_), channel_id=1, source_target_pairs={{2,0},{0,2},{3,1},{1,3},{6,4},{4,6},{7,5},{5,7},{10,8},{8,10},{11,... | collective-permute-start | bytes 196616 | tf_op jit(solution)/shard_map/ppermute | solution.py:244
  27.7 0.0 collective-permute-done.10.refs_3_
  27.7 1.1 %collective-permute-start.15 = (bf16[1,64,512]{2,1,0:T(8,128)(2,1)S(1)}, bf16[1,64,512]{2,1,0:T(8,128)(2,1)S(1)}, u32[]{:S(2)}, u32[]{:S(2)}) collective-permute-start(bf16[1,64,512]{2,1,0:T(8,128)(2,1)S(1)} %collective-permute-done.10.refs_3_), channel_id=1, source_target_pairs={{2,0},{0,2},{3,1},{1,3},{6,4},{4,6},{7,5},{5,7},{10,8},{8,10},{11,... | collective-permute-start | bytes 196616 | tf_op jit(solution)/shard_map/ppermute | solution.py:244
  28.8 0.0 collective-permute-done.7.refs_0_.refs_2_
  28.8 0.0 collective-permute-done.8.refs_1_.refs_3_
  28.8 0.5 collective-permute-done.11.refs_4_
  29.4 0.1 collective-permute-start.12
  29.4 1.6 %collective-permute-done.14.refs_0_ = bf16[1,64,512]{2,1,0:T(8,128)(2,1)S(1)} collective-permute-done((bf16[1,64,512]{2,1,0:T(8,128)(2,1)S(1)}, bf16[1,64,512]{2,1,0:T(8,128)(2,1)S(1)}, u32[]{:S(2)}, u32[]{:S(2)}) %collective-permute-start.14) | collective-permute-done | bytes 65568 | tf_op jit(solution)/shard_map/ppermute | solution.py:244
  31.1 0.9 %collective-permute-done.15.refs_1_ = bf16[1,64,512]{2,1,0:T(8,128)(2,1)S(1)} collective-permute-done((bf16[1,64,512]{2,1,0:T(8,128)(2,1)S(1)}, bf16[1,64,512]{2,1,0:T(8,128)(2,1)S(1)}, u32[]{:S(2)}, u32[]{:S(2)}) %collective-permute-start.15) | collective-permute-done | bytes 65568 | tf_op jit(solution)/shard_map/ppermute | solution.py:244
  32.0 0.1 collective-permute-start.16
  32.1 0.0 collective-permute-done.12.sigma_other.other
  32.1 1.0 %left_products.1 = (f32[4,256,512]{2,1,0:T(8,128)S(1)}, f32[1,4,256,512]{3,2,1,0:T(8,128)S(1)}) custom-call(bf16[4,256,256]{2,1,0:T(8,128)(2,1)S(1)} %get-tuple-element.23._.refs_2_.left_own, bf16[4,256,256]{2,1,0:T(8,128)(2,1)S(1)} %get-tuple-element.26.refs_3_.left_other, bf16[1,256,512]{2,1,0:T(8,128)(2,1)S(1)} %place_own_sector.1.sigma_own.own.refs_1_, ...), custom_call_target="tpu_custom_call" | custom-call | tf_op jit(solution)/shard_map/left_products/pallas_call | solution.py:262
  33.1 0.5 %collective-permute-done.16.other = bf16[1,256,512]{2,1,0:T(8,128)(2,1)S(1)} collective-permute-done((bf16[1,256,512]{2,1,0:T(8,128)(2,1)S(1)}, bf16[1,256,512]{2,1,0:T(8,128)(2,1)S(1)}, u32[]{:S(2)}, u32[]{:S(2)}) %collective-permute-start.16) | collective-permute-done | bytes 262176 | tf_op jit(solution)/shard_map/ppermute | solution.py:244
  33.6 1.1 %second_sigma_terms.1 = (f32[1,64,512]{2,1,0:T(8,128)S(1)}, bf16[1,64,512]{2,1,0:T(8,128)(2,1)S(1)}, bf16[1,64,512]{2,1,0:T(8,128)(2,1)S(1)}, bf16[1,64,512]{2,1,0:T(8,128)(2,1)S(1)}) custom-call(f32[4,2,8,128]{3,2,1,0:T(8,128)S(1)} %get-tuple-element.37.mixing, bf16[4,256,256]{2,1,0:T(8,128)(2,1)S(1)} %get-tuple-element.26.refs_3_.left_other, ...), custom_call_target="tpu_custom_call" | custom-call | tf_op jit(solution)/shard_map/second_sigma_terms/pallas_call | solution.py:262
  34.7 2.3 %collective-permute-start.17 = (bf16[1,64,512]{2,1,0:T(8,128)(2,1)S(1)}, bf16[1,64,512]{2,1,0:T(8,128)(2,1)S(1)}, u32[]{:S(2)}, u32[]{:S(2)}) collective-permute-start(bf16[1,64,512]{2,1,0:T(8,128)(2,1)S(1)} %get-tuple-element.41), channel_id=1, source_target_pairs={{12,0},{8,4},{4,8},{0,12},{13,1},{9,5},{5,9},{1,13},{14,2},{10,6},... | collective-permute-start | bytes 196616 | tf_op jit(solution)/shard_map/ppermute | solution.py:244
  37.0 0.1 collective-permute-start.18
  37.1 2.1 %collective-permute-start.19 = (bf16[1,64,512]{2,1,0:T(8,128)(2,1)S(1)}, bf16[1,64,512]{2,1,0:T(8,128)(2,1)S(1)}, u32[]{:S(2)}, u32[]{:S(2)}) collective-permute-start(bf16[1,64,512]{2,1,0:T(8,128)(2,1)S(1)} %get-tuple-element.43), channel_id=1, source_target_pairs={{4,0},{0,4},{12,8},{8,12},{5,1},{1,5},{13,9},{9,13},{6,2},{2,6},{1... | collective-permute-start | bytes 196616 | tf_op jit(solution)/shard_map/ppermute | solution.py:244
  39.2 0.5 sums_for_rayleigh.1.refs_0_.refs_5_
  39.7 1.2 %collective-permute-start.13 = (f32[3,8,128]{2,1,0:T(8,128)S(1)}, f32[3,8,128]{2,1,0:T(8,128)S(1)}, u32[]{:S(2)}, u32[]{:S(2)}) collective-permute-start(f32[3,8,128]{2,1,0:T(8,128)S(1)} %sums_for_rayleigh.1.refs_0_.refs_5_), channel_id=1, source_target_pairs={{2,0},{0,2},{3,1},{1,3},{6,4},{4,6},{7,5},{5,7},{10,8},{8,10},{11,... | collective-permute-start | bytes 36872 | tf_op jit(solution)/shard_map/ppermute | solution.py:244
  40.9 2.6 %collective-permute-done.13.refs_1_.refs_6_ = f32[3,8,128]{2,1,0:T(8,128)S(1)} collective-permute-done((f32[3,8,128]{2,1,0:T(8,128)S(1)}, f32[3,8,128]{2,1,0:T(8,128)S(1)}, u32[]{:S(2)}, u32[]{:S(2)}) %collective-permute-start.13) | collective-permute-done | bytes 12320 | tf_op jit(solution)/shard_map/ppermute | solution.py:244
  43.5 0.0 collective-permute-done.17.refs_1_
  43.5 0.1 collective-permute-done.18.refs_2_
  43.6 0.0 collective-permute-done.19.refs_3_
  43.6 2.3 %collective-permute-start.20 = (bf16[1,64,512]{2,1,0:T(8,128)(2,1)S(1)}, bf16[1,64,512]{2,1,0:T(8,128)(2,1)S(1)}, u32[]{:S(2)}, u32[]{:S(2)}) collective-permute-start(bf16[1,64,512]{2,1,0:T(8,128)(2,1)S(1)} %sum_second_sigma.1.refs_5_), channel_id=1, source_target_pairs={{12,0},{8,4},{4,8},{0,12},{13,1},{9,5},{5,9},{1,13},{14,2},{10,6},... | collective-permute-start | bytes 196616 | tf_op jit(solution)/shard_map/ppermute | solution.py:244
  45.9 0.0 collective-permute-start.21
  45.9 2.2 %collective-permute-start.22 = (bf16[1,64,512]{2,1,0:T(8,128)(2,1)S(1)}, bf16[1,64,512]{2,1,0:T(8,128)(2,1)S(1)}, u32[]{:S(2)}, u32[]{:S(2)}) collective-permute-start(bf16[1,64,512]{2,1,0:T(8,128)(2,1)S(1)} %sum_second_sigma.1.refs_5_), channel_id=1, source_target_pairs={{4,0},{0,4},{12,8},{8,12},{5,1},{1,5},{13,9},{9,13},{6,2},{2,6},{1... | collective-permute-start | bytes 196616 | tf_op jit(solution)/shard_map/ppermute | solution.py:244
  48.1 1.4 %second_wave.1 = (bf16[1,256,512]{2,1,0:T(8,128)(2,1)}, f32[2,8,128]{2,1,0:T(8,128)S(1)}) custom-call(s32[2,2]{1,0:T(2,128)S(1)} %copy-done.3, bf16[256,512]{1,0:T(8,128)(2,1)S(1)} %get-tuple-element.24.refs_5_.wave_own, bf16[1,256,512]{2,1,0:T(8,128)(2,1)S(1)} %place_own_sector.1.sigma_own.own.refs_1_, f32[3,8,128]{2,1,0:T(8,128)S(1)} %sums_for_rayleigh.1.refs_0_.refs_5_, ...), custom_call_target="tpu_custom_call" | custom-call | tf_op jit(solution)/shard_map/second_wave/pallas_call | solution.py:262
  49.5 0.8 %collective-permute-done.20.refs_2_ = bf16[1,64,512]{2,1,0:T(8,128)(2,1)S(1)} collective-permute-done((bf16[1,64,512]{2,1,0:T(8,128)(2,1)S(1)}, bf16[1,64,512]{2,1,0:T(8,128)(2,1)S(1)}, u32[]{:S(2)}, u32[]{:S(2)}) %collective-permute-start.20) | collective-permute-done | bytes 65568 | tf_op jit(solution)/shard_map/ppermute | solution.py:244
  50.4 2.0 %collective-permute-done.21.refs_3_ = bf16[1,64,512]{2,1,0:T(8,128)(2,1)S(1)} collective-permute-done((bf16[1,64,512]{2,1,0:T(8,128)(2,1)S(1)}, bf16[1,64,512]{2,1,0:T(8,128)(2,1)S(1)}, u32[]{:S(2)}, u32[]{:S(2)}) %collective-permute-start.21) | collective-permute-done | bytes 65568 | tf_op jit(solution)/shard_map/ppermute | solution.py:244
  52.3 0.0 collective-permute-done.22.refs_4_
  52.3 0.9 %join_second_sigma.1 = f32[1,256,512]{2,1,0:T(8,128)} custom-call(f32[2,8,128]{2,1,0:T(8,128)S(1)} %get-tuple-element.36.refs_0_, bf16[1,256,512]{2,1,0:T(8,128)(2,1)S(1)} %place_own_sector.1.sigma_own.own.refs_1_, bf16[1,64,512]{2,1,0:T(8,128)(2,1)S(1)} %collective-permute-done.20.refs_2_, bf16[1,64,512]{2,1,0:T(8,128)(2,1)S(1)} %collective-permute-done.21.refs_3_, ...), custom_call_target="tpu_custom_call" | custom-call | tf_op jit(solution)/shard_map/join_second_sigma/pallas_call | solution.py:262
  (6 shorter events, 0.1 us)
Async XLA Ops:
  0.6 2.0 %copy-start.1 = (bf16[1,256,512]{2,1,0:T(8,128)(2,1)S(1)}, bf16[1,256,512]{2,1,0:T(8,128)(2,1)}, u32[]{:S(2)}) copy-start(bf16[1,256,512]{2,1,0:T(8,128)(2,1)} %wave.1) | copy-start | bytes 786436
  0.6 2.0 %copy-start.3 = (s32[2,2]{1,0:T(2,128)S(1)}, s32[2,2]{1,0:T(2,128)}, u32[]{:S(2)}) copy-start(s32[2,2]{1,0:T(2,128)} %sizes_ref.3) | copy-start | bytes 52
  0.7 2.0 %copy-start.2 = (s32[4,8,2]{1,2,0:T(2,128)S(1)}, s32[4,8,2]{1,2,0:T(2,128)}, u32[]{:S(2)}) copy-start(s32[4,8,2]{1,2,0:T(2,128)} %param.10) | copy-start | bytes 772
  0.7 2.0 %copy-start.4 = (f32[4,8]{1,0:T(4,128)S(1)}, f32[4,8]{1,0:T(4,128)}, u32[]{:S(2)}) copy-start(f32[4,8]{1,0:T(4,128)} %weights_ref.1) | copy-start | bytes 388
  0.7 2.2 %copy-start = (bf16[4,512,512]{2,1,0:T(8,128)(2,1)S(1)}, bf16[4,512,512]{2,1,0:T(8,128)(2,1)}, u32[]{:S(2)}) copy-start(bf16[4,512,512]{2,1,0:T(8,128)(2,1)} %right.1) | copy-start | bytes 6291460
  0.7 2.2 %collective-permute-start = (bf16[1,256,512]{2,1,0:T(8,128)(2,1)}, bf16[1,256,512]{2,1,0:T(8,128)(2,1)S(1)}, u32[]{:S(2)}, u32[]{:S(2)}) collective-permute-start(bf16[1,256,512]{2,1,0:T(8,128)(2,1)} %wave.1), channel_id=1, source_target_pairs={{1,0},{0,1},{3,2},{2,3},{5,4},{4,5},{7,6},{6,7},{9,8},{8,9},{11,10... | collective-permute-start | bytes 786440 | tf_op jit(solution)/shard_map/ppermute | solution.py:244
  4.5 8.6 %collective-permute-start.1 = (bf16[2,64,512]{2,1,0:T(8,128)(2,1)S(1)}, bf16[2,64,512]{2,1,0:T(8,128)(2,1)S(1)}, u32[]{:S(2)}, u32[]{:S(2)}) collective-permute-start(bf16[2,64,512]{2,1,0:T(8,128)(2,1)S(1)} %get-tuple-element.28), channel_id=1, source_target_pairs={{2,0},{0,2},{3,1},{1,3},{6,4},{4,6},{7,5},{5,7},{10,8},{8,10},{11,... | collective-permute-start | bytes 393224 | tf_op jit(solution)/shard_map/ppermute | solution.py:244
  7.3 10.4 %collective-permute-start.3 = (bf16[1,64,512]{2,1,0:T(8,128)(2,1)S(1)}, bf16[1,64,512]{2,1,0:T(8,128)(2,1)S(1)}, u32[]{:S(2)}, u32[]{:S(2)}) collective-permute-start(bf16[1,64,512]{2,1,0:T(8,128)(2,1)S(1)} %get-tuple-element.29), channel_id=1, source_target_pairs={{8,0},{12,4},{0,8},{4,12},{9,1},{13,5},{1,9},{5,13},{10,2},{14,6},... | collective-permute-start | bytes 196616 | tf_op jit(solution)/shard_map/ppermute | solution.py:244
  9.9 7.8 %collective-permute-start.4 = (bf16[1,64,512]{2,1,0:T(8,128)(2,1)S(1)}, bf16[1,64,512]{2,1,0:T(8,128)(2,1)S(1)}, u32[]{:S(2)}, u32[]{:S(2)}) collective-permute-start(bf16[1,64,512]{2,1,0:T(8,128)(2,1)S(1)} %get-tuple-element.30), channel_id=1, source_target_pairs={{4,0},{0,4},{12,8},{8,12},{5,1},{1,5},{13,9},{9,13},{6,2},{2,6},{1... | collective-permute-start | bytes 196616 | tf_op jit(solution)/shard_map/ppermute | solution.py:244
  11.5 8.4 %collective-permute-start.5 = (bf16[1,64,512]{2,1,0:T(8,128)(2,1)S(1)}, bf16[1,64,512]{2,1,0:T(8,128)(2,1)S(1)}, u32[]{:S(2)}, u32[]{:S(2)}) collective-permute-start(bf16[1,64,512]{2,1,0:T(8,128)(2,1)S(1)} %get-tuple-element.31), channel_id=1, source_target_pairs={{10,0},{8,2},{14,4},{12,6},{2,8},{0,10},{6,12},{4,14},{11,1},{9,3}... | collective-permute-start | bytes 196616 | tf_op jit(solution)/shard_map/ppermute | solution.py:244
  11.8 8.1 %collective-permute-start.6 = (bf16[1,64,512]{2,1,0:T(8,128)(2,1)S(1)}, bf16[1,64,512]{2,1,0:T(8,128)(2,1)S(1)}, u32[]{:S(2)}, u32[]{:S(2)}) collective-permute-start(bf16[1,64,512]{2,1,0:T(8,128)(2,1)S(1)} %get-tuple-element.32), channel_id=1, source_target_pairs={{6,0},{4,2},{2,4},{0,6},{14,8},{12,10},{10,12},{8,14},{7,1},{5,3},... | collective-permute-start | bytes 196616 | tf_op jit(solution)/shard_map/ppermute | solution.py:244
  13.2 6.7 %collective-permute-start.2 = (bf16[1,64,512]{2,1,0:T(8,128)(2,1)S(1)}, bf16[1,64,512]{2,1,0:T(8,128)(2,1)S(1)}, u32[]{:S(2)}, u32[]{:S(2)}) collective-permute-start(bf16[1,64,512]{2,1,0:T(8,128)(2,1)S(1)} %sum_far_share.1), channel_id=1, source_target_pairs={{12,0},{8,4},{4,8},{0,12},{13,1},{9,5},{5,9},{1,13},{14,2},{10,6},... | collective-permute-start | bytes 196616 | tf_op jit(solution)/shard_map/ppermute | solution.py:244
  20.0 6.8 %collective-permute-start.9 = (bf16[1,64,512]{2,1,0:T(8,128)(2,1)S(1)}, bf16[1,64,512]{2,1,0:T(8,128)(2,1)S(1)}, u32[]{:S(2)}, u32[]{:S(2)}) collective-permute-start(bf16[1,64,512]{2,1,0:T(8,128)(2,1)S(1)} %sum_first_sigma.1.refs_5_), channel_id=1, source_target_pairs={{8,0},{12,4},{0,8},{4,12},{9,1},{13,5},{1,9},{5,13},{10,2},{14,6},... | collective-permute-start | bytes 196616 | tf_op jit(solution)/shard_map/ppermute | solution.py:244
  21.0 6.7 %collective-permute-start.10 = (bf16[1,64,512]{2,1,0:T(8,128)(2,1)S(1)}, bf16[1,64,512]{2,1,0:T(8,128)(2,1)S(1)}, u32[]{:S(2)}, u32[]{:S(2)}) collective-permute-start(bf16[1,64,512]{2,1,0:T(8,128)(2,1)S(1)} %sum_first_sigma.1.refs_5_), channel_id=1, source_target_pairs={{12,0},{8,4},{4,8},{0,12},{13,1},{9,5},{5,9},{1,13},{14,2},{10,6},... | collective-permute-start | bytes 196616 | tf_op jit(solution)/shard_map/ppermute | solution.py:244
  23.1 5.7 %collective-permute-start.7 = (bf16[1,64,512]{2,1,0:T(8,128)(2,1)S(1)}, bf16[1,64,512]{2,1,0:T(8,128)(2,1)S(1)}, u32[]{:S(2)}, u32[]{:S(2)}) collective-permute-start(bf16[1,64,512]{2,1,0:T(8,128)(2,1)S(1)} %sum_first_sigma.1.refs_5_), channel_id=1, source_target_pairs={{6,0},{4,2},{2,4},{0,6},{14,8},{12,10},{10,12},{8,14},{7,1},{5,3},... | collective-permute-start | bytes 196616 | tf_op jit(solution)/shard_map/ppermute | solution.py:244
  23.6 5.3 %collective-permute-start.8 = (bf16[1,64,512]{2,1,0:T(8,128)(2,1)S(1)}, bf16[1,64,512]{2,1,0:T(8,128)(2,1)S(1)}, u32[]{:S(2)}, u32[]{:S(2)}) collective-permute-start(bf16[1,64,512]{2,1,0:T(8,128)(2,1)S(1)} %sum_first_sigma.1.refs_5_), channel_id=1, source_target_pairs={{2,0},{0,2},{3,1},{1,3},{6,4},{4,6},{7,5},{5,7},{10,8},{8,10},{11,... | collective-permute-start | bytes 196616 | tf_op jit(solution)/shard_map/ppermute | solution.py:244
  25.1 4.3 %collective-permute-start.11 = (bf16[1,64,512]{2,1,0:T(8,128)(2,1)S(1)}, bf16[1,64,512]{2,1,0:T(8,128)(2,1)S(1)}, u32[]{:S(2)}, u32[]{:S(2)}) collective-permute-start(bf16[1,64,512]{2,1,0:T(8,128)(2,1)S(1)} %sum_first_sigma.1.refs_5_), channel_id=1, source_target_pairs={{4,0},{0,4},{12,8},{8,12},{5,1},{1,5},{13,9},{9,13},{6,2},{2,6},{1... | collective-permute-start | bytes 196616 | tf_op jit(solution)/shard_map/ppermute | solution.py:244
  26.8 4.3 %collective-permute-start.14 = (bf16[1,64,512]{2,1,0:T(8,128)(2,1)S(1)}, bf16[1,64,512]{2,1,0:T(8,128)(2,1)S(1)}, u32[]{:S(2)}, u32[]{:S(2)}) collective-permute-start(bf16[1,64,512]{2,1,0:T(8,128)(2,1)S(1)} %collective-permute-done.9.refs_2_), channel_id=1, source_target_pairs={{2,0},{0,2},{3,1},{1,3},{6,4},{4,6},{7,5},{5,7},{10,8},{8,10},{11,... | collective-permute-start | bytes 196616 | tf_op jit(solution)/shard_map/ppermute | solution.py:244
  27.7 4.3 %collective-permute-start.15 = (bf16[1,64,512]{2,1,0:T(8,128)(2,1)S(1)}, bf16[1,64,512]{2,1,0:T(8,128)(2,1)S(1)}, u32[]{:S(2)}, u32[]{:S(2)}) collective-permute-start(bf16[1,64,512]{2,1,0:T(8,128)(2,1)S(1)} %collective-permute-done.10.refs_3_), channel_id=1, source_target_pairs={{2,0},{0,2},{3,1},{1,3},{6,4},{4,6},{7,5},{5,7},{10,8},{8,10},{11,... | collective-permute-start | bytes 196616 | tf_op jit(solution)/shard_map/ppermute | solution.py:244
  29.4 2.7 %collective-permute-start.12 = (bf16[1,256,512]{2,1,0:T(8,128)(2,1)S(1)}, bf16[1,256,512]{2,1,0:T(8,128)(2,1)S(1)}, u32[]{:S(2)}, u32[]{:S(2)}) collective-permute-start(bf16[1,256,512]{2,1,0:T(8,128)(2,1)S(1)} %place_own_sector.1.sigma_own.own.refs_1_), channel_id=1, source_target_pairs={{1,0},{0,1},{3,2},{2,3},{5,4},{4,5},{7,6},{6,7},{9,8},{8,9},{11,10... | collective-permute-start | bytes 786440 | tf_op jit(solution)/shard_map/ppermute | solution.py:244
  32.0 1.6 %collective-permute-start.16 = (bf16[1,256,512]{2,1,0:T(8,128)(2,1)S(1)}, bf16[1,256,512]{2,1,0:T(8,128)(2,1)S(1)}, u32[]{:S(2)}, u32[]{:S(2)}) collective-permute-start(bf16[1,256,512]{2,1,0:T(8,128)(2,1)S(1)} %place_other_sectors.1.across_own), channel_id=1, source_target_pairs={{1,0},{0,1},{3,2},{2,3},{5,4},{4,5},{7,6},{6,7},{9,8},{8,9},{11,10... | collective-permute-start | bytes 786440 | tf_op jit(solution)/shard_map/ppermute | solution.py:244
  34.7 8.7 %collective-permute-start.17 = (bf16[1,64,512]{2,1,0:T(8,128)(2,1)S(1)}, bf16[1,64,512]{2,1,0:T(8,128)(2,1)S(1)}, u32[]{:S(2)}, u32[]{:S(2)}) collective-permute-start(bf16[1,64,512]{2,1,0:T(8,128)(2,1)S(1)} %get-tuple-element.41), channel_id=1, source_target_pairs={{12,0},{8,4},{4,8},{0,12},{13,1},{9,5},{5,9},{1,13},{14,2},{10,6},... | collective-permute-start | bytes 196616 | tf_op jit(solution)/shard_map/ppermute | solution.py:244
  37.0 6.5 %collective-permute-start.18 = (bf16[1,64,512]{2,1,0:T(8,128)(2,1)S(1)}, bf16[1,64,512]{2,1,0:T(8,128)(2,1)S(1)}, u32[]{:S(2)}, u32[]{:S(2)}) collective-permute-start(bf16[1,64,512]{2,1,0:T(8,128)(2,1)S(1)} %get-tuple-element.42), channel_id=1, source_target_pairs={{8,0},{12,4},{0,8},{4,12},{9,1},{13,5},{1,9},{5,13},{10,2},{14,6},... | collective-permute-start | bytes 196616 | tf_op jit(solution)/shard_map/ppermute | solution.py:244
  37.1 6.5 %collective-permute-start.19 = (bf16[1,64,512]{2,1,0:T(8,128)(2,1)S(1)}, bf16[1,64,512]{2,1,0:T(8,128)(2,1)S(1)}, u32[]{:S(2)}, u32[]{:S(2)}) collective-permute-start(bf16[1,64,512]{2,1,0:T(8,128)(2,1)S(1)} %get-tuple-element.43), channel_id=1, source_target_pairs={{4,0},{0,4},{12,8},{8,12},{5,1},{1,5},{13,9},{9,13},{6,2},{2,6},{1... | collective-permute-start | bytes 196616 | tf_op jit(solution)/shard_map/ppermute | solution.py:244
  39.7 3.8 %collective-permute-start.13 = (f32[3,8,128]{2,1,0:T(8,128)S(1)}, f32[3,8,128]{2,1,0:T(8,128)S(1)}, u32[]{:S(2)}, u32[]{:S(2)}) collective-permute-start(f32[3,8,128]{2,1,0:T(8,128)S(1)} %sums_for_rayleigh.1.refs_0_.refs_5_), channel_id=1, source_target_pairs={{2,0},{0,2},{3,1},{1,3},{6,4},{4,6},{7,5},{5,7},{10,8},{8,10},{11,... | collective-permute-start | bytes 36872 | tf_op jit(solution)/shard_map/ppermute | solution.py:244
  43.6 6.7 %collective-permute-start.20 = (bf16[1,64,512]{2,1,0:T(8,128)(2,1)S(1)}, bf16[1,64,512]{2,1,0:T(8,128)(2,1)S(1)}, u32[]{:S(2)}, u32[]{:S(2)}) collective-permute-start(bf16[1,64,512]{2,1,0:T(8,128)(2,1)S(1)} %sum_second_sigma.1.refs_5_), channel_id=1, source_target_pairs={{12,0},{8,4},{4,8},{0,12},{13,1},{9,5},{5,9},{1,13},{14,2},{10,6},... | collective-permute-start | bytes 196616 | tf_op jit(solution)/shard_map/ppermute | solution.py:244
  45.9 6.4 %collective-permute-start.21 = (bf16[1,64,512]{2,1,0:T(8,128)(2,1)S(1)}, bf16[1,64,512]{2,1,0:T(8,128)(2,1)S(1)}, u32[]{:S(2)}, u32[]{:S(2)}) collective-permute-start(bf16[1,64,512]{2,1,0:T(8,128)(2,1)S(1)} %sum_second_sigma.1.refs_5_), channel_id=1, source_target_pairs={{8,0},{12,4},{0,8},{4,12},{9,1},{13,5},{1,9},{5,13},{10,2},{14,6},... | collective-permute-start | bytes 196616 | tf_op jit(solution)/shard_map/ppermute | solution.py:244
  45.9 6.4 %collective-permute-start.22 = (bf16[1,64,512]{2,1,0:T(8,128)(2,1)S(1)}, bf16[1,64,512]{2,1,0:T(8,128)(2,1)S(1)}, u32[]{:S(2)}, u32[]{:S(2)}) collective-permute-start(bf16[1,64,512]{2,1,0:T(8,128)(2,1)S(1)} %sum_second_sigma.1.refs_5_), channel_id=1, source_target_pairs={{4,0},{0,4},{12,8},{8,12},{5,1},{1,5},{13,9},{9,13},{6,2},{2,6},{1... | collective-permute-start | bytes 196616 | tf_op jit(solution)/shard_map/ppermute | solution.py:244

commit v21 on v20

--- a/solution.py
+++ b/solution.py
@@ -339,10 +339,13 @@
         wave_other,
     )
     met = [partner(rest[(far, 0), across], {"sec": across}) for across in range(sectors)]
-    received = [partner(summed("sum_far_share", *met), {"ops": far})]
-    first_two = [(direct[0], 0), (direct[-1], 0)]
-    order = first_two + [spot for spot in rest if spot[0] in direct and spot not in first_two]
+    far_sum = summed("sum_far_share", *met)
+    received = [partner(far_sum, {"ops": far})]
+    nearest = (direct[-1], 0)
+    order = [spot for spot in rest if spot[0] in direct and spot != nearest]
     received += [partner(rest[spot], {"ops": spot[0][0], "sec": spot[1]}) for spot in order]
+    last = summed("hand_on", rest[nearest], after=(far_sum,))
+    received.append(partner(last, {"ops": nearest[0][0]}))
     first_share = summed("sum_first_sigma", *[(piece, 1) for piece in met], *received, live=live)
     along_ops = {along: partner(first_share, {"ops": along}) for along in send_order}
     spots = [(along, across) for along in send_order for across in range(1, sectors)]

time: 53.4 us -> 54.7 us (1.024)
  waiting for transfers between devices: 11.5 us -> 13.7 us
  starting transfers between devices: 31.7 us -> 30.9 us
    ppermute x23, waiting for transfers between devices: 11.5 us -> 13.7 us  [partner(): return lax.ppermute(value, axes, pairs)]
    ppermute x23, starting transfers between devices: 31.7 us -> 30.9 us  [partner(): return lax.ppermute(value, axes, pairs)]
    pallas_call x14 -> x15, Pallas kernels: 9.11 us -> 9.11 us  [call(): pl.pallas_call(kernel, out_shape=out_shape, in_specs=list(in_specs) + [in...]
  transfers between devices with their start and end apart: 23 -> 23, of which waited for: 10 -> 12; matrix products, arithmetic and copies ran while one was open for 0% -> 0% of each run, Pallas kernels for 10% -> 10%
where the time goes in v21:
time: 54.7 us; the launch traced here: 54.5 us
  starting transfers between devices  30.9 us (56%)
  waiting for transfers between devices  13.7 us (25%)
  Pallas kernels  9.11 us (17%)
  between operations  0.84 us (2%)
    ppermute x23, starting transfers between devices, partner(): return lax.ppermute(value, axes, pairs)  30.9 us
    ppermute x23, waiting for transfers between devices, partner(): return lax.ppermute(value, axes, pairs)  13.7 us
    pallas_call x15, Pallas kernels, call(): pl.pallas_call(kernel, out_shape=out_shape, in_specs=list(in_specs) + [in...  9.11 us
  transfers between devices with their start and end apart: 23, of which 12 were waited for; matrix products, arithmetic and copies ran while one was open for 0% of the time, Pallas kernels for 10%

profile of v21, /device:TPU:0, one launch (start us, length us, event | category | flops | bytes accessed | tf_op | source)
XLA Modules:
  0.0 54.5 jit_solution(4076108050612365117)
XLA Ops:
  0.6 0.0 copy-start.1
  0.6 0.0 copy-start.3
  0.7 0.0 copy-start.2
  0.7 0.0 copy-start.4
  0.7 0.5 collective-permute-start
  1.2 1.4 %load_operators.1 = (bf16[4,256,256]{2,1,0:T(8,128)(2,1)S(1)}, bf16[4,256,256]{2,1,0:T(8,128)(2,1)S(1)}) custom-call(bf16[4,512,512]{2,1,0:T(8,128)(2,1)} %left_ref.1), custom_call_target="tpu_custom_call" | custom-call | tf_op jit(solution)/shard_map/load_operators/pallas_call | solution.py:262
  2.6 0.0 copy-done.1
  2.6 0.0 copy-done.3
  2.7 0.0 copy-done.2
  2.7 0.0 copy-done.4
  2.7 0.2 tables_for_first_sigma.1
  2.9 0.0 collective-permute-done.refs_6_
  2.9 1.6 %first_sigma_terms.1 = (bf16[256,512]{1,0:T(8,128)(2,1)S(1)}, f32[2,64,512]{2,1,0:T(8,128)S(1)}, bf16[2,64,512]{2,1,0:T(8,128)(2,1)S(1)}, bf16[1,64,512]{2,1,0:T...) custom-call(s32[2,2]{1,0:T(2,128)S(1)} %copy-done.3, ...), custom_call_target="tpu_custom_call" | custom-call | tf_op jit(solution)/shard_map/first_sigma_terms/pallas_call | solution.py:262
  4.5 2.8 %collective-permute-start.1 = (bf16[2,64,512]{2,1,0:T(8,128)(2,1)S(1)}, bf16[2,64,512]{2,1,0:T(8,128)(2,1)S(1)}, u32[]{:S(2)}, u32[]{:S(2)}) collective-permute-start(bf16[2,64,512]{2,1,0:T(8,128)(2,1)S(1)} %get-tuple-element.28), channel_id=1, source_target_pairs={{2,0},{0,2},{3,1},{1,3},{6,4},{4,6},{7,5},{5,7},{10,8},{8,10},{11,... | collective-permute-start | bytes 393224 | tf_op jit(solution)/shard_map/ppermute | solution.py:244
  7.3 2.6 %collective-permute-start.3 = (bf16[1,64,512]{2,1,0:T(8,128)(2,1)S(1)}, bf16[1,64,512]{2,1,0:T(8,128)(2,1)S(1)}, u32[]{:S(2)}, u32[]{:S(2)}) collective-permute-start(bf16[1,64,512]{2,1,0:T(8,128)(2,1)S(1)} %get-tuple-element.29), channel_id=1, source_target_pairs={{8,0},{12,4},{0,8},{4,12},{9,1},{13,5},{1,9},{5,13},{10,2},{14,6},... | collective-permute-start | bytes 196616 | tf_op jit(solution)/shard_map/ppermute | solution.py:244
  9.9 0.0 collective-permute-start.4
  9.9 2.8 %collective-permute-start.5 = (bf16[1,64,512]{2,1,0:T(8,128)(2,1)S(1)}, bf16[1,64,512]{2,1,0:T(8,128)(2,1)S(1)}, u32[]{:S(2)}, u32[]{:S(2)}) collective-permute-start(bf16[1,64,512]{2,1,0:T(8,128)(2,1)S(1)} %get-tuple-element.31), channel_id=1, source_target_pairs={{6,0},{4,2},{2,4},{0,6},{14,8},{12,10},{10,12},{8,14},{7,1},{5,3},... | collective-permute-start | bytes 196616 | tf_op jit(solution)/shard_map/ppermute | solution.py:244
  12.7 0.0 collective-permute-done.1.refs_1_
  12.7 2.5 %collective-permute-start.2 = (bf16[1,64,512]{2,1,0:T(8,128)(2,1)S(1)}, bf16[1,64,512]{2,1,0:T(8,128)(2,1)S(1)}, u32[]{:S(2)}, u32[]{:S(2)}) collective-permute-start(bf16[1,64,512]{2,1,0:T(8,128)(2,1)S(1)} %sum_far_share.1.refs_1_), channel_id=1, source_target_pairs={{12,0},{8,4},{4,8},{0,12},{13,1},{9,5},{5,9},{1,13},{14,2},{10,6},... | collective-permute-start | bytes 196616 | tf_op jit(solution)/shard_map/ppermute | solution.py:244
  15.3 0.7 %collective-permute-start.6 = (bf16[1,64,512]{2,1,0:T(8,128)(2,1)S(1)}, bf16[1,64,512]{2,1,0:T(8,128)(2,1)S(1)}, u32[]{:S(2)}, u32[]{:S(2)}) collective-permute-start(bf16[1,64,512]{2,1,0:T(8,128)(2,1)S(1)} %hand_on.1), channel_id=1, source_target_pairs={{4,0},{0,4},{12,8},{8,12},{5,1},{1,5},{13,9},{9,13},{6,2},{2,6},{1... | collective-permute-start | bytes 196616 | tf_op jit(solution)/shard_map/ppermute | solution.py:244
  15.9 0.8 %tables_for_second_sigma.1 = (f32[4,2,8,128]{3,2,1,0:T(8,128)S(1)}, f32[256,512]{1,0:T(8,128)S(1)}) custom-call(s32[2,2]{1,0:T(2,128)S(1)} %copy-done.3, s32[4,2,8]{2,1,0:T(2,128)S(1)} %bitcast.2, f32[4,8]{1,0:T(4,128)S(1)} %copy-done.4, bf16[256,512]{1,0:T(8,128)(2,1)S(1)} %get-tuple-element.33._.wave_other), custom_call_target="tpu_custom_call" | custom-call | tf_op jit(solution)/shard_map/tables_for_second_sigma/pallas_call | solution.py:262
  16.7 0.0 collective-permute-done.3.refs_3_
  16.8 1.6 %collective-permute-done.4.refs_4_ = bf16[1,64,512]{2,1,0:T(8,128)(2,1)S(1)} collective-permute-done((bf16[1,64,512]{2,1,0:T(8,128)(2,1)S(1)}, bf16[1,64,512]{2,1,0:T(8,128)(2,1)S(1)}, u32[]{:S(2)}, u32[]{:S(2)}) %collective-permute-start.4) | collective-permute-done | bytes 65568 | tf_op jit(solution)/shard_map/ppermute | solution.py:244
  18.3 0.0 collective-permute-done.5.refs_5_
  18.3 1.1 %collective-permute-done.2.refs_2_ = bf16[1,64,512]{2,1,0:T(8,128)(2,1)S(1)} collective-permute-done((bf16[1,64,512]{2,1,0:T(8,128)(2,1)S(1)}, bf16[1,64,512]{2,1,0:T(8,128)(2,1)S(1)}, u32[]{:S(2)}, u32[]{:S(2)}) %collective-permute-start.2) | collective-permute-done | bytes 65568 | tf_op jit(solution)/shard_map/ppermute | solution.py:244
  19.4 0.5 %collective-permute-done.6.refs_6_ = bf16[1,64,512]{2,1,0:T(8,128)(2,1)S(1)} collective-permute-done((bf16[1,64,512]{2,1,0:T(8,128)(2,1)S(1)}, bf16[1,64,512]{2,1,0:T(8,128)(2,1)S(1)}, u32[]{:S(2)}, u32[]{:S(2)}) %collective-permute-start.6) | collective-permute-done | bytes 65568 | tf_op jit(solution)/shard_map/ppermute | solution.py:244
  19.9 0.1 sum_first_sigma.1.refs_5_
  20.0 1.8 %collective-permute-start.9 = (bf16[1,64,512]{2,1,0:T(8,128)(2,1)S(1)}, bf16[1,64,512]{2,1,0:T(8,128)(2,1)S(1)}, u32[]{:S(2)}, u32[]{:S(2)}) collective-permute-start(bf16[1,64,512]{2,1,0:T(8,128)(2,1)S(1)} %sum_first_sigma.1.refs_5_), channel_id=1, source_target_pairs={{8,0},{12,4},{0,8},{4,12},{9,1},{13,5},{1,9},{5,13},{10,2},{14,6},... | collective-permute-start | bytes 196616 | tf_op jit(solution)/shard_map/ppermute | solution.py:244
  21.8 1.9 %collective-permute-start.10 = (bf16[1,64,512]{2,1,0:T(8,128)(2,1)S(1)}, bf16[1,64,512]{2,1,0:T(8,128)(2,1)S(1)}, u32[]{:S(2)}, u32[]{:S(2)}) collective-permute-start(bf16[1,64,512]{2,1,0:T(8,128)(2,1)S(1)} %sum_first_sigma.1.refs_5_), channel_id=1, source_target_pairs={{12,0},{8,4},{4,8},{0,12},{13,1},{9,5},{5,9},{1,13},{14,2},{10,6},... | collective-permute-start | bytes 196616 | tf_op jit(solution)/shard_map/ppermute | solution.py:244
  23.6 0.6 %collective-permute-start.7 = (bf16[1,64,512]{2,1,0:T(8,128)(2,1)S(1)}, bf16[1,64,512]{2,1,0:T(8,128)(2,1)S(1)}, u32[]{:S(2)}, u32[]{:S(2)}) collective-permute-start(bf16[1,64,512]{2,1,0:T(8,128)(2,1)S(1)} %sum_first_sigma.1.refs_5_), channel_id=1, source_target_pairs={{6,0},{4,2},{2,4},{0,6},{14,8},{12,10},{10,12},{8,14},{7,1},{5,3},... | collective-permute-start | bytes 196616 | tf_op jit(solution)/shard_map/ppermute | solution.py:244
  24.3 1.3 %collective-permute-start.8 = (bf16[1,64,512]{2,1,0:T(8,128)(2,1)S(1)}, bf16[1,64,512]{2,1,0:T(8,128)(2,1)S(1)}, u32[]{:S(2)}, u32[]{:S(2)}) collective-permute-start(bf16[1,64,512]{2,1,0:T(8,128)(2,1)S(1)} %sum_first_sigma.1.refs_5_), channel_id=1, source_target_pairs={{2,0},{0,2},{3,1},{1,3},{6,4},{4,6},{7,5},{5,7},{10,8},{8,10},{11,... | collective-permute-start | bytes 196616 | tf_op jit(solution)/shard_map/ppermute | solution.py:244
  25.6 1.5 %collective-permute-start.11 = (bf16[1,64,512]{2,1,0:T(8,128)(2,1)S(1)}, bf16[1,64,512]{2,1,0:T(8,128)(2,1)S(1)}, u32[]{:S(2)}, u32[]{:S(2)}) collective-permute-start(bf16[1,64,512]{2,1,0:T(8,128)(2,1)S(1)} %sum_first_sigma.1.refs_5_), channel_id=1, source_target_pairs={{4,0},{0,4},{12,8},{8,12},{5,1},{1,5},{13,9},{9,13},{6,2},{2,6},{1... | collective-permute-start | bytes 196616 | tf_op jit(solution)/shard_map/ppermute | solution.py:244
  27.1 0.0 collective-permute-done.9.refs_2_
  27.1 1.9 %collective-permute-start.14 = (bf16[1,64,512]{2,1,0:T(8,128)(2,1)S(1)}, bf16[1,64,512]{2,1,0:T(8,128)(2,1)S(1)}, u32[]{:S(2)}, u32[]{:S(2)}) collective-permute-start(bf16[1,64,512]{2,1,0:T(8,128)(2,1)S(1)} %collective-permute-done.9.refs_2_), channel_id=1, source_target_pairs={{2,0},{0,2},{3,1},{1,3},{6,4},{4,6},{7,5},{5,7},{10,8},{8,10},{11,... | collective-permute-start | bytes 196616 | tf_op jit(solution)/shard_map/ppermute | solution.py:244
  29.1 0.0 collective-permute-done.10.refs_3_
  29.1 0.1 collective-permute-start.15
  29.2 0.7 %collective-permute-done.7.refs_0_.refs_2_ = bf16[1,64,512]{2,1,0:T(8,128)(2,1)S(1)} collective-permute-done((bf16[1,64,512]{2,1,0:T(8,128)(2,1)S(1)}, bf16[1,64,512]{2,1,0:T(8,128)(2,1)S(1)}, u32[]{:S(2)}, u32[]{:S(2)}) %collective-permute-start.7) | collective-permute-done | bytes 65568 | tf_op jit(solution)/shard_map/ppermute | solution.py:244
  29.8 0.3 collective-permute-done.8.refs_1_.refs_3_
  30.1 0.0 collective-permute-done.11.refs_4_
  30.1 0.1 collective-permute-start.12
  30.2 1.5 %collective-permute-done.14.refs_0_ = bf16[1,64,512]{2,1,0:T(8,128)(2,1)S(1)} collective-permute-done((bf16[1,64,512]{2,1,0:T(8,128)(2,1)S(1)}, bf16[1,64,512]{2,1,0:T(8,128)(2,1)S(1)}, u32[]{:S(2)}, u32[]{:S(2)}) %collective-permute-start.14) | collective-permute-done | bytes 65568 | tf_op jit(solution)/shard_map/ppermute | solution.py:244
  31.7 1.6 %collective-permute-done.15.refs_1_ = bf16[1,64,512]{2,1,0:T(8,128)(2,1)S(1)} collective-permute-done((bf16[1,64,512]{2,1,0:T(8,128)(2,1)S(1)}, bf16[1,64,512]{2,1,0:T(8,128)(2,1)S(1)}, u32[]{:S(2)}, u32[]{:S(2)}) %collective-permute-start.15) | collective-permute-done | bytes 65568 | tf_op jit(solution)/shard_map/ppermute | solution.py:244
  33.4 0.1 collective-permute-start.16
  33.4 0.0 collective-permute-done.12.sigma_other.other
  33.5 1.0 %left_products.1 = (f32[4,256,512]{2,1,0:T(8,128)S(1)}, f32[1,4,256,512]{3,2,1,0:T(8,128)S(1)}) custom-call(bf16[4,256,256]{2,1,0:T(8,128)(2,1)S(1)} %get-tuple-element.23._.refs_2_.left_own, bf16[4,256,256]{2,1,0:T(8,128)(2,1)S(1)} %get-tuple-element.26.refs_3_.left_other, bf16[1,256,512]{2,1,0:T(8,128)(2,1)S(1)} %place_own_sector.1.sigma_own.own.refs_1_, ...), custom_call_target="tpu_custom_call" | custom-call | tf_op jit(solution)/shard_map/left_products/pallas_call | solution.py:262
  34.4 0.5 collective-permute-done.16.other
  35.0 1.1 %second_sigma_terms.1 = (f32[1,64,512]{2,1,0:T(8,128)S(1)}, bf16[1,64,512]{2,1,0:T(8,128)(2,1)S(1)}, bf16[1,64,512]{2,1,0:T(8,128)(2,1)S(1)}, bf16[1,64,512]{2,1,0:T(8,128)(2,1)S(1)}) custom-call(f32[4,2,8,128]{3,2,1,0:T(8,128)S(1)} %get-tuple-element.37.mixing, bf16[4,256,256]{2,1,0:T(8,128)(2,1)S(1)} %get-tuple-element.26.refs_3_.left_other, ...), custom_call_target="tpu_custom_call" | custom-call | tf_op jit(solution)/shard_map/second_sigma_terms/pallas_call | solution.py:262
  36.1 2.4 %collective-permute-start.17 = (bf16[1,64,512]{2,1,0:T(8,128)(2,1)S(1)}, bf16[1,64,512]{2,1,0:T(8,128)(2,1)S(1)}, u32[]{:S(2)}, u32[]{:S(2)}) collective-permute-start(bf16[1,64,512]{2,1,0:T(8,128)(2,1)S(1)} %get-tuple-element.41), channel_id=1, source_target_pairs={{12,0},{8,4},{4,8},{0,12},{13,1},{9,5},{5,9},{1,13},{14,2},{10,6},... | collective-permute-start | bytes 196616 | tf_op jit(solution)/shard_map/ppermute | solution.py:244
  38.5 0.0 collective-permute-start.18
  38.5 2.0 %collective-permute-start.19 = (bf16[1,64,512]{2,1,0:T(8,128)(2,1)S(1)}, bf16[1,64,512]{2,1,0:T(8,128)(2,1)S(1)}, u32[]{:S(2)}, u32[]{:S(2)}) collective-permute-start(bf16[1,64,512]{2,1,0:T(8,128)(2,1)S(1)} %get-tuple-element.43), channel_id=1, source_target_pairs={{4,0},{0,4},{12,8},{8,12},{5,1},{1,5},{13,9},{9,13},{6,2},{2,6},{1... | collective-permute-start | bytes 196616 | tf_op jit(solution)/shard_map/ppermute | solution.py:244
  40.5 0.5 sums_for_rayleigh.1.refs_0_.refs_5_
  41.0 0.8 %collective-permute-start.13 = (f32[3,8,128]{2,1,0:T(8,128)S(1)}, f32[3,8,128]{2,1,0:T(8,128)S(1)}, u32[]{:S(2)}, u32[]{:S(2)}) collective-permute-start(f32[3,8,128]{2,1,0:T(8,128)S(1)} %sums_for_rayleigh.1.refs_0_.refs_5_), channel_id=1, source_target_pairs={{2,0},{0,2},{3,1},{1,3},{6,4},{4,6},{7,5},{5,7},{10,8},{8,10},{11,... | collective-permute-start | bytes 36872 | tf_op jit(solution)/shard_map/ppermute | solution.py:244
  41.8 3.0 %collective-permute-done.13.refs_1_.refs_6_ = f32[3,8,128]{2,1,0:T(8,128)S(1)} collective-permute-done((f32[3,8,128]{2,1,0:T(8,128)S(1)}, f32[3,8,128]{2,1,0:T(8,128)S(1)}, u32[]{:S(2)}, u32[]{:S(2)}) %collective-permute-start.13) | collective-permute-done | bytes 12320 | tf_op jit(solution)/shard_map/ppermute | solution.py:244
  44.8 0.0 collective-permute-done.17.refs_1_
  44.8 0.1 collective-permute-done.18.refs_2_
  44.9 0.0 collective-permute-done.19.refs_3_
  45.0 2.5 %collective-permute-start.20 = (bf16[1,64,512]{2,1,0:T(8,128)(2,1)S(1)}, bf16[1,64,512]{2,1,0:T(8,128)(2,1)S(1)}, u32[]{:S(2)}, u32[]{:S(2)}) collective-permute-start(bf16[1,64,512]{2,1,0:T(8,128)(2,1)S(1)} %sum_second_sigma.1.refs_5_), channel_id=1, source_target_pairs={{12,0},{8,4},{4,8},{0,12},{13,1},{9,5},{5,9},{1,13},{14,2},{10,6},... | collective-permute-start | bytes 196616 | tf_op jit(solution)/shard_map/ppermute | solution.py:244
  47.5 0.0 collective-permute-start.21
  47.5 1.9 %collective-permute-start.22 = (bf16[1,64,512]{2,1,0:T(8,128)(2,1)S(1)}, bf16[1,64,512]{2,1,0:T(8,128)(2,1)S(1)}, u32[]{:S(2)}, u32[]{:S(2)}) collective-permute-start(bf16[1,64,512]{2,1,0:T(8,128)(2,1)S(1)} %sum_second_sigma.1.refs_5_), channel_id=1, source_target_pairs={{4,0},{0,4},{12,8},{8,12},{5,1},{1,5},{13,9},{9,13},{6,2},{2,6},{1... | collective-permute-start | bytes 196616 | tf_op jit(solution)/shard_map/ppermute | solution.py:244
  49.4 1.4 %second_wave.1 = (bf16[1,256,512]{2,1,0:T(8,128)(2,1)}, f32[2,8,128]{2,1,0:T(8,128)S(1)}) custom-call(s32[2,2]{1,0:T(2,128)S(1)} %copy-done.3, bf16[256,512]{1,0:T(8,128)(2,1)S(1)} %get-tuple-element.24.refs_5_.wave_own, bf16[1,256,512]{2,1,0:T(8,128)(2,1)S(1)} %place_own_sector.1.sigma_own.own.refs_1_, f32[3,8,128]{2,1,0:T(8,128)S(1)} %sums_for_rayleigh.1.refs_0_.refs_5_, ...), custom_call_target="tpu_custom_call" | custom-call | tf_op jit(solution)/shard_map/second_wave/pallas_call | solution.py:262
  50.9 0.8 %collective-permute-done.20.refs_2_ = bf16[1,64,512]{2,1,0:T(8,128)(2,1)S(1)} collective-permute-done((bf16[1,64,512]{2,1,0:T(8,128)(2,1)S(1)}, bf16[1,64,512]{2,1,0:T(8,128)(2,1)S(1)}, u32[]{:S(2)}, u32[]{:S(2)}) %collective-permute-start.20) | collective-permute-done | bytes 65568 | tf_op jit(solution)/shard_map/ppermute | solution.py:244
  51.6 2.0 %collective-permute-done.21.refs_3_ = bf16[1,64,512]{2,1,0:T(8,128)(2,1)S(1)} collective-permute-done((bf16[1,64,512]{2,1,0:T(8,128)(2,1)S(1)}, bf16[1,64,512]{2,1,0:T(8,128)(2,1)S(1)}, u32[]{:S(2)}, u32[]{:S(2)}) %collective-permute-start.21) | collective-permute-done | bytes 65568 | tf_op jit(solution)/shard_map/ppermute | solution.py:244
  53.6 0.0 collective-permute-done.22.refs_4_
  53.6 0.9 %join_second_sigma.1 = f32[1,256,512]{2,1,0:T(8,128)} custom-call(f32[2,8,128]{2,1,0:T(8,128)S(1)} %get-tuple-element.36.refs_0_, bf16[1,256,512]{2,1,0:T(8,128)(2,1)S(1)} %place_own_sector.1.sigma_own.own.refs_1_, bf16[1,64,512]{2,1,0:T(8,128)(2,1)S(1)} %collective-permute-done.20.refs_2_, bf16[1,64,512]{2,1,0:T(8,128)(2,1)S(1)} %collective-permute-done.21.refs_3_, ...), custom_call_target="tpu_custom_call" | custom-call | tf_op jit(solution)/shard_map/join_second_sigma/pallas_call | solution.py:262
  (7 shorter events, 0.1 us)
Async XLA Ops:
  0.6 2.0 %copy-start.1 = (bf16[1,256,512]{2,1,0:T(8,128)(2,1)S(1)}, bf16[1,256,512]{2,1,0:T(8,128)(2,1)}, u32[]{:S(2)}) copy-start(bf16[1,256,512]{2,1,0:T(8,128)(2,1)} %wave.1) | copy-start | bytes 786436
  0.6 2.0 %copy-start.3 = (s32[2,2]{1,0:T(2,128)S(1)}, s32[2,2]{1,0:T(2,128)}, u32[]{:S(2)}) copy-start(s32[2,2]{1,0:T(2,128)} %sizes_ref.3) | copy-start | bytes 52
  0.7 2.0 %copy-start.2 = (s32[4,8,2]{1,2,0:T(2,128)S(1)}, s32[4,8,2]{1,2,0:T(2,128)}, u32[]{:S(2)}) copy-start(s32[4,8,2]{1,2,0:T(2,128)} %param.10) | copy-start | bytes 772
  0.7 2.0 %copy-start.4 = (f32[4,8]{1,0:T(4,128)S(1)}, f32[4,8]{1,0:T(4,128)}, u32[]{:S(2)}) copy-start(f32[4,8]{1,0:T(4,128)} %weights_ref.1) | copy-start | bytes 388
  0.7 2.2 %copy-start = (bf16[4,512,512]{2,1,0:T(8,128)(2,1)S(1)}, bf16[4,512,512]{2,1,0:T(8,128)(2,1)}, u32[]{:S(2)}) copy-start(bf16[4,512,512]{2,1,0:T(8,128)(2,1)} %right.1) | copy-start | bytes 6291460
  0.7 2.2 %collective-permute-start = (bf16[1,256,512]{2,1,0:T(8,128)(2,1)}, bf16[1,256,512]{2,1,0:T(8,128)(2,1)S(1)}, u32[]{:S(2)}, u32[]{:S(2)}) collective-permute-start(bf16[1,256,512]{2,1,0:T(8,128)(2,1)} %wave.1), channel_id=1, source_target_pairs={{1,0},{0,1},{3,2},{2,3},{5,4},{4,5},{7,6},{6,7},{9,8},{8,9},{11,10... | collective-permute-start | bytes 786440 | tf_op jit(solution)/shard_map/ppermute | solution.py:244
  4.5 8.2 %collective-permute-start.1 = (bf16[2,64,512]{2,1,0:T(8,128)(2,1)S(1)}, bf16[2,64,512]{2,1,0:T(8,128)(2,1)S(1)}, u32[]{:S(2)}, u32[]{:S(2)}) collective-permute-start(bf16[2,64,512]{2,1,0:T(8,128)(2,1)S(1)} %get-tuple-element.28), channel_id=1, source_target_pairs={{2,0},{0,2},{3,1},{1,3},{6,4},{4,6},{7,5},{5,7},{10,8},{8,10},{11,... | collective-permute-start | bytes 393224 | tf_op jit(solution)/shard_map/ppermute | solution.py:244
  7.3 9.5 %collective-permute-start.3 = (bf16[1,64,512]{2,1,0:T(8,128)(2,1)S(1)}, bf16[1,64,512]{2,1,0:T(8,128)(2,1)S(1)}, u32[]{:S(2)}, u32[]{:S(2)}) collective-permute-start(bf16[1,64,512]{2,1,0:T(8,128)(2,1)S(1)} %get-tuple-element.29), channel_id=1, source_target_pairs={{8,0},{12,4},{0,8},{4,12},{9,1},{13,5},{1,9},{5,13},{10,2},{14,6},... | collective-permute-start | bytes 196616 | tf_op jit(solution)/shard_map/ppermute | solution.py:244
  9.9 8.4 %collective-permute-start.4 = (bf16[1,64,512]{2,1,0:T(8,128)(2,1)S(1)}, bf16[1,64,512]{2,1,0:T(8,128)(2,1)S(1)}, u32[]{:S(2)}, u32[]{:S(2)}) collective-permute-start(bf16[1,64,512]{2,1,0:T(8,128)(2,1)S(1)} %get-tuple-element.30), channel_id=1, source_target_pairs={{10,0},{8,2},{14,4},{12,6},{2,8},{0,10},{6,12},{4,14},{11,1},{9,3}... | collective-permute-start | bytes 196616 | tf_op jit(solution)/shard_map/ppermute | solution.py:244
  9.9 8.4 %collective-permute-start.5 = (bf16[1,64,512]{2,1,0:T(8,128)(2,1)S(1)}, bf16[1,64,512]{2,1,0:T(8,128)(2,1)S(1)}, u32[]{:S(2)}, u32[]{:S(2)}) collective-permute-start(bf16[1,64,512]{2,1,0:T(8,128)(2,1)S(1)} %get-tuple-element.31), channel_id=1, source_target_pairs={{6,0},{4,2},{2,4},{0,6},{14,8},{12,10},{10,12},{8,14},{7,1},{5,3},... | collective-permute-start | bytes 196616 | tf_op jit(solution)/shard_map/ppermute | solution.py:244
  12.7 6.7 %collective-permute-start.2 = (bf16[1,64,512]{2,1,0:T(8,128)(2,1)S(1)}, bf16[1,64,512]{2,1,0:T(8,128)(2,1)S(1)}, u32[]{:S(2)}, u32[]{:S(2)}) collective-permute-start(bf16[1,64,512]{2,1,0:T(8,128)(2,1)S(1)} %sum_far_share.1.refs_1_), channel_id=1, source_target_pairs={{12,0},{8,4},{4,8},{0,12},{13,1},{9,5},{5,9},{1,13},{14,2},{10,6},... | collective-permute-start | bytes 196616 | tf_op jit(solution)/shard_map/ppermute | solution.py:244
  15.3 4.7 %collective-permute-start.6 = (bf16[1,64,512]{2,1,0:T(8,128)(2,1)S(1)}, bf16[1,64,512]{2,1,0:T(8,128)(2,1)S(1)}, u32[]{:S(2)}, u32[]{:S(2)}) collective-permute-start(bf16[1,64,512]{2,1,0:T(8,128)(2,1)S(1)} %hand_on.1), channel_id=1, source_target_pairs={{4,0},{0,4},{12,8},{8,12},{5,1},{1,5},{13,9},{9,13},{6,2},{2,6},{1... | collective-permute-start | bytes 196616 | tf_op jit(solution)/shard_map/ppermute | solution.py:244
  20.0 7.1 %collective-permute-start.9 = (bf16[1,64,512]{2,1,0:T(8,128)(2,1)S(1)}, bf16[1,64,512]{2,1,0:T(8,128)(2,1)S(1)}, u32[]{:S(2)}, u32[]{:S(2)}) collective-permute-start(bf16[1,64,512]{2,1,0:T(8,128)(2,1)S(1)} %sum_first_sigma.1.refs_5_), channel_id=1, source_target_pairs={{8,0},{12,4},{0,8},{4,12},{9,1},{13,5},{1,9},{5,13},{10,2},{14,6},... | collective-permute-start | bytes 196616 | tf_op jit(solution)/shard_map/ppermute | solution.py:244
  21.8 7.3 %collective-permute-start.10 = (bf16[1,64,512]{2,1,0:T(8,128)(2,1)S(1)}, bf16[1,64,512]{2,1,0:T(8,128)(2,1)S(1)}, u32[]{:S(2)}, u32[]{:S(2)}) collective-permute-start(bf16[1,64,512]{2,1,0:T(8,128)(2,1)S(1)} %sum_first_sigma.1.refs_5_), channel_id=1, source_target_pairs={{12,0},{8,4},{4,8},{0,12},{13,1},{9,5},{5,9},{1,13},{14,2},{10,6},... | collective-permute-start | bytes 196616 | tf_op jit(solution)/shard_map/ppermute | solution.py:244
  23.6 6.2 %collective-permute-start.7 = (bf16[1,64,512]{2,1,0:T(8,128)(2,1)S(1)}, bf16[1,64,512]{2,1,0:T(8,128)(2,1)S(1)}, u32[]{:S(2)}, u32[]{:S(2)}) collective-permute-start(bf16[1,64,512]{2,1,0:T(8,128)(2,1)S(1)} %sum_first_sigma.1.refs_5_), channel_id=1, source_target_pairs={{6,0},{4,2},{2,4},{0,6},{14,8},{12,10},{10,12},{8,14},{7,1},{5,3},... | collective-permute-start | bytes 196616 | tf_op jit(solution)/shard_map/ppermute | solution.py:244
  24.3 5.8 %collective-permute-start.8 = (bf16[1,64,512]{2,1,0:T(8,128)(2,1)S(1)}, bf16[1,64,512]{2,1,0:T(8,128)(2,1)S(1)}, u32[]{:S(2)}, u32[]{:S(2)}) collective-permute-start(bf16[1,64,512]{2,1,0:T(8,128)(2,1)S(1)} %sum_first_sigma.1.refs_5_), channel_id=1, source_target_pairs={{2,0},{0,2},{3,1},{1,3},{6,4},{4,6},{7,5},{5,7},{10,8},{8,10},{11,... | collective-permute-start | bytes 196616 | tf_op jit(solution)/shard_map/ppermute | solution.py:244
  25.6 4.5 %collective-permute-start.11 = (bf16[1,64,512]{2,1,0:T(8,128)(2,1)S(1)}, bf16[1,64,512]{2,1,0:T(8,128)(2,1)S(1)}, u32[]{:S(2)}, u32[]{:S(2)}) collective-permute-start(bf16[1,64,512]{2,1,0:T(8,128)(2,1)S(1)} %sum_first_sigma.1.refs_5_), channel_id=1, source_target_pairs={{4,0},{0,4},{12,8},{8,12},{5,1},{1,5},{13,9},{9,13},{6,2},{2,6},{1... | collective-permute-start | bytes 196616 | tf_op jit(solution)/shard_map/ppermute | solution.py:244
  27.1 4.6 %collective-permute-start.14 = (bf16[1,64,512]{2,1,0:T(8,128)(2,1)S(1)}, bf16[1,64,512]{2,1,0:T(8,128)(2,1)S(1)}, u32[]{:S(2)}, u32[]{:S(2)}) collective-permute-start(bf16[1,64,512]{2,1,0:T(8,128)(2,1)S(1)} %collective-permute-done.9.refs_2_), channel_id=1, source_target_pairs={{2,0},{0,2},{3,1},{1,3},{6,4},{4,6},{7,5},{5,7},{10,8},{8,10},{11,... | collective-permute-start | bytes 196616 | tf_op jit(solution)/shard_map/ppermute | solution.py:244
  29.1 4.3 %collective-permute-start.15 = (bf16[1,64,512]{2,1,0:T(8,128)(2,1)S(1)}, bf16[1,64,512]{2,1,0:T(8,128)(2,1)S(1)}, u32[]{:S(2)}, u32[]{:S(2)}) collective-permute-start(bf16[1,64,512]{2,1,0:T(8,128)(2,1)S(1)} %collective-permute-done.10.refs_3_), channel_id=1, source_target_pairs={{2,0},{0,2},{3,1},{1,3},{6,4},{4,6},{7,5},{5,7},{10,8},{8,10},{11,... | collective-permute-start | bytes 196616 | tf_op jit(solution)/shard_map/ppermute | solution.py:244
  30.1 3.3 %collective-permute-start.12 = (bf16[1,256,512]{2,1,0:T(8,128)(2,1)S(1)}, bf16[1,256,512]{2,1,0:T(8,128)(2,1)S(1)}, u32[]{:S(2)}, u32[]{:S(2)}) collective-permute-start(bf16[1,256,512]{2,1,0:T(8,128)(2,1)S(1)} %place_own_sector.1.sigma_own.own.refs_1_), channel_id=1, source_target_pairs={{1,0},{0,1},{3,2},{2,3},{5,4},{4,5},{7,6},{6,7},{9,8},{8,9},{11,10... | collective-permute-start | bytes 786440 | tf_op jit(solution)/shard_map/ppermute | solution.py:244
  33.4 1.6 %collective-permute-start.16 = (bf16[1,256,512]{2,1,0:T(8,128)(2,1)S(1)}, bf16[1,256,512]{2,1,0:T(8,128)(2,1)S(1)}, u32[]{:S(2)}, u32[]{:S(2)}) collective-permute-start(bf16[1,256,512]{2,1,0:T(8,128)(2,1)S(1)} %place_other_sectors.1.across_own), channel_id=1, source_target_pairs={{1,0},{0,1},{3,2},{2,3},{5,4},{4,5},{7,6},{6,7},{9,8},{8,9},{11,10... | collective-permute-start | bytes 786440 | tf_op jit(solution)/shard_map/ppermute | solution.py:244
  36.1 8.7 %collective-permute-start.17 = (bf16[1,64,512]{2,1,0:T(8,128)(2,1)S(1)}, bf16[1,64,512]{2,1,0:T(8,128)(2,1)S(1)}, u32[]{:S(2)}, u32[]{:S(2)}) collective-permute-start(bf16[1,64,512]{2,1,0:T(8,128)(2,1)S(1)} %get-tuple-element.41), channel_id=1, source_target_pairs={{12,0},{8,4},{4,8},{0,12},{13,1},{9,5},{5,9},{1,13},{14,2},{10,6},... | collective-permute-start | bytes 196616 | tf_op jit(solution)/shard_map/ppermute | solution.py:244
  38.5 6.4 %collective-permute-start.18 = (bf16[1,64,512]{2,1,0:T(8,128)(2,1)S(1)}, bf16[1,64,512]{2,1,0:T(8,128)(2,1)S(1)}, u32[]{:S(2)}, u32[]{:S(2)}) collective-permute-start(bf16[1,64,512]{2,1,0:T(8,128)(2,1)S(1)} %get-tuple-element.42), channel_id=1, source_target_pairs={{8,0},{12,4},{0,8},{4,12},{9,1},{13,5},{1,9},{5,13},{10,2},{14,6},... | collective-permute-start | bytes 196616 | tf_op jit(solution)/shard_map/ppermute | solution.py:244
  38.5 6.4 %collective-permute-start.19 = (bf16[1,64,512]{2,1,0:T(8,128)(2,1)S(1)}, bf16[1,64,512]{2,1,0:T(8,128)(2,1)S(1)}, u32[]{:S(2)}, u32[]{:S(2)}) collective-permute-start(bf16[1,64,512]{2,1,0:T(8,128)(2,1)S(1)} %get-tuple-element.43), channel_id=1, source_target_pairs={{4,0},{0,4},{12,8},{8,12},{5,1},{1,5},{13,9},{9,13},{6,2},{2,6},{1... | collective-permute-start | bytes 196616 | tf_op jit(solution)/shard_map/ppermute | solution.py:244
  41.0 3.8 %collective-permute-start.13 = (f32[3,8,128]{2,1,0:T(8,128)S(1)}, f32[3,8,128]{2,1,0:T(8,128)S(1)}, u32[]{:S(2)}, u32[]{:S(2)}) collective-permute-start(f32[3,8,128]{2,1,0:T(8,128)S(1)} %sums_for_rayleigh.1.refs_0_.refs_5_), channel_id=1, source_target_pairs={{2,0},{0,2},{3,1},{1,3},{6,4},{4,6},{7,5},{5,7},{10,8},{8,10},{11,... | collective-permute-start | bytes 36872 | tf_op jit(solution)/shard_map/ppermute | solution.py:244
  45.0 6.7 %collective-permute-start.20 = (bf16[1,64,512]{2,1,0:T(8,128)(2,1)S(1)}, bf16[1,64,512]{2,1,0:T(8,128)(2,1)S(1)}, u32[]{:S(2)}, u32[]{:S(2)}) collective-permute-start(bf16[1,64,512]{2,1,0:T(8,128)(2,1)S(1)} %sum_second_sigma.1.refs_5_), channel_id=1, source_target_pairs={{12,0},{8,4},{4,8},{0,12},{13,1},{9,5},{5,9},{1,13},{14,2},{10,6},... | collective-permute-start | bytes 196616 | tf_op jit(solution)/shard_map/ppermute | solution.py:244
  47.5 6.1 %collective-permute-start.21 = (bf16[1,64,512]{2,1,0:T(8,128)(2,1)S(1)}, bf16[1,64,512]{2,1,0:T(8,128)(2,1)S(1)}, u32[]{:S(2)}, u32[]{:S(2)}) collective-permute-start(bf16[1,64,512]{2,1,0:T(8,128)(2,1)S(1)} %sum_second_sigma.1.refs_5_), channel_id=1, source_target_pairs={{8,0},{12,4},{0,8},{4,12},{9,1},{13,5},{1,9},{5,13},{10,2},{14,6},... | collective-permute-start | bytes 196616 | tf_op jit(solution)/shard_map/ppermute | solution.py:244
  47.5 6.1 %collective-permute-start.22 = (bf16[1,64,512]{2,1,0:T(8,128)(2,1)S(1)}, bf16[1,64,512]{2,1,0:T(8,128)(2,1)S(1)}, u32[]{:S(2)}, u32[]{:S(2)}) collective-permute-start(bf16[1,64,512]{2,1,0:T(8,128)(2,1)S(1)} %sum_second_sigma.1.refs_5_), channel_id=1, source_target_pairs={{4,0},{0,4},{12,8},{8,12},{5,1},{1,5},{13,9},{9,13},{6,2},{2,6},{1... | collective-permute-start | bytes 196616 | tf_op jit(solution)/shard_map/ppermute | solution.py:244

commit v22 on v20

--- a/solution.py
+++ b/solution.py
@@ -21,10 +21,6 @@
     row = row_start + lax.broadcasted_iota(jnp.int32, (rows, columns), 0)
     column = lax.broadcasted_iota(jnp.int32, (rows, columns), 1)
     return (row < sizes_ref[sector, 0]) & (column < sizes_ref[sector, 1])
-
-
-def masked(values, live):
-    return jnp.where(live, values.astype(jnp.float32), 0.0).astype(values.dtype)
 
 
 def left_times(lefts, blocks):
@@ -344,13 +340,16 @@
     order = first_two + [spot for spot in rest if spot[0] in direct and spot not in first_two]
     received += [partner(rest[spot], {"ops": spot[0][0], "sec": spot[1]}) for spot in order]
     first_share = summed("sum_first_sigma", *[(piece, 1) for piece in met], *received, live=live)
-    along_ops = {along: partner(first_share, {"ops": along}) for along in send_order}
+    crossed = {
+        along: partner(first_share, {"ops": along}) for along in send_order if along % 2 == 0
+    }
     spots = [(along, across) for along in send_order for across in range(1, sectors)]
     pieces = {
-        (along, across): partner(first_share, {"ops": along, "sec": across})
-        if along < 2
-        else partner(along_ops[along], {"sec": across})
+        (along, across): partner(crossed[along // 2 * 2], {"ops": along % 2, "sec": across})
         for along, across in spots
+    }
+    along_ops = {
+        along: partner(crossed[along // 2 * 2], {"ops": along % 2}) for along in send_order
     }
     ahead = [pieces[along, across] for along, across in spots if along < 2]
     sigma_own = call(

time: 53.4 us -> 54.3 us (1.017)
  waiting for transfers between devices: 11.5 us -> 12.1 us
    ppermute x23, waiting for transfers between devices: 11.5 us -> 12.1 us  [partner(): return lax.ppermute(value, axes, pairs)]
where the time goes in v22:
time: 54.3 us; the launch traced here: 54.1 us
  starting transfers between devices  32 us (59%)
  waiting for transfers between devices  12.1 us (22%)
  Pallas kernels  9.12 us (17%)
  between operations  0.85 us (2%)
    ppermute x23, starting transfers between devices, partner(): return lax.ppermute(value, axes, pairs)  32 us
    ppermute x23, waiting for transfers between devices, partner(): return lax.ppermute(value, axes, pairs)  12.1 us
    pallas_call x14, Pallas kernels, call(): pl.pallas_call(kernel, out_shape=out_shape, in_specs=list(in_specs) + [in...  9.12 us
  transfers between devices with their start and end apart: 23, of which 10 were waited for; matrix products, arithmetic and copies ran while one was open for 0% of the time, Pallas kernels for 10%

profile of v22, /device:TPU:0, one launch (start us, length us, event | category | flops | bytes accessed | tf_op | source)
XLA Modules:
  0.0 54.1 jit_solution(8076456926429720269)
XLA Ops:
  0.6 0.0 copy-start.1
  0.6 0.0 copy-start.3
  0.7 0.0 copy-start.2
  0.7 0.0 copy-start.4
  0.7 0.0 copy-start
  0.7 0.5 collective-permute-start
  1.2 1.4 %load_operators.1 = (bf16[4,256,256]{2,1,0:T(8,128)(2,1)S(1)}, bf16[4,256,256]{2,1,0:T(8,128)(2,1)S(1)}) custom-call(bf16[4,512,512]{2,1,0:T(8,128)(2,1)} %left_ref.1), custom_call_target="tpu_custom_call" | custom-call | tf_op jit(solution)/shard_map/load_operators/pallas_call | solution.py:258
  2.6 0.0 copy-done.1
  2.6 0.0 copy-done.3
  2.7 0.0 copy-done.2
  2.7 0.2 tables_for_first_sigma.1
  2.9 0.0 collective-permute-done.refs_6_
  2.9 1.6 %first_sigma_terms.1 = (bf16[256,512]{1,0:T(8,128)(2,1)S(1)}, f32[2,64,512]{2,1,0:T(8,128)S(1)}, bf16[2,64,512]{2,1,0:T(8,128)(2,1)S(1)}, bf16[1,64,512]{2,1,0:T...) custom-call(s32[2,2]{1,0:T(2,128)S(1)} %copy-done.3, ...), custom_call_target="tpu_custom_call" | custom-call | tf_op jit(solution)/shard_map/first_sigma_terms/pallas_call | solution.py:258
  4.5 2.8 %collective-permute-start.1 = (bf16[2,64,512]{2,1,0:T(8,128)(2,1)S(1)}, bf16[2,64,512]{2,1,0:T(8,128)(2,1)S(1)}, u32[]{:S(2)}, u32[]{:S(2)}) collective-permute-start(bf16[2,64,512]{2,1,0:T(8,128)(2,1)S(1)} %get-tuple-element.28), channel_id=1, source_target_pairs={{2,0},{0,2},{3,1},{1,3},{6,4},{4,6},{7,5},{5,7},{10,8},{8,10},{11,... | collective-permute-start | bytes 393224 | tf_op jit(solution)/shard_map/ppermute | solution.py:240
  7.3 2.6 %collective-permute-start.3 = (bf16[1,64,512]{2,1,0:T(8,128)(2,1)S(1)}, bf16[1,64,512]{2,1,0:T(8,128)(2,1)S(1)}, u32[]{:S(2)}, u32[]{:S(2)}) collective-permute-start(bf16[1,64,512]{2,1,0:T(8,128)(2,1)S(1)} %get-tuple-element.29), channel_id=1, source_target_pairs={{8,0},{12,4},{0,8},{4,12},{9,1},{13,5},{1,9},{5,13},{10,2},{14,6},... | collective-permute-start | bytes 196616 | tf_op jit(solution)/shard_map/ppermute | solution.py:240
  9.9 1.6 %collective-permute-start.4 = (bf16[1,64,512]{2,1,0:T(8,128)(2,1)S(1)}, bf16[1,64,512]{2,1,0:T(8,128)(2,1)S(1)}, u32[]{:S(2)}, u32[]{:S(2)}) collective-permute-start(bf16[1,64,512]{2,1,0:T(8,128)(2,1)S(1)} %get-tuple-element.30), channel_id=1, source_target_pairs={{4,0},{0,4},{12,8},{8,12},{5,1},{1,5},{13,9},{9,13},{6,2},{2,6},{1... | collective-permute-start | bytes 196616 | tf_op jit(solution)/shard_map/ppermute | solution.py:240
  11.5 0.3 collective-permute-start.5
  11.8 1.4 %collective-permute-start.6 = (bf16[1,64,512]{2,1,0:T(8,128)(2,1)S(1)}, bf16[1,64,512]{2,1,0:T(8,128)(2,1)S(1)}, u32[]{:S(2)}, u32[]{:S(2)}) collective-permute-start(bf16[1,64,512]{2,1,0:T(8,128)(2,1)S(1)} %get-tuple-element.32), channel_id=1, source_target_pairs={{6,0},{4,2},{2,4},{0,6},{14,8},{12,10},{10,12},{8,14},{7,1},{5,3},... | collective-permute-start | bytes 196616 | tf_op jit(solution)/shard_map/ppermute | solution.py:240
  13.1 0.0 collective-permute-done.1.refs_1_
  13.2 3.7 %collective-permute-start.2 = (bf16[1,64,512]{2,1,0:T(8,128)(2,1)S(1)}, bf16[1,64,512]{2,1,0:T(8,128)(2,1)S(1)}, u32[]{:S(2)}, u32[]{:S(2)}) collective-permute-start(bf16[1,64,512]{2,1,0:T(8,128)(2,1)S(1)} %sum_far_share.1), channel_id=1, source_target_pairs={{12,0},{8,4},{4,8},{0,12},{13,1},{9,5},{5,9},{1,13},{14,2},{10,6},... | collective-permute-start | bytes 196616 | tf_op jit(solution)/shard_map/ppermute | solution.py:240
  16.8 0.8 %tables_for_second_sigma.1 = (f32[4,2,8,128]{3,2,1,0:T(8,128)S(1)}, f32[256,512]{1,0:T(8,128)S(1)}) custom-call(s32[2,2]{1,0:T(2,128)S(1)} %copy-done.3, s32[4,2,8]{2,1,0:T(2,128)S(1)} %bitcast.2, f32[4,8]{1,0:T(4,128)S(1)} %copy-done.4, bf16[256,512]{1,0:T(8,128)(2,1)S(1)} %get-tuple-element.33._.wave_other), custom_call_target="tpu_custom_call" | custom-call | tf_op jit(solution)/shard_map/tables_for_second_sigma/pallas_call | solution.py:258
  17.6 0.0 collective-permute-done.3.refs_3_
  17.7 0.0 collective-permute-done.4.refs_4_
  17.7 2.2 %collective-permute-done.5.refs_5_ = bf16[1,64,512]{2,1,0:T(8,128)(2,1)S(1)} collective-permute-done((bf16[1,64,512]{2,1,0:T(8,128)(2,1)S(1)}, bf16[1,64,512]{2,1,0:T(8,128)(2,1)S(1)}, u32[]{:S(2)}, u32[]{:S(2)}) %collective-permute-start.5) | collective-permute-done | bytes 65568 | tf_op jit(solution)/shard_map/ppermute | solution.py:240
  19.9 0.0 collective-permute-done.6.refs_6_
  19.9 0.0 collective-permute-done.2.refs_2_
  19.9 0.1 sum_first_sigma.1.refs_5_
  20.0 1.1 %collective-permute-start.9 = (bf16[1,64,512]{2,1,0:T(8,128)(2,1)S(1)}, bf16[1,64,512]{2,1,0:T(8,128)(2,1)S(1)}, u32[]{:S(2)}, u32[]{:S(2)}) collective-permute-start(bf16[1,64,512]{2,1,0:T(8,128)(2,1)S(1)} %sum_first_sigma.1.refs_5_), channel_id=1, source_target_pairs={{8,0},{12,4},{0,8},{4,12},{9,1},{13,5},{1,9},{5,13},{10,2},{14,6},... | collective-permute-start | bytes 196616 | tf_op jit(solution)/shard_map/ppermute | solution.py:240
  21.0 2.5 %collective-permute-start.7 = (bf16[1,64,512]{2,1,0:T(8,128)(2,1)S(1)}, bf16[1,64,512]{2,1,0:T(8,128)(2,1)S(1)}, u32[]{:S(2)}, u32[]{:S(2)}) collective-permute-start(bf16[1,64,512]{2,1,0:T(8,128)(2,1)S(1)} %sum_first_sigma.1.refs_5_), channel_id=1, source_target_pairs={{6,0},{4,2},{2,4},{0,6},{14,8},{12,10},{10,12},{8,14},{7,1},{5,3},... | collective-permute-start | bytes 196616 | tf_op jit(solution)/shard_map/ppermute | solution.py:240
  23.6 1.5 %collective-permute-start.8 = (bf16[1,64,512]{2,1,0:T(8,128)(2,1)S(1)}, bf16[1,64,512]{2,1,0:T(8,128)(2,1)S(1)}, u32[]{:S(2)}, u32[]{:S(2)}) collective-permute-start(bf16[1,64,512]{2,1,0:T(8,128)(2,1)S(1)} %sum_first_sigma.1.refs_5_), channel_id=1, source_target_pairs={{2,0},{0,2},{3,1},{1,3},{6,4},{4,6},{7,5},{5,7},{10,8},{8,10},{11,... | collective-permute-start | bytes 196616 | tf_op jit(solution)/shard_map/ppermute | solution.py:240
  25.1 0.0 collective-permute-start.11
  25.1 0.9 %collective-permute-done.9.refs_2_ = bf16[1,64,512]{2,1,0:T(8,128)(2,1)S(1)} collective-permute-done((bf16[1,64,512]{2,1,0:T(8,128)(2,1)S(1)}, bf16[1,64,512]{2,1,0:T(8,128)(2,1)S(1)}, u32[]{:S(2)}, u32[]{:S(2)}) %collective-permute-start.9) | collective-permute-done | bytes 65568 | tf_op jit(solution)/shard_map/ppermute | solution.py:240
  26.0 1.1 %collective-permute-start.10 = (bf16[1,64,512]{2,1,0:T(8,128)(2,1)S(1)}, bf16[1,64,512]{2,1,0:T(8,128)(2,1)S(1)}, u32[]{:S(2)}, u32[]{:S(2)}) collective-permute-start(bf16[1,64,512]{2,1,0:T(8,128)(2,1)S(1)} %collective-permute-done.9.refs_2_), channel_id=1, source_target_pairs={{4,0},{0,4},{12,8},{8,12},{5,1},{1,5},{13,9},{9,13},{6,2},{2,6},{1... | collective-permute-start | bytes 196616 | tf_op jit(solution)/shard_map/ppermute | solution.py:240
  27.1 0.5 collective-permute-start.14
  27.6 0.0 collective-permute-done.7.refs_0_.refs_2_
  27.6 1.9 %collective-permute-start.15 = (bf16[1,64,512]{2,1,0:T(8,128)(2,1)S(1)}, bf16[1,64,512]{2,1,0:T(8,128)(2,1)S(1)}, u32[]{:S(2)}, u32[]{:S(2)}) collective-permute-start(bf16[1,64,512]{2,1,0:T(8,128)(2,1)S(1)} %collective-permute-done.9.refs_2_), channel_id=1, source_target_pairs={{6,0},{4,2},{2,4},{0,6},{14,8},{12,10},{10,12},{8,14},{7,1},{5,3},... | collective-permute-start | bytes 196616 | tf_op jit(solution)/shard_map/ppermute | solution.py:240
  29.5 0.0 collective-permute-done.8.refs_1_.refs_3_
  29.5 0.0 collective-permute-done.11.refs_4_
  29.5 0.8 %collective-permute-done.10.refs_3_ = bf16[1,64,512]{2,1,0:T(8,128)(2,1)S(1)} collective-permute-done((bf16[1,64,512]{2,1,0:T(8,128)(2,1)S(1)}, bf16[1,64,512]{2,1,0:T(8,128)(2,1)S(1)}, u32[]{:S(2)}, u32[]{:S(2)}) %collective-permute-start.10) | collective-permute-done | bytes 65568 | tf_op jit(solution)/shard_map/ppermute | solution.py:240
  30.3 0.1 collective-permute-start.12
  30.4 1.0 %collective-permute-done.14.refs_0_ = bf16[1,64,512]{2,1,0:T(8,128)(2,1)S(1)} collective-permute-done((bf16[1,64,512]{2,1,0:T(8,128)(2,1)S(1)}, bf16[1,64,512]{2,1,0:T(8,128)(2,1)S(1)}, u32[]{:S(2)}, u32[]{:S(2)}) %collective-permute-start.14) | collective-permute-done | bytes 65568 | tf_op jit(solution)/shard_map/ppermute | solution.py:240
  31.4 1.4 %collective-permute-done.15.refs_1_ = bf16[1,64,512]{2,1,0:T(8,128)(2,1)S(1)} collective-permute-done((bf16[1,64,512]{2,1,0:T(8,128)(2,1)S(1)}, bf16[1,64,512]{2,1,0:T(8,128)(2,1)S(1)}, u32[]{:S(2)}, u32[]{:S(2)}) %collective-permute-start.15) | collective-permute-done | bytes 65568 | tf_op jit(solution)/shard_map/ppermute | solution.py:240
  32.8 0.1 collective-permute-start.16
  32.9 0.0 collective-permute-done.12.sigma_other.other
  32.9 1.0 %left_products.1 = (f32[4,256,512]{2,1,0:T(8,128)S(1)}, f32[1,4,256,512]{3,2,1,0:T(8,128)S(1)}) custom-call(bf16[4,256,256]{2,1,0:T(8,128)(2,1)S(1)} %get-tuple-element.23._.refs_2_.left_own, bf16[4,256,256]{2,1,0:T(8,128)(2,1)S(1)} %get-tuple-element.26.refs_3_.left_other, bf16[1,256,512]{2,1,0:T(8,128)(2,1)S(1)} %place_own_sector.1.sigma_own.own.refs_1_, ...), custom_call_target="tpu_custom_call" | custom-call | tf_op jit(solution)/shard_map/left_products/pallas_call | solution.py:258
  33.9 0.5 collective-permute-done.16.other
  34.4 1.1 %second_sigma_terms.1 = (f32[1,64,512]{2,1,0:T(8,128)S(1)}, bf16[1,64,512]{2,1,0:T(8,128)(2,1)S(1)}, bf16[1,64,512]{2,1,0:T(8,128)(2,1)S(1)}, bf16[1,64,512]{2,1,0:T(8,128)(2,1)S(1)}) custom-call(f32[4,2,8,128]{3,2,1,0:T(8,128)S(1)} %get-tuple-element.37.mixing, bf16[4,256,256]{2,1,0:T(8,128)(2,1)S(1)} %get-tuple-element.26.refs_3_.left_other, ...), custom_call_target="tpu_custom_call" | custom-call | tf_op jit(solution)/shard_map/second_sigma_terms/pallas_call | solution.py:258
  35.6 1.8 %collective-permute-start.17 = (bf16[1,64,512]{2,1,0:T(8,128)(2,1)S(1)}, bf16[1,64,512]{2,1,0:T(8,128)(2,1)S(1)}, u32[]{:S(2)}, u32[]{:S(2)}) collective-permute-start(bf16[1,64,512]{2,1,0:T(8,128)(2,1)S(1)} %get-tuple-element.41), channel_id=1, source_target_pairs={{12,0},{8,4},{4,8},{0,12},{13,1},{9,5},{5,9},{1,13},{14,2},{10,6},... | collective-permute-start | bytes 196616 | tf_op jit(solution)/shard_map/ppermute | solution.py:240
  37.4 1.0 %collective-permute-start.18 = (bf16[1,64,512]{2,1,0:T(8,128)(2,1)S(1)}, bf16[1,64,512]{2,1,0:T(8,128)(2,1)S(1)}, u32[]{:S(2)}, u32[]{:S(2)}) collective-permute-start(bf16[1,64,512]{2,1,0:T(8,128)(2,1)S(1)} %get-tuple-element.42), channel_id=1, source_target_pairs={{8,0},{12,4},{0,8},{4,12},{9,1},{13,5},{1,9},{5,13},{10,2},{14,6},... | collective-permute-start | bytes 196616 | tf_op jit(solution)/shard_map/ppermute | solution.py:240
  38.3 1.7 %collective-permute-start.19 = (bf16[1,64,512]{2,1,0:T(8,128)(2,1)S(1)}, bf16[1,64,512]{2,1,0:T(8,128)(2,1)S(1)}, u32[]{:S(2)}, u32[]{:S(2)}) collective-permute-start(bf16[1,64,512]{2,1,0:T(8,128)(2,1)S(1)} %get-tuple-element.43), channel_id=1, source_target_pairs={{4,0},{0,4},{12,8},{8,12},{5,1},{1,5},{13,9},{9,13},{6,2},{2,6},{1... | collective-permute-start | bytes 196616 | tf_op jit(solution)/shard_map/ppermute | solution.py:240
  40.0 0.5 sums_for_rayleigh.1.refs_0_.refs_5_
  40.5 1.6 %collective-permute-start.13 = (f32[3,8,128]{2,1,0:T(8,128)S(1)}, f32[3,8,128]{2,1,0:T(8,128)S(1)}, u32[]{:S(2)}, u32[]{:S(2)}) collective-permute-start(f32[3,8,128]{2,1,0:T(8,128)S(1)} %sums_for_rayleigh.1.refs_0_.refs_5_), channel_id=1, source_target_pairs={{2,0},{0,2},{3,1},{1,3},{6,4},{4,6},{7,5},{5,7},{10,8},{8,10},{11,... | collective-permute-start | bytes 36872 | tf_op jit(solution)/shard_map/ppermute | solution.py:240
  42.1 2.2 %collective-permute-done.13.refs_1_.refs_6_ = f32[3,8,128]{2,1,0:T(8,128)S(1)} collective-permute-done((f32[3,8,128]{2,1,0:T(8,128)S(1)}, f32[3,8,128]{2,1,0:T(8,128)S(1)}, u32[]{:S(2)}, u32[]{:S(2)}) %collective-permute-start.13) | collective-permute-done | bytes 12320 | tf_op jit(solution)/shard_map/ppermute | solution.py:240
  44.3 0.0 collective-permute-done.17.refs_1_
  44.3 0.5 collective-permute-done.18.refs_2_
  44.8 0.0 collective-permute-done.19.refs_3_
  44.8 2.0 %collective-permute-start.20 = (bf16[1,64,512]{2,1,0:T(8,128)(2,1)S(1)}, bf16[1,64,512]{2,1,0:T(8,128)(2,1)S(1)}, u32[]{:S(2)}, u32[]{:S(2)}) collective-permute-start(bf16[1,64,512]{2,1,0:T(8,128)(2,1)S(1)} %sum_second_sigma.1.refs_5_), channel_id=1, source_target_pairs={{12,0},{8,4},{4,8},{0,12},{13,1},{9,5},{5,9},{1,13},{14,2},{10,6},... | collective-permute-start | bytes 196616 | tf_op jit(solution)/shard_map/ppermute | solution.py:240
  46.9 0.0 collective-permute-start.21
  46.9 2.4 %collective-permute-start.22 = (bf16[1,64,512]{2,1,0:T(8,128)(2,1)S(1)}, bf16[1,64,512]{2,1,0:T(8,128)(2,1)S(1)}, u32[]{:S(2)}, u32[]{:S(2)}) collective-permute-start(bf16[1,64,512]{2,1,0:T(8,128)(2,1)S(1)} %sum_second_sigma.1.refs_5_), channel_id=1, source_target_pairs={{4,0},{0,4},{12,8},{8,12},{5,1},{1,5},{13,9},{9,13},{6,2},{2,6},{1... | collective-permute-start | bytes 196616 | tf_op jit(solution)/shard_map/ppermute | solution.py:240
  49.3 1.4 %second_wave.1 = (bf16[1,256,512]{2,1,0:T(8,128)(2,1)}, f32[2,8,128]{2,1,0:T(8,128)S(1)}) custom-call(s32[2,2]{1,0:T(2,128)S(1)} %copy-done.3, bf16[256,512]{1,0:T(8,128)(2,1)S(1)} %get-tuple-element.24.refs_5_.wave_own, bf16[1,256,512]{2,1,0:T(8,128)(2,1)S(1)} %place_own_sector.1.sigma_own.own.refs_1_, f32[3,8,128]{2,1,0:T(8,128)S(1)} %sums_for_rayleigh.1.refs_0_.refs_5_, ...), custom_call_target="tpu_custom_call" | custom-call | tf_op jit(solution)/shard_map/second_wave/pallas_call | solution.py:258
  50.7 0.9 %collective-permute-done.20.refs_2_ = bf16[1,64,512]{2,1,0:T(8,128)(2,1)S(1)} collective-permute-done((bf16[1,64,512]{2,1,0:T(8,128)(2,1)S(1)}, bf16[1,64,512]{2,1,0:T(8,128)(2,1)S(1)}, u32[]{:S(2)}, u32[]{:S(2)}) %collective-permute-start.20) | collective-permute-done | bytes 65568 | tf_op jit(solution)/shard_map/ppermute | solution.py:240
  51.6 1.6 %collective-permute-done.21.refs_3_ = bf16[1,64,512]{2,1,0:T(8,128)(2,1)S(1)} collective-permute-done((bf16[1,64,512]{2,1,0:T(8,128)(2,1)S(1)}, bf16[1,64,512]{2,1,0:T(8,128)(2,1)S(1)}, u32[]{:S(2)}, u32[]{:S(2)}) %collective-permute-start.21) | collective-permute-done | bytes 65568 | tf_op jit(solution)/shard_map/ppermute | solution.py:240
  53.3 0.0 collective-permute-done.22.refs_4_
  53.3 0.9 %join_second_sigma.1 = f32[1,256,512]{2,1,0:T(8,128)} custom-call(f32[2,8,128]{2,1,0:T(8,128)S(1)} %get-tuple-element.36.refs_0_, bf16[1,256,512]{2,1,0:T(8,128)(2,1)S(1)} %place_own_sector.1.sigma_own.own.refs_1_, bf16[1,64,512]{2,1,0:T(8,128)(2,1)S(1)} %collective-permute-done.20.refs_2_, bf16[1,64,512]{2,1,0:T(8,128)(2,1)S(1)} %collective-permute-done.21.refs_3_, ...), custom_call_target="tpu_custom_call" | custom-call | tf_op jit(solution)/shard_map/join_second_sigma/pallas_call | solution.py:258
  (6 shorter events, 0.1 us)
Async XLA Ops:
  0.6 2.0 %copy-start.1 = (bf16[1,256,512]{2,1,0:T(8,128)(2,1)S(1)}, bf16[1,256,512]{2,1,0:T(8,128)(2,1)}, u32[]{:S(2)}) copy-start(bf16[1,256,512]{2,1,0:T(8,128)(2,1)} %wave.1) | copy-start | bytes 786436
  0.6 2.0 %copy-start.3 = (s32[2,2]{1,0:T(2,128)S(1)}, s32[2,2]{1,0:T(2,128)}, u32[]{:S(2)}) copy-start(s32[2,2]{1,0:T(2,128)} %sizes_ref.3) | copy-start | bytes 52
  0.7 2.0 %copy-start.2 = (s32[4,8,2]{1,2,0:T(2,128)S(1)}, s32[4,8,2]{1,2,0:T(2,128)}, u32[]{:S(2)}) copy-start(s32[4,8,2]{1,2,0:T(2,128)} %param.10) | copy-start | bytes 772
  0.7 2.0 %copy-start.4 = (f32[4,8]{1,0:T(4,128)S(1)}, f32[4,8]{1,0:T(4,128)}, u32[]{:S(2)}) copy-start(f32[4,8]{1,0:T(4,128)} %weights_ref.1) | copy-start | bytes 388
  0.7 2.2 %copy-start = (bf16[4,512,512]{2,1,0:T(8,128)(2,1)S(1)}, bf16[4,512,512]{2,1,0:T(8,128)(2,1)}, u32[]{:S(2)}) copy-start(bf16[4,512,512]{2,1,0:T(8,128)(2,1)} %right.1) | copy-start | bytes 6291460
  0.7 2.2 %collective-permute-start = (bf16[1,256,512]{2,1,0:T(8,128)(2,1)}, bf16[1,256,512]{2,1,0:T(8,128)(2,1)S(1)}, u32[]{:S(2)}, u32[]{:S(2)}) collective-permute-start(bf16[1,256,512]{2,1,0:T(8,128)(2,1)} %wave.1), channel_id=1, source_target_pairs={{1,0},{0,1},{3,2},{2,3},{5,4},{4,5},{7,6},{6,7},{9,8},{8,9},{11,10... | collective-permute-start | bytes 786440 | tf_op jit(solution)/shard_map/ppermute | solution.py:240
  4.5 8.6 %collective-permute-start.1 = (bf16[2,64,512]{2,1,0:T(8,128)(2,1)S(1)}, bf16[2,64,512]{2,1,0:T(8,128)(2,1)S(1)}, u32[]{:S(2)}, u32[]{:S(2)}) collective-permute-start(bf16[2,64,512]{2,1,0:T(8,128)(2,1)S(1)} %get-tuple-element.28), channel_id=1, source_target_pairs={{2,0},{0,2},{3,1},{1,3},{6,4},{4,6},{7,5},{5,7},{10,8},{8,10},{11,... | collective-permute-start | bytes 393224 | tf_op jit(solution)/shard_map/ppermute | solution.py:240
  7.3 10.4 %collective-permute-start.3 = (bf16[1,64,512]{2,1,0:T(8,128)(2,1)S(1)}, bf16[1,64,512]{2,1,0:T(8,128)(2,1)S(1)}, u32[]{:S(2)}, u32[]{:S(2)}) collective-permute-start(bf16[1,64,512]{2,1,0:T(8,128)(2,1)S(1)} %get-tuple-element.29), channel_id=1, source_target_pairs={{8,0},{12,4},{0,8},{4,12},{9,1},{13,5},{1,9},{5,13},{10,2},{14,6},... | collective-permute-start | bytes 196616 | tf_op jit(solution)/shard_map/ppermute | solution.py:240
  9.9 7.8 %collective-permute-start.4 = (bf16[1,64,512]{2,1,0:T(8,128)(2,1)S(1)}, bf16[1,64,512]{2,1,0:T(8,128)(2,1)S(1)}, u32[]{:S(2)}, u32[]{:S(2)}) collective-permute-start(bf16[1,64,512]{2,1,0:T(8,128)(2,1)S(1)} %get-tuple-element.30), channel_id=1, source_target_pairs={{4,0},{0,4},{12,8},{8,12},{5,1},{1,5},{13,9},{9,13},{6,2},{2,6},{1... | collective-permute-start | bytes 196616 | tf_op jit(solution)/shard_map/ppermute | solution.py:240
  11.5 8.4 %collective-permute-start.5 = (bf16[1,64,512]{2,1,0:T(8,128)(2,1)S(1)}, bf16[1,64,512]{2,1,0:T(8,128)(2,1)S(1)}, u32[]{:S(2)}, u32[]{:S(2)}) collective-permute-start(bf16[1,64,512]{2,1,0:T(8,128)(2,1)S(1)} %get-tuple-element.31), channel_id=1, source_target_pairs={{10,0},{8,2},{14,4},{12,6},{2,8},{0,10},{6,12},{4,14},{11,1},{9,3}... | collective-permute-start | bytes 196616 | tf_op jit(solution)/shard_map/ppermute | solution.py:240
  11.8 8.1 %collective-permute-start.6 = (bf16[1,64,512]{2,1,0:T(8,128)(2,1)S(1)}, bf16[1,64,512]{2,1,0:T(8,128)(2,1)S(1)}, u32[]{:S(2)}, u32[]{:S(2)}) collective-permute-start(bf16[1,64,512]{2,1,0:T(8,128)(2,1)S(1)} %get-tuple-element.32), channel_id=1, source_target_pairs={{6,0},{4,2},{2,4},{0,6},{14,8},{12,10},{10,12},{8,14},{7,1},{5,3},... | collective-permute-start | bytes 196616 | tf_op jit(solution)/shard_map/ppermute | solution.py:240
  13.2 6.7 %collective-permute-start.2 = (bf16[1,64,512]{2,1,0:T(8,128)(2,1)S(1)}, bf16[1,64,512]{2,1,0:T(8,128)(2,1)S(1)}, u32[]{:S(2)}, u32[]{:S(2)}) collective-permute-start(bf16[1,64,512]{2,1,0:T(8,128)(2,1)S(1)} %sum_far_share.1), channel_id=1, source_target_pairs={{12,0},{8,4},{4,8},{0,12},{13,1},{9,5},{5,9},{1,13},{14,2},{10,6},... | collective-permute-start | bytes 196616 | tf_op jit(solution)/shard_map/ppermute | solution.py:240
  20.0 6.0 %collective-permute-start.9 = (bf16[1,64,512]{2,1,0:T(8,128)(2,1)S(1)}, bf16[1,64,512]{2,1,0:T(8,128)(2,1)S(1)}, u32[]{:S(2)}, u32[]{:S(2)}) collective-permute-start(bf16[1,64,512]{2,1,0:T(8,128)(2,1)S(1)} %sum_first_sigma.1.refs_5_), channel_id=1, source_target_pairs={{8,0},{12,4},{0,8},{4,12},{9,1},{13,5},{1,9},{5,13},{10,2},{14,6},... | collective-permute-start | bytes 196616 | tf_op jit(solution)/shard_map/ppermute | solution.py:240
  21.0 6.6 %collective-permute-start.7 = (bf16[1,64,512]{2,1,0:T(8,128)(2,1)S(1)}, bf16[1,64,512]{2,1,0:T(8,128)(2,1)S(1)}, u32[]{:S(2)}, u32[]{:S(2)}) collective-permute-start(bf16[1,64,512]{2,1,0:T(8,128)(2,1)S(1)} %sum_first_sigma.1.refs_5_), channel_id=1, source_target_pairs={{6,0},{4,2},{2,4},{0,6},{14,8},{12,10},{10,12},{8,14},{7,1},{5,3},... | collective-permute-start | bytes 196616 | tf_op jit(solution)/shard_map/ppermute | solution.py:240
  23.6 5.9 %collective-permute-start.8 = (bf16[1,64,512]{2,1,0:T(8,128)(2,1)S(1)}, bf16[1,64,512]{2,1,0:T(8,128)(2,1)S(1)}, u32[]{:S(2)}, u32[]{:S(2)}) collective-permute-start(bf16[1,64,512]{2,1,0:T(8,128)(2,1)S(1)} %sum_first_sigma.1.refs_5_), channel_id=1, source_target_pairs={{2,0},{0,2},{3,1},{1,3},{6,4},{4,6},{7,5},{5,7},{10,8},{8,10},{11,... | collective-permute-start | bytes 196616 | tf_op jit(solution)/shard_map/ppermute | solution.py:240
  25.1 4.4 %collective-permute-start.11 = (bf16[1,64,512]{2,1,0:T(8,128)(2,1)S(1)}, bf16[1,64,512]{2,1,0:T(8,128)(2,1)S(1)}, u32[]{:S(2)}, u32[]{:S(2)}) collective-permute-start(bf16[1,64,512]{2,1,0:T(8,128)(2,1)S(1)} %sum_first_sigma.1.refs_5_), channel_id=1, source_target_pairs={{4,0},{0,4},{12,8},{8,12},{5,1},{1,5},{13,9},{9,13},{6,2},{2,6},{1... | collective-permute-start | bytes 196616 | tf_op jit(solution)/shard_map/ppermute | solution.py:240
  26.0 4.3 %collective-permute-start.10 = (bf16[1,64,512]{2,1,0:T(8,128)(2,1)S(1)}, bf16[1,64,512]{2,1,0:T(8,128)(2,1)S(1)}, u32[]{:S(2)}, u32[]{:S(2)}) collective-permute-start(bf16[1,64,512]{2,1,0:T(8,128)(2,1)S(1)} %collective-permute-done.9.refs_2_), channel_id=1, source_target_pairs={{4,0},{0,4},{12,8},{8,12},{5,1},{1,5},{13,9},{9,13},{6,2},{2,6},{1... | collective-permute-start | bytes 196616 | tf_op jit(solution)/shard_map/ppermute | solution.py:240
  27.1 4.3 %collective-permute-start.14 = (bf16[1,64,512]{2,1,0:T(8,128)(2,1)S(1)}, bf16[1,64,512]{2,1,0:T(8,128)(2,1)S(1)}, u32[]{:S(2)}, u32[]{:S(2)}) collective-permute-start(bf16[1,64,512]{2,1,0:T(8,128)(2,1)S(1)} %collective-permute-done.9.refs_2_), channel_id=1, source_target_pairs={{2,0},{0,2},{3,1},{1,3},{6,4},{4,6},{7,5},{5,7},{10,8},{8,10},{11,... | collective-permute-start | bytes 196616 | tf_op jit(solution)/shard_map/ppermute | solution.py:240
  27.6 5.2 %collective-permute-start.15 = (bf16[1,64,512]{2,1,0:T(8,128)(2,1)S(1)}, bf16[1,64,512]{2,1,0:T(8,128)(2,1)S(1)}, u32[]{:S(2)}, u32[]{:S(2)}) collective-permute-start(bf16[1,64,512]{2,1,0:T(8,128)(2,1)S(1)} %collective-permute-done.9.refs_2_), channel_id=1, source_target_pairs={{6,0},{4,2},{2,4},{0,6},{14,8},{12,10},{10,12},{8,14},{7,1},{5,3},... | collective-permute-start | bytes 196616 | tf_op jit(solution)/shard_map/ppermute | solution.py:240
  30.3 2.6 %collective-permute-start.12 = (bf16[1,256,512]{2,1,0:T(8,128)(2,1)S(1)}, bf16[1,256,512]{2,1,0:T(8,128)(2,1)S(1)}, u32[]{:S(2)}, u32[]{:S(2)}) collective-permute-start(bf16[1,256,512]{2,1,0:T(8,128)(2,1)S(1)} %place_own_sector.1.sigma_own.own.refs_1_), channel_id=1, source_target_pairs={{1,0},{0,1},{3,2},{2,3},{5,4},{4,5},{7,6},{6,7},{9,8},{8,9},{11,10... | collective-permute-start | bytes 786440 | tf_op jit(solution)/shard_map/ppermute | solution.py:240
  32.8 1.6 %collective-permute-start.16 = (bf16[1,256,512]{2,1,0:T(8,128)(2,1)S(1)}, bf16[1,256,512]{2,1,0:T(8,128)(2,1)S(1)}, u32[]{:S(2)}, u32[]{:S(2)}) collective-permute-start(bf16[1,256,512]{2,1,0:T(8,128)(2,1)S(1)} %place_other_sectors.1.across_own), channel_id=1, source_target_pairs={{1,0},{0,1},{3,2},{2,3},{5,4},{4,5},{7,6},{6,7},{9,8},{8,9},{11,10... | collective-permute-start | bytes 786440 | tf_op jit(solution)/shard_map/ppermute | solution.py:240
  35.6 8.7 %collective-permute-start.17 = (bf16[1,64,512]{2,1,0:T(8,128)(2,1)S(1)}, bf16[1,64,512]{2,1,0:T(8,128)(2,1)S(1)}, u32[]{:S(2)}, u32[]{:S(2)}) collective-permute-start(bf16[1,64,512]{2,1,0:T(8,128)(2,1)S(1)} %get-tuple-element.41), channel_id=1, source_target_pairs={{12,0},{8,4},{4,8},{0,12},{13,1},{9,5},{5,9},{1,13},{14,2},{10,6},... | collective-permute-start | bytes 196616 | tf_op jit(solution)/shard_map/ppermute | solution.py:240
  37.4 7.4 %collective-permute-start.18 = (bf16[1,64,512]{2,1,0:T(8,128)(2,1)S(1)}, bf16[1,64,512]{2,1,0:T(8,128)(2,1)S(1)}, u32[]{:S(2)}, u32[]{:S(2)}) collective-permute-start(bf16[1,64,512]{2,1,0:T(8,128)(2,1)S(1)} %get-tuple-element.42), channel_id=1, source_target_pairs={{8,0},{12,4},{0,8},{4,12},{9,1},{13,5},{1,9},{5,13},{10,2},{14,6},... | collective-permute-start | bytes 196616 | tf_op jit(solution)/shard_map/ppermute | solution.py:240
  38.3 6.5 %collective-permute-start.19 = (bf16[1,64,512]{2,1,0:T(8,128)(2,1)S(1)}, bf16[1,64,512]{2,1,0:T(8,128)(2,1)S(1)}, u32[]{:S(2)}, u32[]{:S(2)}) collective-permute-start(bf16[1,64,512]{2,1,0:T(8,128)(2,1)S(1)} %get-tuple-element.43), channel_id=1, source_target_pairs={{4,0},{0,4},{12,8},{8,12},{5,1},{1,5},{13,9},{9,13},{6,2},{2,6},{1... | collective-permute-start | bytes 196616 | tf_op jit(solution)/shard_map/ppermute | solution.py:240
  40.5 3.8 %collective-permute-start.13 = (f32[3,8,128]{2,1,0:T(8,128)S(1)}, f32[3,8,128]{2,1,0:T(8,128)S(1)}, u32[]{:S(2)}, u32[]{:S(2)}) collective-permute-start(f32[3,8,128]{2,1,0:T(8,128)S(1)} %sums_for_rayleigh.1.refs_0_.refs_5_), channel_id=1, source_target_pairs={{2,0},{0,2},{3,1},{1,3},{6,4},{4,6},{7,5},{5,7},{10,8},{8,10},{11,... | collective-permute-start | bytes 36872 | tf_op jit(solution)/shard_map/ppermute | solution.py:240
  44.8 6.8 %collective-permute-start.20 = (bf16[1,64,512]{2,1,0:T(8,128)(2,1)S(1)}, bf16[1,64,512]{2,1,0:T(8,128)(2,1)S(1)}, u32[]{:S(2)}, u32[]{:S(2)}) collective-permute-start(bf16[1,64,512]{2,1,0:T(8,128)(2,1)S(1)} %sum_second_sigma.1.refs_5_), channel_id=1, source_target_pairs={{12,0},{8,4},{4,8},{0,12},{13,1},{9,5},{5,9},{1,13},{14,2},{10,6},... | collective-permute-start | bytes 196616 | tf_op jit(solution)/shard_map/ppermute | solution.py:240
  46.9 6.4 %collective-permute-start.21 = (bf16[1,64,512]{2,1,0:T(8,128)(2,1)S(1)}, bf16[1,64,512]{2,1,0:T(8,128)(2,1)S(1)}, u32[]{:S(2)}, u32[]{:S(2)}) collective-permute-start(bf16[1,64,512]{2,1,0:T(8,128)(2,1)S(1)} %sum_second_sigma.1.refs_5_), channel_id=1, source_target_pairs={{8,0},{12,4},{0,8},{4,12},{9,1},{13,5},{1,9},{5,13},{10,2},{14,6},... | collective-permute-start | bytes 196616 | tf_op jit(solution)/shard_map/ppermute | solution.py:240
  46.9 6.4 %collective-permute-start.22 = (bf16[1,64,512]{2,1,0:T(8,128)(2,1)S(1)}, bf16[1,64,512]{2,1,0:T(8,128)(2,1)S(1)}, u32[]{:S(2)}, u32[]{:S(2)}) collective-permute-start(bf16[1,64,512]{2,1,0:T(8,128)(2,1)S(1)} %sum_second_sigma.1.refs_5_), channel_id=1, source_target_pairs={{4,0},{0,4},{12,8},{8,12},{5,1},{1,5},{13,9},{9,13},{6,2},{2,6},{1... | collective-permute-start | bytes 196616 | tf_op jit(solution)/shard_map/ppermute | solution.py:240

commit v23 on v19

--- a/solution.py
+++ b/solution.py
@@ -211,18 +211,18 @@
     second[0] = (sigma_factor * sigma - wave_factor * wave).astype(second.dtype)
 
 
-def join_kernel(order, factors, sigma_own, *refs):
-    pieces, (out, held, sems) = refs[:-3], refs[-3:]
+def join_kernel(steps, factors, sigma_own, *refs):
+    pieces, (out, held, sems) = refs[: len(steps)], refs[-3:]
     _, share, columns = pieces[0].shape
     place = lax.axis_index("ops")
     scale = jnp.broadcast_to(factors[0][:1, :1], (share, columns))
     shift = jnp.broadcast_to(factors[1][:1, :1], (share, columns))
     copies = []
-    for step, piece in zip(order, pieces):
+    for index, (step, piece) in enumerate(zip(steps, pieces)):
         rows = pl.ds(pl.multiple_of((place ^ step) * share, share), share)
         moved = shift * sigma_own[0, rows, :].astype(jnp.float32)
-        held[step] = scale * piece[0].astype(jnp.float32) - moved
-        copies.append(pltpu.make_async_copy(held.at[step], out.at[0, rows], sems.at[step]))
+        held[index] = scale * piece[0].astype(jnp.float32) - moved
+        copies.append(pltpu.make_async_copy(held.at[index], out.at[0, rows], sems.at[index]))
         copies[-1].start()
     for copy in copies:
         copy.wait()
@@ -419,20 +419,31 @@
         sigma_own,
         *sums,
     )
-    second_sigma = call(
-        lambda *refs: join_kernel(farthest_first, *refs),
-        "join_second_sigma",
-        shape(1, rows, columns, dtype=f32),
-        [],
-        factors,
-        sigma_own,
-        *[partner(second_share, {"ops": step}) for step in farthest_first],
-        scratch=[
-            pltpu.VMEM((ops_count, share, columns), f32),
-            pltpu.SemaphoreType.DMA((ops_count,)),
-        ],
-        out=outside,
-    )
+    arrived = {along: partner(second_share, {"ops": along}) for along in farthest_first}
+    early = [farthest_first[0], 0]
+    late = farthest_first[1:-1]
+    second_sigma = None
+    for steps, name in ((early, "join_early_shares"), (late, "join_late_shares")):
+        operands = [factors, sigma_own, *[arrived[along] for along in steps]]
+        specs = [inside] * len(operands)
+        aliases = {}
+        if second_sigma is not None:
+            aliases = {len(operands): 0}
+            operands.append(second_sigma)
+            specs.append(outside)
+        second_sigma = pl.pallas_call(
+            lambda *refs, steps=steps: join_kernel(steps, *refs),
+            out_shape=shape(1, rows, columns, dtype=f32),
+            in_specs=specs,
+            out_specs=outside,
+            input_output_aliases=aliases,
+            scratch_shapes=[
+                pltpu.VMEM((len(steps), share, columns), f32),
+                pltpu.SemaphoreType.DMA((len(steps),)),
+            ],
+            compiler_params=pltpu.CompilerParams(vmem_limit_bytes=16 * mebibyte),
+            name=name,
+        )(*operands)
     return (second_wave, second_sigma)
 
 

time: 53.5 us -> 53.4 us (level)
  waiting for transfers between devices: 12 us -> 11.2 us
  Pallas kernels: 9.11 us -> 9.78 us
    pallas_call x0 -> x2, Pallas kernels: none -> 1.54 us  [local(): pl.pallas_call(lambda *refs, steps=steps: join_kernel(steps, *refs), out_...]
    pallas_call x14 -> x13, Pallas kernels: 9.11 us -> 8.24 us  [call(): pl.pallas_call(kernel, out_shape=out_shape, in_specs=list(in_specs) + [in...]
    ppermute x23, waiting for transfers between devices: 12 us -> 11.2 us  [partner(): return lax.ppermute(value, axes, pairs)]
  transfers between devices with their start and end apart: 23 -> 23, of which waited for: 12 -> 12; matrix products, arithmetic and copies ran while one was open for 0% -> 0% of each run, Pallas kernels for 10% -> 12%
where the time goes in v23:
time: 53.4 us; the launch traced here: 53.2 us
  starting transfers between devices  31.4 us (59%)
  waiting for transfers between devices  11.2 us (21%)
  Pallas kernels  9.78 us (18%)
  between operations  0.86 us (2%)
    ppermute x23, starting transfers between devices, partner(): return lax.ppermute(value, axes, pairs)  31.4 us
    ppermute x23, waiting for transfers between devices, partner(): return lax.ppermute(value, axes, pairs)  11.2 us
    pallas_call x13, Pallas kernels, call(): pl.pallas_call(kernel, out_shape=out_shape, in_specs=list(in_specs) + [in...  8.24 us
    pallas_call x2, Pallas kernels, local(): pl.pallas_call(lambda *refs, steps=steps: join_kernel(steps, *refs), out_...  1.54 us
  transfers between devices with their start and end apart: 23, of which 12 were waited for; matrix products, arithmetic and copies ran while one was open for 0% of the time, Pallas kernels for 12%

profile of v23, /device:TPU:0, one launch (start us, length us, event | category | flops | bytes accessed | tf_op | source)
XLA Modules:
  0.0 53.2 jit_solution(5695752702996837085)
XLA Ops:
  0.6 0.0 copy-start.1
  0.6 0.0 copy-start.3
  0.7 0.0 copy-start.2
  0.7 0.0 copy-start.4
  0.7 0.0 copy-start
  0.7 0.5 collective-permute-start
  1.2 1.4 %load_operators.1 = (bf16[4,256,256]{2,1,0:T(8,128)(2,1)S(1)}, bf16[4,256,256]{2,1,0:T(8,128)(2,1)S(1)}) custom-call(bf16[4,512,512]{2,1,0:T(8,128)(2,1)} %left_ref.1), custom_call_target="tpu_custom_call" | custom-call | tf_op jit(solution)/shard_map/load_operators/pallas_call | solution.py:262
  2.6 0.0 copy-done.1
  2.6 0.0 copy-done.3
  2.7 0.2 tables_for_first_sigma.1
  2.9 0.0 collective-permute-done.refs_6_
  2.9 1.6 %first_sigma_terms.1 = (bf16[256,512]{1,0:T(8,128)(2,1)S(1)}, f32[2,64,512]{2,1,0:T(8,128)S(1)}, bf16[2,64,512]{2,1,0:T(8,128)(2,1)S(1)}, bf16[1,64,512]{2,1,0:T...) custom-call(s32[2,2]{1,0:T(2,128)S(1)} %copy-done.3, ...), custom_call_target="tpu_custom_call" | custom-call | tf_op jit(solution)/shard_map/first_sigma_terms/pallas_call | solution.py:262
  4.5 2.8 %collective-permute-start.1 = (bf16[2,64,512]{2,1,0:T(8,128)(2,1)S(1)}, bf16[2,64,512]{2,1,0:T(8,128)(2,1)S(1)}, u32[]{:S(2)}, u32[]{:S(2)}) collective-permute-start(bf16[2,64,512]{2,1,0:T(8,128)(2,1)S(1)} %get-tuple-element.28), channel_id=1, source_target_pairs={{2,0},{0,2},{3,1},{1,3},{6,4},{4,6},{7,5},{5,7},{10,8},{8,10},{11,... | collective-permute-start | bytes 393224 | tf_op jit(solution)/shard_map/ppermute | solution.py:244
  7.3 2.6 %collective-permute-start.3 = (bf16[1,64,512]{2,1,0:T(8,128)(2,1)S(1)}, bf16[1,64,512]{2,1,0:T(8,128)(2,1)S(1)}, u32[]{:S(2)}, u32[]{:S(2)}) collective-permute-start(bf16[1,64,512]{2,1,0:T(8,128)(2,1)S(1)} %get-tuple-element.29), channel_id=1, source_target_pairs={{8,0},{12,4},{0,8},{4,12},{9,1},{13,5},{1,9},{5,13},{10,2},{14,6},... | collective-permute-start | bytes 196616 | tf_op jit(solution)/shard_map/ppermute | solution.py:244
  9.9 1.6 %collective-permute-start.4 = (bf16[1,64,512]{2,1,0:T(8,128)(2,1)S(1)}, bf16[1,64,512]{2,1,0:T(8,128)(2,1)S(1)}, u32[]{:S(2)}, u32[]{:S(2)}) collective-permute-start(bf16[1,64,512]{2,1,0:T(8,128)(2,1)S(1)} %get-tuple-element.30), channel_id=1, source_target_pairs={{4,0},{0,4},{12,8},{8,12},{5,1},{1,5},{13,9},{9,13},{6,2},{2,6},{1... | collective-permute-start | bytes 196616 | tf_op jit(solution)/shard_map/ppermute | solution.py:244
  11.5 0.3 collective-permute-start.5
  11.8 1.4 %collective-permute-start.6 = (bf16[1,64,512]{2,1,0:T(8,128)(2,1)S(1)}, bf16[1,64,512]{2,1,0:T(8,128)(2,1)S(1)}, u32[]{:S(2)}, u32[]{:S(2)}) collective-permute-start(bf16[1,64,512]{2,1,0:T(8,128)(2,1)S(1)} %get-tuple-element.32), channel_id=1, source_target_pairs={{6,0},{4,2},{2,4},{0,6},{14,8},{12,10},{10,12},{8,14},{7,1},{5,3},... | collective-permute-start | bytes 196616 | tf_op jit(solution)/shard_map/ppermute | solution.py:244
  13.1 0.0 collective-permute-done.1.refs_1_
  13.2 3.7 %collective-permute-start.2 = (bf16[1,64,512]{2,1,0:T(8,128)(2,1)S(1)}, bf16[1,64,512]{2,1,0:T(8,128)(2,1)S(1)}, u32[]{:S(2)}, u32[]{:S(2)}) collective-permute-start(bf16[1,64,512]{2,1,0:T(8,128)(2,1)S(1)} %sum_far_share.1), channel_id=1, source_target_pairs={{12,0},{8,4},{4,8},{0,12},{13,1},{9,5},{5,9},{1,13},{14,2},{10,6},... | collective-permute-start | bytes 196616 | tf_op jit(solution)/shard_map/ppermute | solution.py:244
  16.8 0.8 %tables_for_second_sigma.1 = (f32[4,2,8,128]{3,2,1,0:T(8,128)S(1)}, f32[256,512]{1,0:T(8,128)S(1)}) custom-call(s32[2,2]{1,0:T(2,128)S(1)} %copy-done.3, s32[4,2,8]{2,1,0:T(2,128)S(1)} %bitcast.2, f32[4,8]{1,0:T(4,128)S(1)} %copy-done.4, bf16[256,512]{1,0:T(8,128)(2,1)S(1)} %get-tuple-element.33._.wave_other), custom_call_target="tpu_custom_call" | custom-call | tf_op jit(solution)/shard_map/tables_for_second_sigma/pallas_call | solution.py:262
  17.6 0.0 collective-permute-done.3.refs_3_
  17.7 0.0 collective-permute-done.4.refs_4_
  17.7 2.2 %collective-permute-done.5.refs_5_ = bf16[1,64,512]{2,1,0:T(8,128)(2,1)S(1)} collective-permute-done((bf16[1,64,512]{2,1,0:T(8,128)(2,1)S(1)}, bf16[1,64,512]{2,1,0:T(8,128)(2,1)S(1)}, u32[]{:S(2)}, u32[]{:S(2)}) %collective-permute-start.5) | collective-permute-done | bytes 65568 | tf_op jit(solution)/shard_map/ppermute | solution.py:244
  19.9 0.0 collective-permute-done.6.refs_6_
  19.9 0.0 collective-permute-done.2.refs_2_
  19.9 0.1 sum_first_sigma.1.refs_3_
  20.0 1.1 %collective-permute-start.7 = (bf16[1,64,512]{2,1,0:T(8,128)(2,1)S(1)}, bf16[1,64,512]{2,1,0:T(8,128)(2,1)S(1)}, u32[]{:S(2)}, u32[]{:S(2)}) collective-permute-start(bf16[1,64,512]{2,1,0:T(8,128)(2,1)S(1)} %sum_first_sigma.1.refs_3_), channel_id=1, source_target_pairs={{8,0},{12,4},{0,8},{4,12},{9,1},{13,5},{1,9},{5,13},{10,2},{14,6},... | collective-permute-start | bytes 196616 | tf_op jit(solution)/shard_map/ppermute | solution.py:244
  21.0 2.1 %collective-permute-start.8 = (bf16[1,64,512]{2,1,0:T(8,128)(2,1)S(1)}, bf16[1,64,512]{2,1,0:T(8,128)(2,1)S(1)}, u32[]{:S(2)}, u32[]{:S(2)}) collective-permute-start(bf16[1,64,512]{2,1,0:T(8,128)(2,1)S(1)} %sum_first_sigma.1.refs_3_), channel_id=1, source_target_pairs={{12,0},{8,4},{4,8},{0,12},{13,1},{9,5},{5,9},{1,13},{14,2},{10,6},... | collective-permute-start | bytes 196616 | tf_op jit(solution)/shard_map/ppermute | solution.py:244
  23.1 0.5 collective-permute-start.9
  23.6 2.1 %collective-permute-start.14 = (bf16[1,64,512]{2,1,0:T(8,128)(2,1)S(1)}, bf16[1,64,512]{2,1,0:T(8,128)(2,1)S(1)}, u32[]{:S(2)}, u32[]{:S(2)}) collective-permute-start(bf16[1,64,512]{2,1,0:T(8,128)(2,1)S(1)} %sum_first_sigma.1.refs_3_), channel_id=1, source_target_pairs={{6,0},{4,2},{2,4},{0,6},{14,8},{12,10},{10,12},{8,14},{7,1},{5,3},... | collective-permute-start | bytes 196616 | tf_op jit(solution)/shard_map/ppermute | solution.py:244
  25.7 0.9 %collective-permute-start.15 = (bf16[1,64,512]{2,1,0:T(8,128)(2,1)S(1)}, bf16[1,64,512]{2,1,0:T(8,128)(2,1)S(1)}, u32[]{:S(2)}, u32[]{:S(2)}) collective-permute-start(bf16[1,64,512]{2,1,0:T(8,128)(2,1)S(1)} %sum_first_sigma.1.refs_3_), channel_id=1, source_target_pairs={{2,0},{0,2},{3,1},{1,3},{6,4},{4,6},{7,5},{5,7},{10,8},{8,10},{11,... | collective-permute-start | bytes 196616 | tf_op jit(solution)/shard_map/ppermute | solution.py:244
  26.6 0.1 collective-permute-done.7.refs_0_
  26.7 1.0 %collective-permute-start.12 = (bf16[1,64,512]{2,1,0:T(8,128)(2,1)S(1)}, bf16[1,64,512]{2,1,0:T(8,128)(2,1)S(1)}, u32[]{:S(2)}, u32[]{:S(2)}) collective-permute-start(bf16[1,64,512]{2,1,0:T(8,128)(2,1)S(1)} %collective-permute-done.7.refs_0_), channel_id=1, source_target_pairs={{2,0},{0,2},{3,1},{1,3},{6,4},{4,6},{7,5},{5,7},{10,8},{8,10},{11,... | collective-permute-start | bytes 196616 | tf_op jit(solution)/shard_map/ppermute | solution.py:244
  27.7 0.2 collective-permute-done.8.refs_1_
  27.9 0.9 %collective-permute-start.13 = (bf16[1,64,512]{2,1,0:T(8,128)(2,1)S(1)}, bf16[1,64,512]{2,1,0:T(8,128)(2,1)S(1)}, u32[]{:S(2)}, u32[]{:S(2)}) collective-permute-start(bf16[1,64,512]{2,1,0:T(8,128)(2,1)S(1)} %collective-permute-done.8.refs_1_), channel_id=1, source_target_pairs={{2,0},{0,2},{3,1},{1,3},{6,4},{4,6},{7,5},{5,7},{10,8},{8,10},{11,... | collective-permute-start | bytes 196616 | tf_op jit(solution)/shard_map/ppermute | solution.py:244
  28.8 0.0 collective-permute-done.9.refs_2_
  28.8 0.1 collective-permute-start.10
  28.9 0.2 collective-permute-done.14.refs_2_
  29.0 1.4 %collective-permute-done.15.refs_3_ = bf16[1,64,512]{2,1,0:T(8,128)(2,1)S(1)} collective-permute-done((bf16[1,64,512]{2,1,0:T(8,128)(2,1)S(1)}, bf16[1,64,512]{2,1,0:T(8,128)(2,1)S(1)}, u32[]{:S(2)}, u32[]{:S(2)}) %collective-permute-start.15) | collective-permute-done | bytes 65568 | tf_op jit(solution)/shard_map/ppermute | solution.py:244
  30.4 0.7 %collective-permute-done.12.refs_0_ = bf16[1,64,512]{2,1,0:T(8,128)(2,1)S(1)} collective-permute-done((bf16[1,64,512]{2,1,0:T(8,128)(2,1)S(1)}, bf16[1,64,512]{2,1,0:T(8,128)(2,1)S(1)}, u32[]{:S(2)}, u32[]{:S(2)}) %collective-permute-start.12) | collective-permute-done | bytes 65568 | tf_op jit(solution)/shard_map/ppermute | solution.py:244
  31.1 1.0 %collective-permute-done.13.refs_1_ = bf16[1,64,512]{2,1,0:T(8,128)(2,1)S(1)} collective-permute-done((bf16[1,64,512]{2,1,0:T(8,128)(2,1)S(1)}, bf16[1,64,512]{2,1,0:T(8,128)(2,1)S(1)}, u32[]{:S(2)}, u32[]{:S(2)}) %collective-permute-start.13) | collective-permute-done | bytes 65568 | tf_op jit(solution)/shard_map/ppermute | solution.py:244
  32.2 0.1 collective-permute-start.16
  32.2 0.0 collective-permute-done.10.sigma_other.other
  32.3 1.0 %left_products.1 = (f32[4,256,512]{2,1,0:T(8,128)S(1)}, f32[1,4,256,512]{3,2,1,0:T(8,128)S(1)}) custom-call(bf16[4,256,256]{2,1,0:T(8,128)(2,1)S(1)} %get-tuple-element.23._.refs_2_.left_own, bf16[4,256,256]{2,1,0:T(8,128)(2,1)S(1)} %get-tuple-element.26.refs_3_.left_other, bf16[1,256,512]{2,1,0:T(8,128)(2,1)S(1)} %place_own_sector.1.sigma_own.own.refs_1_, ...), custom_call_target="tpu_custom_call" | custom-call | tf_op jit(solution)/shard_map/left_products/pallas_call | solution.py:262
  33.2 0.5 %collective-permute-done.16.other = bf16[1,256,512]{2,1,0:T(8,128)(2,1)S(1)} collective-permute-done((bf16[1,256,512]{2,1,0:T(8,128)(2,1)S(1)}, bf16[1,256,512]{2,1,0:T(8,128)(2,1)S(1)}, u32[]{:S(2)}, u32[]{:S(2)}) %collective-permute-start.16) | collective-permute-done | bytes 262176 | tf_op jit(solution)/shard_map/ppermute | solution.py:244
  33.8 1.1 %second_sigma_terms.1 = (f32[1,64,512]{2,1,0:T(8,128)S(1)}, bf16[1,64,512]{2,1,0:T(8,128)(2,1)S(1)}, bf16[1,64,512]{2,1,0:T(8,128)(2,1)S(1)}, bf16[1,64,512]{2,1,0:T(8,128)(2,1)S(1)}) custom-call(f32[4,2,8,128]{3,2,1,0:T(8,128)S(1)} %get-tuple-element.37.mixing, bf16[4,256,256]{2,1,0:T(8,128)(2,1)S(1)} %get-tuple-element.26.refs_3_.left_other, ...), custom_call_target="tpu_custom_call" | custom-call | tf_op jit(solution)/shard_map/second_sigma_terms/pallas_call | solution.py:262
  34.9 2.5 %collective-permute-start.17 = (bf16[1,64,512]{2,1,0:T(8,128)(2,1)S(1)}, bf16[1,64,512]{2,1,0:T(8,128)(2,1)S(1)}, u32[]{:S(2)}, u32[]{:S(2)}) collective-permute-start(bf16[1,64,512]{2,1,0:T(8,128)(2,1)S(1)} %get-tuple-element.41), channel_id=1, source_target_pairs={{12,0},{8,4},{4,8},{0,12},{13,1},{9,5},{5,9},{1,13},{14,2},{10,6},... | collective-permute-start | bytes 196616 | tf_op jit(solution)/shard_map/ppermute | solution.py:244
  37.4 0.0 collective-permute-start.18
  37.4 1.9 %collective-permute-start.19 = (bf16[1,64,512]{2,1,0:T(8,128)(2,1)S(1)}, bf16[1,64,512]{2,1,0:T(8,128)(2,1)S(1)}, u32[]{:S(2)}, u32[]{:S(2)}) collective-permute-start(bf16[1,64,512]{2,1,0:T(8,128)(2,1)S(1)} %get-tuple-element.43), channel_id=1, source_target_pairs={{4,0},{0,4},{12,8},{8,12},{5,1},{1,5},{13,9},{9,13},{6,2},{2,6},{1... | collective-permute-start | bytes 196616 | tf_op jit(solution)/shard_map/ppermute | solution.py:244
  39.4 0.5 sums_for_rayleigh.1.refs_0_.refs_5_
  39.9 1.0 %collective-permute-start.11 = (f32[3,8,128]{2,1,0:T(8,128)S(1)}, f32[3,8,128]{2,1,0:T(8,128)S(1)}, u32[]{:S(2)}, u32[]{:S(2)}) collective-permute-start(f32[3,8,128]{2,1,0:T(8,128)S(1)} %sums_for_rayleigh.1.refs_0_.refs_5_), channel_id=1, source_target_pairs={{2,0},{0,2},{3,1},{1,3},{6,4},{4,6},{7,5},{5,7},{10,8},{8,10},{11,... | collective-permute-start | bytes 36872 | tf_op jit(solution)/shard_map/ppermute | solution.py:244
  40.8 2.8 %collective-permute-done.11.refs_1_.refs_6_ = f32[3,8,128]{2,1,0:T(8,128)S(1)} collective-permute-done((f32[3,8,128]{2,1,0:T(8,128)S(1)}, f32[3,8,128]{2,1,0:T(8,128)S(1)}, u32[]{:S(2)}, u32[]{:S(2)}) %collective-permute-start.11) | collective-permute-done | bytes 12320 | tf_op jit(solution)/shard_map/ppermute | solution.py:244
  43.6 0.0 collective-permute-done.17.refs_1_
  43.6 0.1 collective-permute-done.18.refs_2_
  43.7 0.0 collective-permute-done.19.refs_3_
  43.7 2.5 %collective-permute-start.22 = (bf16[1,64,512]{2,1,0:T(8,128)(2,1)S(1)}, bf16[1,64,512]{2,1,0:T(8,128)(2,1)S(1)}, u32[]{:S(2)}, u32[]{:S(2)}) collective-permute-start(bf16[1,64,512]{2,1,0:T(8,128)(2,1)S(1)} %sum_second_sigma.1.refs_3_), channel_id=1, source_target_pairs={{12,0},{8,4},{4,8},{0,12},{13,1},{9,5},{5,9},{1,13},{14,2},{10,6},... | collective-permute-start | bytes 196616 | tf_op jit(solution)/shard_map/ppermute | solution.py:244
  46.3 0.0 collective-permute-start.20
  46.3 1.9 %collective-permute-start.21 = (bf16[1,64,512]{2,1,0:T(8,128)(2,1)S(1)}, bf16[1,64,512]{2,1,0:T(8,128)(2,1)S(1)}, u32[]{:S(2)}, u32[]{:S(2)}) collective-permute-start(bf16[1,64,512]{2,1,0:T(8,128)(2,1)S(1)} %sum_second_sigma.1.refs_3_), channel_id=1, source_target_pairs={{4,0},{0,4},{12,8},{8,12},{5,1},{1,5},{13,9},{9,13},{6,2},{2,6},{1... | collective-permute-start | bytes 196616 | tf_op jit(solution)/shard_map/ppermute | solution.py:244
  48.2 1.4 %second_wave.1 = (bf16[1,256,512]{2,1,0:T(8,128)(2,1)}, f32[2,8,128]{2,1,0:T(8,128)S(1)}) custom-call(s32[2,2]{1,0:T(2,128)S(1)} %copy-done.3, bf16[256,512]{1,0:T(8,128)(2,1)S(1)} %get-tuple-element.24.refs_5_.wave_own, bf16[1,256,512]{2,1,0:T(8,128)(2,1)S(1)} %place_own_sector.1.sigma_own.own.refs_1_, f32[3,8,128]{2,1,0:T(8,128)S(1)} %sums_for_rayleigh.1.refs_0_.refs_5_, ...), custom_call_target="tpu_custom_call" | custom-call | tf_op jit(solution)/shard_map/second_wave/pallas_call | solution.py:262
  49.6 0.8 %collective-permute-done.22.refs_2_ = bf16[1,64,512]{2,1,0:T(8,128)(2,1)S(1)} collective-permute-done((bf16[1,64,512]{2,1,0:T(8,128)(2,1)S(1)}, bf16[1,64,512]{2,1,0:T(8,128)(2,1)S(1)}, u32[]{:S(2)}, u32[]{:S(2)}) %collective-permute-start.22) | collective-permute-done | bytes 65568 | tf_op jit(solution)/shard_map/ppermute | solution.py:244
  50.4 0.8 %join_early_shares.1.refs_4_ = f32[1,256,512]{2,1,0:T(8,128)} custom-call(f32[2,8,128]{2,1,0:T(8,128)S(1)} %get-tuple-element.36.refs_0_, bf16[1,256,512]{2,1,0:T(8,128)(2,1)S(1)} %place_own_sector.1.sigma_own.own.refs_1_, bf16[1,64,512]{2,1,0:T(8,128)(2,1)S(1)} %collective-permute-done.22.refs_2_, bf16[1,64,512]{2,1,0:T(8,128)(2,1)S(1)} %sum_second_sigma.1.refs_3_), custom_call_target="tpu_custom_call" | custom-call | tf_op jit(solution)/shard_map/join_early_shares/pallas_call | solution.py:434
  51.2 1.2 %collective-permute-done.20.refs_2_ = bf16[1,64,512]{2,1,0:T(8,128)(2,1)S(1)} collective-permute-done((bf16[1,64,512]{2,1,0:T(8,128)(2,1)S(1)}, bf16[1,64,512]{2,1,0:T(8,128)(2,1)S(1)}, u32[]{:S(2)}, u32[]{:S(2)}) %collective-permute-start.20) | collective-permute-done | bytes 65568 | tf_op jit(solution)/shard_map/ppermute | solution.py:244
  52.4 0.0 collective-permute-done.21.refs_3_
  52.4 0.8 %join_late_shares.1 = f32[1,256,512]{2,1,0:T(8,128)} custom-call(f32[2,8,128]{2,1,0:T(8,128)S(1)} %get-tuple-element.36.refs_0_, bf16[1,256,512]{2,1,0:T(8,128)(2,1)S(1)} %place_own_sector.1.sigma_own.own.refs_1_, bf16[1,64,512]{2,1,0:T(8,128)(2,1)S(1)} %collective-permute-done.20.refs_2_, ...), custom_call_target="tpu_custom_call", output_to_operand_aliasing={{}: (4, {})} | custom-call | tf_op jit(solution)/shard_map/join_late_shares/pallas_call | solution.py:434
  (7 shorter events, 0.1 us)
Async XLA Ops:
  0.6 2.0 %copy-start.1 = (bf16[1,256,512]{2,1,0:T(8,128)(2,1)S(1)}, bf16[1,256,512]{2,1,0:T(8,128)(2,1)}, u32[]{:S(2)}) copy-start(bf16[1,256,512]{2,1,0:T(8,128)(2,1)} %wave.1) | copy-start | bytes 786436
  0.6 2.0 %copy-start.3 = (s32[2,2]{1,0:T(2,128)S(1)}, s32[2,2]{1,0:T(2,128)}, u32[]{:S(2)}) copy-start(s32[2,2]{1,0:T(2,128)} %sizes_ref.3) | copy-start | bytes 52
  0.7 2.0 %copy-start.2 = (s32[4,8,2]{1,2,0:T(2,128)S(1)}, s32[4,8,2]{1,2,0:T(2,128)}, u32[]{:S(2)}) copy-start(s32[4,8,2]{1,2,0:T(2,128)} %param.10) | copy-start | bytes 772
  0.7 2.0 %copy-start.4 = (f32[4,8]{1,0:T(4,128)S(1)}, f32[4,8]{1,0:T(4,128)}, u32[]{:S(2)}) copy-start(f32[4,8]{1,0:T(4,128)} %weights_ref.1) | copy-start | bytes 388
  0.7 2.2 %copy-start = (bf16[4,512,512]{2,1,0:T(8,128)(2,1)S(1)}, bf16[4,512,512]{2,1,0:T(8,128)(2,1)}, u32[]{:S(2)}) copy-start(bf16[4,512,512]{2,1,0:T(8,128)(2,1)} %right.1) | copy-start | bytes 6291460
  0.7 2.2 %collective-permute-start = (bf16[1,256,512]{2,1,0:T(8,128)(2,1)}, bf16[1,256,512]{2,1,0:T(8,128)(2,1)S(1)}, u32[]{:S(2)}, u32[]{:S(2)}) collective-permute-start(bf16[1,256,512]{2,1,0:T(8,128)(2,1)} %wave.1), channel_id=1, source_target_pairs={{1,0},{0,1},{3,2},{2,3},{5,4},{4,5},{7,6},{6,7},{9,8},{8,9},{11,10... | collective-permute-start | bytes 786440 | tf_op jit(solution)/shard_map/ppermute | solution.py:244
  4.5 8.6 %collective-permute-start.1 = (bf16[2,64,512]{2,1,0:T(8,128)(2,1)S(1)}, bf16[2,64,512]{2,1,0:T(8,128)(2,1)S(1)}, u32[]{:S(2)}, u32[]{:S(2)}) collective-permute-start(bf16[2,64,512]{2,1,0:T(8,128)(2,1)S(1)} %get-tuple-element.28), channel_id=1, source_target_pairs={{2,0},{0,2},{3,1},{1,3},{6,4},{4,6},{7,5},{5,7},{10,8},{8,10},{11,... | collective-permute-start | bytes 393224 | tf_op jit(solution)/shard_map/ppermute | solution.py:244
  7.3 10.4 %collective-permute-start.3 = (bf16[1,64,512]{2,1,0:T(8,128)(2,1)S(1)}, bf16[1,64,512]{2,1,0:T(8,128)(2,1)S(1)}, u32[]{:S(2)}, u32[]{:S(2)}) collective-permute-start(bf16[1,64,512]{2,1,0:T(8,128)(2,1)S(1)} %get-tuple-element.29), channel_id=1, source_target_pairs={{8,0},{12,4},{0,8},{4,12},{9,1},{13,5},{1,9},{5,13},{10,2},{14,6},... | collective-permute-start | bytes 196616 | tf_op jit(solution)/shard_map/ppermute | solution.py:244
  9.9 7.8 %collective-permute-start.4 = (bf16[1,64,512]{2,1,0:T(8,128)(2,1)S(1)}, bf16[1,64,512]{2,1,0:T(8,128)(2,1)S(1)}, u32[]{:S(2)}, u32[]{:S(2)}) collective-permute-start(bf16[1,64,512]{2,1,0:T(8,128)(2,1)S(1)} %get-tuple-element.30), channel_id=1, source_target_pairs={{4,0},{0,4},{12,8},{8,12},{5,1},{1,5},{13,9},{9,13},{6,2},{2,6},{1... | collective-permute-start | bytes 196616 | tf_op jit(solution)/shard_map/ppermute | solution.py:244
  11.5 8.4 %collective-permute-start.5 = (bf16[1,64,512]{2,1,0:T(8,128)(2,1)S(1)}, bf16[1,64,512]{2,1,0:T(8,128)(2,1)S(1)}, u32[]{:S(2)}, u32[]{:S(2)}) collective-permute-start(bf16[1,64,512]{2,1,0:T(8,128)(2,1)S(1)} %get-tuple-element.31), channel_id=1, source_target_pairs={{10,0},{8,2},{14,4},{12,6},{2,8},{0,10},{6,12},{4,14},{11,1},{9,3}... | collective-permute-start | bytes 196616 | tf_op jit(solution)/shard_map/ppermute | solution.py:244
  11.8 8.1 %collective-permute-start.6 = (bf16[1,64,512]{2,1,0:T(8,128)(2,1)S(1)}, bf16[1,64,512]{2,1,0:T(8,128)(2,1)S(1)}, u32[]{:S(2)}, u32[]{:S(2)}) collective-permute-start(bf16[1,64,512]{2,1,0:T(8,128)(2,1)S(1)} %get-tuple-element.32), channel_id=1, source_target_pairs={{6,0},{4,2},{2,4},{0,6},{14,8},{12,10},{10,12},{8,14},{7,1},{5,3},... | collective-permute-start | bytes 196616 | tf_op jit(solution)/shard_map/ppermute | solution.py:244
  13.2 6.7 %collective-permute-start.2 = (bf16[1,64,512]{2,1,0:T(8,128)(2,1)S(1)}, bf16[1,64,512]{2,1,0:T(8,128)(2,1)S(1)}, u32[]{:S(2)}, u32[]{:S(2)}) collective-permute-start(bf16[1,64,512]{2,1,0:T(8,128)(2,1)S(1)} %sum_far_share.1), channel_id=1, source_target_pairs={{12,0},{8,4},{4,8},{0,12},{13,1},{9,5},{5,9},{1,13},{14,2},{10,6},... | collective-permute-start | bytes 196616 | tf_op jit(solution)/shard_map/ppermute | solution.py:244
  20.0 6.8 %collective-permute-start.7 = (bf16[1,64,512]{2,1,0:T(8,128)(2,1)S(1)}, bf16[1,64,512]{2,1,0:T(8,128)(2,1)S(1)}, u32[]{:S(2)}, u32[]{:S(2)}) collective-permute-start(bf16[1,64,512]{2,1,0:T(8,128)(2,1)S(1)} %sum_first_sigma.1.refs_3_), channel_id=1, source_target_pairs={{8,0},{12,4},{0,8},{4,12},{9,1},{13,5},{1,9},{5,13},{10,2},{14,6},... | collective-permute-start | bytes 196616 | tf_op jit(solution)/shard_map/ppermute | solution.py:244
  21.0 6.8 %collective-permute-start.8 = (bf16[1,64,512]{2,1,0:T(8,128)(2,1)S(1)}, bf16[1,64,512]{2,1,0:T(8,128)(2,1)S(1)}, u32[]{:S(2)}, u32[]{:S(2)}) collective-permute-start(bf16[1,64,512]{2,1,0:T(8,128)(2,1)S(1)} %sum_first_sigma.1.refs_3_), channel_id=1, source_target_pairs={{12,0},{8,4},{4,8},{0,12},{13,1},{9,5},{5,9},{1,13},{14,2},{10,6},... | collective-permute-start | bytes 196616 | tf_op jit(solution)/shard_map/ppermute | solution.py:244
  23.1 5.7 %collective-permute-start.9 = (bf16[1,64,512]{2,1,0:T(8,128)(2,1)S(1)}, bf16[1,64,512]{2,1,0:T(8,128)(2,1)S(1)}, u32[]{:S(2)}, u32[]{:S(2)}) collective-permute-start(bf16[1,64,512]{2,1,0:T(8,128)(2,1)S(1)} %sum_first_sigma.1.refs_3_), channel_id=1, source_target_pairs={{4,0},{0,4},{12,8},{8,12},{5,1},{1,5},{13,9},{9,13},{6,2},{2,6},{1... | collective-permute-start | bytes 196616 | tf_op jit(solution)/shard_map/ppermute | solution.py:244
  23.6 5.4 %collective-permute-start.14 = (bf16[1,64,512]{2,1,0:T(8,128)(2,1)S(1)}, bf16[1,64,512]{2,1,0:T(8,128)(2,1)S(1)}, u32[]{:S(2)}, u32[]{:S(2)}) collective-permute-start(bf16[1,64,512]{2,1,0:T(8,128)(2,1)S(1)} %sum_first_sigma.1.refs_3_), channel_id=1, source_target_pairs={{6,0},{4,2},{2,4},{0,6},{14,8},{12,10},{10,12},{8,14},{7,1},{5,3},... | collective-permute-start | bytes 196616 | tf_op jit(solution)/shard_map/ppermute | solution.py:244
  25.7 4.7 %collective-permute-start.15 = (bf16[1,64,512]{2,1,0:T(8,128)(2,1)S(1)}, bf16[1,64,512]{2,1,0:T(8,128)(2,1)S(1)}, u32[]{:S(2)}, u32[]{:S(2)}) collective-permute-start(bf16[1,64,512]{2,1,0:T(8,128)(2,1)S(1)} %sum_first_sigma.1.refs_3_), channel_id=1, source_target_pairs={{2,0},{0,2},{3,1},{1,3},{6,4},{4,6},{7,5},{5,7},{10,8},{8,10},{11,... | collective-permute-start | bytes 196616 | tf_op jit(solution)/shard_map/ppermute | solution.py:244
  26.7 4.4 %collective-permute-start.12 = (bf16[1,64,512]{2,1,0:T(8,128)(2,1)S(1)}, bf16[1,64,512]{2,1,0:T(8,128)(2,1)S(1)}, u32[]{:S(2)}, u32[]{:S(2)}) collective-permute-start(bf16[1,64,512]{2,1,0:T(8,128)(2,1)S(1)} %collective-permute-done.7.refs_0_), channel_id=1, source_target_pairs={{2,0},{0,2},{3,1},{1,3},{6,4},{4,6},{7,5},{5,7},{10,8},{8,10},{11,... | collective-permute-start | bytes 196616 | tf_op jit(solution)/shard_map/ppermute | solution.py:244
  27.9 4.3 %collective-permute-start.13 = (bf16[1,64,512]{2,1,0:T(8,128)(2,1)S(1)}, bf16[1,64,512]{2,1,0:T(8,128)(2,1)S(1)}, u32[]{:S(2)}, u32[]{:S(2)}) collective-permute-start(bf16[1,64,512]{2,1,0:T(8,128)(2,1)S(1)} %collective-permute-done.8.refs_1_), channel_id=1, source_target_pairs={{2,0},{0,2},{3,1},{1,3},{6,4},{4,6},{7,5},{5,7},{10,8},{8,10},{11,... | collective-permute-start | bytes 196616 | tf_op jit(solution)/shard_map/ppermute | solution.py:244
  28.8 3.4 %collective-permute-start.10 = (bf16[1,256,512]{2,1,0:T(8,128)(2,1)S(1)}, bf16[1,256,512]{2,1,0:T(8,128)(2,1)S(1)}, u32[]{:S(2)}, u32[]{:S(2)}) collective-permute-start(bf16[1,256,512]{2,1,0:T(8,128)(2,1)S(1)} %place_own_sector.1.sigma_own.own.refs_1_), channel_id=1, source_target_pairs={{1,0},{0,1},{3,2},{2,3},{5,4},{4,5},{7,6},{6,7},{9,8},{8,9},{11,10... | collective-permute-start | bytes 786440 | tf_op jit(solution)/shard_map/ppermute | solution.py:244
  32.2 1.6 %collective-permute-start.16 = (bf16[1,256,512]{2,1,0:T(8,128)(2,1)S(1)}, bf16[1,256,512]{2,1,0:T(8,128)(2,1)S(1)}, u32[]{:S(2)}, u32[]{:S(2)}) collective-permute-start(bf16[1,256,512]{2,1,0:T(8,128)(2,1)S(1)} %place_other_sectors.1.across_own), channel_id=1, source_target_pairs={{1,0},{0,1},{3,2},{2,3},{5,4},{4,5},{7,6},{6,7},{9,8},{8,9},{11,10... | collective-permute-start | bytes 786440 | tf_op jit(solution)/shard_map/ppermute | solution.py:244
  34.9 8.7 %collective-permute-start.17 = (bf16[1,64,512]{2,1,0:T(8,128)(2,1)S(1)}, bf16[1,64,512]{2,1,0:T(8,128)(2,1)S(1)}, u32[]{:S(2)}, u32[]{:S(2)}) collective-permute-start(bf16[1,64,512]{2,1,0:T(8,128)(2,1)S(1)} %get-tuple-element.41), channel_id=1, source_target_pairs={{12,0},{8,4},{4,8},{0,12},{13,1},{9,5},{5,9},{1,13},{14,2},{10,6},... | collective-permute-start | bytes 196616 | tf_op jit(solution)/shard_map/ppermute | solution.py:244
  37.4 6.3 %collective-permute-start.18 = (bf16[1,64,512]{2,1,0:T(8,128)(2,1)S(1)}, bf16[1,64,512]{2,1,0:T(8,128)(2,1)S(1)}, u32[]{:S(2)}, u32[]{:S(2)}) collective-permute-start(bf16[1,64,512]{2,1,0:T(8,128)(2,1)S(1)} %get-tuple-element.42), channel_id=1, source_target_pairs={{8,0},{12,4},{0,8},{4,12},{9,1},{13,5},{1,9},{5,13},{10,2},{14,6},... | collective-permute-start | bytes 196616 | tf_op jit(solution)/shard_map/ppermute | solution.py:244
  37.4 6.3 %collective-permute-start.19 = (bf16[1,64,512]{2,1,0:T(8,128)(2,1)S(1)}, bf16[1,64,512]{2,1,0:T(8,128)(2,1)S(1)}, u32[]{:S(2)}, u32[]{:S(2)}) collective-permute-start(bf16[1,64,512]{2,1,0:T(8,128)(2,1)S(1)} %get-tuple-element.43), channel_id=1, source_target_pairs={{4,0},{0,4},{12,8},{8,12},{5,1},{1,5},{13,9},{9,13},{6,2},{2,6},{1... | collective-permute-start | bytes 196616 | tf_op jit(solution)/shard_map/ppermute | solution.py:244
  39.9 3.8 %collective-permute-start.11 = (f32[3,8,128]{2,1,0:T(8,128)S(1)}, f32[3,8,128]{2,1,0:T(8,128)S(1)}, u32[]{:S(2)}, u32[]{:S(2)}) collective-permute-start(f32[3,8,128]{2,1,0:T(8,128)S(1)} %sums_for_rayleigh.1.refs_0_.refs_5_), channel_id=1, source_target_pairs={{2,0},{0,2},{3,1},{1,3},{6,4},{4,6},{7,5},{5,7},{10,8},{8,10},{11,... | collective-permute-start | bytes 36872 | tf_op jit(solution)/shard_map/ppermute | solution.py:244
  43.7 6.7 %collective-permute-start.22 = (bf16[1,64,512]{2,1,0:T(8,128)(2,1)S(1)}, bf16[1,64,512]{2,1,0:T(8,128)(2,1)S(1)}, u32[]{:S(2)}, u32[]{:S(2)}) collective-permute-start(bf16[1,64,512]{2,1,0:T(8,128)(2,1)S(1)} %sum_second_sigma.1.refs_3_), channel_id=1, source_target_pairs={{12,0},{8,4},{4,8},{0,12},{13,1},{9,5},{5,9},{1,13},{14,2},{10,6},... | collective-permute-start | bytes 196616 | tf_op jit(solution)/shard_map/ppermute | solution.py:244
  46.3 6.2 %collective-permute-start.20 = (bf16[1,64,512]{2,1,0:T(8,128)(2,1)S(1)}, bf16[1,64,512]{2,1,0:T(8,128)(2,1)S(1)}, u32[]{:S(2)}, u32[]{:S(2)}) collective-permute-start(bf16[1,64,512]{2,1,0:T(8,128)(2,1)S(1)} %sum_second_sigma.1.refs_3_), channel_id=1, source_target_pairs={{8,0},{12,4},{0,8},{4,12},{9,1},{13,5},{1,9},{5,13},{10,2},{14,6},... | collective-permute-start | bytes 196616 | tf_op jit(solution)/shard_map/ppermute | solution.py:244
  46.3 6.2 %collective-permute-start.21 = (bf16[1,64,512]{2,1,0:T(8,128)(2,1)S(1)}, bf16[1,64,512]{2,1,0:T(8,128)(2,1)S(1)}, u32[]{:S(2)}, u32[]{:S(2)}) collective-permute-start(bf16[1,64,512]{2,1,0:T(8,128)(2,1)S(1)} %sum_second_sigma.1.refs_3_), channel_id=1, source_target_pairs={{4,0},{0,4},{12,8},{8,12},{5,1},{1,5},{13,9},{9,13},{6,2},{2,6},{1... | collective-permute-start | bytes 196616 | tf_op jit(solution)/shard_map/ppermute | solution.py:244

commit v24 on v23

--- a/solution.py
+++ b/solution.py
@@ -21,10 +21,6 @@
     row = row_start + lax.broadcasted_iota(jnp.int32, (rows, columns), 0)
     column = lax.broadcasted_iota(jnp.int32, (rows, columns), 1)
     return (row < sizes_ref[sector, 0]) & (column < sizes_ref[sector, 1])
-
-
-def masked(values, live):
-    return jnp.where(live, values.astype(jnp.float32), 0.0).astype(values.dtype)
 
 
 def left_times(lefts, blocks):
@@ -345,27 +341,29 @@
     received += [partner(rest[spot], {"ops": spot[0][0], "sec": spot[1]}) for spot in order]
     first_share = summed("sum_first_sigma", *[(piece, 1) for piece in met], *received, live=live)
     along_ops = {along: partner(first_share, {"ops": along}) for along in send_order}
-    sigma_own = call(
-        lambda *refs: place_kernel([(along, 0) for along in send_order], *refs),
-        "place_own_sector",
-        shape(1, rows, columns),
-        [],
-        *along_ops.values(),
-    )
-    sigma_other = partner(sigma_own, {"rep": 1})
     spots = [(along, across) for along in send_order for across in range(1, sectors)]
-    pieces = [
-        partner(first_share, {"ops": along, "sec": across})
+    pieces = {
+        (along, across): partner(first_share, {"ops": along, "sec": across})
         if along < 2
         else partner(along_ops[along], {"sec": across})
         for along, across in spots
-    ]
+    }
+    ahead = [pieces[along, across] for along, across in spots if along < 2]
+    sigma_own = call(
+        lambda *refs: place_kernel([(along, 0) for along in send_order], *refs[len(ahead) :]),
+        "place_own_sector",
+        shape(1, rows, columns),
+        [],
+        *ahead,
+        *along_ops.values(),
+    )
+    sigma_other = partner(sigma_own, {"rep": 1})
     across_own = call(
         lambda *refs: place_kernel([(along, across - 1) for along, across in spots], *refs),
         "place_other_sectors",
         shape(sectors - 1, rows, columns),
         [],
-        *pieces,
+        *pieces.values(),
     )
     across_other = partner(across_own, {"rep": 1})
 

time: 53.4 us -> 53.3 us (level)
  transfers between devices with their start and end apart: 23 -> 23, of which waited for: 12 -> 10; matrix products, arithmetic and copies ran while one was open for 0% -> 0% of each run, Pallas kernels for 12% -> 12%
where the time goes in v24:
time: 53.3 us; the launch traced here: 53.1 us
  starting transfers between devices  31.7 us (59%)
  waiting for transfers between devices  10.8 us (20%)
  Pallas kernels  9.78 us (18%)
  between operations  0.86 us (2%)
    ppermute x23, starting transfers between devices, partner(): return lax.ppermute(value, axes, pairs)  31.7 us
    ppermute x23, waiting for transfers between devices, partner(): return lax.ppermute(value, axes, pairs)  10.8 us
    pallas_call x13, Pallas kernels, call(): pl.pallas_call(kernel, out_shape=out_shape, in_specs=list(in_specs) + [in...  8.23 us
    pallas_call x2, Pallas kernels, local(): pl.pallas_call(lambda *refs, steps=steps: join_kernel(steps, *refs), out_...  1.54 us
  transfers between devices with their start and end apart: 23, of which 10 were waited for; matrix products, arithmetic and copies ran while one was open for 0% of the time, Pallas kernels for 12%

profile of v24, /device:TPU:0, one launch (start us, length us, event | category | flops | bytes accessed | tf_op | source)
XLA Modules:
  0.0 53.1 jit_solution(5213721399471528939)
XLA Ops:
  0.6 0.0 copy-start.1
  0.6 0.0 copy-start.3
  0.7 0.0 copy-start.2
  0.7 0.5 collective-permute-start
  1.2 1.4 %load_operators.1 = (bf16[4,256,256]{2,1,0:T(8,128)(2,1)S(1)}, bf16[4,256,256]{2,1,0:T(8,128)(2,1)S(1)}) custom-call(bf16[4,512,512]{2,1,0:T(8,128)(2,1)} %left_ref.1), custom_call_target="tpu_custom_call" | custom-call | tf_op jit(solution)/shard_map/load_operators/pallas_call | solution.py:258
  2.6 0.0 copy-done.1
  2.6 0.0 copy-done.3
  2.7 0.0 copy-done.2
  2.7 0.0 copy-done.4
  2.7 0.2 tables_for_first_sigma.1
  2.9 0.0 collective-permute-done.refs_6_
  2.9 1.6 %first_sigma_terms.1 = (bf16[256,512]{1,0:T(8,128)(2,1)S(1)}, f32[2,64,512]{2,1,0:T(8,128)S(1)}, bf16[2,64,512]{2,1,0:T(8,128)(2,1)S(1)}, bf16[1,64,512]{2,1,0:T...) custom-call(s32[2,2]{1,0:T(2,128)S(1)} %copy-done.3, ...), custom_call_target="tpu_custom_call" | custom-call | tf_op jit(solution)/shard_map/first_sigma_terms/pallas_call | solution.py:258
  4.5 2.8 %collective-permute-start.1 = (bf16[2,64,512]{2,1,0:T(8,128)(2,1)S(1)}, bf16[2,64,512]{2,1,0:T(8,128)(2,1)S(1)}, u32[]{:S(2)}, u32[]{:S(2)}) collective-permute-start(bf16[2,64,512]{2,1,0:T(8,128)(2,1)S(1)} %get-tuple-element.28), channel_id=1, source_target_pairs={{2,0},{0,2},{3,1},{1,3},{6,4},{4,6},{7,5},{5,7},{10,8},{8,10},{11,... | collective-permute-start | bytes 393224 | tf_op jit(solution)/shard_map/ppermute | solution.py:240
  7.3 2.6 %collective-permute-start.3 = (bf16[1,64,512]{2,1,0:T(8,128)(2,1)S(1)}, bf16[1,64,512]{2,1,0:T(8,128)(2,1)S(1)}, u32[]{:S(2)}, u32[]{:S(2)}) collective-permute-start(bf16[1,64,512]{2,1,0:T(8,128)(2,1)S(1)} %get-tuple-element.29), channel_id=1, source_target_pairs={{8,0},{12,4},{0,8},{4,12},{9,1},{13,5},{1,9},{5,13},{10,2},{14,6},... | collective-permute-start | bytes 196616 | tf_op jit(solution)/shard_map/ppermute | solution.py:240
  9.9 1.6 %collective-permute-start.4 = (bf16[1,64,512]{2,1,0:T(8,128)(2,1)S(1)}, bf16[1,64,512]{2,1,0:T(8,128)(2,1)S(1)}, u32[]{:S(2)}, u32[]{:S(2)}) collective-permute-start(bf16[1,64,512]{2,1,0:T(8,128)(2,1)S(1)} %get-tuple-element.30), channel_id=1, source_target_pairs={{4,0},{0,4},{12,8},{8,12},{5,1},{1,5},{13,9},{9,13},{6,2},{2,6},{1... | collective-permute-start | bytes 196616 | tf_op jit(solution)/shard_map/ppermute | solution.py:240
  11.5 0.3 collective-permute-start.5
  11.8 1.4 %collective-permute-start.6 = (bf16[1,64,512]{2,1,0:T(8,128)(2,1)S(1)}, bf16[1,64,512]{2,1,0:T(8,128)(2,1)S(1)}, u32[]{:S(2)}, u32[]{:S(2)}) collective-permute-start(bf16[1,64,512]{2,1,0:T(8,128)(2,1)S(1)} %get-tuple-element.32), channel_id=1, source_target_pairs={{6,0},{4,2},{2,4},{0,6},{14,8},{12,10},{10,12},{8,14},{7,1},{5,3},... | collective-permute-start | bytes 196616 | tf_op jit(solution)/shard_map/ppermute | solution.py:240
  13.1 0.0 collective-permute-done.1.refs_1_
  13.2 3.7 %collective-permute-start.2 = (bf16[1,64,512]{2,1,0:T(8,128)(2,1)S(1)}, bf16[1,64,512]{2,1,0:T(8,128)(2,1)S(1)}, u32[]{:S(2)}, u32[]{:S(2)}) collective-permute-start(bf16[1,64,512]{2,1,0:T(8,128)(2,1)S(1)} %sum_far_share.1), channel_id=1, source_target_pairs={{12,0},{8,4},{4,8},{0,12},{13,1},{9,5},{5,9},{1,13},{14,2},{10,6},... | collective-permute-start | bytes 196616 | tf_op jit(solution)/shard_map/ppermute | solution.py:240
  16.8 0.8 %tables_for_second_sigma.1 = (f32[4,2,8,128]{3,2,1,0:T(8,128)S(1)}, f32[256,512]{1,0:T(8,128)S(1)}) custom-call(s32[2,2]{1,0:T(2,128)S(1)} %copy-done.3, s32[4,2,8]{2,1,0:T(2,128)S(1)} %bitcast.2, f32[4,8]{1,0:T(4,128)S(1)} %copy-done.4, bf16[256,512]{1,0:T(8,128)(2,1)S(1)} %get-tuple-element.33._.wave_other), custom_call_target="tpu_custom_call" | custom-call | tf_op jit(solution)/shard_map/tables_for_second_sigma/pallas_call | solution.py:258
  17.6 0.0 collective-permute-done.3.refs_3_
  17.7 0.0 collective-permute-done.4.refs_4_
  17.7 2.2 %collective-permute-done.5.refs_5_ = bf16[1,64,512]{2,1,0:T(8,128)(2,1)S(1)} collective-permute-done((bf16[1,64,512]{2,1,0:T(8,128)(2,1)S(1)}, bf16[1,64,512]{2,1,0:T(8,128)(2,1)S(1)}, u32[]{:S(2)}, u32[]{:S(2)}) %collective-permute-start.5) | collective-permute-done | bytes 65568 | tf_op jit(solution)/shard_map/ppermute | solution.py:240
  19.9 0.0 collective-permute-done.6.refs_6_
  19.9 0.0 collective-permute-done.2.refs_2_
  19.9 0.1 sum_first_sigma.1.refs_5_
  20.0 1.1 %collective-permute-start.9 = (bf16[1,64,512]{2,1,0:T(8,128)(2,1)S(1)}, bf16[1,64,512]{2,1,0:T(8,128)(2,1)S(1)}, u32[]{:S(2)}, u32[]{:S(2)}) collective-permute-start(bf16[1,64,512]{2,1,0:T(8,128)(2,1)S(1)} %sum_first_sigma.1.refs_5_), channel_id=1, source_target_pairs={{8,0},{12,4},{0,8},{4,12},{9,1},{13,5},{1,9},{5,13},{10,2},{14,6},... | collective-permute-start | bytes 196616 | tf_op jit(solution)/shard_map/ppermute | solution.py:240
  21.0 2.1 %collective-permute-start.10 = (bf16[1,64,512]{2,1,0:T(8,128)(2,1)S(1)}, bf16[1,64,512]{2,1,0:T(8,128)(2,1)S(1)}, u32[]{:S(2)}, u32[]{:S(2)}) collective-permute-start(bf16[1,64,512]{2,1,0:T(8,128)(2,1)S(1)} %sum_first_sigma.1.refs_5_), channel_id=1, source_target_pairs={{12,0},{8,4},{4,8},{0,12},{13,1},{9,5},{5,9},{1,13},{14,2},{10,6},... | collective-permute-start | bytes 196616 | tf_op jit(solution)/shard_map/ppermute | solution.py:240
  23.1 0.5 collective-permute-start.7
  23.6 1.5 %collective-permute-start.8 = (bf16[1,64,512]{2,1,0:T(8,128)(2,1)S(1)}, bf16[1,64,512]{2,1,0:T(8,128)(2,1)S(1)}, u32[]{:S(2)}, u32[]{:S(2)}) collective-permute-start(bf16[1,64,512]{2,1,0:T(8,128)(2,1)S(1)} %sum_first_sigma.1.refs_5_), channel_id=1, source_target_pairs={{2,0},{0,2},{3,1},{1,3},{6,4},{4,6},{7,5},{5,7},{10,8},{8,10},{11,... | collective-permute-start | bytes 196616 | tf_op jit(solution)/shard_map/ppermute | solution.py:240
  25.1 1.5 %collective-permute-start.11 = (bf16[1,64,512]{2,1,0:T(8,128)(2,1)S(1)}, bf16[1,64,512]{2,1,0:T(8,128)(2,1)S(1)}, u32[]{:S(2)}, u32[]{:S(2)}) collective-permute-start(bf16[1,64,512]{2,1,0:T(8,128)(2,1)S(1)} %sum_first_sigma.1.refs_5_), channel_id=1, source_target_pairs={{4,0},{0,4},{12,8},{8,12},{5,1},{1,5},{13,9},{9,13},{6,2},{2,6},{1... | collective-permute-start | bytes 196616 | tf_op jit(solution)/shard_map/ppermute | solution.py:240
  26.6 0.2 collective-permute-done.9.refs_2_
  26.8 0.9 %collective-permute-start.14 = (bf16[1,64,512]{2,1,0:T(8,128)(2,1)S(1)}, bf16[1,64,512]{2,1,0:T(8,128)(2,1)S(1)}, u32[]{:S(2)}, u32[]{:S(2)}) collective-permute-start(bf16[1,64,512]{2,1,0:T(8,128)(2,1)S(1)} %collective-permute-done.9.refs_2_), channel_id=1, source_target_pairs={{2,0},{0,2},{3,1},{1,3},{6,4},{4,6},{7,5},{5,7},{10,8},{8,10},{11,... | collective-permute-start | bytes 196616 | tf_op jit(solution)/shard_map/ppermute | solution.py:240
  27.7 0.0 collective-permute-done.10.refs_3_
  27.7 1.1 %collective-permute-start.15 = (bf16[1,64,512]{2,1,0:T(8,128)(2,1)S(1)}, bf16[1,64,512]{2,1,0:T(8,128)(2,1)S(1)}, u32[]{:S(2)}, u32[]{:S(2)}) collective-permute-start(bf16[1,64,512]{2,1,0:T(8,128)(2,1)S(1)} %collective-permute-done.10.refs_3_), channel_id=1, source_target_pairs={{2,0},{0,2},{3,1},{1,3},{6,4},{4,6},{7,5},{5,7},{10,8},{8,10},{11,... | collective-permute-start | bytes 196616 | tf_op jit(solution)/shard_map/ppermute | solution.py:240
  28.8 0.0 collective-permute-done.7.refs_0_.refs_2_
  28.8 0.0 collective-permute-done.8.refs_1_.refs_3_
  28.8 0.5 collective-permute-done.11.refs_4_
  29.4 0.1 collective-permute-start.12
  29.4 1.6 %collective-permute-done.14.refs_0_ = bf16[1,64,512]{2,1,0:T(8,128)(2,1)S(1)} collective-permute-done((bf16[1,64,512]{2,1,0:T(8,128)(2,1)S(1)}, bf16[1,64,512]{2,1,0:T(8,128)(2,1)S(1)}, u32[]{:S(2)}, u32[]{:S(2)}) %collective-permute-start.14) | collective-permute-done | bytes 65568 | tf_op jit(solution)/shard_map/ppermute | solution.py:240
  31.1 0.9 %collective-permute-done.15.refs_1_ = bf16[1,64,512]{2,1,0:T(8,128)(2,1)S(1)} collective-permute-done((bf16[1,64,512]{2,1,0:T(8,128)(2,1)S(1)}, bf16[1,64,512]{2,1,0:T(8,128)(2,1)S(1)}, u32[]{:S(2)}, u32[]{:S(2)}) %collective-permute-start.15) | collective-permute-done | bytes 65568 | tf_op jit(solution)/shard_map/ppermute | solution.py:240
  32.0 0.1 collective-permute-start.16
  32.1 0.0 collective-permute-done.12.sigma_other.other
  32.1 1.0 %left_products.1 = (f32[4,256,512]{2,1,0:T(8,128)S(1)}, f32[1,4,256,512]{3,2,1,0:T(8,128)S(1)}) custom-call(bf16[4,256,256]{2,1,0:T(8,128)(2,1)S(1)} %get-tuple-element.23._.refs_2_.left_own, bf16[4,256,256]{2,1,0:T(8,128)(2,1)S(1)} %get-tuple-element.26.refs_3_.left_other, bf16[1,256,512]{2,1,0:T(8,128)(2,1)S(1)} %place_own_sector.1.sigma_own.own.refs_1_, ...), custom_call_target="tpu_custom_call" | custom-call | tf_op jit(solution)/shard_map/left_products/pallas_call | solution.py:258
  33.1 0.5 %collective-permute-done.16.other = bf16[1,256,512]{2,1,0:T(8,128)(2,1)S(1)} collective-permute-done((bf16[1,256,512]{2,1,0:T(8,128)(2,1)S(1)}, bf16[1,256,512]{2,1,0:T(8,128)(2,1)S(1)}, u32[]{:S(2)}, u32[]{:S(2)}) %collective-permute-start.16) | collective-permute-done | bytes 262176 | tf_op jit(solution)/shard_map/ppermute | solution.py:240
  33.6 1.1 %second_sigma_terms.1 = (f32[1,64,512]{2,1,0:T(8,128)S(1)}, bf16[1,64,512]{2,1,0:T(8,128)(2,1)S(1)}, bf16[1,64,512]{2,1,0:T(8,128)(2,1)S(1)}, bf16[1,64,512]{2,1,0:T(8,128)(2,1)S(1)}) custom-call(f32[4,2,8,128]{3,2,1,0:T(8,128)S(1)} %get-tuple-element.37.mixing, bf16[4,256,256]{2,1,0:T(8,128)(2,1)S(1)} %get-tuple-element.26.refs_3_.left_other, ...), custom_call_target="tpu_custom_call" | custom-call | tf_op jit(solution)/shard_map/second_sigma_terms/pallas_call | solution.py:258
  34.7 2.3 %collective-permute-start.17 = (bf16[1,64,512]{2,1,0:T(8,128)(2,1)S(1)}, bf16[1,64,512]{2,1,0:T(8,128)(2,1)S(1)}, u32[]{:S(2)}, u32[]{:S(2)}) collective-permute-start(bf16[1,64,512]{2,1,0:T(8,128)(2,1)S(1)} %get-tuple-element.41), channel_id=1, source_target_pairs={{12,0},{8,4},{4,8},{0,12},{13,1},{9,5},{5,9},{1,13},{14,2},{10,6},... | collective-permute-start | bytes 196616 | tf_op jit(solution)/shard_map/ppermute | solution.py:240
  37.0 0.1 collective-permute-start.18
  37.1 2.1 %collective-permute-start.19 = (bf16[1,64,512]{2,1,0:T(8,128)(2,1)S(1)}, bf16[1,64,512]{2,1,0:T(8,128)(2,1)S(1)}, u32[]{:S(2)}, u32[]{:S(2)}) collective-permute-start(bf16[1,64,512]{2,1,0:T(8,128)(2,1)S(1)} %get-tuple-element.43), channel_id=1, source_target_pairs={{4,0},{0,4},{12,8},{8,12},{5,1},{1,5},{13,9},{9,13},{6,2},{2,6},{1... | collective-permute-start | bytes 196616 | tf_op jit(solution)/shard_map/ppermute | solution.py:240
  39.2 0.5 sums_for_rayleigh.1.refs_0_.refs_5_
  39.7 1.2 %collective-permute-start.13 = (f32[3,8,128]{2,1,0:T(8,128)S(1)}, f32[3,8,128]{2,1,0:T(8,128)S(1)}, u32[]{:S(2)}, u32[]{:S(2)}) collective-permute-start(f32[3,8,128]{2,1,0:T(8,128)S(1)} %sums_for_rayleigh.1.refs_0_.refs_5_), channel_id=1, source_target_pairs={{2,0},{0,2},{3,1},{1,3},{6,4},{4,6},{7,5},{5,7},{10,8},{8,10},{11,... | collective-permute-start | bytes 36872 | tf_op jit(solution)/shard_map/ppermute | solution.py:240
  40.9 2.6 %collective-permute-done.13.refs_1_.refs_6_ = f32[3,8,128]{2,1,0:T(8,128)S(1)} collective-permute-done((f32[3,8,128]{2,1,0:T(8,128)S(1)}, f32[3,8,128]{2,1,0:T(8,128)S(1)}, u32[]{:S(2)}, u32[]{:S(2)}) %collective-permute-start.13) | collective-permute-done | bytes 12320 | tf_op jit(solution)/shard_map/ppermute | solution.py:240
  43.5 0.0 collective-permute-done.17.refs_1_
  43.5 0.1 collective-permute-done.18.refs_2_
  43.6 0.0 collective-permute-done.19.refs_3_
  43.6 2.3 %collective-permute-start.22 = (bf16[1,64,512]{2,1,0:T(8,128)(2,1)S(1)}, bf16[1,64,512]{2,1,0:T(8,128)(2,1)S(1)}, u32[]{:S(2)}, u32[]{:S(2)}) collective-permute-start(bf16[1,64,512]{2,1,0:T(8,128)(2,1)S(1)} %sum_second_sigma.1.refs_3_), channel_id=1, source_target_pairs={{12,0},{8,4},{4,8},{0,12},{13,1},{9,5},{5,9},{1,13},{14,2},{10,6},... | collective-permute-start | bytes 196616 | tf_op jit(solution)/shard_map/ppermute | solution.py:240
  45.9 0.0 collective-permute-start.20
  45.9 2.2 %collective-permute-start.21 = (bf16[1,64,512]{2,1,0:T(8,128)(2,1)S(1)}, bf16[1,64,512]{2,1,0:T(8,128)(2,1)S(1)}, u32[]{:S(2)}, u32[]{:S(2)}) collective-permute-start(bf16[1,64,512]{2,1,0:T(8,128)(2,1)S(1)} %sum_second_sigma.1.refs_3_), channel_id=1, source_target_pairs={{4,0},{0,4},{12,8},{8,12},{5,1},{1,5},{13,9},{9,13},{6,2},{2,6},{1... | collective-permute-start | bytes 196616 | tf_op jit(solution)/shard_map/ppermute | solution.py:240
  48.1 1.4 %second_wave.1 = (bf16[1,256,512]{2,1,0:T(8,128)(2,1)}, f32[2,8,128]{2,1,0:T(8,128)S(1)}) custom-call(s32[2,2]{1,0:T(2,128)S(1)} %copy-done.3, bf16[256,512]{1,0:T(8,128)(2,1)S(1)} %get-tuple-element.24.refs_5_.wave_own, bf16[1,256,512]{2,1,0:T(8,128)(2,1)S(1)} %place_own_sector.1.sigma_own.own.refs_1_, f32[3,8,128]{2,1,0:T(8,128)S(1)} %sums_for_rayleigh.1.refs_0_.refs_5_, ...), custom_call_target="tpu_custom_call" | custom-call | tf_op jit(solution)/shard_map/second_wave/pallas_call | solution.py:258
  49.5 0.8 %collective-permute-done.22.refs_2_ = bf16[1,64,512]{2,1,0:T(8,128)(2,1)S(1)} collective-permute-done((bf16[1,64,512]{2,1,0:T(8,128)(2,1)S(1)}, bf16[1,64,512]{2,1,0:T(8,128)(2,1)S(1)}, u32[]{:S(2)}, u32[]{:S(2)}) %collective-permute-start.22) | collective-permute-done | bytes 65568 | tf_op jit(solution)/shard_map/ppermute | solution.py:240
  50.4 0.8 %join_early_shares.1.refs_4_ = f32[1,256,512]{2,1,0:T(8,128)} custom-call(f32[2,8,128]{2,1,0:T(8,128)S(1)} %get-tuple-element.36.refs_0_, bf16[1,256,512]{2,1,0:T(8,128)(2,1)S(1)} %place_own_sector.1.sigma_own.own.refs_1_, bf16[1,64,512]{2,1,0:T(8,128)(2,1)S(1)} %collective-permute-done.22.refs_2_, bf16[1,64,512]{2,1,0:T(8,128)(2,1)S(1)} %sum_second_sigma.1.refs_3_), custom_call_target="tpu_custom_call" | custom-call | tf_op jit(solution)/shard_map/join_early_shares/pallas_call | solution.py:432
  51.1 1.2 %collective-permute-done.20.refs_2_ = bf16[1,64,512]{2,1,0:T(8,128)(2,1)S(1)} collective-permute-done((bf16[1,64,512]{2,1,0:T(8,128)(2,1)S(1)}, bf16[1,64,512]{2,1,0:T(8,128)(2,1)S(1)}, u32[]{:S(2)}, u32[]{:S(2)}) %collective-permute-start.20) | collective-permute-done | bytes 65568 | tf_op jit(solution)/shard_map/ppermute | solution.py:240
  52.3 0.0 collective-permute-done.21.refs_3_
  52.3 0.8 %join_late_shares.1 = f32[1,256,512]{2,1,0:T(8,128)} custom-call(f32[2,8,128]{2,1,0:T(8,128)S(1)} %get-tuple-element.36.refs_0_, bf16[1,256,512]{2,1,0:T(8,128)(2,1)S(1)} %place_own_sector.1.sigma_own.own.refs_1_, bf16[1,64,512]{2,1,0:T(8,128)(2,1)S(1)} %collective-permute-done.20.refs_2_, ...), custom_call_target="tpu_custom_call", output_to_operand_aliasing={{}: (4, {})} | custom-call | tf_op jit(solution)/shard_map/join_late_shares/pallas_call | solution.py:432
  (7 shorter events, 0.1 us)
Async XLA Ops:
  0.6 2.0 %copy-start.1 = (bf16[1,256,512]{2,1,0:T(8,128)(2,1)S(1)}, bf16[1,256,512]{2,1,0:T(8,128)(2,1)}, u32[]{:S(2)}) copy-start(bf16[1,256,512]{2,1,0:T(8,128)(2,1)} %wave.1) | copy-start | bytes 786436
  0.6 2.0 %copy-start.3 = (s32[2,2]{1,0:T(2,128)S(1)}, s32[2,2]{1,0:T(2,128)}, u32[]{:S(2)}) copy-start(s32[2,2]{1,0:T(2,128)} %sizes_ref.3) | copy-start | bytes 52
  0.7 2.0 %copy-start.2 = (s32[4,8,2]{1,2,0:T(2,128)S(1)}, s32[4,8,2]{1,2,0:T(2,128)}, u32[]{:S(2)}) copy-start(s32[4,8,2]{1,2,0:T(2,128)} %param.10) | copy-start | bytes 772
  0.7 2.0 %copy-start.4 = (f32[4,8]{1,0:T(4,128)S(1)}, f32[4,8]{1,0:T(4,128)}, u32[]{:S(2)}) copy-start(f32[4,8]{1,0:T(4,128)} %weights_ref.1) | copy-start | bytes 388
  0.7 2.2 %copy-start = (bf16[4,512,512]{2,1,0:T(8,128)(2,1)S(1)}, bf16[4,512,512]{2,1,0:T(8,128)(2,1)}, u32[]{:S(2)}) copy-start(bf16[4,512,512]{2,1,0:T(8,128)(2,1)} %right.1) | copy-start | bytes 6291460
  0.7 2.2 %collective-permute-start = (bf16[1,256,512]{2,1,0:T(8,128)(2,1)}, bf16[1,256,512]{2,1,0:T(8,128)(2,1)S(1)}, u32[]{:S(2)}, u32[]{:S(2)}) collective-permute-start(bf16[1,256,512]{2,1,0:T(8,128)(2,1)} %wave.1), channel_id=1, source_target_pairs={{1,0},{0,1},{3,2},{2,3},{5,4},{4,5},{7,6},{6,7},{9,8},{8,9},{11,10... | collective-permute-start | bytes 786440 | tf_op jit(solution)/shard_map/ppermute | solution.py:240
  4.5 8.6 %collective-permute-start.1 = (bf16[2,64,512]{2,1,0:T(8,128)(2,1)S(1)}, bf16[2,64,512]{2,1,0:T(8,128)(2,1)S(1)}, u32[]{:S(2)}, u32[]{:S(2)}) collective-permute-start(bf16[2,64,512]{2,1,0:T(8,128)(2,1)S(1)} %get-tuple-element.28), channel_id=1, source_target_pairs={{2,0},{0,2},{3,1},{1,3},{6,4},{4,6},{7,5},{5,7},{10,8},{8,10},{11,... | collective-permute-start | bytes 393224 | tf_op jit(solution)/shard_map/ppermute | solution.py:240
  7.3 10.4 %collective-permute-start.3 = (bf16[1,64,512]{2,1,0:T(8,128)(2,1)S(1)}, bf16[1,64,512]{2,1,0:T(8,128)(2,1)S(1)}, u32[]{:S(2)}, u32[]{:S(2)}) collective-permute-start(bf16[1,64,512]{2,1,0:T(8,128)(2,1)S(1)} %get-tuple-element.29), channel_id=1, source_target_pairs={{8,0},{12,4},{0,8},{4,12},{9,1},{13,5},{1,9},{5,13},{10,2},{14,6},... | collective-permute-start | bytes 196616 | tf_op jit(solution)/shard_map/ppermute | solution.py:240
  9.9 7.8 %collective-permute-start.4 = (bf16[1,64,512]{2,1,0:T(8,128)(2,1)S(1)}, bf16[1,64,512]{2,1,0:T(8,128)(2,1)S(1)}, u32[]{:S(2)}, u32[]{:S(2)}) collective-permute-start(bf16[1,64,512]{2,1,0:T(8,128)(2,1)S(1)} %get-tuple-element.30), channel_id=1, source_target_pairs={{4,0},{0,4},{12,8},{8,12},{5,1},{1,5},{13,9},{9,13},{6,2},{2,6},{1... | collective-permute-start | bytes 196616 | tf_op jit(solution)/shard_map/ppermute | solution.py:240
  11.5 8.4 %collective-permute-start.5 = (bf16[1,64,512]{2,1,0:T(8,128)(2,1)S(1)}, bf16[1,64,512]{2,1,0:T(8,128)(2,1)S(1)}, u32[]{:S(2)}, u32[]{:S(2)}) collective-permute-start(bf16[1,64,512]{2,1,0:T(8,128)(2,1)S(1)} %get-tuple-element.31), channel_id=1, source_target_pairs={{10,0},{8,2},{14,4},{12,6},{2,8},{0,10},{6,12},{4,14},{11,1},{9,3}... | collective-permute-start | bytes 196616 | tf_op jit(solution)/shard_map/ppermute | solution.py:240
  11.8 8.1 %collective-permute-start.6 = (bf16[1,64,512]{2,1,0:T(8,128)(2,1)S(1)}, bf16[1,64,512]{2,1,0:T(8,128)(2,1)S(1)}, u32[]{:S(2)}, u32[]{:S(2)}) collective-permute-start(bf16[1,64,512]{2,1,0:T(8,128)(2,1)S(1)} %get-tuple-element.32), channel_id=1, source_target_pairs={{6,0},{4,2},{2,4},{0,6},{14,8},{12,10},{10,12},{8,14},{7,1},{5,3},... | collective-permute-start | bytes 196616 | tf_op jit(solution)/shard_map/ppermute | solution.py:240
  13.2 6.7 %collective-permute-start.2 = (bf16[1,64,512]{2,1,0:T(8,128)(2,1)S(1)}, bf16[1,64,512]{2,1,0:T(8,128)(2,1)S(1)}, u32[]{:S(2)}, u32[]{:S(2)}) collective-permute-start(bf16[1,64,512]{2,1,0:T(8,128)(2,1)S(1)} %sum_far_share.1), channel_id=1, source_target_pairs={{12,0},{8,4},{4,8},{0,12},{13,1},{9,5},{5,9},{1,13},{14,2},{10,6},... | collective-permute-start | bytes 196616 | tf_op jit(solution)/shard_map/ppermute | solution.py:240
  20.0 6.8 %collective-permute-start.9 = (bf16[1,64,512]{2,1,0:T(8,128)(2,1)S(1)}, bf16[1,64,512]{2,1,0:T(8,128)(2,1)S(1)}, u32[]{:S(2)}, u32[]{:S(2)}) collective-permute-start(bf16[1,64,512]{2,1,0:T(8,128)(2,1)S(1)} %sum_first_sigma.1.refs_5_), channel_id=1, source_target_pairs={{8,0},{12,4},{0,8},{4,12},{9,1},{13,5},{1,9},{5,13},{10,2},{14,6},... | collective-permute-start | bytes 196616 | tf_op jit(solution)/shard_map/ppermute | solution.py:240
  21.0 6.7 %collective-permute-start.10 = (bf16[1,64,512]{2,1,0:T(8,128)(2,1)S(1)}, bf16[1,64,512]{2,1,0:T(8,128)(2,1)S(1)}, u32[]{:S(2)}, u32[]{:S(2)}) collective-permute-start(bf16[1,64,512]{2,1,0:T(8,128)(2,1)S(1)} %sum_first_sigma.1.refs_5_), channel_id=1, source_target_pairs={{12,0},{8,4},{4,8},{0,12},{13,1},{9,5},{5,9},{1,13},{14,2},{10,6},... | collective-permute-start | bytes 196616 | tf_op jit(solution)/shard_map/ppermute | solution.py:240
  23.1 5.7 %collective-permute-start.7 = (bf16[1,64,512]{2,1,0:T(8,128)(2,1)S(1)}, bf16[1,64,512]{2,1,0:T(8,128)(2,1)S(1)}, u32[]{:S(2)}, u32[]{:S(2)}) collective-permute-start(bf16[1,64,512]{2,1,0:T(8,128)(2,1)S(1)} %sum_first_sigma.1.refs_5_), channel_id=1, source_target_pairs={{6,0},{4,2},{2,4},{0,6},{14,8},{12,10},{10,12},{8,14},{7,1},{5,3},... | collective-permute-start | bytes 196616 | tf_op jit(solution)/shard_map/ppermute | solution.py:240
  23.6 5.3 %collective-permute-start.8 = (bf16[1,64,512]{2,1,0:T(8,128)(2,1)S(1)}, bf16[1,64,512]{2,1,0:T(8,128)(2,1)S(1)}, u32[]{:S(2)}, u32[]{:S(2)}) collective-permute-start(bf16[1,64,512]{2,1,0:T(8,128)(2,1)S(1)} %sum_first_sigma.1.refs_5_), channel_id=1, source_target_pairs={{2,0},{0,2},{3,1},{1,3},{6,4},{4,6},{7,5},{5,7},{10,8},{8,10},{11,... | collective-permute-start | bytes 196616 | tf_op jit(solution)/shard_map/ppermute | solution.py:240
  25.1 4.3 %collective-permute-start.11 = (bf16[1,64,512]{2,1,0:T(8,128)(2,1)S(1)}, bf16[1,64,512]{2,1,0:T(8,128)(2,1)S(1)}, u32[]{:S(2)}, u32[]{:S(2)}) collective-permute-start(bf16[1,64,512]{2,1,0:T(8,128)(2,1)S(1)} %sum_first_sigma.1.refs_5_), channel_id=1, source_target_pairs={{4,0},{0,4},{12,8},{8,12},{5,1},{1,5},{13,9},{9,13},{6,2},{2,6},{1... | collective-permute-start | bytes 196616 | tf_op jit(solution)/shard_map/ppermute | solution.py:240
  26.8 4.3 %collective-permute-start.14 = (bf16[1,64,512]{2,1,0:T(8,128)(2,1)S(1)}, bf16[1,64,512]{2,1,0:T(8,128)(2,1)S(1)}, u32[]{:S(2)}, u32[]{:S(2)}) collective-permute-start(bf16[1,64,512]{2,1,0:T(8,128)(2,1)S(1)} %collective-permute-done.9.refs_2_), channel_id=1, source_target_pairs={{2,0},{0,2},{3,1},{1,3},{6,4},{4,6},{7,5},{5,7},{10,8},{8,10},{11,... | collective-permute-start | bytes 196616 | tf_op jit(solution)/shard_map/ppermute | solution.py:240
  27.7 4.3 %collective-permute-start.15 = (bf16[1,64,512]{2,1,0:T(8,128)(2,1)S(1)}, bf16[1,64,512]{2,1,0:T(8,128)(2,1)S(1)}, u32[]{:S(2)}, u32[]{:S(2)}) collective-permute-start(bf16[1,64,512]{2,1,0:T(8,128)(2,1)S(1)} %collective-permute-done.10.refs_3_), channel_id=1, source_target_pairs={{2,0},{0,2},{3,1},{1,3},{6,4},{4,6},{7,5},{5,7},{10,8},{8,10},{11,... | collective-permute-start | bytes 196616 | tf_op jit(solution)/shard_map/ppermute | solution.py:240
  29.4 2.7 %collective-permute-start.12 = (bf16[1,256,512]{2,1,0:T(8,128)(2,1)S(1)}, bf16[1,256,512]{2,1,0:T(8,128)(2,1)S(1)}, u32[]{:S(2)}, u32[]{:S(2)}) collective-permute-start(bf16[1,256,512]{2,1,0:T(8,128)(2,1)S(1)} %place_own_sector.1.sigma_own.own.refs_1_), channel_id=1, source_target_pairs={{1,0},{0,1},{3,2},{2,3},{5,4},{4,5},{7,6},{6,7},{9,8},{8,9},{11,10... | collective-permute-start | bytes 786440 | tf_op jit(solution)/shard_map/ppermute | solution.py:240
  32.0 1.6 %collective-permute-start.16 = (bf16[1,256,512]{2,1,0:T(8,128)(2,1)S(1)}, bf16[1,256,512]{2,1,0:T(8,128)(2,1)S(1)}, u32[]{:S(2)}, u32[]{:S(2)}) collective-permute-start(bf16[1,256,512]{2,1,0:T(8,128)(2,1)S(1)} %place_other_sectors.1.across_own), channel_id=1, source_target_pairs={{1,0},{0,1},{3,2},{2,3},{5,4},{4,5},{7,6},{6,7},{9,8},{8,9},{11,10... | collective-permute-start | bytes 786440 | tf_op jit(solution)/shard_map/ppermute | solution.py:240
  34.7 8.7 %collective-permute-start.17 = (bf16[1,64,512]{2,1,0:T(8,128)(2,1)S(1)}, bf16[1,64,512]{2,1,0:T(8,128)(2,1)S(1)}, u32[]{:S(2)}, u32[]{:S(2)}) collective-permute-start(bf16[1,64,512]{2,1,0:T(8,128)(2,1)S(1)} %get-tuple-element.41), channel_id=1, source_target_pairs={{12,0},{8,4},{4,8},{0,12},{13,1},{9,5},{5,9},{1,13},{14,2},{10,6},... | collective-permute-start | bytes 196616 | tf_op jit(solution)/shard_map/ppermute | solution.py:240
  37.0 6.5 %collective-permute-start.18 = (bf16[1,64,512]{2,1,0:T(8,128)(2,1)S(1)}, bf16[1,64,512]{2,1,0:T(8,128)(2,1)S(1)}, u32[]{:S(2)}, u32[]{:S(2)}) collective-permute-start(bf16[1,64,512]{2,1,0:T(8,128)(2,1)S(1)} %get-tuple-element.42), channel_id=1, source_target_pairs={{8,0},{12,4},{0,8},{4,12},{9,1},{13,5},{1,9},{5,13},{10,2},{14,6},... | collective-permute-start | bytes 196616 | tf_op jit(solution)/shard_map/ppermute | solution.py:240
  37.1 6.5 %collective-permute-start.19 = (bf16[1,64,512]{2,1,0:T(8,128)(2,1)S(1)}, bf16[1,64,512]{2,1,0:T(8,128)(2,1)S(1)}, u32[]{:S(2)}, u32[]{:S(2)}) collective-permute-start(bf16[1,64,512]{2,1,0:T(8,128)(2,1)S(1)} %get-tuple-element.43), channel_id=1, source_target_pairs={{4,0},{0,4},{12,8},{8,12},{5,1},{1,5},{13,9},{9,13},{6,2},{2,6},{1... | collective-permute-start | bytes 196616 | tf_op jit(solution)/shard_map/ppermute | solution.py:240
  39.7 3.8 %collective-permute-start.13 = (f32[3,8,128]{2,1,0:T(8,128)S(1)}, f32[3,8,128]{2,1,0:T(8,128)S(1)}, u32[]{:S(2)}, u32[]{:S(2)}) collective-permute-start(f32[3,8,128]{2,1,0:T(8,128)S(1)} %sums_for_rayleigh.1.refs_0_.refs_5_), channel_id=1, source_target_pairs={{2,0},{0,2},{3,1},{1,3},{6,4},{4,6},{7,5},{5,7},{10,8},{8,10},{11,... | collective-permute-start | bytes 36872 | tf_op jit(solution)/shard_map/ppermute | solution.py:240
  43.6 6.7 %collective-permute-start.22 = (bf16[1,64,512]{2,1,0:T(8,128)(2,1)S(1)}, bf16[1,64,512]{2,1,0:T(8,128)(2,1)S(1)}, u32[]{:S(2)}, u32[]{:S(2)}) collective-permute-start(bf16[1,64,512]{2,1,0:T(8,128)(2,1)S(1)} %sum_second_sigma.1.refs_3_), channel_id=1, source_target_pairs={{12,0},{8,4},{4,8},{0,12},{13,1},{9,5},{5,9},{1,13},{14,2},{10,6},... | collective-permute-start | bytes 196616 | tf_op jit(solution)/shard_map/ppermute | solution.py:240
  45.9 6.4 %collective-permute-start.20 = (bf16[1,64,512]{2,1,0:T(8,128)(2,1)S(1)}, bf16[1,64,512]{2,1,0:T(8,128)(2,1)S(1)}, u32[]{:S(2)}, u32[]{:S(2)}) collective-permute-start(bf16[1,64,512]{2,1,0:T(8,128)(2,1)S(1)} %sum_second_sigma.1.refs_3_), channel_id=1, source_target_pairs={{8,0},{12,4},{0,8},{4,12},{9,1},{13,5},{1,9},{5,13},{10,2},{14,6},... | collective-permute-start | bytes 196616 | tf_op jit(solution)/shard_map/ppermute | solution.py:240
  45.9 6.4 %collective-permute-start.21 = (bf16[1,64,512]{2,1,0:T(8,128)(2,1)S(1)}, bf16[1,64,512]{2,1,0:T(8,128)(2,1)S(1)}, u32[]{:S(2)}, u32[]{:S(2)}) collective-permute-start(bf16[1,64,512]{2,1,0:T(8,128)(2,1)S(1)} %sum_second_sigma.1.refs_3_), channel_id=1, source_target_pairs={{4,0},{0,4},{12,8},{8,12},{5,1},{1,5},{13,9},{9,13},{6,2},{2,6},{1... | collective-permute-start | bytes 196616 | tf_op jit(solution)/shard_map/ppermute | solution.py:240

commit v25 on v24

--- a/solution.py
+++ b/solution.py
@@ -336,7 +336,7 @@
     )
     met = [partner(rest[(far, 0), across], {"sec": across}) for across in range(sectors)]
     received = [partner(summed("sum_far_share", *met), {"ops": far})]
-    first_two = [(direct[0], 0), (direct[-1], 0)]
+    first_two = [(direct[-1], 0), (direct[0], 0)]
     order = first_two + [spot for spot in rest if spot[0] in direct and spot not in first_two]
     received += [partner(rest[spot], {"ops": spot[0][0], "sec": spot[1]}) for spot in order]
     first_share = summed("sum_first_sigma", *[(piece, 1) for piece in met], *received, live=live)

time: 53.3 us -> 53.5 us (level)
  starting transfers between devices: 31.7 us -> 32.8 us
  waiting for transfers between devices: 10.8 us -> 9.91 us
    ppermute x23, starting transfers between devices: 31.7 us -> 32.8 us  [partner(): return lax.ppermute(value, axes, pairs)]
    ppermute x23, waiting for transfers between devices: 10.8 us -> 9.91 us  [partner(): return lax.ppermute(value, axes, pairs)]
  transfers between devices with their start and end apart: 23 -> 23, of which waited for: 10 -> 9; matrix products, arithmetic and copies ran while one was open for 0% -> 0% of each run, Pallas kernels for 12% -> 12%
where the time goes in v25:
time: 53.5 us; the launch traced here: 53.3 us
  starting transfers between devices  32.8 us (61%)
  waiting for transfers between devices  9.91 us (19%)
  Pallas kernels  9.78 us (18%)
  between operations  0.86 us (2%)
    ppermute x23, starting transfers between devices, partner(): return lax.ppermute(value, axes, pairs)  32.8 us
    ppermute x23, waiting for transfers between devices, partner(): return lax.ppermute(value, axes, pairs)  9.91 us
    pallas_call x13, Pallas kernels, call(): pl.pallas_call(kernel, out_shape=out_shape, in_specs=list(in_specs) + [in...  8.23 us
    pallas_call x2, Pallas kernels, local(): pl.pallas_call(lambda *refs, steps=steps: join_kernel(steps, *refs), out_...  1.54 us
  transfers between devices with their start and end apart: 23, of which 9 were waited for; matrix products, arithmetic and copies ran while one was open for 0% of the time, Pallas kernels for 12%

profile of v25, /device:TPU:0, one launch (start us, length us, event | category | flops | bytes accessed | tf_op | source)
XLA Modules:
  0.0 53.3 jit_solution(11828674833428346865)
XLA Ops:
  0.6 0.0 copy-start.1
  0.6 0.0 copy-start.3
  0.7 0.0 copy-start.2
  0.7 0.0 copy-start.4
  0.7 0.0 copy-start
  0.7 0.5 collective-permute-start
  1.2 1.4 %load_operators.1 = (bf16[4,256,256]{2,1,0:T(8,128)(2,1)S(1)}, bf16[4,256,256]{2,1,0:T(8,128)(2,1)S(1)}) custom-call(bf16[4,512,512]{2,1,0:T(8,128)(2,1)} %left_ref.1), custom_call_target="tpu_custom_call" | custom-call | tf_op jit(solution)/shard_map/load_operators/pallas_call | solution.py:258
  2.6 0.0 copy-done.1
  2.6 0.0 copy-done.3
  2.7 0.2 tables_for_first_sigma.1
  2.9 0.0 collective-permute-done.refs_6_
  2.9 1.6 %first_sigma_terms.1 = (bf16[256,512]{1,0:T(8,128)(2,1)S(1)}, f32[2,64,512]{2,1,0:T(8,128)S(1)}, bf16[2,64,512]{2,1,0:T(8,128)(2,1)S(1)}, bf16[1,64,512]{2,1,0:T...) custom-call(s32[2,2]{1,0:T(2,128)S(1)} %copy-done.3, ...), custom_call_target="tpu_custom_call" | custom-call | tf_op jit(solution)/shard_map/first_sigma_terms/pallas_call | solution.py:258
  4.5 2.8 %collective-permute-start.1 = (bf16[2,64,512]{2,1,0:T(8,128)(2,1)S(1)}, bf16[2,64,512]{2,1,0:T(8,128)(2,1)S(1)}, u32[]{:S(2)}, u32[]{:S(2)}) collective-permute-start(bf16[2,64,512]{2,1,0:T(8,128)(2,1)S(1)} %get-tuple-element.28), channel_id=1, source_target_pairs={{2,0},{0,2},{3,1},{1,3},{6,4},{4,6},{7,5},{5,7},{10,8},{8,10},{11,... | collective-permute-start | bytes 393224 | tf_op jit(solution)/shard_map/ppermute | solution.py:240
  7.3 1.6 %collective-permute-start.3 = (bf16[1,64,512]{2,1,0:T(8,128)(2,1)S(1)}, bf16[1,64,512]{2,1,0:T(8,128)(2,1)S(1)}, u32[]{:S(2)}, u32[]{:S(2)}) collective-permute-start(bf16[1,64,512]{2,1,0:T(8,128)(2,1)S(1)} %get-tuple-element.29), channel_id=1, source_target_pairs={{4,0},{0,4},{12,8},{8,12},{5,1},{1,5},{13,9},{9,13},{6,2},{2,6},{1... | collective-permute-start | bytes 196616 | tf_op jit(solution)/shard_map/ppermute | solution.py:240
  8.9 2.6 %collective-permute-start.4 = (bf16[1,64,512]{2,1,0:T(8,128)(2,1)S(1)}, bf16[1,64,512]{2,1,0:T(8,128)(2,1)S(1)}, u32[]{:S(2)}, u32[]{:S(2)}) collective-permute-start(bf16[1,64,512]{2,1,0:T(8,128)(2,1)S(1)} %get-tuple-element.30), channel_id=1, source_target_pairs={{8,0},{12,4},{0,8},{4,12},{9,1},{13,5},{1,9},{5,13},{10,2},{14,6},... | collective-permute-start | bytes 196616 | tf_op jit(solution)/shard_map/ppermute | solution.py:240
  11.5 0.3 collective-permute-start.5
  11.8 1.4 %collective-permute-start.6 = (bf16[1,64,512]{2,1,0:T(8,128)(2,1)S(1)}, bf16[1,64,512]{2,1,0:T(8,128)(2,1)S(1)}, u32[]{:S(2)}, u32[]{:S(2)}) collective-permute-start(bf16[1,64,512]{2,1,0:T(8,128)(2,1)S(1)} %get-tuple-element.32), channel_id=1, source_target_pairs={{6,0},{4,2},{2,4},{0,6},{14,8},{12,10},{10,12},{8,14},{7,1},{5,3},... | collective-permute-start | bytes 196616 | tf_op jit(solution)/shard_map/ppermute | solution.py:240
  13.1 0.0 collective-permute-done.1.refs_1_
  13.2 3.7 %collective-permute-start.2 = (bf16[1,64,512]{2,1,0:T(8,128)(2,1)S(1)}, bf16[1,64,512]{2,1,0:T(8,128)(2,1)S(1)}, u32[]{:S(2)}, u32[]{:S(2)}) collective-permute-start(bf16[1,64,512]{2,1,0:T(8,128)(2,1)S(1)} %sum_far_share.1), channel_id=1, source_target_pairs={{12,0},{8,4},{4,8},{0,12},{13,1},{9,5},{5,9},{1,13},{14,2},{10,6},... | collective-permute-start | bytes 196616 | tf_op jit(solution)/shard_map/ppermute | solution.py:240
  16.8 0.8 %tables_for_second_sigma.1 = (f32[4,2,8,128]{3,2,1,0:T(8,128)S(1)}, f32[256,512]{1,0:T(8,128)S(1)}) custom-call(s32[2,2]{1,0:T(2,128)S(1)} %copy-done.3, s32[4,2,8]{2,1,0:T(2,128)S(1)} %bitcast.2, f32[4,8]{1,0:T(4,128)S(1)} %copy-done.4, bf16[256,512]{1,0:T(8,128)(2,1)S(1)} %get-tuple-element.33._.wave_other), custom_call_target="tpu_custom_call" | custom-call | tf_op jit(solution)/shard_map/tables_for_second_sigma/pallas_call | solution.py:258
  17.6 0.0 collective-permute-done.3.refs_3_
  17.7 0.0 collective-permute-done.4.refs_4_
  17.7 2.2 %collective-permute-done.5.refs_5_ = bf16[1,64,512]{2,1,0:T(8,128)(2,1)S(1)} collective-permute-done((bf16[1,64,512]{2,1,0:T(8,128)(2,1)S(1)}, bf16[1,64,512]{2,1,0:T(8,128)(2,1)S(1)}, u32[]{:S(2)}, u32[]{:S(2)}) %collective-permute-start.5) | collective-permute-done | bytes 65568 | tf_op jit(solution)/shard_map/ppermute | solution.py:240
  19.9 0.0 collective-permute-done.6.refs_6_
  19.9 0.0 collective-permute-done.2.refs_2_
  19.9 0.1 sum_first_sigma.1.refs_5_
  20.0 1.3 %collective-permute-start.9 = (bf16[1,64,512]{2,1,0:T(8,128)(2,1)S(1)}, bf16[1,64,512]{2,1,0:T(8,128)(2,1)S(1)}, u32[]{:S(2)}, u32[]{:S(2)}) collective-permute-start(bf16[1,64,512]{2,1,0:T(8,128)(2,1)S(1)} %sum_first_sigma.1.refs_5_), channel_id=1, source_target_pairs={{8,0},{12,4},{0,8},{4,12},{9,1},{13,5},{1,9},{5,13},{10,2},{14,6},... | collective-permute-start | bytes 196616 | tf_op jit(solution)/shard_map/ppermute | solution.py:240
  21.3 2.1 %collective-permute-start.10 = (bf16[1,64,512]{2,1,0:T(8,128)(2,1)S(1)}, bf16[1,64,512]{2,1,0:T(8,128)(2,1)S(1)}, u32[]{:S(2)}, u32[]{:S(2)}) collective-permute-start(bf16[1,64,512]{2,1,0:T(8,128)(2,1)S(1)} %sum_first_sigma.1.refs_5_), channel_id=1, source_target_pairs={{12,0},{8,4},{4,8},{0,12},{13,1},{9,5},{5,9},{1,13},{14,2},{10,6},... | collective-permute-start | bytes 196616 | tf_op jit(solution)/shard_map/ppermute | solution.py:240
  23.4 0.3 collective-permute-start.7
  23.7 1.4 %collective-permute-start.8 = (bf16[1,64,512]{2,1,0:T(8,128)(2,1)S(1)}, bf16[1,64,512]{2,1,0:T(8,128)(2,1)S(1)}, u32[]{:S(2)}, u32[]{:S(2)}) collective-permute-start(bf16[1,64,512]{2,1,0:T(8,128)(2,1)S(1)} %sum_first_sigma.1.refs_5_), channel_id=1, source_target_pairs={{2,0},{0,2},{3,1},{1,3},{6,4},{4,6},{7,5},{5,7},{10,8},{8,10},{11,... | collective-permute-start | bytes 196616 | tf_op jit(solution)/shard_map/ppermute | solution.py:240
  25.1 1.8 %collective-permute-start.11 = (bf16[1,64,512]{2,1,0:T(8,128)(2,1)S(1)}, bf16[1,64,512]{2,1,0:T(8,128)(2,1)S(1)}, u32[]{:S(2)}, u32[]{:S(2)}) collective-permute-start(bf16[1,64,512]{2,1,0:T(8,128)(2,1)S(1)} %sum_first_sigma.1.refs_5_), channel_id=1, source_target_pairs={{4,0},{0,4},{12,8},{8,12},{5,1},{1,5},{13,9},{9,13},{6,2},{2,6},{1... | collective-permute-start | bytes 196616 | tf_op jit(solution)/shard_map/ppermute | solution.py:240
  26.9 0.0 collective-permute-done.9.refs_2_
  26.9 0.8 %collective-permute-start.14 = (bf16[1,64,512]{2,1,0:T(8,128)(2,1)S(1)}, bf16[1,64,512]{2,1,0:T(8,128)(2,1)S(1)}, u32[]{:S(2)}, u32[]{:S(2)}) collective-permute-start(bf16[1,64,512]{2,1,0:T(8,128)(2,1)S(1)} %collective-permute-done.9.refs_2_), channel_id=1, source_target_pairs={{2,0},{0,2},{3,1},{1,3},{6,4},{4,6},{7,5},{5,7},{10,8},{8,10},{11,... | collective-permute-start | bytes 196616 | tf_op jit(solution)/shard_map/ppermute | solution.py:240
  27.7 0.3 collective-permute-done.10.refs_3_
  28.0 1.5 %collective-permute-start.15 = (bf16[1,64,512]{2,1,0:T(8,128)(2,1)S(1)}, bf16[1,64,512]{2,1,0:T(8,128)(2,1)S(1)}, u32[]{:S(2)}, u32[]{:S(2)}) collective-permute-start(bf16[1,64,512]{2,1,0:T(8,128)(2,1)S(1)} %collective-permute-done.10.refs_3_), channel_id=1, source_target_pairs={{2,0},{0,2},{3,1},{1,3},{6,4},{4,6},{7,5},{5,7},{10,8},{8,10},{11,... | collective-permute-start | bytes 196616 | tf_op jit(solution)/shard_map/ppermute | solution.py:240
  29.5 0.0 collective-permute-done.7.refs_0_.refs_2_
  29.5 0.0 collective-permute-done.8.refs_1_.refs_3_
  29.5 0.0 collective-permute-done.11.refs_4_
  29.6 0.1 collective-permute-start.12
  29.7 1.5 %collective-permute-done.14.refs_0_ = bf16[1,64,512]{2,1,0:T(8,128)(2,1)S(1)} collective-permute-done((bf16[1,64,512]{2,1,0:T(8,128)(2,1)S(1)}, bf16[1,64,512]{2,1,0:T(8,128)(2,1)S(1)}, u32[]{:S(2)}, u32[]{:S(2)}) %collective-permute-start.14) | collective-permute-done | bytes 65568 | tf_op jit(solution)/shard_map/ppermute | solution.py:240
  31.2 1.1 %collective-permute-done.15.refs_1_ = bf16[1,64,512]{2,1,0:T(8,128)(2,1)S(1)} collective-permute-done((bf16[1,64,512]{2,1,0:T(8,128)(2,1)S(1)}, bf16[1,64,512]{2,1,0:T(8,128)(2,1)S(1)}, u32[]{:S(2)}, u32[]{:S(2)}) %collective-permute-start.15) | collective-permute-done | bytes 65568 | tf_op jit(solution)/shard_map/ppermute | solution.py:240
  32.3 0.1 collective-permute-start.16
  32.4 0.0 collective-permute-done.12.sigma_other.other
  32.4 1.0 %left_products.1 = (f32[4,256,512]{2,1,0:T(8,128)S(1)}, f32[1,4,256,512]{3,2,1,0:T(8,128)S(1)}) custom-call(bf16[4,256,256]{2,1,0:T(8,128)(2,1)S(1)} %get-tuple-element.23._.refs_2_.left_own, bf16[4,256,256]{2,1,0:T(8,128)(2,1)S(1)} %get-tuple-element.26.refs_3_.left_other, bf16[1,256,512]{2,1,0:T(8,128)(2,1)S(1)} %place_own_sector.1.sigma_own.own.refs_1_, ...), custom_call_target="tpu_custom_call" | custom-call | tf_op jit(solution)/shard_map/left_products/pallas_call | solution.py:258
  33.4 0.5 %collective-permute-done.16.other = bf16[1,256,512]{2,1,0:T(8,128)(2,1)S(1)} collective-permute-done((bf16[1,256,512]{2,1,0:T(8,128)(2,1)S(1)}, bf16[1,256,512]{2,1,0:T(8,128)(2,1)S(1)}, u32[]{:S(2)}, u32[]{:S(2)}) %collective-permute-start.16) | collective-permute-done | bytes 262176 | tf_op jit(solution)/shard_map/ppermute | solution.py:240
  33.9 1.1 %second_sigma_terms.1 = (f32[1,64,512]{2,1,0:T(8,128)S(1)}, bf16[1,64,512]{2,1,0:T(8,128)(2,1)S(1)}, bf16[1,64,512]{2,1,0:T(8,128)(2,1)S(1)}, bf16[1,64,512]{2,1,0:T(8,128)(2,1)S(1)}) custom-call(f32[4,2,8,128]{3,2,1,0:T(8,128)S(1)} %get-tuple-element.37.mixing, bf16[4,256,256]{2,1,0:T(8,128)(2,1)S(1)} %get-tuple-element.26.refs_3_.left_other, ...), custom_call_target="tpu_custom_call" | custom-call | tf_op jit(solution)/shard_map/second_sigma_terms/pallas_call | solution.py:258
  35.0 2.2 %collective-permute-start.17 = (bf16[1,64,512]{2,1,0:T(8,128)(2,1)S(1)}, bf16[1,64,512]{2,1,0:T(8,128)(2,1)S(1)}, u32[]{:S(2)}, u32[]{:S(2)}) collective-permute-start(bf16[1,64,512]{2,1,0:T(8,128)(2,1)S(1)} %get-tuple-element.41), channel_id=1, source_target_pairs={{12,0},{8,4},{4,8},{0,12},{13,1},{9,5},{5,9},{1,13},{14,2},{10,6},... | collective-permute-start | bytes 196616 | tf_op jit(solution)/shard_map/ppermute | solution.py:240
  37.3 0.0 collective-permute-start.18
  37.3 2.2 %collective-permute-start.19 = (bf16[1,64,512]{2,1,0:T(8,128)(2,1)S(1)}, bf16[1,64,512]{2,1,0:T(8,128)(2,1)S(1)}, u32[]{:S(2)}, u32[]{:S(2)}) collective-permute-start(bf16[1,64,512]{2,1,0:T(8,128)(2,1)S(1)} %get-tuple-element.43), channel_id=1, source_target_pairs={{4,0},{0,4},{12,8},{8,12},{5,1},{1,5},{13,9},{9,13},{6,2},{2,6},{1... | collective-permute-start | bytes 196616 | tf_op jit(solution)/shard_map/ppermute | solution.py:240
  39.5 0.5 sums_for_rayleigh.1.refs_0_.refs_5_
  40.0 1.6 %collective-permute-start.13 = (f32[3,8,128]{2,1,0:T(8,128)S(1)}, f32[3,8,128]{2,1,0:T(8,128)S(1)}, u32[]{:S(2)}, u32[]{:S(2)}) collective-permute-start(f32[3,8,128]{2,1,0:T(8,128)S(1)} %sums_for_rayleigh.1.refs_0_.refs_5_), channel_id=1, source_target_pairs={{2,0},{0,2},{3,1},{1,3},{6,4},{4,6},{7,5},{5,7},{10,8},{8,10},{11,... | collective-permute-start | bytes 36872 | tf_op jit(solution)/shard_map/ppermute | solution.py:240
  41.6 2.1 %collective-permute-done.13.refs_1_.refs_6_ = f32[3,8,128]{2,1,0:T(8,128)S(1)} collective-permute-done((f32[3,8,128]{2,1,0:T(8,128)S(1)}, f32[3,8,128]{2,1,0:T(8,128)S(1)}, u32[]{:S(2)}, u32[]{:S(2)}) %collective-permute-start.13) | collective-permute-done | bytes 12320 | tf_op jit(solution)/shard_map/ppermute | solution.py:240
  43.7 0.0 collective-permute-done.17.refs_1_
  43.7 0.1 collective-permute-done.18.refs_2_
  43.8 0.0 collective-permute-done.19.refs_3_
  43.9 2.2 %collective-permute-start.22 = (bf16[1,64,512]{2,1,0:T(8,128)(2,1)S(1)}, bf16[1,64,512]{2,1,0:T(8,128)(2,1)S(1)}, u32[]{:S(2)}, u32[]{:S(2)}) collective-permute-start(bf16[1,64,512]{2,1,0:T(8,128)(2,1)S(1)} %sum_second_sigma.1.refs_3_), channel_id=1, source_target_pairs={{12,0},{8,4},{4,8},{0,12},{13,1},{9,5},{5,9},{1,13},{14,2},{10,6},... | collective-permute-start | bytes 196616 | tf_op jit(solution)/shard_map/ppermute | solution.py:240
  46.1 0.0 collective-permute-start.20
  46.1 2.2 %collective-permute-start.21 = (bf16[1,64,512]{2,1,0:T(8,128)(2,1)S(1)}, bf16[1,64,512]{2,1,0:T(8,128)(2,1)S(1)}, u32[]{:S(2)}, u32[]{:S(2)}) collective-permute-start(bf16[1,64,512]{2,1,0:T(8,128)(2,1)S(1)} %sum_second_sigma.1.refs_3_), channel_id=1, source_target_pairs={{4,0},{0,4},{12,8},{8,12},{5,1},{1,5},{13,9},{9,13},{6,2},{2,6},{1... | collective-permute-start | bytes 196616 | tf_op jit(solution)/shard_map/ppermute | solution.py:240
  48.3 1.4 %second_wave.1 = (bf16[1,256,512]{2,1,0:T(8,128)(2,1)}, f32[2,8,128]{2,1,0:T(8,128)S(1)}) custom-call(s32[2,2]{1,0:T(2,128)S(1)} %copy-done.3, bf16[256,512]{1,0:T(8,128)(2,1)S(1)} %get-tuple-element.24.refs_5_.wave_own, bf16[1,256,512]{2,1,0:T(8,128)(2,1)S(1)} %place_own_sector.1.sigma_own.own.refs_1_, f32[3,8,128]{2,1,0:T(8,128)S(1)} %sums_for_rayleigh.1.refs_0_.refs_5_, ...), custom_call_target="tpu_custom_call" | custom-call | tf_op jit(solution)/shard_map/second_wave/pallas_call | solution.py:258
  49.8 0.8 %collective-permute-done.22.refs_2_ = bf16[1,64,512]{2,1,0:T(8,128)(2,1)S(1)} collective-permute-done((bf16[1,64,512]{2,1,0:T(8,128)(2,1)S(1)}, bf16[1,64,512]{2,1,0:T(8,128)(2,1)S(1)}, u32[]{:S(2)}, u32[]{:S(2)}) %collective-permute-start.22) | collective-permute-done | bytes 65568 | tf_op jit(solution)/shard_map/ppermute | solution.py:240
  50.6 0.8 %join_early_shares.1.refs_4_ = f32[1,256,512]{2,1,0:T(8,128)} custom-call(f32[2,8,128]{2,1,0:T(8,128)S(1)} %get-tuple-element.36.refs_0_, bf16[1,256,512]{2,1,0:T(8,128)(2,1)S(1)} %place_own_sector.1.sigma_own.own.refs_1_, bf16[1,64,512]{2,1,0:T(8,128)(2,1)S(1)} %collective-permute-done.22.refs_2_, bf16[1,64,512]{2,1,0:T(8,128)(2,1)S(1)} %sum_second_sigma.1.refs_3_), custom_call_target="tpu_custom_call" | custom-call | tf_op jit(solution)/shard_map/join_early_shares/pallas_call | solution.py:432
  51.4 1.2 %collective-permute-done.20.refs_2_ = bf16[1,64,512]{2,1,0:T(8,128)(2,1)S(1)} collective-permute-done((bf16[1,64,512]{2,1,0:T(8,128)(2,1)S(1)}, bf16[1,64,512]{2,1,0:T(8,128)(2,1)S(1)}, u32[]{:S(2)}, u32[]{:S(2)}) %collective-permute-start.20) | collective-permute-done | bytes 65568 | tf_op jit(solution)/shard_map/ppermute | solution.py:240
  52.6 0.0 collective-permute-done.21.refs_3_
  52.6 0.8 %join_late_shares.1 = f32[1,256,512]{2,1,0:T(8,128)} custom-call(f32[2,8,128]{2,1,0:T(8,128)S(1)} %get-tuple-element.36.refs_0_, bf16[1,256,512]{2,1,0:T(8,128)(2,1)S(1)} %place_own_sector.1.sigma_own.own.refs_1_, bf16[1,64,512]{2,1,0:T(8,128)(2,1)S(1)} %collective-permute-done.20.refs_2_, ...), custom_call_target="tpu_custom_call", output_to_operand_aliasing={{}: (4, {})} | custom-call | tf_op jit(solution)/shard_map/join_late_shares/pallas_call | solution.py:432
  (7 shorter events, 0.1 us)
Async XLA Ops:
  0.6 2.0 %copy-start.1 = (bf16[1,256,512]{2,1,0:T(8,128)(2,1)S(1)}, bf16[1,256,512]{2,1,0:T(8,128)(2,1)}, u32[]{:S(2)}) copy-start(bf16[1,256,512]{2,1,0:T(8,128)(2,1)} %wave.1) | copy-start | bytes 786436
  0.6 2.0 %copy-start.3 = (s32[2,2]{1,0:T(2,128)S(1)}, s32[2,2]{1,0:T(2,128)}, u32[]{:S(2)}) copy-start(s32[2,2]{1,0:T(2,128)} %sizes_ref.3) | copy-start | bytes 52
  0.7 2.0 %copy-start.2 = (s32[4,8,2]{1,2,0:T(2,128)S(1)}, s32[4,8,2]{1,2,0:T(2,128)}, u32[]{:S(2)}) copy-start(s32[4,8,2]{1,2,0:T(2,128)} %param.10) | copy-start | bytes 772
  0.7 2.0 %copy-start.4 = (f32[4,8]{1,0:T(4,128)S(1)}, f32[4,8]{1,0:T(4,128)}, u32[]{:S(2)}) copy-start(f32[4,8]{1,0:T(4,128)} %weights_ref.1) | copy-start | bytes 388
  0.7 2.2 %copy-start = (bf16[4,512,512]{2,1,0:T(8,128)(2,1)S(1)}, bf16[4,512,512]{2,1,0:T(8,128)(2,1)}, u32[]{:S(2)}) copy-start(bf16[4,512,512]{2,1,0:T(8,128)(2,1)} %right.1) | copy-start | bytes 6291460
  0.7 2.2 %collective-permute-start = (bf16[1,256,512]{2,1,0:T(8,128)(2,1)}, bf16[1,256,512]{2,1,0:T(8,128)(2,1)S(1)}, u32[]{:S(2)}, u32[]{:S(2)}) collective-permute-start(bf16[1,256,512]{2,1,0:T(8,128)(2,1)} %wave.1), channel_id=1, source_target_pairs={{1,0},{0,1},{3,2},{2,3},{5,4},{4,5},{7,6},{6,7},{9,8},{8,9},{11,10... | collective-permute-start | bytes 786440 | tf_op jit(solution)/shard_map/ppermute | solution.py:240
  4.5 8.6 %collective-permute-start.1 = (bf16[2,64,512]{2,1,0:T(8,128)(2,1)S(1)}, bf16[2,64,512]{2,1,0:T(8,128)(2,1)S(1)}, u32[]{:S(2)}, u32[]{:S(2)}) collective-permute-start(bf16[2,64,512]{2,1,0:T(8,128)(2,1)S(1)} %get-tuple-element.28), channel_id=1, source_target_pairs={{2,0},{0,2},{3,1},{1,3},{6,4},{4,6},{7,5},{5,7},{10,8},{8,10},{11,... | collective-permute-start | bytes 393224 | tf_op jit(solution)/shard_map/ppermute | solution.py:240
  7.3 10.4 %collective-permute-start.3 = (bf16[1,64,512]{2,1,0:T(8,128)(2,1)S(1)}, bf16[1,64,512]{2,1,0:T(8,128)(2,1)S(1)}, u32[]{:S(2)}, u32[]{:S(2)}) collective-permute-start(bf16[1,64,512]{2,1,0:T(8,128)(2,1)S(1)} %get-tuple-element.29), channel_id=1, source_target_pairs={{4,0},{0,4},{12,8},{8,12},{5,1},{1,5},{13,9},{9,13},{6,2},{2,6},{1... | collective-permute-start | bytes 196616 | tf_op jit(solution)/shard_map/ppermute | solution.py:240
  8.9 8.8 %collective-permute-start.4 = (bf16[1,64,512]{2,1,0:T(8,128)(2,1)S(1)}, bf16[1,64,512]{2,1,0:T(8,128)(2,1)S(1)}, u32[]{:S(2)}, u32[]{:S(2)}) collective-permute-start(bf16[1,64,512]{2,1,0:T(8,128)(2,1)S(1)} %get-tuple-element.30), channel_id=1, source_target_pairs={{8,0},{12,4},{0,8},{4,12},{9,1},{13,5},{1,9},{5,13},{10,2},{14,6},... | collective-permute-start | bytes 196616 | tf_op jit(solution)/shard_map/ppermute | solution.py:240
  11.5 8.4 %collective-permute-start.5 = (bf16[1,64,512]{2,1,0:T(8,128)(2,1)S(1)}, bf16[1,64,512]{2,1,0:T(8,128)(2,1)S(1)}, u32[]{:S(2)}, u32[]{:S(2)}) collective-permute-start(bf16[1,64,512]{2,1,0:T(8,128)(2,1)S(1)} %get-tuple-element.31), channel_id=1, source_target_pairs={{10,0},{8,2},{14,4},{12,6},{2,8},{0,10},{6,12},{4,14},{11,1},{9,3}... | collective-permute-start | bytes 196616 | tf_op jit(solution)/shard_map/ppermute | solution.py:240
  11.8 8.1 %collective-permute-start.6 = (bf16[1,64,512]{2,1,0:T(8,128)(2,1)S(1)}, bf16[1,64,512]{2,1,0:T(8,128)(2,1)S(1)}, u32[]{:S(2)}, u32[]{:S(2)}) collective-permute-start(bf16[1,64,512]{2,1,0:T(8,128)(2,1)S(1)} %get-tuple-element.32), channel_id=1, source_target_pairs={{6,0},{4,2},{2,4},{0,6},{14,8},{12,10},{10,12},{8,14},{7,1},{5,3},... | collective-permute-start | bytes 196616 | tf_op jit(solution)/shard_map/ppermute | solution.py:240
  13.2 6.7 %collective-permute-start.2 = (bf16[1,64,512]{2,1,0:T(8,128)(2,1)S(1)}, bf16[1,64,512]{2,1,0:T(8,128)(2,1)S(1)}, u32[]{:S(2)}, u32[]{:S(2)}) collective-permute-start(bf16[1,64,512]{2,1,0:T(8,128)(2,1)S(1)} %sum_far_share.1), channel_id=1, source_target_pairs={{12,0},{8,4},{4,8},{0,12},{13,1},{9,5},{5,9},{1,13},{14,2},{10,6},... | collective-permute-start | bytes 196616 | tf_op jit(solution)/shard_map/ppermute | solution.py:240
  20.0 6.9 %collective-permute-start.9 = (bf16[1,64,512]{2,1,0:T(8,128)(2,1)S(1)}, bf16[1,64,512]{2,1,0:T(8,128)(2,1)S(1)}, u32[]{:S(2)}, u32[]{:S(2)}) collective-permute-start(bf16[1,64,512]{2,1,0:T(8,128)(2,1)S(1)} %sum_first_sigma.1.refs_5_), channel_id=1, source_target_pairs={{8,0},{12,4},{0,8},{4,12},{9,1},{13,5},{1,9},{5,13},{10,2},{14,6},... | collective-permute-start | bytes 196616 | tf_op jit(solution)/shard_map/ppermute | solution.py:240
  21.3 6.7 %collective-permute-start.10 = (bf16[1,64,512]{2,1,0:T(8,128)(2,1)S(1)}, bf16[1,64,512]{2,1,0:T(8,128)(2,1)S(1)}, u32[]{:S(2)}, u32[]{:S(2)}) collective-permute-start(bf16[1,64,512]{2,1,0:T(8,128)(2,1)S(1)} %sum_first_sigma.1.refs_5_), channel_id=1, source_target_pairs={{12,0},{8,4},{4,8},{0,12},{13,1},{9,5},{5,9},{1,13},{14,2},{10,6},... | collective-permute-start | bytes 196616 | tf_op jit(solution)/shard_map/ppermute | solution.py:240
  23.4 6.1 %collective-permute-start.7 = (bf16[1,64,512]{2,1,0:T(8,128)(2,1)S(1)}, bf16[1,64,512]{2,1,0:T(8,128)(2,1)S(1)}, u32[]{:S(2)}, u32[]{:S(2)}) collective-permute-start(bf16[1,64,512]{2,1,0:T(8,128)(2,1)S(1)} %sum_first_sigma.1.refs_5_), channel_id=1, source_target_pairs={{6,0},{4,2},{2,4},{0,6},{14,8},{12,10},{10,12},{8,14},{7,1},{5,3},... | collective-permute-start | bytes 196616 | tf_op jit(solution)/shard_map/ppermute | solution.py:240
  23.7 5.9 %collective-permute-start.8 = (bf16[1,64,512]{2,1,0:T(8,128)(2,1)S(1)}, bf16[1,64,512]{2,1,0:T(8,128)(2,1)S(1)}, u32[]{:S(2)}, u32[]{:S(2)}) collective-permute-start(bf16[1,64,512]{2,1,0:T(8,128)(2,1)S(1)} %sum_first_sigma.1.refs_5_), channel_id=1, source_target_pairs={{2,0},{0,2},{3,1},{1,3},{6,4},{4,6},{7,5},{5,7},{10,8},{8,10},{11,... | collective-permute-start | bytes 196616 | tf_op jit(solution)/shard_map/ppermute | solution.py:240
  25.1 4.5 %collective-permute-start.11 = (bf16[1,64,512]{2,1,0:T(8,128)(2,1)S(1)}, bf16[1,64,512]{2,1,0:T(8,128)(2,1)S(1)}, u32[]{:S(2)}, u32[]{:S(2)}) collective-permute-start(bf16[1,64,512]{2,1,0:T(8,128)(2,1)S(1)} %sum_first_sigma.1.refs_5_), channel_id=1, source_target_pairs={{4,0},{0,4},{12,8},{8,12},{5,1},{1,5},{13,9},{9,13},{6,2},{2,6},{1... | collective-permute-start | bytes 196616 | tf_op jit(solution)/shard_map/ppermute | solution.py:240
  26.9 4.3 %collective-permute-start.14 = (bf16[1,64,512]{2,1,0:T(8,128)(2,1)S(1)}, bf16[1,64,512]{2,1,0:T(8,128)(2,1)S(1)}, u32[]{:S(2)}, u32[]{:S(2)}) collective-permute-start(bf16[1,64,512]{2,1,0:T(8,128)(2,1)S(1)} %collective-permute-done.9.refs_2_), channel_id=1, source_target_pairs={{2,0},{0,2},{3,1},{1,3},{6,4},{4,6},{7,5},{5,7},{10,8},{8,10},{11,... | collective-permute-start | bytes 196616 | tf_op jit(solution)/shard_map/ppermute | solution.py:240
  28.0 4.3 %collective-permute-start.15 = (bf16[1,64,512]{2,1,0:T(8,128)(2,1)S(1)}, bf16[1,64,512]{2,1,0:T(8,128)(2,1)S(1)}, u32[]{:S(2)}, u32[]{:S(2)}) collective-permute-start(bf16[1,64,512]{2,1,0:T(8,128)(2,1)S(1)} %collective-permute-done.10.refs_3_), channel_id=1, source_target_pairs={{2,0},{0,2},{3,1},{1,3},{6,4},{4,6},{7,5},{5,7},{10,8},{8,10},{11,... | collective-permute-start | bytes 196616 | tf_op jit(solution)/shard_map/ppermute | solution.py:240
  29.6 2.8 %collective-permute-start.12 = (bf16[1,256,512]{2,1,0:T(8,128)(2,1)S(1)}, bf16[1,256,512]{2,1,0:T(8,128)(2,1)S(1)}, u32[]{:S(2)}, u32[]{:S(2)}) collective-permute-start(bf16[1,256,512]{2,1,0:T(8,128)(2,1)S(1)} %place_own_sector.1.sigma_own.own.refs_1_), channel_id=1, source_target_pairs={{1,0},{0,1},{3,2},{2,3},{5,4},{4,5},{7,6},{6,7},{9,8},{8,9},{11,10... | collective-permute-start | bytes 786440 | tf_op jit(solution)/shard_map/ppermute | solution.py:240
  32.3 1.6 %collective-permute-start.16 = (bf16[1,256,512]{2,1,0:T(8,128)(2,1)S(1)}, bf16[1,256,512]{2,1,0:T(8,128)(2,1)S(1)}, u32[]{:S(2)}, u32[]{:S(2)}) collective-permute-start(bf16[1,256,512]{2,1,0:T(8,128)(2,1)S(1)} %place_other_sectors.1.across_own), channel_id=1, source_target_pairs={{1,0},{0,1},{3,2},{2,3},{5,4},{4,5},{7,6},{6,7},{9,8},{8,9},{11,10... | collective-permute-start | bytes 786440 | tf_op jit(solution)/shard_map/ppermute | solution.py:240
  35.0 8.7 %collective-permute-start.17 = (bf16[1,64,512]{2,1,0:T(8,128)(2,1)S(1)}, bf16[1,64,512]{2,1,0:T(8,128)(2,1)S(1)}, u32[]{:S(2)}, u32[]{:S(2)}) collective-permute-start(bf16[1,64,512]{2,1,0:T(8,128)(2,1)S(1)} %get-tuple-element.41), channel_id=1, source_target_pairs={{12,0},{8,4},{4,8},{0,12},{13,1},{9,5},{5,9},{1,13},{14,2},{10,6},... | collective-permute-start | bytes 196616 | tf_op jit(solution)/shard_map/ppermute | solution.py:240
  37.3 6.6 %collective-permute-start.18 = (bf16[1,64,512]{2,1,0:T(8,128)(2,1)S(1)}, bf16[1,64,512]{2,1,0:T(8,128)(2,1)S(1)}, u32[]{:S(2)}, u32[]{:S(2)}) collective-permute-start(bf16[1,64,512]{2,1,0:T(8,128)(2,1)S(1)} %get-tuple-element.42), channel_id=1, source_target_pairs={{8,0},{12,4},{0,8},{4,12},{9,1},{13,5},{1,9},{5,13},{10,2},{14,6},... | collective-permute-start | bytes 196616 | tf_op jit(solution)/shard_map/ppermute | solution.py:240
  37.3 6.6 %collective-permute-start.19 = (bf16[1,64,512]{2,1,0:T(8,128)(2,1)S(1)}, bf16[1,64,512]{2,1,0:T(8,128)(2,1)S(1)}, u32[]{:S(2)}, u32[]{:S(2)}) collective-permute-start(bf16[1,64,512]{2,1,0:T(8,128)(2,1)S(1)} %get-tuple-element.43), channel_id=1, source_target_pairs={{4,0},{0,4},{12,8},{8,12},{5,1},{1,5},{13,9},{9,13},{6,2},{2,6},{1... | collective-permute-start | bytes 196616 | tf_op jit(solution)/shard_map/ppermute | solution.py:240
  40.0 3.8 %collective-permute-start.13 = (f32[3,8,128]{2,1,0:T(8,128)S(1)}, f32[3,8,128]{2,1,0:T(8,128)S(1)}, u32[]{:S(2)}, u32[]{:S(2)}) collective-permute-start(f32[3,8,128]{2,1,0:T(8,128)S(1)} %sums_for_rayleigh.1.refs_0_.refs_5_), channel_id=1, source_target_pairs={{2,0},{0,2},{3,1},{1,3},{6,4},{4,6},{7,5},{5,7},{10,8},{8,10},{11,... | collective-permute-start | bytes 36872 | tf_op jit(solution)/shard_map/ppermute | solution.py:240
  43.9 6.7 %collective-permute-start.22 = (bf16[1,64,512]{2,1,0:T(8,128)(2,1)S(1)}, bf16[1,64,512]{2,1,0:T(8,128)(2,1)S(1)}, u32[]{:S(2)}, u32[]{:S(2)}) collective-permute-start(bf16[1,64,512]{2,1,0:T(8,128)(2,1)S(1)} %sum_second_sigma.1.refs_3_), channel_id=1, source_target_pairs={{12,0},{8,4},{4,8},{0,12},{13,1},{9,5},{5,9},{1,13},{14,2},{10,6},... | collective-permute-start | bytes 196616 | tf_op jit(solution)/shard_map/ppermute | solution.py:240
  46.1 6.5 %collective-permute-start.20 = (bf16[1,64,512]{2,1,0:T(8,128)(2,1)S(1)}, bf16[1,64,512]{2,1,0:T(8,128)(2,1)S(1)}, u32[]{:S(2)}, u32[]{:S(2)}) collective-permute-start(bf16[1,64,512]{2,1,0:T(8,128)(2,1)S(1)} %sum_second_sigma.1.refs_3_), channel_id=1, source_target_pairs={{8,0},{12,4},{0,8},{4,12},{9,1},{13,5},{1,9},{5,13},{10,2},{14,6},... | collective-permute-start | bytes 196616 | tf_op jit(solution)/shard_map/ppermute | solution.py:240
  46.1 6.5 %collective-permute-start.21 = (bf16[1,64,512]{2,1,0:T(8,128)(2,1)S(1)}, bf16[1,64,512]{2,1,0:T(8,128)(2,1)S(1)}, u32[]{:S(2)}, u32[]{:S(2)}) collective-permute-start(bf16[1,64,512]{2,1,0:T(8,128)(2,1)S(1)} %sum_second_sigma.1.refs_3_), channel_id=1, source_target_pairs={{4,0},{0,4},{12,8},{8,12},{5,1},{1,5},{13,9},{9,13},{6,2},{2,6},{1... | collective-permute-start | bytes 196616 | tf_op jit(solution)/shard_map/ppermute | solution.py:240
